TPU v7x, 32 devices: a whole 2x2x4 slice. The times are simulated.
32 devices in a mesh: head: 4 (over x, core), ctx: 8 (over z, y).
Axes of the slice: x: 2, y: 2, z: 4, core: 2. Of those that a mesh axis runs over, the one named last changes fastest.
Arguments:
- queries: bfloat16 [8192, 4096], P('ctx', 'head'), may hold values from -108 to 108
- key_states: bfloat16 [8192, 1024], P(('ctx', 'head')), may hold values from -9 to 9
- value_states: bfloat16 [8192, 1024], P(('ctx', 'head')), may hold values from -6 to 6
- block_lists: int32 [128, 8], P('ctx'), may hold values from 0 to 127, as said below
- out_grad: bfloat16 [8192, 4096], P('ctx', 'head'), may hold values from -12 to 12
Outputs:
- attended: bfloat16 [8192, 4096], P('ctx', 'head')
- query_grad: bfloat16 [8192, 4096], P('ctx', 'head')
- key_grad: bfloat16 [8192, 1024], P(('ctx', 'head'))
- value_grad: bfloat16 [8192, 1024], P(('ctx', 'head'))
Inputs may be any that keep to these rules, and one draw needn't show every extreme that they name: `block_lists`: row i's first entry is i and every entry is at most i (repeats allowed). The lists of the 16 query blocks of one ctx index c name at most 3 distinct blocks held by any other ctx index (index c holds blocks c * 16 to c * 16 + 15).
All inputs are finite; a program needn't handle non-finite values.
Results may differ from a plain program's by a relative error of at most 0.04.
Values may be sent and summed in bfloat16 or wider, within the bound.
No kernel may reach another device: no remote copies, remote signals or barrier semaphores. Data moves between devices by JAX's collectives and lax.ppermute only.
A program may use at most 128 MiB of HBM per device.

v0:
```python
import jax
import jax.numpy as jnp
from jax import lax
from jax.sharding import PartitionSpec as P

HEAD_DIM = 128
GROUP = 4
BLK = 64
LIST = 8
CAP = 3


NEG_FILL = -1e30


def attend_group(args):
    query_rows, grad_rows, key_rows, value_rows, visible = args
    softmax_scale = HEAD_DIM ** (-0.5)
    scores = (
        jnp.einsum("qtkgd,qskd->qkgts", query_rows, key_rows, preferred_element_type=jnp.float32)
        * softmax_scale
    )
    scores = jnp.where(visible[:, None, None], scores, NEG_FILL)
    row_peak = jnp.max(scores, axis=-1, keepdims=True)
    expo = jnp.exp(scores - row_peak)
    attn_probs = expo / jnp.sum(expo, axis=-1, keepdims=True)
    probs_low = attn_probs.astype(jnp.bfloat16)
    attended = jnp.einsum(
        "qkgts,qskd->qtkgd", probs_low, value_rows, preferred_element_type=jnp.float32
    ).astype(jnp.bfloat16)
    row_delta = jnp.sum(grad_rows.astype(jnp.float32) * attended.astype(jnp.float32), axis=-1)
    row_delta = jnp.transpose(row_delta, (0, 2, 3, 1))[..., None]
    dprob = jnp.einsum(
        "qtkgd,qskd->qkgts", grad_rows, value_rows, preferred_element_type=jnp.float32
    )
    dscore = (attn_probs * (dprob - row_delta)).astype(jnp.bfloat16)
    query_grad = (
        jnp.einsum("qkgts,qskd->qtkgd", dscore, key_rows, preferred_element_type=jnp.float32)
        * softmax_scale
    ).astype(jnp.bfloat16)
    key_terms = (
        jnp.einsum("qkgts,qtkgd->qskd", dscore, query_rows, preferred_element_type=jnp.float32)
        * softmax_scale
    )
    value_terms = jnp.einsum(
        "qkgts,qtkgd->qskd", probs_low, grad_rows, preferred_element_type=jnp.float32
    )
    return (attended, query_grad, key_terms, value_terms)


def per_device(queries, key_states, value_states, block_lists, out_grad):
    shard_index = lax.axis_index("ctx")
    shard_count = lax.axis_size("ctx")
    key_local, value_local = (
        lax.all_to_all(key_states, "head", split_axis=1, concat_axis=0, tiled=True),
        lax.all_to_all(value_states, "head", split_axis=1, concat_axis=0, tiled=True),
    )
    tokens_here = queries.shape[0]
    blocks_here = tokens_here // BLK
    row_width = key_local.shape[1]
    head_count = row_width // HEAD_DIM
    flat_ids = block_lists.reshape(-1)
    owner_shard = flat_ids // blocks_here
    inner_index = flat_ids % blocks_here
    every_block = jnp.arange(shard_count * blocks_here, dtype=jnp.int32)
    block_hits = jnp.any(flat_ids[:, None] == every_block[None, :], axis=0).reshape(
        shard_count, blocks_here
    )
    needed = block_hits & (jnp.arange(shard_count) != shard_index)[:, None]
    slot_rank = jnp.cumsum(needed.astype(jnp.int32), axis=1) - 1
    slot_pick = needed[:, :, None] & (slot_rank[:, :, None] == jnp.arange(CAP)[None, None, :])
    requests = jnp.sum(
        jnp.where(slot_pick, jnp.arange(blocks_here, dtype=jnp.int32)[None, :, None], 0), axis=1
    )
    ref_rank = slot_rank[owner_shard, inner_index]
    is_local = owner_shard == shard_index
    source = jnp.where(is_local, inner_index, blocks_here + owner_shard * CAP + ref_rank)
    all_keys, all_values = (
        lax.all_gather(key_local, "ctx", axis=0, tiled=True),
        lax.all_gather(value_local, "ctx", axis=0, tiled=True),
    )
    asked_in = lax.all_to_all(requests, "ctx", split_axis=0, concat_axis=0, tiled=True)
    listed_keys = all_keys.reshape(-1, BLK, row_width)[flat_ids]
    listed_values = all_values.reshape(-1, BLK, row_width)[flat_ids]
    step_blocks = min(8, blocks_here)
    group_count = blocks_here // step_blocks
    key_rows = listed_keys.reshape(group_count, step_blocks, LIST * BLK, head_count, HEAD_DIM)
    value_rows = listed_values.reshape(group_count, step_blocks, LIST * BLK, head_count, HEAD_DIM)
    query_rows = queries.reshape(group_count, step_blocks, BLK, head_count, GROUP, HEAD_DIM)
    grad_rows = out_grad.reshape(group_count, step_blocks, BLK, head_count, GROUP, HEAD_DIM)
    offsets = jnp.arange(BLK, dtype=jnp.int32)
    key_pos = (block_lists[:, :, None] * BLK + offsets[None, None, :]).reshape(
        blocks_here, LIST * BLK
    )
    query_pos = (shard_index * blocks_here + jnp.arange(blocks_here, dtype=jnp.int32))[
        :, None
    ] * BLK + offsets[None, :]
    visible = (key_pos[:, None, :] <= query_pos[:, :, None]).reshape(
        group_count, step_blocks, BLK, LIST * BLK
    )
    attended, query_grad, key_terms, value_terms = lax.map(
        attend_group, (query_rows, grad_rows, key_rows, value_rows, visible)
    )
    ref_count = blocks_here * LIST
    dest_count = blocks_here + shard_count * CAP
    empty_dest = jnp.zeros((dest_count, BLK * row_width), jnp.float32)
    key_dest = empty_dest.at[source].add(key_terms.reshape(ref_count, BLK * row_width))
    value_dest = empty_dest.at[source].add(value_terms.reshape(ref_count, BLK * row_width))
    key_out = key_dest[blocks_here:].reshape(shard_count, CAP, BLK, row_width)
    value_out = value_dest[blocks_here:].reshape(shard_count, CAP, BLK, row_width)
    key_back, value_back = (
        lax.all_to_all(key_out, "ctx", split_axis=0, concat_axis=0, tiled=True),
        lax.all_to_all(value_out, "ctx", split_axis=0, concat_axis=0, tiled=True),
    )
    asked_flat = asked_in.reshape(-1)
    key_total = (
        key_dest[:blocks_here]
        .at[asked_flat]
        .add(key_back.reshape(shard_count * CAP, BLK * row_width))
    )
    value_total = (
        value_dest[:blocks_here]
        .at[asked_flat]
        .add(value_back.reshape(shard_count * CAP, BLK * row_width))
    )
    key_low = key_total.reshape(tokens_here, row_width).astype(jnp.bfloat16)
    value_low = value_total.reshape(tokens_here, row_width).astype(jnp.bfloat16)
    key_grad, value_grad = (
        lax.all_to_all(key_low, "head", split_axis=0, concat_axis=1, tiled=True),
        lax.all_to_all(value_low, "head", split_axis=0, concat_axis=1, tiled=True),
    )
    return (
        attended.reshape(tokens_here, -1),
        query_grad.reshape(tokens_here, -1),
        key_grad,
        value_grad,
    )


def solution(mesh):
    return jax.shard_map(
        per_device,
        mesh=mesh,
        in_specs=(
            P("ctx", "head"),
            P(("ctx", "head"), None),
            P(("ctx", "head"), None),
            P("ctx", None),
            P("ctx", "head"),
        ),
        out_specs=(
            P("ctx", "head"),
            P("ctx", "head"),
            P(("ctx", "head"), None),
            P(("ctx", "head"), None),
        ),
        check_vma=False,
    )
```

profile of v0, /device:TPU:0, one launch (start us, length us, event | category | flops | bytes accessed | tf_op | source)
XLA Modules:
  0.0 451.7 jit_solution(3616256248409031278)
XLA Ops:
  8.5 12.9 %all_to_all.89 = bf16[256,4,256]{0,2,1:T(8,128)(2,1)S(1)} all-to-all(bf16[256,4,256]{0,2,1:T(8,128)(2,1)S(1)} %bitcast.182), channel_id=1, replica_groups=mesh['head'=4,'ctx'=8] {'head'}, dimensions={1} | all-to-all | bytes 1048576 | tf_op jit(solution)/shard_map/all_to_all | solution.py:55
  23.7 11.2 %all_to_all.90 = bf16[256,4,256]{0,2,1:T(8,128)(2,1)S(1)} all-to-all(bf16[256,4,256]{0,2,1:T(8,128)(2,1)S(1)} %bitcast.183), channel_id=1, replica_groups=mesh['head'=4,'ctx'=8] {'head'}, dimensions={1} | all-to-all | bytes 1048576 | tf_op jit(solution)/shard_map/all_to_all | solution.py:56
  37.4 5.8 %all-to-all-start.2 = ((s32[8,1,3]{2,1,0:T(1,128)}), s32[8,1,3]{2,1,0:T(1,128)}, u32[]{:S(2)}, u32[]{:S(2)}) async-start(s32[8,1,3]{2,1,0:T(1,128)} %copy.81), calls=%async_computation.2 | async-start | bytes 8192 | tf_op jit(solution)/shard_map/all_to_all | solution.py:82
  44.7 3.2 reshape.381
  48.0 4.4 reshape.382
  54.2 42.2 %all-gather.5.cloned.1.call-done = bf16[8192,256]{1,0:T(8,128)(2,1)} async-done(((bf16[1024,256]{1,0:T(8,128)(2,1)}), bf16[8192,256]{1,0:T(8,128)(2,1)}) %all-gather.5.cloned.1.call-update) | async-done | bytes 4194320 | tf_op jit(solution)/shard_map/all_gather | solution.py:79
  96.3 4.9 %gather_fusion.1 = bf16[128,64,256]{2,1,0:T(8,128)(2,1)} fusion(bf16[128,64,256]{2,1,0:T(8,128)(2,1)} %bitcast.172, s32[1024]{0:T(1024)S(1)} %pad_clamp_fusion), kind=kCustom, calls=%fused_computation.1 | custom fusion | bytes 8389120 | tf_op jit(solution)/shard_map/gather | solution.py:83
  101.3 7.0 %reshape.380 = bf16[2,8,512,2,128]{4,3,2,1,0:T(2,128)(2,1)} reshape(bf16[128,64,256]{2,1,0:T(8,128)(2,1)} %gather_fusion.1) | data formatting | bytes 8388608 | tf_op jit(solution)/shard_map/reshape | solution.py:87
  108.3 62.5 %all-gather.3.cloned.1.call-done = bf16[8192,256]{1,0:T(8,128)(2,1)} async-done(((bf16[1024,256]{1,0:T(8,128)(2,1)}), bf16[8192,256]{1,0:T(8,128)(2,1)}) %all-gather.3.cloned.1.call-update) | async-done | bytes 4194320 | tf_op jit(solution)/shard_map/all_gather | solution.py:80
  170.7 5.0 %gather_fusion = bf16[128,64,256]{2,1,0:T(8,128)(2,1)} fusion(bf16[128,64,256]{2,1,0:T(8,128)(2,1)} %bitcast.173, s32[1024]{0:T(1024)S(1)} %pad_clamp_fusion), kind=kCustom, calls=%fused_computation | custom fusion | bytes 8389120 | tf_op jit(solution)/shard_map/gather | solution.py:84
  175.7 6.9 %reshape.378 = bf16[2,8,512,2,128]{4,3,2,1,0:T(2,128)(2,1)} reshape(bf16[128,64,256]{2,1,0:T(8,128)(2,1)} %gather_fusion) | data formatting | bytes 8388608 | tf_op jit(solution)/shard_map/reshape | solution.py:88
  182.6 127.9 %while.16 = (s32[]{:T(128)}, bf16[2,8,64,2,4,128]{5,4,3,2,1,0:T(4,128)(2,1)}, bf16[2,8,64,2,4,128]{5,4,3,2,1,0:T(4,128)(2,1)}, f32[2,8,512,2,128]{4,3,2,1,0:T(2,...) while((s32[]{:T(128)}, ...), condition=%wide.region_4.5_spmd, body=%wide.region_0.4_spmd.sunk | while | flops 3251106304 | bytes 264061392 | solution.py:101
  189.8 4.5 fusion.51
  194.3 9.3 %fusion.52 = (f32[8,2,4,64]{3,2,1,0:T(4,128)S(1)}, f32[8,2,4,64,512]{4,3,2,1,0:T(8,128)S(1)}) fusion(f32[8,2,512,64,4]{2,3,4,1,0:T(8,128)} %fusion.51, pred[8,64,512]{2,1,0:T(8,128)(4,1)S(1)} %dynamic-slice_bitcast_fusion.2), kind=kOutput, calls=%fused_computation.84.clone.1 | output fusion | flops 12583423 | bytes 17055744 | tf_op jit(solution)/shard_map/while/body/eval_jaxpr/sub | solution.py:25
  204.5 2.4 copy-done.1
  209.2 2.8 convolution_bitcast_fusion.2
  211.9 7.2 %copy.153 = f32[1,8,512,2,128]{4,3,2,1,0:T(2,128)} copy(f32[1,8,512,2,128]{2,4,3,1,0:T(8,128)} %convolution_bitcast_fusion.2) | data formatting | bytes 8388608 | tf_op jit(solution)/shard_map/while/body/jit(dynamic_update_index_in_dim)/dynamic_update_slice | solution.py:101
  219.2 5.6 %fusion.54 = bf16[8,2,4,64,512]{4,3,2,1,0:T(8,128)(2,1)S(1)} fusion(f32[8,2,4,64]{3,2,1,0:T(4,128)S(1)} %bitcast.185, f32[8,2,4,64,512]{4,3,2,1,0:T(8,128)} %copy-done.1, f32[8,2,4,64]{3,2,1,0:T(4,128)S(1)} %get-tuple-element.219, bf16[1,8,512,2,128]{4,3,2,1,0:T(2,128)(2,1)} %copy-done.5, bf16[1,8,64,2,4,128]{5,4,3,2,1,0:T(4,128)(2,1)} %copy-done.3), kind=kOutput, calls=%fused_computation.10.clone.1 | convolution fusion | flops 545259520 | bytes 15761408 | tf_op jit(solution)/shard_map/while/body/eval_jaxpr/qtkgd,qskd->qkgts/dot_general | solution.py:33
  227.0 2.9 fusion.56
  229.9 7.3 %copy.154 = f32[1,8,512,2,128]{4,3,2,1,0:T(2,128)} copy(f32[1,8,512,2,128]{2,4,3,1,0:T(8,128)} %fusion.56) | data formatting | bytes 8388608 | tf_op jit(solution)/shard_map/while/body/jit(dynamic_update_index_in_dim)/dynamic_update_slice | solution.py:101
  237.2 3.1 copy_dynamic-update-slice_fusion.3
  240.3 6.2 %constant_dynamic-update-slice_fusion.3 = (f32[2,8,512,2,128]{4,3,2,1,0:T(2,128)}, f32[2,8,512,2,128]{4,3,2,1,0:T(2,128)}) fusion(f32[2,8,512,2,128]{4,3,2,1,0:T(2,128)} %get-tuple-element.241, f32[1,8,512,2,128]{4,3,2,1,0:T(2,128)S(1)} %copy-done, s32[]{:T(128)S(6)} %copy.164, f32[2,8,512,2,128]{4,3,2,1,0:T(2,128)} %get-tuple-element.240, ...), kind=kLoop, calls=%fused_computation.36.clone.1 | loop fusion | bytes 16777220 | tf_op jit(solution)/shard_map/while/body/jit(dynamic_update_index_in_dim)/dynamic_update_slice | solution.py:101
  253.5 4.5 fusion.51
  258.0 9.3 %fusion.52 = (f32[8,2,4,64]{3,2,1,0:T(4,128)S(1)}, f32[8,2,4,64,512]{4,3,2,1,0:T(8,128)S(1)}) fusion(f32[8,2,512,64,4]{2,3,4,1,0:T(8,128)} %fusion.51, pred[8,64,512]{2,1,0:T(8,128)(4,1)S(1)} %dynamic-slice_bitcast_fusion.2), kind=kOutput, calls=%fused_computation.84.clone.1 | output fusion | flops 12583423 | bytes 17055744 | tf_op jit(solution)/shard_map/while/body/eval_jaxpr/sub | solution.py:25
  272.8 2.8 convolution_bitcast_fusion.2
  275.6 7.2 %copy.153 = f32[1,8,512,2,128]{4,3,2,1,0:T(2,128)} copy(f32[1,8,512,2,128]{2,4,3,1,0:T(8,128)} %convolution_bitcast_fusion.2) | data formatting | bytes 8388608 | tf_op jit(solution)/shard_map/while/body/jit(dynamic_update_index_in_dim)/dynamic_update_slice | solution.py:101
  282.8 5.6 %fusion.54 = bf16[8,2,4,64,512]{4,3,2,1,0:T(8,128)(2,1)S(1)} fusion(f32[8,2,4,64]{3,2,1,0:T(4,128)S(1)} %bitcast.185, f32[8,2,4,64,512]{4,3,2,1,0:T(8,128)} %copy-done.1, f32[8,2,4,64]{3,2,1,0:T(4,128)S(1)} %get-tuple-element.219, bf16[1,8,512,2,128]{4,3,2,1,0:T(2,128)(2,1)} %copy-done.5, bf16[1,8,64,2,4,128]{5,4,3,2,1,0:T(4,128)(2,1)} %copy-done.3), kind=kOutput, calls=%fused_computation.10.clone.1 | convolution fusion | flops 545259520 | bytes 15761408 | tf_op jit(solution)/shard_map/while/body/eval_jaxpr/qtkgd,qskd->qkgts/dot_general | solution.py:33
  290.7 2.9 fusion.56
  293.5 7.3 %copy.154 = f32[1,8,512,2,128]{4,3,2,1,0:T(2,128)} copy(f32[1,8,512,2,128]{2,4,3,1,0:T(8,128)} %fusion.56) | data formatting | bytes 8388608 | tf_op jit(solution)/shard_map/while/body/jit(dynamic_update_index_in_dim)/dynamic_update_slice | solution.py:101
  300.9 3.1 copy_dynamic-update-slice_fusion.3
  303.9 6.2 %constant_dynamic-update-slice_fusion.3 = (f32[2,8,512,2,128]{4,3,2,1,0:T(2,128)}, f32[2,8,512,2,128]{4,3,2,1,0:T(2,128)}) fusion(f32[2,8,512,2,128]{4,3,2,1,0:T(2,128)} %get-tuple-element.241, f32[1,8,512,2,128]{4,3,2,1,0:T(2,128)S(1)} %copy-done, s32[]{:T(128)S(6)} %copy.164, f32[2,8,512,2,128]{4,3,2,1,0:T(2,128)} %get-tuple-element.240, ...), kind=kLoop, calls=%fused_computation.36.clone.1 | loop fusion | bytes 16777220 | tf_op jit(solution)/shard_map/while/body/jit(dynamic_update_index_in_dim)/dynamic_update_slice | solution.py:101
  310.5 11.5 %reshape.435 = f32[128,16384]{1,0:T(8,128)} reshape(f32[2,8,512,2,128]{4,3,2,1,0:T(2,128)} %get-tuple-element.62) | data formatting | bytes 16777216 | tf_op jit(solution)/shard_map/reshape | solution.py:108
  322.1 13.2 %scatter_custom_fusion.2 = f32[40,16384]{1,0:T(8,128)S(1)} fusion(s32[128]{0:T(128)} %fusion.30, f32[128,16384]{1,0:T(8,128)} %reshape.435, f32[]{:T(128)} %constant.77.clone.1), kind=kCustom, calls=%fused_computation.44 | custom fusion | flops 2097152 | bytes 2621952 | tf_op jit(solution)/shard_map/scatter-add | solution.py:108
  337.2 4.5 all-to-all-start.5
  341.7 11.5 %reshape.419 = f32[128,16384]{1,0:T(8,128)} reshape(f32[2,8,512,2,128]{4,3,2,1,0:T(2,128)} %get-tuple-element.61) | data formatting | bytes 16777216 | tf_op jit(solution)/shard_map/reshape | solution.py:107
  353.2 13.2 %scatter_custom_fusion = f32[40,16384]{1,0:T(8,128)S(1)} fusion(s32[128]{0:T(128)} %fusion.30, f32[128,16384]{1,0:T(8,128)} %reshape.419, f32[]{:T(128)} %constant.77.clone.1), kind=kCustom, calls=%fused_computation.46 | custom fusion | flops 2097152 | bytes 2621952 | tf_op jit(solution)/shard_map/scatter-add | solution.py:107
  368.4 9.5 %all-to-all-done.5 = f32[8,3,64,256]{3,2,1,0:T(8,128)} async-done(((f32[8,3,64,256]{3,2,1,0:T(8,128)}), f32[8,3,64,256]{3,2,1,0:T(8,128)}, u32[]{:S(2)}, u32[]{:S(2)}) %all-to-all-start.5) | async-done | bytes 1572896 | tf_op jit(solution)/shard_map/all_to_all | solution.py:113
  377.8 4.5 all-to-all-start.3
  386.6 3.5 copy.106
  390.1 5.3 %scatter_fusion.1 = f32[16,16384]{1,0:T(8,128)} fusion(f32[16,16384]{1,0:T(8,128)} %slice.24, s32[24]{0:T(128)S(1)} %fusion.28, f32[24,16384]{1,0:T(8,128)} %bitcast.169), kind=kCustom, calls=%fused_computation.6 | custom fusion | flops 393216 | bytes 4718688 | tf_op jit(solution)/shard_map/scatter-add | solution.py:124
  397.7 21.1 %all-to-all-done.3 = f32[8,3,64,256]{3,2,1,0:T(8,128)} async-done(((f32[8,3,64,256]{3,2,1,0:T(8,128)}), f32[8,3,64,256]{3,2,1,0:T(8,128)}, u32[]{:S(2)}, u32[]{:S(2)}) %all-to-all-start.3) | async-done | bytes 1572896 | tf_op jit(solution)/shard_map/all_to_all | solution.py:112
  418.9 3.5 all-to-all-start.6
  422.4 2.4 copy.104
  424.8 2.7 scatter_fusion
  428.6 2.6 all-to-all-done.6
  431.1 3.5 all-to-all-start.4
  434.6 4.4 reshape.383
  439.1 2.7 reshape.384
  (121 shorter events, 50.7 us)
Async XLA Ops:
  7.2 28.8 %copy-start.13 = (s32[16,8]{0,1:T(8,128)S(1)}, s32[16,8]{0,1:T(8,128)}, u32[]{:S(2)}) copy-start(s32[16,8]{0,1:T(8,128)} %param.10) | copy-start | bytes 1540
  7.2 89.2 %all-gather.5.cloned.1.call-start = ((), (), s32[]{:S(2)}) async-start(), calls=%async_computation.8 | async-start | bytes 4718592 | tf_op jit(solution)/shard_map/all_gather | solution.py:79
  22.4 148.3 %all-gather.3.cloned.1.call-start = ((), (), s32[]{:S(2)}) async-start(), calls=%async_computation.7 | async-start | bytes 4718592 | tf_op jit(solution)/shard_map/all_gather | solution.py:80
  37.4 299.8 %all-to-all-start.2 = ((s32[8,1,3]{2,1,0:T(1,128)}), s32[8,1,3]{2,1,0:T(1,128)}, u32[]{:S(2)}, u32[]{:S(2)}) async-start(s32[8,1,3]{2,1,0:T(1,128)} %copy.81), calls=%async_computation.2 | async-start | bytes 8192 | tf_op jit(solution)/shard_map/all_to_all | solution.py:82
  182.8 3.7 copy-start.9
  182.8 4.1 copy-start.6
  184.1 4.2 copy-start.7
  186.5 22.7 %copy-start.3 = (bf16[1,8,64,2,4,128]{5,4,3,2,1,0:T(4,128)(2,1)}, bf16[1,8,64,2,4,128]{5,4,3,2,1,0:T(4,128)(2,1)S(1)}, u32[]{:S(2)}) copy-start(bf16[1,8,64,2,4,128]{5,4,3,2,1,0:T(4,128)(2,1)S(1)} %constant_dynamic-slice_fusion.8) | copy-start | bytes 3145732 | tf_op jit(solution)/shard_map/while
  189.8 14.7 %copy-start.5 = (bf16[1,8,512,2,128]{4,3,2,1,0:T(2,128)(2,1)}, bf16[1,8,512,2,128]{4,3,2,1,0:T(2,128)(2,1)S(1)}, u32[]{:S(2)}) copy-start(bf16[1,8,512,2,128]{4,3,2,1,0:T(2,128)(2,1)S(1)} %constant_dynamic-slice_fusion.11) | copy-start | bytes 6291460 | tf_op jit(solution)/shard_map/while
  203.7 3.2 copy-start.1
  229.9 7.3 %copy-start.4 = (bf16[1,8,64,2,4,128]{5,2,4,3,1,0:T(8,128)(2,1)S(1)}, bf16[1,8,64,2,4,128]{5,2,4,3,1,0:T(8,128)(2,1)}, u32[]{:S(2)}) copy-start(bf16[1,8,64,2,4,128]{5,2,4,3,1,0:T(8,128)(2,1)} %fusion.55) | copy-start | bytes 3145732 | tf_op jit(solution)/shard_map/while
  229.9 7.3 %copy-start.8 = (bf16[8,2,128,4,64]{2,4,3,1,0:T(8,128)(2,1)S(1)}, bf16[8,2,128,4,64]{2,4,3,1,0:T(8,128)(2,1)}, u32[]{:S(2)}) copy-start(bf16[8,2,128,4,64]{2,4,3,1,0:T(8,128)(2,1)} %get-tuple-element.221) | copy-start | bytes 3145732 | tf_op jit(solution)/shard_map/while
  237.2 3.1 copy-start
  240.3 6.2 %copy-start.10 = (bf16[2,8,64,2,4,128]{5,4,3,2,1,0:T(4,128)(2,1)S(1)}, bf16[2,8,64,2,4,128]{5,4,3,2,1,0:T(4,128)(2,1)}, u32[]{:S(2)}) copy-start(bf16[2,8,64,2,4,128]{5,4,3,2,1,0:T(4,128)(2,1)} %copy-done.9) | copy-start | bytes 6291460 | tf_op jit(solution)/shard_map/while
  246.5 3.7 copy-start.9
  246.5 4.1 copy-start.6
  247.8 4.2 copy-start.7
  250.2 22.7 %copy-start.3 = (bf16[1,8,64,2,4,128]{5,4,3,2,1,0:T(4,128)(2,1)}, bf16[1,8,64,2,4,128]{5,4,3,2,1,0:T(4,128)(2,1)S(1)}, u32[]{:S(2)}) copy-start(bf16[1,8,64,2,4,128]{5,4,3,2,1,0:T(4,128)(2,1)S(1)} %constant_dynamic-slice_fusion.8) | copy-start | bytes 3145732 | tf_op jit(solution)/shard_map/while
  253.5 14.7 %copy-start.5 = (bf16[1,8,512,2,128]{4,3,2,1,0:T(2,128)(2,1)}, bf16[1,8,512,2,128]{4,3,2,1,0:T(2,128)(2,1)S(1)}, u32[]{:S(2)}) copy-start(bf16[1,8,512,2,128]{4,3,2,1,0:T(2,128)(2,1)S(1)} %constant_dynamic-slice_fusion.11) | copy-start | bytes 6291460 | tf_op jit(solution)/shard_map/while
  267.3 3.2 copy-start.1
  293.5 7.3 %copy-start.4 = (bf16[1,8,64,2,4,128]{5,2,4,3,1,0:T(8,128)(2,1)S(1)}, bf16[1,8,64,2,4,128]{5,2,4,3,1,0:T(8,128)(2,1)}, u32[]{:S(2)}) copy-start(bf16[1,8,64,2,4,128]{5,2,4,3,1,0:T(8,128)(2,1)} %fusion.55) | copy-start | bytes 3145732 | tf_op jit(solution)/shard_map/while
  293.5 7.3 %copy-start.8 = (bf16[8,2,128,4,64]{2,4,3,1,0:T(8,128)(2,1)S(1)}, bf16[8,2,128,4,64]{2,4,3,1,0:T(8,128)(2,1)}, u32[]{:S(2)}) copy-start(bf16[8,2,128,4,64]{2,4,3,1,0:T(8,128)(2,1)} %get-tuple-element.221) | copy-start | bytes 3145732 | tf_op jit(solution)/shard_map/while
  300.9 3.1 copy-start
  303.9 6.2 %copy-start.10 = (bf16[2,8,64,2,4,128]{5,4,3,2,1,0:T(4,128)(2,1)S(1)}, bf16[2,8,64,2,4,128]{5,4,3,2,1,0:T(4,128)(2,1)}, u32[]{:S(2)}) copy-start(bf16[2,8,64,2,4,128]{5,4,3,2,1,0:T(4,128)(2,1)} %copy-done.9) | copy-start | bytes 6291460 | tf_op jit(solution)/shard_map/while
  335.2 2.0 copy-start.11
  337.2 40.6 %all-to-all-start.5 = ((f32[8,3,64,256]{3,2,1,0:T(8,128)}), f32[8,3,64,256]{3,2,1,0:T(8,128)}, u32[]{:S(2)}, u32[]{:S(2)}) async-start(f32[8,3,64,256]{3,2,1,0:T(8,128)} %bitcast.167), calls=%async_computation.5 | async-start | bytes 3145728 | tf_op jit(solution)/shard_map/all_to_all | solution.py:113
  366.4 56.0 %copy-start.2 = (f32[40,16384]{1,0:T(8,128)}, f32[40,16384]{1,0:T(8,128)S(1)}, u32[]{:S(2)}) copy-start(f32[40,16384]{1,0:T(8,128)S(1)} %scatter_custom_fusion) | copy-start | bytes 7864324
  377.8 41.0 %all-to-all-start.3 = ((f32[8,3,64,256]{3,2,1,0:T(8,128)}), f32[8,3,64,256]{3,2,1,0:T(8,128)}, u32[]{:S(2)}, u32[]{:S(2)}) async-start(f32[8,3,64,256]{3,2,1,0:T(8,128)} %bitcast.166), calls=%async_computation.3 | async-start | bytes 3145728 | tf_op jit(solution)/shard_map/all_to_all | solution.py:112
  418.9 12.3 %all-to-all-start.6 = ((bf16[4,256,256]{2,1,0:T(8,128)(2,1)}), bf16[4,256,256]{2,1,0:T(8,128)(2,1)S(1)}, u32[]{:S(2)}, u32[]{:S(2)}) async-start(bf16[4,256,256]{2,1,0:T(8,128)(2,1)} %convert_element_type.45), calls=%async_computation.6 | async-start | bytes 1048576 | tf_op jit(solution)/shard_map/all_to_all | solution.py:130
  422.3 2.4 slice-start
  428.6 10.5 %copy-start.12 = (bf16[2,8,64,2,4,128]{5,4,3,2,1,0:T(4,128)(2,1)S(1)}, bf16[2,8,64,2,4,128]{5,4,3,2,1,0:T(4,128)(2,1)}, u32[]{:S(2)}) copy-start(bf16[2,8,64,2,4,128]{5,4,3,2,1,0:T(4,128)(2,1)} %get-tuple-element.60) | copy-start | bytes 6291460
  431.1 12.3 %all-to-all-start.4 = ((bf16[4,256,256]{2,1,0:T(8,128)(2,1)}), bf16[4,256,256]{2,1,0:T(8,128)(2,1)S(1)}, u32[]{:S(2)}, u32[]{:S(2)}) async-start(bf16[4,256,256]{2,1,0:T(8,128)(2,1)} %convert_element_type.43), calls=%async_computation.4 | async-start | bytes 1048576 | tf_op jit(solution)/shard_map/all_to_all | solution.py:129
Sparse Core Ops, SparseCore 0:
  22.5 73.7 all-gather.4
  99.0 71.6 all-gather.2
where the time goes:
time: 457 us; the launch traced here: 452 us
  local copies, waits for them, and re-layouts  152 us (33%)
  waiting for transfers between devices  138 us (30%)
  other arithmetic  59.7 us (13%)
  matrix products  40.4 us (9%)
  blocking collectives  24.1 us (5%)
  starting transfers between devices  21.8 us (5%)
  between operations  14.5 us (3%)
    all_gather x1, waiting for transfers between devices, per_device(): lax.all_gather(value_local, 'ctx', axis=0, tiled=True)  62.5 us
    dynamic_update_slice x8, local copies, waits for them, and re-layouts, per_device(): lax.map(attend_group, (query_rows, grad_rows, key_rows, value_rows, visib...  47.6 us
    all_gather x1, waiting for transfers between devices, per_device(): lax.all_gather(key_local, 'ctx', axis=0, tiled=True)  42.2 us
    all_to_all x1, waiting for transfers between devices, per_device(): lax.all_to_all(key_out, 'ctx', split_axis=0, concat_axis=0, tiled=True)  21.1 us
    sub x2, other arithmetic, attend_group(): expo = jnp.exp(scores - row_peak)  18.7 us
    unnamed x17, local copies, waits for them, and re-layouts  14.2 us
    scatter-add x1, other arithmetic, per_device(): empty_dest.at[source].add(value_terms.reshape(ref_count, BLK * row_width))  13.2 us
    scatter-add x1, other arithmetic, per_device(): empty_dest.at[source].add(key_terms.reshape(ref_count, BLK * row_width))  13.2 us
  transfers between devices with their start and end apart: 7, of which 6 were waited for; matrix products, arithmetic and copies ran while one was open for 54% of the time, Pallas kernels for 0%

commit v1 on v0

v1 whole, which is shorter than its diff:
```python
import functools

import jax
import jax.numpy as jnp
from jax import lax
from jax.experimental import pallas as pl
from jax.experimental.pallas import tpu as pltpu
from jax.sharding import PartitionSpec as P

HEAD_DIM = 128
GROUP = 4
BLK = 64
LIST = 8
CAP = 3
STEP_BLOCKS = 2
NEG_FILL = -1e30
SCALE = HEAD_DIM ** (-0.5)
LOG2E = 1.4426950408889634
VMEM_LIMIT = 50 * 1024 * 1024

NT = (((1,), (1,)), ((), ()))
NN = (((1,), (0,)), ((), ()))
TN = (((0,), (0,)), ((), ()))


def dot(a, b, dims):
    return lax.dot_general(a, b, dims, preferred_element_type=jnp.float32)


def params(**kw):
    return pltpu.CompilerParams(vmem_limit_bytes=VMEM_LIMIT, **kw)


def pick_kernel(asked, own, out):
    per_quarter = own.shape[2] // BLK
    for c in range(out.shape[0]):
        for s in range(CAP):
            block = asked[c * CAP + s]
            quarter = block // per_quarter
            row = pl.multiple_of((block % per_quarter) * BLK, BLK)
            for kv in range(2):
                out[c, kv, s] = own[quarter, kv, pl.ds(row, BLK), :]


def attend_kernel(source, q_ref, g_ref, own, far, *rest):
    o_ref, dq_ref, near_out, far_out, table, total = rest[-6:]
    step = pl.program_id(0)
    heads, _, quarter_rows, _ = own.shape
    per_quarter = quarter_rows // BLK
    blocks_here = heads * per_quarter
    shard_count = far.shape[0]

    @pl.when(step == 0)
    def _():
        for kv in range(2):
            for quarter in range(heads):
                for j in range(per_quarter):
                    table[kv, quarter * per_quarter + j] = own[quarter, kv, j * BLK : (j + 1) * BLK, :]
            for c in range(shard_count):
                for s in range(CAP):
                    table[kv, blocks_here + c * CAP + s] = far[c, kv, s]
        total[...] = jnp.zeros_like(total)

    key_row = lax.broadcasted_iota(jnp.int32, (BLK, GROUP * BLK), 0)
    query_col = lax.broadcasted_iota(jnp.int32, (BLK, GROUP * BLK), 1) % BLK
    hidden = key_row > query_col
    for sub in range(STEP_BLOCKS):
        block = step * STEP_BLOCKS + sub
        rows = slice(sub * BLK, (sub + 1) * BLK)
        listed = [source[block * LIST + e] for e in range(LIST)]
        q = jnp.concatenate([q_ref[rows, g * HEAD_DIM : (g + 1) * HEAD_DIM] for g in range(GROUP)], axis=0)
        g_out = jnp.concatenate([g_ref[rows, g * HEAD_DIM : (g + 1) * HEAD_DIM] for g in range(GROUP)], axis=0)
        keys = jnp.concatenate([table[0, at] for at in listed], axis=0)
        values = jnp.concatenate([table[1, at] for at in listed], axis=0)
        scores = dot(keys, q, NT)
        parts = []
        for e in range(LIST):
            part = scores[e * BLK : (e + 1) * BLK]
            mask = hidden if e == 0 else hidden & (listed[e] == block)
            parts.append(jnp.where(mask, NEG_FILL, part))
        scores = jnp.concatenate(parts, axis=0)
        peak = jnp.max(scores, axis=0, keepdims=True)
        expo = jnp.exp2((scores - peak) * (SCALE * LOG2E))
        probs = expo * (1.0 / jnp.sum(expo, axis=0, keepdims=True))
        probs_low = probs.astype(jnp.bfloat16)
        dprob = dot(values, g_out, NT)
        delta = jnp.sum(probs * dprob, axis=0, keepdims=True)
        dscore = (probs * (dprob - delta)).astype(jnp.bfloat16)
        attended = dot(values, probs_low, TN).T.astype(jnp.bfloat16)
        dq = (dot(keys, dscore, TN) * SCALE).T.astype(jnp.bfloat16)
        for g in range(GROUP):
            cols = slice(g * HEAD_DIM, (g + 1) * HEAD_DIM)
            o_ref[rows, cols] = attended[g * BLK : (g + 1) * BLK]
            dq_ref[rows, cols] = dq[g * BLK : (g + 1) * BLK]
        dk = dot(dscore, q, NN)
        dv = dot(probs_low, g_out, NN)
        for e in range(LIST):
            total[0, listed[e]] += dk[e * BLK : (e + 1) * BLK]
            total[1, listed[e]] += dv[e * BLK : (e + 1) * BLK]

    @pl.when(step == pl.num_programs(0) - 1)
    def _():
        for kv, factor in ((0, SCALE), (1, 1.0)):
            near_out[kv] = total[kv, :blocks_here] * factor
            for c in range(shard_count):
                first = blocks_here + c * CAP
                far_out[c, kv] = (total[kv, first : first + CAP] * factor).astype(jnp.bfloat16)


def gather_sum_kernel(asked, near, back, out, total):
    heads, _, quarter_rows, _ = out.shape
    per_quarter = quarter_rows // BLK
    total[...] = near[...]
    for c in range(back.shape[0]):
        for s in range(CAP):
            block = asked[c * CAP + s]
            for kv in range(2):
                total[kv, block] += back[c, kv, s].astype(jnp.float32)
    for quarter in range(heads):
        for kv in range(2):
            for j in range(per_quarter):
                out[quarter, kv, j * BLK : (j + 1) * BLK, :] = total[kv, quarter * per_quarter + j].astype(jnp.bfloat16)


def whole(shape):
    return pl.BlockSpec(shape, lambda *_: (0,) * len(shape))


def pick(asked, own, shard_count):
    shape = (shard_count, 2, CAP, BLK, HEAD_DIM)
    return pl.pallas_call(
        pick_kernel,
        grid_spec=pltpu.PrefetchScalarGridSpec(
            num_scalar_prefetch=1, grid=(1,), in_specs=[whole(own.shape)], out_specs=whole(shape)
        ),
        out_shape=jax.ShapeDtypeStruct(shape, jnp.bfloat16),
        compiler_params=params(),
        name="pick",
    )(asked, own)


def attend(source, queries, out_grad, own, far, head, earlier):
    tokens_here, width = queries.shape
    blocks_here = tokens_here // BLK
    slots = blocks_here + far.shape[0] * CAP
    tile = pl.BlockSpec((STEP_BLOCKS * BLK, GROUP * HEAD_DIM), lambda i, *_: (i, head))
    near_shape = (2, blocks_here, BLK, HEAD_DIM)
    aliases = {5: 0, 6: 1} if earlier else {}
    return pl.pallas_call(
        attend_kernel,
        grid_spec=pltpu.PrefetchScalarGridSpec(
            num_scalar_prefetch=1,
            grid=(blocks_here // STEP_BLOCKS,),
            in_specs=[tile, tile, whole(own.shape), whole(far.shape)]
            + [pl.BlockSpec(memory_space=pl.ANY)] * len(earlier),
            out_specs=[tile, tile, whole(near_shape), whole(far.shape)],
            scratch_shapes=[
                pltpu.VMEM((2, slots, BLK, HEAD_DIM), jnp.bfloat16),
                pltpu.VMEM((2, slots, BLK, HEAD_DIM), jnp.float32),
            ],
        ),
        out_shape=[
            jax.ShapeDtypeStruct((tokens_here, width), jnp.bfloat16),
            jax.ShapeDtypeStruct((tokens_here, width), jnp.bfloat16),
            jax.ShapeDtypeStruct(near_shape, jnp.float32),
            jax.ShapeDtypeStruct(far.shape, jnp.bfloat16),
        ],
        input_output_aliases=aliases,
        compiler_params=params(),
        cost_estimate=pl.CostEstimate(
            flops=12 * blocks_here * LIST * BLK * GROUP * BLK * HEAD_DIM,
            bytes_accessed=20 * 1024 * 1024,
            transcendentals=blocks_here * LIST * BLK * GROUP * BLK,
        ),
        name="attend",
    )(source, queries, out_grad, own, far, *earlier)


def gather_sum(asked, near, back, shape):
    return pl.pallas_call(
        gather_sum_kernel,
        grid_spec=pltpu.PrefetchScalarGridSpec(
            num_scalar_prefetch=1,
            grid=(1,),
            in_specs=[whole(near.shape), whole(back.shape)],
            out_specs=whole(shape),
            scratch_shapes=[pltpu.VMEM(near.shape, jnp.float32)],
        ),
        out_shape=jax.ShapeDtypeStruct(shape, jnp.bfloat16),
        compiler_params=params(),
        name="gather_sum",
    )(asked, near, back)


def swap(x, axis):
    return lax.all_to_all(x, axis, split_axis=0, concat_axis=0, tiled=True)


def per_device(queries, key_states, value_states, block_lists, out_grad):
    shard_index = lax.axis_index("ctx")
    shard_count = lax.axis_size("ctx")
    heads = lax.axis_size("head")
    tokens_here = queries.shape[0]
    blocks_here = tokens_here // BLK
    quarter = key_states.shape[0]
    head_count = key_states.shape[1] // heads // HEAD_DIM

    flat_ids = block_lists.reshape(-1)
    owner_shard = flat_ids // blocks_here
    inner_index = flat_ids % blocks_here
    every_block = jnp.arange(shard_count * blocks_here, dtype=jnp.int32)
    block_hits = jnp.any(flat_ids[:, None] == every_block[None, :], axis=0).reshape(shard_count, blocks_here)
    needed = block_hits & (jnp.arange(shard_count) != shard_index)[:, None]
    slot_rank = jnp.cumsum(needed.astype(jnp.int32), axis=1) - 1
    slot_pick = needed[:, :, None] & (slot_rank[:, :, None] == jnp.arange(CAP)[None, None, :])
    requests = jnp.sum(jnp.where(slot_pick, jnp.arange(blocks_here, dtype=jnp.int32)[None, :, None], 0), axis=1)
    ref_rank = jnp.sum(
        jnp.where(flat_ids[:, None] == every_block[None, :], slot_rank.reshape(-1)[None, :], 0), axis=1
    )
    source = jnp.where(owner_shard == shard_index, inner_index, blocks_here + owner_shard * CAP + ref_rank)
    asked = swap(requests, "ctx").reshape(-1)

    key_parts = key_states.reshape(quarter, heads, head_count, HEAD_DIM)
    value_parts = value_states.reshape(quarter, heads, head_count, HEAD_DIM)
    both = jnp.stack([key_parts, value_parts])
    own, far = [], []
    for h in range(head_count):
        own.append(swap(jnp.transpose(both[:, :, :, h], (2, 0, 1, 3)), "head"))
    for h in range(head_count):
        far.append(swap(pick(asked, own[h], shard_count), "ctx"))
    earlier, nears, backs = [], [], []
    for h in range(head_count):
        attended, query_grad, near, far_grad = attend(source, queries, out_grad, own[h], far[h], h, earlier)
        earlier = [attended, query_grad]
        nears.append(near)
        backs.append(swap(far_grad, "ctx"))
    done = []
    for h in range(head_count):
        done.append(swap(gather_sum(asked, nears[h], backs[h], own[h].shape), "head"))
    grads = jnp.stack(done)
    key_grad = jnp.transpose(grads[:, :, 0], (2, 1, 0, 3)).reshape(quarter, -1)
    value_grad = jnp.transpose(grads[:, :, 1], (2, 1, 0, 3)).reshape(quarter, -1)
    return attended, query_grad, key_grad, value_grad


def solution(mesh):
    return jax.shard_map(
        per_device,
        mesh=mesh,
        in_specs=(
            P("ctx", "head"),
            P(("ctx", "head"), None),
            P(("ctx", "head"), None),
            P("ctx", None),
            P("ctx", "head"),
        ),
        out_specs=(
            P("ctx", "head"),
            P("ctx", "head"),
            P(("ctx", "head"), None),
            P(("ctx", "head"), None),
        ),
        check_vma=False,
    )
```

time: 457 us -> 163 us (0.36)
  local copies, waits for them, and re-layouts: 152 us -> 11.9 us
  waiting for transfers between devices: 138 us -> 58.7 us
  other arithmetic: 59.7 us -> 2.35 us
  matrix products: 40.4 us -> 0 us
  Pallas kernels: 0 us -> 37 us
  between operations: 14.5 us -> 0.8 us
  starting transfers between devices: 21.8 us -> 28.5 us
    all_gather x2 -> x0, waiting for transfers between devices: 105 us -> none  [the longest x1 62.5 us: per_device(): lax.all_gather(value_local, 'ctx', axis=0, tiled=True)]
    reshape x9 -> x1, local copies, waits for them, and re-layouts: 51.8 us -> 0.08 us  [per_device(): asked = swap(requests, 'ctx').reshape(-1)]
    dynamic_update_slice x8 -> x0, local copies, waits for them, and re-layouts: 47.6 us -> none  [per_device(): lax.map(attend_group, (query_rows, grad_rows, key_rows, value_rows, visib...]
    dot_general x12 -> x0, matrix products: 40.4 us -> none  [the longest x2 11.2 us: attend_group(): jnp.einsum('qtkgd,qskd->qkgts', grad_rows, value_rows, preferred_element_...]
    pallas_call x0 -> x6, Pallas kernels: none -> 37 us  [the longest x2 31.2 us: attend(): pl.pallas_call(attend_kernel, grid_spec=pltpu.PrefetchScalarGridSpec(num_...]
    scatter-add x4 -> x0, other arithmetic: 34.4 us -> none  [the longest x1 13.2 us: per_device(): empty_dest.at[source].add(value_terms.reshape(ref_count, BLK * row_width))]
    all_to_all x5 -> x7, waiting for transfers between devices: 33.6 us -> 58.7 us  [swap(): return lax.all_to_all(x, axis, split_axis=0, concat_axis=0, tiled=True)]
    sub x2 -> x0, other arithmetic: 18.7 us -> none  [attend_group(): expo = jnp.exp(scores - row_peak)]
  transfers between devices with their start and end apart: 7 -> 7, of which waited for: 6 -> 7; matrix products, arithmetic and copies ran while one was open for 54% -> 3% of each run, Pallas kernels for 0% -> 23%
where the time goes in v1:
time: 163 us; the launch traced here: 162 us
  waiting for transfers between devices  58.7 us (36%)
  Pallas kernels  37 us (23%)
  starting transfers between devices  28.5 us (17%)
  blocking collectives  22.6 us (14%)
  local copies, waits for them, and re-layouts  11.9 us (7%)
  other arithmetic  2.35 us (1%)
    all_to_all x7, waiting for transfers between devices, swap(): return lax.all_to_all(x, axis, split_axis=0, concat_axis=0, tiled=True)  58.7 us
    pallas_call x2, Pallas kernels, attend(): pl.pallas_call(attend_kernel, grid_spec=pltpu.PrefetchScalarGridSpec(num_...  31.2 us
    all_to_all x7, starting transfers between devices, swap(): return lax.all_to_all(x, axis, split_axis=0, concat_axis=0, tiled=True)  28.5 us
    all_to_all x2, blocking collectives, swap(): return lax.all_to_all(x, axis, split_axis=0, concat_axis=0, tiled=True)  22.6 us
    unnamed x19, local copies, waits for them, and re-layouts  9.41 us
  transfers between devices with their start and end apart: 7, of which 7 were waited for; matrix products, arithmetic and copies ran while one was open for 3% of the time, Pallas kernels for 23%

profile of v1, /device:TPU:0, one launch (start us, length us, event | category | flops | bytes accessed | tf_op | source)
XLA Modules:
  0.0 161.8 jit_solution(13247986548419568493)
XLA Ops:
  0.7 0.8 copy.33
  1.5 0.1 reshape.60
  1.6 0.1 fusion.6
  1.7 0.1 reshape.61
  1.8 0.2 reduce_window_sum.11
  2.0 0.2 select_reduce_fusion.1
  2.2 0.7 copy.38
  2.8 7.3 %all-to-all-start.1 = ((s32[8,1,3]{2,1,0:T(1,128)}), s32[8,1,3]{2,1,0:T(1,128)S(1)}, u32[]{:S(2)}, u32[]{:S(2)}) async-start(s32[8,1,3]{2,1,0:T(1,128)} %copy.38), calls=%async_computation.1 | async-start | bytes 8192 | tf_op jit(solution)/shard_map/all_to_all | solution.py:196
  10.1 1.2 copy.34
  11.4 0.3 copy.36
  11.7 0.2 copy.35
  11.9 0.3 copy.37
  12.1 0.9 fusion.5
  13.0 3.5 %all-to-all-done.1 = s32[8,1,3]{2,1,0:T(1,128)S(1)} async-done(((s32[8,1,3]{2,1,0:T(1,128)}), s32[8,1,3]{2,1,0:T(1,128)S(1)}, u32[]{:S(2)}, u32[]{:S(2)}) %all-to-all-start.1) | async-done | bytes 128 | tf_op jit(solution)/shard_map/all_to_all | solution.py:196
  16.5 11.4 %all_to_all.49.own = bf16[4,2,256,128]{3,2,1,0:T(8,128)(2,1)S(1)} all-to-all(bf16[4,2,256,128]{3,2,1,0:T(8,128)(2,1)S(1)} %get-tuple-element.36), channel_id=1, replica_groups=mesh['head'=4,'ctx'=8] {'head'}, dimensions={0} | all-to-all | bytes 1048576 | tf_op jit(solution)/shard_map/all_to_all | solution.py:196
  27.9 3.5 %all-to-all-start = ((bf16[4,2,256,128]{3,2,1,0:T(8,128)(2,1)}), bf16[4,2,256,128]{3,2,1,0:T(8,128)(2,1)S(1)}, u32[]{:S(2)}, u32[]{:S(2)}) async-start(bf16[4,2,256,128]{3,2,1,0:T(8,128)(2,1)} %get-tuple-element.37), calls=%async_computation | async-start | bytes 1048576 | tf_op jit(solution)/shard_map/all_to_all | solution.py:196
  31.4 0.5 broadcast.50
  31.9 0.7 reduce.3
  32.7 1.6 pick.3
  34.2 6.0 %all-to-all-done.own = bf16[4,2,256,128]{3,2,1,0:T(8,128)(2,1)S(1)} async-done(((bf16[4,2,256,128]{3,2,1,0:T(8,128)(2,1)}), bf16[4,2,256,128]{3,2,1,0:T(8,128)(2,1)S(1)}, u32[]{:S(2)}, u32[]{:S(2)}) %all-to-all-start) | async-done | bytes 524320 | tf_op jit(solution)/shard_map/all_to_all | solution.py:196
  40.2 3.5 %all-to-all-start.4 = ((bf16[8,2,3,64,128]{4,3,2,1,0:T(8,128)(2,1)}), bf16[8,2,3,64,128]{4,3,2,1,0:T(8,128)(2,1)S(1)}, u32[]{:S(2)}, u32[]{:S(2)}) async-start(bf16[8,2,3,64,128]{4,3,2,1,0:T(8,128)(2,1)} %pick.3), calls=%async_computation.4 | async-start | bytes 1572864 | tf_op jit(solution)/shard_map/all_to_all | solution.py:196
  43.8 1.6 pick.2
  45.4 18.6 %all-to-all-done.4.far = bf16[8,2,3,64,128]{4,3,2,1,0:T(8,128)(2,1)S(1)} async-done(((bf16[8,2,3,64,128]{4,3,2,1,0:T(8,128)(2,1)}), bf16[8,2,3,64,128]{4,3,2,1,0:T(8,128)(2,1)S(1)}, u32[]{:S(2)}, u32[]{:S(2)}) %all-to-all-start.4) | async-done | bytes 786464 | tf_op jit(solution)/shard_map/all_to_all | solution.py:196
  64.0 3.5 %all-to-all-start.2 = ((bf16[8,2,3,64,128]{4,3,2,1,0:T(8,128)(2,1)}), bf16[8,2,3,64,128]{4,3,2,1,0:T(8,128)(2,1)S(1)}, u32[]{:S(2)}, u32[]{:S(2)}) async-start(bf16[8,2,3,64,128]{4,3,2,1,0:T(8,128)(2,1)} %pick.2), calls=%async_computation.2 | async-start | bytes 1572864 | tf_op jit(solution)/shard_map/all_to_all | solution.py:196
  67.5 0.1 sub.14
  67.6 0.2 select_reduce_fusion
  67.8 1.1 copy-done.3
  68.9 15.6 %attend.2 = (bf16[1024,1024]{1,0:T(8,128)(2,1)}, bf16[1024,1024]{1,0:T(8,128)(2,1)}, f32[2,16,64,128]{3,2,1,0:T(8,128)S(1)}, bf16[8,2,3,64,128]{4,3,2,1,0:T(8,128)(2,1)S(1)}) custom-call(s32[128]{0:T(128)S(1)} %compare_select_fusion.source, bf16[1024,1024]{1,0:T(8,128)(2,1)} %q_ref.3, bf16[1024,1024]{1,0:T(8,128)(2,1)} %g_ref.3, ...), custom_call_target="tpu_custom_call" | custom-call | flops 3221225472 | bytes 20971520 | tf_op jit(solution)/shard_map/attend/pallas_call | solution.py:149
  84.6 0.9 copy-done.4
  85.5 2.4 %all-to-all-done.2.far = bf16[8,2,3,64,128]{4,3,2,1,0:T(8,128)(2,1)S(1)} async-done(((bf16[8,2,3,64,128]{4,3,2,1,0:T(8,128)(2,1)}), bf16[8,2,3,64,128]{4,3,2,1,0:T(8,128)(2,1)S(1)}, u32[]{:S(2)}, u32[]{:S(2)}) %all-to-all-start.2) | async-done | bytes 786464 | tf_op jit(solution)/shard_map/all_to_all | solution.py:196
  87.9 3.6 %all-to-all-start.5 = ((bf16[8,2,3,64,128]{4,3,2,1,0:T(8,128)(2,1)}), bf16[8,2,3,64,128]{4,3,2,1,0:T(8,128)(2,1)S(1)}, u32[]{:S(2)}, u32[]{:S(2)}) async-start(bf16[8,2,3,64,128]{4,3,2,1,0:T(8,128)(2,1)} %copy-done.4), calls=%async_computation.5 | async-start | bytes 1572864 | tf_op jit(solution)/shard_map/all_to_all | solution.py:196
  91.5 15.6 %attend.3 = (bf16[1024,1024]{1,0:T(8,128)(2,1)}, bf16[1024,1024]{1,0:T(8,128)(2,1)}, f32[2,16,64,128]{3,2,1,0:T(8,128)S(1)}, bf16[8,2,3,64,128]{4,3,2,1,0:T(8,128)(2,1)S(1)}) custom-call(s32[128]{0:T(128)S(1)} %compare_select_fusion.source, bf16[1024,1024]{1,0:T(8,128)(2,1)} %q_ref.3, ...), custom_call_target="tpu_custom_call", output_to_operand_aliasing={{0}: (5, {}), {1}: (6, {})} | custom-call | flops 3221225472 | bytes 20971520 | tf_op jit(solution)/shard_map/attend/pallas_call | solution.py:149
  107.1 1.0 copy-done
  108.1 0.9 copy-done.5
  108.9 2.8 %all-to-all-done.5.back = bf16[8,2,3,64,128]{4,3,2,1,0:T(8,128)(2,1)S(1)} async-done(((bf16[8,2,3,64,128]{4,3,2,1,0:T(8,128)(2,1)}), bf16[8,2,3,64,128]{4,3,2,1,0:T(8,128)(2,1)S(1)}, u32[]{:S(2)}, u32[]{:S(2)}) %all-to-all-start.5) | async-done | bytes 786464 | tf_op jit(solution)/shard_map/all_to_all | solution.py:196
  111.8 3.5 %all-to-all-start.7 = ((bf16[8,2,3,64,128]{4,3,2,1,0:T(8,128)(2,1)}), bf16[8,2,3,64,128]{4,3,2,1,0:T(8,128)(2,1)S(1)}, u32[]{:S(2)}, u32[]{:S(2)}) async-start(bf16[8,2,3,64,128]{4,3,2,1,0:T(8,128)(2,1)} %copy-done.5), calls=%async_computation.7 | async-start | bytes 1572864 | tf_op jit(solution)/shard_map/all_to_all | solution.py:196
  115.3 1.7 %gather_sum.2 = bf16[4,2,256,128]{3,2,1,0:T(8,128)(2,1)} custom-call(s32[24]{0:T(128)S(1)} %reshape.62.asked, f32[2,16,64,128]{3,2,1,0:T(8,128)S(1)} %get-tuple-element.16.near, bf16[8,2,3,64,128]{4,3,2,1,0:T(8,128)(2,1)S(1)} %all-to-all-done.5.back), custom_call_target="tpu_custom_call" | custom-call | tf_op jit(solution)/shard_map/gather_sum/pallas_call | solution.py:180
  117.0 18.7 %all-to-all-done.7.back = bf16[8,2,3,64,128]{4,3,2,1,0:T(8,128)(2,1)S(1)} async-done(((bf16[8,2,3,64,128]{4,3,2,1,0:T(8,128)(2,1)}), bf16[8,2,3,64,128]{4,3,2,1,0:T(8,128)(2,1)S(1)}, u32[]{:S(2)}, u32[]{:S(2)}) %all-to-all-start.7) | async-done | bytes 786464 | tf_op jit(solution)/shard_map/all_to_all | solution.py:196
  135.7 3.5 %all-to-all-start.6 = ((bf16[4,2,256,128]{3,2,1,0:T(8,128)(2,1)}), bf16[4,2,256,128]{3,2,1,0:T(8,128)(2,1)S(1)}, u32[]{:S(2)}, u32[]{:S(2)}) async-start(bf16[4,2,256,128]{3,2,1,0:T(8,128)(2,1)} %gather_sum.2), calls=%async_computation.6 | async-start | bytes 1048576 | tf_op jit(solution)/shard_map/all_to_all | solution.py:196
  139.2 1.2 copy-done.1
  140.4 0.9 gather_sum.3
  141.3 6.7 %all-to-all-done.6 = bf16[4,2,256,128]{3,2,1,0:T(8,128)(2,1)S(1)} async-done(((bf16[4,2,256,128]{3,2,1,0:T(8,128)(2,1)}), bf16[4,2,256,128]{3,2,1,0:T(8,128)(2,1)S(1)}, u32[]{:S(2)}, u32[]{:S(2)}) %all-to-all-start.6) | async-done | bytes 524320 | tf_op jit(solution)/shard_map/all_to_all | solution.py:196
  148.0 11.2 %all_to_all.50 = bf16[4,2,256,128]{3,2,1,0:T(8,128)(2,1)S(1)} all-to-all(bf16[4,2,256,128]{3,2,1,0:T(8,128)(2,1)S(1)} %gather_sum.3), channel_id=1, replica_groups=mesh['head'=4,'ctx'=8] {'head'}, dimensions={0} | all-to-all | bytes 1048576 | tf_op jit(solution)/shard_map/all_to_all | solution.py:196
  159.2 0.1 fusion.4
  159.3 0.2 copy.40
  159.6 1.0 copy.42
  160.6 0.2 copy.39
  160.8 1.0 copy.41
  (14 shorter events, 0.2 us)
Async XLA Ops:
  0.6 11.0 %copy-start.6 = (bf16[256,1024]{1,0:T(8,128)(2,1)S(1)}, bf16[256,1024]{1,0:T(8,128)(2,1)}, u32[]{:S(2)}) copy-start(bf16[256,1024]{1,0:T(8,128)(2,1)} %param.7) | copy-start | bytes 1572868
  2.8 13.7 %all-to-all-start.1 = ((s32[8,1,3]{2,1,0:T(1,128)}), s32[8,1,3]{2,1,0:T(1,128)S(1)}, u32[]{:S(2)}, u32[]{:S(2)}) async-start(s32[8,1,3]{2,1,0:T(1,128)} %copy.38), calls=%async_computation.1 | async-start | bytes 8192 | tf_op jit(solution)/shard_map/all_to_all | solution.py:196
  27.9 12.3 %all-to-all-start = ((bf16[4,2,256,128]{3,2,1,0:T(8,128)(2,1)}), bf16[4,2,256,128]{3,2,1,0:T(8,128)(2,1)S(1)}, u32[]{:S(2)}, u32[]{:S(2)}) async-start(bf16[4,2,256,128]{3,2,1,0:T(8,128)(2,1)} %get-tuple-element.37), calls=%async_computation | async-start | bytes 1048576 | tf_op jit(solution)/shard_map/all_to_all | solution.py:196
  40.2 23.8 %all-to-all-start.4 = ((bf16[8,2,3,64,128]{4,3,2,1,0:T(8,128)(2,1)}), bf16[8,2,3,64,128]{4,3,2,1,0:T(8,128)(2,1)S(1)}, u32[]{:S(2)}, u32[]{:S(2)}) async-start(bf16[8,2,3,64,128]{4,3,2,1,0:T(8,128)(2,1)} %pick.3), calls=%async_computation.4 | async-start | bytes 1572864 | tf_op jit(solution)/shard_map/all_to_all | solution.py:196
  64.0 3.8 %copy-start.2 = (bf16[8,2,3,64,128]{4,3,2,1,0:T(8,128)(2,1)}, bf16[8,2,3,64,128]{4,3,2,1,0:T(8,128)(2,1)S(1)}, u32[]{:S(2)}) copy-start(bf16[8,2,3,64,128]{4,3,2,1,0:T(8,128)(2,1)S(1)} %all-to-all-done.4.far) | copy-start | bytes 2359300
  64.0 23.9 %all-to-all-start.2 = ((bf16[8,2,3,64,128]{4,3,2,1,0:T(8,128)(2,1)}), bf16[8,2,3,64,128]{4,3,2,1,0:T(8,128)(2,1)S(1)}, u32[]{:S(2)}, u32[]{:S(2)}) async-start(bf16[8,2,3,64,128]{4,3,2,1,0:T(8,128)(2,1)} %pick.2), calls=%async_computation.2 | async-start | bytes 1572864 | tf_op jit(solution)/shard_map/all_to_all | solution.py:196
  67.8 1.1 copy-start.3
  84.6 0.9 copy-start.4
  87.9 23.9 %all-to-all-start.5 = ((bf16[8,2,3,64,128]{4,3,2,1,0:T(8,128)(2,1)}), bf16[8,2,3,64,128]{4,3,2,1,0:T(8,128)(2,1)S(1)}, u32[]{:S(2)}, u32[]{:S(2)}) async-start(bf16[8,2,3,64,128]{4,3,2,1,0:T(8,128)(2,1)} %copy-done.4), calls=%async_computation.5 | async-start | bytes 1572864 | tf_op jit(solution)/shard_map/all_to_all | solution.py:196
  107.1 1.0 copy-start
  108.1 0.9 copy-start.5
  111.8 23.9 %all-to-all-start.7 = ((bf16[8,2,3,64,128]{4,3,2,1,0:T(8,128)(2,1)}), bf16[8,2,3,64,128]{4,3,2,1,0:T(8,128)(2,1)S(1)}, u32[]{:S(2)}, u32[]{:S(2)}) async-start(bf16[8,2,3,64,128]{4,3,2,1,0:T(8,128)(2,1)} %copy-done.5), calls=%async_computation.7 | async-start | bytes 1572864 | tf_op jit(solution)/shard_map/all_to_all | solution.py:196
  135.7 12.3 %all-to-all-start.6 = ((bf16[4,2,256,128]{3,2,1,0:T(8,128)(2,1)}), bf16[4,2,256,128]{3,2,1,0:T(8,128)(2,1)S(1)}, u32[]{:S(2)}, u32[]{:S(2)}) async-start(bf16[4,2,256,128]{3,2,1,0:T(8,128)(2,1)} %gather_sum.2), calls=%async_computation.6 | async-start | bytes 1048576 | tf_op jit(solution)/shard_map/all_to_all | solution.py:196
  139.2 1.2 copy-start.1

commit v2 on v1

v2 whole, which is shorter than its diff:
```python
import functools

import jax
import jax.numpy as jnp
from jax import lax
from jax.experimental import pallas as pl
from jax.experimental.pallas import tpu as pltpu
from jax.sharding import PartitionSpec as P

HEAD_DIM = 128
GROUP = 4
BLK = 64
LIST = 8
CAP = 3
STEP_BLOCKS = 2
NEG_FILL = -1e30
SCALE = HEAD_DIM ** (-0.5)
LOG2E = 1.4426950408889634
VMEM_LIMIT = 50 * 1024 * 1024

NT = (((1,), (1,)), ((), ()))
NN = (((1,), (0,)), ((), ()))
TN = (((0,), (0,)), ((), ()))


def dot(a, b, dims):
    return lax.dot_general(a, b, dims, preferred_element_type=jnp.float32)


def params(**kw):
    return pltpu.CompilerParams(vmem_limit_bytes=VMEM_LIMIT, **kw)


def split_kernel(place, *refs):
    k_ref, v_ref, *outs = refs
    heads = len(outs)
    me = place[1]
    h = place[2]
    head_count = k_ref.shape[1] // heads // HEAD_DIM
    for r, out in enumerate(outs):
        peer = lax.rem(me + r, heads)
        col = pl.multiple_of((peer * head_count + h) * HEAD_DIM, HEAD_DIM)
        out[0] = k_ref[:, pl.ds(col, HEAD_DIM)]
        out[1] = v_ref[:, pl.ds(col, HEAD_DIM)]


def fill_table(place, own, table):
    heads = len(own)
    per_quarter = own[0].shape[1] // BLK
    for r in range(heads):
        first = lax.rem(place[1] + heads - r, heads) * per_quarter
        for kv in range(2):
            for j in range(per_quarter):
                table[kv, first + j] = own[r][kv, j * BLK : (j + 1) * BLK, :]


def pick_kernel(place, asked, *refs, heads):
    own, (*outs, table) = refs[:heads], refs[heads:]
    fill_table(place, own, table)
    shard_count = len(outs) + 1
    for d, out in enumerate(outs, 1):
        c = lax.rem(place[0] + d, shard_count)
        for s in range(CAP):
            block = asked[c * CAP + s]
            for kv in range(2):
                out[kv, s] = table[kv, block]


def attend_kernel(place, source, q_ref, g_ref, *refs, heads, steps):
    own, far = refs[:heads], refs[heads : heads + steps]
    table, total = refs[-2:]
    far_out = refs[-2 - steps : -2]
    o_ref, dq_ref, near_out = refs[-5 - steps : -2 - steps]
    step = pl.program_id(0)
    blocks_here = near_out.shape[1]

    @pl.when(step == 0)
    def _():
        fill_table(place, own, table)
        for kv in range(2):
            for d in range(steps):
                for s in range(CAP):
                    table[kv, blocks_here + d * CAP + s] = far[d][kv, s]
        total[...] = jnp.zeros_like(total)

    key_row = lax.broadcasted_iota(jnp.int32, (BLK, GROUP * BLK), 0)
    query_col = lax.broadcasted_iota(jnp.int32, (BLK, GROUP * BLK), 1) % BLK
    hidden = key_row > query_col
    for sub in range(STEP_BLOCKS):
        block = step * STEP_BLOCKS + sub
        rows = slice(sub * BLK, (sub + 1) * BLK)
        listed = [source[block * LIST + e] for e in range(LIST)]
        q = jnp.concatenate([q_ref[rows, g * HEAD_DIM : (g + 1) * HEAD_DIM] for g in range(GROUP)], axis=0)
        g_out = jnp.concatenate([g_ref[rows, g * HEAD_DIM : (g + 1) * HEAD_DIM] for g in range(GROUP)], axis=0)
        keys = jnp.concatenate([table[0, at] for at in listed], axis=0)
        values = jnp.concatenate([table[1, at] for at in listed], axis=0)
        scores = dot(keys, q, NT)
        parts = []
        for e in range(LIST):
            part = scores[e * BLK : (e + 1) * BLK]
            mask = hidden if e == 0 else hidden & (listed[e] == block)
            parts.append(jnp.where(mask, NEG_FILL, part))
        scores = jnp.concatenate(parts, axis=0)
        peak = jnp.max(scores, axis=0, keepdims=True)
        expo = jnp.exp2((scores - peak) * (SCALE * LOG2E))
        probs = expo * (1.0 / jnp.sum(expo, axis=0, keepdims=True))
        probs_low = probs.astype(jnp.bfloat16)
        dprob = dot(values, g_out, NT)
        delta = jnp.sum(probs * dprob, axis=0, keepdims=True)
        dscore = (probs * (dprob - delta)).astype(jnp.bfloat16)
        attended = dot(values, probs_low, TN).T.astype(jnp.bfloat16)
        dq = (dot(keys, dscore, TN) * SCALE).T.astype(jnp.bfloat16)
        for g in range(GROUP):
            cols = slice(g * HEAD_DIM, (g + 1) * HEAD_DIM)
            o_ref[rows, cols] = attended[g * BLK : (g + 1) * BLK]
            dq_ref[rows, cols] = dq[g * BLK : (g + 1) * BLK]
        dk = dot(dscore, q, NN)
        dv = dot(probs_low, g_out, NN)
        for e in range(LIST):
            total[0, listed[e]] += dk[e * BLK : (e + 1) * BLK]
            total[1, listed[e]] += dv[e * BLK : (e + 1) * BLK]

    @pl.when(step == pl.num_programs(0) - 1)
    def _():
        for kv, factor in ((0, SCALE), (1, 1.0)):
            near_out[kv] = total[kv, :blocks_here] * factor
            for d in range(steps):
                first = blocks_here + d * CAP
                far_out[d][kv] = (total[kv, first : first + CAP] * factor).astype(jnp.bfloat16)


def gather_sum_kernel(place, asked, near, *refs, steps):
    back, (*outs, total) = refs[:steps], refs[steps:]
    heads = len(outs)
    per_quarter = outs[0].shape[1] // BLK
    total[...] = near[...]
    for d in range(1, steps + 1):
        c = lax.rem(place[0] + d, steps + 1)
        for s in range(CAP):
            block = asked[c * CAP + s]
            for kv in range(2):
                total[kv, block] += back[d - 1][kv, s].astype(jnp.float32)
    for r in range(heads):
        first = lax.rem(place[1] + heads - r, heads) * per_quarter
        for kv in range(2):
            for j in range(per_quarter):
                outs[r][kv, j * BLK : (j + 1) * BLK, :] = total[kv, first + j].astype(jnp.bfloat16)


def join_kernel(place, *refs, heads):
    *pieces, k_ref, v_ref = refs
    head_count = len(pieces) // heads
    for h in range(head_count):
        for r in range(heads):
            peer = lax.rem(place[1] + r, heads)
            col = pl.multiple_of((peer * head_count + h) * HEAD_DIM, HEAD_DIM)
            k_ref[:, pl.ds(col, HEAD_DIM)] = pieces[h * heads + r][0]
            v_ref[:, pl.ds(col, HEAD_DIM)] = pieces[h * heads + r][1]


def whole(shape):
    return pl.BlockSpec(tuple(shape), lambda *_: (0,) * len(shape))


def call(kernel, scalars, arrays, out_shapes, scratch=(), name=None):
    return pl.pallas_call(
        kernel,
        grid_spec=pltpu.PrefetchScalarGridSpec(
            num_scalar_prefetch=len(scalars),
            grid=(1,),
            in_specs=[whole(x.shape) for x in arrays],
            out_specs=[whole(x.shape) for x in out_shapes],
            scratch_shapes=list(scratch),
        ),
        out_shape=list(out_shapes),
        compiler_params=params(),
        name=name,
    )(*scalars, *arrays)


def attend(place, source, queries, out_grad, own, far, head, earlier):
    tokens_here, width = queries.shape
    blocks_here = tokens_here // BLK
    slots = blocks_here + len(far) * CAP
    tile = pl.BlockSpec((STEP_BLOCKS * BLK, GROUP * HEAD_DIM), lambda i, *_: (i, head))
    near_shape = (2, blocks_here, BLK, HEAD_DIM)
    first = 4 + len(own) + len(far)
    aliases = {first: 0, first + 1: 1} if earlier else {}
    arrays = [*own, *far]
    return pl.pallas_call(
        functools.partial(attend_kernel, heads=len(own), steps=len(far)),
        grid_spec=pltpu.PrefetchScalarGridSpec(
            num_scalar_prefetch=2,
            grid=(blocks_here // STEP_BLOCKS,),
            in_specs=[tile, tile]
            + [whole(x.shape) for x in arrays]
            + [pl.BlockSpec(memory_space=pl.ANY)] * len(earlier),
            out_specs=[tile, tile, whole(near_shape)] + [whole(x.shape) for x in far],
            scratch_shapes=[
                pltpu.VMEM((2, slots, BLK, HEAD_DIM), jnp.bfloat16),
                pltpu.VMEM((2, slots, BLK, HEAD_DIM), jnp.float32),
            ],
        ),
        out_shape=[
            jax.ShapeDtypeStruct((tokens_here, width), jnp.bfloat16),
            jax.ShapeDtypeStruct((tokens_here, width), jnp.bfloat16),
            jax.ShapeDtypeStruct(near_shape, jnp.float32),
        ]
        + [jax.ShapeDtypeStruct(x.shape, jnp.bfloat16) for x in far],
        input_output_aliases=aliases,
        compiler_params=params(),
        cost_estimate=pl.CostEstimate(
            flops=12 * blocks_here * LIST * BLK * GROUP * BLK * HEAD_DIM,
            bytes_accessed=20 * 1024 * 1024,
            transcendentals=blocks_here * LIST * BLK * GROUP * BLK,
        ),
        name="attend",
    )(place, source, queries, out_grad, *arrays, *earlier)


def turn(x, axis, count, by):
    return lax.ppermute(x, axis, [(i, (i + by) % count) for i in range(count)])


def up(x, count, by):
    return lax.ppermute(x, "ctx", [(i, i + by) for i in range(count - by)])


def down(x, count, by):
    return lax.ppermute(x, "ctx", [(i + by, i) for i in range(count - by)])


def per_device(queries, key_states, value_states, block_lists, out_grad):
    shard_index = lax.axis_index("ctx")
    shard_count = lax.axis_size("ctx")
    heads = lax.axis_size("head")
    blocks_here = queries.shape[0] // BLK
    quarter = key_states.shape[0]
    head_count = key_states.shape[1] // heads // HEAD_DIM
    head_index = lax.axis_index("head")
    place = jnp.stack([shard_index, head_index]).astype(jnp.int32)

    piece = jax.ShapeDtypeStruct((2, quarter, HEAD_DIM), jnp.bfloat16)
    own = []
    for h in range(head_count):
        here = jnp.concatenate([place, jnp.full((1,), h, jnp.int32)])
        parts = call(split_kernel, [here], [key_states, value_states], [piece] * heads, name="split")
        own.append([parts[0]] + [turn(parts[r], "head", heads, r) for r in range(1, heads)])

    flat_ids = block_lists.reshape(-1)
    owner_shard = flat_ids // blocks_here
    inner_index = flat_ids % blocks_here
    every_block = jnp.arange(shard_count * blocks_here, dtype=jnp.int32)
    hits = flat_ids[:, None] == every_block[None, :]
    block_hits = jnp.any(hits, axis=0).reshape(shard_count, blocks_here)
    needed = block_hits & (jnp.arange(shard_count) != shard_index)[:, None]
    slot_rank = jnp.cumsum(needed.astype(jnp.int32), axis=1) - 1
    slot_pick = needed[:, :, None] & (slot_rank[:, :, None] == jnp.arange(CAP)[None, None, :])
    requests = jnp.sum(jnp.where(slot_pick, jnp.arange(blocks_here, dtype=jnp.int32)[None, :, None], 0), axis=1)
    ref_rank = jnp.sum(jnp.where(hits, slot_rank.reshape(-1)[None, :], 0), axis=1)
    distance = shard_index - owner_shard
    source = jnp.where(distance == 0, inner_index, blocks_here + (distance - 1) * CAP + ref_rank)
    asked = lax.all_to_all(requests, "ctx", split_axis=0, concat_axis=0, tiled=True).reshape(-1)

    slots = jax.ShapeDtypeStruct((2, CAP, BLK, HEAD_DIM), jnp.bfloat16)
    table = pltpu.VMEM((2, blocks_here, BLK, HEAD_DIM), jnp.bfloat16)
    far = []
    for h in range(head_count):
        picked = call(
            functools.partial(pick_kernel, heads=heads), [place, asked], own[h], [slots] * (shard_count - 1), [table], "pick"
        )
        far.append([up(x, shard_count, d) for d, x in enumerate(picked, 1)])
    earlier, nears, backs = [], [], []
    for h in range(head_count):
        attended, query_grad, near, *far_grad = attend(
            place, source, queries, out_grad, own[h], far[h], h, earlier
        )
        earlier = [attended, query_grad]
        nears.append(near)
        backs.append([down(x, shard_count, d) for d, x in enumerate(far_grad, 1)])
    total = pltpu.VMEM((2, blocks_here, BLK, HEAD_DIM), jnp.float32)
    done = []
    for h in range(head_count):
        sums = call(
            functools.partial(gather_sum_kernel, steps=shard_count - 1),
            [place, asked], [nears[h], *backs[h]], [piece] * heads, [total], "gather_sum",
        )
        done.append([sums[0]] + [turn(sums[r], "head", heads, -r) for r in range(1, heads)])
    pieces = [x for group in done for x in group]
    grad = jax.ShapeDtypeStruct(key_states.shape, jnp.bfloat16)
    key_grad, value_grad = call(functools.partial(join_kernel, heads=heads), [place], pieces, [grad, grad], name="join")
    return attended, query_grad, key_grad, value_grad


def solution(mesh):
    return jax.shard_map(
        per_device,
        mesh=mesh,
        in_specs=(
            P("ctx", "head"),
            P(("ctx", "head"), None),
            P(("ctx", "head"), None),
            P("ctx", None),
            P("ctx", "head"),
        ),
        out_specs=(
            P("ctx", "head"),
            P("ctx", "head"),
            P(("ctx", "head"), None),
            P(("ctx", "head"), None),
        ),
        check_vma=False,
    )
```

time: 163 us -> 149 us (0.914)
  starting transfers between devices: 28.5 us -> 69.6 us
  waiting for transfers between devices: 58.7 us -> 32.1 us
  blocking collectives: 22.6 us -> 0 us
  local copies, waits for them, and re-layouts: 11.9 us -> 6.45 us
    ppermute x0 -> x40, starting transfers between devices: none -> 63.7 us  [the longest x14 37.1 us: up(): return lax.ppermute(x, 'ctx', [(i, i + by) for i in range(count - by)])]
    all_to_all x7 -> x1, waiting for transfers between devices: 58.7 us -> 1.4 us  [per_device(): lax.all_to_all(requests, 'ctx', split_axis=0, concat_axis=0, tiled=True)]
    ppermute x0 -> x40, waiting for transfers between devices: none -> 30.7 us  [the longest x14 23.5 us: down(): return lax.ppermute(x, 'ctx', [(i + by, i) for i in range(count - by)])]
    all_to_all x2 -> x0, blocking collectives: 22.6 us -> none  [swap(): return lax.all_to_all(x, axis, split_axis=0, concat_axis=0, tiled=True)]
    all_to_all x7 -> x1, starting transfers between devices: 28.5 us -> 5.84 us  [per_device(): lax.all_to_all(requests, 'ctx', split_axis=0, concat_axis=0, tiled=True)]
    unnamed x19 -> x9, local copies, waits for them, and re-layouts: 9.41 us -> 4.92 us
    pallas_call x6 -> x9, Pallas kernels: 37 us -> 37.2 us  [the longest x2 31.2 us: attend(): pl.pallas_call(functools.partial(attend_kernel, heads=len(own), steps=len...]
  transfers between devices with their start and end apart: 7 -> 41, of which waited for: 7 -> 11; matrix products, arithmetic and copies ran while one was open for 3% -> 3% of each run, Pallas kernels for 23% -> 24%
where the time goes in v2:
time: 149 us; the launch traced here: 148 us
  starting transfers between devices  69.6 us (47%)
  Pallas kernels  37.2 us (25%)
  waiting for transfers between devices  32.1 us (22%)
  local copies, waits for them, and re-layouts  6.45 us (4%)
  other arithmetic  1.51 us (1%)
    ppermute x14, starting transfers between devices, up(): return lax.ppermute(x, 'ctx', [(i, i + by) for i in range(count - by)])  37.1 us
    pallas_call x2, Pallas kernels, attend(): pl.pallas_call(functools.partial(attend_kernel, heads=len(own), steps=len...  31.2 us
    ppermute x14, waiting for transfers between devices, down(): return lax.ppermute(x, 'ctx', [(i + by, i) for i in range(count - by)])  23.5 us
    ppermute x14, starting transfers between devices, down(): return lax.ppermute(x, 'ctx', [(i + by, i) for i in range(count - by)])  18 us
    ppermute x12, starting transfers between devices, turn(): return lax.ppermute(x, axis, [(i, (i + by) % count) for i in range(count)])  8.54 us
    ppermute x12, waiting for transfers between devices, turn(): return lax.ppermute(x, axis, [(i, (i + by) % count) for i in range(count)])  7.19 us
    pallas_call x7, Pallas kernels, call(): pl.pallas_call(kernel, grid_spec=pltpu.PrefetchScalarGridSpec(num_scalar_...  6 us
    all_to_all x1, starting transfers between devices, per_device(): lax.all_to_all(requests, 'ctx', split_axis=0, concat_axis=0, tiled=True)  5.84 us
  transfers between devices with their start and end apart: 41, of which 11 were waited for; matrix products, arithmetic and copies ran while one was open for 3% of the time, Pallas kernels for 24%

profile of v2, /device:TPU:0, one launch (start us, length us, event | category | flops | bytes accessed | tf_op | source)
XLA Modules:
  0.0 148.0 jit_solution(5087020012968653846)
XLA Ops:
  0.7 1.0 copy-done
  4.0 2.6 %collective-permute-start.11 = (bf16[2,256,128]{2,1,0:T(8,128)(2,1)S(1)}, bf16[2,256,128]{2,1,0:T(8,128)(2,1)S(1)}, u32[]{:S(2)}, u32[]{:S(2)}) collective-permute-start(bf16[2,256,128]{2,1,0:T(8,128)(2,1)S(1)} %get-tuple-element.69), channel_id=1, source_target_pairs={{0,16},{8,24},{16,0},{24,8},{1,17},{9,25},{17,1},{25,9},{2,18},{10... | collective-permute-start | bytes 393224 | tf_op jit(solution)/shard_map/ppermute | solution.py:222
  6.6 1.4 collective-permute-start.12
  10.1 5.8 %all-to-all-start = ((s32[8,1,3]{2,1,0:T(1,128)}), s32[8,1,3]{2,1,0:T(1,128)S(1)}, u32[]{:S(2)}, u32[]{:S(2)}) async-start(s32[8,1,3]{2,1,0:T(1,128)} %copy.18), calls=%async_computation | async-start | bytes 8192 | tf_op jit(solution)/shard_map/all_to_all | solution.py:263
  17.0 1.0 copy-done.3
  19.4 1.4 collective-permute-start.2
  20.9 1.4 all-to-all-done
  24.2 2.5 %collective-permute-start.13 = (bf16[2,3,64,128]{3,2,1,0:T(8,128)(2,1)S(1)}, bf16[2,3,64,128]{3,2,1,0:T(8,128)(2,1)S(1)}, u32[]{:S(2)}, u32[]{:S(2)}) collective-permute-start(bf16[2,3,64,128]{3,2,1,0:T(8,128)(2,1)S(1)} %get-tuple-element.71), channel_id=1, source_target_pairs={{0,1},{1,2},{2,3},{3,4},{4,5},{5,6},{6,7},{8,9},{9,10},{10,11},{11... | collective-permute-start | bytes 294920 | tf_op jit(solution)/shard_map/ppermute | solution.py:226
  26.8 3.4 %collective-permute-start.14 = (bf16[2,3,64,128]{3,2,1,0:T(8,128)(2,1)S(1)}, bf16[2,3,64,128]{3,2,1,0:T(8,128)(2,1)S(1)}, u32[]{:S(2)}, u32[]{:S(2)}) collective-permute-start(bf16[2,3,64,128]{3,2,1,0:T(8,128)(2,1)S(1)} %get-tuple-element.72), channel_id=1, source_target_pairs={{0,2},{1,3},{2,4},{3,5},{4,6},{5,7},{8,10},{9,11},{10,12},{11,13},... | collective-permute-start | bytes 294920 | tf_op jit(solution)/shard_map/ppermute | solution.py:226
  30.3 4.3 %collective-permute-start.15 = (bf16[2,3,64,128]{3,2,1,0:T(8,128)(2,1)S(1)}, bf16[2,3,64,128]{3,2,1,0:T(8,128)(2,1)S(1)}, u32[]{:S(2)}, u32[]{:S(2)}) collective-permute-start(bf16[2,3,64,128]{3,2,1,0:T(8,128)(2,1)S(1)} %get-tuple-element.73), channel_id=1, source_target_pairs={{0,3},{1,4},{2,5},{3,6},{4,7},{8,11},{9,12},{10,13},{11,14},{12,15... | collective-permute-start | bytes 294920 | tf_op jit(solution)/shard_map/ppermute | solution.py:226
  34.6 1.9 %collective-permute-start.16 = (bf16[2,3,64,128]{3,2,1,0:T(8,128)(2,1)S(1)}, bf16[2,3,64,128]{3,2,1,0:T(8,128)(2,1)S(1)}, u32[]{:S(2)}, u32[]{:S(2)}) collective-permute-start(bf16[2,3,64,128]{3,2,1,0:T(8,128)(2,1)S(1)} %get-tuple-element.74), channel_id=1, source_target_pairs={{0,4},{1,5},{2,6},{3,7},{8,12},{9,13},{10,14},{11,15},{16,20},{17,... | collective-permute-start | bytes 294920 | tf_op jit(solution)/shard_map/ppermute | solution.py:226
  36.6 1.3 collective-permute-start.17
  37.9 1.3 collective-permute-start.18
  39.2 1.3 collective-permute-start.19
  41.2 2.1 %collective-permute-start.3 = (bf16[2,3,64,128]{3,2,1,0:T(8,128)(2,1)S(1)}, bf16[2,3,64,128]{3,2,1,0:T(8,128)(2,1)S(1)}, u32[]{:S(2)}, u32[]{:S(2)}) collective-permute-start(bf16[2,3,64,128]{3,2,1,0:T(8,128)(2,1)S(1)} %get-tuple-element.60), channel_id=1, source_target_pairs={{0,1},{1,2},{2,3},{3,4},{4,5},{5,6},{6,7},{8,9},{9,10},{10,11},{11... | collective-permute-start | bytes 294920 | tf_op jit(solution)/shard_map/ppermute | solution.py:226
  43.3 7.6 %collective-permute-start.4 = (bf16[2,3,64,128]{3,2,1,0:T(8,128)(2,1)S(1)}, bf16[2,3,64,128]{3,2,1,0:T(8,128)(2,1)S(1)}, u32[]{:S(2)}, u32[]{:S(2)}) collective-permute-start(bf16[2,3,64,128]{3,2,1,0:T(8,128)(2,1)S(1)} %get-tuple-element.61), channel_id=1, source_target_pairs={{0,2},{1,3},{2,4},{3,5},{4,6},{5,7},{8,10},{9,11},{10,12},{11,13},... | collective-permute-start | bytes 294920 | tf_op jit(solution)/shard_map/ppermute | solution.py:226
  50.9 6.2 %collective-permute-start.5 = (bf16[2,3,64,128]{3,2,1,0:T(8,128)(2,1)S(1)}, bf16[2,3,64,128]{3,2,1,0:T(8,128)(2,1)S(1)}, u32[]{:S(2)}, u32[]{:S(2)}) collective-permute-start(bf16[2,3,64,128]{3,2,1,0:T(8,128)(2,1)S(1)} %get-tuple-element.62), channel_id=1, source_target_pairs={{0,3},{1,4},{2,5},{3,6},{4,7},{8,11},{9,12},{10,13},{11,14},{12,15... | collective-permute-start | bytes 294920 | tf_op jit(solution)/shard_map/ppermute | solution.py:226
  57.1 1.4 collective-permute-start.6
  58.5 1.3 collective-permute-start.7
  59.8 15.6 %attend.2 = (bf16[1024,1024]{1,0:T(8,128)(2,1)}, bf16[1024,1024]{1,0:T(8,128)(2,1)}, f32[2,16,64,128]{3,2,1,0:T(8,128)S(1)}, bf16[2,3,64,128]{3,2,1,0:T(8,128)(2...) custom-call(s32[2]{0:T(128)S(1)} %pad_add_fusion.place, ...), custom_call_target="tpu_custom_call" | custom-call | flops 3221225472 | bytes 20971520 | tf_op jit(solution)/shard_map/attend/pallas_call | solution.py:190
  75.4 1.3 collective-permute-start.8
  76.7 1.3 collective-permute-start.9
  78.0 1.3 collective-permute-start.20
  79.4 1.3 collective-permute-start.21
  80.7 1.3 collective-permute-start.22
  82.0 1.3 collective-permute-start.23
  83.3 1.3 collective-permute-start.24
  84.6 1.3 collective-permute-start.25
  85.9 1.2 collective-permute-done.21.refs_1_
  87.1 1.3 collective-permute-start.26
  88.4 15.6 %attend.3 = (bf16[1024,1024]{1,0:T(8,128)(2,1)}, bf16[1024,1024]{1,0:T(8,128)(2,1)}, f32[2,16,64,128]{3,2,1,0:T(8,128)S(1)}, bf16[2,3,64,128]{3,2,1,0:T(8,128)(2...) custom-call(s32[2]{0:T(128)S(1)} %pad_add_fusion.place, ...), custom_call_target="tpu_custom_call", output_to_operand_aliasing={{0}: (15, {}), {1}: (16, {})} | custom-call | flops 3221225472 | bytes 20971520 | tf_op jit(solution)/shard_map/attend/pallas_call | solution.py:190
  104.0 1.3 collective-permute-start.30
  105.3 1.3 collective-permute-start.31
  106.6 1.3 collective-permute-start.32
  108.9 1.3 collective-permute-start.33
  110.2 1.4 collective-permute-done.30.refs_0_
  111.6 1.3 collective-permute-start.34
  112.9 5.5 %collective-permute-done.31.refs_1_ = bf16[2,3,64,128]{3,2,1,0:T(8,128)(2,1)S(1)} collective-permute-done((bf16[2,3,64,128]{3,2,1,0:T(8,128)(2,1)S(1)}, bf16[2,3,64,128]{3,2,1,0:T(8,128)(2,1)S(1)}, u32[]{:S(2)}, u32[]{:S(2)}) %collective-permute-start.31) | collective-permute-done | bytes 98336 | tf_op jit(solution)/shard_map/ppermute | solution.py:230
  118.4 1.3 collective-permute-start.35
  119.7 2.1 %collective-permute-done.32.refs_2_ = bf16[2,3,64,128]{3,2,1,0:T(8,128)(2,1)S(1)} collective-permute-done((bf16[2,3,64,128]{3,2,1,0:T(8,128)(2,1)S(1)}, bf16[2,3,64,128]{3,2,1,0:T(8,128)(2,1)S(1)}, u32[]{:S(2)}, u32[]{:S(2)}) %collective-permute-start.32) | collective-permute-done | bytes 98336 | tf_op jit(solution)/shard_map/ppermute | solution.py:230
  121.8 1.3 collective-permute-start.36
  123.0 9.2 %collective-permute-done.33.refs_3_ = bf16[2,3,64,128]{3,2,1,0:T(8,128)(2,1)S(1)} collective-permute-done((bf16[2,3,64,128]{3,2,1,0:T(8,128)(2,1)S(1)}, bf16[2,3,64,128]{3,2,1,0:T(8,128)(2,1)S(1)}, u32[]{:S(2)}, u32[]{:S(2)}) %collective-permute-start.33) | collective-permute-done | bytes 98336 | tf_op jit(solution)/shard_map/ppermute | solution.py:230
  132.2 4.1 %collective-permute-done.34.refs_4_ = bf16[2,3,64,128]{3,2,1,0:T(8,128)(2,1)S(1)} collective-permute-done((bf16[2,3,64,128]{3,2,1,0:T(8,128)(2,1)S(1)}, bf16[2,3,64,128]{3,2,1,0:T(8,128)(2,1)S(1)}, u32[]{:S(2)}, u32[]{:S(2)}) %collective-permute-start.34) | collective-permute-done | bytes 98336 | tf_op jit(solution)/shard_map/ppermute | solution.py:230
  137.1 1.8 %collective-permute-start.37 = (bf16[2,256,128]{2,1,0:T(8,128)(2,1)S(1)}, bf16[2,256,128]{2,1,0:T(8,128)(2,1)S(1)}, u32[]{:S(2)}, u32[]{:S(2)}) collective-permute-start(bf16[2,256,128]{2,1,0:T(8,128)(2,1)S(1)} %get-tuple-element.103), channel_id=1, source_target_pairs={{0,24},{8,0},{16,8},{24,16},{1,25},{9,1},{17,9},{25,17},{2,26},{10... | collective-permute-start | bytes 393224 | tf_op jit(solution)/shard_map/ppermute | solution.py:222
  139.1 2.0 %collective-permute-done.29.refs_3_ = bf16[2,256,128]{2,1,0:T(8,128)(2,1)S(1)} collective-permute-done((bf16[2,256,128]{2,1,0:T(8,128)(2,1)S(1)}, bf16[2,256,128]{2,1,0:T(8,128)(2,1)S(1)}, u32[]{:S(2)}, u32[]{:S(2)}) %collective-permute-start.29) | collective-permute-done | bytes 131104 | tf_op jit(solution)/shard_map/ppermute | solution.py:222
  141.1 1.6 %collective-permute-done.37.refs_5_ = bf16[2,256,128]{2,1,0:T(8,128)(2,1)S(1)} collective-permute-done((bf16[2,256,128]{2,1,0:T(8,128)(2,1)S(1)}, bf16[2,256,128]{2,1,0:T(8,128)(2,1)S(1)}, u32[]{:S(2)}, u32[]{:S(2)}) %collective-permute-start.37) | collective-permute-done | bytes 131104 | tf_op jit(solution)/shard_map/ppermute | solution.py:222
  142.7 3.1 %collective-permute-done.38.refs_6_ = bf16[2,256,128]{2,1,0:T(8,128)(2,1)S(1)} collective-permute-done((bf16[2,256,128]{2,1,0:T(8,128)(2,1)S(1)}, bf16[2,256,128]{2,1,0:T(8,128)(2,1)S(1)}, u32[]{:S(2)}, u32[]{:S(2)}) %collective-permute-start.38) | collective-permute-done | bytes 131104 | tf_op jit(solution)/shard_map/ppermute | solution.py:222
  146.3 1.7 %join.1 = (bf16[256,1024]{1,0:T(8,128)(2,1)}, bf16[256,1024]{1,0:T(8,128)(2,1)}) custom-call(s32[2]{0:T(128)S(1)} %pad_add_fusion.place, bf16[2,256,128]{2,1,0:T(8,128)(2,1)S(1)} %get-tuple-element.90.refs_0_, bf16[2,256,128]{2,1,0:T(8,128)(2,1)S(1)} %collective-permute-done.27.refs_1_, bf16[2,256,128]{2,1,0:T(8,128)(2,1)S(1)} %collective-permute-done.28.refs_2_, ...), custom_call_target="tpu_custom_call" | custom-call | tf_op jit(solution)/shard_map/join/pallas_call | solution.py:166
  (69 shorter events, 12.1 us)
Async XLA Ops:
  0.7 1.0 copy-start
  1.8 1.0 copy-start.2
  3.5 15.9 %collective-permute-start.10 = (bf16[2,256,128]{2,1,0:T(8,128)(2,1)S(1)}, bf16[2,256,128]{2,1,0:T(8,128)(2,1)S(1)}, u32[]{:S(2)}, u32[]{:S(2)}) collective-permute-start(bf16[2,256,128]{2,1,0:T(8,128)(2,1)S(1)} %get-tuple-element.68), channel_id=1, source_target_pairs={{0,8},{8,16},{16,24},{24,0},{1,9},{9,17},{17,25},{25,1},{2,10},{10... | collective-permute-start | bytes 393224 | tf_op jit(solution)/shard_map/ppermute | solution.py:222
  4.0 19.6 %collective-permute-start.11 = (bf16[2,256,128]{2,1,0:T(8,128)(2,1)S(1)}, bf16[2,256,128]{2,1,0:T(8,128)(2,1)S(1)}, u32[]{:S(2)}, u32[]{:S(2)}) collective-permute-start(bf16[2,256,128]{2,1,0:T(8,128)(2,1)S(1)} %get-tuple-element.69), channel_id=1, source_target_pairs={{0,16},{8,24},{16,0},{24,8},{1,17},{9,25},{17,1},{25,9},{2,18},{10... | collective-permute-start | bytes 393224 | tf_op jit(solution)/shard_map/ppermute | solution.py:222
  6.6 17.0 %collective-permute-start.12 = (bf16[2,256,128]{2,1,0:T(8,128)(2,1)S(1)}, bf16[2,256,128]{2,1,0:T(8,128)(2,1)S(1)}, u32[]{:S(2)}, u32[]{:S(2)}) collective-permute-start(bf16[2,256,128]{2,1,0:T(8,128)(2,1)S(1)} %get-tuple-element.70), channel_id=1, source_target_pairs={{0,24},{8,0},{16,8},{24,16},{1,25},{9,1},{17,9},{25,17},{2,26},{10... | collective-permute-start | bytes 393224 | tf_op jit(solution)/shard_map/ppermute | solution.py:222
  10.1 12.2 %all-to-all-start = ((s32[8,1,3]{2,1,0:T(1,128)}), s32[8,1,3]{2,1,0:T(1,128)S(1)}, u32[]{:S(2)}, u32[]{:S(2)}) async-start(s32[8,1,3]{2,1,0:T(1,128)} %copy.18), calls=%async_computation | async-start | bytes 8192 | tf_op jit(solution)/shard_map/all_to_all | solution.py:263
  15.9 1.0 copy-start.1
  17.0 1.0 copy-start.3
  18.7 11.6 %collective-permute-start = (bf16[2,256,128]{2,1,0:T(8,128)(2,1)S(1)}, bf16[2,256,128]{2,1,0:T(8,128)(2,1)S(1)}, u32[]{:S(2)}, u32[]{:S(2)}) collective-permute-start(bf16[2,256,128]{2,1,0:T(8,128)(2,1)S(1)} %get-tuple-element.57), channel_id=1, source_target_pairs={{0,8},{8,16},{16,24},{24,0},{1,9},{9,17},{17,25},{25,1},{2,10},{10... | collective-permute-start | bytes 393224 | tf_op jit(solution)/shard_map/ppermute | solution.py:222
  18.8 15.9 %collective-permute-start.1 = (bf16[2,256,128]{2,1,0:T(8,128)(2,1)S(1)}, bf16[2,256,128]{2,1,0:T(8,128)(2,1)S(1)}, u32[]{:S(2)}, u32[]{:S(2)}) collective-permute-start(bf16[2,256,128]{2,1,0:T(8,128)(2,1)S(1)} %get-tuple-element.58), channel_id=1, source_target_pairs={{0,16},{8,24},{16,0},{24,8},{1,17},{9,25},{17,1},{25,9},{2,18},{10... | collective-permute-start | bytes 393224 | tf_op jit(solution)/shard_map/ppermute | solution.py:222
  19.4 17.2 %collective-permute-start.2 = (bf16[2,256,128]{2,1,0:T(8,128)(2,1)S(1)}, bf16[2,256,128]{2,1,0:T(8,128)(2,1)S(1)}, u32[]{:S(2)}, u32[]{:S(2)}) collective-permute-start(bf16[2,256,128]{2,1,0:T(8,128)(2,1)S(1)} %get-tuple-element.59), channel_id=1, source_target_pairs={{0,24},{8,0},{16,8},{24,16},{1,25},{9,1},{17,9},{25,17},{2,26},{10... | collective-permute-start | bytes 393224 | tf_op jit(solution)/shard_map/ppermute | solution.py:222
  24.2 13.6 %collective-permute-start.13 = (bf16[2,3,64,128]{3,2,1,0:T(8,128)(2,1)S(1)}, bf16[2,3,64,128]{3,2,1,0:T(8,128)(2,1)S(1)}, u32[]{:S(2)}, u32[]{:S(2)}) collective-permute-start(bf16[2,3,64,128]{3,2,1,0:T(8,128)(2,1)S(1)} %get-tuple-element.71), channel_id=1, source_target_pairs={{0,1},{1,2},{2,3},{3,4},{4,5},{5,6},{6,7},{8,9},{9,10},{10,11},{11... | collective-permute-start | bytes 294920 | tf_op jit(solution)/shard_map/ppermute | solution.py:226
  26.8 12.4 %collective-permute-start.14 = (bf16[2,3,64,128]{3,2,1,0:T(8,128)(2,1)S(1)}, bf16[2,3,64,128]{3,2,1,0:T(8,128)(2,1)S(1)}, u32[]{:S(2)}, u32[]{:S(2)}) collective-permute-start(bf16[2,3,64,128]{3,2,1,0:T(8,128)(2,1)S(1)} %get-tuple-element.72), channel_id=1, source_target_pairs={{0,2},{1,3},{2,4},{3,5},{4,6},{5,7},{8,10},{9,11},{10,12},{11,13},... | collective-permute-start | bytes 294920 | tf_op jit(solution)/shard_map/ppermute | solution.py:226
  30.3 10.8 %collective-permute-start.15 = (bf16[2,3,64,128]{3,2,1,0:T(8,128)(2,1)S(1)}, bf16[2,3,64,128]{3,2,1,0:T(8,128)(2,1)S(1)}, u32[]{:S(2)}, u32[]{:S(2)}) collective-permute-start(bf16[2,3,64,128]{3,2,1,0:T(8,128)(2,1)S(1)} %get-tuple-element.73), channel_id=1, source_target_pairs={{0,3},{1,4},{2,5},{3,6},{4,7},{8,11},{9,12},{10,13},{11,14},{12,15... | collective-permute-start | bytes 294920 | tf_op jit(solution)/shard_map/ppermute | solution.py:226
  34.6 8.7 %collective-permute-start.16 = (bf16[2,3,64,128]{3,2,1,0:T(8,128)(2,1)S(1)}, bf16[2,3,64,128]{3,2,1,0:T(8,128)(2,1)S(1)}, u32[]{:S(2)}, u32[]{:S(2)}) collective-permute-start(bf16[2,3,64,128]{3,2,1,0:T(8,128)(2,1)S(1)} %get-tuple-element.74), channel_id=1, source_target_pairs={{0,4},{1,5},{2,6},{3,7},{8,12},{9,13},{10,14},{11,15},{16,20},{17,... | collective-permute-start | bytes 294920 | tf_op jit(solution)/shard_map/ppermute | solution.py:226
  36.6 14.3 %collective-permute-start.17 = (bf16[2,3,64,128]{3,2,1,0:T(8,128)(2,1)S(1)}, bf16[2,3,64,128]{3,2,1,0:T(8,128)(2,1)S(1)}, u32[]{:S(2)}, u32[]{:S(2)}) collective-permute-start(bf16[2,3,64,128]{3,2,1,0:T(8,128)(2,1)S(1)} %get-tuple-element.75), channel_id=1, source_target_pairs={{0,5},{1,6},{2,7},{8,13},{9,14},{10,15},{16,21},{17,22},{18,23},{2... | collective-permute-start | bytes 294920 | tf_op jit(solution)/shard_map/ppermute | solution.py:226
  37.9 19.3 %collective-permute-start.18 = (bf16[2,3,64,128]{3,2,1,0:T(8,128)(2,1)S(1)}, bf16[2,3,64,128]{3,2,1,0:T(8,128)(2,1)S(1)}, u32[]{:S(2)}, u32[]{:S(2)}) collective-permute-start(bf16[2,3,64,128]{3,2,1,0:T(8,128)(2,1)S(1)} %get-tuple-element.76), channel_id=1, source_target_pairs={{0,6},{1,7},{8,14},{9,15},{16,22},{17,23},{24,30},{25,31}} | collective-permute-start | bytes 294920 | tf_op jit(solution)/shard_map/ppermute | solution.py:226
  39.2 19.3 %collective-permute-start.19 = (bf16[2,3,64,128]{3,2,1,0:T(8,128)(2,1)S(1)}, bf16[2,3,64,128]{3,2,1,0:T(8,128)(2,1)S(1)}, u32[]{:S(2)}, u32[]{:S(2)}) collective-permute-start(bf16[2,3,64,128]{3,2,1,0:T(8,128)(2,1)S(1)} %get-tuple-element.77), channel_id=1, source_target_pairs={{0,7},{8,15},{16,23},{24,31}} | collective-permute-start | bytes 294920 | tf_op jit(solution)/shard_map/ppermute | solution.py:226
  41.2 34.3 %collective-permute-start.3 = (bf16[2,3,64,128]{3,2,1,0:T(8,128)(2,1)S(1)}, bf16[2,3,64,128]{3,2,1,0:T(8,128)(2,1)S(1)}, u32[]{:S(2)}, u32[]{:S(2)}) collective-permute-start(bf16[2,3,64,128]{3,2,1,0:T(8,128)(2,1)S(1)} %get-tuple-element.60), channel_id=1, source_target_pairs={{0,1},{1,2},{2,3},{3,4},{4,5},{5,6},{6,7},{8,9},{9,10},{10,11},{11... | collective-permute-start | bytes 294920 | tf_op jit(solution)/shard_map/ppermute | solution.py:226
  43.3 33.4 %collective-permute-start.4 = (bf16[2,3,64,128]{3,2,1,0:T(8,128)(2,1)S(1)}, bf16[2,3,64,128]{3,2,1,0:T(8,128)(2,1)S(1)}, u32[]{:S(2)}, u32[]{:S(2)}) collective-permute-start(bf16[2,3,64,128]{3,2,1,0:T(8,128)(2,1)S(1)} %get-tuple-element.61), channel_id=1, source_target_pairs={{0,2},{1,3},{2,4},{3,5},{4,6},{5,7},{8,10},{9,11},{10,12},{11,13},... | collective-permute-start | bytes 294920 | tf_op jit(solution)/shard_map/ppermute | solution.py:226
  50.9 27.1 %collective-permute-start.5 = (bf16[2,3,64,128]{3,2,1,0:T(8,128)(2,1)S(1)}, bf16[2,3,64,128]{3,2,1,0:T(8,128)(2,1)S(1)}, u32[]{:S(2)}, u32[]{:S(2)}) collective-permute-start(bf16[2,3,64,128]{3,2,1,0:T(8,128)(2,1)S(1)} %get-tuple-element.62), channel_id=1, source_target_pairs={{0,3},{1,4},{2,5},{3,6},{4,7},{8,11},{9,12},{10,13},{11,14},{12,15... | collective-permute-start | bytes 294920 | tf_op jit(solution)/shard_map/ppermute | solution.py:226
  57.1 22.2 %collective-permute-start.6 = (bf16[2,3,64,128]{3,2,1,0:T(8,128)(2,1)S(1)}, bf16[2,3,64,128]{3,2,1,0:T(8,128)(2,1)S(1)}, u32[]{:S(2)}, u32[]{:S(2)}) collective-permute-start(bf16[2,3,64,128]{3,2,1,0:T(8,128)(2,1)S(1)} %get-tuple-element.63), channel_id=1, source_target_pairs={{0,4},{1,5},{2,6},{3,7},{8,12},{9,13},{10,14},{11,15},{16,20},{17,... | collective-permute-start | bytes 294920 | tf_op jit(solution)/shard_map/ppermute | solution.py:226
  58.5 22.1 %collective-permute-start.7 = (bf16[2,3,64,128]{3,2,1,0:T(8,128)(2,1)S(1)}, bf16[2,3,64,128]{3,2,1,0:T(8,128)(2,1)S(1)}, u32[]{:S(2)}, u32[]{:S(2)}) collective-permute-start(bf16[2,3,64,128]{3,2,1,0:T(8,128)(2,1)S(1)} %get-tuple-element.64), channel_id=1, source_target_pairs={{0,5},{1,6},{2,7},{8,13},{9,14},{10,15},{16,21},{17,22},{18,23},{2... | collective-permute-start | bytes 294920 | tf_op jit(solution)/shard_map/ppermute | solution.py:226
  75.4 6.5 %collective-permute-start.8 = (bf16[2,3,64,128]{3,2,1,0:T(8,128)(2,1)S(1)}, bf16[2,3,64,128]{3,2,1,0:T(8,128)(2,1)S(1)}, u32[]{:S(2)}, u32[]{:S(2)}) collective-permute-start(bf16[2,3,64,128]{3,2,1,0:T(8,128)(2,1)S(1)} %get-tuple-element.65), channel_id=1, source_target_pairs={{0,6},{1,7},{8,14},{9,15},{16,22},{17,23},{24,30},{25,31}} | collective-permute-start | bytes 294920 | tf_op jit(solution)/shard_map/ppermute | solution.py:226
  76.7 6.5 %collective-permute-start.9 = (bf16[2,3,64,128]{3,2,1,0:T(8,128)(2,1)S(1)}, bf16[2,3,64,128]{3,2,1,0:T(8,128)(2,1)S(1)}, u32[]{:S(2)}, u32[]{:S(2)}) collective-permute-start(bf16[2,3,64,128]{3,2,1,0:T(8,128)(2,1)S(1)} %get-tuple-element.66), channel_id=1, source_target_pairs={{0,7},{8,15},{16,23},{24,31}} | collective-permute-start | bytes 294920 | tf_op jit(solution)/shard_map/ppermute | solution.py:226
  78.0 6.5 %collective-permute-start.20 = (bf16[2,3,64,128]{3,2,1,0:T(8,128)(2,1)S(1)}, bf16[2,3,64,128]{3,2,1,0:T(8,128)(2,1)S(1)}, u32[]{:S(2)}, u32[]{:S(2)}) collective-permute-start(bf16[2,3,64,128]{3,2,1,0:T(8,128)(2,1)S(1)} %get-tuple-element.83), channel_id=1, source_target_pairs={{1,0},{2,1},{3,2},{4,3},{5,4},{6,5},{7,6},{9,8},{10,9},{11,10},{12... | collective-permute-start | bytes 294920 | tf_op jit(solution)/shard_map/ppermute | solution.py:230
  79.4 7.8 %collective-permute-start.21 = (bf16[2,3,64,128]{3,2,1,0:T(8,128)(2,1)S(1)}, bf16[2,3,64,128]{3,2,1,0:T(8,128)(2,1)S(1)}, u32[]{:S(2)}, u32[]{:S(2)}) collective-permute-start(bf16[2,3,64,128]{3,2,1,0:T(8,128)(2,1)S(1)} %get-tuple-element.84), channel_id=1, source_target_pairs={{2,0},{3,1},{4,2},{5,3},{6,4},{7,5},{10,8},{11,9},{12,10},{13,11},... | collective-permute-start | bytes 294920 | tf_op jit(solution)/shard_map/ppermute | solution.py:230
  80.7 23.4 %collective-permute-start.22 = (bf16[2,3,64,128]{3,2,1,0:T(8,128)(2,1)S(1)}, bf16[2,3,64,128]{3,2,1,0:T(8,128)(2,1)S(1)}, u32[]{:S(2)}, u32[]{:S(2)}) collective-permute-start(bf16[2,3,64,128]{3,2,1,0:T(8,128)(2,1)S(1)} %get-tuple-element.85), channel_id=1, source_target_pairs={{3,0},{4,1},{5,2},{6,3},{7,4},{11,8},{12,9},{13,10},{14,11},{15,12... | collective-permute-start | bytes 294920 | tf_op jit(solution)/shard_map/ppermute | solution.py:230
  82.0 23.3 %collective-permute-start.23 = (bf16[2,3,64,128]{3,2,1,0:T(8,128)(2,1)S(1)}, bf16[2,3,64,128]{3,2,1,0:T(8,128)(2,1)S(1)}, u32[]{:S(2)}, u32[]{:S(2)}) collective-permute-start(bf16[2,3,64,128]{3,2,1,0:T(8,128)(2,1)S(1)} %get-tuple-element.86), channel_id=1, source_target_pairs={{4,0},{5,1},{6,2},{7,3},{12,8},{13,9},{14,10},{15,11},{20,16},{21,... | collective-permute-start | bytes 294920 | tf_op jit(solution)/shard_map/ppermute | solution.py:230
  83.3 23.3 %collective-permute-start.24 = (bf16[2,3,64,128]{3,2,1,0:T(8,128)(2,1)S(1)}, bf16[2,3,64,128]{3,2,1,0:T(8,128)(2,1)S(1)}, u32[]{:S(2)}, u32[]{:S(2)}) collective-permute-start(bf16[2,3,64,128]{3,2,1,0:T(8,128)(2,1)S(1)} %get-tuple-element.87), channel_id=1, source_target_pairs={{5,0},{6,1},{7,2},{13,8},{14,9},{15,10},{21,16},{22,17},{23,18},{2... | collective-permute-start | bytes 294920 | tf_op jit(solution)/shard_map/ppermute | solution.py:230
  84.6 23.3 %collective-permute-start.25 = (bf16[2,3,64,128]{3,2,1,0:T(8,128)(2,1)S(1)}, bf16[2,3,64,128]{3,2,1,0:T(8,128)(2,1)S(1)}, u32[]{:S(2)}, u32[]{:S(2)}) collective-permute-start(bf16[2,3,64,128]{3,2,1,0:T(8,128)(2,1)S(1)} %get-tuple-element.88), channel_id=1, source_target_pairs={{6,0},{7,1},{14,8},{15,9},{22,16},{23,17},{30,24},{31,25}} | collective-permute-start | bytes 294920 | tf_op jit(solution)/shard_map/ppermute | solution.py:230
  87.1 20.8 %collective-permute-start.26 = (bf16[2,3,64,128]{3,2,1,0:T(8,128)(2,1)S(1)}, bf16[2,3,64,128]{3,2,1,0:T(8,128)(2,1)S(1)}, u32[]{:S(2)}, u32[]{:S(2)}) collective-permute-start(bf16[2,3,64,128]{3,2,1,0:T(8,128)(2,1)S(1)} %get-tuple-element.89), channel_id=1, source_target_pairs={{7,0},{15,8},{23,16},{31,24}} | collective-permute-start | bytes 294920 | tf_op jit(solution)/shard_map/ppermute | solution.py:230
  104.0 7.6 %collective-permute-start.30 = (bf16[2,3,64,128]{3,2,1,0:T(8,128)(2,1)S(1)}, bf16[2,3,64,128]{3,2,1,0:T(8,128)(2,1)S(1)}, u32[]{:S(2)}, u32[]{:S(2)}) collective-permute-start(bf16[2,3,64,128]{3,2,1,0:T(8,128)(2,1)S(1)} %get-tuple-element.95), channel_id=1, source_target_pairs={{1,0},{2,1},{3,2},{4,3},{5,4},{6,5},{7,6},{9,8},{10,9},{11,10},{12... | collective-permute-start | bytes 294920 | tf_op jit(solution)/shard_map/ppermute | solution.py:230
  105.3 13.0 %collective-permute-start.31 = (bf16[2,3,64,128]{3,2,1,0:T(8,128)(2,1)S(1)}, bf16[2,3,64,128]{3,2,1,0:T(8,128)(2,1)S(1)}, u32[]{:S(2)}, u32[]{:S(2)}) collective-permute-start(bf16[2,3,64,128]{3,2,1,0:T(8,128)(2,1)S(1)} %get-tuple-element.96), channel_id=1, source_target_pairs={{2,0},{3,1},{4,2},{5,3},{6,4},{7,5},{10,8},{11,9},{12,10},{13,11},... | collective-permute-start | bytes 294920 | tf_op jit(solution)/shard_map/ppermute | solution.py:230
  106.6 15.1 %collective-permute-start.32 = (bf16[2,3,64,128]{3,2,1,0:T(8,128)(2,1)S(1)}, bf16[2,3,64,128]{3,2,1,0:T(8,128)(2,1)S(1)}, u32[]{:S(2)}, u32[]{:S(2)}) collective-permute-start(bf16[2,3,64,128]{3,2,1,0:T(8,128)(2,1)S(1)} %get-tuple-element.97), channel_id=1, source_target_pairs={{3,0},{4,1},{5,2},{6,3},{7,4},{11,8},{12,9},{13,10},{14,11},{15,12... | collective-permute-start | bytes 294920 | tf_op jit(solution)/shard_map/ppermute | solution.py:230
  108.8 30.1 %collective-permute-start.27 = (bf16[2,256,128]{2,1,0:T(8,128)(2,1)S(1)}, bf16[2,256,128]{2,1,0:T(8,128)(2,1)S(1)}, u32[]{:S(2)}, u32[]{:S(2)}) collective-permute-start(bf16[2,256,128]{2,1,0:T(8,128)(2,1)S(1)} %get-tuple-element.91), channel_id=1, source_target_pairs={{0,24},{8,0},{16,8},{24,16},{1,25},{9,1},{17,9},{25,17},{2,26},{10... | collective-permute-start | bytes 393224 | tf_op jit(solution)/shard_map/ppermute | solution.py:222
  108.9 23.3 %collective-permute-start.33 = (bf16[2,3,64,128]{3,2,1,0:T(8,128)(2,1)S(1)}, bf16[2,3,64,128]{3,2,1,0:T(8,128)(2,1)S(1)}, u32[]{:S(2)}, u32[]{:S(2)}) collective-permute-start(bf16[2,3,64,128]{3,2,1,0:T(8,128)(2,1)S(1)} %get-tuple-element.98), channel_id=1, source_target_pairs={{4,0},{5,1},{6,2},{7,3},{12,8},{13,9},{14,10},{15,11},{20,16},{21,... | collective-permute-start | bytes 294920 | tf_op jit(solution)/shard_map/ppermute | solution.py:230
  111.6 24.7 %collective-permute-start.34 = (bf16[2,3,64,128]{3,2,1,0:T(8,128)(2,1)S(1)}, bf16[2,3,64,128]{3,2,1,0:T(8,128)(2,1)S(1)}, u32[]{:S(2)}, u32[]{:S(2)}) collective-permute-start(bf16[2,3,64,128]{3,2,1,0:T(8,128)(2,1)S(1)} %get-tuple-element.99), channel_id=1, source_target_pairs={{5,0},{6,1},{7,2},{13,8},{14,9},{15,10},{21,16},{22,17},{23,18},{2... | collective-permute-start | bytes 294920 | tf_op jit(solution)/shard_map/ppermute | solution.py:230
  118.4 17.9 %collective-permute-start.35 = (bf16[2,3,64,128]{3,2,1,0:T(8,128)(2,1)S(1)}, bf16[2,3,64,128]{3,2,1,0:T(8,128)(2,1)S(1)}, u32[]{:S(2)}, u32[]{:S(2)}) collective-permute-start(bf16[2,3,64,128]{3,2,1,0:T(8,128)(2,1)S(1)} %get-tuple-element.100), channel_id=1, source_target_pairs={{6,0},{7,1},{14,8},{15,9},{22,16},{23,17},{30,24},{31,25}} | collective-permute-start | bytes 294920 | tf_op jit(solution)/shard_map/ppermute | solution.py:230
  121.8 14.5 %collective-permute-start.36 = (bf16[2,3,64,128]{3,2,1,0:T(8,128)(2,1)S(1)}, bf16[2,3,64,128]{3,2,1,0:T(8,128)(2,1)S(1)}, u32[]{:S(2)}, u32[]{:S(2)}) collective-permute-start(bf16[2,3,64,128]{3,2,1,0:T(8,128)(2,1)S(1)} %get-tuple-element.101), channel_id=1, source_target_pairs={{7,0},{15,8},{23,16},{31,24}} | collective-permute-start | bytes 294920 | tf_op jit(solution)/shard_map/ppermute | solution.py:230
  132.2 6.9 %collective-permute-start.28 = (bf16[2,256,128]{2,1,0:T(8,128)(2,1)S(1)}, bf16[2,256,128]{2,1,0:T(8,128)(2,1)S(1)}, u32[]{:S(2)}, u32[]{:S(2)}) collective-permute-start(bf16[2,256,128]{2,1,0:T(8,128)(2,1)S(1)} %get-tuple-element.92), channel_id=1, source_target_pairs={{0,16},{8,24},{16,0},{24,8},{1,17},{9,25},{17,1},{25,9},{2,18},{10... | collective-permute-start | bytes 393224 | tf_op jit(solution)/shard_map/ppermute | solution.py:222
  136.3 4.8 %collective-permute-start.29 = (bf16[2,256,128]{2,1,0:T(8,128)(2,1)S(1)}, bf16[2,256,128]{2,1,0:T(8,128)(2,1)S(1)}, u32[]{:S(2)}, u32[]{:S(2)}) collective-permute-start(bf16[2,256,128]{2,1,0:T(8,128)(2,1)S(1)} %get-tuple-element.93), channel_id=1, source_target_pairs={{0,8},{8,16},{16,24},{24,0},{1,9},{9,17},{17,25},{25,1},{2,10},{10... | collective-permute-start | bytes 393224 | tf_op jit(solution)/shard_map/ppermute | solution.py:222
  137.1 5.6 %collective-permute-start.37 = (bf16[2,256,128]{2,1,0:T(8,128)(2,1)S(1)}, bf16[2,256,128]{2,1,0:T(8,128)(2,1)S(1)}, u32[]{:S(2)}, u32[]{:S(2)}) collective-permute-start(bf16[2,256,128]{2,1,0:T(8,128)(2,1)S(1)} %get-tuple-element.103), channel_id=1, source_target_pairs={{0,24},{8,0},{16,8},{24,16},{1,25},{9,1},{17,9},{25,17},{2,26},{10... | collective-permute-start | bytes 393224 | tf_op jit(solution)/shard_map/ppermute | solution.py:222
  138.9 6.9 %collective-permute-start.38 = (bf16[2,256,128]{2,1,0:T(8,128)(2,1)S(1)}, bf16[2,256,128]{2,1,0:T(8,128)(2,1)S(1)}, u32[]{:S(2)}, u32[]{:S(2)}) collective-permute-start(bf16[2,256,128]{2,1,0:T(8,128)(2,1)S(1)} %get-tuple-element.104), channel_id=1, source_target_pairs={{0,16},{8,24},{16,0},{24,8},{1,17},{9,25},{17,1},{25,9},{2,18},{10... | collective-permute-start | bytes 393224 | tf_op jit(solution)/shard_map/ppermute | solution.py:222
  138.9 7.4 %collective-permute-start.39 = (bf16[2,256,128]{2,1,0:T(8,128)(2,1)S(1)}, bf16[2,256,128]{2,1,0:T(8,128)(2,1)S(1)}, u32[]{:S(2)}, u32[]{:S(2)}) collective-permute-start(bf16[2,256,128]{2,1,0:T(8,128)(2,1)S(1)} %get-tuple-element.105), channel_id=1, source_target_pairs={{0,8},{8,16},{16,24},{24,0},{1,9},{9,17},{17,25},{25,1},{2,10},{10... | collective-permute-start | bytes 393224 | tf_op jit(solution)/shard_map/ppermute | solution.py:222

commit v3 on v2

--- a/solution.py
+++ b/solution.py
@@ -31,24 +31,38 @@
     return pltpu.CompilerParams(vmem_limit_bytes=VMEM_LIMIT, **kw)
 
 
-def split_kernel(place, *refs):
-    k_ref, v_ref, *outs = refs
-    heads = len(outs)
-    me = place[1]
-    h = place[2]
-    head_count = k_ref.shape[1] // heads // HEAD_DIM
-    for r, out in enumerate(outs):
-        peer = lax.rem(me + r, heads)
-        col = pl.multiple_of((peer * head_count + h) * HEAD_DIM, HEAD_DIM)
-        out[0] = k_ref[:, pl.ds(col, HEAD_DIM)]
-        out[1] = v_ref[:, pl.ds(col, HEAD_DIM)]
+def partner(me, r, count):
+    return me ^ r if count & (count - 1) == 0 else (me + r) % count
+
+
+def origin(me, r, count):
+    return me ^ r if count & (count - 1) == 0 else (me + count - r) % count
+
+
+def split_kernel(place, k_ref, v_ref, *refs, heads):
+    *outs, sem = refs
+    head_count = len(outs) // heads
+    copies = []
+    for h in range(head_count):
+        for r in range(heads):
+            peer = partner(place[1], r, heads)
+            col = pl.multiple_of((peer * head_count + h) * HEAD_DIM, HEAD_DIM)
+            for kv, ref in enumerate((k_ref, v_ref)):
+                at = h * heads + r
+                copies.append(
+                    pltpu.make_async_copy(ref.at[:, pl.ds(col, HEAD_DIM)], outs[at].at[kv], sem.at[2 * at + kv])
+                )
+    for copy in copies:
+        copy.start()
+    for copy in copies:
+        copy.wait()
 
 
 def fill_table(place, own, table):
     heads = len(own)
     per_quarter = own[0].shape[1] // BLK
     for r in range(heads):
-        first = lax.rem(place[1] + heads - r, heads) * per_quarter
+        first = origin(place[1], r, heads) * per_quarter
         for kv in range(2):
             for j in range(per_quarter):
                 table[kv, first + j] = own[r][kv, j * BLK : (j + 1) * BLK, :]
@@ -57,11 +71,9 @@
 def pick_kernel(place, asked, *refs, heads):
     own, (*outs, table) = refs[:heads], refs[heads:]
     fill_table(place, own, table)
-    shard_count = len(outs) + 1
-    for d, out in enumerate(outs, 1):
-        c = lax.rem(place[0] + d, shard_count)
+    for d, out in enumerate(outs):
         for s in range(CAP):
-            block = asked[c * CAP + s]
+            block = asked[d * CAP + s]
             for kv in range(2):
                 out[kv, s] = table[kv, block]
 
@@ -134,14 +146,13 @@
     heads = len(outs)
     per_quarter = outs[0].shape[1] // BLK
     total[...] = near[...]
-    for d in range(1, steps + 1):
-        c = lax.rem(place[0] + d, steps + 1)
+    for d in range(steps):
         for s in range(CAP):
-            block = asked[c * CAP + s]
+            block = asked[d * CAP + s]
             for kv in range(2):
-                total[kv, block] += back[d - 1][kv, s].astype(jnp.float32)
+                total[kv, block] += back[d][kv, s].astype(jnp.float32)
     for r in range(heads):
-        first = lax.rem(place[1] + heads - r, heads) * per_quarter
+        first = origin(place[1], r, heads) * per_quarter
         for kv in range(2):
             for j in range(per_quarter):
                 outs[r][kv, j * BLK : (j + 1) * BLK, :] = total[kv, first + j].astype(jnp.bfloat16)
@@ -152,7 +163,7 @@
     head_count = len(pieces) // heads
     for h in range(head_count):
         for r in range(heads):
-            peer = lax.rem(place[1] + r, heads)
+            peer = partner(place[1], r, heads)
             col = pl.multiple_of((peer * head_count + h) * HEAD_DIM, HEAD_DIM)
             k_ref[:, pl.ds(col, HEAD_DIM)] = pieces[h * heads + r][0]
             v_ref[:, pl.ds(col, HEAD_DIM)] = pieces[h * heads + r][1]
@@ -218,16 +229,18 @@
     )(place, source, queries, out_grad, *arrays, *earlier)
 
 
-def turn(x, axis, count, by):
-    return lax.ppermute(x, axis, [(i, (i + by) % count) for i in range(count)])
-
-
-def up(x, count, by):
-    return lax.ppermute(x, "ctx", [(i, i + by) for i in range(count - by)])
-
-
-def down(x, count, by):
-    return lax.ppermute(x, "ctx", [(i + by, i) for i in range(count - by)])
+def send(x, axis, count, r):
+    return lax.ppermute(x, axis, [(i, partner(i, r, count)) for i in range(count)])
+
+
+def send_back(x, axis, count, r):
+    return lax.ppermute(x, axis, [(i, origin(i, r, count)) for i in range(count)])
+
+
+def rank_of(hits):
+    n = hits.shape[-1]
+    before = jnp.arange(n)[:, None] < jnp.arange(n)[None, :]
+    return jnp.sum((hits[:, :, None] & before[None]).astype(jnp.int32), axis=1)
 
 
 def per_device(queries, key_states, value_states, block_lists, out_grad):
@@ -239,28 +252,50 @@
     head_count = key_states.shape[1] // heads // HEAD_DIM
     head_index = lax.axis_index("head")
     place = jnp.stack([shard_index, head_index]).astype(jnp.int32)
+    inner = jnp.arange(blocks_here, dtype=jnp.int32)
+
+    flat_ids = block_lists.reshape(1, -1)
+    others = [send(flat_ids, "ctx", shard_count, d) for d in range(1, shard_count)]
 
     piece = jax.ShapeDtypeStruct((2, quarter, HEAD_DIM), jnp.bfloat16)
+    pieces = pl.pallas_call(
+        functools.partial(split_kernel, heads=heads),
+        grid_spec=pltpu.PrefetchScalarGridSpec(
+            num_scalar_prefetch=1,
+            grid=(1,),
+            in_specs=[pl.BlockSpec(memory_space=pl.ANY)] * 2,
+            out_specs=[pl.BlockSpec(memory_space=pl.ANY)] * (heads * head_count),
+            scratch_shapes=[pltpu.SemaphoreType.DMA((2 * heads * head_count,))],
+        ),
+        out_shape=[piece] * (heads * head_count),
+        compiler_params=params(),
+        name="split",
+    )(place, key_states, value_states)
     own = []
     for h in range(head_count):
-        here = jnp.concatenate([place, jnp.full((1,), h, jnp.int32)])
-        parts = call(split_kernel, [here], [key_states, value_states], [piece] * heads, name="split")
-        own.append([parts[0]] + [turn(parts[r], "head", heads, r) for r in range(1, heads)])
-
-    flat_ids = block_lists.reshape(-1)
-    owner_shard = flat_ids // blocks_here
-    inner_index = flat_ids % blocks_here
+        parts = pieces[h * heads : (h + 1) * heads]
+        own.append([parts[0]] + [send(parts[r], "head", heads, r) for r in range(1, heads)])
+
+    asked_hits = jnp.any(
+        jnp.concatenate(others)[:, :, None] == (shard_index * blocks_here + inner)[None, None, :], axis=1
+    )
+    asked_rank = rank_of(asked_hits)
+    asked = jnp.sum(
+        jnp.where(asked_hits[:, None] & (asked_rank[:, None] == jnp.arange(CAP)[None, :, None]), inner[None, None], 0),
+        axis=2,
+    ).reshape(-1)
+
+    flat_ids = flat_ids.reshape(-1)
+    owner = flat_ids // blocks_here
     every_block = jnp.arange(shard_count * blocks_here, dtype=jnp.int32)
-    hits = flat_ids[:, None] == every_block[None, :]
-    block_hits = jnp.any(hits, axis=0).reshape(shard_count, blocks_here)
-    needed = block_hits & (jnp.arange(shard_count) != shard_index)[:, None]
-    slot_rank = jnp.cumsum(needed.astype(jnp.int32), axis=1) - 1
-    slot_pick = needed[:, :, None] & (slot_rank[:, :, None] == jnp.arange(CAP)[None, None, :])
-    requests = jnp.sum(jnp.where(slot_pick, jnp.arange(blocks_here, dtype=jnp.int32)[None, :, None], 0), axis=1)
-    ref_rank = jnp.sum(jnp.where(hits, slot_rank.reshape(-1)[None, :], 0), axis=1)
-    distance = shard_index - owner_shard
-    source = jnp.where(distance == 0, inner_index, blocks_here + (distance - 1) * CAP + ref_rank)
-    asked = lax.all_to_all(requests, "ctx", split_axis=0, concat_axis=0, tiled=True).reshape(-1)
+    listed = jnp.any(flat_ids[:, None] == every_block[None, :], axis=0)
+    same_owner = owner[:, None] == (every_block // blocks_here)[None, :]
+    rank = jnp.sum((same_owner & listed[None, :] & (every_block[None, :] < flat_ids[:, None])).astype(jnp.int32), axis=1)
+    if shard_count & (shard_count - 1) == 0:
+        distance = shard_index ^ owner
+    else:
+        distance = (shard_index + shard_count - owner) % shard_count
+    source = jnp.where(distance == 0, flat_ids % blocks_here, blocks_here + (distance - 1) * CAP + rank)
 
     slots = jax.ShapeDtypeStruct((2, CAP, BLK, HEAD_DIM), jnp.bfloat16)
     table = pltpu.VMEM((2, blocks_here, BLK, HEAD_DIM), jnp.bfloat16)
@@ -269,7 +304,7 @@
         picked = call(
             functools.partial(pick_kernel, heads=heads), [place, asked], own[h], [slots] * (shard_count - 1), [table], "pick"
         )
-        far.append([up(x, shard_count, d) for d, x in enumerate(picked, 1)])
+        far.append([send(x, "ctx", shard_count, d) for d, x in enumerate(picked, 1)])
     earlier, nears, backs = [], [], []
     for h in range(head_count):
         attended, query_grad, near, *far_grad = attend(
@@ -277,7 +312,7 @@
         )
         earlier = [attended, query_grad]
         nears.append(near)
-        backs.append([down(x, shard_count, d) for d, x in enumerate(far_grad, 1)])
+        backs.append([send_back(x, "ctx", shard_count, d) for d, x in enumerate(far_grad, 1)])
     total = pltpu.VMEM((2, blocks_here, BLK, HEAD_DIM), jnp.float32)
     done = []
     for h in range(head_count):
@@ -285,7 +320,7 @@
             functools.partial(gather_sum_kernel, steps=shard_count - 1),
             [place, asked], [nears[h], *backs[h]], [piece] * heads, [total], "gather_sum",
         )
-        done.append([sums[0]] + [turn(sums[r], "head", heads, -r) for r in range(1, heads)])
+        done.append([sums[0]] + [send_back(sums[r], "head", heads, r) for r in range(1, heads)])
     pieces = [x for group in done for x in group]
     grad = jax.ShapeDtypeStruct(key_states.shape, jnp.bfloat16)
     key_grad, value_grad = call(functools.partial(join_kernel, heads=heads), [place], pieces, [grad, grad], name="join")

time: 149 us -> 140 us (0.940)
  waiting for transfers between devices: 32.1 us -> 24.9 us
  starting transfers between devices: 69.6 us -> 73.2 us
  local copies, waits for them, and re-layouts: 6.45 us -> 3.21 us
    ppermute x40 -> x47, starting transfers between devices: 63.7 us -> 73.2 us  [the longest x27 48.5 us: send(): lax.ppermute(x, axis, [(i, partner(i, r, count)) for i in range(count)])]
    all_to_all x1 -> x0, starting transfers between devices: 5.84 us -> none  [per_device(): lax.all_to_all(requests, 'ctx', split_axis=0, concat_axis=0, tiled=True)]
    ppermute x40 -> x47, waiting for transfers between devices: 30.7 us -> 24.9 us  [the longest x20 14.9 us: send_back(): lax.ppermute(x, axis, [(i, origin(i, r, count)) for i in range(count)])]
    unnamed x9 -> x5, local copies, waits for them, and re-layouts: 4.92 us -> 2.84 us
    pallas_call x7 -> x5, Pallas kernels: 6 us -> 4.7 us  [call(): pl.pallas_call(kernel, grid_spec=pltpu.PrefetchScalarGridSpec(num_scalar_...]
  transfers between devices with their start and end apart: 41 -> 47, of which waited for: 11 -> 11; matrix products, arithmetic and copies ran while one was open for 3% -> 1% of each run, Pallas kernels for 24% -> 25%
where the time goes in v3:
time: 140 us
  starting transfers between devices  73.2 us (52%)
  Pallas kernels  36.9 us (26%)
  waiting for transfers between devices  24.9 us (18%)
  local copies, waits for them, and re-layouts  3.21 us (2%)
    ppermute x27, starting transfers between devices, send(): lax.ppermute(x, axis, [(i, partner(i, r, count)) for i in range(count)])  48.5 us
    pallas_call x2, Pallas kernels, attend(): pl.pallas_call(functools.partial(attend_kernel, heads=len(own), steps=len...  31.2 us
    ppermute x20, starting transfers between devices, send_back(): lax.ppermute(x, axis, [(i, origin(i, r, count)) for i in range(count)])  24.7 us
    ppermute x20, waiting for transfers between devices, send_back(): lax.ppermute(x, axis, [(i, origin(i, r, count)) for i in range(count)])  14.9 us
    ppermute x27, waiting for transfers between devices, send(): lax.ppermute(x, axis, [(i, partner(i, r, count)) for i in range(count)])  10 us
    pallas_call x5, Pallas kernels, call(): pl.pallas_call(kernel, grid_spec=pltpu.PrefetchScalarGridSpec(num_scalar_...  4.7 us
    unnamed x5, local copies, waits for them, and re-layouts  2.84 us
  transfers between devices with their start and end apart: 47, of which 11 were waited for; matrix products, arithmetic and copies ran while one was open for 1% of the time, Pallas kernels for 25%

profile of v3, /device:TPU:0, one launch (start us, length us, event | category | flops | bytes accessed | tf_op | source)
XLA Modules:
  0.0 139.9 jit_solution(16092473491154010213)
XLA Ops:
  1.5 6.1 %collective-permute-start.9 = (s32[1,128]{1,0:T(1,128)S(1)}, s32[1,128]{1,0:T(1,128)S(1)}, u32[]{:S(2)}, u32[]{:S(2)}) collective-permute-start(s32[1,128]{1,0:T(1,128)S(1)} %reshape.77), channel_id=1, source_target_pairs={{0,7},{1,6},{2,5},{3,4},{4,3},{5,2},{6,1},{7,0},{8,15},{9,14},{10,... | collective-permute-start | bytes 1544 | tf_op jit(solution)/shard_map/ppermute | solution.py:233
  8.5 2.0 %collective-permute-start.6 = (s32[1,128]{1,0:T(1,128)S(1)}, s32[1,128]{1,0:T(1,128)S(1)}, u32[]{:S(2)}, u32[]{:S(2)}) collective-permute-start(s32[1,128]{1,0:T(1,128)S(1)} %reshape.77), channel_id=1, source_target_pairs={{0,4},{1,5},{2,6},{3,7},{4,0},{5,1},{6,2},{7,3},{8,12},{9,13},{10,... | collective-permute-start | bytes 1544 | tf_op jit(solution)/shard_map/ppermute | solution.py:233
  10.6 2.3 %collective-permute-start.5 = (s32[1,128]{1,0:T(1,128)S(1)}, s32[1,128]{1,0:T(1,128)S(1)}, u32[]{:S(2)}, u32[]{:S(2)}) collective-permute-start(s32[1,128]{1,0:T(1,128)S(1)} %reshape.77), channel_id=1, source_target_pairs={{0,3},{1,2},{2,1},{3,0},{4,7},{5,6},{6,5},{7,4},{8,11},{9,10},{10,... | collective-permute-start | bytes 1544 | tf_op jit(solution)/shard_map/ppermute | solution.py:233
  13.2 1.0 copy-done
  14.2 1.0 copy-done.1
  15.2 1.0 split.1
  16.3 0.8 collective-permute-start.4
  17.5 1.6 %collective-permute-start.1 = (bf16[2,256,128]{2,1,0:T(8,128)(2,1)S(1)}, bf16[2,256,128]{2,1,0:T(8,128)(2,1)S(1)}, u32[]{:S(2)}, u32[]{:S(2)}) collective-permute-start(bf16[2,256,128]{2,1,0:T(8,128)(2,1)S(1)} %get-tuple-element.58), channel_id=1, source_target_pairs={{0,16},{8,24},{16,0},{24,8},{1,17},{9,25},{17,1},{25,9},{2,18},{10... | collective-permute-start | bytes 393224 | tf_op jit(solution)/shard_map/ppermute | solution.py:233
  19.9 1.5 %collective-permute-start.18 = (bf16[2,256,128]{2,1,0:T(8,128)(2,1)S(1)}, bf16[2,256,128]{2,1,0:T(8,128)(2,1)S(1)}, u32[]{:S(2)}, u32[]{:S(2)}) collective-permute-start(bf16[2,256,128]{2,1,0:T(8,128)(2,1)S(1)} %get-tuple-element.69), channel_id=1, source_target_pairs={{0,16},{8,24},{16,0},{24,8},{1,17},{9,25},{17,1},{25,9},{2,18},{10... | collective-permute-start | bytes 393224 | tf_op jit(solution)/shard_map/ppermute | solution.py:233
  21.8 1.8 %collective-permute-start.2 = (bf16[2,256,128]{2,1,0:T(8,128)(2,1)S(1)}, bf16[2,256,128]{2,1,0:T(8,128)(2,1)S(1)}, u32[]{:S(2)}, u32[]{:S(2)}) collective-permute-start(bf16[2,256,128]{2,1,0:T(8,128)(2,1)S(1)} %get-tuple-element.59), channel_id=1, source_target_pairs={{0,24},{8,16},{16,8},{24,0},{1,25},{9,17},{17,9},{25,1},{2,26},{10... | collective-permute-start | bytes 393224 | tf_op jit(solution)/shard_map/ppermute | solution.py:233
  23.9 2.8 %collective-permute-done.18.refs_2_ = bf16[2,256,128]{2,1,0:T(8,128)(2,1)S(1)} collective-permute-done((bf16[2,256,128]{2,1,0:T(8,128)(2,1)S(1)}, bf16[2,256,128]{2,1,0:T(8,128)(2,1)S(1)}, u32[]{:S(2)}, u32[]{:S(2)}) %collective-permute-start.18) | collective-permute-done | bytes 131104 | tf_op jit(solution)/shard_map/ppermute | solution.py:233
  26.7 1.9 %collective-permute-done.19.refs_3_ = bf16[2,256,128]{2,1,0:T(8,128)(2,1)S(1)} collective-permute-done((bf16[2,256,128]{2,1,0:T(8,128)(2,1)S(1)}, bf16[2,256,128]{2,1,0:T(8,128)(2,1)S(1)}, u32[]{:S(2)}, u32[]{:S(2)}) %collective-permute-start.19) | collective-permute-done | bytes 131104 | tf_op jit(solution)/shard_map/ppermute | solution.py:233
  29.3 1.6 %collective-permute-start.20 = (bf16[2,3,64,128]{3,2,1,0:T(8,128)(2,1)S(1)}, bf16[2,3,64,128]{3,2,1,0:T(8,128)(2,1)S(1)}, u32[]{:S(2)}, u32[]{:S(2)}) collective-permute-start(bf16[2,3,64,128]{3,2,1,0:T(8,128)(2,1)S(1)} %get-tuple-element.71), channel_id=1, source_target_pairs={{0,1},{1,0},{2,3},{3,2},{4,5},{5,4},{6,7},{7,6},{8,9},{9,8},{10,11... | collective-permute-start | bytes 294920 | tf_op jit(solution)/shard_map/ppermute | solution.py:233
  30.9 1.2 collective-permute-start.21
  33.1 2.4 %collective-permute-start.23 = (bf16[2,3,64,128]{3,2,1,0:T(8,128)(2,1)S(1)}, bf16[2,3,64,128]{3,2,1,0:T(8,128)(2,1)S(1)}, u32[]{:S(2)}, u32[]{:S(2)}) collective-permute-start(bf16[2,3,64,128]{3,2,1,0:T(8,128)(2,1)S(1)} %get-tuple-element.74), channel_id=1, source_target_pairs={{0,4},{1,5},{2,6},{3,7},{4,0},{5,1},{6,2},{7,3},{8,12},{9,13},{10,... | collective-permute-start | bytes 294920 | tf_op jit(solution)/shard_map/ppermute | solution.py:233
  35.5 1.5 %collective-permute-start.24 = (bf16[2,3,64,128]{3,2,1,0:T(8,128)(2,1)S(1)}, bf16[2,3,64,128]{3,2,1,0:T(8,128)(2,1)S(1)}, u32[]{:S(2)}, u32[]{:S(2)}) collective-permute-start(bf16[2,3,64,128]{3,2,1,0:T(8,128)(2,1)S(1)} %get-tuple-element.75), channel_id=1, source_target_pairs={{0,5},{1,4},{2,7},{3,6},{4,1},{5,0},{6,3},{7,2},{8,13},{9,12},{10,... | collective-permute-start | bytes 294920 | tf_op jit(solution)/shard_map/ppermute | solution.py:233
  37.0 3.6 %collective-permute-start.25 = (bf16[2,3,64,128]{3,2,1,0:T(8,128)(2,1)S(1)}, bf16[2,3,64,128]{3,2,1,0:T(8,128)(2,1)S(1)}, u32[]{:S(2)}, u32[]{:S(2)}) collective-permute-start(bf16[2,3,64,128]{3,2,1,0:T(8,128)(2,1)S(1)} %get-tuple-element.76), channel_id=1, source_target_pairs={{0,6},{1,7},{2,4},{3,5},{4,2},{5,3},{6,0},{7,1},{8,14},{9,15},{10,... | collective-permute-start | bytes 294920 | tf_op jit(solution)/shard_map/ppermute | solution.py:233
  41.5 1.5 %collective-permute-start.10 = (bf16[2,3,64,128]{3,2,1,0:T(8,128)(2,1)S(1)}, bf16[2,3,64,128]{3,2,1,0:T(8,128)(2,1)S(1)}, u32[]{:S(2)}, u32[]{:S(2)}) collective-permute-start(bf16[2,3,64,128]{3,2,1,0:T(8,128)(2,1)S(1)} %get-tuple-element.60), channel_id=1, source_target_pairs={{0,1},{1,0},{2,3},{3,2},{4,5},{5,4},{6,7},{7,6},{8,9},{9,8},{10,11... | collective-permute-start | bytes 294920 | tf_op jit(solution)/shard_map/ppermute | solution.py:233
  43.0 5.8 %collective-permute-start.11 = (bf16[2,3,64,128]{3,2,1,0:T(8,128)(2,1)S(1)}, bf16[2,3,64,128]{3,2,1,0:T(8,128)(2,1)S(1)}, u32[]{:S(2)}, u32[]{:S(2)}) collective-permute-start(bf16[2,3,64,128]{3,2,1,0:T(8,128)(2,1)S(1)} %get-tuple-element.61), channel_id=1, source_target_pairs={{0,2},{1,3},{2,0},{3,1},{4,6},{5,7},{6,4},{7,5},{8,10},{9,11},{10,... | collective-permute-start | bytes 294920 | tf_op jit(solution)/shard_map/ppermute | solution.py:233
  48.9 2.3 %collective-permute-done.24.refs_8_ = bf16[2,3,64,128]{3,2,1,0:T(8,128)(2,1)S(1)} collective-permute-done((bf16[2,3,64,128]{3,2,1,0:T(8,128)(2,1)S(1)}, bf16[2,3,64,128]{3,2,1,0:T(8,128)(2,1)S(1)}, u32[]{:S(2)}, u32[]{:S(2)}) %collective-permute-start.24) | collective-permute-done | bytes 98336 | tf_op jit(solution)/shard_map/ppermute | solution.py:233
  51.4 3.8 %collective-permute-start.13 = (bf16[2,3,64,128]{3,2,1,0:T(8,128)(2,1)S(1)}, bf16[2,3,64,128]{3,2,1,0:T(8,128)(2,1)S(1)}, u32[]{:S(2)}, u32[]{:S(2)}) collective-permute-start(bf16[2,3,64,128]{3,2,1,0:T(8,128)(2,1)S(1)} %get-tuple-element.63), channel_id=1, source_target_pairs={{0,4},{1,5},{2,6},{3,7},{4,0},{5,1},{6,2},{7,3},{8,12},{9,13},{10,... | collective-permute-start | bytes 294920 | tf_op jit(solution)/shard_map/ppermute | solution.py:233
  55.3 3.1 %collective-permute-start.14 = (bf16[2,3,64,128]{3,2,1,0:T(8,128)(2,1)S(1)}, bf16[2,3,64,128]{3,2,1,0:T(8,128)(2,1)S(1)}, u32[]{:S(2)}, u32[]{:S(2)}) collective-permute-start(bf16[2,3,64,128]{3,2,1,0:T(8,128)(2,1)S(1)} %get-tuple-element.64), channel_id=1, source_target_pairs={{0,5},{1,4},{2,7},{3,6},{4,1},{5,0},{6,3},{7,2},{8,13},{9,12},{10,... | collective-permute-start | bytes 294920 | tf_op jit(solution)/shard_map/ppermute | solution.py:233
  58.4 15.6 %attend.2 = (bf16[1024,1024]{1,0:T(8,128)(2,1)}, bf16[1024,1024]{1,0:T(8,128)(2,1)}, f32[2,16,64,128]{3,2,1,0:T(8,128)S(1)}, bf16[2,3,64,128]{3,2,1,0:T(8,128)(2...) custom-call(s32[2]{0:T(128)S(1)} %pad_add_fusion.place, ...), custom_call_target="tpu_custom_call" | custom-call | flops 3221225472 | bytes 20971520 | tf_op jit(solution)/shard_map/attend/pallas_call | solution.py:201
  74.0 1.9 %collective-permute-start.15 = (bf16[2,3,64,128]{3,2,1,0:T(8,128)(2,1)S(1)}, bf16[2,3,64,128]{3,2,1,0:T(8,128)(2,1)S(1)}, u32[]{:S(2)}, u32[]{:S(2)}) collective-permute-start(bf16[2,3,64,128]{3,2,1,0:T(8,128)(2,1)S(1)} %get-tuple-element.65), channel_id=1, source_target_pairs={{0,6},{1,7},{2,4},{3,5},{4,2},{5,3},{6,0},{7,1},{8,14},{9,15},{10,... | collective-permute-start | bytes 294920 | tf_op jit(solution)/shard_map/ppermute | solution.py:233
  75.9 3.0 %collective-permute-start.16 = (bf16[2,3,64,128]{3,2,1,0:T(8,128)(2,1)S(1)}, bf16[2,3,64,128]{3,2,1,0:T(8,128)(2,1)S(1)}, u32[]{:S(2)}, u32[]{:S(2)}) collective-permute-start(bf16[2,3,64,128]{3,2,1,0:T(8,128)(2,1)S(1)} %get-tuple-element.66), channel_id=1, source_target_pairs={{0,7},{1,6},{2,5},{3,4},{4,3},{5,2},{6,1},{7,0},{8,15},{9,14},{10,... | collective-permute-start | bytes 294920 | tf_op jit(solution)/shard_map/ppermute | solution.py:233
  79.4 3.0 %collective-permute-start.29 = (bf16[2,3,64,128]{3,2,1,0:T(8,128)(2,1)S(1)}, bf16[2,3,64,128]{3,2,1,0:T(8,128)(2,1)S(1)}, u32[]{:S(2)}, u32[]{:S(2)}) collective-permute-start(bf16[2,3,64,128]{3,2,1,0:T(8,128)(2,1)S(1)} %get-tuple-element.85), channel_id=1, source_target_pairs={{0,3},{1,2},{2,1},{3,0},{4,7},{5,6},{6,5},{7,4},{8,11},{9,10},{10,... | collective-permute-start | bytes 294920 | tf_op jit(solution)/shard_map/ppermute | solution.py:237
  82.4 2.4 %collective-permute-done.16.refs_10_ = bf16[2,3,64,128]{3,2,1,0:T(8,128)(2,1)S(1)} collective-permute-done((bf16[2,3,64,128]{3,2,1,0:T(8,128)(2,1)S(1)}, bf16[2,3,64,128]{3,2,1,0:T(8,128)(2,1)S(1)}, u32[]{:S(2)}, u32[]{:S(2)}) %collective-permute-start.16) | collective-permute-done | bytes 98336 | tf_op jit(solution)/shard_map/ppermute | solution.py:233
  84.7 0.8 collective-permute-start.31
  85.5 1.5 %collective-permute-start.32 = (bf16[2,3,64,128]{3,2,1,0:T(8,128)(2,1)S(1)}, bf16[2,3,64,128]{3,2,1,0:T(8,128)(2,1)S(1)}, u32[]{:S(2)}, u32[]{:S(2)}) collective-permute-start(bf16[2,3,64,128]{3,2,1,0:T(8,128)(2,1)S(1)} %get-tuple-element.88), channel_id=1, source_target_pairs={{0,6},{1,7},{2,4},{3,5},{4,2},{5,3},{6,0},{7,1},{8,14},{9,15},{10,... | collective-permute-start | bytes 294920 | tf_op jit(solution)/shard_map/ppermute | solution.py:237
  87.1 3.0 %collective-permute-start.33 = (bf16[2,3,64,128]{3,2,1,0:T(8,128)(2,1)S(1)}, bf16[2,3,64,128]{3,2,1,0:T(8,128)(2,1)S(1)}, u32[]{:S(2)}, u32[]{:S(2)}) collective-permute-start(bf16[2,3,64,128]{3,2,1,0:T(8,128)(2,1)S(1)} %get-tuple-element.89), channel_id=1, source_target_pairs={{0,7},{1,6},{2,5},{3,4},{4,3},{5,2},{6,1},{7,0},{8,15},{9,14},{10,... | collective-permute-start | bytes 294920 | tf_op jit(solution)/shard_map/ppermute | solution.py:237
  90.0 15.6 %attend.3 = (bf16[1024,1024]{1,0:T(8,128)(2,1)}, bf16[1024,1024]{1,0:T(8,128)(2,1)}, f32[2,16,64,128]{3,2,1,0:T(8,128)S(1)}, bf16[2,3,64,128]{3,2,1,0:T(8,128)(2...) custom-call(s32[2]{0:T(128)S(1)} %pad_add_fusion.place, ...), custom_call_target="tpu_custom_call", output_to_operand_aliasing={{0}: (15, {}), {1}: (16, {})} | custom-call | flops 3221225472 | bytes 20971520 | tf_op jit(solution)/shard_map/attend/pallas_call | solution.py:201
  105.7 1.2 collective-permute-start.37
  107.0 2.2 %collective-permute-start.39 = (bf16[2,3,64,128]{3,2,1,0:T(8,128)(2,1)S(1)}, bf16[2,3,64,128]{3,2,1,0:T(8,128)(2,1)S(1)}, u32[]{:S(2)}, u32[]{:S(2)}) collective-permute-start(bf16[2,3,64,128]{3,2,1,0:T(8,128)(2,1)S(1)} %get-tuple-element.97), channel_id=1, source_target_pairs={{0,3},{1,2},{2,1},{3,0},{4,7},{5,6},{6,5},{7,4},{8,11},{9,10},{10,... | collective-permute-start | bytes 294920 | tf_op jit(solution)/shard_map/ppermute | solution.py:237
  109.2 0.8 gather_sum.2
  110.1 1.0 collective-permute-start.40
  111.1 2.6 %collective-permute-start.41 = (bf16[2,3,64,128]{3,2,1,0:T(8,128)(2,1)S(1)}, bf16[2,3,64,128]{3,2,1,0:T(8,128)(2,1)S(1)}, u32[]{:S(2)}, u32[]{:S(2)}) collective-permute-start(bf16[2,3,64,128]{3,2,1,0:T(8,128)(2,1)S(1)} %get-tuple-element.99), channel_id=1, source_target_pairs={{0,5},{1,4},{2,7},{3,6},{4,1},{5,0},{6,3},{7,2},{8,13},{9,12},{10,... | collective-permute-start | bytes 294920 | tf_op jit(solution)/shard_map/ppermute | solution.py:237
  113.7 1.3 collective-permute-start.42
  114.9 2.9 %collective-permute-start.43 = (bf16[2,3,64,128]{3,2,1,0:T(8,128)(2,1)S(1)}, bf16[2,3,64,128]{3,2,1,0:T(8,128)(2,1)S(1)}, u32[]{:S(2)}, u32[]{:S(2)}) collective-permute-start(bf16[2,3,64,128]{3,2,1,0:T(8,128)(2,1)S(1)} %get-tuple-element.101), channel_id=1, source_target_pairs={{0,7},{1,6},{2,5},{3,4},{4,3},{5,2},{6,1},{7,0},{8,15},{9,14},{10,... | collective-permute-start | bytes 294920 | tf_op jit(solution)/shard_map/ppermute | solution.py:237
  117.8 6.9 %collective-permute-done.40.refs_3_ = bf16[2,3,64,128]{3,2,1,0:T(8,128)(2,1)S(1)} collective-permute-done((bf16[2,3,64,128]{3,2,1,0:T(8,128)(2,1)S(1)}, bf16[2,3,64,128]{3,2,1,0:T(8,128)(2,1)S(1)}, u32[]{:S(2)}, u32[]{:S(2)}) %collective-permute-start.40) | collective-permute-done | bytes 98336 | tf_op jit(solution)/shard_map/ppermute | solution.py:237
  124.7 1.5 %collective-permute-start.35 = (bf16[2,256,128]{2,1,0:T(8,128)(2,1)S(1)}, bf16[2,256,128]{2,1,0:T(8,128)(2,1)S(1)}, u32[]{:S(2)}, u32[]{:S(2)}) collective-permute-start(bf16[2,256,128]{2,1,0:T(8,128)(2,1)S(1)} %get-tuple-element.92), channel_id=1, source_target_pairs={{0,16},{8,24},{16,0},{24,8},{1,17},{9,25},{17,1},{25,9},{2,18},{10... | collective-permute-start | bytes 393224 | tf_op jit(solution)/shard_map/ppermute | solution.py:237
  126.2 0.8 collective-permute-done.41.refs_4_
  127.0 1.1 collective-permute-start.36
  128.1 0.8 gather_sum.3
  130.0 0.9 collective-permute-start.46
  130.9 1.7 %collective-permute-done.36.refs_3_ = bf16[2,256,128]{2,1,0:T(8,128)(2,1)S(1)} collective-permute-done((bf16[2,256,128]{2,1,0:T(8,128)(2,1)S(1)}, bf16[2,256,128]{2,1,0:T(8,128)(2,1)S(1)}, u32[]{:S(2)}, u32[]{:S(2)}) %collective-permute-start.36) | collective-permute-done | bytes 131104 | tf_op jit(solution)/shard_map/ppermute | solution.py:237
  132.6 3.3 %collective-permute-done.45.refs_6_ = bf16[2,256,128]{2,1,0:T(8,128)(2,1)S(1)} collective-permute-done((bf16[2,256,128]{2,1,0:T(8,128)(2,1)S(1)}, bf16[2,256,128]{2,1,0:T(8,128)(2,1)S(1)}, u32[]{:S(2)}, u32[]{:S(2)}) %collective-permute-start.45) | collective-permute-done | bytes 131104 | tf_op jit(solution)/shard_map/ppermute | solution.py:237
  135.9 2.2 %collective-permute-done.46.refs_7_ = bf16[2,256,128]{2,1,0:T(8,128)(2,1)S(1)} collective-permute-done((bf16[2,256,128]{2,1,0:T(8,128)(2,1)S(1)}, bf16[2,256,128]{2,1,0:T(8,128)(2,1)S(1)}, u32[]{:S(2)}, u32[]{:S(2)}) %collective-permute-start.46) | collective-permute-done | bytes 131104 | tf_op jit(solution)/shard_map/ppermute | solution.py:237
  138.1 1.8 %join.1 = (bf16[256,1024]{1,0:T(8,128)(2,1)}, bf16[256,1024]{1,0:T(8,128)(2,1)}) custom-call(s32[2]{0:T(128)S(1)} %pad_add_fusion.place, bf16[2,256,128]{2,1,0:T(8,128)(2,1)S(1)} %get-tuple-element.90.refs_0_, bf16[2,256,128]{2,1,0:T(8,128)(2,1)S(1)} %collective-permute-done.34.refs_1_, bf16[2,256,128]{2,1,0:T(8,128)(2,1)S(1)} %collective-permute-done.35.refs_2_, ...), custom_call_target="tpu_custom_call" | custom-call | tf_op jit(solution)/shard_map/join/pallas_call | solution.py:177
  (75 shorter events, 8.6 us)
Async XLA Ops:
  1.5 14.8 %collective-permute-start.9 = (s32[1,128]{1,0:T(1,128)S(1)}, s32[1,128]{1,0:T(1,128)S(1)}, u32[]{:S(2)}, u32[]{:S(2)}) collective-permute-start(s32[1,128]{1,0:T(1,128)S(1)} %reshape.77), channel_id=1, source_target_pairs={{0,7},{1,6},{2,5},{3,4},{4,3},{5,2},{6,1},{7,0},{8,15},{9,14},{10,... | collective-permute-start | bytes 1544 | tf_op jit(solution)/shard_map/ppermute | solution.py:233
  7.5 9.6 %collective-permute-start.8 = (s32[1,128]{1,0:T(1,128)S(1)}, s32[1,128]{1,0:T(1,128)S(1)}, u32[]{:S(2)}, u32[]{:S(2)}) collective-permute-start(s32[1,128]{1,0:T(1,128)S(1)} %reshape.77), channel_id=1, source_target_pairs={{0,6},{1,7},{2,4},{3,5},{4,2},{5,3},{6,0},{7,1},{8,14},{9,15},{10,... | collective-permute-start | bytes 1544 | tf_op jit(solution)/shard_map/ppermute | solution.py:233
  7.8 9.8 %collective-permute-start.7 = (s32[1,128]{1,0:T(1,128)S(1)}, s32[1,128]{1,0:T(1,128)S(1)}, u32[]{:S(2)}, u32[]{:S(2)}) collective-permute-start(s32[1,128]{1,0:T(1,128)S(1)} %reshape.77), channel_id=1, source_target_pairs={{0,5},{1,4},{2,7},{3,6},{4,1},{5,0},{6,3},{7,2},{8,13},{9,12},{10,... | collective-permute-start | bytes 1544 | tf_op jit(solution)/shard_map/ppermute | solution.py:233
  8.5 9.0 %collective-permute-start.6 = (s32[1,128]{1,0:T(1,128)S(1)}, s32[1,128]{1,0:T(1,128)S(1)}, u32[]{:S(2)}, u32[]{:S(2)}) collective-permute-start(s32[1,128]{1,0:T(1,128)S(1)} %reshape.77), channel_id=1, source_target_pairs={{0,4},{1,5},{2,6},{3,7},{4,0},{5,1},{6,2},{7,3},{8,12},{9,13},{10,... | collective-permute-start | bytes 1544 | tf_op jit(solution)/shard_map/ppermute | solution.py:233
  10.6 8.6 %collective-permute-start.5 = (s32[1,128]{1,0:T(1,128)S(1)}, s32[1,128]{1,0:T(1,128)S(1)}, u32[]{:S(2)}, u32[]{:S(2)}) collective-permute-start(s32[1,128]{1,0:T(1,128)S(1)} %reshape.77), channel_id=1, source_target_pairs={{0,3},{1,2},{2,1},{3,0},{4,7},{5,6},{6,5},{7,4},{8,11},{9,10},{10,... | collective-permute-start | bytes 1544 | tf_op jit(solution)/shard_map/ppermute | solution.py:233
  13.2 1.0 copy-start
  16.3 3.6 %collective-permute-start.4 = (s32[1,128]{1,0:T(1,128)S(1)}, s32[1,128]{1,0:T(1,128)S(1)}, u32[]{:S(2)}, u32[]{:S(2)}) collective-permute-start(s32[1,128]{1,0:T(1,128)S(1)} %reshape.77), channel_id=1, source_target_pairs={{0,2},{1,3},{2,0},{3,1},{4,6},{5,7},{6,4},{7,5},{8,10},{9,11},{10,... | collective-permute-start | bytes 1544 | tf_op jit(solution)/shard_map/ppermute | solution.py:233
  17.1 4.2 %collective-permute-start.3 = (s32[1,128]{1,0:T(1,128)S(1)}, s32[1,128]{1,0:T(1,128)S(1)}, u32[]{:S(2)}, u32[]{:S(2)}) collective-permute-start(s32[1,128]{1,0:T(1,128)S(1)} %reshape.77), channel_id=1, source_target_pairs={{0,1},{1,0},{2,3},{3,2},{4,5},{5,4},{6,7},{7,6},{8,9},{9,8},{10,11... | collective-permute-start | bytes 1544 | tf_op jit(solution)/shard_map/ppermute | solution.py:233
  17.5 14.8 %collective-permute-start = (bf16[2,256,128]{2,1,0:T(8,128)(2,1)S(1)}, bf16[2,256,128]{2,1,0:T(8,128)(2,1)S(1)}, u32[]{:S(2)}, u32[]{:S(2)}) collective-permute-start(bf16[2,256,128]{2,1,0:T(8,128)(2,1)S(1)} %get-tuple-element.57), channel_id=1, source_target_pairs={{0,8},{8,0},{16,24},{24,16},{1,9},{9,1},{17,25},{25,17},{2,10},{10... | collective-permute-start | bytes 393224 | tf_op jit(solution)/shard_map/ppermute | solution.py:233
  17.5 15.5 %collective-permute-start.1 = (bf16[2,256,128]{2,1,0:T(8,128)(2,1)S(1)}, bf16[2,256,128]{2,1,0:T(8,128)(2,1)S(1)}, u32[]{:S(2)}, u32[]{:S(2)}) collective-permute-start(bf16[2,256,128]{2,1,0:T(8,128)(2,1)S(1)} %get-tuple-element.58), channel_id=1, source_target_pairs={{0,16},{8,24},{16,0},{24,8},{1,17},{9,25},{17,1},{25,9},{2,18},{10... | collective-permute-start | bytes 393224 | tf_op jit(solution)/shard_map/ppermute | solution.py:233
  19.2 2.6 %collective-permute-start.17 = (bf16[2,256,128]{2,1,0:T(8,128)(2,1)S(1)}, bf16[2,256,128]{2,1,0:T(8,128)(2,1)S(1)}, u32[]{:S(2)}, u32[]{:S(2)}) collective-permute-start(bf16[2,256,128]{2,1,0:T(8,128)(2,1)S(1)} %get-tuple-element.68), channel_id=1, source_target_pairs={{0,8},{8,0},{16,24},{24,16},{1,9},{9,1},{17,25},{25,17},{2,10},{10... | collective-permute-start | bytes 393224 | tf_op jit(solution)/shard_map/ppermute | solution.py:233
  19.9 6.9 %collective-permute-start.18 = (bf16[2,256,128]{2,1,0:T(8,128)(2,1)S(1)}, bf16[2,256,128]{2,1,0:T(8,128)(2,1)S(1)}, u32[]{:S(2)}, u32[]{:S(2)}) collective-permute-start(bf16[2,256,128]{2,1,0:T(8,128)(2,1)S(1)} %get-tuple-element.69), channel_id=1, source_target_pairs={{0,16},{8,24},{16,0},{24,8},{1,17},{9,25},{17,1},{25,9},{2,18},{10... | collective-permute-start | bytes 393224 | tf_op jit(solution)/shard_map/ppermute | solution.py:233
  21.4 7.3 %collective-permute-start.19 = (bf16[2,256,128]{2,1,0:T(8,128)(2,1)S(1)}, bf16[2,256,128]{2,1,0:T(8,128)(2,1)S(1)}, u32[]{:S(2)}, u32[]{:S(2)}) collective-permute-start(bf16[2,256,128]{2,1,0:T(8,128)(2,1)S(1)} %get-tuple-element.70), channel_id=1, source_target_pairs={{0,24},{8,16},{16,8},{24,0},{1,25},{9,17},{17,9},{25,1},{2,26},{10... | collective-permute-start | bytes 393224 | tf_op jit(solution)/shard_map/ppermute | solution.py:233
  21.8 13.7 %collective-permute-start.2 = (bf16[2,256,128]{2,1,0:T(8,128)(2,1)S(1)}, bf16[2,256,128]{2,1,0:T(8,128)(2,1)S(1)}, u32[]{:S(2)}, u32[]{:S(2)}) collective-permute-start(bf16[2,256,128]{2,1,0:T(8,128)(2,1)S(1)} %get-tuple-element.59), channel_id=1, source_target_pairs={{0,24},{8,16},{16,8},{24,0},{1,25},{9,17},{17,9},{25,1},{2,26},{10... | collective-permute-start | bytes 393224 | tf_op jit(solution)/shard_map/ppermute | solution.py:233
  29.3 7.8 %collective-permute-start.20 = (bf16[2,3,64,128]{3,2,1,0:T(8,128)(2,1)S(1)}, bf16[2,3,64,128]{3,2,1,0:T(8,128)(2,1)S(1)}, u32[]{:S(2)}, u32[]{:S(2)}) collective-permute-start(bf16[2,3,64,128]{3,2,1,0:T(8,128)(2,1)S(1)} %get-tuple-element.71), channel_id=1, source_target_pairs={{0,1},{1,0},{2,3},{3,2},{4,5},{5,4},{6,7},{7,6},{8,9},{9,8},{10,11... | collective-permute-start | bytes 294920 | tf_op jit(solution)/shard_map/ppermute | solution.py:233
  30.9 9.7 %collective-permute-start.21 = (bf16[2,3,64,128]{3,2,1,0:T(8,128)(2,1)S(1)}, bf16[2,3,64,128]{3,2,1,0:T(8,128)(2,1)S(1)}, u32[]{:S(2)}, u32[]{:S(2)}) collective-permute-start(bf16[2,3,64,128]{3,2,1,0:T(8,128)(2,1)S(1)} %get-tuple-element.72), channel_id=1, source_target_pairs={{0,2},{1,3},{2,0},{3,1},{4,6},{5,7},{6,4},{7,5},{8,10},{9,11},{10,... | collective-permute-start | bytes 294920 | tf_op jit(solution)/shard_map/ppermute | solution.py:233
  32.3 9.2 %collective-permute-start.22 = (bf16[2,3,64,128]{3,2,1,0:T(8,128)(2,1)S(1)}, bf16[2,3,64,128]{3,2,1,0:T(8,128)(2,1)S(1)}, u32[]{:S(2)}, u32[]{:S(2)}) collective-permute-start(bf16[2,3,64,128]{3,2,1,0:T(8,128)(2,1)S(1)} %get-tuple-element.73), channel_id=1, source_target_pairs={{0,3},{1,2},{2,1},{3,0},{4,7},{5,6},{6,5},{7,4},{8,11},{9,10},{10,... | collective-permute-start | bytes 294920 | tf_op jit(solution)/shard_map/ppermute | solution.py:233
  33.1 10.0 %collective-permute-start.23 = (bf16[2,3,64,128]{3,2,1,0:T(8,128)(2,1)S(1)}, bf16[2,3,64,128]{3,2,1,0:T(8,128)(2,1)S(1)}, u32[]{:S(2)}, u32[]{:S(2)}) collective-permute-start(bf16[2,3,64,128]{3,2,1,0:T(8,128)(2,1)S(1)} %get-tuple-element.74), channel_id=1, source_target_pairs={{0,4},{1,5},{2,6},{3,7},{4,0},{5,1},{6,2},{7,3},{8,12},{9,13},{10,... | collective-permute-start | bytes 294920 | tf_op jit(solution)/shard_map/ppermute | solution.py:233
  35.5 15.7 %collective-permute-start.24 = (bf16[2,3,64,128]{3,2,1,0:T(8,128)(2,1)S(1)}, bf16[2,3,64,128]{3,2,1,0:T(8,128)(2,1)S(1)}, u32[]{:S(2)}, u32[]{:S(2)}) collective-permute-start(bf16[2,3,64,128]{3,2,1,0:T(8,128)(2,1)S(1)} %get-tuple-element.75), channel_id=1, source_target_pairs={{0,5},{1,4},{2,7},{3,6},{4,1},{5,0},{6,3},{7,2},{8,13},{9,12},{10,... | collective-permute-start | bytes 294920 | tf_op jit(solution)/shard_map/ppermute | solution.py:233
  37.0 14.4 %collective-permute-start.25 = (bf16[2,3,64,128]{3,2,1,0:T(8,128)(2,1)S(1)}, bf16[2,3,64,128]{3,2,1,0:T(8,128)(2,1)S(1)}, u32[]{:S(2)}, u32[]{:S(2)}) collective-permute-start(bf16[2,3,64,128]{3,2,1,0:T(8,128)(2,1)S(1)} %get-tuple-element.76), channel_id=1, source_target_pairs={{0,6},{1,7},{2,4},{3,5},{4,2},{5,3},{6,0},{7,1},{8,14},{9,15},{10,... | collective-permute-start | bytes 294920 | tf_op jit(solution)/shard_map/ppermute | solution.py:233
  40.6 14.6 %collective-permute-start.26 = (bf16[2,3,64,128]{3,2,1,0:T(8,128)(2,1)S(1)}, bf16[2,3,64,128]{3,2,1,0:T(8,128)(2,1)S(1)}, u32[]{:S(2)}, u32[]{:S(2)}) collective-permute-start(bf16[2,3,64,128]{3,2,1,0:T(8,128)(2,1)S(1)} %get-tuple-element.77), channel_id=1, source_target_pairs={{0,7},{1,6},{2,5},{3,4},{4,3},{5,2},{6,1},{7,0},{8,15},{9,14},{10,... | collective-permute-start | bytes 294920 | tf_op jit(solution)/shard_map/ppermute | solution.py:233
  41.5 32.5 %collective-permute-start.10 = (bf16[2,3,64,128]{3,2,1,0:T(8,128)(2,1)S(1)}, bf16[2,3,64,128]{3,2,1,0:T(8,128)(2,1)S(1)}, u32[]{:S(2)}, u32[]{:S(2)}) collective-permute-start(bf16[2,3,64,128]{3,2,1,0:T(8,128)(2,1)S(1)} %get-tuple-element.60), channel_id=1, source_target_pairs={{0,1},{1,0},{2,3},{3,2},{4,5},{5,4},{6,7},{7,6},{8,9},{9,8},{10,11... | collective-permute-start | bytes 294920 | tf_op jit(solution)/shard_map/ppermute | solution.py:233
  43.0 32.8 %collective-permute-start.11 = (bf16[2,3,64,128]{3,2,1,0:T(8,128)(2,1)S(1)}, bf16[2,3,64,128]{3,2,1,0:T(8,128)(2,1)S(1)}, u32[]{:S(2)}, u32[]{:S(2)}) collective-permute-start(bf16[2,3,64,128]{3,2,1,0:T(8,128)(2,1)S(1)} %get-tuple-element.61), channel_id=1, source_target_pairs={{0,2},{1,3},{2,0},{3,1},{4,6},{5,7},{6,4},{7,5},{8,10},{9,11},{10,... | collective-permute-start | bytes 294920 | tf_op jit(solution)/shard_map/ppermute | solution.py:233
  51.1 27.7 %collective-permute-start.12 = (bf16[2,3,64,128]{3,2,1,0:T(8,128)(2,1)S(1)}, bf16[2,3,64,128]{3,2,1,0:T(8,128)(2,1)S(1)}, u32[]{:S(2)}, u32[]{:S(2)}) collective-permute-start(bf16[2,3,64,128]{3,2,1,0:T(8,128)(2,1)S(1)} %get-tuple-element.62), channel_id=1, source_target_pairs={{0,3},{1,2},{2,1},{3,0},{4,7},{5,6},{6,5},{7,4},{8,11},{9,10},{10,... | collective-permute-start | bytes 294920 | tf_op jit(solution)/shard_map/ppermute | solution.py:233
  51.4 27.9 %collective-permute-start.13 = (bf16[2,3,64,128]{3,2,1,0:T(8,128)(2,1)S(1)}, bf16[2,3,64,128]{3,2,1,0:T(8,128)(2,1)S(1)}, u32[]{:S(2)}, u32[]{:S(2)}) collective-permute-start(bf16[2,3,64,128]{3,2,1,0:T(8,128)(2,1)S(1)} %get-tuple-element.63), channel_id=1, source_target_pairs={{0,4},{1,5},{2,6},{3,7},{4,0},{5,1},{6,2},{7,3},{8,12},{9,13},{10,... | collective-permute-start | bytes 294920 | tf_op jit(solution)/shard_map/ppermute | solution.py:233
  55.3 24.1 %collective-permute-start.14 = (bf16[2,3,64,128]{3,2,1,0:T(8,128)(2,1)S(1)}, bf16[2,3,64,128]{3,2,1,0:T(8,128)(2,1)S(1)}, u32[]{:S(2)}, u32[]{:S(2)}) collective-permute-start(bf16[2,3,64,128]{3,2,1,0:T(8,128)(2,1)S(1)} %get-tuple-element.64), channel_id=1, source_target_pairs={{0,5},{1,4},{2,7},{3,6},{4,1},{5,0},{6,3},{7,2},{8,13},{9,12},{10,... | collective-permute-start | bytes 294920 | tf_op jit(solution)/shard_map/ppermute | solution.py:233
  74.0 8.4 %collective-permute-start.15 = (bf16[2,3,64,128]{3,2,1,0:T(8,128)(2,1)S(1)}, bf16[2,3,64,128]{3,2,1,0:T(8,128)(2,1)S(1)}, u32[]{:S(2)}, u32[]{:S(2)}) collective-permute-start(bf16[2,3,64,128]{3,2,1,0:T(8,128)(2,1)S(1)} %get-tuple-element.65), channel_id=1, source_target_pairs={{0,6},{1,7},{2,4},{3,5},{4,2},{5,3},{6,0},{7,1},{8,14},{9,15},{10,... | collective-permute-start | bytes 294920 | tf_op jit(solution)/shard_map/ppermute | solution.py:233
  75.9 8.9 %collective-permute-start.16 = (bf16[2,3,64,128]{3,2,1,0:T(8,128)(2,1)S(1)}, bf16[2,3,64,128]{3,2,1,0:T(8,128)(2,1)S(1)}, u32[]{:S(2)}, u32[]{:S(2)}) collective-permute-start(bf16[2,3,64,128]{3,2,1,0:T(8,128)(2,1)S(1)} %get-tuple-element.66), channel_id=1, source_target_pairs={{0,7},{1,6},{2,5},{3,4},{4,3},{5,2},{6,1},{7,0},{8,15},{9,14},{10,... | collective-permute-start | bytes 294920 | tf_op jit(solution)/shard_map/ppermute | solution.py:233
  78.9 6.6 %collective-permute-start.27 = (bf16[2,3,64,128]{3,2,1,0:T(8,128)(2,1)S(1)}, bf16[2,3,64,128]{3,2,1,0:T(8,128)(2,1)S(1)}, u32[]{:S(2)}, u32[]{:S(2)}) collective-permute-start(bf16[2,3,64,128]{3,2,1,0:T(8,128)(2,1)S(1)} %get-tuple-element.83), channel_id=1, source_target_pairs={{0,1},{1,0},{2,3},{3,2},{4,5},{5,4},{6,7},{7,6},{8,9},{9,8},{10,11... | collective-permute-start | bytes 294920 | tf_op jit(solution)/shard_map/ppermute | solution.py:237
  79.4 7.7 %collective-permute-start.28 = (bf16[2,3,64,128]{3,2,1,0:T(8,128)(2,1)S(1)}, bf16[2,3,64,128]{3,2,1,0:T(8,128)(2,1)S(1)}, u32[]{:S(2)}, u32[]{:S(2)}) collective-permute-start(bf16[2,3,64,128]{3,2,1,0:T(8,128)(2,1)S(1)} %get-tuple-element.84), channel_id=1, source_target_pairs={{0,2},{1,3},{2,0},{3,1},{4,6},{5,7},{6,4},{7,5},{8,10},{9,11},{10,... | collective-permute-start | bytes 294920 | tf_op jit(solution)/shard_map/ppermute | solution.py:237
  79.4 26.3 %collective-permute-start.29 = (bf16[2,3,64,128]{3,2,1,0:T(8,128)(2,1)S(1)}, bf16[2,3,64,128]{3,2,1,0:T(8,128)(2,1)S(1)}, u32[]{:S(2)}, u32[]{:S(2)}) collective-permute-start(bf16[2,3,64,128]{3,2,1,0:T(8,128)(2,1)S(1)} %get-tuple-element.85), channel_id=1, source_target_pairs={{0,3},{1,2},{2,1},{3,0},{4,7},{5,6},{6,5},{7,4},{8,11},{9,10},{10,... | collective-permute-start | bytes 294920 | tf_op jit(solution)/shard_map/ppermute | solution.py:237
  82.4 24.4 %collective-permute-start.30 = (bf16[2,3,64,128]{3,2,1,0:T(8,128)(2,1)S(1)}, bf16[2,3,64,128]{3,2,1,0:T(8,128)(2,1)S(1)}, u32[]{:S(2)}, u32[]{:S(2)}) collective-permute-start(bf16[2,3,64,128]{3,2,1,0:T(8,128)(2,1)S(1)} %get-tuple-element.86), channel_id=1, source_target_pairs={{0,4},{1,5},{2,6},{3,7},{4,0},{5,1},{6,2},{7,3},{8,12},{9,13},{10,... | collective-permute-start | bytes 294920 | tf_op jit(solution)/shard_map/ppermute | solution.py:237
  84.7 22.3 %collective-permute-start.31 = (bf16[2,3,64,128]{3,2,1,0:T(8,128)(2,1)S(1)}, bf16[2,3,64,128]{3,2,1,0:T(8,128)(2,1)S(1)}, u32[]{:S(2)}, u32[]{:S(2)}) collective-permute-start(bf16[2,3,64,128]{3,2,1,0:T(8,128)(2,1)S(1)} %get-tuple-element.87), channel_id=1, source_target_pairs={{0,5},{1,4},{2,7},{3,6},{4,1},{5,0},{6,3},{7,2},{8,13},{9,12},{10,... | collective-permute-start | bytes 294920 | tf_op jit(solution)/shard_map/ppermute | solution.py:237
  85.5 23.7 %collective-permute-start.32 = (bf16[2,3,64,128]{3,2,1,0:T(8,128)(2,1)S(1)}, bf16[2,3,64,128]{3,2,1,0:T(8,128)(2,1)S(1)}, u32[]{:S(2)}, u32[]{:S(2)}) collective-permute-start(bf16[2,3,64,128]{3,2,1,0:T(8,128)(2,1)S(1)} %get-tuple-element.88), channel_id=1, source_target_pairs={{0,6},{1,7},{2,4},{3,5},{4,2},{5,3},{6,0},{7,1},{8,14},{9,15},{10,... | collective-permute-start | bytes 294920 | tf_op jit(solution)/shard_map/ppermute | solution.py:237
  87.1 22.1 %collective-permute-start.33 = (bf16[2,3,64,128]{3,2,1,0:T(8,128)(2,1)S(1)}, bf16[2,3,64,128]{3,2,1,0:T(8,128)(2,1)S(1)}, u32[]{:S(2)}, u32[]{:S(2)}) collective-permute-start(bf16[2,3,64,128]{3,2,1,0:T(8,128)(2,1)S(1)} %get-tuple-element.89), channel_id=1, source_target_pairs={{0,7},{1,6},{2,5},{3,4},{4,3},{5,2},{6,1},{7,0},{8,15},{9,14},{10,... | collective-permute-start | bytes 294920 | tf_op jit(solution)/shard_map/ppermute | solution.py:237
  105.7 5.4 %collective-permute-start.37 = (bf16[2,3,64,128]{3,2,1,0:T(8,128)(2,1)S(1)}, bf16[2,3,64,128]{3,2,1,0:T(8,128)(2,1)S(1)}, u32[]{:S(2)}, u32[]{:S(2)}) collective-permute-start(bf16[2,3,64,128]{3,2,1,0:T(8,128)(2,1)S(1)} %get-tuple-element.95), channel_id=1, source_target_pairs={{0,1},{1,0},{2,3},{3,2},{4,5},{5,4},{6,7},{7,6},{8,9},{9,8},{10,11... | collective-permute-start | bytes 294920 | tf_op jit(solution)/shard_map/ppermute | solution.py:237
  106.8 6.8 %collective-permute-start.38 = (bf16[2,3,64,128]{3,2,1,0:T(8,128)(2,1)S(1)}, bf16[2,3,64,128]{3,2,1,0:T(8,128)(2,1)S(1)}, u32[]{:S(2)}, u32[]{:S(2)}) collective-permute-start(bf16[2,3,64,128]{3,2,1,0:T(8,128)(2,1)S(1)} %get-tuple-element.96), channel_id=1, source_target_pairs={{0,2},{1,3},{2,0},{3,1},{4,6},{5,7},{6,4},{7,5},{8,10},{9,11},{10,... | collective-permute-start | bytes 294920 | tf_op jit(solution)/shard_map/ppermute | solution.py:237
  107.0 7.9 %collective-permute-start.39 = (bf16[2,3,64,128]{3,2,1,0:T(8,128)(2,1)S(1)}, bf16[2,3,64,128]{3,2,1,0:T(8,128)(2,1)S(1)}, u32[]{:S(2)}, u32[]{:S(2)}) collective-permute-start(bf16[2,3,64,128]{3,2,1,0:T(8,128)(2,1)S(1)} %get-tuple-element.97), channel_id=1, source_target_pairs={{0,3},{1,2},{2,1},{3,0},{4,7},{5,6},{6,5},{7,4},{8,11},{9,10},{10,... | collective-permute-start | bytes 294920 | tf_op jit(solution)/shard_map/ppermute | solution.py:237
  110.0 20.0 %collective-permute-start.34 = (bf16[2,256,128]{2,1,0:T(8,128)(2,1)S(1)}, bf16[2,256,128]{2,1,0:T(8,128)(2,1)S(1)}, u32[]{:S(2)}, u32[]{:S(2)}) collective-permute-start(bf16[2,256,128]{2,1,0:T(8,128)(2,1)S(1)} %get-tuple-element.91), channel_id=1, source_target_pairs={{0,8},{8,0},{16,24},{24,16},{1,9},{9,1},{17,25},{25,17},{2,10},{10... | collective-permute-start | bytes 393224 | tf_op jit(solution)/shard_map/ppermute | solution.py:237
  110.1 14.6 %collective-permute-start.40 = (bf16[2,3,64,128]{3,2,1,0:T(8,128)(2,1)S(1)}, bf16[2,3,64,128]{3,2,1,0:T(8,128)(2,1)S(1)}, u32[]{:S(2)}, u32[]{:S(2)}) collective-permute-start(bf16[2,3,64,128]{3,2,1,0:T(8,128)(2,1)S(1)} %get-tuple-element.98), channel_id=1, source_target_pairs={{0,4},{1,5},{2,6},{3,7},{4,0},{5,1},{6,2},{7,3},{8,12},{9,13},{10,... | collective-permute-start | bytes 294920 | tf_op jit(solution)/shard_map/ppermute | solution.py:237
  111.1 15.9 %collective-permute-start.41 = (bf16[2,3,64,128]{3,2,1,0:T(8,128)(2,1)S(1)}, bf16[2,3,64,128]{3,2,1,0:T(8,128)(2,1)S(1)}, u32[]{:S(2)}, u32[]{:S(2)}) collective-permute-start(bf16[2,3,64,128]{3,2,1,0:T(8,128)(2,1)S(1)} %get-tuple-element.99), channel_id=1, source_target_pairs={{0,5},{1,4},{2,7},{3,6},{4,1},{5,0},{6,3},{7,2},{8,13},{9,12},{10,... | collective-permute-start | bytes 294920 | tf_op jit(solution)/shard_map/ppermute | solution.py:237
  113.7 14.5 %collective-permute-start.42 = (bf16[2,3,64,128]{3,2,1,0:T(8,128)(2,1)S(1)}, bf16[2,3,64,128]{3,2,1,0:T(8,128)(2,1)S(1)}, u32[]{:S(2)}, u32[]{:S(2)}) collective-permute-start(bf16[2,3,64,128]{3,2,1,0:T(8,128)(2,1)S(1)} %get-tuple-element.100), channel_id=1, source_target_pairs={{0,6},{1,7},{2,4},{3,5},{4,2},{5,3},{6,0},{7,1},{8,14},{9,15},{10,... | collective-permute-start | bytes 294920 | tf_op jit(solution)/shard_map/ppermute | solution.py:237
  114.9 13.2 %collective-permute-start.43 = (bf16[2,3,64,128]{3,2,1,0:T(8,128)(2,1)S(1)}, bf16[2,3,64,128]{3,2,1,0:T(8,128)(2,1)S(1)}, u32[]{:S(2)}, u32[]{:S(2)}) collective-permute-start(bf16[2,3,64,128]{3,2,1,0:T(8,128)(2,1)S(1)} %get-tuple-element.101), channel_id=1, source_target_pairs={{0,7},{1,6},{2,5},{3,4},{4,3},{5,2},{6,1},{7,0},{8,15},{9,14},{10,... | collective-permute-start | bytes 294920 | tf_op jit(solution)/shard_map/ppermute | solution.py:237
  124.7 6.2 %collective-permute-start.35 = (bf16[2,256,128]{2,1,0:T(8,128)(2,1)S(1)}, bf16[2,256,128]{2,1,0:T(8,128)(2,1)S(1)}, u32[]{:S(2)}, u32[]{:S(2)}) collective-permute-start(bf16[2,256,128]{2,1,0:T(8,128)(2,1)S(1)} %get-tuple-element.92), channel_id=1, source_target_pairs={{0,16},{8,24},{16,0},{24,8},{1,17},{9,25},{17,1},{25,9},{2,18},{10... | collective-permute-start | bytes 393224 | tf_op jit(solution)/shard_map/ppermute | solution.py:237
  127.0 5.6 %collective-permute-start.36 = (bf16[2,256,128]{2,1,0:T(8,128)(2,1)S(1)}, bf16[2,256,128]{2,1,0:T(8,128)(2,1)S(1)}, u32[]{:S(2)}, u32[]{:S(2)}) collective-permute-start(bf16[2,256,128]{2,1,0:T(8,128)(2,1)S(1)} %get-tuple-element.93), channel_id=1, source_target_pairs={{0,24},{8,16},{16,8},{24,0},{1,25},{9,17},{17,9},{25,1},{2,26},{10... | collective-permute-start | bytes 393224 | tf_op jit(solution)/shard_map/ppermute | solution.py:237
  128.9 3.7 %collective-permute-start.44 = (bf16[2,256,128]{2,1,0:T(8,128)(2,1)S(1)}, bf16[2,256,128]{2,1,0:T(8,128)(2,1)S(1)}, u32[]{:S(2)}, u32[]{:S(2)}) collective-permute-start(bf16[2,256,128]{2,1,0:T(8,128)(2,1)S(1)} %get-tuple-element.103), channel_id=1, source_target_pairs={{0,8},{8,0},{16,24},{24,16},{1,9},{9,1},{17,25},{25,17},{2,10},{10... | collective-permute-start | bytes 393224 | tf_op jit(solution)/shard_map/ppermute | solution.py:237
  129.5 6.4 %collective-permute-start.45 = (bf16[2,256,128]{2,1,0:T(8,128)(2,1)S(1)}, bf16[2,256,128]{2,1,0:T(8,128)(2,1)S(1)}, u32[]{:S(2)}, u32[]{:S(2)}) collective-permute-start(bf16[2,256,128]{2,1,0:T(8,128)(2,1)S(1)} %get-tuple-element.104), channel_id=1, source_target_pairs={{0,16},{8,24},{16,0},{24,8},{1,17},{9,25},{17,1},{25,9},{2,18},{10... | collective-permute-start | bytes 393224 | tf_op jit(solution)/shard_map/ppermute | solution.py:237
  130.0 8.0 %collective-permute-start.46 = (bf16[2,256,128]{2,1,0:T(8,128)(2,1)S(1)}, bf16[2,256,128]{2,1,0:T(8,128)(2,1)S(1)}, u32[]{:S(2)}, u32[]{:S(2)}) collective-permute-start(bf16[2,256,128]{2,1,0:T(8,128)(2,1)S(1)} %get-tuple-element.105), channel_id=1, source_target_pairs={{0,24},{8,16},{16,8},{24,0},{1,25},{9,17},{17,9},{25,1},{2,26},{10... | collective-permute-start | bytes 393224 | tf_op jit(solution)/shard_map/ppermute | solution.py:237
  (1 other events, 1.0 us)

commit v4 on v3

--- a/solution.py
+++ b/solution.py
@@ -16,7 +16,8 @@
 NEG_FILL = -1e30
 SCALE = HEAD_DIM ** (-0.5)
 LOG2E = 1.4426950408889634
-VMEM_LIMIT = 50 * 1024 * 1024
+VMEM_LIMIT = 40 * 1024 * 1024
+VMEM_MOST = 60 * 1024 * 1024
 
 NT = (((1,), (1,)), ((), ()))
 NN = (((1,), (0,)), ((), ()))
@@ -27,8 +28,8 @@
     return lax.dot_general(a, b, dims, preferred_element_type=jnp.float32)
 
 
-def params(**kw):
-    return pltpu.CompilerParams(vmem_limit_bytes=VMEM_LIMIT, **kw)
+def params(limit=VMEM_LIMIT):
+    return pltpu.CompilerParams(vmem_limit_bytes=limit)
 
 
 def partner(me, r, count):
@@ -45,17 +46,53 @@
     copies = []
     for h in range(head_count):
         for r in range(heads):
-            peer = partner(place[1], r, heads)
-            col = pl.multiple_of((peer * head_count + h) * HEAD_DIM, HEAD_DIM)
+            at = h * heads + r
             for kv, ref in enumerate((k_ref, v_ref)):
-                at = h * heads + r
-                copies.append(
-                    pltpu.make_async_copy(ref.at[:, pl.ds(col, HEAD_DIM)], outs[at].at[kv], sem.at[2 * at + kv])
-                )
+                cols = head_columns(place, r, heads, h, head_count)
+                copies.append(pltpu.make_async_copy(ref.at[:, cols], outs[at].at[kv], sem.at[2 * at + kv]))
+    run(copies)
+
+
+def join_kernel(place, *refs, heads):
+    *pieces, k_ref, v_ref, sem = refs
+    head_count = len(pieces) // heads
+    copies = []
+    for h in range(head_count):
+        for r in range(heads):
+            at = h * heads + r
+            for kv, ref in enumerate((k_ref, v_ref)):
+                cols = head_columns(place, r, heads, h, head_count)
+                copies.append(pltpu.make_async_copy(pieces[at].at[kv], ref.at[:, cols], sem.at[2 * at + kv]))
+    run(copies)
+
+
+def head_columns(place, r, heads, h, head_count):
+    col = (partner(place[1], r, heads) * head_count + h) * HEAD_DIM
+    return pl.ds(pl.multiple_of(col, HEAD_DIM), HEAD_DIM)
+
+
+def run(copies):
     for copy in copies:
         copy.start()
     for copy in copies:
         copy.wait()
+
+
+def by_copies(kernel, place, arrays, out_shapes, name, limit):
+    here = pl.BlockSpec(memory_space=pl.ANY)
+    return pl.pallas_call(
+        kernel,
+        grid_spec=pltpu.PrefetchScalarGridSpec(
+            num_scalar_prefetch=1,
+            grid=(1,),
+            in_specs=[here] * len(arrays),
+            out_specs=[here] * len(out_shapes),
+            scratch_shapes=[pltpu.SemaphoreType.DMA((2 * max(len(arrays), len(out_shapes)),))],
+        ),
+        out_shape=out_shapes,
+        compiler_params=params(limit),
+        name=name,
+    )(place, *arrays)
 
 
 def fill_table(place, own, table):
@@ -68,17 +105,22 @@
                 table[kv, first + j] = own[r][kv, j * BLK : (j + 1) * BLK, :]
 
 
-def pick_kernel(place, asked, *refs, heads):
-    own, (*outs, table) = refs[:heads], refs[heads:]
-    fill_table(place, own, table)
-    for d, out in enumerate(outs):
+def pick_kernel(place, asked, *refs, heads, head_count, first, single):
+    own, (*outs, table) = refs[: heads * head_count], refs[heads * head_count :]
+    for h in range(head_count):
+        fill_table(place, own[h * heads : (h + 1) * heads], table.at[h])
+    for d, out in enumerate(outs, first):
         for s in range(CAP):
-            block = asked[d * CAP + s]
+            block = asked[(d - 1) * CAP + s]
             for kv in range(2):
-                out[kv, s] = table[kv, block]
-
-
-def attend_kernel(place, source, q_ref, g_ref, *refs, heads, steps):
+                if d < single:
+                    for h in range(head_count):
+                        out[h, kv, s] = table[h, kv, block]
+                else:
+                    out[kv, s] = table[head_count - 1, kv, block]
+
+
+def attend_kernel(place, source, q_ref, g_ref, *refs, heads, steps, head):
     own, far = refs[:heads], refs[heads : heads + steps]
     table, total = refs[-2:]
     far_out = refs[-2 - steps : -2]
@@ -92,7 +134,8 @@
         for kv in range(2):
             for d in range(steps):
                 for s in range(CAP):
-                    table[kv, blocks_here + d * CAP + s] = far[d][kv, s]
+                    from_there = far[d].at[head] if len(far[d].shape) == 5 else far[d]
+                    table[kv, blocks_here + d * CAP + s] = from_there[kv, s]
         total[...] = jnp.zeros_like(total)
 
     key_row = lax.broadcasted_iota(jnp.int32, (BLK, GROUP * BLK), 0)
@@ -158,17 +201,6 @@
                 outs[r][kv, j * BLK : (j + 1) * BLK, :] = total[kv, first + j].astype(jnp.bfloat16)
 
 
-def join_kernel(place, *refs, heads):
-    *pieces, k_ref, v_ref = refs
-    head_count = len(pieces) // heads
-    for h in range(head_count):
-        for r in range(heads):
-            peer = partner(place[1], r, heads)
-            col = pl.multiple_of((peer * head_count + h) * HEAD_DIM, HEAD_DIM)
-            k_ref[:, pl.ds(col, HEAD_DIM)] = pieces[h * heads + r][0]
-            v_ref[:, pl.ds(col, HEAD_DIM)] = pieces[h * heads + r][1]
-
-
 def whole(shape):
     return pl.BlockSpec(tuple(shape), lambda *_: (0,) * len(shape))
 
@@ -199,14 +231,14 @@
     aliases = {first: 0, first + 1: 1} if earlier else {}
     arrays = [*own, *far]
     return pl.pallas_call(
-        functools.partial(attend_kernel, heads=len(own), steps=len(far)),
+        functools.partial(attend_kernel, heads=len(own), steps=len(far), head=head),
         grid_spec=pltpu.PrefetchScalarGridSpec(
             num_scalar_prefetch=2,
             grid=(blocks_here // STEP_BLOCKS,),
             in_specs=[tile, tile]
             + [whole(x.shape) for x in arrays]
             + [pl.BlockSpec(memory_space=pl.ANY)] * len(earlier),
-            out_specs=[tile, tile, whole(near_shape)] + [whole(x.shape) for x in far],
+            out_specs=[tile, tile, whole(near_shape)] + [whole(x.shape[-4:]) for x in far],
             scratch_shapes=[
                 pltpu.VMEM((2, slots, BLK, HEAD_DIM), jnp.bfloat16),
                 pltpu.VMEM((2, slots, BLK, HEAD_DIM), jnp.float32),
@@ -217,7 +249,7 @@
             jax.ShapeDtypeStruct((tokens_here, width), jnp.bfloat16),
             jax.ShapeDtypeStruct(near_shape, jnp.float32),
         ]
-        + [jax.ShapeDtypeStruct(x.shape, jnp.bfloat16) for x in far],
+        + [jax.ShapeDtypeStruct(x.shape[-4:], jnp.bfloat16) for x in far],
         input_output_aliases=aliases,
         compiler_params=params(),
         cost_estimate=pl.CostEstimate(
@@ -235,6 +267,15 @@
 
 def send_back(x, axis, count, r):
     return lax.ppermute(x, axis, [(i, origin(i, r, count)) for i in range(count)])
+
+
+def lists_of_others(block_lists, count):
+    if count & (count - 1):
+        return jnp.stack([send_back(block_lists, "ctx", count, d) for d in range(1, count)])
+    known = block_lists[None]
+    while known.shape[0] < count:
+        known = jnp.concatenate([known, send(known, "ctx", count, known.shape[0])])
+    return known[1:]
 
 
 def rank_of(hits):
@@ -254,30 +295,19 @@
     place = jnp.stack([shard_index, head_index]).astype(jnp.int32)
     inner = jnp.arange(blocks_here, dtype=jnp.int32)
 
-    flat_ids = block_lists.reshape(1, -1)
-    others = [send(flat_ids, "ctx", shard_count, d) for d in range(1, shard_count)]
-
     piece = jax.ShapeDtypeStruct((2, quarter, HEAD_DIM), jnp.bfloat16)
-    pieces = pl.pallas_call(
-        functools.partial(split_kernel, heads=heads),
-        grid_spec=pltpu.PrefetchScalarGridSpec(
-            num_scalar_prefetch=1,
-            grid=(1,),
-            in_specs=[pl.BlockSpec(memory_space=pl.ANY)] * 2,
-            out_specs=[pl.BlockSpec(memory_space=pl.ANY)] * (heads * head_count),
-            scratch_shapes=[pltpu.SemaphoreType.DMA((2 * heads * head_count,))],
-        ),
-        out_shape=[piece] * (heads * head_count),
-        compiler_params=params(),
-        name="split",
-    )(place, key_states, value_states)
+    pieces = by_copies(
+        functools.partial(split_kernel, heads=heads), place, [key_states, value_states], [piece] * (heads * head_count), "split", VMEM_MOST
+    )
     own = []
     for h in range(head_count):
         parts = pieces[h * heads : (h + 1) * heads]
         own.append([parts[0]] + [send(parts[r], "head", heads, r) for r in range(1, heads)])
 
+    lists, _ = lax.optimization_barrier((block_lists, pieces[0]))
     asked_hits = jnp.any(
-        jnp.concatenate(others)[:, :, None] == (shard_index * blocks_here + inner)[None, None, :], axis=1
+        lists_of_others(lists, shard_count)[:, :, :, None] == (shard_index * blocks_here + inner)[None, None, None, :],
+        axis=(1, 2),
     )
     asked_rank = rank_of(asked_hits)
     asked = jnp.sum(
@@ -285,7 +315,7 @@
         axis=2,
     ).reshape(-1)
 
-    flat_ids = flat_ids.reshape(-1)
+    flat_ids = block_lists.reshape(-1)
     owner = flat_ids // blocks_here
     every_block = jnp.arange(shard_count * blocks_here, dtype=jnp.int32)
     listed = jnp.any(flat_ids[:, None] == every_block[None, :], axis=0)
@@ -297,14 +327,25 @@
         distance = (shard_index + shard_count - owner) % shard_count
     source = jnp.where(distance == 0, flat_ids % blocks_here, blocks_here + (distance - 1) * CAP + rank)
 
-    slots = jax.ShapeDtypeStruct((2, CAP, BLK, HEAD_DIM), jnp.bfloat16)
-    table = pltpu.VMEM((2, blocks_here, BLK, HEAD_DIM), jnp.bfloat16)
-    far = []
-    for h in range(head_count):
+    wide = max(1, shard_count // 2)
+    one = (2, CAP, BLK, HEAD_DIM)
+    far = [[] for _ in range(head_count)]
+    near_shape = jax.ShapeDtypeStruct((head_count, *one), jnp.bfloat16)
+    for h in range(head_count):
+        last = h == head_count - 1
+        first = 1 if last else wide
         picked = call(
-            functools.partial(pick_kernel, heads=heads), [place, asked], own[h], [slots] * (shard_count - 1), [table], "pick"
+            functools.partial(pick_kernel, heads=heads, head_count=h + 1, first=first, single=wide),
+            [place, asked],
+            [x for group in own[: h + 1] for x in group],
+            [near_shape] * (wide - 1) * last + [jax.ShapeDtypeStruct(one, jnp.bfloat16)] * (shard_count - wide),
+            [pltpu.VMEM((h + 1, 2, blocks_here, BLK, HEAD_DIM), jnp.bfloat16)],
+            "pick",
         )
-        far.append([send(x, "ctx", shard_count, d) for d, x in enumerate(picked, 1)])
+        sent = {d: send(x, "ctx", shard_count, d) for d, x in enumerate(picked, first)}
+        far[h] = [sent[d] for d in range(wide, shard_count)]
+    near = [sent[d] for d in range(1, wide)]
+    far = [near + group for group in far]
     earlier, nears, backs = [], [], []
     for h in range(head_count):
         attended, query_grad, near, *far_grad = attend(
@@ -321,9 +362,10 @@
             [place, asked], [nears[h], *backs[h]], [piece] * heads, [total], "gather_sum",
         )
         done.append([sums[0]] + [send_back(sums[r], "head", heads, r) for r in range(1, heads)])
-    pieces = [x for group in done for x in group]
     grad = jax.ShapeDtypeStruct(key_states.shape, jnp.bfloat16)
-    key_grad, value_grad = call(functools.partial(join_kernel, heads=heads), [place], pieces, [grad, grad], name="join")
+    key_grad, value_grad = by_copies(
+        functools.partial(join_kernel, heads=heads), place, [x for group in done for x in group], [grad, grad], "join", VMEM_LIMIT
+    )
     return attended, query_grad, key_grad, value_grad
 
 

time: 140 us -> 172 us (1.23)
  Pallas kernels: 36.9 us -> 67.9 us
  starting transfers between devices: 73.2 us -> 61.7 us
  waiting for transfers between devices: 24.9 us -> 32.2 us
  local copies, waits for them, and re-layouts: 3.21 us -> 6.71 us
  other arithmetic: 0.93 us -> 2.76 us
    pallas_call x1 -> x2, Pallas kernels: 1.01 us -> 35.3 us  [by_copies(): pl.pallas_call(kernel, grid_spec=pltpu.PrefetchScalarGridSpec(num_scalar_...]
    ppermute x27 -> x20, starting transfers between devices: 48.5 us -> 31.6 us  [send(): lax.ppermute(x, axis, [(i, partner(i, r, count)) for i in range(count)])]
    ppermute x20, starting transfers between devices: 24.7 us -> 30.1 us  [send_back(): lax.ppermute(x, axis, [(i, origin(i, r, count)) for i in range(count)])]
    ppermute x27 -> x20, waiting for transfers between devices: 10 us -> 14.5 us  [send(): lax.ppermute(x, axis, [(i, partner(i, r, count)) for i in range(count)])]
    unnamed x5 -> x13, local copies, waits for them, and re-layouts: 2.84 us -> 6.37 us
    ppermute x20, waiting for transfers between devices: 14.9 us -> 17.7 us  [send_back(): lax.ppermute(x, axis, [(i, origin(i, r, count)) for i in range(count)])]
    pallas_call x5 -> x4, Pallas kernels: 4.7 us -> 2.92 us  [call(): pl.pallas_call(kernel, grid_spec=pltpu.PrefetchScalarGridSpec(num_scalar_...]
  transfers between devices with their start and end apart: 47 -> 40, of which waited for: 11 -> 10; matrix products, arithmetic and copies ran while one was open for 1% -> 2% of each run, Pallas kernels for 25% -> 19%
where the time goes in v4:
time: 172 us
  Pallas kernels  67.9 us (39%)
  starting transfers between devices  61.7 us (36%)
  waiting for transfers between devices  32.2 us (19%)
  local copies, waits for them, and re-layouts  6.71 us (4%)
  other arithmetic  2.76 us (2%)
    pallas_call x2, Pallas kernels, by_copies(): pl.pallas_call(kernel, grid_spec=pltpu.PrefetchScalarGridSpec(num_scalar_...  35.3 us
    ppermute x20, starting transfers between devices, send(): lax.ppermute(x, axis, [(i, partner(i, r, count)) for i in range(count)])  31.6 us
    ppermute x20, starting transfers between devices, send_back(): lax.ppermute(x, axis, [(i, origin(i, r, count)) for i in range(count)])  30.1 us
    pallas_call x2, Pallas kernels, attend(): pl.pallas_call(functools.partial(attend_kernel, heads=len(own), steps=len...  29.6 us
    ppermute x20, waiting for transfers between devices, send_back(): lax.ppermute(x, axis, [(i, origin(i, r, count)) for i in range(count)])  17.7 us
    ppermute x20, waiting for transfers between devices, send(): lax.ppermute(x, axis, [(i, partner(i, r, count)) for i in range(count)])  14.5 us
    unnamed x13, local copies, waits for them, and re-layouts  6.37 us
  transfers between devices with their start and end apart: 40, of which 10 were waited for; matrix products, arithmetic and copies ran while one was open for 2% of the time, Pallas kernels for 19%

profile of v4, /device:TPU:0, one launch (start us, length us, event | category | flops | bytes accessed | tf_op | source)
XLA Modules:
  0.0 172.1 jit_solution(11390475958247155178)
XLA Ops:
  1.2 33.7 %split.1 = (bf16[2,256,128]{2,1,0:T(8,128)(2,1)}, bf16[2,256,128]{2,1,0:T(8,128)(2,1)}, bf16[2,256,128]{2,1,0:T(8,128)(2,1)}, bf16[2,256,128]{2,1,0:T(8,128)(2,1...) custom-call(s32[2]{0:T(128)} %pad_add_fusion.3.place, ...), custom_call_target="tpu_custom_call" | custom-call | tf_op jit(solution)/shard_map/split/pallas_call | solution.py:83
  34.9 3.0 %collective-permute-start.3 = (s32[1,16,8]{1,2,0:T(8,128)}, s32[1,16,8]{1,2,0:T(8,128)S(1)}, u32[]{:S(2)}, u32[]{:S(2)}) collective-permute-start(s32[1,16,8]{1,2,0:T(8,128)} %bitcast.3), channel_id=1, source_target_pairs={{0,1},{1,0},{2,3},{3,2},{4,5},{5,4},{6,7},{7,6},{8,9},{9,8},{10,11... | collective-permute-start | bytes 1544 | tf_op jit(solution)/shard_map/ppermute | solution.py:265
  38.0 1.5 collective-permute-start.1
  40.2 0.8 copy.15
  41.2 0.7 pad_add_fusion.2
  41.9 1.6 collective-permute-start.4
  43.5 2.1 %collective-permute-done.4 = s32[2,16,8]{1,2,0:T(8,128)S(1)} collective-permute-done((s32[2,16,8]{1,2,0:T(8,128)S(1)}, s32[2,16,8]{1,2,0:T(8,128)S(1)}, u32[]{:S(2)}, u32[]{:S(2)}) %collective-permute-start.4) | collective-permute-done | bytes 1056 | tf_op jit(solution)/shard_map/ppermute | solution.py:265
  45.5 0.7 pad_add_fusion.1
  46.2 2.6 %collective-permute-start.5 = (s32[4,16,8]{1,2,0:T(8,128)S(1)}, s32[4,16,8]{1,2,0:T(8,128)S(1)}, u32[]{:S(2)}, u32[]{:S(2)}) collective-permute-start(s32[4,16,8]{1,2,0:T(8,128)S(1)} %pad_add_fusion.1), channel_id=1, source_target_pairs={{0,4},{1,5},{2,6},{3,7},{4,0},{5,1},{6,2},{7,3},{8,12},{9,13},{10,... | collective-permute-start | bytes 6152 | tf_op jit(solution)/shard_map/ppermute | solution.py:265
  48.8 2.0 %collective-permute-done.5 = s32[4,16,8]{1,2,0:T(8,128)S(1)} collective-permute-done((s32[4,16,8]{1,2,0:T(8,128)S(1)}, s32[4,16,8]{1,2,0:T(8,128)S(1)}, u32[]{:S(2)}, u32[]{:S(2)}) %collective-permute-start.5) | collective-permute-done | bytes 2080 | tf_op jit(solution)/shard_map/ppermute | solution.py:265
  51.3 1.8 %collective-permute-start.2 = (bf16[2,256,128]{2,1,0:T(8,128)(2,1)}, bf16[2,256,128]{2,1,0:T(8,128)(2,1)S(1)}, u32[]{:S(2)}, u32[]{:S(2)}) collective-permute-start(bf16[2,256,128]{2,1,0:T(8,128)(2,1)} %get-tuple-element.57), channel_id=1, source_target_pairs={{0,24},{8,16},{16,8},{24,0},{1,25},{9,17},{17,9},{25,1},{2,26},{10... | collective-permute-start | bytes 393224 | tf_op jit(solution)/shard_map/ppermute | solution.py:265
  53.4 3.4 %collective-permute-done.8.refs_3_ = bf16[2,256,128]{2,1,0:T(8,128)(2,1)S(1)} collective-permute-done((bf16[2,256,128]{2,1,0:T(8,128)(2,1)}, bf16[2,256,128]{2,1,0:T(8,128)(2,1)S(1)}, u32[]{:S(2)}, u32[]{:S(2)}) %collective-permute-start.8) | collective-permute-done | bytes 131104 | tf_op jit(solution)/shard_map/ppermute | solution.py:265
  56.8 0.9 copy-done
  59.0 2.7 %collective-permute-start.16 = (bf16[2,3,64,128]{3,2,1,0:T(8,128)(2,1)S(1)}, bf16[2,3,64,128]{3,2,1,0:T(8,128)(2,1)S(1)}, u32[]{:S(2)}, u32[]{:S(2)}) collective-permute-start(bf16[2,3,64,128]{3,2,1,0:T(8,128)(2,1)S(1)} %get-tuple-element.70), channel_id=1, source_target_pairs={{0,4},{1,5},{2,6},{3,7},{4,0},{5,1},{6,2},{7,3},{8,12},{9,13},{10,... | collective-permute-start | bytes 294920 | tf_op jit(solution)/shard_map/ppermute | solution.py:265
  62.2 3.7 %collective-permute-start.18 = (bf16[2,3,64,128]{3,2,1,0:T(8,128)(2,1)S(1)}, bf16[2,3,64,128]{3,2,1,0:T(8,128)(2,1)S(1)}, u32[]{:S(2)}, u32[]{:S(2)}) collective-permute-start(bf16[2,3,64,128]{3,2,1,0:T(8,128)(2,1)S(1)} %get-tuple-element.72), channel_id=1, source_target_pairs={{0,6},{1,7},{2,4},{3,5},{4,2},{5,3},{6,0},{7,1},{8,14},{9,15},{10,... | collective-permute-start | bytes 294920 | tf_op jit(solution)/shard_map/ppermute | solution.py:265
  65.9 1.1 collective-permute-start.19
  66.9 0.9 copy-done.1
  67.9 0.7 pick.2
  69.2 4.9 %collective-permute-done.16.refs_7_ = bf16[2,3,64,128]{3,2,1,0:T(8,128)(2,1)S(1)} collective-permute-done((bf16[2,3,64,128]{3,2,1,0:T(8,128)(2,1)S(1)}, bf16[2,3,64,128]{3,2,1,0:T(8,128)(2,1)S(1)}, u32[]{:S(2)}, u32[]{:S(2)}) %collective-permute-start.16) | collective-permute-done | bytes 98336 | tf_op jit(solution)/shard_map/ppermute | solution.py:265
  74.0 2.1 %collective-permute-done.17.refs_8_ = bf16[2,3,64,128]{3,2,1,0:T(8,128)(2,1)S(1)} collective-permute-done((bf16[2,3,64,128]{3,2,1,0:T(8,128)(2,1)S(1)}, bf16[2,3,64,128]{3,2,1,0:T(8,128)(2,1)S(1)}, u32[]{:S(2)}, u32[]{:S(2)}) %collective-permute-start.17) | collective-permute-done | bytes 98336 | tf_op jit(solution)/shard_map/ppermute | solution.py:265
  76.2 4.4 %collective-permute-start.12 = (bf16[2,3,64,128]{3,2,1,0:T(8,128)(2,1)S(1)}, bf16[2,3,64,128]{3,2,1,0:T(8,128)(2,1)S(1)}, u32[]{:S(2)}, u32[]{:S(2)}) collective-permute-start(bf16[2,3,64,128]{3,2,1,0:T(8,128)(2,1)S(1)} %get-tuple-element.66), channel_id=1, source_target_pairs={{0,4},{1,5},{2,6},{3,7},{4,0},{5,1},{6,2},{7,3},{8,12},{9,13},{10,... | collective-permute-start | bytes 294920 | tf_op jit(solution)/shard_map/ppermute | solution.py:265
  80.6 2.8 %collective-permute-start.13 = (bf16[2,3,64,128]{3,2,1,0:T(8,128)(2,1)S(1)}, bf16[2,3,64,128]{3,2,1,0:T(8,128)(2,1)S(1)}, u32[]{:S(2)}, u32[]{:S(2)}) collective-permute-start(bf16[2,3,64,128]{3,2,1,0:T(8,128)(2,1)S(1)} %get-tuple-element.67), channel_id=1, source_target_pairs={{0,5},{1,4},{2,7},{3,6},{4,1},{5,0},{6,3},{7,2},{8,13},{9,12},{10,... | collective-permute-start | bytes 294920 | tf_op jit(solution)/shard_map/ppermute | solution.py:265
  83.6 4.4 %collective-permute-start.15 = (bf16[2,3,64,128]{3,2,1,0:T(8,128)(2,1)S(1)}, bf16[2,3,64,128]{3,2,1,0:T(8,128)(2,1)S(1)}, u32[]{:S(2)}, u32[]{:S(2)}) collective-permute-start(bf16[2,3,64,128]{3,2,1,0:T(8,128)(2,1)S(1)} %get-tuple-element.69), channel_id=1, source_target_pairs={{0,7},{1,6},{2,5},{3,4},{4,3},{5,2},{6,1},{7,0},{8,15},{9,14},{10,... | collective-permute-start | bytes 294920 | tf_op jit(solution)/shard_map/ppermute | solution.py:265
  88.0 1.6 copy-done.4
  89.6 1.6 copy-done.5
  91.2 14.8 %attend.2 = (bf16[1024,1024]{1,0:T(8,128)(2,1)}, bf16[1024,1024]{1,0:T(8,128)(2,1)}, f32[2,16,64,128]{3,2,1,0:T(8,128)S(1)}, bf16[2,3,64,128]{3,2,1,0:T(8,128)(2...) custom-call(s32[2]{0:T(128)S(1)} %copy-done.3, ...), custom_call_target="tpu_custom_call" | custom-call | flops 3221225472 | bytes 20971520 | tf_op jit(solution)/shard_map/attend/pallas_call | solution.py:233
  106.1 1.7 collective-permute-start.20
  107.8 1.8 %collective-permute-start.22 = (bf16[2,3,64,128]{3,2,1,0:T(8,128)(2,1)S(1)}, bf16[2,3,64,128]{3,2,1,0:T(8,128)(2,1)S(1)}, u32[]{:S(2)}, u32[]{:S(2)}) collective-permute-start(bf16[2,3,64,128]{3,2,1,0:T(8,128)(2,1)S(1)} %get-tuple-element.81), channel_id=1, source_target_pairs={{0,3},{1,2},{2,1},{3,0},{4,7},{5,6},{6,5},{7,4},{8,11},{9,10},{10,... | collective-permute-start | bytes 294920 | tf_op jit(solution)/shard_map/ppermute | solution.py:269
  109.6 6.5 %collective-permute-start.23 = (bf16[2,3,64,128]{3,2,1,0:T(8,128)(2,1)S(1)}, bf16[2,3,64,128]{3,2,1,0:T(8,128)(2,1)S(1)}, u32[]{:S(2)}, u32[]{:S(2)}) collective-permute-start(bf16[2,3,64,128]{3,2,1,0:T(8,128)(2,1)S(1)} %get-tuple-element.82), channel_id=1, source_target_pairs={{0,4},{1,5},{2,6},{3,7},{4,0},{5,1},{6,2},{7,3},{8,12},{9,13},{10,... | collective-permute-start | bytes 294920 | tf_op jit(solution)/shard_map/ppermute | solution.py:269
  116.1 1.0 collective-permute-start.24
  117.1 4.2 %collective-permute-start.25 = (bf16[2,3,64,128]{3,2,1,0:T(8,128)(2,1)S(1)}, bf16[2,3,64,128]{3,2,1,0:T(8,128)(2,1)S(1)}, u32[]{:S(2)}, u32[]{:S(2)}) collective-permute-start(bf16[2,3,64,128]{3,2,1,0:T(8,128)(2,1)S(1)} %get-tuple-element.84), channel_id=1, source_target_pairs={{0,6},{1,7},{2,4},{3,5},{4,2},{5,3},{6,0},{7,1},{8,14},{9,15},{10,... | collective-permute-start | bytes 294920 | tf_op jit(solution)/shard_map/ppermute | solution.py:269
  121.3 1.4 collective-permute-start.26
  122.7 14.8 %attend.3 = (bf16[1024,1024]{1,0:T(8,128)(2,1)}, bf16[1024,1024]{1,0:T(8,128)(2,1)}, f32[2,16,64,128]{3,2,1,0:T(8,128)S(1)}, bf16[2,3,64,128]{3,2,1,0:T(8,128)(2...) custom-call(s32[2]{0:T(128)S(1)} %copy-done.3, ...), custom_call_target="tpu_custom_call", output_to_operand_aliasing={{0}: (15, {}), {1}: (16, {})} | custom-call | flops 3221225472 | bytes 20971520 | tf_op jit(solution)/shard_map/attend/pallas_call | solution.py:233
  137.6 1.0 collective-permute-start.30
  138.6 2.5 %collective-permute-start.32 = (bf16[2,3,64,128]{3,2,1,0:T(8,128)(2,1)S(1)}, bf16[2,3,64,128]{3,2,1,0:T(8,128)(2,1)S(1)}, u32[]{:S(2)}, u32[]{:S(2)}) collective-permute-start(bf16[2,3,64,128]{3,2,1,0:T(8,128)(2,1)S(1)} %get-tuple-element.93), channel_id=1, source_target_pairs={{0,3},{1,2},{2,1},{3,0},{4,7},{5,6},{6,5},{7,4},{8,11},{9,10},{10,... | collective-permute-start | bytes 294920 | tf_op jit(solution)/shard_map/ppermute | solution.py:269
  141.1 0.8 gather_sum.2
  142.0 1.1 collective-permute-start.33
  143.0 2.4 %collective-permute-start.34 = (bf16[2,3,64,128]{3,2,1,0:T(8,128)(2,1)S(1)}, bf16[2,3,64,128]{3,2,1,0:T(8,128)(2,1)S(1)}, u32[]{:S(2)}, u32[]{:S(2)}) collective-permute-start(bf16[2,3,64,128]{3,2,1,0:T(8,128)(2,1)S(1)} %get-tuple-element.95), channel_id=1, source_target_pairs={{0,5},{1,4},{2,7},{3,6},{4,1},{5,0},{6,3},{7,2},{8,13},{9,12},{10,... | collective-permute-start | bytes 294920 | tf_op jit(solution)/shard_map/ppermute | solution.py:269
  145.4 2.9 %collective-permute-start.35 = (bf16[2,3,64,128]{3,2,1,0:T(8,128)(2,1)S(1)}, bf16[2,3,64,128]{3,2,1,0:T(8,128)(2,1)S(1)}, u32[]{:S(2)}, u32[]{:S(2)}) collective-permute-start(bf16[2,3,64,128]{3,2,1,0:T(8,128)(2,1)S(1)} %get-tuple-element.96), channel_id=1, source_target_pairs={{0,6},{1,7},{2,4},{3,5},{4,2},{5,3},{6,0},{7,1},{8,14},{9,15},{10,... | collective-permute-start | bytes 294920 | tf_op jit(solution)/shard_map/ppermute | solution.py:269
  148.3 1.4 collective-permute-start.36
  149.7 6.5 %collective-permute-done.33.refs_3_ = bf16[2,3,64,128]{3,2,1,0:T(8,128)(2,1)S(1)} collective-permute-done((bf16[2,3,64,128]{3,2,1,0:T(8,128)(2,1)S(1)}, bf16[2,3,64,128]{3,2,1,0:T(8,128)(2,1)S(1)}, u32[]{:S(2)}, u32[]{:S(2)}) %collective-permute-start.33) | collective-permute-done | bytes 98336 | tf_op jit(solution)/shard_map/ppermute | solution.py:269
  156.2 3.2 %collective-permute-done.34.refs_4_ = bf16[2,3,64,128]{3,2,1,0:T(8,128)(2,1)S(1)} collective-permute-done((bf16[2,3,64,128]{3,2,1,0:T(8,128)(2,1)S(1)}, bf16[2,3,64,128]{3,2,1,0:T(8,128)(2,1)S(1)}, u32[]{:S(2)}, u32[]{:S(2)}) %collective-permute-start.34) | collective-permute-done | bytes 98336 | tf_op jit(solution)/shard_map/ppermute | solution.py:269
  159.3 0.8 gather_sum.3
  160.3 2.1 %collective-permute-start.38 = (bf16[2,256,128]{2,1,0:T(8,128)(2,1)S(1)}, bf16[2,256,128]{2,1,0:T(8,128)(2,1)S(1)}, u32[]{:S(2)}, u32[]{:S(2)}) collective-permute-start(bf16[2,256,128]{2,1,0:T(8,128)(2,1)S(1)} %get-tuple-element.100), channel_id=1, source_target_pairs={{0,16},{8,24},{16,0},{24,8},{1,17},{9,25},{17,1},{25,9},{2,18},{10... | collective-permute-start | bytes 393224 | tf_op jit(solution)/shard_map/ppermute | solution.py:269
  162.4 2.7 %collective-permute-done.29.refs_3_ = bf16[2,256,128]{2,1,0:T(8,128)(2,1)S(1)} collective-permute-done((bf16[2,256,128]{2,1,0:T(8,128)(2,1)S(1)}, bf16[2,256,128]{2,1,0:T(8,128)(2,1)S(1)}, u32[]{:S(2)}, u32[]{:S(2)}) %collective-permute-start.29) | collective-permute-done | bytes 131104 | tf_op jit(solution)/shard_map/ppermute | solution.py:269
  165.1 2.2 %collective-permute-done.38.refs_6_ = bf16[2,256,128]{2,1,0:T(8,128)(2,1)S(1)} collective-permute-done((bf16[2,256,128]{2,1,0:T(8,128)(2,1)S(1)}, bf16[2,256,128]{2,1,0:T(8,128)(2,1)S(1)}, u32[]{:S(2)}, u32[]{:S(2)}) %collective-permute-start.38) | collective-permute-done | bytes 131104 | tf_op jit(solution)/shard_map/ppermute | solution.py:269
  167.3 3.1 %collective-permute-done.39.refs_7_ = bf16[2,256,128]{2,1,0:T(8,128)(2,1)S(1)} collective-permute-done((bf16[2,256,128]{2,1,0:T(8,128)(2,1)S(1)}, bf16[2,256,128]{2,1,0:T(8,128)(2,1)S(1)}, u32[]{:S(2)}, u32[]{:S(2)}) %collective-permute-start.39) | collective-permute-done | bytes 131104 | tf_op jit(solution)/shard_map/ppermute | solution.py:269
  170.4 1.6 join.1
  (71 shorter events, 5.2 us)
Async XLA Ops:
  34.9 6.3 %collective-permute-start.3 = (s32[1,16,8]{1,2,0:T(8,128)}, s32[1,16,8]{1,2,0:T(8,128)S(1)}, u32[]{:S(2)}, u32[]{:S(2)}) collective-permute-start(s32[1,16,8]{1,2,0:T(8,128)} %bitcast.3), channel_id=1, source_target_pairs={{0,1},{1,0},{2,3},{3,2},{4,5},{5,4},{6,7},{7,6},{8,9},{9,8},{10,11... | collective-permute-start | bytes 1544 | tf_op jit(solution)/shard_map/ppermute | solution.py:265
  37.9 24.2 %collective-permute-start = (bf16[2,256,128]{2,1,0:T(8,128)(2,1)}, bf16[2,256,128]{2,1,0:T(8,128)(2,1)S(1)}, u32[]{:S(2)}, u32[]{:S(2)}) collective-permute-start(bf16[2,256,128]{2,1,0:T(8,128)(2,1)} %get-tuple-element.55), channel_id=1, source_target_pairs={{0,8},{8,0},{16,24},{24,16},{1,9},{9,1},{17,25},{25,17},{2,10},{10... | collective-permute-start | bytes 393224 | tf_op jit(solution)/shard_map/ppermute | solution.py:265
  38.0 27.9 %collective-permute-start.1 = (bf16[2,256,128]{2,1,0:T(8,128)(2,1)}, bf16[2,256,128]{2,1,0:T(8,128)(2,1)S(1)}, u32[]{:S(2)}, u32[]{:S(2)}) collective-permute-start(bf16[2,256,128]{2,1,0:T(8,128)(2,1)} %get-tuple-element.56), channel_id=1, source_target_pairs={{0,16},{8,24},{16,0},{24,8},{1,17},{9,25},{17,1},{25,9},{2,18},{10... | collective-permute-start | bytes 393224 | tf_op jit(solution)/shard_map/ppermute | solution.py:265
  39.4 11.8 %collective-permute-start.6 = (bf16[2,256,128]{2,1,0:T(8,128)(2,1)}, bf16[2,256,128]{2,1,0:T(8,128)(2,1)S(1)}, u32[]{:S(2)}, u32[]{:S(2)}) collective-permute-start(bf16[2,256,128]{2,1,0:T(8,128)(2,1)} %get-tuple-element.60), channel_id=1, source_target_pairs={{0,8},{8,0},{16,24},{24,16},{1,9},{9,1},{17,25},{25,17},{2,10},{10... | collective-permute-start | bytes 393224 | tf_op jit(solution)/shard_map/ppermute | solution.py:265
  39.7 13.7 %collective-permute-start.7 = (bf16[2,256,128]{2,1,0:T(8,128)(2,1)}, bf16[2,256,128]{2,1,0:T(8,128)(2,1)S(1)}, u32[]{:S(2)}, u32[]{:S(2)}) collective-permute-start(bf16[2,256,128]{2,1,0:T(8,128)(2,1)} %get-tuple-element.61), channel_id=1, source_target_pairs={{0,16},{8,24},{16,0},{24,8},{1,17},{9,25},{17,1},{25,9},{2,18},{10... | collective-permute-start | bytes 393224 | tf_op jit(solution)/shard_map/ppermute | solution.py:265
  41.9 3.7 %collective-permute-start.4 = (s32[2,16,8]{1,2,0:T(8,128)S(1)}, s32[2,16,8]{1,2,0:T(8,128)S(1)}, u32[]{:S(2)}, u32[]{:S(2)}) collective-permute-start(s32[2,16,8]{1,2,0:T(8,128)S(1)} %pad_add_fusion.2), channel_id=1, source_target_pairs={{0,2},{1,3},{2,0},{3,1},{4,6},{5,7},{6,4},{7,5},{8,10},{9,11},{10,... | collective-permute-start | bytes 3080 | tf_op jit(solution)/shard_map/ppermute | solution.py:265
  46.2 4.6 %collective-permute-start.5 = (s32[4,16,8]{1,2,0:T(8,128)S(1)}, s32[4,16,8]{1,2,0:T(8,128)S(1)}, u32[]{:S(2)}, u32[]{:S(2)}) collective-permute-start(s32[4,16,8]{1,2,0:T(8,128)S(1)} %pad_add_fusion.1), channel_id=1, source_target_pairs={{0,4},{1,5},{2,6},{3,7},{4,0},{5,1},{6,2},{7,3},{8,12},{9,13},{10,... | collective-permute-start | bytes 6152 | tf_op jit(solution)/shard_map/ppermute | solution.py:265
  50.9 6.0 %collective-permute-start.8 = (bf16[2,256,128]{2,1,0:T(8,128)(2,1)}, bf16[2,256,128]{2,1,0:T(8,128)(2,1)S(1)}, u32[]{:S(2)}, u32[]{:S(2)}) collective-permute-start(bf16[2,256,128]{2,1,0:T(8,128)(2,1)} %get-tuple-element.62), channel_id=1, source_target_pairs={{0,24},{8,16},{16,8},{24,0},{1,25},{9,17},{17,9},{25,1},{2,26},{10... | collective-permute-start | bytes 393224 | tf_op jit(solution)/shard_map/ppermute | solution.py:265
  51.3 15.7 %collective-permute-start.2 = (bf16[2,256,128]{2,1,0:T(8,128)(2,1)}, bf16[2,256,128]{2,1,0:T(8,128)(2,1)S(1)}, u32[]{:S(2)}, u32[]{:S(2)}) collective-permute-start(bf16[2,256,128]{2,1,0:T(8,128)(2,1)} %get-tuple-element.57), channel_id=1, source_target_pairs={{0,24},{8,16},{16,8},{24,0},{1,25},{9,17},{17,9},{25,1},{2,26},{10... | collective-permute-start | bytes 393224 | tf_op jit(solution)/shard_map/ppermute | solution.py:265
  56.8 0.9 copy-start
  57.7 0.6 copy-start.3
  59.0 15.1 %collective-permute-start.16 = (bf16[2,3,64,128]{3,2,1,0:T(8,128)(2,1)S(1)}, bf16[2,3,64,128]{3,2,1,0:T(8,128)(2,1)S(1)}, u32[]{:S(2)}, u32[]{:S(2)}) collective-permute-start(bf16[2,3,64,128]{3,2,1,0:T(8,128)(2,1)S(1)} %get-tuple-element.70), channel_id=1, source_target_pairs={{0,4},{1,5},{2,6},{3,7},{4,0},{5,1},{6,2},{7,3},{8,12},{9,13},{10,... | collective-permute-start | bytes 294920 | tf_op jit(solution)/shard_map/ppermute | solution.py:265
  61.6 14.5 %collective-permute-start.17 = (bf16[2,3,64,128]{3,2,1,0:T(8,128)(2,1)S(1)}, bf16[2,3,64,128]{3,2,1,0:T(8,128)(2,1)S(1)}, u32[]{:S(2)}, u32[]{:S(2)}) collective-permute-start(bf16[2,3,64,128]{3,2,1,0:T(8,128)(2,1)S(1)} %get-tuple-element.71), channel_id=1, source_target_pairs={{0,5},{1,4},{2,7},{3,6},{4,1},{5,0},{6,3},{7,2},{8,13},{9,12},{10,... | collective-permute-start | bytes 294920 | tf_op jit(solution)/shard_map/ppermute | solution.py:265
  62.2 14.0 %collective-permute-start.18 = (bf16[2,3,64,128]{3,2,1,0:T(8,128)(2,1)S(1)}, bf16[2,3,64,128]{3,2,1,0:T(8,128)(2,1)S(1)}, u32[]{:S(2)}, u32[]{:S(2)}) collective-permute-start(bf16[2,3,64,128]{3,2,1,0:T(8,128)(2,1)S(1)} %get-tuple-element.72), channel_id=1, source_target_pairs={{0,6},{1,7},{2,4},{3,5},{4,2},{5,3},{6,0},{7,1},{8,14},{9,15},{10,... | collective-permute-start | bytes 294920 | tf_op jit(solution)/shard_map/ppermute | solution.py:265
  65.9 14.7 %collective-permute-start.19 = (bf16[2,3,64,128]{3,2,1,0:T(8,128)(2,1)S(1)}, bf16[2,3,64,128]{3,2,1,0:T(8,128)(2,1)S(1)}, u32[]{:S(2)}, u32[]{:S(2)}) collective-permute-start(bf16[2,3,64,128]{3,2,1,0:T(8,128)(2,1)S(1)} %get-tuple-element.73), channel_id=1, source_target_pairs={{0,7},{1,6},{2,5},{3,4},{4,3},{5,2},{6,1},{7,0},{8,15},{9,14},{10,... | collective-permute-start | bytes 294920 | tf_op jit(solution)/shard_map/ppermute | solution.py:265
  66.9 0.9 copy-start.1
  68.5 14.9 %collective-permute-start.9 = (bf16[2,2,3,64,128]{4,3,2,1,0:T(8,128)(2,1)S(1)}, bf16[2,2,3,64,128]{4,3,2,1,0:T(8,128)(2,1)S(1)}, u32[]{:S(2)}, u32[]{:S(2)}) collective-permute-start(bf16[2,2,3,64,128]{4,3,2,1,0:T(8,128)(2,1)S(1)} %get-tuple-element.63), channel_id=1, source_target_pairs={{0,1},{1,0},{2,3},{3,2},{4,5},{5,4},{6,7},{7,6},{8,9},{9,8},{10,11... | collective-permute-start | bytes 589832 | tf_op jit(solution)/shard_map/ppermute | solution.py:265
  74.0 9.6 %collective-permute-start.10 = (bf16[2,2,3,64,128]{4,3,2,1,0:T(8,128)(2,1)S(1)}, bf16[2,2,3,64,128]{4,3,2,1,0:T(8,128)(2,1)S(1)}, u32[]{:S(2)}, u32[]{:S(2)}) collective-permute-start(bf16[2,2,3,64,128]{4,3,2,1,0:T(8,128)(2,1)S(1)} %get-tuple-element.64), channel_id=1, source_target_pairs={{0,2},{1,3},{2,0},{3,1},{4,6},{5,7},{6,4},{7,5},{8,10},{9,11},{10,... | collective-permute-start | bytes 589832 | tf_op jit(solution)/shard_map/ppermute | solution.py:265
  76.1 11.9 %collective-permute-start.11 = (bf16[2,2,3,64,128]{4,3,2,1,0:T(8,128)(2,1)S(1)}, bf16[2,2,3,64,128]{4,3,2,1,0:T(8,128)(2,1)S(1)}, u32[]{:S(2)}, u32[]{:S(2)}) collective-permute-start(bf16[2,2,3,64,128]{4,3,2,1,0:T(8,128)(2,1)S(1)} %get-tuple-element.65), channel_id=1, source_target_pairs={{0,3},{1,2},{2,1},{3,0},{4,7},{5,6},{6,5},{7,4},{8,11},{9,10},{10,... | collective-permute-start | bytes 589832 | tf_op jit(solution)/shard_map/ppermute | solution.py:265
  76.2 31.6 %collective-permute-start.12 = (bf16[2,3,64,128]{3,2,1,0:T(8,128)(2,1)S(1)}, bf16[2,3,64,128]{3,2,1,0:T(8,128)(2,1)S(1)}, u32[]{:S(2)}, u32[]{:S(2)}) collective-permute-start(bf16[2,3,64,128]{3,2,1,0:T(8,128)(2,1)S(1)} %get-tuple-element.66), channel_id=1, source_target_pairs={{0,4},{1,5},{2,6},{3,7},{4,0},{5,1},{6,2},{7,3},{8,12},{9,13},{10,... | collective-permute-start | bytes 294920 | tf_op jit(solution)/shard_map/ppermute | solution.py:265
  80.6 27.2 %collective-permute-start.13 = (bf16[2,3,64,128]{3,2,1,0:T(8,128)(2,1)S(1)}, bf16[2,3,64,128]{3,2,1,0:T(8,128)(2,1)S(1)}, u32[]{:S(2)}, u32[]{:S(2)}) collective-permute-start(bf16[2,3,64,128]{3,2,1,0:T(8,128)(2,1)S(1)} %get-tuple-element.67), channel_id=1, source_target_pairs={{0,5},{1,4},{2,7},{3,6},{4,1},{5,0},{6,3},{7,2},{8,13},{9,12},{10,... | collective-permute-start | bytes 294920 | tf_op jit(solution)/shard_map/ppermute | solution.py:265
  83.4 26.2 %collective-permute-start.14 = (bf16[2,3,64,128]{3,2,1,0:T(8,128)(2,1)S(1)}, bf16[2,3,64,128]{3,2,1,0:T(8,128)(2,1)S(1)}, u32[]{:S(2)}, u32[]{:S(2)}) collective-permute-start(bf16[2,3,64,128]{3,2,1,0:T(8,128)(2,1)S(1)} %get-tuple-element.68), channel_id=1, source_target_pairs={{0,6},{1,7},{2,4},{3,5},{4,2},{5,3},{6,0},{7,1},{8,14},{9,15},{10,... | collective-permute-start | bytes 294920 | tf_op jit(solution)/shard_map/ppermute | solution.py:265
  83.6 39.1 %copy-start.2 = (bf16[2,256,128]{2,1,0:T(8,128)(2,1)S(1)}, bf16[2,256,128]{2,1,0:T(8,128)(2,1)}, u32[]{:S(2)}) copy-start(bf16[2,256,128]{2,1,0:T(8,128)(2,1)} %get-tuple-element.54.refs_4_.refs_0_) | copy-start | bytes 393220
  83.6 32.5 %collective-permute-start.15 = (bf16[2,3,64,128]{3,2,1,0:T(8,128)(2,1)S(1)}, bf16[2,3,64,128]{3,2,1,0:T(8,128)(2,1)S(1)}, u32[]{:S(2)}, u32[]{:S(2)}) collective-permute-start(bf16[2,3,64,128]{3,2,1,0:T(8,128)(2,1)S(1)} %get-tuple-element.69), channel_id=1, source_target_pairs={{0,7},{1,6},{2,5},{3,4},{4,3},{5,2},{6,1},{7,0},{8,15},{9,14},{10,... | collective-permute-start | bytes 294920 | tf_op jit(solution)/shard_map/ppermute | solution.py:265
  88.0 1.6 copy-start.4
  89.6 1.6 copy-start.5
  106.1 11.0 %collective-permute-start.20 = (bf16[2,3,64,128]{3,2,1,0:T(8,128)(2,1)S(1)}, bf16[2,3,64,128]{3,2,1,0:T(8,128)(2,1)S(1)}, u32[]{:S(2)}, u32[]{:S(2)}) collective-permute-start(bf16[2,3,64,128]{3,2,1,0:T(8,128)(2,1)S(1)} %get-tuple-element.79), channel_id=1, source_target_pairs={{0,1},{1,0},{2,3},{3,2},{4,5},{5,4},{6,7},{7,6},{8,9},{9,8},{10,11... | collective-permute-start | bytes 294920 | tf_op jit(solution)/shard_map/ppermute | solution.py:269
  107.8 13.6 %collective-permute-start.21 = (bf16[2,3,64,128]{3,2,1,0:T(8,128)(2,1)S(1)}, bf16[2,3,64,128]{3,2,1,0:T(8,128)(2,1)S(1)}, u32[]{:S(2)}, u32[]{:S(2)}) collective-permute-start(bf16[2,3,64,128]{3,2,1,0:T(8,128)(2,1)S(1)} %get-tuple-element.80), channel_id=1, source_target_pairs={{0,2},{1,3},{2,0},{3,1},{4,6},{5,7},{6,4},{7,5},{8,10},{9,11},{10,... | collective-permute-start | bytes 294920 | tf_op jit(solution)/shard_map/ppermute | solution.py:269
  107.8 29.8 %collective-permute-start.22 = (bf16[2,3,64,128]{3,2,1,0:T(8,128)(2,1)S(1)}, bf16[2,3,64,128]{3,2,1,0:T(8,128)(2,1)S(1)}, u32[]{:S(2)}, u32[]{:S(2)}) collective-permute-start(bf16[2,3,64,128]{3,2,1,0:T(8,128)(2,1)S(1)} %get-tuple-element.81), channel_id=1, source_target_pairs={{0,3},{1,2},{2,1},{3,0},{4,7},{5,6},{6,5},{7,4},{8,11},{9,10},{10,... | collective-permute-start | bytes 294920 | tf_op jit(solution)/shard_map/ppermute | solution.py:269
  109.6 29.0 %collective-permute-start.23 = (bf16[2,3,64,128]{3,2,1,0:T(8,128)(2,1)S(1)}, bf16[2,3,64,128]{3,2,1,0:T(8,128)(2,1)S(1)}, u32[]{:S(2)}, u32[]{:S(2)}) collective-permute-start(bf16[2,3,64,128]{3,2,1,0:T(8,128)(2,1)S(1)} %get-tuple-element.82), channel_id=1, source_target_pairs={{0,4},{1,5},{2,6},{3,7},{4,0},{5,1},{6,2},{7,3},{8,12},{9,13},{10,... | collective-permute-start | bytes 294920 | tf_op jit(solution)/shard_map/ppermute | solution.py:269
  116.1 22.4 %collective-permute-start.24 = (bf16[2,3,64,128]{3,2,1,0:T(8,128)(2,1)S(1)}, bf16[2,3,64,128]{3,2,1,0:T(8,128)(2,1)S(1)}, u32[]{:S(2)}, u32[]{:S(2)}) collective-permute-start(bf16[2,3,64,128]{3,2,1,0:T(8,128)(2,1)S(1)} %get-tuple-element.83), channel_id=1, source_target_pairs={{0,5},{1,4},{2,7},{3,6},{4,1},{5,0},{6,3},{7,2},{8,13},{9,12},{10,... | collective-permute-start | bytes 294920 | tf_op jit(solution)/shard_map/ppermute | solution.py:269
  117.1 24.0 %collective-permute-start.25 = (bf16[2,3,64,128]{3,2,1,0:T(8,128)(2,1)S(1)}, bf16[2,3,64,128]{3,2,1,0:T(8,128)(2,1)S(1)}, u32[]{:S(2)}, u32[]{:S(2)}) collective-permute-start(bf16[2,3,64,128]{3,2,1,0:T(8,128)(2,1)S(1)} %get-tuple-element.84), channel_id=1, source_target_pairs={{0,6},{1,7},{2,4},{3,5},{4,2},{5,3},{6,0},{7,1},{8,14},{9,15},{10,... | collective-permute-start | bytes 294920 | tf_op jit(solution)/shard_map/ppermute | solution.py:269
  121.3 19.7 %collective-permute-start.26 = (bf16[2,3,64,128]{3,2,1,0:T(8,128)(2,1)S(1)}, bf16[2,3,64,128]{3,2,1,0:T(8,128)(2,1)S(1)}, u32[]{:S(2)}, u32[]{:S(2)}) collective-permute-start(bf16[2,3,64,128]{3,2,1,0:T(8,128)(2,1)S(1)} %get-tuple-element.85), channel_id=1, source_target_pairs={{0,7},{1,6},{2,5},{3,4},{4,3},{5,2},{6,1},{7,0},{8,15},{9,14},{10,... | collective-permute-start | bytes 294920 | tf_op jit(solution)/shard_map/ppermute | solution.py:269
  137.6 5.5 %collective-permute-start.30 = (bf16[2,3,64,128]{3,2,1,0:T(8,128)(2,1)S(1)}, bf16[2,3,64,128]{3,2,1,0:T(8,128)(2,1)S(1)}, u32[]{:S(2)}, u32[]{:S(2)}) collective-permute-start(bf16[2,3,64,128]{3,2,1,0:T(8,128)(2,1)S(1)} %get-tuple-element.91), channel_id=1, source_target_pairs={{0,1},{1,0},{2,3},{3,2},{4,5},{5,4},{6,7},{7,6},{8,9},{9,8},{10,11... | collective-permute-start | bytes 294920 | tf_op jit(solution)/shard_map/ppermute | solution.py:269
  138.5 6.8 %collective-permute-start.31 = (bf16[2,3,64,128]{3,2,1,0:T(8,128)(2,1)S(1)}, bf16[2,3,64,128]{3,2,1,0:T(8,128)(2,1)S(1)}, u32[]{:S(2)}, u32[]{:S(2)}) collective-permute-start(bf16[2,3,64,128]{3,2,1,0:T(8,128)(2,1)S(1)} %get-tuple-element.92), channel_id=1, source_target_pairs={{0,2},{1,3},{2,0},{3,1},{4,6},{5,7},{6,4},{7,5},{8,10},{9,11},{10,... | collective-permute-start | bytes 294920 | tf_op jit(solution)/shard_map/ppermute | solution.py:269
  138.6 9.8 %collective-permute-start.32 = (bf16[2,3,64,128]{3,2,1,0:T(8,128)(2,1)S(1)}, bf16[2,3,64,128]{3,2,1,0:T(8,128)(2,1)S(1)}, u32[]{:S(2)}, u32[]{:S(2)}) collective-permute-start(bf16[2,3,64,128]{3,2,1,0:T(8,128)(2,1)S(1)} %get-tuple-element.93), channel_id=1, source_target_pairs={{0,3},{1,2},{2,1},{3,0},{4,7},{5,6},{6,5},{7,4},{8,11},{9,10},{10,... | collective-permute-start | bytes 294920 | tf_op jit(solution)/shard_map/ppermute | solution.py:269
  141.9 20.5 %collective-permute-start.27 = (bf16[2,256,128]{2,1,0:T(8,128)(2,1)S(1)}, bf16[2,256,128]{2,1,0:T(8,128)(2,1)S(1)}, u32[]{:S(2)}, u32[]{:S(2)}) collective-permute-start(bf16[2,256,128]{2,1,0:T(8,128)(2,1)S(1)} %get-tuple-element.87), channel_id=1, source_target_pairs={{0,8},{8,0},{16,24},{24,16},{1,9},{9,1},{17,25},{25,17},{2,10},{10... | collective-permute-start | bytes 393224 | tf_op jit(solution)/shard_map/ppermute | solution.py:269
  142.0 14.2 %collective-permute-start.33 = (bf16[2,3,64,128]{3,2,1,0:T(8,128)(2,1)S(1)}, bf16[2,3,64,128]{3,2,1,0:T(8,128)(2,1)S(1)}, u32[]{:S(2)}, u32[]{:S(2)}) collective-permute-start(bf16[2,3,64,128]{3,2,1,0:T(8,128)(2,1)S(1)} %get-tuple-element.94), channel_id=1, source_target_pairs={{0,4},{1,5},{2,6},{3,7},{4,0},{5,1},{6,2},{7,3},{8,12},{9,13},{10,... | collective-permute-start | bytes 294920 | tf_op jit(solution)/shard_map/ppermute | solution.py:269
  143.0 16.3 %collective-permute-start.34 = (bf16[2,3,64,128]{3,2,1,0:T(8,128)(2,1)S(1)}, bf16[2,3,64,128]{3,2,1,0:T(8,128)(2,1)S(1)}, u32[]{:S(2)}, u32[]{:S(2)}) collective-permute-start(bf16[2,3,64,128]{3,2,1,0:T(8,128)(2,1)S(1)} %get-tuple-element.95), channel_id=1, source_target_pairs={{0,5},{1,4},{2,7},{3,6},{4,1},{5,0},{6,3},{7,2},{8,13},{9,12},{10,... | collective-permute-start | bytes 294920 | tf_op jit(solution)/shard_map/ppermute | solution.py:269
  145.4 14.0 %collective-permute-start.35 = (bf16[2,3,64,128]{3,2,1,0:T(8,128)(2,1)S(1)}, bf16[2,3,64,128]{3,2,1,0:T(8,128)(2,1)S(1)}, u32[]{:S(2)}, u32[]{:S(2)}) collective-permute-start(bf16[2,3,64,128]{3,2,1,0:T(8,128)(2,1)S(1)} %get-tuple-element.96), channel_id=1, source_target_pairs={{0,6},{1,7},{2,4},{3,5},{4,2},{5,3},{6,0},{7,1},{8,14},{9,15},{10,... | collective-permute-start | bytes 294920 | tf_op jit(solution)/shard_map/ppermute | solution.py:269
  148.3 11.0 %collective-permute-start.36 = (bf16[2,3,64,128]{3,2,1,0:T(8,128)(2,1)S(1)}, bf16[2,3,64,128]{3,2,1,0:T(8,128)(2,1)S(1)}, u32[]{:S(2)}, u32[]{:S(2)}) collective-permute-start(bf16[2,3,64,128]{3,2,1,0:T(8,128)(2,1)S(1)} %get-tuple-element.97), channel_id=1, source_target_pairs={{0,7},{1,6},{2,5},{3,4},{4,3},{5,2},{6,1},{7,0},{8,15},{9,14},{10,... | collective-permute-start | bytes 294920 | tf_op jit(solution)/shard_map/ppermute | solution.py:269
  156.2 6.2 %collective-permute-start.28 = (bf16[2,256,128]{2,1,0:T(8,128)(2,1)S(1)}, bf16[2,256,128]{2,1,0:T(8,128)(2,1)S(1)}, u32[]{:S(2)}, u32[]{:S(2)}) collective-permute-start(bf16[2,256,128]{2,1,0:T(8,128)(2,1)S(1)} %get-tuple-element.88), channel_id=1, source_target_pairs={{0,16},{8,24},{16,0},{24,8},{1,17},{9,25},{17,1},{25,9},{2,18},{10... | collective-permute-start | bytes 393224 | tf_op jit(solution)/shard_map/ppermute | solution.py:269
  159.3 5.8 %collective-permute-start.29 = (bf16[2,256,128]{2,1,0:T(8,128)(2,1)S(1)}, bf16[2,256,128]{2,1,0:T(8,128)(2,1)S(1)}, u32[]{:S(2)}, u32[]{:S(2)}) collective-permute-start(bf16[2,256,128]{2,1,0:T(8,128)(2,1)S(1)} %get-tuple-element.89), channel_id=1, source_target_pairs={{0,24},{8,16},{16,8},{24,0},{1,25},{9,17},{17,9},{25,1},{2,26},{10... | collective-permute-start | bytes 393224 | tf_op jit(solution)/shard_map/ppermute | solution.py:269
  160.2 5.0 %collective-permute-start.37 = (bf16[2,256,128]{2,1,0:T(8,128)(2,1)S(1)}, bf16[2,256,128]{2,1,0:T(8,128)(2,1)S(1)}, u32[]{:S(2)}, u32[]{:S(2)}) collective-permute-start(bf16[2,256,128]{2,1,0:T(8,128)(2,1)S(1)} %get-tuple-element.99), channel_id=1, source_target_pairs={{0,8},{8,0},{16,24},{24,16},{1,9},{9,1},{17,25},{25,17},{2,10},{10... | collective-permute-start | bytes 393224 | tf_op jit(solution)/shard_map/ppermute | solution.py:269
  160.3 7.1 %collective-permute-start.38 = (bf16[2,256,128]{2,1,0:T(8,128)(2,1)S(1)}, bf16[2,256,128]{2,1,0:T(8,128)(2,1)S(1)}, u32[]{:S(2)}, u32[]{:S(2)}) collective-permute-start(bf16[2,256,128]{2,1,0:T(8,128)(2,1)S(1)} %get-tuple-element.100), channel_id=1, source_target_pairs={{0,16},{8,24},{16,0},{24,8},{1,17},{9,25},{17,1},{25,9},{2,18},{10... | collective-permute-start | bytes 393224 | tf_op jit(solution)/shard_map/ppermute | solution.py:269
  162.4 8.1 %collective-permute-start.39 = (bf16[2,256,128]{2,1,0:T(8,128)(2,1)S(1)}, bf16[2,256,128]{2,1,0:T(8,128)(2,1)S(1)}, u32[]{:S(2)}, u32[]{:S(2)}) collective-permute-start(bf16[2,256,128]{2,1,0:T(8,128)(2,1)S(1)} %get-tuple-element.101), channel_id=1, source_target_pairs={{0,24},{8,16},{16,8},{24,0},{1,25},{9,17},{17,9},{25,1},{2,26},{10... | collective-permute-start | bytes 393224 | tf_op jit(solution)/shard_map/ppermute | solution.py:269

commit v5 on v3

v5 whole, which is shorter than its diff:
```python
import functools

import jax
import jax.numpy as jnp
from jax import lax
from jax.experimental import pallas as pl
from jax.experimental.pallas import tpu as pltpu
from jax.sharding import PartitionSpec as P

HEAD_DIM = 128
GROUP = 4
BLK = 64
LIST = 8
CAP = 3
STEP_BLOCKS = 2
NEG_FILL = -1e30
SCALE = HEAD_DIM ** (-0.5)
LOG2E = 1.4426950408889634
VMEM_LIMIT = 50 * 1024 * 1024
VMEM_MOST = 60 * 1024 * 1024

NT = (((1,), (1,)), ((), ()))
NN = (((1,), (0,)), ((), ()))
TN = (((0,), (0,)), ((), ()))


def dot(a, b, dims):
    return lax.dot_general(a, b, dims, preferred_element_type=jnp.float32)


def params(limit=VMEM_LIMIT):
    return pltpu.CompilerParams(vmem_limit_bytes=limit)


def partner(me, r, count):
    return me ^ r if count & (count - 1) == 0 else (me + r) % count


def origin(me, r, count):
    return me ^ r if count & (count - 1) == 0 else (me + count - r) % count


def head_columns(place, r, heads, h, head_count):
    col = (partner(place[1], r, heads) * head_count + h) * HEAD_DIM
    return pl.ds(pl.multiple_of(col, HEAD_DIM), HEAD_DIM)


def split_kernel(place, k_ref, v_ref, *refs):
    *outs, sem = refs
    heads, head_count = len(outs), outs[0].shape[0]
    copies = []
    for r, out in enumerate(outs):
        for h in range(head_count):
            cols = head_columns(place, r, heads, h, head_count)
            for kv, ref in enumerate((k_ref, v_ref)):
                at = (r * head_count + h) * 2 + kv
                copies.append(pltpu.make_async_copy(ref.at[:, cols], out.at[h, kv], sem.at[at]))
    for copy in copies:
        copy.start()
    for copy in copies:
        copy.wait()


def join_kernel(place, *refs, heads):
    *pieces, k_ref, v_ref, sem = refs
    head_count = len(pieces) // heads
    copies = []
    for at, piece in enumerate(pieces):
        cols = head_columns(place, at % heads, heads, at // heads, head_count)
        for kv, ref in enumerate((k_ref, v_ref)):
            copies.append(pltpu.make_async_copy(piece.at[kv], ref.at[:, cols], sem.at[2 * at + kv]))
    for copy in copies:
        copy.start()
    for copy in copies:
        copy.wait()


def fill_table(place, own, h, table):
    heads = len(own)
    per_quarter = own[0].shape[2] // BLK
    for r in range(heads):
        first = origin(place[1], r, heads) * per_quarter
        for kv in range(2):
            for j in range(per_quarter):
                table[kv, first + j] = own[r][h, kv, j * BLK : (j + 1) * BLK, :]


def parts_of(refs, place, at, shard_count):
    if len(refs) == 1 and len(refs[0].shape) == 5:
        return [(refs[0].at[c], c) for c in range(shard_count)]
    return [(ref, at(place[0], r, shard_count)) for r, ref in enumerate(refs, 1)]


def pick_kernel(place, asked, *refs, heads, head_count, shard_count):
    own, outs, table = refs[:heads], refs[heads:-1], refs[-1]
    for h in range(head_count):
        fill_table(place, own, h, table)
        steps = shard_count - 1
        mine = outs[:steps] if h == 0 else outs[steps + h - 1 : steps + h]
        for out, c in parts_of(mine, place, partner, shard_count):
            for s in range(CAP):
                block = asked[c, s]
                for kv in range(2):
                    out[kv, s] = table[kv, block]


def attend_kernel(place, source, q_ref, g_ref, *refs, heads, fars, outs, head, shard_count):
    own, far = refs[:heads], refs[heads : heads + fars]
    table, total = refs[-2:]
    far_out = refs[-2 - outs : -2]
    o_ref, dq_ref, near_out = refs[-5 - outs : -2 - outs]
    step = pl.program_id(0)
    blocks_here = near_out.shape[1]

    @pl.when(step == 0)
    def _():
        fill_table(place, own, head, table)
        for part, c in parts_of(far, place, origin, shard_count):
            for kv in range(2):
                for s in range(CAP):
                    table[kv, blocks_here + c * CAP + s] = part[kv, s]
        total[...] = jnp.zeros_like(total)

    key_row = lax.broadcasted_iota(jnp.int32, (BLK, GROUP * BLK), 0)
    query_col = lax.broadcasted_iota(jnp.int32, (BLK, GROUP * BLK), 1) % BLK
    hidden = key_row > query_col
    for sub in range(STEP_BLOCKS):
        block = step * STEP_BLOCKS + sub
        rows = slice(sub * BLK, (sub + 1) * BLK)
        listed = [source[block * LIST + e] for e in range(LIST)]
        q = jnp.concatenate([q_ref[rows, g * HEAD_DIM : (g + 1) * HEAD_DIM] for g in range(GROUP)], axis=0)
        g_out = jnp.concatenate([g_ref[rows, g * HEAD_DIM : (g + 1) * HEAD_DIM] for g in range(GROUP)], axis=0)
        keys = jnp.concatenate([table[0, at] for at in listed], axis=0)
        values = jnp.concatenate([table[1, at] for at in listed], axis=0)
        scores = dot(keys, q, NT)
        parts = []
        for e in range(LIST):
            part = scores[e * BLK : (e + 1) * BLK]
            mask = hidden if e == 0 else hidden & (listed[e] == block)
            parts.append(jnp.where(mask, NEG_FILL, part))
        scores = jnp.concatenate(parts, axis=0)
        peak = jnp.max(scores, axis=0, keepdims=True)
        expo = jnp.exp2((scores - peak) * (SCALE * LOG2E))
        probs = expo * (1.0 / jnp.sum(expo, axis=0, keepdims=True))
        probs_low = probs.astype(jnp.bfloat16)
        dprob = dot(values, g_out, NT)
        delta = jnp.sum(probs * dprob, axis=0, keepdims=True)
        dscore = (probs * (dprob - delta)).astype(jnp.bfloat16)
        attended = dot(values, probs_low, TN).T.astype(jnp.bfloat16)
        dq = (dot(keys, dscore, TN) * SCALE).T.astype(jnp.bfloat16)
        for g in range(GROUP):
            cols = slice(g * HEAD_DIM, (g + 1) * HEAD_DIM)
            o_ref[rows, cols] = attended[g * BLK : (g + 1) * BLK]
            dq_ref[rows, cols] = dq[g * BLK : (g + 1) * BLK]
        dk = dot(dscore, q, NN)
        dv = dot(probs_low, g_out, NN)
        for e in range(LIST):
            total[0, listed[e]] += dk[e * BLK : (e + 1) * BLK]
            total[1, listed[e]] += dv[e * BLK : (e + 1) * BLK]

    @pl.when(step == pl.num_programs(0) - 1)
    def _():
        for kv, factor in ((0, SCALE), (1, 1.0)):
            near_out[kv] = total[kv, :blocks_here] * factor
            for out, c in parts_of(far_out, place, origin, shard_count):
                for s in range(CAP):
                    out[kv, s] = (total[kv, blocks_here + c * CAP + s] * factor).astype(jnp.bfloat16)


def gather_sum_kernel(place, asked, near, *refs, heads, shard_count):
    back, outs, total = refs[: -heads - 1], refs[-heads - 1 : -1], refs[-1]
    per_quarter = outs[0].shape[1] // BLK
    total[...] = near[...]
    for part, c in parts_of(back, place, partner, shard_count):
        for s in range(CAP):
            block = asked[c, s]
            for kv in range(2):
                total[kv, block] += part[kv, s].astype(jnp.float32)
    for r in range(heads):
        first = origin(place[1], r, heads) * per_quarter
        for kv in range(2):
            for j in range(per_quarter):
                outs[r][kv, j * BLK : (j + 1) * BLK, :] = total[kv, first + j].astype(jnp.bfloat16)


def whole(shape):
    return pl.BlockSpec(tuple(shape), lambda *_: (0,) * len(shape))


ANYWHERE = pl.BlockSpec(memory_space=pl.ANY)


def bf16(*shape):
    return jax.ShapeDtypeStruct(shape, jnp.bfloat16)


def call(kernel, scalars, arrays, out_shapes, scratch, name, any_in=False, any_out=False, limit=VMEM_LIMIT):
    return pl.pallas_call(
        kernel,
        grid_spec=pltpu.PrefetchScalarGridSpec(
            num_scalar_prefetch=len(scalars),
            grid=(1,),
            in_specs=[ANYWHERE if any_in else whole(x.shape) for x in arrays],
            out_specs=[ANYWHERE if any_out else whole(x.shape) for x in out_shapes],
            scratch_shapes=scratch,
        ),
        out_shape=out_shapes,
        compiler_params=params(limit),
        name=name,
    )(*scalars, *arrays)


def attend(place, source, queries, out_grad, own, far, out_shapes, head, earlier, shard_count):
    tokens_here, width = queries.shape
    blocks_here = tokens_here // BLK
    slots = blocks_here + shard_count * CAP
    tile = pl.BlockSpec((STEP_BLOCKS * BLK, GROUP * HEAD_DIM), lambda i, *_: (i, head))
    near_shape = (2, blocks_here, BLK, HEAD_DIM)
    arrays = [*own, *far]
    first = 4 + len(arrays)
    return pl.pallas_call(
        functools.partial(
            attend_kernel, heads=len(own), fars=len(far), outs=len(out_shapes), head=head, shard_count=shard_count
        ),
        grid_spec=pltpu.PrefetchScalarGridSpec(
            num_scalar_prefetch=2,
            grid=(blocks_here // STEP_BLOCKS,),
            in_specs=[tile, tile] + [whole(x.shape) for x in arrays] + [ANYWHERE] * len(earlier),
            out_specs=[tile, tile, whole(near_shape)] + [whole(x.shape) for x in out_shapes],
            scratch_shapes=[
                pltpu.VMEM((2, slots, BLK, HEAD_DIM), jnp.bfloat16),
                pltpu.VMEM((2, slots, BLK, HEAD_DIM), jnp.float32),
            ],
        ),
        out_shape=[bf16(tokens_here, width), bf16(tokens_here, width), jax.ShapeDtypeStruct(near_shape, jnp.float32)]
        + out_shapes,
        input_output_aliases={first: 0, first + 1: 1} if earlier else {},
        compiler_params=params(),
        cost_estimate=pl.CostEstimate(
            flops=12 * blocks_here * LIST * BLK * GROUP * BLK * HEAD_DIM,
            bytes_accessed=20 * 1024 * 1024,
            transcendentals=blocks_here * LIST * BLK * GROUP * BLK,
        ),
        name="attend",
    )(place, source, queries, out_grad, *arrays, *earlier)


def send(x, axis, count, r):
    return lax.ppermute(x, axis, [(i, partner(i, r, count)) for i in range(count)])


def send_back(x, axis, count, r):
    return lax.ppermute(x, axis, [(i, origin(i, r, count)) for i in range(count)])


def swap(x):
    return lax.all_to_all(x, "ctx", split_axis=0, concat_axis=0, tiled=True)


def requests_of(flat_ids, blocks_here, shard_index, shard_count):
    owner = flat_ids // blocks_here
    shards = jnp.arange(shard_count, dtype=jnp.int32)
    inner = jnp.arange(blocks_here, dtype=jnp.int32)
    every_block = jnp.arange(shard_count * blocks_here, dtype=jnp.int32)
    listed = jnp.any(flat_ids[:, None] == every_block[None, :], axis=0)
    grid = listed.reshape(shard_count, blocks_here) & (shards != shard_index)[:, None]
    rank = jnp.sum((grid[:, :, None] & (inner[:, None] < inner[None, :])[None]).astype(jnp.int32), axis=1)
    hit = grid[:, None] & (rank[:, None] == jnp.arange(128, dtype=jnp.int32)[None, :, None])
    requests = jnp.sum(jnp.where(hit, inner[None, None], 0), axis=2)
    same_owner = owner[:, None] == (every_block // blocks_here)[None, :]
    place_of = jnp.sum((same_owner & listed[None, :] & (every_block[None, :] < flat_ids[:, None])).astype(jnp.int32), axis=1)
    source = jnp.where(owner == shard_index, flat_ids % blocks_here, blocks_here + owner * CAP + place_of)
    return requests, source


def per_device(queries, key_states, value_states, block_lists, out_grad):
    shard_index = lax.axis_index("ctx")
    shard_count = lax.axis_size("ctx")
    heads = lax.axis_size("head")
    blocks_here = queries.shape[0] // BLK
    quarter = key_states.shape[0]
    head_count = key_states.shape[1] // heads // HEAD_DIM
    place = jnp.stack([shard_index, lax.axis_index("head")]).astype(jnp.int32)

    pieces = call(
        split_kernel,
        [place],
        [key_states, value_states],
        [bf16(head_count, 2, quarter, HEAD_DIM)] * heads,
        [pltpu.SemaphoreType.DMA((2 * heads * head_count,))],
        "split",
        any_in=True,
        limit=VMEM_MOST,
    )
    own = [pieces[0]] + [send(pieces[r], "head", heads, r) for r in range(1, heads)]

    requests, source = requests_of(block_lists.reshape(-1), blocks_here, shard_index, shard_count)
    asked = swap(requests)

    one = (2, CAP, BLK, HEAD_DIM)
    by_step = [bf16(*one)] * (shard_count - 1)
    at_once = [bf16(shard_count, *one)]
    picked = call(
        functools.partial(pick_kernel, heads=heads, head_count=head_count, shard_count=shard_count),
        [place, asked],
        own,
        by_step + at_once * (head_count - 1),
        [pltpu.VMEM((2, blocks_here, BLK, HEAD_DIM), jnp.bfloat16)],
        "pick",
    )
    far = [[send(picked[r - 1], "ctx", shard_count, r) for r in range(1, shard_count)]]
    far += [[swap(x)] for x in picked[shard_count - 1 :]]
    earlier, nears, backs = [], [], []
    for h in range(head_count):
        last = h == head_count - 1
        attended, query_grad, near, *far_grad = attend(
            place, source, queries, out_grad, own, far[h], by_step if last else at_once, h, earlier, shard_count
        )
        earlier = [attended, query_grad]
        nears.append(near)
        if last:
            backs.append([send_back(x, "ctx", shard_count, r) for r, x in enumerate(far_grad, 1)])
        else:
            backs.append([swap(far_grad[0])])
    done = []
    for h in range(head_count):
        sums = call(
            functools.partial(gather_sum_kernel, heads=heads, shard_count=shard_count),
            [place, asked],
            [nears[h], *backs[h]],
            [bf16(2, quarter, HEAD_DIM)] * heads,
            [pltpu.VMEM((2, blocks_here, BLK, HEAD_DIM), jnp.float32)],
            "gather_sum",
        )
        done += [sums[0]] + [send_back(sums[r], "head", heads, r) for r in range(1, heads)]
    key_grad, value_grad = call(
        functools.partial(join_kernel, heads=heads),
        [place],
        done,
        [bf16(*key_states.shape)] * 2,
        [pltpu.SemaphoreType.DMA((2 * heads * head_count,))],
        "join",
        any_in=True,
        any_out=True,
    )
    return attended, query_grad, key_grad, value_grad


def solution(mesh):
    return jax.shard_map(
        per_device,
        mesh=mesh,
        in_specs=(
            P("ctx", "head"),
            P(("ctx", "head"), None),
            P(("ctx", "head"), None),
            P("ctx", None),
            P("ctx", "head"),
        ),
        out_specs=(
            P("ctx", "head"),
            P("ctx", "head"),
            P(("ctx", "head"), None),
            P(("ctx", "head"), None),
        ),
        check_vma=False,
    )
```

time: 140 us -> 142 us (1.014)
  starting transfers between devices: 73.2 us -> 45 us
  waiting for transfers between devices: 24.9 us -> 37.8 us
  blocking collectives: 0 us -> 12.3 us
  Pallas kernels: 36.9 us -> 39.9 us
    ppermute x27 -> x10, starting transfers between devices: 48.5 us -> 20.2 us  [send(): lax.ppermute(x, axis, [(i, partner(i, r, count)) for i in range(count)])]
    all_to_all x0 -> x1, blocking collectives: none -> 12.3 us  [swap(): return lax.all_to_all(x, 'ctx', split_axis=0, concat_axis=0, tiled=True)]
    all_to_all x0 -> x2, starting transfers between devices: none -> 9.75 us  [swap(): return lax.all_to_all(x, 'ctx', split_axis=0, concat_axis=0, tiled=True)]
    ppermute x20 -> x13, starting transfers between devices: 24.7 us -> 15.1 us  [send_back(): lax.ppermute(x, axis, [(i, origin(i, r, count)) for i in range(count)])]
    ppermute x27 -> x10, waiting for transfers between devices: 10 us -> 17.8 us  [send(): lax.ppermute(x, axis, [(i, partner(i, r, count)) for i in range(count)])]
    ppermute x20 -> x13, waiting for transfers between devices: 14.9 us -> 20 us  [send_back(): lax.ppermute(x, axis, [(i, origin(i, r, count)) for i in range(count)])]
    pallas_call x5, Pallas kernels: 4.7 us -> 8.29 us  [call(): pl.pallas_call(kernel, grid_spec=pltpu.PrefetchScalarGridSpec(num_scalar_...]
    pallas_call x3 -> x2, Pallas kernels: 32.2 us -> 31.6 us  [attend(): pl.pallas_call(functools.partial(attend_kernel, heads=len(own), fars=len(...]
  transfers between devices with their start and end apart: 47 -> 25, of which waited for: 11 -> 9; matrix products, arithmetic and copies ran while one was open for 1% -> 1% of each run, Pallas kernels for 25% -> 24%
where the time goes in v5:
time: 142 us; the launch traced here: 141 us
  starting transfers between devices  45 us (32%)
  Pallas kernels  39.9 us (28%)
  waiting for transfers between devices  37.8 us (27%)
  blocking collectives  12.3 us (9%)
  local copies, waits for them, and re-layouts  3.53 us (2%)
    pallas_call x2, Pallas kernels, attend(): pl.pallas_call(functools.partial(attend_kernel, heads=len(own), fars=len(...  31.6 us
    ppermute x10, starting transfers between devices, send(): lax.ppermute(x, axis, [(i, partner(i, r, count)) for i in range(count)])  20.2 us
    ppermute x13, waiting for transfers between devices, send_back(): lax.ppermute(x, axis, [(i, origin(i, r, count)) for i in range(count)])  20 us
    ppermute x10, waiting for transfers between devices, send(): lax.ppermute(x, axis, [(i, partner(i, r, count)) for i in range(count)])  17.8 us
    ppermute x13, starting transfers between devices, send_back(): lax.ppermute(x, axis, [(i, origin(i, r, count)) for i in range(count)])  15.1 us
    all_to_all x1, blocking collectives, swap(): return lax.all_to_all(x, 'ctx', split_axis=0, concat_axis=0, tiled=True)  12.3 us
    all_to_all x2, starting transfers between devices, swap(): return lax.all_to_all(x, 'ctx', split_axis=0, concat_axis=0, tiled=True)  9.75 us
    pallas_call x5, Pallas kernels, call(): pl.pallas_call(kernel, grid_spec=pltpu.PrefetchScalarGridSpec(num_scalar_...  8.29 us
  transfers between devices with their start and end apart: 25, of which 9 were waited for; matrix products, arithmetic and copies ran while one was open for 1% of the time, Pallas kernels for 24%

profile of v5, /device:TPU:0, one launch (start us, length us, event | category | flops | bytes accessed | tf_op | source)
XLA Modules:
  0.0 140.5 jit_solution(4185984228055394399)
XLA Ops:
  0.6 0.6 pad_add_fusion.place
  1.2 3.2 %split.1 = (bf16[2,2,256,128]{3,2,1,0:T(8,128)(2,1)}, bf16[2,2,256,128]{3,2,1,0:T(8,128)(2,1)}, bf16[2,2,256,128]{3,2,1,0:T(8,128)(2,1)}, bf16[2,2,256,128]{3,2,1,0:T(8,128)(2,1)}) custom-call(s32[2]{0:T(128)} %pad_add_fusion.place, bf16[256,1024]{1,0:T(8,128)(2,1)} %k_ref.1, bf16[256,1024]{1,0:T(8,128)(2,1)} %v_ref.1), custom_call_target="tpu_custom_call" | custom-call | tf_op jit(solution)/shard_map/split/pallas_call | solution.py:198
  4.4 0.5 collective-permute-start
  4.9 2.6 %collective-permute-start.1 = (bf16[2,2,256,128]{3,2,1,0:T(8,128)(2,1)}, bf16[2,2,256,128]{3,2,1,0:T(8,128)(2,1)S(1)}, u32[]{:S(2)}, u32[]{:S(2)}) collective-permute-start(bf16[2,2,256,128]{3,2,1,0:T(8,128)(2,1)} %get-tuple-element.42), channel_id=1, source_target_pairs={{0,16},{8,24},{16,0},{24,8},{1,17},{9,25},{17,1},{25,9},{2,18},{10... | collective-permute-start | bytes 786440 | tf_op jit(solution)/shard_map/ppermute | solution.py:249
  7.5 0.8 copy.14
  8.4 0.1 fusion
  8.7 0.1 convert_reduce_fusion
  8.8 0.1 select_reduce_fusion
  8.9 12.3 %all_to_all.21 = s32[8,1,128]{2,1,0:T(1,128)S(1)} all-to-all(s32[8,1,128]{2,1,0:T(1,128)S(1)} %bitcast.9), channel_id=1, replica_groups=mesh['head'=4,'ctx'=8] {'ctx'}, dimensions={0} | all-to-all | bytes 8192 | tf_op jit(solution)/shard_map/all_to_all | solution.py:257
  21.3 1.0 copy-done
  22.3 0.6 copy-done.4
  22.9 1.7 %pick.1 = (bf16[2,3,64,128]{3,2,1,0:T(8,128)(2,1)S(1)}, bf16[2,3,64,128]{3,2,1,0:T(8,128)(2,1)S(1)}, bf16[2,3,64,128]{3,2,1,0:T(8,128)(2,1)S(1)}, bf16[2,3,64,12...) custom-call(s32[2]{0:T(128)S(1)} %copy-done.4, ...), custom_call_target="tpu_custom_call" | custom-call | tf_op jit(solution)/shard_map/pick/pallas_call | solution.py:198
  24.7 4.6 %all-to-all-start.1 = ((bf16[8,2,3,64,128]{4,3,2,1,0:T(8,128)(2,1)}), bf16[8,2,3,64,128]{4,3,2,1,0:T(8,128)(2,1)S(1)}, u32[]{:S(2)}, u32[]{:S(2)}) async-start(bf16[8,2,3,64,128]{4,3,2,1,0:T(8,128)(2,1)} %get-tuple-element.44), calls=%async_computation.1 | async-start | bytes 1572864 | tf_op jit(solution)/shard_map/all_to_all | solution.py:257
  29.3 2.1 %collective-permute-start.3 = (bf16[2,3,64,128]{3,2,1,0:T(8,128)(2,1)S(1)}, bf16[2,3,64,128]{3,2,1,0:T(8,128)(2,1)S(1)}, u32[]{:S(2)}, u32[]{:S(2)}) collective-permute-start(bf16[2,3,64,128]{3,2,1,0:T(8,128)(2,1)S(1)} %get-tuple-element.45), channel_id=1, source_target_pairs={{0,1},{1,0},{2,3},{3,2},{4,5},{5,4},{6,7},{7,6},{8,9},{9,8},{10,11... | collective-permute-start | bytes 294920 | tf_op jit(solution)/shard_map/ppermute | solution.py:249
  31.3 1.5 %collective-permute-start.4 = (bf16[2,3,64,128]{3,2,1,0:T(8,128)(2,1)S(1)}, bf16[2,3,64,128]{3,2,1,0:T(8,128)(2,1)S(1)}, u32[]{:S(2)}, u32[]{:S(2)}) collective-permute-start(bf16[2,3,64,128]{3,2,1,0:T(8,128)(2,1)S(1)} %get-tuple-element.46), channel_id=1, source_target_pairs={{0,2},{1,3},{2,0},{3,1},{4,6},{5,7},{6,4},{7,5},{8,10},{9,11},{10,... | collective-permute-start | bytes 294920 | tf_op jit(solution)/shard_map/ppermute | solution.py:249
  32.8 0.2 convert_reduce_fusion.1
  33.0 0.1 collective-permute-start.5
  33.1 2.8 %collective-permute-start.6 = (bf16[2,3,64,128]{3,2,1,0:T(8,128)(2,1)S(1)}, bf16[2,3,64,128]{3,2,1,0:T(8,128)(2,1)S(1)}, u32[]{:S(2)}, u32[]{:S(2)}) collective-permute-start(bf16[2,3,64,128]{3,2,1,0:T(8,128)(2,1)S(1)} %get-tuple-element.48), channel_id=1, source_target_pairs={{0,4},{1,5},{2,6},{3,7},{4,0},{5,1},{6,2},{7,3},{8,12},{9,13},{10,... | collective-permute-start | bytes 294920 | tf_op jit(solution)/shard_map/ppermute | solution.py:249
  36.0 1.5 %collective-permute-start.7 = (bf16[2,3,64,128]{3,2,1,0:T(8,128)(2,1)S(1)}, bf16[2,3,64,128]{3,2,1,0:T(8,128)(2,1)S(1)}, u32[]{:S(2)}, u32[]{:S(2)}) collective-permute-start(bf16[2,3,64,128]{3,2,1,0:T(8,128)(2,1)S(1)} %get-tuple-element.49), channel_id=1, source_target_pairs={{0,5},{1,4},{2,7},{3,6},{4,1},{5,0},{6,3},{7,2},{8,13},{9,12},{10,... | collective-permute-start | bytes 294920 | tf_op jit(solution)/shard_map/ppermute | solution.py:249
  37.4 2.4 %collective-permute-done.3.refs_4_ = bf16[2,3,64,128]{3,2,1,0:T(8,128)(2,1)S(1)} collective-permute-done((bf16[2,3,64,128]{3,2,1,0:T(8,128)(2,1)S(1)}, bf16[2,3,64,128]{3,2,1,0:T(8,128)(2,1)S(1)}, u32[]{:S(2)}, u32[]{:S(2)}) %collective-permute-start.3) | collective-permute-done | bytes 98336 | tf_op jit(solution)/shard_map/ppermute | solution.py:249
  39.8 4.6 %collective-permute-start.8 = (bf16[2,3,64,128]{3,2,1,0:T(8,128)(2,1)S(1)}, bf16[2,3,64,128]{3,2,1,0:T(8,128)(2,1)S(1)}, u32[]{:S(2)}, u32[]{:S(2)}) collective-permute-start(bf16[2,3,64,128]{3,2,1,0:T(8,128)(2,1)S(1)} %get-tuple-element.50), channel_id=1, source_target_pairs={{0,6},{1,7},{2,4},{3,5},{4,2},{5,3},{6,0},{7,1},{8,14},{9,15},{10,... | collective-permute-start | bytes 294920 | tf_op jit(solution)/shard_map/ppermute | solution.py:249
  44.4 1.2 collective-permute-done.4.refs_5_
  45.6 4.4 %collective-permute-start.9 = (bf16[2,3,64,128]{3,2,1,0:T(8,128)(2,1)S(1)}, bf16[2,3,64,128]{3,2,1,0:T(8,128)(2,1)S(1)}, u32[]{:S(2)}, u32[]{:S(2)}) collective-permute-start(bf16[2,3,64,128]{3,2,1,0:T(8,128)(2,1)S(1)} %get-tuple-element.51), channel_id=1, source_target_pairs={{0,7},{1,6},{2,5},{3,4},{4,3},{5,2},{6,1},{7,0},{8,15},{9,14},{10,... | collective-permute-start | bytes 294920 | tf_op jit(solution)/shard_map/ppermute | solution.py:249
  50.0 11.3 %collective-permute-done.6.refs_7_ = bf16[2,3,64,128]{3,2,1,0:T(8,128)(2,1)S(1)} collective-permute-done((bf16[2,3,64,128]{3,2,1,0:T(8,128)(2,1)S(1)}, bf16[2,3,64,128]{3,2,1,0:T(8,128)(2,1)S(1)}, u32[]{:S(2)}, u32[]{:S(2)}) %collective-permute-start.6) | collective-permute-done | bytes 98336 | tf_op jit(solution)/shard_map/ppermute | solution.py:249
  61.3 3.0 %collective-permute-done.7.refs_8_ = bf16[2,3,64,128]{3,2,1,0:T(8,128)(2,1)S(1)} collective-permute-done((bf16[2,3,64,128]{3,2,1,0:T(8,128)(2,1)S(1)}, bf16[2,3,64,128]{3,2,1,0:T(8,128)(2,1)S(1)}, u32[]{:S(2)}, u32[]{:S(2)}) %collective-permute-start.7) | collective-permute-done | bytes 98336 | tf_op jit(solution)/shard_map/ppermute | solution.py:249
  64.3 15.9 %attend.2 = (bf16[1024,1024]{1,0:T(8,128)(2,1)}, bf16[1024,1024]{1,0:T(8,128)(2,1)}, f32[2,16,64,128]{3,2,1,0:T(8,128)S(1)}, bf16[8,2,3,64,128]{4,3,2,1,0:T(8,128)(2,1)}) custom-call(s32[2]{0:T(128)S(1)} %copy-done.5, s32[128]{0:T(128)S(1)} %compare_select_fusion.source, bf16[1024,1024]{1,0:T(8,128)(2,1)} %q_ref.3, bf16[1024,1024]{1,0:T(8,128)(2,1)} %g_ref.3, ...), custom_call_target="tpu_custom_call" | custom-call | flops 3221225472 | bytes 20971520 | tf_op jit(solution)/shard_map/attend/pallas_call | solution.py:221
  80.3 5.2 %all-to-all-start.2 = ((bf16[8,2,3,64,128]{4,3,2,1,0:T(8,128)(2,1)}), bf16[8,2,3,64,128]{4,3,2,1,0:T(8,128)(2,1)S(1)}, u32[]{:S(2)}, u32[]{:S(2)}) async-start(bf16[8,2,3,64,128]{4,3,2,1,0:T(8,128)(2,1)} %get-tuple-element.57), calls=%async_computation.2 | async-start | bytes 1572864 | tf_op jit(solution)/shard_map/all_to_all | solution.py:257
  85.4 0.9 copy-done.3
  86.4 15.6 %attend.3 = (bf16[1024,1024]{1,0:T(8,128)(2,1)}, bf16[1024,1024]{1,0:T(8,128)(2,1)}, f32[2,16,64,128]{3,2,1,0:T(8,128)S(1)}, bf16[2,3,64,128]{3,2,1,0:T(8,128)(2...) custom-call(s32[2]{0:T(128)S(1)} %copy-done.5, ...), custom_call_target="tpu_custom_call", output_to_operand_aliasing={{0}: (9, {}), {1}: (10, {})} | custom-call | flops 3221225472 | bytes 20971520 | tf_op jit(solution)/shard_map/attend/pallas_call | solution.py:221
  102.0 2.0 %collective-permute-start.13 = (bf16[2,3,64,128]{3,2,1,0:T(8,128)(2,1)S(1)}, bf16[2,3,64,128]{3,2,1,0:T(8,128)(2,1)S(1)}, u32[]{:S(2)}, u32[]{:S(2)}) collective-permute-start(bf16[2,3,64,128]{3,2,1,0:T(8,128)(2,1)S(1)} %get-tuple-element.63), channel_id=1, source_target_pairs={{0,1},{1,0},{2,3},{3,2},{4,5},{5,4},{6,7},{7,6},{8,9},{9,8},{10,11... | collective-permute-start | bytes 294920 | tf_op jit(solution)/shard_map/ppermute | solution.py:253
  104.0 1.5 %collective-permute-start.14 = (bf16[2,3,64,128]{3,2,1,0:T(8,128)(2,1)S(1)}, bf16[2,3,64,128]{3,2,1,0:T(8,128)(2,1)S(1)}, u32[]{:S(2)}, u32[]{:S(2)}) collective-permute-start(bf16[2,3,64,128]{3,2,1,0:T(8,128)(2,1)S(1)} %get-tuple-element.64), channel_id=1, source_target_pairs={{0,2},{1,3},{2,0},{3,1},{4,6},{5,7},{6,4},{7,5},{8,10},{9,11},{10,... | collective-permute-start | bytes 294920 | tf_op jit(solution)/shard_map/ppermute | solution.py:253
  105.5 0.1 collective-permute-start.15
  105.6 2.8 %collective-permute-start.16 = (bf16[2,3,64,128]{3,2,1,0:T(8,128)(2,1)S(1)}, bf16[2,3,64,128]{3,2,1,0:T(8,128)(2,1)S(1)}, u32[]{:S(2)}, u32[]{:S(2)}) collective-permute-start(bf16[2,3,64,128]{3,2,1,0:T(8,128)(2,1)S(1)} %get-tuple-element.66), channel_id=1, source_target_pairs={{0,4},{1,5},{2,6},{3,7},{4,0},{5,1},{6,2},{7,3},{8,12},{9,13},{10,... | collective-permute-start | bytes 294920 | tf_op jit(solution)/shard_map/ppermute | solution.py:253
  108.4 1.5 %collective-permute-start.17 = (bf16[2,3,64,128]{3,2,1,0:T(8,128)(2,1)S(1)}, bf16[2,3,64,128]{3,2,1,0:T(8,128)(2,1)S(1)}, u32[]{:S(2)}, u32[]{:S(2)}) collective-permute-start(bf16[2,3,64,128]{3,2,1,0:T(8,128)(2,1)S(1)} %get-tuple-element.67), channel_id=1, source_target_pairs={{0,5},{1,4},{2,7},{3,6},{4,1},{5,0},{6,3},{7,2},{8,13},{9,12},{10,... | collective-permute-start | bytes 294920 | tf_op jit(solution)/shard_map/ppermute | solution.py:253
  109.9 3.3 %collective-permute-start.18 = (bf16[2,3,64,128]{3,2,1,0:T(8,128)(2,1)S(1)}, bf16[2,3,64,128]{3,2,1,0:T(8,128)(2,1)S(1)}, u32[]{:S(2)}, u32[]{:S(2)}) collective-permute-start(bf16[2,3,64,128]{3,2,1,0:T(8,128)(2,1)S(1)} %get-tuple-element.68), channel_id=1, source_target_pairs={{0,6},{1,7},{2,4},{3,5},{4,2},{5,3},{6,0},{7,1},{8,14},{9,15},{10,... | collective-permute-start | bytes 294920 | tf_op jit(solution)/shard_map/ppermute | solution.py:253
  113.1 0.1 collective-permute-start.19
  113.3 10.8 %collective-permute-done.17.refs_4_ = bf16[2,3,64,128]{3,2,1,0:T(8,128)(2,1)S(1)} collective-permute-done((bf16[2,3,64,128]{3,2,1,0:T(8,128)(2,1)S(1)}, bf16[2,3,64,128]{3,2,1,0:T(8,128)(2,1)S(1)}, u32[]{:S(2)}, u32[]{:S(2)}) %collective-permute-start.17) | collective-permute-done | bytes 98336 | tf_op jit(solution)/shard_map/ppermute | solution.py:253
  124.0 0.9 gather_sum.3
  125.0 1.6 %collective-permute-start.21 = (bf16[2,256,128]{2,1,0:T(8,128)(2,1)S(1)}, bf16[2,256,128]{2,1,0:T(8,128)(2,1)S(1)}, u32[]{:S(2)}, u32[]{:S(2)}) collective-permute-start(bf16[2,256,128]{2,1,0:T(8,128)(2,1)S(1)} %get-tuple-element.72), channel_id=1, source_target_pairs={{0,16},{8,24},{16,0},{24,8},{1,17},{9,25},{17,1},{25,9},{2,18},{10... | collective-permute-start | bytes 393224 | tf_op jit(solution)/shard_map/ppermute | solution.py:253
  126.6 0.3 collective-permute-start.22
  126.9 0.9 gather_sum.2
  127.8 0.4 collective-permute-start.10
  128.2 1.5 %collective-permute-start.11 = (bf16[2,256,128]{2,1,0:T(8,128)(2,1)S(1)}, bf16[2,256,128]{2,1,0:T(8,128)(2,1)S(1)}, u32[]{:S(2)}, u32[]{:S(2)}) collective-permute-start(bf16[2,256,128]{2,1,0:T(8,128)(2,1)S(1)} %get-tuple-element.60), channel_id=1, source_target_pairs={{0,16},{8,24},{16,0},{24,8},{1,17},{9,25},{17,1},{25,9},{2,18},{10... | collective-permute-start | bytes 393224 | tf_op jit(solution)/shard_map/ppermute | solution.py:253
  129.7 1.7 %collective-permute-done.21.refs_6_ = bf16[2,256,128]{2,1,0:T(8,128)(2,1)S(1)} collective-permute-done((bf16[2,256,128]{2,1,0:T(8,128)(2,1)S(1)}, bf16[2,256,128]{2,1,0:T(8,128)(2,1)S(1)}, u32[]{:S(2)}, u32[]{:S(2)}) %collective-permute-start.21) | collective-permute-done | bytes 131104 | tf_op jit(solution)/shard_map/ppermute | solution.py:253
  131.4 1.9 %collective-permute-done.22.refs_7_ = bf16[2,256,128]{2,1,0:T(8,128)(2,1)S(1)} collective-permute-done((bf16[2,256,128]{2,1,0:T(8,128)(2,1)S(1)}, bf16[2,256,128]{2,1,0:T(8,128)(2,1)S(1)}, u32[]{:S(2)}, u32[]{:S(2)}) %collective-permute-start.22) | collective-permute-done | bytes 131104 | tf_op jit(solution)/shard_map/ppermute | solution.py:253
  133.3 3.7 %collective-permute-done.11.refs_2_ = bf16[2,256,128]{2,1,0:T(8,128)(2,1)S(1)} collective-permute-done((bf16[2,256,128]{2,1,0:T(8,128)(2,1)S(1)}, bf16[2,256,128]{2,1,0:T(8,128)(2,1)S(1)}, u32[]{:S(2)}, u32[]{:S(2)}) %collective-permute-start.11) | collective-permute-done | bytes 131104 | tf_op jit(solution)/shard_map/ppermute | solution.py:253
  137.0 1.9 %collective-permute-done.12.refs_3_ = bf16[2,256,128]{2,1,0:T(8,128)(2,1)S(1)} collective-permute-done((bf16[2,256,128]{2,1,0:T(8,128)(2,1)S(1)}, bf16[2,256,128]{2,1,0:T(8,128)(2,1)S(1)}, u32[]{:S(2)}, u32[]{:S(2)}) %collective-permute-start.12) | collective-permute-done | bytes 131104 | tf_op jit(solution)/shard_map/ppermute | solution.py:253
  138.9 1.6 %join.1 = (bf16[256,1024]{1,0:T(8,128)(2,1)}, bf16[256,1024]{1,0:T(8,128)(2,1)}) custom-call(s32[2]{0:T(128)S(1)} %copy-done.5, bf16[2,256,128]{2,1,0:T(8,128)(2,1)S(1)} %get-tuple-element.58.refs_0_, bf16[2,256,128]{2,1,0:T(8,128)(2,1)S(1)} %collective-permute-done.10.refs_1_, bf16[2,256,128]{2,1,0:T(8,128)(2,1)S(1)} %collective-permute-done.11.refs_2_, ...), custom_call_target="tpu_custom_call" | custom-call | tf_op jit(solution)/shard_map/join/pallas_call | solution.py:198
  (36 shorter events, 0.5 us)
Async XLA Ops:
  1.2 63.1 %copy-start.5 = (s32[2]{0:T(128)S(1)}, s32[2]{0:T(128)}, u32[]{:S(2)}) copy-start(s32[2]{0:T(128)} %pad_add_fusion.place) | copy-start | bytes 28
  4.4 16.9 %collective-permute-start = (bf16[2,2,256,128]{3,2,1,0:T(8,128)(2,1)}, bf16[2,2,256,128]{3,2,1,0:T(8,128)(2,1)S(1)}, u32[]{:S(2)}, u32[]{:S(2)}) collective-permute-start(bf16[2,2,256,128]{3,2,1,0:T(8,128)(2,1)} %get-tuple-element.41), channel_id=1, source_target_pairs={{0,8},{8,0},{16,24},{24,16},{1,9},{9,1},{17,25},{25,17},{2,10},{10... | collective-permute-start | bytes 786440 | tf_op jit(solution)/shard_map/ppermute | solution.py:249
  4.9 16.3 %collective-permute-start.1 = (bf16[2,2,256,128]{3,2,1,0:T(8,128)(2,1)}, bf16[2,2,256,128]{3,2,1,0:T(8,128)(2,1)S(1)}, u32[]{:S(2)}, u32[]{:S(2)}) collective-permute-start(bf16[2,2,256,128]{3,2,1,0:T(8,128)(2,1)} %get-tuple-element.42), channel_id=1, source_target_pairs={{0,16},{8,24},{16,0},{24,8},{1,17},{9,25},{17,1},{25,9},{2,18},{10... | collective-permute-start | bytes 786440 | tf_op jit(solution)/shard_map/ppermute | solution.py:249
  7.5 13.8 %collective-permute-start.2 = (bf16[2,2,256,128]{3,2,1,0:T(8,128)(2,1)}, bf16[2,2,256,128]{3,2,1,0:T(8,128)(2,1)S(1)}, u32[]{:S(2)}, u32[]{:S(2)}) collective-permute-start(bf16[2,2,256,128]{3,2,1,0:T(8,128)(2,1)} %get-tuple-element.43), channel_id=1, source_target_pairs={{0,24},{8,16},{16,8},{24,0},{1,25},{9,17},{17,9},{25,1},{2,26},{10... | collective-permute-start | bytes 786440 | tf_op jit(solution)/shard_map/ppermute | solution.py:249
  21.2 59.0 %copy-start.2 = (bf16[2,2,256,128]{3,2,1,0:T(8,128)(2,1)}, bf16[2,2,256,128]{3,2,1,0:T(8,128)(2,1)S(1)}, u32[]{:S(2)}) copy-start(bf16[2,2,256,128]{3,2,1,0:T(8,128)(2,1)S(1)} %collective-permute-done.2.refs_3_) | copy-start | bytes 786436
  21.3 1.0 copy-start
  22.3 0.6 copy-start.4
  22.9 41.4 %copy-start.1 = (bf16[2,2,256,128]{3,2,1,0:T(8,128)(2,1)S(1)}, bf16[2,2,256,128]{3,2,1,0:T(8,128)(2,1)}, u32[]{:S(2)}) copy-start(bf16[2,2,256,128]{3,2,1,0:T(8,128)(2,1)} %get-tuple-element.40.refs_0_) | copy-start | bytes 786436
  24.7 55.6 %all-to-all-start.1 = ((bf16[8,2,3,64,128]{4,3,2,1,0:T(8,128)(2,1)}), bf16[8,2,3,64,128]{4,3,2,1,0:T(8,128)(2,1)S(1)}, u32[]{:S(2)}, u32[]{:S(2)}) async-start(bf16[8,2,3,64,128]{4,3,2,1,0:T(8,128)(2,1)} %get-tuple-element.44), calls=%async_computation.1 | async-start | bytes 1572864 | tf_op jit(solution)/shard_map/all_to_all | solution.py:257
  29.3 10.5 %collective-permute-start.3 = (bf16[2,3,64,128]{3,2,1,0:T(8,128)(2,1)S(1)}, bf16[2,3,64,128]{3,2,1,0:T(8,128)(2,1)S(1)}, u32[]{:S(2)}, u32[]{:S(2)}) collective-permute-start(bf16[2,3,64,128]{3,2,1,0:T(8,128)(2,1)S(1)} %get-tuple-element.45), channel_id=1, source_target_pairs={{0,1},{1,0},{2,3},{3,2},{4,5},{5,4},{6,7},{7,6},{8,9},{9,8},{10,11... | collective-permute-start | bytes 294920 | tf_op jit(solution)/shard_map/ppermute | solution.py:249
  31.3 14.2 %collective-permute-start.4 = (bf16[2,3,64,128]{3,2,1,0:T(8,128)(2,1)S(1)}, bf16[2,3,64,128]{3,2,1,0:T(8,128)(2,1)S(1)}, u32[]{:S(2)}, u32[]{:S(2)}) collective-permute-start(bf16[2,3,64,128]{3,2,1,0:T(8,128)(2,1)S(1)} %get-tuple-element.46), channel_id=1, source_target_pairs={{0,2},{1,3},{2,0},{3,1},{4,6},{5,7},{6,4},{7,5},{8,10},{9,11},{10,... | collective-permute-start | bytes 294920 | tf_op jit(solution)/shard_map/ppermute | solution.py:249
  33.0 17.1 %collective-permute-start.5 = (bf16[2,3,64,128]{3,2,1,0:T(8,128)(2,1)S(1)}, bf16[2,3,64,128]{3,2,1,0:T(8,128)(2,1)S(1)}, u32[]{:S(2)}, u32[]{:S(2)}) collective-permute-start(bf16[2,3,64,128]{3,2,1,0:T(8,128)(2,1)S(1)} %get-tuple-element.47), channel_id=1, source_target_pairs={{0,3},{1,2},{2,1},{3,0},{4,7},{5,6},{6,5},{7,4},{8,11},{9,10},{10,... | collective-permute-start | bytes 294920 | tf_op jit(solution)/shard_map/ppermute | solution.py:249
  33.1 28.2 %collective-permute-start.6 = (bf16[2,3,64,128]{3,2,1,0:T(8,128)(2,1)S(1)}, bf16[2,3,64,128]{3,2,1,0:T(8,128)(2,1)S(1)}, u32[]{:S(2)}, u32[]{:S(2)}) collective-permute-start(bf16[2,3,64,128]{3,2,1,0:T(8,128)(2,1)S(1)} %get-tuple-element.48), channel_id=1, source_target_pairs={{0,4},{1,5},{2,6},{3,7},{4,0},{5,1},{6,2},{7,3},{8,12},{9,13},{10,... | collective-permute-start | bytes 294920 | tf_op jit(solution)/shard_map/ppermute | solution.py:249
  36.0 28.3 %collective-permute-start.7 = (bf16[2,3,64,128]{3,2,1,0:T(8,128)(2,1)S(1)}, bf16[2,3,64,128]{3,2,1,0:T(8,128)(2,1)S(1)}, u32[]{:S(2)}, u32[]{:S(2)}) collective-permute-start(bf16[2,3,64,128]{3,2,1,0:T(8,128)(2,1)S(1)} %get-tuple-element.49), channel_id=1, source_target_pairs={{0,5},{1,4},{2,7},{3,6},{4,1},{5,0},{6,3},{7,2},{8,13},{9,12},{10,... | collective-permute-start | bytes 294920 | tf_op jit(solution)/shard_map/ppermute | solution.py:249
  39.8 24.5 %collective-permute-start.8 = (bf16[2,3,64,128]{3,2,1,0:T(8,128)(2,1)S(1)}, bf16[2,3,64,128]{3,2,1,0:T(8,128)(2,1)S(1)}, u32[]{:S(2)}, u32[]{:S(2)}) collective-permute-start(bf16[2,3,64,128]{3,2,1,0:T(8,128)(2,1)S(1)} %get-tuple-element.50), channel_id=1, source_target_pairs={{0,6},{1,7},{2,4},{3,5},{4,2},{5,3},{6,0},{7,1},{8,14},{9,15},{10,... | collective-permute-start | bytes 294920 | tf_op jit(solution)/shard_map/ppermute | solution.py:249
  45.6 18.7 %collective-permute-start.9 = (bf16[2,3,64,128]{3,2,1,0:T(8,128)(2,1)S(1)}, bf16[2,3,64,128]{3,2,1,0:T(8,128)(2,1)S(1)}, u32[]{:S(2)}, u32[]{:S(2)}) collective-permute-start(bf16[2,3,64,128]{3,2,1,0:T(8,128)(2,1)S(1)} %get-tuple-element.51), channel_id=1, source_target_pairs={{0,7},{1,6},{2,5},{3,4},{4,3},{5,2},{6,1},{7,0},{8,15},{9,14},{10,... | collective-permute-start | bytes 294920 | tf_op jit(solution)/shard_map/ppermute | solution.py:249
  80.3 46.6 %all-to-all-start.2 = ((bf16[8,2,3,64,128]{4,3,2,1,0:T(8,128)(2,1)}), bf16[8,2,3,64,128]{4,3,2,1,0:T(8,128)(2,1)S(1)}, u32[]{:S(2)}, u32[]{:S(2)}) async-start(bf16[8,2,3,64,128]{4,3,2,1,0:T(8,128)(2,1)} %get-tuple-element.57), calls=%async_computation.2 | async-start | bytes 1572864 | tf_op jit(solution)/shard_map/all_to_all | solution.py:257
  85.4 0.9 copy-start.3
  102.0 7.9 %collective-permute-start.13 = (bf16[2,3,64,128]{3,2,1,0:T(8,128)(2,1)S(1)}, bf16[2,3,64,128]{3,2,1,0:T(8,128)(2,1)S(1)}, u32[]{:S(2)}, u32[]{:S(2)}) collective-permute-start(bf16[2,3,64,128]{3,2,1,0:T(8,128)(2,1)S(1)} %get-tuple-element.63), channel_id=1, source_target_pairs={{0,1},{1,0},{2,3},{3,2},{4,5},{5,4},{6,7},{7,6},{8,9},{9,8},{10,11... | collective-permute-start | bytes 294920 | tf_op jit(solution)/shard_map/ppermute | solution.py:253
  104.0 9.1 %collective-permute-start.14 = (bf16[2,3,64,128]{3,2,1,0:T(8,128)(2,1)S(1)}, bf16[2,3,64,128]{3,2,1,0:T(8,128)(2,1)S(1)}, u32[]{:S(2)}, u32[]{:S(2)}) collective-permute-start(bf16[2,3,64,128]{3,2,1,0:T(8,128)(2,1)S(1)} %get-tuple-element.64), channel_id=1, source_target_pairs={{0,2},{1,3},{2,0},{3,1},{4,6},{5,7},{6,4},{7,5},{8,10},{9,11},{10,... | collective-permute-start | bytes 294920 | tf_op jit(solution)/shard_map/ppermute | solution.py:253
  105.5 7.8 %collective-permute-start.15 = (bf16[2,3,64,128]{3,2,1,0:T(8,128)(2,1)S(1)}, bf16[2,3,64,128]{3,2,1,0:T(8,128)(2,1)S(1)}, u32[]{:S(2)}, u32[]{:S(2)}) collective-permute-start(bf16[2,3,64,128]{3,2,1,0:T(8,128)(2,1)S(1)} %get-tuple-element.65), channel_id=1, source_target_pairs={{0,3},{1,2},{2,1},{3,0},{4,7},{5,6},{6,5},{7,4},{8,11},{9,10},{10,... | collective-permute-start | bytes 294920 | tf_op jit(solution)/shard_map/ppermute | solution.py:253
  105.6 7.7 %collective-permute-start.16 = (bf16[2,3,64,128]{3,2,1,0:T(8,128)(2,1)S(1)}, bf16[2,3,64,128]{3,2,1,0:T(8,128)(2,1)S(1)}, u32[]{:S(2)}, u32[]{:S(2)}) collective-permute-start(bf16[2,3,64,128]{3,2,1,0:T(8,128)(2,1)S(1)} %get-tuple-element.66), channel_id=1, source_target_pairs={{0,4},{1,5},{2,6},{3,7},{4,0},{5,1},{6,2},{7,3},{8,12},{9,13},{10,... | collective-permute-start | bytes 294920 | tf_op jit(solution)/shard_map/ppermute | solution.py:253
  108.4 15.6 %collective-permute-start.17 = (bf16[2,3,64,128]{3,2,1,0:T(8,128)(2,1)S(1)}, bf16[2,3,64,128]{3,2,1,0:T(8,128)(2,1)S(1)}, u32[]{:S(2)}, u32[]{:S(2)}) collective-permute-start(bf16[2,3,64,128]{3,2,1,0:T(8,128)(2,1)S(1)} %get-tuple-element.67), channel_id=1, source_target_pairs={{0,5},{1,4},{2,7},{3,6},{4,1},{5,0},{6,3},{7,2},{8,13},{9,12},{10,... | collective-permute-start | bytes 294920 | tf_op jit(solution)/shard_map/ppermute | solution.py:253
  109.9 14.2 %collective-permute-start.18 = (bf16[2,3,64,128]{3,2,1,0:T(8,128)(2,1)S(1)}, bf16[2,3,64,128]{3,2,1,0:T(8,128)(2,1)S(1)}, u32[]{:S(2)}, u32[]{:S(2)}) collective-permute-start(bf16[2,3,64,128]{3,2,1,0:T(8,128)(2,1)S(1)} %get-tuple-element.68), channel_id=1, source_target_pairs={{0,6},{1,7},{2,4},{3,5},{4,2},{5,3},{6,0},{7,1},{8,14},{9,15},{10,... | collective-permute-start | bytes 294920 | tf_op jit(solution)/shard_map/ppermute | solution.py:253
  113.1 10.9 %collective-permute-start.19 = (bf16[2,3,64,128]{3,2,1,0:T(8,128)(2,1)S(1)}, bf16[2,3,64,128]{3,2,1,0:T(8,128)(2,1)S(1)}, u32[]{:S(2)}, u32[]{:S(2)}) collective-permute-start(bf16[2,3,64,128]{3,2,1,0:T(8,128)(2,1)S(1)} %get-tuple-element.69), channel_id=1, source_target_pairs={{0,7},{1,6},{2,5},{3,4},{4,3},{5,2},{6,1},{7,0},{8,15},{9,14},{10,... | collective-permute-start | bytes 294920 | tf_op jit(solution)/shard_map/ppermute | solution.py:253
  124.9 4.7 %collective-permute-start.20 = (bf16[2,256,128]{2,1,0:T(8,128)(2,1)S(1)}, bf16[2,256,128]{2,1,0:T(8,128)(2,1)S(1)}, u32[]{:S(2)}, u32[]{:S(2)}) collective-permute-start(bf16[2,256,128]{2,1,0:T(8,128)(2,1)S(1)} %get-tuple-element.71), channel_id=1, source_target_pairs={{0,8},{8,0},{16,24},{24,16},{1,9},{9,1},{17,25},{25,17},{2,10},{10... | collective-permute-start | bytes 393224 | tf_op jit(solution)/shard_map/ppermute | solution.py:253
  125.0 6.4 %collective-permute-start.21 = (bf16[2,256,128]{2,1,0:T(8,128)(2,1)S(1)}, bf16[2,256,128]{2,1,0:T(8,128)(2,1)S(1)}, u32[]{:S(2)}, u32[]{:S(2)}) collective-permute-start(bf16[2,256,128]{2,1,0:T(8,128)(2,1)S(1)} %get-tuple-element.72), channel_id=1, source_target_pairs={{0,16},{8,24},{16,0},{24,8},{1,17},{9,25},{17,1},{25,9},{2,18},{10... | collective-permute-start | bytes 393224 | tf_op jit(solution)/shard_map/ppermute | solution.py:253
  126.6 6.7 %collective-permute-start.22 = (bf16[2,256,128]{2,1,0:T(8,128)(2,1)S(1)}, bf16[2,256,128]{2,1,0:T(8,128)(2,1)S(1)}, u32[]{:S(2)}, u32[]{:S(2)}) collective-permute-start(bf16[2,256,128]{2,1,0:T(8,128)(2,1)S(1)} %get-tuple-element.73), channel_id=1, source_target_pairs={{0,24},{8,16},{16,8},{24,0},{1,25},{9,17},{17,9},{25,1},{2,26},{10... | collective-permute-start | bytes 393224 | tf_op jit(solution)/shard_map/ppermute | solution.py:253
  127.8 5.5 %collective-permute-start.10 = (bf16[2,256,128]{2,1,0:T(8,128)(2,1)S(1)}, bf16[2,256,128]{2,1,0:T(8,128)(2,1)S(1)}, u32[]{:S(2)}, u32[]{:S(2)}) collective-permute-start(bf16[2,256,128]{2,1,0:T(8,128)(2,1)S(1)} %get-tuple-element.59), channel_id=1, source_target_pairs={{0,8},{8,0},{16,24},{24,16},{1,9},{9,1},{17,25},{25,17},{2,10},{10... | collective-permute-start | bytes 393224 | tf_op jit(solution)/shard_map/ppermute | solution.py:253
  128.2 8.8 %collective-permute-start.11 = (bf16[2,256,128]{2,1,0:T(8,128)(2,1)S(1)}, bf16[2,256,128]{2,1,0:T(8,128)(2,1)S(1)}, u32[]{:S(2)}, u32[]{:S(2)}) collective-permute-start(bf16[2,256,128]{2,1,0:T(8,128)(2,1)S(1)} %get-tuple-element.60), channel_id=1, source_target_pairs={{0,16},{8,24},{16,0},{24,8},{1,17},{9,25},{17,1},{25,9},{2,18},{10... | collective-permute-start | bytes 393224 | tf_op jit(solution)/shard_map/ppermute | solution.py:253
  129.7 9.2 %collective-permute-start.12 = (bf16[2,256,128]{2,1,0:T(8,128)(2,1)S(1)}, bf16[2,256,128]{2,1,0:T(8,128)(2,1)S(1)}, u32[]{:S(2)}, u32[]{:S(2)}) collective-permute-start(bf16[2,256,128]{2,1,0:T(8,128)(2,1)S(1)} %get-tuple-element.61), channel_id=1, source_target_pairs={{0,24},{8,16},{16,8},{24,0},{1,25},{9,17},{17,9},{25,1},{2,26},{10... | collective-permute-start | bytes 393224 | tf_op jit(solution)/shard_map/ppermute | solution.py:253

commit v6 on v5

--- a/solution.py
+++ b/solution.py
@@ -40,25 +40,20 @@
     return me ^ r if count & (count - 1) == 0 else (me + count - r) % count
 
 
+def step_to(me, there, count):
+    return me ^ there if count & (count - 1) == 0 else (there + count - me) % count
+
+
 def head_columns(place, r, heads, h, head_count):
     col = (partner(place[1], r, heads) * head_count + h) * HEAD_DIM
     return pl.ds(pl.multiple_of(col, HEAD_DIM), HEAD_DIM)
 
 
-def split_kernel(place, k_ref, v_ref, *refs):
-    *outs, sem = refs
-    heads, head_count = len(outs), outs[0].shape[0]
-    copies = []
-    for r, out in enumerate(outs):
-        for h in range(head_count):
-            cols = head_columns(place, r, heads, h, head_count)
-            for kv, ref in enumerate((k_ref, v_ref)):
-                at = (r * head_count + h) * 2 + kv
-                copies.append(pltpu.make_async_copy(ref.at[:, cols], out.at[h, kv], sem.at[at]))
-    for copy in copies:
-        copy.start()
-    for copy in copies:
-        copy.wait()
+def split_kernel(place, k_ref, v_ref, *outs, heads):
+    for at, out in enumerate(outs):
+        cols = head_columns(place, at % heads, heads, at // heads, len(outs) // heads)
+        out[0] = k_ref[:, cols]
+        out[1] = v_ref[:, cols]
 
 
 def join_kernel(place, *refs, heads):
@@ -75,36 +70,33 @@
         copy.wait()
 
 
-def fill_table(place, own, h, table):
+def fill_table(place, own, table):
     heads = len(own)
-    per_quarter = own[0].shape[2] // BLK
+    per_quarter = own[0].shape[1] // BLK
     for r in range(heads):
         first = origin(place[1], r, heads) * per_quarter
         for kv in range(2):
             for j in range(per_quarter):
-                table[kv, first + j] = own[r][h, kv, j * BLK : (j + 1) * BLK, :]
+                table[kv, first + j] = own[r][kv, j * BLK : (j + 1) * BLK, :]
 
 
 def parts_of(refs, place, at, shard_count):
     if len(refs) == 1 and len(refs[0].shape) == 5:
-        return [(refs[0].at[c], c) for c in range(shard_count)]
-    return [(ref, at(place[0], r, shard_count)) for r, ref in enumerate(refs, 1)]
-
-
-def pick_kernel(place, asked, *refs, heads, head_count, shard_count):
+        return [(refs[0].at[c], c, step_to(place[0], c, shard_count)) for c in range(shard_count)]
+    return [(ref, at(place[0], r, shard_count), r) for r, ref in enumerate(refs, 1)]
+
+
+def pick_kernel(place, asked, *refs, heads, shard_count):
     own, outs, table = refs[:heads], refs[heads:-1], refs[-1]
-    for h in range(head_count):
-        fill_table(place, own, h, table)
-        steps = shard_count - 1
-        mine = outs[:steps] if h == 0 else outs[steps + h - 1 : steps + h]
-        for out, c in parts_of(mine, place, partner, shard_count):
-            for s in range(CAP):
-                block = asked[c, s]
-                for kv in range(2):
-                    out[kv, s] = table[kv, block]
-
-
-def attend_kernel(place, source, q_ref, g_ref, *refs, heads, fars, outs, head, shard_count):
+    fill_table(place, own, table)
+    for out, _, r in parts_of(outs, place, partner, shard_count):
+        for s in range(CAP):
+            block = asked[r * CAP + s]
+            for kv in range(2):
+                out[kv, s] = table[kv, block]
+
+
+def attend_kernel(place, source, q_ref, g_ref, *refs, heads, fars, outs, shard_count):
     own, far = refs[:heads], refs[heads : heads + fars]
     table, total = refs[-2:]
     far_out = refs[-2 - outs : -2]
@@ -114,8 +106,8 @@
 
     @pl.when(step == 0)
     def _():
-        fill_table(place, own, head, table)
-        for part, c in parts_of(far, place, origin, shard_count):
+        fill_table(place, own, table)
+        for part, c, _ in parts_of(far, place, origin, shard_count):
             for kv in range(2):
                 for s in range(CAP):
                     table[kv, blocks_here + c * CAP + s] = part[kv, s]
@@ -162,7 +154,7 @@
     def _():
         for kv, factor in ((0, SCALE), (1, 1.0)):
             near_out[kv] = total[kv, :blocks_here] * factor
-            for out, c in parts_of(far_out, place, origin, shard_count):
+            for out, c, _ in parts_of(far_out, place, origin, shard_count):
                 for s in range(CAP):
                     out[kv, s] = (total[kv, blocks_here + c * CAP + s] * factor).astype(jnp.bfloat16)
 
@@ -171,9 +163,9 @@
     back, outs, total = refs[: -heads - 1], refs[-heads - 1 : -1], refs[-1]
     per_quarter = outs[0].shape[1] // BLK
     total[...] = near[...]
-    for part, c in parts_of(back, place, partner, shard_count):
+    for part, _, r in parts_of(back, place, partner, shard_count):
         for s in range(CAP):
-            block = asked[c, s]
+            block = asked[r * CAP + s]
             for kv in range(2):
                 total[kv, block] += part[kv, s].astype(jnp.float32)
     for r in range(heads):
@@ -220,7 +212,7 @@
     first = 4 + len(arrays)
     return pl.pallas_call(
         functools.partial(
-            attend_kernel, heads=len(own), fars=len(far), outs=len(out_shapes), head=head, shard_count=shard_count
+            attend_kernel, heads=len(own), fars=len(far), outs=len(out_shapes), shard_count=shard_count
         ),
         grid_spec=pltpu.PrefetchScalarGridSpec(
             num_scalar_prefetch=2,
@@ -257,20 +249,26 @@
     return lax.all_to_all(x, "ctx", split_axis=0, concat_axis=0, tiled=True)
 
 
-def requests_of(flat_ids, blocks_here, shard_index, shard_count):
+def asked_of(lists, blocks_here, shard_index):
+    inner = jnp.arange(blocks_here, dtype=jnp.int32)
+    hits = jnp.any(lists[:, :, :, None] == (shard_index * blocks_here + inner)[None, None, None, :], axis=(1, 2))
+    rank = jnp.sum((hits[:, :, None] & (inner[:, None] < inner[None, :])[None]).astype(jnp.int32), axis=1)
+    slot = hits[:, None] & (rank[:, None] == jnp.arange(CAP, dtype=jnp.int32)[None, :, None])
+    blocks = jnp.sum(jnp.where(slot, inner[None, None], 0), axis=2)
+    return jnp.pad(blocks.reshape(-1), (CAP, 0))
+
+
+def source_of(flat_ids, blocks_here, shard_index, shard_count):
     owner = flat_ids // blocks_here
-    shards = jnp.arange(shard_count, dtype=jnp.int32)
-    inner = jnp.arange(blocks_here, dtype=jnp.int32)
     every_block = jnp.arange(shard_count * blocks_here, dtype=jnp.int32)
     listed = jnp.any(flat_ids[:, None] == every_block[None, :], axis=0)
-    grid = listed.reshape(shard_count, blocks_here) & (shards != shard_index)[:, None]
-    rank = jnp.sum((grid[:, :, None] & (inner[:, None] < inner[None, :])[None]).astype(jnp.int32), axis=1)
-    hit = grid[:, None] & (rank[:, None] == jnp.arange(128, dtype=jnp.int32)[None, :, None])
-    requests = jnp.sum(jnp.where(hit, inner[None, None], 0), axis=2)
     same_owner = owner[:, None] == (every_block // blocks_here)[None, :]
-    place_of = jnp.sum((same_owner & listed[None, :] & (every_block[None, :] < flat_ids[:, None])).astype(jnp.int32), axis=1)
-    source = jnp.where(owner == shard_index, flat_ids % blocks_here, blocks_here + owner * CAP + place_of)
-    return requests, source
+    rank = jnp.sum((same_owner & listed[None, :] & (every_block[None, :] < flat_ids[:, None])).astype(jnp.int32), axis=1)
+    return jnp.where(owner == shard_index, flat_ids % blocks_here, blocks_here + owner * CAP + rank)
+
+
+def after(x, *others):
+    return lax.optimization_barrier((x, *others))[0]
 
 
 def per_device(queries, key_states, value_states, block_lists, out_grad):
@@ -283,51 +281,61 @@
     place = jnp.stack([shard_index, lax.axis_index("head")]).astype(jnp.int32)
 
     pieces = call(
-        split_kernel,
+        functools.partial(split_kernel, heads=heads),
         [place],
         [key_states, value_states],
-        [bf16(head_count, 2, quarter, HEAD_DIM)] * heads,
-        [pltpu.SemaphoreType.DMA((2 * heads * head_count,))],
+        [bf16(2, quarter, HEAD_DIM)] * (heads * head_count),
+        [],
         "split",
-        any_in=True,
         limit=VMEM_MOST,
     )
-    own = [pieces[0]] + [send(pieces[r], "head", heads, r) for r in range(1, heads)]
-
-    requests, source = requests_of(block_lists.reshape(-1), blocks_here, shard_index, shard_count)
-    asked = swap(requests)
+    own, lists = [], []
+    for h in range(head_count):
+        parts = pieces[h * heads : (h + 1) * heads]
+        if h:
+            parts = [after(x, lists[0]) for x in parts]
+        own.append([parts[0]] + [send(parts[r], "head", heads, r) for r in range(1, heads)])
+        if not h:
+            lists_here = after(block_lists, *own[0][:2])
+            lists = [send_back(lists_here, "ctx", shard_count, r) for r in range(1, shard_count)]
+    asked = asked_of(jnp.stack(lists), blocks_here, shard_index)
+    source = source_of(block_lists.reshape(-1), blocks_here, shard_index, shard_count)
 
     one = (2, CAP, BLK, HEAD_DIM)
     by_step = [bf16(*one)] * (shard_count - 1)
     at_once = [bf16(shard_count, *one)]
-    picked = call(
-        functools.partial(pick_kernel, heads=heads, head_count=head_count, shard_count=shard_count),
-        [place, asked],
-        own,
-        by_step + at_once * (head_count - 1),
-        [pltpu.VMEM((2, blocks_here, BLK, HEAD_DIM), jnp.bfloat16)],
-        "pick",
-    )
-    far = [[send(picked[r - 1], "ctx", shard_count, r) for r in range(1, shard_count)]]
-    far += [[swap(x)] for x in picked[shard_count - 1 :]]
+    far = []
+    for h in range(head_count):
+        picked = call(
+            functools.partial(pick_kernel, heads=heads, shard_count=shard_count),
+            [place, asked],
+            own[h],
+            at_once if h else by_step,
+            [pltpu.VMEM((2, blocks_here, BLK, HEAD_DIM), jnp.bfloat16)],
+            "pick",
+        )
+        if h:
+            far.append([swap(after(picked[0], far[0][-2]))])
+        else:
+            far.append([send(x, "ctx", shard_count, r) for r, x in enumerate(picked, 1)])
     earlier, nears, backs = [], [], []
     for h in range(head_count):
         last = h == head_count - 1
         attended, query_grad, near, *far_grad = attend(
-            place, source, queries, out_grad, own, far[h], by_step if last else at_once, h, earlier, shard_count
+            place, source, queries, out_grad, own[h], far[h], by_step if last else at_once, h, earlier, shard_count
         )
         earlier = [attended, query_grad]
         nears.append(near)
         if last:
             backs.append([send_back(x, "ctx", shard_count, r) for r, x in enumerate(far_grad, 1)])
         else:
-            backs.append([swap(far_grad[0])])
+            backs.append([swap(after(far_grad[0], *far[h + 1]))])
     done = []
     for h in range(head_count):
         sums = call(
             functools.partial(gather_sum_kernel, heads=heads, shard_count=shard_count),
             [place, asked],
-            [nears[h], *backs[h]],
+            [after(nears[h], *done[-1:]), *backs[h]],
             [bf16(2, quarter, HEAD_DIM)] * heads,
             [pltpu.VMEM((2, blocks_here, BLK, HEAD_DIM), jnp.float32)],
             "gather_sum",

time: 142 us -> 172 us (1.21)
  waiting for transfers between devices: 37.8 us -> 67.8 us
  blocking collectives: 12.3 us -> 0 us
  starting transfers between devices: 45 us -> 56.9 us
    all_to_all x2, waiting for transfers between devices: 0.01 us -> 19.7 us  [swap(): return lax.all_to_all(x, 'ctx', split_axis=0, concat_axis=0, tiled=True)]
    all_to_all x1 -> x0, blocking collectives: 12.3 us -> none  [swap(): return lax.all_to_all(x, 'ctx', split_axis=0, concat_axis=0, tiled=True)]
    ppermute x13 -> x20, starting transfers between devices: 15.1 us -> 26.5 us  [send_back(): lax.ppermute(x, axis, [(i, origin(i, r, count)) for i in range(count)])]
    ppermute x13 -> x20, waiting for transfers between devices: 20 us -> 27.4 us  [send_back(): lax.ppermute(x, axis, [(i, origin(i, r, count)) for i in range(count)])]
    ppermute x10 -> x13, waiting for transfers between devices: 17.8 us -> 20.6 us  [send(): lax.ppermute(x, axis, [(i, partner(i, r, count)) for i in range(count)])]
    ppermute x10 -> x13, starting transfers between devices: 20.2 us -> 21.1 us  [send(): lax.ppermute(x, axis, [(i, partner(i, r, count)) for i in range(count)])]
    pallas_call x5 -> x6, Pallas kernels: 8.29 us -> 8.63 us  [call(): pl.pallas_call(kernel, grid_spec=pltpu.PrefetchScalarGridSpec(num_scalar_...]
  transfers between devices with their start and end apart: 25 -> 35, of which waited for: 9 -> 16; matrix products, arithmetic and copies ran while one was open for 1% -> 1% of each run, Pallas kernels for 24% -> 20%
where the time goes in v6:
time: 172 us; the launch traced here: 170 us
  waiting for transfers between devices  67.8 us (39%)
  starting transfers between devices  56.9 us (33%)
  Pallas kernels  40.2 us (23%)
  local copies, waits for them, and re-layouts  2.89 us (2%)
    pallas_call x2, Pallas kernels, attend(): pl.pallas_call(functools.partial(attend_kernel, heads=len(own), fars=len(...  31.5 us
    ppermute x20, waiting for transfers between devices, send_back(): lax.ppermute(x, axis, [(i, origin(i, r, count)) for i in range(count)])  27.4 us
    ppermute x20, starting transfers between devices, send_back(): lax.ppermute(x, axis, [(i, origin(i, r, count)) for i in range(count)])  26.5 us
    ppermute x13, starting transfers between devices, send(): lax.ppermute(x, axis, [(i, partner(i, r, count)) for i in range(count)])  21.1 us
    ppermute x13, waiting for transfers between devices, send(): lax.ppermute(x, axis, [(i, partner(i, r, count)) for i in range(count)])  20.6 us
    all_to_all x2, waiting for transfers between devices, swap(): return lax.all_to_all(x, 'ctx', split_axis=0, concat_axis=0, tiled=True)  19.7 us
    all_to_all x2, starting transfers between devices, swap(): return lax.all_to_all(x, 'ctx', split_axis=0, concat_axis=0, tiled=True)  9.36 us
    pallas_call x6, Pallas kernels, call(): pl.pallas_call(kernel, grid_spec=pltpu.PrefetchScalarGridSpec(num_scalar_...  8.63 us
  transfers between devices with their start and end apart: 35, of which 16 were waited for; matrix products, arithmetic and copies ran while one was open for 1% of the time, Pallas kernels for 20%

profile of v6, /device:TPU:0, one launch (start us, length us, event | category | flops | bytes accessed | tf_op | source)
XLA Modules:
  0.0 169.9 jit_solution(7173465997332898103)
XLA Ops:
  1.2 3.2 %split.1 = (bf16[2,256,128]{2,1,0:T(8,128)(2,1)}, bf16[2,256,128]{2,1,0:T(8,128)(2,1)}, bf16[2,256,128]{2,1,0:T(8,128)(2,1)}, bf16[2,256,128]{2,1,0:T(8,128)(2,1...) custom-call(s32[2]{0:T(128)} %pad_add_fusion.place, ...), custom_call_target="tpu_custom_call" | custom-call | tf_op jit(solution)/shard_map/split/pallas_call | solution.py:190
  4.9 2.6 %collective-permute-start.11 = (bf16[2,256,128]{2,1,0:T(8,128)(2,1)}, bf16[2,256,128]{2,1,0:T(8,128)(2,1)S(1)}, u32[]{:S(2)}, u32[]{:S(2)}) collective-permute-start(bf16[2,256,128]{2,1,0:T(8,128)(2,1)} %get-tuple-element.62), channel_id=1, source_target_pairs={{0,16},{8,24},{16,0},{24,8},{1,17},{9,25},{17,1},{25,9},{2,18},{10... | collective-permute-start | bytes 393224 | tf_op jit(solution)/shard_map/ppermute | solution.py:241
  7.6 1.8 %collective-permute-start.1 = (s32[16,8]{0,1:T(8,128)}, s32[16,8]{0,1:T(8,128)S(1)}, u32[]{:S(2)}, u32[]{:S(2)}) collective-permute-start(s32[16,8]{0,1:T(8,128)} %param.8), channel_id=1, source_target_pairs={{0,1},{1,0},{2,3},{3,2},{4,5},{5,4},{6,7},{7,6},{8,9},{9,8},{10,11... | collective-permute-start | bytes 1544 | tf_op jit(solution)/shard_map/ppermute | solution.py:245
  9.4 3.5 %collective-permute-start.10 = (s32[16,8]{0,1:T(8,128)}, s32[16,8]{0,1:T(8,128)S(1)}, u32[]{:S(2)}, u32[]{:S(2)}) collective-permute-start(s32[16,8]{0,1:T(8,128)} %param.8), channel_id=1, source_target_pairs={{0,7},{1,6},{2,5},{3,4},{4,3},{5,2},{6,1},{7,0},{8,15},{9,14},{10,... | collective-permute-start | bytes 1544 | tf_op jit(solution)/shard_map/ppermute | solution.py:245
  13.3 3.6 %collective-permute-done.5 = s32[16,8]{0,1:T(8,128)S(1)} collective-permute-done((s32[16,8]{0,1:T(8,128)}, s32[16,8]{0,1:T(8,128)S(1)}, u32[]{:S(2)}, u32[]{:S(2)}) %collective-permute-start.5) | collective-permute-done | bytes 544 | tf_op jit(solution)/shard_map/ppermute | solution.py:245
  16.8 1.2 collective-permute-start.6
  18.0 3.5 %collective-permute-done.6 = s32[16,8]{0,1:T(8,128)S(1)} collective-permute-done((s32[16,8]{0,1:T(8,128)}, s32[16,8]{0,1:T(8,128)S(1)}, u32[]{:S(2)}, u32[]{:S(2)}) %collective-permute-start.6) | collective-permute-done | bytes 544 | tf_op jit(solution)/shard_map/ppermute | solution.py:245
  21.5 2.4 %collective-permute-start.7 = (s32[16,8]{0,1:T(8,128)}, s32[16,8]{0,1:T(8,128)S(1)}, u32[]{:S(2)}, u32[]{:S(2)}) collective-permute-start(s32[16,8]{0,1:T(8,128)} %param.8), channel_id=1, source_target_pairs={{0,4},{1,5},{2,6},{3,7},{4,0},{5,1},{6,2},{7,3},{8,12},{9,13},{10,... | collective-permute-start | bytes 1544 | tf_op jit(solution)/shard_map/ppermute | solution.py:245
  23.9 2.4 %collective-permute-done.7 = s32[16,8]{0,1:T(8,128)S(1)} collective-permute-done((s32[16,8]{0,1:T(8,128)}, s32[16,8]{0,1:T(8,128)S(1)}, u32[]{:S(2)}, u32[]{:S(2)}) %collective-permute-start.7) | collective-permute-done | bytes 544 | tf_op jit(solution)/shard_map/ppermute | solution.py:245
  26.2 3.3 %collective-permute-start.8 = (s32[16,8]{0,1:T(8,128)}, s32[16,8]{0,1:T(8,128)S(1)}, u32[]{:S(2)}, u32[]{:S(2)}) collective-permute-start(s32[16,8]{0,1:T(8,128)} %param.8), channel_id=1, source_target_pairs={{0,5},{1,4},{2,7},{3,6},{4,1},{5,0},{6,3},{7,2},{8,13},{9,12},{10,... | collective-permute-start | bytes 1544 | tf_op jit(solution)/shard_map/ppermute | solution.py:245
  29.5 2.3 %collective-permute-done.8 = s32[16,8]{0,1:T(8,128)S(1)} collective-permute-done((s32[16,8]{0,1:T(8,128)}, s32[16,8]{0,1:T(8,128)S(1)}, u32[]{:S(2)}, u32[]{:S(2)}) %collective-permute-start.8) | collective-permute-done | bytes 544 | tf_op jit(solution)/shard_map/ppermute | solution.py:245
  32.0 1.7 %collective-permute-start.3 = (bf16[2,256,128]{2,1,0:T(8,128)(2,1)}, bf16[2,256,128]{2,1,0:T(8,128)(2,1)S(1)}, u32[]{:S(2)}, u32[]{:S(2)}) collective-permute-start(bf16[2,256,128]{2,1,0:T(8,128)(2,1)} %get-tuple-element.59), channel_id=1, source_target_pairs={{0,16},{8,24},{16,0},{24,8},{1,17},{9,25},{17,1},{25,9},{2,18},{10... | collective-permute-start | bytes 393224 | tf_op jit(solution)/shard_map/ppermute | solution.py:241
  34.6 0.9 copy-done.2
  36.7 3.8 %collective-permute-start.13 = (bf16[2,3,64,128]{3,2,1,0:T(8,128)(2,1)S(1)}, bf16[2,3,64,128]{3,2,1,0:T(8,128)(2,1)S(1)}, u32[]{:S(2)}, u32[]{:S(2)}) collective-permute-start(bf16[2,3,64,128]{3,2,1,0:T(8,128)(2,1)S(1)} %get-tuple-element.64), channel_id=1, source_target_pairs={{0,6},{1,7},{2,4},{3,5},{4,2},{5,3},{6,0},{7,1},{8,14},{9,15},{10,... | collective-permute-start | bytes 294920 | tf_op jit(solution)/shard_map/ppermute | solution.py:241
  40.6 0.9 copy-done
  41.5 1.5 pick.2
  43.0 1.0 collective-permute-done.13.refs_9_
  43.9 5.7 %all-to-all-start = ((bf16[8,2,3,64,128]{4,3,2,1,0:T(8,128)(2,1)}), bf16[8,2,3,64,128]{4,3,2,1,0:T(8,128)(2,1)S(1)}, u32[]{:S(2)}, u32[]{:S(2)}) async-start(bf16[8,2,3,64,128]{4,3,2,1,0:T(8,128)(2,1)} %pick.2), calls=%async_computation | async-start | bytes 1572864 | tf_op jit(solution)/shard_map/all_to_all | solution.py:249
  49.9 2.1 %collective-permute-start.14 = (bf16[2,3,64,128]{3,2,1,0:T(8,128)(2,1)S(1)}, bf16[2,3,64,128]{3,2,1,0:T(8,128)(2,1)S(1)}, u32[]{:S(2)}, u32[]{:S(2)}) collective-permute-start(bf16[2,3,64,128]{3,2,1,0:T(8,128)(2,1)S(1)} %get-tuple-element.66), channel_id=1, source_target_pairs={{0,1},{1,0},{2,3},{3,2},{4,5},{5,4},{6,7},{7,6},{8,9},{9,8},{10,11... | collective-permute-start | bytes 294920 | tf_op jit(solution)/shard_map/ppermute | solution.py:241
  52.2 1.5 collective-permute-start.15
  53.8 2.8 %collective-permute-start.17 = (bf16[2,3,64,128]{3,2,1,0:T(8,128)(2,1)S(1)}, bf16[2,3,64,128]{3,2,1,0:T(8,128)(2,1)S(1)}, u32[]{:S(2)}, u32[]{:S(2)}) collective-permute-start(bf16[2,3,64,128]{3,2,1,0:T(8,128)(2,1)S(1)} %get-tuple-element.69), channel_id=1, source_target_pairs={{0,4},{1,5},{2,6},{3,7},{4,0},{5,1},{6,2},{7,3},{8,12},{9,13},{10,... | collective-permute-start | bytes 294920 | tf_op jit(solution)/shard_map/ppermute | solution.py:241
  56.6 1.5 collective-permute-start.18
  58.1 0.8 collective-permute-done.14.refs_4_
  58.9 4.2 %collective-permute-start.19 = (bf16[2,3,64,128]{3,2,1,0:T(8,128)(2,1)S(1)}, bf16[2,3,64,128]{3,2,1,0:T(8,128)(2,1)S(1)}, u32[]{:S(2)}, u32[]{:S(2)}) collective-permute-start(bf16[2,3,64,128]{3,2,1,0:T(8,128)(2,1)S(1)} %get-tuple-element.71), channel_id=1, source_target_pairs={{0,7},{1,6},{2,5},{3,4},{4,3},{5,2},{6,1},{7,0},{8,15},{9,14},{10,... | collective-permute-start | bytes 294920 | tf_op jit(solution)/shard_map/ppermute | solution.py:241
  63.1 2.6 %collective-permute-done.15.refs_5_ = bf16[2,3,64,128]{3,2,1,0:T(8,128)(2,1)S(1)} collective-permute-done((bf16[2,3,64,128]{3,2,1,0:T(8,128)(2,1)S(1)}, bf16[2,3,64,128]{3,2,1,0:T(8,128)(2,1)S(1)}, u32[]{:S(2)}, u32[]{:S(2)}) %collective-permute-start.15) | collective-permute-done | bytes 98336 | tf_op jit(solution)/shard_map/ppermute | solution.py:241
  65.7 2.3 %collective-permute-done.16.refs_6_ = bf16[2,3,64,128]{3,2,1,0:T(8,128)(2,1)S(1)} collective-permute-done((bf16[2,3,64,128]{3,2,1,0:T(8,128)(2,1)S(1)}, bf16[2,3,64,128]{3,2,1,0:T(8,128)(2,1)S(1)}, u32[]{:S(2)}, u32[]{:S(2)}) %collective-permute-start.16) | collective-permute-done | bytes 98336 | tf_op jit(solution)/shard_map/ppermute | solution.py:241
  68.0 11.7 %collective-permute-done.17.refs_7_ = bf16[2,3,64,128]{3,2,1,0:T(8,128)(2,1)S(1)} collective-permute-done((bf16[2,3,64,128]{3,2,1,0:T(8,128)(2,1)S(1)}, bf16[2,3,64,128]{3,2,1,0:T(8,128)(2,1)S(1)}, u32[]{:S(2)}, u32[]{:S(2)}) %collective-permute-start.17) | collective-permute-done | bytes 98336 | tf_op jit(solution)/shard_map/ppermute | solution.py:241
  79.6 2.3 %collective-permute-done.18.refs_8_ = bf16[2,3,64,128]{3,2,1,0:T(8,128)(2,1)S(1)} collective-permute-done((bf16[2,3,64,128]{3,2,1,0:T(8,128)(2,1)S(1)}, bf16[2,3,64,128]{3,2,1,0:T(8,128)(2,1)S(1)}, u32[]{:S(2)}, u32[]{:S(2)}) %collective-permute-start.18) | collective-permute-done | bytes 98336 | tf_op jit(solution)/shard_map/ppermute | solution.py:241
  82.0 15.9 %attend.2 = (bf16[1024,1024]{1,0:T(8,128)(2,1)}, bf16[1024,1024]{1,0:T(8,128)(2,1)}, f32[2,16,64,128]{3,2,1,0:T(8,128)S(1)}, bf16[8,2,3,64,128]{4,3,2,1,0:T(8,128)(2,1)}) custom-call(s32[2]{0:T(128)S(1)} %copy-done.5, s32[128]{0:T(128)S(1)} %compare_select_fusion.source, bf16[1024,1024]{1,0:T(8,128)(2,1)} %q_ref.3, bf16[1024,1024]{1,0:T(8,128)(2,1)} %g_ref.3, ...), custom_call_target="tpu_custom_call" | custom-call | flops 3221225472 | bytes 20971520 | tf_op jit(solution)/shard_map/attend/pallas_call | solution.py:213
  97.9 3.7 %all-to-all-start.1 = ((bf16[8,2,3,64,128]{4,3,2,1,0:T(8,128)(2,1)}), bf16[8,2,3,64,128]{4,3,2,1,0:T(8,128)(2,1)S(1)}, u32[]{:S(2)}, u32[]{:S(2)}) async-start(bf16[8,2,3,64,128]{4,3,2,1,0:T(8,128)(2,1)} %get-tuple-element.78), calls=%async_computation.1 | async-start | bytes 1572864 | tf_op jit(solution)/shard_map/all_to_all | solution.py:249
  101.6 19.7 %all-to-all-done.1.refs_0_ = bf16[8,2,3,64,128]{4,3,2,1,0:T(8,128)(2,1)S(1)} async-done(((bf16[8,2,3,64,128]{4,3,2,1,0:T(8,128)(2,1)}), bf16[8,2,3,64,128]{4,3,2,1,0:T(8,128)(2,1)S(1)}, u32[]{:S(2)}, u32[]{:S(2)}) %all-to-all-start.1) | async-done | bytes 786464 | tf_op jit(solution)/shard_map/all_to_all | solution.py:249
  121.3 0.8 gather_sum.2
  122.3 15.6 %attend.3 = (bf16[1024,1024]{1,0:T(8,128)(2,1)}, bf16[1024,1024]{1,0:T(8,128)(2,1)}, f32[2,16,64,128]{3,2,1,0:T(8,128)S(1)}, bf16[2,3,64,128]{3,2,1,0:T(8,128)(2...) custom-call(s32[2]{0:T(128)S(1)} %copy-done.5, ...), custom_call_target="tpu_custom_call", output_to_operand_aliasing={{0}: (9, {}), {1}: (10, {})} | custom-call | flops 3221225472 | bytes 20971520 | tf_op jit(solution)/shard_map/attend/pallas_call | solution.py:213
  137.9 1.4 collective-permute-start.23
  139.3 2.1 %collective-permute-start.25 = (bf16[2,3,64,128]{3,2,1,0:T(8,128)(2,1)S(1)}, bf16[2,3,64,128]{3,2,1,0:T(8,128)(2,1)S(1)}, u32[]{:S(2)}, u32[]{:S(2)}) collective-permute-start(bf16[2,3,64,128]{3,2,1,0:T(8,128)(2,1)S(1)} %get-tuple-element.87), channel_id=1, source_target_pairs={{0,3},{1,2},{2,1},{3,0},{4,7},{5,6},{6,5},{7,4},{8,11},{9,10},{10,... | collective-permute-start | bytes 294920 | tf_op jit(solution)/shard_map/ppermute | solution.py:245
  141.4 1.0 collective-permute-start.26
  142.3 0.7 collective-permute-done.23.refs_0_
  143.0 2.2 %collective-permute-start.27 = (bf16[2,3,64,128]{3,2,1,0:T(8,128)(2,1)S(1)}, bf16[2,3,64,128]{3,2,1,0:T(8,128)(2,1)S(1)}, u32[]{:S(2)}, u32[]{:S(2)}) collective-permute-start(bf16[2,3,64,128]{3,2,1,0:T(8,128)(2,1)S(1)} %get-tuple-element.89), channel_id=1, source_target_pairs={{0,5},{1,4},{2,7},{3,6},{4,1},{5,0},{6,3},{7,2},{8,13},{9,12},{10,... | collective-permute-start | bytes 294920 | tf_op jit(solution)/shard_map/ppermute | solution.py:245
  145.2 4.3 %collective-permute-start.28 = (bf16[2,3,64,128]{3,2,1,0:T(8,128)(2,1)S(1)}, bf16[2,3,64,128]{3,2,1,0:T(8,128)(2,1)S(1)}, u32[]{:S(2)}, u32[]{:S(2)}) collective-permute-start(bf16[2,3,64,128]{3,2,1,0:T(8,128)(2,1)S(1)} %get-tuple-element.90), channel_id=1, source_target_pairs={{0,6},{1,7},{2,4},{3,5},{4,2},{5,3},{6,0},{7,1},{8,14},{9,15},{10,... | collective-permute-start | bytes 294920 | tf_op jit(solution)/shard_map/ppermute | solution.py:245
  149.6 6.8 %collective-permute-done.26.refs_3_ = bf16[2,3,64,128]{3,2,1,0:T(8,128)(2,1)S(1)} collective-permute-done((bf16[2,3,64,128]{3,2,1,0:T(8,128)(2,1)S(1)}, bf16[2,3,64,128]{3,2,1,0:T(8,128)(2,1)S(1)}, u32[]{:S(2)}, u32[]{:S(2)}) %collective-permute-start.26) | collective-permute-done | bytes 98336 | tf_op jit(solution)/shard_map/ppermute | solution.py:245
  156.4 0.9 collective-permute-start.21
  157.3 1.8 %collective-permute-done.27.refs_4_ = bf16[2,3,64,128]{3,2,1,0:T(8,128)(2,1)S(1)} collective-permute-done((bf16[2,3,64,128]{3,2,1,0:T(8,128)(2,1)S(1)}, bf16[2,3,64,128]{3,2,1,0:T(8,128)(2,1)S(1)}, u32[]{:S(2)}, u32[]{:S(2)}) %collective-permute-start.27) | collective-permute-done | bytes 98336 | tf_op jit(solution)/shard_map/ppermute | solution.py:245
  159.1 0.8 gather_sum.3
  160.0 1.1 collective-permute-start.31
  161.1 0.8 collective-permute-start.32
  161.9 4.5 %collective-permute-done.31.refs_6_ = bf16[2,256,128]{2,1,0:T(8,128)(2,1)S(1)} collective-permute-done((bf16[2,256,128]{2,1,0:T(8,128)(2,1)S(1)}, bf16[2,256,128]{2,1,0:T(8,128)(2,1)S(1)}, u32[]{:S(2)}, u32[]{:S(2)}) %collective-permute-start.31) | collective-permute-done | bytes 131104 | tf_op jit(solution)/shard_map/ppermute | solution.py:245
  166.4 1.9 %collective-permute-done.32.refs_7_ = bf16[2,256,128]{2,1,0:T(8,128)(2,1)S(1)} collective-permute-done((bf16[2,256,128]{2,1,0:T(8,128)(2,1)S(1)}, bf16[2,256,128]{2,1,0:T(8,128)(2,1)S(1)}, u32[]{:S(2)}, u32[]{:S(2)}) %collective-permute-start.32) | collective-permute-done | bytes 131104 | tf_op jit(solution)/shard_map/ppermute | solution.py:245
  168.3 1.6 join.1
  (68 shorter events, 4.4 us)
Async XLA Ops:
  1.2 48.4 %copy-start.6 = (s32[16,8]{0,1:T(8,128)S(1)}, s32[16,8]{0,1:T(8,128)}, u32[]{:S(2)}) copy-start(s32[16,8]{0,1:T(8,128)} %param.8) | copy-start | bytes 1540
  4.4 77.5 %copy-start.3 = (bf16[2,256,128]{2,1,0:T(8,128)(2,1)S(1)}, bf16[2,256,128]{2,1,0:T(8,128)(2,1)}, u32[]{:S(2)}) copy-start(bf16[2,256,128]{2,1,0:T(8,128)(2,1)} %get-tuple-element.52.refs_0_) | copy-start | bytes 393220
  4.4 77.5 %copy-start.5 = (s32[2]{0:T(128)S(1)}, s32[2]{0:T(128)}, u32[]{:S(2)}) copy-start(s32[2]{0:T(128)} %pad_add_fusion.place) | copy-start | bytes 28
  4.4 3.1 %collective-permute-start = (bf16[2,256,128]{2,1,0:T(8,128)(2,1)}, bf16[2,256,128]{2,1,0:T(8,128)(2,1)S(1)}, u32[]{:S(2)}, u32[]{:S(2)}) collective-permute-start(bf16[2,256,128]{2,1,0:T(8,128)(2,1)} %get-tuple-element.53), channel_id=1, source_target_pairs={{0,8},{8,0},{16,24},{24,16},{1,9},{9,1},{17,25},{25,17},{2,10},{10... | collective-permute-start | bytes 393224 | tf_op jit(solution)/shard_map/ppermute | solution.py:241
  4.9 29.7 %collective-permute-start.11 = (bf16[2,256,128]{2,1,0:T(8,128)(2,1)}, bf16[2,256,128]{2,1,0:T(8,128)(2,1)S(1)}, u32[]{:S(2)}, u32[]{:S(2)}) collective-permute-start(bf16[2,256,128]{2,1,0:T(8,128)(2,1)} %get-tuple-element.62), channel_id=1, source_target_pairs={{0,16},{8,24},{16,0},{24,8},{1,17},{9,25},{17,1},{25,9},{2,18},{10... | collective-permute-start | bytes 393224 | tf_op jit(solution)/shard_map/ppermute | solution.py:241
  7.5 27.1 %collective-permute-start.12 = (bf16[2,256,128]{2,1,0:T(8,128)(2,1)}, bf16[2,256,128]{2,1,0:T(8,128)(2,1)S(1)}, u32[]{:S(2)}, u32[]{:S(2)}) collective-permute-start(bf16[2,256,128]{2,1,0:T(8,128)(2,1)} %get-tuple-element.63), channel_id=1, source_target_pairs={{0,24},{8,16},{16,8},{24,0},{1,25},{9,17},{17,9},{25,1},{2,26},{10... | collective-permute-start | bytes 393224 | tf_op jit(solution)/shard_map/ppermute | solution.py:241
  7.6 5.4 %collective-permute-start.1 = (s32[16,8]{0,1:T(8,128)}, s32[16,8]{0,1:T(8,128)S(1)}, u32[]{:S(2)}, u32[]{:S(2)}) collective-permute-start(s32[16,8]{0,1:T(8,128)} %param.8), channel_id=1, source_target_pairs={{0,1},{1,0},{2,3},{3,2},{4,5},{5,4},{6,7},{7,6},{8,9},{9,8},{10,11... | collective-permute-start | bytes 1544 | tf_op jit(solution)/shard_map/ppermute | solution.py:245
  9.4 22.5 %collective-permute-start.10 = (s32[16,8]{0,1:T(8,128)}, s32[16,8]{0,1:T(8,128)S(1)}, u32[]{:S(2)}, u32[]{:S(2)}) collective-permute-start(s32[16,8]{0,1:T(8,128)} %param.8), channel_id=1, source_target_pairs={{0,7},{1,6},{2,5},{3,4},{4,3},{5,2},{6,1},{7,0},{8,15},{9,14},{10,... | collective-permute-start | bytes 1544 | tf_op jit(solution)/shard_map/ppermute | solution.py:245
  12.9 18.9 %collective-permute-start.9 = (s32[16,8]{0,1:T(8,128)}, s32[16,8]{0,1:T(8,128)S(1)}, u32[]{:S(2)}, u32[]{:S(2)}) collective-permute-start(s32[16,8]{0,1:T(8,128)} %param.8), channel_id=1, source_target_pairs={{0,6},{1,7},{2,4},{3,5},{4,2},{5,3},{6,0},{7,1},{8,14},{9,15},{10,... | collective-permute-start | bytes 1544 | tf_op jit(solution)/shard_map/ppermute | solution.py:245
  13.0 3.8 %collective-permute-start.5 = (s32[16,8]{0,1:T(8,128)}, s32[16,8]{0,1:T(8,128)S(1)}, u32[]{:S(2)}, u32[]{:S(2)}) collective-permute-start(s32[16,8]{0,1:T(8,128)} %param.8), channel_id=1, source_target_pairs={{0,2},{1,3},{2,0},{3,1},{4,6},{5,7},{6,4},{7,5},{8,10},{9,11},{10,... | collective-permute-start | bytes 1544 | tf_op jit(solution)/shard_map/ppermute | solution.py:245
  16.8 4.7 %collective-permute-start.6 = (s32[16,8]{0,1:T(8,128)}, s32[16,8]{0,1:T(8,128)S(1)}, u32[]{:S(2)}, u32[]{:S(2)}) collective-permute-start(s32[16,8]{0,1:T(8,128)} %param.8), channel_id=1, source_target_pairs={{0,3},{1,2},{2,1},{3,0},{4,7},{5,6},{6,5},{7,4},{8,11},{9,10},{10,... | collective-permute-start | bytes 1544 | tf_op jit(solution)/shard_map/ppermute | solution.py:245
  21.5 4.7 %collective-permute-start.7 = (s32[16,8]{0,1:T(8,128)}, s32[16,8]{0,1:T(8,128)S(1)}, u32[]{:S(2)}, u32[]{:S(2)}) collective-permute-start(s32[16,8]{0,1:T(8,128)} %param.8), channel_id=1, source_target_pairs={{0,4},{1,5},{2,6},{3,7},{4,0},{5,1},{6,2},{7,3},{8,12},{9,13},{10,... | collective-permute-start | bytes 1544 | tf_op jit(solution)/shard_map/ppermute | solution.py:245
  26.2 5.6 %collective-permute-start.8 = (s32[16,8]{0,1:T(8,128)}, s32[16,8]{0,1:T(8,128)S(1)}, u32[]{:S(2)}, u32[]{:S(2)}) collective-permute-start(s32[16,8]{0,1:T(8,128)} %param.8), channel_id=1, source_target_pairs={{0,5},{1,4},{2,7},{3,6},{4,1},{5,0},{6,3},{7,2},{8,13},{9,12},{10,... | collective-permute-start | bytes 1544 | tf_op jit(solution)/shard_map/ppermute | solution.py:245
  32.0 8.6 %collective-permute-start.2 = (bf16[2,256,128]{2,1,0:T(8,128)(2,1)}, bf16[2,256,128]{2,1,0:T(8,128)(2,1)S(1)}, u32[]{:S(2)}, u32[]{:S(2)}) collective-permute-start(bf16[2,256,128]{2,1,0:T(8,128)(2,1)} %get-tuple-element.57), channel_id=1, source_target_pairs={{0,8},{8,0},{16,24},{24,16},{1,9},{9,1},{17,25},{25,17},{2,10},{10... | collective-permute-start | bytes 393224 | tf_op jit(solution)/shard_map/ppermute | solution.py:241
  32.0 8.5 %collective-permute-start.3 = (bf16[2,256,128]{2,1,0:T(8,128)(2,1)}, bf16[2,256,128]{2,1,0:T(8,128)(2,1)S(1)}, u32[]{:S(2)}, u32[]{:S(2)}) collective-permute-start(bf16[2,256,128]{2,1,0:T(8,128)(2,1)} %get-tuple-element.59), channel_id=1, source_target_pairs={{0,16},{8,24},{16,0},{24,8},{1,17},{9,25},{17,1},{25,9},{2,18},{10... | collective-permute-start | bytes 393224 | tf_op jit(solution)/shard_map/ppermute | solution.py:241
  33.7 6.8 %collective-permute-start.4 = (bf16[2,256,128]{2,1,0:T(8,128)(2,1)}, bf16[2,256,128]{2,1,0:T(8,128)(2,1)S(1)}, u32[]{:S(2)}, u32[]{:S(2)}) collective-permute-start(bf16[2,256,128]{2,1,0:T(8,128)(2,1)} %get-tuple-element.61), channel_id=1, source_target_pairs={{0,24},{8,16},{16,8},{24,0},{1,25},{9,17},{17,9},{25,1},{2,26},{10... | collective-permute-start | bytes 393224 | tf_op jit(solution)/shard_map/ppermute | solution.py:241
  34.6 0.9 copy-start.2
  35.5 0.6 copy-start.4
  36.7 7.2 %collective-permute-start.13 = (bf16[2,3,64,128]{3,2,1,0:T(8,128)(2,1)S(1)}, bf16[2,3,64,128]{3,2,1,0:T(8,128)(2,1)S(1)}, u32[]{:S(2)}, u32[]{:S(2)}) collective-permute-start(bf16[2,3,64,128]{3,2,1,0:T(8,128)(2,1)S(1)} %get-tuple-element.64), channel_id=1, source_target_pairs={{0,6},{1,7},{2,4},{3,5},{4,2},{5,3},{6,0},{7,1},{8,14},{9,15},{10,... | collective-permute-start | bytes 294920 | tf_op jit(solution)/shard_map/ppermute | solution.py:241
  40.6 0.9 copy-start
  43.9 53.9 %all-to-all-start = ((bf16[8,2,3,64,128]{4,3,2,1,0:T(8,128)(2,1)}), bf16[8,2,3,64,128]{4,3,2,1,0:T(8,128)(2,1)S(1)}, u32[]{:S(2)}, u32[]{:S(2)}) async-start(bf16[8,2,3,64,128]{4,3,2,1,0:T(8,128)(2,1)} %pick.2), calls=%async_computation | async-start | bytes 1572864 | tf_op jit(solution)/shard_map/all_to_all | solution.py:249
  49.9 9.0 %collective-permute-start.14 = (bf16[2,3,64,128]{3,2,1,0:T(8,128)(2,1)S(1)}, bf16[2,3,64,128]{3,2,1,0:T(8,128)(2,1)S(1)}, u32[]{:S(2)}, u32[]{:S(2)}) collective-permute-start(bf16[2,3,64,128]{3,2,1,0:T(8,128)(2,1)S(1)} %get-tuple-element.66), channel_id=1, source_target_pairs={{0,1},{1,0},{2,3},{3,2},{4,5},{5,4},{6,7},{7,6},{8,9},{9,8},{10,11... | collective-permute-start | bytes 294920 | tf_op jit(solution)/shard_map/ppermute | solution.py:241
  52.2 13.5 %collective-permute-start.15 = (bf16[2,3,64,128]{3,2,1,0:T(8,128)(2,1)S(1)}, bf16[2,3,64,128]{3,2,1,0:T(8,128)(2,1)S(1)}, u32[]{:S(2)}, u32[]{:S(2)}) collective-permute-start(bf16[2,3,64,128]{3,2,1,0:T(8,128)(2,1)S(1)} %get-tuple-element.67), channel_id=1, source_target_pairs={{0,2},{1,3},{2,0},{3,1},{4,6},{5,7},{6,4},{7,5},{8,10},{9,11},{10,... | collective-permute-start | bytes 294920 | tf_op jit(solution)/shard_map/ppermute | solution.py:241
  53.7 14.3 %collective-permute-start.16 = (bf16[2,3,64,128]{3,2,1,0:T(8,128)(2,1)S(1)}, bf16[2,3,64,128]{3,2,1,0:T(8,128)(2,1)S(1)}, u32[]{:S(2)}, u32[]{:S(2)}) collective-permute-start(bf16[2,3,64,128]{3,2,1,0:T(8,128)(2,1)S(1)} %get-tuple-element.68), channel_id=1, source_target_pairs={{0,3},{1,2},{2,1},{3,0},{4,7},{5,6},{6,5},{7,4},{8,11},{9,10},{10,... | collective-permute-start | bytes 294920 | tf_op jit(solution)/shard_map/ppermute | solution.py:241
  53.8 25.9 %collective-permute-start.17 = (bf16[2,3,64,128]{3,2,1,0:T(8,128)(2,1)S(1)}, bf16[2,3,64,128]{3,2,1,0:T(8,128)(2,1)S(1)}, u32[]{:S(2)}, u32[]{:S(2)}) collective-permute-start(bf16[2,3,64,128]{3,2,1,0:T(8,128)(2,1)S(1)} %get-tuple-element.69), channel_id=1, source_target_pairs={{0,4},{1,5},{2,6},{3,7},{4,0},{5,1},{6,2},{7,3},{8,12},{9,13},{10,... | collective-permute-start | bytes 294920 | tf_op jit(solution)/shard_map/ppermute | solution.py:241
  56.6 25.3 %collective-permute-start.18 = (bf16[2,3,64,128]{3,2,1,0:T(8,128)(2,1)S(1)}, bf16[2,3,64,128]{3,2,1,0:T(8,128)(2,1)S(1)}, u32[]{:S(2)}, u32[]{:S(2)}) collective-permute-start(bf16[2,3,64,128]{3,2,1,0:T(8,128)(2,1)S(1)} %get-tuple-element.70), channel_id=1, source_target_pairs={{0,5},{1,4},{2,7},{3,6},{4,1},{5,0},{6,3},{7,2},{8,13},{9,12},{10,... | collective-permute-start | bytes 294920 | tf_op jit(solution)/shard_map/ppermute | solution.py:241
  58.9 23.0 %collective-permute-start.19 = (bf16[2,3,64,128]{3,2,1,0:T(8,128)(2,1)S(1)}, bf16[2,3,64,128]{3,2,1,0:T(8,128)(2,1)S(1)}, u32[]{:S(2)}, u32[]{:S(2)}) collective-permute-start(bf16[2,3,64,128]{3,2,1,0:T(8,128)(2,1)S(1)} %get-tuple-element.71), channel_id=1, source_target_pairs={{0,7},{1,6},{2,5},{3,4},{4,3},{5,2},{6,1},{7,0},{8,15},{9,14},{10,... | collective-permute-start | bytes 294920 | tf_op jit(solution)/shard_map/ppermute | solution.py:241
  97.9 24.4 %copy-start.1 = (bf16[2,256,128]{2,1,0:T(8,128)(2,1)S(1)}, bf16[2,256,128]{2,1,0:T(8,128)(2,1)}, u32[]{:S(2)}) copy-start(bf16[2,256,128]{2,1,0:T(8,128)(2,1)} %get-tuple-element.55.refs_0_) | copy-start | bytes 393220
  97.9 23.4 %all-to-all-start.1 = ((bf16[8,2,3,64,128]{4,3,2,1,0:T(8,128)(2,1)}), bf16[8,2,3,64,128]{4,3,2,1,0:T(8,128)(2,1)S(1)}, u32[]{:S(2)}, u32[]{:S(2)}) async-start(bf16[8,2,3,64,128]{4,3,2,1,0:T(8,128)(2,1)} %get-tuple-element.78), calls=%async_computation.1 | async-start | bytes 1572864 | tf_op jit(solution)/shard_map/all_to_all | solution.py:249
  122.2 27.3 %collective-permute-start.22 = (bf16[2,256,128]{2,1,0:T(8,128)(2,1)S(1)}, bf16[2,256,128]{2,1,0:T(8,128)(2,1)S(1)}, u32[]{:S(2)}, u32[]{:S(2)}) collective-permute-start(bf16[2,256,128]{2,1,0:T(8,128)(2,1)S(1)} %get-tuple-element.82), channel_id=1, source_target_pairs={{0,24},{8,16},{16,8},{24,0},{1,25},{9,17},{17,9},{25,1},{2,26},{10... | collective-permute-start | bytes 393224 | tf_op jit(solution)/shard_map/ppermute | solution.py:245
  137.9 5.1 %collective-permute-start.23 = (bf16[2,3,64,128]{3,2,1,0:T(8,128)(2,1)S(1)}, bf16[2,3,64,128]{3,2,1,0:T(8,128)(2,1)S(1)}, u32[]{:S(2)}, u32[]{:S(2)}) collective-permute-start(bf16[2,3,64,128]{3,2,1,0:T(8,128)(2,1)S(1)} %get-tuple-element.85), channel_id=1, source_target_pairs={{0,1},{1,0},{2,3},{3,2},{4,5},{5,4},{6,7},{7,6},{8,9},{9,8},{10,11... | collective-permute-start | bytes 294920 | tf_op jit(solution)/shard_map/ppermute | solution.py:245
  139.3 5.9 %collective-permute-start.24 = (bf16[2,3,64,128]{3,2,1,0:T(8,128)(2,1)S(1)}, bf16[2,3,64,128]{3,2,1,0:T(8,128)(2,1)S(1)}, u32[]{:S(2)}, u32[]{:S(2)}) collective-permute-start(bf16[2,3,64,128]{3,2,1,0:T(8,128)(2,1)S(1)} %get-tuple-element.86), channel_id=1, source_target_pairs={{0,2},{1,3},{2,0},{3,1},{4,6},{5,7},{6,4},{7,5},{8,10},{9,11},{10,... | collective-permute-start | bytes 294920 | tf_op jit(solution)/shard_map/ppermute | solution.py:245
  139.3 10.2 %collective-permute-start.25 = (bf16[2,3,64,128]{3,2,1,0:T(8,128)(2,1)S(1)}, bf16[2,3,64,128]{3,2,1,0:T(8,128)(2,1)S(1)}, u32[]{:S(2)}, u32[]{:S(2)}) collective-permute-start(bf16[2,3,64,128]{3,2,1,0:T(8,128)(2,1)S(1)} %get-tuple-element.87), channel_id=1, source_target_pairs={{0,3},{1,2},{2,1},{3,0},{4,7},{5,6},{6,5},{7,4},{8,11},{9,10},{10,... | collective-permute-start | bytes 294920 | tf_op jit(solution)/shard_map/ppermute | solution.py:245
  141.4 15.0 %collective-permute-start.26 = (bf16[2,3,64,128]{3,2,1,0:T(8,128)(2,1)S(1)}, bf16[2,3,64,128]{3,2,1,0:T(8,128)(2,1)S(1)}, u32[]{:S(2)}, u32[]{:S(2)}) collective-permute-start(bf16[2,3,64,128]{3,2,1,0:T(8,128)(2,1)S(1)} %get-tuple-element.88), channel_id=1, source_target_pairs={{0,4},{1,5},{2,6},{3,7},{4,0},{5,1},{6,2},{7,3},{8,12},{9,13},{10,... | collective-permute-start | bytes 294920 | tf_op jit(solution)/shard_map/ppermute | solution.py:245
  143.0 16.1 %collective-permute-start.27 = (bf16[2,3,64,128]{3,2,1,0:T(8,128)(2,1)S(1)}, bf16[2,3,64,128]{3,2,1,0:T(8,128)(2,1)S(1)}, u32[]{:S(2)}, u32[]{:S(2)}) collective-permute-start(bf16[2,3,64,128]{3,2,1,0:T(8,128)(2,1)S(1)} %get-tuple-element.89), channel_id=1, source_target_pairs={{0,5},{1,4},{2,7},{3,6},{4,1},{5,0},{6,3},{7,2},{8,13},{9,12},{10,... | collective-permute-start | bytes 294920 | tf_op jit(solution)/shard_map/ppermute | solution.py:245
  145.2 14.0 %collective-permute-start.28 = (bf16[2,3,64,128]{3,2,1,0:T(8,128)(2,1)S(1)}, bf16[2,3,64,128]{3,2,1,0:T(8,128)(2,1)S(1)}, u32[]{:S(2)}, u32[]{:S(2)}) collective-permute-start(bf16[2,3,64,128]{3,2,1,0:T(8,128)(2,1)S(1)} %get-tuple-element.90), channel_id=1, source_target_pairs={{0,6},{1,7},{2,4},{3,5},{4,2},{5,3},{6,0},{7,1},{8,14},{9,15},{10,... | collective-permute-start | bytes 294920 | tf_op jit(solution)/shard_map/ppermute | solution.py:245
  149.5 9.6 %collective-permute-start.29 = (bf16[2,3,64,128]{3,2,1,0:T(8,128)(2,1)S(1)}, bf16[2,3,64,128]{3,2,1,0:T(8,128)(2,1)S(1)}, u32[]{:S(2)}, u32[]{:S(2)}) collective-permute-start(bf16[2,3,64,128]{3,2,1,0:T(8,128)(2,1)S(1)} %get-tuple-element.91), channel_id=1, source_target_pairs={{0,7},{1,6},{2,5},{3,4},{4,3},{5,2},{6,1},{7,0},{8,15},{9,14},{10,... | collective-permute-start | bytes 294920 | tf_op jit(solution)/shard_map/ppermute | solution.py:245
  149.5 12.4 %collective-permute-start.20 = (bf16[2,256,128]{2,1,0:T(8,128)(2,1)S(1)}, bf16[2,256,128]{2,1,0:T(8,128)(2,1)S(1)}, u32[]{:S(2)}, u32[]{:S(2)}) collective-permute-start(bf16[2,256,128]{2,1,0:T(8,128)(2,1)S(1)} %get-tuple-element.80), channel_id=1, source_target_pairs={{0,8},{8,0},{16,24},{24,16},{1,9},{9,1},{17,25},{25,17},{2,10},{10... | collective-permute-start | bytes 393224 | tf_op jit(solution)/shard_map/ppermute | solution.py:245
  156.4 5.5 %collective-permute-start.21 = (bf16[2,256,128]{2,1,0:T(8,128)(2,1)S(1)}, bf16[2,256,128]{2,1,0:T(8,128)(2,1)S(1)}, u32[]{:S(2)}, u32[]{:S(2)}) collective-permute-start(bf16[2,256,128]{2,1,0:T(8,128)(2,1)S(1)} %get-tuple-element.81), channel_id=1, source_target_pairs={{0,16},{8,24},{16,0},{24,8},{1,17},{9,25},{17,1},{25,9},{2,18},{10... | collective-permute-start | bytes 393224 | tf_op jit(solution)/shard_map/ppermute | solution.py:245
  160.0 2.0 %collective-permute-start.30 = (bf16[2,256,128]{2,1,0:T(8,128)(2,1)S(1)}, bf16[2,256,128]{2,1,0:T(8,128)(2,1)S(1)}, u32[]{:S(2)}, u32[]{:S(2)}) collective-permute-start(bf16[2,256,128]{2,1,0:T(8,128)(2,1)S(1)} %get-tuple-element.93), channel_id=1, source_target_pairs={{0,8},{8,0},{16,24},{24,16},{1,9},{9,1},{17,25},{25,17},{2,10},{10... | collective-permute-start | bytes 393224 | tf_op jit(solution)/shard_map/ppermute | solution.py:245
  160.0 6.4 %collective-permute-start.31 = (bf16[2,256,128]{2,1,0:T(8,128)(2,1)S(1)}, bf16[2,256,128]{2,1,0:T(8,128)(2,1)S(1)}, u32[]{:S(2)}, u32[]{:S(2)}) collective-permute-start(bf16[2,256,128]{2,1,0:T(8,128)(2,1)S(1)} %get-tuple-element.94), channel_id=1, source_target_pairs={{0,16},{8,24},{16,0},{24,8},{1,17},{9,25},{17,1},{25,9},{2,18},{10... | collective-permute-start | bytes 393224 | tf_op jit(solution)/shard_map/ppermute | solution.py:245
  161.1 7.2 %collective-permute-start.32 = (bf16[2,256,128]{2,1,0:T(8,128)(2,1)S(1)}, bf16[2,256,128]{2,1,0:T(8,128)(2,1)S(1)}, u32[]{:S(2)}, u32[]{:S(2)}) collective-permute-start(bf16[2,256,128]{2,1,0:T(8,128)(2,1)S(1)} %get-tuple-element.95), channel_id=1, source_target_pairs={{0,24},{8,16},{16,8},{24,0},{1,25},{9,17},{17,9},{25,1},{2,26},{10... | collective-permute-start | bytes 393224 | tf_op jit(solution)/shard_map/ppermute | solution.py:245

commit v7 on v5

--- a/solution.py
+++ b/solution.py
@@ -273,6 +273,10 @@
     return requests, source
 
 
+def after(x, *others):
+    return lax.optimization_barrier((x, *others))[0]
+
+
 def per_device(queries, key_states, value_states, block_lists, out_grad):
     shard_index = lax.axis_index("ctx")
     shard_count = lax.axis_size("ctx")
@@ -309,7 +313,8 @@
         "pick",
     )
     far = [[send(picked[r - 1], "ctx", shard_count, r) for r in range(1, shard_count)]]
-    far += [[swap(x)] for x in picked[shard_count - 1 :]]
+    for x in picked[shard_count - 1 :]:
+        far.append([swap(after(x, *far[-1]))])
     earlier, nears, backs = [], [], []
     for h in range(head_count):
         last = h == head_count - 1
@@ -321,13 +326,13 @@
         if last:
             backs.append([send_back(x, "ctx", shard_count, r) for r, x in enumerate(far_grad, 1)])
         else:
-            backs.append([swap(far_grad[0])])
+            backs.append([swap(after(far_grad[0], *far[h + 1]))])
     done = []
     for h in range(head_count):
         sums = call(
             functools.partial(gather_sum_kernel, heads=heads, shard_count=shard_count),
             [place, asked],
-            [nears[h], *backs[h]],
+            [after(nears[h], nears[-1], *done[-1:]), *backs[h]],
             [bf16(2, quarter, HEAD_DIM)] * heads,
             [pltpu.VMEM((2, blocks_here, BLK, HEAD_DIM), jnp.float32)],
             "gather_sum",

time: 142 us -> 136 us (0.958)
  the two profiles are of different devices: /device:TPU:0 before, /device:TPU:17 now
where the time goes in v7:
time: 136 us; the launch traced here: 135 us
  waiting for transfers between devices  41.6 us (31%)
  Pallas kernels  39.8 us (29%)
  starting transfers between devices  31.8 us (23%)
  local copies, waits for them, and re-layouts  11.3 us (8%)
  blocking collectives  8.64 us (6%)
    pallas_call x2, Pallas kernels, attend(): pl.pallas_call(functools.partial(attend_kernel, heads=len(own), fars=len(...  31.5 us
    ppermute x13, waiting for transfers between devices, send_back(): lax.ppermute(x, axis, [(i, origin(i, r, count)) for i in range(count)])  23.3 us
    ppermute x10, waiting for transfers between devices, send(): lax.ppermute(x, axis, [(i, partner(i, r, count)) for i in range(count)])  18.1 us
    ppermute x13, starting transfers between devices, send_back(): lax.ppermute(x, axis, [(i, origin(i, r, count)) for i in range(count)])  11.7 us
    unnamed x37, local copies, waits for them, and re-layouts  11.1 us
    all_to_all x2, starting transfers between devices, swap(): return lax.all_to_all(x, 'ctx', split_axis=0, concat_axis=0, tiled=True)  10.3 us
    ppermute x10, starting transfers between devices, send(): lax.ppermute(x, axis, [(i, partner(i, r, count)) for i in range(count)])  9.83 us
    all_to_all x1, blocking collectives, swap(): return lax.all_to_all(x, 'ctx', split_axis=0, concat_axis=0, tiled=True)  8.64 us
  transfers between devices with their start and end apart: 25, of which 14 were waited for; matrix products, arithmetic and copies ran while one was open for 1% of the time, Pallas kernels for 24%

profile of v7, /device:TPU:17, one launch (start us, length us, event | category | flops | bytes accessed | tf_op | source)
XLA Modules:
  0.0 135.2 jit_solution(2676094144264380285)
XLA Ops:
  1.2 3.2 %split.1 = (bf16[2,2,256,128]{3,2,1,0:T(8,128)(2,1)}, bf16[2,2,256,128]{3,2,1,0:T(8,128)(2,1)}, bf16[2,2,256,128]{3,2,1,0:T(8,128)(2,1)}, bf16[2,2,256,128]{3,2,1,0:T(8,128)(2,1)}) custom-call(s32[2]{0:T(128)} %pad_add_fusion.place, bf16[256,1024]{1,0:T(8,128)(2,1)} %k_ref.1, bf16[256,1024]{1,0:T(8,128)(2,1)} %v_ref.1), custom_call_target="tpu_custom_call" | custom-call | tf_op jit(solution)/shard_map/split/pallas_call | solution.py:198
  4.4 0.7 collective-permute-start
  5.2 1.2 collective-permute-start.1
  6.9 0.8 copy.14
  8.2 8.6 %all_to_all.21 = s32[8,1,128]{2,1,0:T(1,128)S(1)} all-to-all(s32[8,1,128]{2,1,0:T(1,128)S(1)} %bitcast.9), channel_id=1, replica_groups=mesh['head'=4,'ctx'=8] {'ctx'}, dimensions={0} | all-to-all | bytes 8192 | tf_op jit(solution)/shard_map/all_to_all | solution.py:257
  16.9 2.2 %collective-permute-done.2.refs_3_ = bf16[2,2,256,128]{3,2,1,0:T(8,128)(2,1)S(1)} collective-permute-done((bf16[2,2,256,128]{3,2,1,0:T(8,128)(2,1)}, bf16[2,2,256,128]{3,2,1,0:T(8,128)(2,1)S(1)}, u32[]{:S(2)}, u32[]{:S(2)}) %collective-permute-start.2) | collective-permute-done | bytes 262176 | tf_op jit(solution)/shard_map/ppermute | solution.py:249
  19.0 1.0 copy-done.2
  20.7 1.8 %pick.1 = (bf16[2,3,64,128]{3,2,1,0:T(8,128)(2,1)S(1)}, bf16[2,3,64,128]{3,2,1,0:T(8,128)(2,1)S(1)}, bf16[2,3,64,128]{3,2,1,0:T(8,128)(2,1)S(1)}, bf16[2,3,64,12...) custom-call(s32[2]{0:T(128)S(1)} %copy-done.8, ...), custom_call_target="tpu_custom_call" | custom-call | tf_op jit(solution)/shard_map/pick/pallas_call | solution.py:198
  22.5 1.2 collective-permute-start.3
  23.7 1.3 collective-permute-start.4
  25.2 3.2 %collective-permute-start.7 = (bf16[2,3,64,128]{3,2,1,0:T(8,128)(2,1)S(1)}, bf16[2,3,64,128]{3,2,1,0:T(8,128)(2,1)S(1)}, u32[]{:S(2)}, u32[]{:S(2)}) collective-permute-start(bf16[2,3,64,128]{3,2,1,0:T(8,128)(2,1)S(1)} %get-tuple-element.53), channel_id=1, source_target_pairs={{0,5},{1,4},{2,7},{3,6},{4,1},{5,0},{6,3},{7,2},{8,13},{9,12},{10,... | collective-permute-start | bytes 294920 | tf_op jit(solution)/shard_map/ppermute | solution.py:249
  28.6 1.2 collective-permute-start.9
  29.9 1.7 %collective-permute-done.6.refs_7_ = bf16[2,3,64,128]{3,2,1,0:T(8,128)(2,1)S(1)} collective-permute-done((bf16[2,3,64,128]{3,2,1,0:T(8,128)(2,1)S(1)}, bf16[2,3,64,128]{3,2,1,0:T(8,128)(2,1)S(1)}, u32[]{:S(2)}, u32[]{:S(2)}) %collective-permute-start.6) | collective-permute-done | bytes 98336 | tf_op jit(solution)/shard_map/ppermute | solution.py:249
  31.6 7.7 %collective-permute-done.7.refs_8_ = bf16[2,3,64,128]{3,2,1,0:T(8,128)(2,1)S(1)} collective-permute-done((bf16[2,3,64,128]{3,2,1,0:T(8,128)(2,1)S(1)}, bf16[2,3,64,128]{3,2,1,0:T(8,128)(2,1)S(1)}, u32[]{:S(2)}, u32[]{:S(2)}) %collective-permute-start.7) | collective-permute-done | bytes 98336 | tf_op jit(solution)/shard_map/ppermute | solution.py:249
  39.4 2.7 %collective-permute-done.8.refs_9_ = bf16[2,3,64,128]{3,2,1,0:T(8,128)(2,1)S(1)} collective-permute-done((bf16[2,3,64,128]{3,2,1,0:T(8,128)(2,1)S(1)}, bf16[2,3,64,128]{3,2,1,0:T(8,128)(2,1)S(1)}, u32[]{:S(2)}, u32[]{:S(2)}) %collective-permute-start.8) | collective-permute-done | bytes 98336 | tf_op jit(solution)/shard_map/ppermute | solution.py:249
  42.1 3.7 %collective-permute-done.9.refs_10_ = bf16[2,3,64,128]{3,2,1,0:T(8,128)(2,1)S(1)} collective-permute-done((bf16[2,3,64,128]{3,2,1,0:T(8,128)(2,1)S(1)}, bf16[2,3,64,128]{3,2,1,0:T(8,128)(2,1)S(1)}, u32[]{:S(2)}, u32[]{:S(2)}) %collective-permute-start.9) | collective-permute-done | bytes 98336 | tf_op jit(solution)/shard_map/ppermute | solution.py:249
  45.8 3.6 %all-to-all-start.1 = ((bf16[8,2,3,64,128]{4,3,2,1,0:T(8,128)(2,1)}), bf16[8,2,3,64,128]{4,3,2,1,0:T(8,128)(2,1)S(1)}, u32[]{:S(2)}, u32[]{:S(2)}) async-start(bf16[8,2,3,64,128]{4,3,2,1,0:T(8,128)(2,1)} %get-tuple-element.56), calls=%async_computation.1 | async-start | bytes 1572864 | tf_op jit(solution)/shard_map/all_to_all | solution.py:257
  49.7 0.9 copy-done.17
  50.6 15.9 %attend.2 = (bf16[1024,1024]{1,0:T(8,128)(2,1)}, bf16[1024,1024]{1,0:T(8,128)(2,1)}, f32[2,16,64,128]{3,2,1,0:T(8,128)S(1)}, bf16[8,2,3,64,128]{4,3,2,1,0:T(8,128)(2,1)}) custom-call(s32[2]{0:T(128)S(1)} %copy-done.9, s32[128]{0:T(128)S(1)} %compare_select_fusion.source, bf16[1024,1024]{1,0:T(8,128)(2,1)} %q_ref.3, bf16[1024,1024]{1,0:T(8,128)(2,1)} %g_ref.3, ...), custom_call_target="tpu_custom_call" | custom-call | flops 3221225472 | bytes 20971520 | tf_op jit(solution)/shard_map/attend/pallas_call | solution.py:221
  66.7 0.9 copy-done
  67.6 6.6 %all-to-all-start.2 = ((bf16[8,2,3,64,128]{4,3,2,1,0:T(8,128)(2,1)}), bf16[8,2,3,64,128]{4,3,2,1,0:T(8,128)(2,1)S(1)}, u32[]{:S(2)}, u32[]{:S(2)}) async-start(bf16[8,2,3,64,128]{4,3,2,1,0:T(8,128)(2,1)} %get-tuple-element.65), calls=%async_computation.2 | async-start | bytes 1572864 | tf_op jit(solution)/shard_map/all_to_all | solution.py:257
  74.3 1.1 copy-done.1
  75.4 0.9 copy-done.5
  76.4 0.9 copy-done.7
  77.3 15.6 %attend.3 = (bf16[1024,1024]{1,0:T(8,128)(2,1)}, bf16[1024,1024]{1,0:T(8,128)(2,1)}, f32[2,16,64,128]{3,2,1,0:T(8,128)S(1)}, bf16[2,3,64,128]{3,2,1,0:T(8,128)(2...) custom-call(s32[2]{0:T(128)S(1)} %copy-done.9, ...), custom_call_target="tpu_custom_call", output_to_operand_aliasing={{0}: (9, {}), {1}: (10, {})} | custom-call | flops 3221225472 | bytes 20971520 | tf_op jit(solution)/shard_map/attend/pallas_call | solution.py:221
  92.9 0.6 copy-done.10
  93.6 0.6 copy-done.11
  94.2 0.6 copy-done.12
  94.8 0.6 copy-done.13
  95.5 0.6 copy-done.14
  96.1 0.6 copy-done.15
  96.8 0.9 gather_sum.2
  97.7 2.2 %collective-permute-start.12 = (bf16[2,256,128]{2,1,0:T(8,128)(2,1)S(1)}, bf16[2,256,128]{2,1,0:T(8,128)(2,1)S(1)}, u32[]{:S(2)}, u32[]{:S(2)}) collective-permute-start(bf16[2,256,128]{2,1,0:T(8,128)(2,1)S(1)} %get-tuple-element.69), channel_id=1, source_target_pairs={{0,24},{8,16},{16,8},{24,0},{1,25},{9,17},{17,9},{25,1},{2,26},{10... | collective-permute-start | bytes 393224 | tf_op jit(solution)/shard_map/ppermute | solution.py:253
  99.9 1.2 collective-permute-start.13
  101.1 1.2 collective-permute-start.14
  102.5 2.3 %collective-permute-done.13.refs_0_ = bf16[2,3,64,128]{3,2,1,0:T(8,128)(2,1)S(1)} collective-permute-done((bf16[2,3,64,128]{3,2,1,0:T(8,128)(2,1)}, bf16[2,3,64,128]{3,2,1,0:T(8,128)(2,1)S(1)}, u32[]{:S(2)}, u32[]{:S(2)}) %collective-permute-start.13) | collective-permute-done | bytes 98336 | tf_op jit(solution)/shard_map/ppermute | solution.py:253
  104.8 1.2 collective-permute-start.17
  106.0 2.1 %collective-permute-start.18 = (bf16[2,3,64,128]{3,2,1,0:T(8,128)(2,1)}, bf16[2,3,64,128]{3,2,1,0:T(8,128)(2,1)S(1)}, u32[]{:S(2)}, u32[]{:S(2)}) collective-permute-start(bf16[2,3,64,128]{3,2,1,0:T(8,128)(2,1)} %copy-done.10), channel_id=1, source_target_pairs={{0,6},{1,7},{2,4},{3,5},{4,2},{5,3},{6,0},{7,1},{8,14},{9,15},{10,... | collective-permute-start | bytes 294920 | tf_op jit(solution)/shard_map/ppermute | solution.py:253
  108.2 0.8 collective-permute-done.15.refs_2_
  110.2 6.6 %collective-permute-done.17.refs_4_ = bf16[2,3,64,128]{3,2,1,0:T(8,128)(2,1)S(1)} collective-permute-done((bf16[2,3,64,128]{3,2,1,0:T(8,128)(2,1)}, bf16[2,3,64,128]{3,2,1,0:T(8,128)(2,1)S(1)}, u32[]{:S(2)}, u32[]{:S(2)}) %collective-permute-start.17) | collective-permute-done | bytes 98336 | tf_op jit(solution)/shard_map/ppermute | solution.py:253
  116.8 4.2 %collective-permute-done.18.refs_5_ = bf16[2,3,64,128]{3,2,1,0:T(8,128)(2,1)S(1)} collective-permute-done((bf16[2,3,64,128]{3,2,1,0:T(8,128)(2,1)}, bf16[2,3,64,128]{3,2,1,0:T(8,128)(2,1)S(1)}, u32[]{:S(2)}, u32[]{:S(2)}) %collective-permute-start.18) | collective-permute-done | bytes 98336 | tf_op jit(solution)/shard_map/ppermute | solution.py:253
  121.0 2.4 %collective-permute-done.19.refs_6_ = bf16[2,3,64,128]{3,2,1,0:T(8,128)(2,1)S(1)} collective-permute-done((bf16[2,3,64,128]{3,2,1,0:T(8,128)(2,1)S(1)}, bf16[2,3,64,128]{3,2,1,0:T(8,128)(2,1)S(1)}, u32[]{:S(2)}, u32[]{:S(2)}) %collective-permute-start.19) | collective-permute-done | bytes 98336 | tf_op jit(solution)/shard_map/ppermute | solution.py:253
  123.4 0.9 gather_sum.3
  124.3 1.2 collective-permute-start.20
  125.8 1.4 %collective-permute-start.22 = (bf16[2,256,128]{2,1,0:T(8,128)(2,1)S(1)}, bf16[2,256,128]{2,1,0:T(8,128)(2,1)S(1)}, u32[]{:S(2)}, u32[]{:S(2)}) collective-permute-start(bf16[2,256,128]{2,1,0:T(8,128)(2,1)S(1)} %get-tuple-element.81), channel_id=1, source_target_pairs={{0,24},{8,16},{16,8},{24,0},{1,25},{9,17},{17,9},{25,1},{2,26},{10... | collective-permute-start | bytes 393224 | tf_op jit(solution)/shard_map/ppermute | solution.py:253
  127.2 3.4 %collective-permute-done.21.refs_6_ = bf16[2,256,128]{2,1,0:T(8,128)(2,1)S(1)} collective-permute-done((bf16[2,256,128]{2,1,0:T(8,128)(2,1)S(1)}, bf16[2,256,128]{2,1,0:T(8,128)(2,1)S(1)}, u32[]{:S(2)}, u32[]{:S(2)}) %collective-permute-start.21) | collective-permute-done | bytes 131104 | tf_op jit(solution)/shard_map/ppermute | solution.py:253
  130.6 3.0 %collective-permute-done.22.refs_7_ = bf16[2,256,128]{2,1,0:T(8,128)(2,1)S(1)} collective-permute-done((bf16[2,256,128]{2,1,0:T(8,128)(2,1)S(1)}, bf16[2,256,128]{2,1,0:T(8,128)(2,1)S(1)}, u32[]{:S(2)}, u32[]{:S(2)}) %collective-permute-start.22) | collective-permute-done | bytes 131104 | tf_op jit(solution)/shard_map/ppermute | solution.py:253
  133.5 1.6 %join.1 = (bf16[256,1024]{1,0:T(8,128)(2,1)}, bf16[256,1024]{1,0:T(8,128)(2,1)}) custom-call(s32[2]{0:T(128)S(1)} %copy-done.9, bf16[2,256,128]{2,1,0:T(8,128)(2,1)S(1)} %get-tuple-element.66.refs_0_, bf16[2,256,128]{2,1,0:T(8,128)(2,1)S(1)} %collective-permute-done.10.refs_1_, bf16[2,256,128]{2,1,0:T(8,128)(2,1)S(1)} %collective-permute-done.11.refs_2_, ...), custom_call_target="tpu_custom_call" | custom-call | tf_op jit(solution)/shard_map/join/pallas_call | solution.py:198
  (60 shorter events, 5.0 us)
Async XLA Ops:
  1.2 48.4 %copy-start.9 = (s32[2]{0:T(128)S(1)}, s32[2]{0:T(128)}, u32[]{:S(2)}) copy-start(s32[2]{0:T(128)} %pad_add_fusion.place) | copy-start | bytes 28
  4.4 12.5 %collective-permute-start = (bf16[2,2,256,128]{3,2,1,0:T(8,128)(2,1)}, bf16[2,2,256,128]{3,2,1,0:T(8,128)(2,1)S(1)}, u32[]{:S(2)}, u32[]{:S(2)}) collective-permute-start(bf16[2,2,256,128]{3,2,1,0:T(8,128)(2,1)} %get-tuple-element.45), channel_id=1, source_target_pairs={{0,8},{8,0},{16,24},{24,16},{1,9},{9,1},{17,25},{25,17},{2,10},{10... | collective-permute-start | bytes 786440 | tf_op jit(solution)/shard_map/ppermute | solution.py:249
  5.2 11.7 %collective-permute-start.1 = (bf16[2,2,256,128]{3,2,1,0:T(8,128)(2,1)}, bf16[2,2,256,128]{3,2,1,0:T(8,128)(2,1)S(1)}, u32[]{:S(2)}, u32[]{:S(2)}) collective-permute-start(bf16[2,2,256,128]{3,2,1,0:T(8,128)(2,1)} %get-tuple-element.46), channel_id=1, source_target_pairs={{0,16},{8,24},{16,0},{24,8},{1,17},{9,25},{17,1},{25,9},{2,18},{10... | collective-permute-start | bytes 786440 | tf_op jit(solution)/shard_map/ppermute | solution.py:249
  6.4 12.6 %collective-permute-start.2 = (bf16[2,2,256,128]{3,2,1,0:T(8,128)(2,1)}, bf16[2,2,256,128]{3,2,1,0:T(8,128)(2,1)S(1)}, u32[]{:S(2)}, u32[]{:S(2)}) collective-permute-start(bf16[2,2,256,128]{3,2,1,0:T(8,128)(2,1)} %get-tuple-element.47), channel_id=1, source_target_pairs={{0,24},{8,16},{16,8},{24,0},{1,25},{9,17},{17,9},{25,1},{2,26},{10... | collective-permute-start | bytes 786440 | tf_op jit(solution)/shard_map/ppermute | solution.py:249
  16.9 49.6 %copy-start.4 = (bf16[2,2,256,128]{3,2,1,0:T(8,128)(2,1)}, bf16[2,2,256,128]{3,2,1,0:T(8,128)(2,1)S(1)}, u32[]{:S(2)}) copy-start(bf16[2,2,256,128]{3,2,1,0:T(8,128)(2,1)S(1)} %collective-permute-done.1.refs_2_) | copy-start | bytes 786436
  19.0 47.4 %copy-start.6 = (bf16[2,2,256,128]{3,2,1,0:T(8,128)(2,1)}, bf16[2,2,256,128]{3,2,1,0:T(8,128)(2,1)S(1)}, u32[]{:S(2)}) copy-start(bf16[2,2,256,128]{3,2,1,0:T(8,128)(2,1)S(1)} %collective-permute-done.2.refs_3_) | copy-start | bytes 786436
  19.0 1.0 copy-start.2
  20.1 0.6 copy-start.8
  20.7 28.9 %copy-start.3 = (bf16[2,2,256,128]{3,2,1,0:T(8,128)(2,1)S(1)}, bf16[2,2,256,128]{3,2,1,0:T(8,128)(2,1)}, u32[]{:S(2)}) copy-start(bf16[2,2,256,128]{3,2,1,0:T(8,128)(2,1)} %get-tuple-element.44.refs_0_) | copy-start | bytes 786436
  22.5 6.0 %collective-permute-start.3 = (bf16[2,3,64,128]{3,2,1,0:T(8,128)(2,1)S(1)}, bf16[2,3,64,128]{3,2,1,0:T(8,128)(2,1)S(1)}, u32[]{:S(2)}, u32[]{:S(2)}) collective-permute-start(bf16[2,3,64,128]{3,2,1,0:T(8,128)(2,1)S(1)} %get-tuple-element.49), channel_id=1, source_target_pairs={{0,1},{1,0},{2,3},{3,2},{4,5},{5,4},{6,7},{7,6},{8,9},{9,8},{10,11... | collective-permute-start | bytes 294920 | tf_op jit(solution)/shard_map/ppermute | solution.py:249
  23.7 4.9 %collective-permute-start.4 = (bf16[2,3,64,128]{3,2,1,0:T(8,128)(2,1)S(1)}, bf16[2,3,64,128]{3,2,1,0:T(8,128)(2,1)S(1)}, u32[]{:S(2)}, u32[]{:S(2)}) collective-permute-start(bf16[2,3,64,128]{3,2,1,0:T(8,128)(2,1)S(1)} %get-tuple-element.50), channel_id=1, source_target_pairs={{0,2},{1,3},{2,0},{3,1},{4,6},{5,7},{6,4},{7,5},{8,10},{9,11},{10,... | collective-permute-start | bytes 294920 | tf_op jit(solution)/shard_map/ppermute | solution.py:249
  25.0 4.9 %collective-permute-start.5 = (bf16[2,3,64,128]{3,2,1,0:T(8,128)(2,1)S(1)}, bf16[2,3,64,128]{3,2,1,0:T(8,128)(2,1)S(1)}, u32[]{:S(2)}, u32[]{:S(2)}) collective-permute-start(bf16[2,3,64,128]{3,2,1,0:T(8,128)(2,1)S(1)} %get-tuple-element.51), channel_id=1, source_target_pairs={{0,3},{1,2},{2,1},{3,0},{4,7},{5,6},{6,5},{7,4},{8,11},{9,10},{10,... | collective-permute-start | bytes 294920 | tf_op jit(solution)/shard_map/ppermute | solution.py:249
  25.1 6.5 %collective-permute-start.6 = (bf16[2,3,64,128]{3,2,1,0:T(8,128)(2,1)S(1)}, bf16[2,3,64,128]{3,2,1,0:T(8,128)(2,1)S(1)}, u32[]{:S(2)}, u32[]{:S(2)}) collective-permute-start(bf16[2,3,64,128]{3,2,1,0:T(8,128)(2,1)S(1)} %get-tuple-element.52), channel_id=1, source_target_pairs={{0,4},{1,5},{2,6},{3,7},{4,0},{5,1},{6,2},{7,3},{8,12},{9,13},{10,... | collective-permute-start | bytes 294920 | tf_op jit(solution)/shard_map/ppermute | solution.py:249
  25.2 14.2 %collective-permute-start.7 = (bf16[2,3,64,128]{3,2,1,0:T(8,128)(2,1)S(1)}, bf16[2,3,64,128]{3,2,1,0:T(8,128)(2,1)S(1)}, u32[]{:S(2)}, u32[]{:S(2)}) collective-permute-start(bf16[2,3,64,128]{3,2,1,0:T(8,128)(2,1)S(1)} %get-tuple-element.53), channel_id=1, source_target_pairs={{0,5},{1,4},{2,7},{3,6},{4,1},{5,0},{6,3},{7,2},{8,13},{9,12},{10,... | collective-permute-start | bytes 294920 | tf_op jit(solution)/shard_map/ppermute | solution.py:249
  28.4 13.7 %collective-permute-start.8 = (bf16[2,3,64,128]{3,2,1,0:T(8,128)(2,1)S(1)}, bf16[2,3,64,128]{3,2,1,0:T(8,128)(2,1)S(1)}, u32[]{:S(2)}, u32[]{:S(2)}) collective-permute-start(bf16[2,3,64,128]{3,2,1,0:T(8,128)(2,1)S(1)} %get-tuple-element.54), channel_id=1, source_target_pairs={{0,6},{1,7},{2,4},{3,5},{4,2},{5,3},{6,0},{7,1},{8,14},{9,15},{10,... | collective-permute-start | bytes 294920 | tf_op jit(solution)/shard_map/ppermute | solution.py:249
  28.6 17.2 %collective-permute-start.9 = (bf16[2,3,64,128]{3,2,1,0:T(8,128)(2,1)S(1)}, bf16[2,3,64,128]{3,2,1,0:T(8,128)(2,1)S(1)}, u32[]{:S(2)}, u32[]{:S(2)}) collective-permute-start(bf16[2,3,64,128]{3,2,1,0:T(8,128)(2,1)S(1)} %get-tuple-element.55), channel_id=1, source_target_pairs={{0,7},{1,6},{2,5},{3,4},{4,3},{5,2},{6,1},{7,0},{8,15},{9,14},{10,... | collective-permute-start | bytes 294920 | tf_op jit(solution)/shard_map/ppermute | solution.py:249
  45.8 3.8 %copy-start.16 = (bf16[2,3,64,128]{3,2,1,0:T(8,128)(2,1)}, bf16[2,3,64,128]{3,2,1,0:T(8,128)(2,1)S(1)}, u32[]{:S(2)}) copy-start(bf16[2,3,64,128]{3,2,1,0:T(8,128)(2,1)S(1)} %collective-permute-done.9.refs_10_) | copy-start | bytes 294916
  45.8 20.9 %all-to-all-start.1 = ((bf16[8,2,3,64,128]{4,3,2,1,0:T(8,128)(2,1)}), bf16[8,2,3,64,128]{4,3,2,1,0:T(8,128)(2,1)S(1)}, u32[]{:S(2)}, u32[]{:S(2)}) async-start(bf16[8,2,3,64,128]{4,3,2,1,0:T(8,128)(2,1)} %get-tuple-element.56), calls=%async_computation.1 | async-start | bytes 1572864 | tf_op jit(solution)/shard_map/all_to_all | solution.py:257
  49.7 0.9 copy-start.17
  66.7 0.9 copy-start
  67.6 29.1 %all-to-all-start.2 = ((bf16[8,2,3,64,128]{4,3,2,1,0:T(8,128)(2,1)}), bf16[8,2,3,64,128]{4,3,2,1,0:T(8,128)(2,1)S(1)}, u32[]{:S(2)}, u32[]{:S(2)}) async-start(bf16[8,2,3,64,128]{4,3,2,1,0:T(8,128)(2,1)} %get-tuple-element.65), calls=%async_computation.2 | async-start | bytes 1572864 | tf_op jit(solution)/shard_map/all_to_all | solution.py:257
  74.3 1.1 copy-start.1
  75.4 0.9 copy-start.5
  76.4 0.9 copy-start.7
  92.9 0.6 copy-start.10
  93.6 0.6 copy-start.11
  94.2 0.6 copy-start.12
  94.8 0.7 copy-start.13
  95.5 0.6 copy-start.14
  96.1 0.6 copy-start.15
  97.7 10.5 %collective-permute-start.12 = (bf16[2,256,128]{2,1,0:T(8,128)(2,1)S(1)}, bf16[2,256,128]{2,1,0:T(8,128)(2,1)S(1)}, u32[]{:S(2)}, u32[]{:S(2)}) collective-permute-start(bf16[2,256,128]{2,1,0:T(8,128)(2,1)S(1)} %get-tuple-element.69), channel_id=1, source_target_pairs={{0,24},{8,16},{16,8},{24,0},{1,25},{9,17},{17,9},{25,1},{2,26},{10... | collective-permute-start | bytes 393224 | tf_op jit(solution)/shard_map/ppermute | solution.py:253
  99.9 4.9 %collective-permute-start.13 = (bf16[2,3,64,128]{3,2,1,0:T(8,128)(2,1)}, bf16[2,3,64,128]{3,2,1,0:T(8,128)(2,1)S(1)}, u32[]{:S(2)}, u32[]{:S(2)}) collective-permute-start(bf16[2,3,64,128]{3,2,1,0:T(8,128)(2,1)} %copy-done.15), channel_id=1, source_target_pairs={{0,1},{1,0},{2,3},{3,2},{4,5},{5,4},{6,7},{7,6},{8,9},{9,8},{10,11... | collective-permute-start | bytes 294920 | tf_op jit(solution)/shard_map/ppermute | solution.py:253
  101.1 4.9 %collective-permute-start.14 = (bf16[2,3,64,128]{3,2,1,0:T(8,128)(2,1)}, bf16[2,3,64,128]{3,2,1,0:T(8,128)(2,1)S(1)}, u32[]{:S(2)}, u32[]{:S(2)}) collective-permute-start(bf16[2,3,64,128]{3,2,1,0:T(8,128)(2,1)} %copy-done.14), channel_id=1, source_target_pairs={{0,2},{1,3},{2,0},{3,1},{4,6},{5,7},{6,4},{7,5},{8,10},{9,11},{10,... | collective-permute-start | bytes 294920 | tf_op jit(solution)/shard_map/ppermute | solution.py:253
  102.3 6.7 %collective-permute-start.15 = (bf16[2,3,64,128]{3,2,1,0:T(8,128)(2,1)}, bf16[2,3,64,128]{3,2,1,0:T(8,128)(2,1)S(1)}, u32[]{:S(2)}, u32[]{:S(2)}) collective-permute-start(bf16[2,3,64,128]{3,2,1,0:T(8,128)(2,1)} %copy-done.13), channel_id=1, source_target_pairs={{0,3},{1,2},{2,1},{3,0},{4,7},{5,6},{6,5},{7,4},{8,11},{9,10},{10,... | collective-permute-start | bytes 294920 | tf_op jit(solution)/shard_map/ppermute | solution.py:253
  102.5 7.6 %collective-permute-start.16 = (bf16[2,3,64,128]{3,2,1,0:T(8,128)(2,1)}, bf16[2,3,64,128]{3,2,1,0:T(8,128)(2,1)S(1)}, u32[]{:S(2)}, u32[]{:S(2)}) collective-permute-start(bf16[2,3,64,128]{3,2,1,0:T(8,128)(2,1)} %copy-done.12), channel_id=1, source_target_pairs={{0,4},{1,5},{2,6},{3,7},{4,0},{5,1},{6,2},{7,3},{8,12},{9,13},{10,... | collective-permute-start | bytes 294920 | tf_op jit(solution)/shard_map/ppermute | solution.py:253
  104.8 11.9 %collective-permute-start.17 = (bf16[2,3,64,128]{3,2,1,0:T(8,128)(2,1)}, bf16[2,3,64,128]{3,2,1,0:T(8,128)(2,1)S(1)}, u32[]{:S(2)}, u32[]{:S(2)}) collective-permute-start(bf16[2,3,64,128]{3,2,1,0:T(8,128)(2,1)} %copy-done.11), channel_id=1, source_target_pairs={{0,5},{1,4},{2,7},{3,6},{4,1},{5,0},{6,3},{7,2},{8,13},{9,12},{10,... | collective-permute-start | bytes 294920 | tf_op jit(solution)/shard_map/ppermute | solution.py:253
  106.0 15.0 %collective-permute-start.18 = (bf16[2,3,64,128]{3,2,1,0:T(8,128)(2,1)}, bf16[2,3,64,128]{3,2,1,0:T(8,128)(2,1)S(1)}, u32[]{:S(2)}, u32[]{:S(2)}) collective-permute-start(bf16[2,3,64,128]{3,2,1,0:T(8,128)(2,1)} %copy-done.10), channel_id=1, source_target_pairs={{0,6},{1,7},{2,4},{3,5},{4,2},{5,3},{6,0},{7,1},{8,14},{9,15},{10,... | collective-permute-start | bytes 294920 | tf_op jit(solution)/shard_map/ppermute | solution.py:253
  108.1 15.3 %collective-permute-start.19 = (bf16[2,3,64,128]{3,2,1,0:T(8,128)(2,1)S(1)}, bf16[2,3,64,128]{3,2,1,0:T(8,128)(2,1)S(1)}, u32[]{:S(2)}, u32[]{:S(2)}) collective-permute-start(bf16[2,3,64,128]{3,2,1,0:T(8,128)(2,1)S(1)} %get-tuple-element.77), channel_id=1, source_target_pairs={{0,7},{1,6},{2,5},{3,4},{4,3},{5,2},{6,1},{7,0},{8,15},{9,14},{10,... | collective-permute-start | bytes 294920 | tf_op jit(solution)/shard_map/ppermute | solution.py:253
  109.0 18.2 %collective-permute-start.10 = (bf16[2,256,128]{2,1,0:T(8,128)(2,1)S(1)}, bf16[2,256,128]{2,1,0:T(8,128)(2,1)S(1)}, u32[]{:S(2)}, u32[]{:S(2)}) collective-permute-start(bf16[2,256,128]{2,1,0:T(8,128)(2,1)S(1)} %get-tuple-element.67), channel_id=1, source_target_pairs={{0,8},{8,0},{16,24},{24,16},{1,9},{9,1},{17,25},{25,17},{2,10},{10... | collective-permute-start | bytes 393224 | tf_op jit(solution)/shard_map/ppermute | solution.py:253
  110.2 17.0 %collective-permute-start.11 = (bf16[2,256,128]{2,1,0:T(8,128)(2,1)S(1)}, bf16[2,256,128]{2,1,0:T(8,128)(2,1)S(1)}, u32[]{:S(2)}, u32[]{:S(2)}) collective-permute-start(bf16[2,256,128]{2,1,0:T(8,128)(2,1)S(1)} %get-tuple-element.68), channel_id=1, source_target_pairs={{0,16},{8,24},{16,0},{24,8},{1,17},{9,25},{17,1},{25,9},{2,18},{10... | collective-permute-start | bytes 393224 | tf_op jit(solution)/shard_map/ppermute | solution.py:253
  124.3 2.9 %collective-permute-start.20 = (bf16[2,256,128]{2,1,0:T(8,128)(2,1)S(1)}, bf16[2,256,128]{2,1,0:T(8,128)(2,1)S(1)}, u32[]{:S(2)}, u32[]{:S(2)}) collective-permute-start(bf16[2,256,128]{2,1,0:T(8,128)(2,1)S(1)} %get-tuple-element.79), channel_id=1, source_target_pairs={{0,8},{8,0},{16,24},{24,16},{1,9},{9,1},{17,25},{25,17},{2,10},{10... | collective-permute-start | bytes 393224 | tf_op jit(solution)/shard_map/ppermute | solution.py:253
  125.5 5.1 %collective-permute-start.21 = (bf16[2,256,128]{2,1,0:T(8,128)(2,1)S(1)}, bf16[2,256,128]{2,1,0:T(8,128)(2,1)S(1)}, u32[]{:S(2)}, u32[]{:S(2)}) collective-permute-start(bf16[2,256,128]{2,1,0:T(8,128)(2,1)S(1)} %get-tuple-element.80), channel_id=1, source_target_pairs={{0,16},{8,24},{16,0},{24,8},{1,17},{9,25},{17,1},{25,9},{2,18},{10... | collective-permute-start | bytes 393224 | tf_op jit(solution)/shard_map/ppermute | solution.py:253
  125.8 7.8 %collective-permute-start.22 = (bf16[2,256,128]{2,1,0:T(8,128)(2,1)S(1)}, bf16[2,256,128]{2,1,0:T(8,128)(2,1)S(1)}, u32[]{:S(2)}, u32[]{:S(2)}) collective-permute-start(bf16[2,256,128]{2,1,0:T(8,128)(2,1)S(1)} %get-tuple-element.81), channel_id=1, source_target_pairs={{0,24},{8,16},{16,8},{24,0},{1,25},{9,17},{17,9},{25,1},{2,26},{10... | collective-permute-start | bytes 393224 | tf_op jit(solution)/shard_map/ppermute | solution.py:253

commit v8 on v7

--- a/solution.py
+++ b/solution.py
@@ -85,40 +85,37 @@
                 table[kv, first + j] = own[r][h, kv, j * BLK : (j + 1) * BLK, :]
 
 
-def parts_of(refs, place, at, shard_count):
-    if len(refs) == 1 and len(refs[0].shape) == 5:
-        return [(refs[0].at[c], c) for c in range(shard_count)]
-    return [(ref, at(place[0], r, shard_count)) for r, ref in enumerate(refs, 1)]
-
-
-def pick_kernel(place, asked, *refs, heads, head_count, shard_count):
+def pick(table, asked, there, out):
+    for s in range(CAP):
+        block = asked[there, s]
+        for kv in range(2):
+            out[kv, s] = table[kv, block]
+
+
+def pick_kernel(place, asked, *refs, heads, shard_count):
     own, outs, table = refs[:heads], refs[heads:-1], refs[-1]
-    for h in range(head_count):
-        fill_table(place, own, h, table)
-        steps = shard_count - 1
-        mine = outs[:steps] if h == 0 else outs[steps + h - 1 : steps + h]
-        for out, c in parts_of(mine, place, partner, shard_count):
-            for s in range(CAP):
-                block = asked[c, s]
-                for kv in range(2):
-                    out[kv, s] = table[kv, block]
-
-
-def attend_kernel(place, source, q_ref, g_ref, *refs, heads, fars, outs, head, shard_count):
-    own, far = refs[:heads], refs[heads : heads + fars]
+    fill_table(place, own, 0, table)
+    for r, out in enumerate(outs, 1):
+        pick(table, asked, partner(place[0], r, shard_count), out)
+
+
+def attend_kernel(place, source, asked, q_ref, g_ref, *refs, heads, head, last, shard_count):
+    steps = shard_count - 1
+    own, far = refs[:heads], refs[heads : heads + steps]
     table, total = refs[-2:]
-    far_out = refs[-2 - outs : -2]
-    o_ref, dq_ref, near_out = refs[-5 - outs : -2 - outs]
+    outs = refs[-2 - steps : -2]
+    o_ref, dq_ref, near_out = refs[-5 - steps : -2 - steps]
     step = pl.program_id(0)
     blocks_here = near_out.shape[1]
 
     @pl.when(step == 0)
     def _():
         fill_table(place, own, head, table)
-        for part, c in parts_of(far, place, origin, shard_count):
+        for r, part in enumerate(far, 1):
+            first = blocks_here + origin(place[0], r, shard_count) * CAP
             for kv in range(2):
                 for s in range(CAP):
-                    table[kv, blocks_here + c * CAP + s] = part[kv, s]
+                    table[kv, first + s] = part[kv, s]
         total[...] = jnp.zeros_like(total)
 
     key_row = lax.broadcasted_iota(jnp.int32, (BLK, GROUP * BLK), 0)
@@ -162,20 +159,39 @@
     def _():
         for kv, factor in ((0, SCALE), (1, 1.0)):
             near_out[kv] = total[kv, :blocks_here] * factor
-            for out, c in parts_of(far_out, place, origin, shard_count):
-                for s in range(CAP):
-                    out[kv, s] = (total[kv, blocks_here + c * CAP + s] * factor).astype(jnp.bfloat16)
+        if not last:
+            fill_table(place, own, head + 1, table)
+        for r, out in enumerate(outs, 1):
+            there = partner(place[0], r, shard_count)
+
+            @pl.when(there < place[0])
+            def _():
+                for kv, factor in ((0, SCALE), (1, 1.0)):
+                    for s in range(CAP):
+                        out[kv, s] = (total[kv, blocks_here + there * CAP + s] * factor).astype(jnp.bfloat16)
+
+            @pl.when(there > place[0])
+            def _():
+                if last:
+                    out[...] = jnp.zeros_like(out)
+                else:
+                    pick(table, asked, there, out)
 
 
 def gather_sum_kernel(place, asked, near, *refs, heads, shard_count):
     back, outs, total = refs[: -heads - 1], refs[-heads - 1 : -1], refs[-1]
     per_quarter = outs[0].shape[1] // BLK
     total[...] = near[...]
-    for part, c in parts_of(back, place, partner, shard_count):
-        for s in range(CAP):
-            block = asked[c, s]
-            for kv in range(2):
-                total[kv, block] += part[kv, s].astype(jnp.float32)
+    for r, part in enumerate(back, 1):
+        there = origin(place[0], r, shard_count)
+
+        @pl.when(there > place[0])
+        def _():
+            for s in range(CAP):
+                block = asked[there, s]
+                for kv in range(2):
+                    total[kv, block] += part[kv, s].astype(jnp.float32)
+
     for r in range(heads):
         first = origin(place[1], r, heads) * per_quarter
         for kv in range(2):
@@ -210,20 +226,21 @@
     )(*scalars, *arrays)
 
 
-def attend(place, source, queries, out_grad, own, far, out_shapes, head, earlier, shard_count):
+def attend(place, source, asked, queries, out_grad, own, far, head, last, earlier, shard_count):
     tokens_here, width = queries.shape
     blocks_here = tokens_here // BLK
     slots = blocks_here + shard_count * CAP
     tile = pl.BlockSpec((STEP_BLOCKS * BLK, GROUP * HEAD_DIM), lambda i, *_: (i, head))
     near_shape = (2, blocks_here, BLK, HEAD_DIM)
     arrays = [*own, *far]
-    first = 4 + len(arrays)
+    first = 5 + len(arrays)
+    out_shapes = [bf16(2, CAP, BLK, HEAD_DIM)] * (shard_count - 1)
     return pl.pallas_call(
         functools.partial(
-            attend_kernel, heads=len(own), fars=len(far), outs=len(out_shapes), head=head, shard_count=shard_count
+            attend_kernel, heads=len(own), head=head, last=last, shard_count=shard_count
         ),
         grid_spec=pltpu.PrefetchScalarGridSpec(
-            num_scalar_prefetch=2,
+            num_scalar_prefetch=3,
             grid=(blocks_here // STEP_BLOCKS,),
             in_specs=[tile, tile] + [whole(x.shape) for x in arrays] + [ANYWHERE] * len(earlier),
             out_specs=[tile, tile, whole(near_shape)] + [whole(x.shape) for x in out_shapes],
@@ -242,7 +259,7 @@
             transcendentals=blocks_here * LIST * BLK * GROUP * BLK,
         ),
         name="attend",
-    )(place, source, queries, out_grad, *arrays, *earlier)
+    )(place, source, asked, queries, out_grad, *arrays, *earlier)
 
 
 def send(x, axis, count, r):
@@ -251,10 +268,6 @@
 
 def send_back(x, axis, count, r):
     return lax.ppermute(x, axis, [(i, origin(i, r, count)) for i in range(count)])
-
-
-def swap(x):
-    return lax.all_to_all(x, "ctx", split_axis=0, concat_axis=0, tiled=True)
 
 
 def requests_of(flat_ids, blocks_here, shard_index, shard_count):
@@ -299,34 +312,28 @@
     own = [pieces[0]] + [send(pieces[r], "head", heads, r) for r in range(1, heads)]
 
     requests, source = requests_of(block_lists.reshape(-1), blocks_here, shard_index, shard_count)
-    asked = swap(requests)
-
-    one = (2, CAP, BLK, HEAD_DIM)
-    by_step = [bf16(*one)] * (shard_count - 1)
-    at_once = [bf16(shard_count, *one)]
+    asked = lax.all_to_all(requests, "ctx", split_axis=0, concat_axis=0, tiled=True)
+
+    def exchange(arrays):
+        return [send(x, "ctx", shard_count, r) for r, x in enumerate(arrays, 1)]
+
     picked = call(
-        functools.partial(pick_kernel, heads=heads, head_count=head_count, shard_count=shard_count),
+        functools.partial(pick_kernel, heads=heads, shard_count=shard_count),
         [place, asked],
         own,
-        by_step + at_once * (head_count - 1),
+        [bf16(2, CAP, BLK, HEAD_DIM)] * (shard_count - 1),
         [pltpu.VMEM((2, blocks_here, BLK, HEAD_DIM), jnp.bfloat16)],
         "pick",
     )
-    far = [[send(picked[r - 1], "ctx", shard_count, r) for r in range(1, shard_count)]]
-    for x in picked[shard_count - 1 :]:
-        far.append([swap(after(x, *far[-1]))])
-    earlier, nears, backs = [], [], []
+    come, earlier, nears, backs = exchange(picked), [], [], []
     for h in range(head_count):
-        last = h == head_count - 1
-        attended, query_grad, near, *far_grad = attend(
-            place, source, queries, out_grad, own, far[h], by_step if last else at_once, h, earlier, shard_count
+        attended, query_grad, near, *go = attend(
+            place, source, asked, queries, out_grad, own, come, h, h == head_count - 1, earlier, shard_count
         )
         earlier = [attended, query_grad]
         nears.append(near)
-        if last:
-            backs.append([send_back(x, "ctx", shard_count, r) for r, x in enumerate(far_grad, 1)])
-        else:
-            backs.append([swap(after(far_grad[0], *far[h + 1]))])
+        come = exchange(go)
+        backs.append(come)
     done = []
     for h in range(head_count):
         sums = call(

time: 136 us -> 144 us (1.059)
  the two profiles are of different devices: /device:TPU:17 before, /device:TPU:0 now
where the time goes in v8:
time: 144 us; the launch traced here: 142 us
  starting transfers between devices  51.7 us (36%)
  waiting for transfers between devices  45.9 us (32%)
  Pallas kernels  38.7 us (27%)
  local copies, waits for them, and re-layouts  2.57 us (2%)
  other arithmetic  1.88 us (1%)
    ppermute x24, starting transfers between devices, send(): lax.ppermute(x, axis, [(i, partner(i, r, count)) for i in range(count)])  40.7 us
    ppermute x24, waiting for transfers between devices, send(): lax.ppermute(x, axis, [(i, partner(i, r, count)) for i in range(count)])  38.7 us
    pallas_call x2, Pallas kernels, attend(): pl.pallas_call(functools.partial(attend_kernel, heads=len(own), head=head...  31.6 us
    all_to_all x1, starting transfers between devices, per_device(): lax.all_to_all(requests, 'ctx', split_axis=0, concat_axis=0, tiled=True)  7.28 us
    pallas_call x5, Pallas kernels, call(): pl.pallas_call(kernel, grid_spec=pltpu.PrefetchScalarGridSpec(num_scalar_...  7.16 us
    ppermute x6, waiting for transfers between devices, send_back(): lax.ppermute(x, axis, [(i, origin(i, r, count)) for i in range(count)])  6.4 us
    ppermute x6, starting transfers between devices, send_back(): lax.ppermute(x, axis, [(i, origin(i, r, count)) for i in range(count)])  3.66 us
  transfers between devices with their start and end apart: 31, of which 9 were waited for; matrix products, arithmetic and copies ran while one was open for 1% of the time, Pallas kernels for 3%

profile of v8, /device:TPU:0, one launch (start us, length us, event | category | flops | bytes accessed | tf_op | source)
XLA Modules:
  0.0 141.5 jit_solution(12687168017121771991)
XLA Ops:
  0.7 0.8 copy.14
  1.5 0.1 fusion
  1.9 0.7 select_reduce_fusion
  2.6 7.3 %all-to-all-start = ((s32[8,1,128]{2,1,0:T(1,128)}), s32[8,1,128]{2,1,0:T(1,128)S(1)}, u32[]{:S(2)}, u32[]{:S(2)}) async-start(s32[8,1,128]{2,1,0:T(1,128)} %bitcast.3), calls=%async_computation | async-start | bytes 8192 | tf_op jit(solution)/shard_map/all_to_all | solution.py:315
  9.9 0.7 pad_add_fusion.place
  10.6 3.0 %split.1 = (bf16[2,2,256,128]{3,2,1,0:T(8,128)(2,1)}, bf16[2,2,256,128]{3,2,1,0:T(8,128)(2,1)}, bf16[2,2,256,128]{3,2,1,0:T(8,128)(2,1)}, bf16[2,2,256,128]{3,2,1,0:T(8,128)(2,1)}) custom-call(s32[2]{0:T(128)} %pad_add_fusion.place, bf16[256,1024]{1,0:T(8,128)(2,1)} %k_ref.1, bf16[256,1024]{1,0:T(8,128)(2,1)} %v_ref.1), custom_call_target="tpu_custom_call" | custom-call | tf_op jit(solution)/shard_map/split/pallas_call | solution.py:214
  13.7 1.6 %collective-permute-start.1 = (bf16[2,2,256,128]{3,2,1,0:T(8,128)(2,1)}, bf16[2,2,256,128]{3,2,1,0:T(8,128)(2,1)S(1)}, u32[]{:S(2)}, u32[]{:S(2)}) collective-permute-start(bf16[2,2,256,128]{3,2,1,0:T(8,128)(2,1)} %get-tuple-element.49), channel_id=1, source_target_pairs={{0,16},{8,24},{16,0},{24,8},{1,17},{9,25},{17,1},{25,9},{2,18},{10... | collective-permute-start | bytes 786440 | tf_op jit(solution)/shard_map/ppermute | solution.py:266
  15.2 0.3 collective-permute-start.2
  15.5 0.8 all-to-all-done
  16.3 6.7 %collective-permute-done.1.refs_2_ = bf16[2,2,256,128]{3,2,1,0:T(8,128)(2,1)S(1)} collective-permute-done((bf16[2,2,256,128]{3,2,1,0:T(8,128)(2,1)}, bf16[2,2,256,128]{3,2,1,0:T(8,128)(2,1)S(1)}, u32[]{:S(2)}, u32[]{:S(2)}) %collective-permute-start.1) | collective-permute-done | bytes 262176 | tf_op jit(solution)/shard_map/ppermute | solution.py:266
  23.1 4.7 %collective-permute-done.2.refs_3_ = bf16[2,2,256,128]{3,2,1,0:T(8,128)(2,1)S(1)} collective-permute-done((bf16[2,2,256,128]{3,2,1,0:T(8,128)(2,1)}, bf16[2,2,256,128]{3,2,1,0:T(8,128)(2,1)S(1)}, u32[]{:S(2)}, u32[]{:S(2)}) %collective-permute-start.2) | collective-permute-done | bytes 262176 | tf_op jit(solution)/shard_map/ppermute | solution.py:266
  27.8 0.9 copy-done
  28.7 0.7 copy-done.1
  29.4 0.7 pick.1
  30.1 2.1 %collective-permute-start.3 = (bf16[2,3,64,128]{3,2,1,0:T(8,128)(2,1)S(1)}, bf16[2,3,64,128]{3,2,1,0:T(8,128)(2,1)S(1)}, u32[]{:S(2)}, u32[]{:S(2)}) collective-permute-start(bf16[2,3,64,128]{3,2,1,0:T(8,128)(2,1)S(1)} %get-tuple-element.51), channel_id=1, source_target_pairs={{0,1},{1,0},{2,3},{3,2},{4,5},{5,4},{6,7},{7,6},{8,9},{9,8},{10,11... | collective-permute-start | bytes 294920 | tf_op jit(solution)/shard_map/ppermute | solution.py:266
  32.2 1.5 %collective-permute-start.4 = (bf16[2,3,64,128]{3,2,1,0:T(8,128)(2,1)S(1)}, bf16[2,3,64,128]{3,2,1,0:T(8,128)(2,1)S(1)}, u32[]{:S(2)}, u32[]{:S(2)}) collective-permute-start(bf16[2,3,64,128]{3,2,1,0:T(8,128)(2,1)S(1)} %get-tuple-element.52), channel_id=1, source_target_pairs={{0,2},{1,3},{2,0},{3,1},{4,6},{5,7},{6,4},{7,5},{8,10},{9,11},{10,... | collective-permute-start | bytes 294920 | tf_op jit(solution)/shard_map/ppermute | solution.py:266
  33.6 0.2 convert_reduce_fusion.1
  33.8 0.1 collective-permute-start.5
  34.0 2.8 %collective-permute-start.6 = (bf16[2,3,64,128]{3,2,1,0:T(8,128)(2,1)S(1)}, bf16[2,3,64,128]{3,2,1,0:T(8,128)(2,1)S(1)}, u32[]{:S(2)}, u32[]{:S(2)}) collective-permute-start(bf16[2,3,64,128]{3,2,1,0:T(8,128)(2,1)S(1)} %get-tuple-element.54), channel_id=1, source_target_pairs={{0,4},{1,5},{2,6},{3,7},{4,0},{5,1},{6,2},{7,3},{8,12},{9,13},{10,... | collective-permute-start | bytes 294920 | tf_op jit(solution)/shard_map/ppermute | solution.py:266
  36.8 1.5 %collective-permute-start.7 = (bf16[2,3,64,128]{3,2,1,0:T(8,128)(2,1)S(1)}, bf16[2,3,64,128]{3,2,1,0:T(8,128)(2,1)S(1)}, u32[]{:S(2)}, u32[]{:S(2)}) collective-permute-start(bf16[2,3,64,128]{3,2,1,0:T(8,128)(2,1)S(1)} %get-tuple-element.55), channel_id=1, source_target_pairs={{0,5},{1,4},{2,7},{3,6},{4,1},{5,0},{6,3},{7,2},{8,13},{9,12},{10,... | collective-permute-start | bytes 294920 | tf_op jit(solution)/shard_map/ppermute | solution.py:266
  38.3 3.3 %collective-permute-start.8 = (bf16[2,3,64,128]{3,2,1,0:T(8,128)(2,1)S(1)}, bf16[2,3,64,128]{3,2,1,0:T(8,128)(2,1)S(1)}, u32[]{:S(2)}, u32[]{:S(2)}) collective-permute-start(bf16[2,3,64,128]{3,2,1,0:T(8,128)(2,1)S(1)} %get-tuple-element.56), channel_id=1, source_target_pairs={{0,6},{1,7},{2,4},{3,5},{4,2},{5,3},{6,0},{7,1},{8,14},{9,15},{10,... | collective-permute-start | bytes 294920 | tf_op jit(solution)/shard_map/ppermute | solution.py:266
  41.7 10.6 %collective-permute-done.7.refs_8_ = bf16[2,3,64,128]{3,2,1,0:T(8,128)(2,1)S(1)} collective-permute-done((bf16[2,3,64,128]{3,2,1,0:T(8,128)(2,1)S(1)}, bf16[2,3,64,128]{3,2,1,0:T(8,128)(2,1)S(1)}, u32[]{:S(2)}, u32[]{:S(2)}) %collective-permute-start.7) | collective-permute-done | bytes 98336 | tf_op jit(solution)/shard_map/ppermute | solution.py:266
  52.2 15.8 %attend.2 = (bf16[1024,1024]{1,0:T(8,128)(2,1)}, bf16[1024,1024]{1,0:T(8,128)(2,1)}, f32[2,16,64,128]{3,2,1,0:T(8,128)S(1)}, bf16[2,3,64,128]{3,2,1,0:T(8,128)(2...) custom-call(s32[2]{0:T(128)S(1)} %copy-done.1, ...), custom_call_target="tpu_custom_call" | custom-call | flops 3221225472 | bytes 20971520 | tf_op jit(solution)/shard_map/attend/pallas_call | solution.py:238
  68.0 0.7 collective-permute-start.10
  68.7 4.0 %collective-permute-start.11 = (bf16[2,3,64,128]{3,2,1,0:T(8,128)(2,1)S(1)}, bf16[2,3,64,128]{3,2,1,0:T(8,128)(2,1)S(1)}, u32[]{:S(2)}, u32[]{:S(2)}) collective-permute-start(bf16[2,3,64,128]{3,2,1,0:T(8,128)(2,1)S(1)} %get-tuple-element.59), channel_id=1, source_target_pairs={{0,2},{1,3},{2,0},{3,1},{4,6},{5,7},{6,4},{7,5},{8,10},{9,11},{10,... | collective-permute-start | bytes 294920 | tf_op jit(solution)/shard_map/ppermute | solution.py:266
  72.7 0.7 collective-permute-start.12
  73.4 3.4 %collective-permute-start.13 = (bf16[2,3,64,128]{3,2,1,0:T(8,128)(2,1)S(1)}, bf16[2,3,64,128]{3,2,1,0:T(8,128)(2,1)S(1)}, u32[]{:S(2)}, u32[]{:S(2)}) collective-permute-start(bf16[2,3,64,128]{3,2,1,0:T(8,128)(2,1)S(1)} %get-tuple-element.61), channel_id=1, source_target_pairs={{0,4},{1,5},{2,6},{3,7},{4,0},{5,1},{6,2},{7,3},{8,12},{9,13},{10,... | collective-permute-start | bytes 294920 | tf_op jit(solution)/shard_map/ppermute | solution.py:266
  76.8 2.4 %collective-permute-start.15 = (bf16[2,3,64,128]{3,2,1,0:T(8,128)(2,1)S(1)}, bf16[2,3,64,128]{3,2,1,0:T(8,128)(2,1)S(1)}, u32[]{:S(2)}, u32[]{:S(2)}) collective-permute-start(bf16[2,3,64,128]{3,2,1,0:T(8,128)(2,1)S(1)} %get-tuple-element.63), channel_id=1, source_target_pairs={{0,6},{1,7},{2,4},{3,5},{4,2},{5,3},{6,0},{7,1},{8,14},{9,15},{10,... | collective-permute-start | bytes 294920 | tf_op jit(solution)/shard_map/ppermute | solution.py:266
  79.1 2.4 %collective-permute-start.16 = (bf16[2,3,64,128]{3,2,1,0:T(8,128)(2,1)S(1)}, bf16[2,3,64,128]{3,2,1,0:T(8,128)(2,1)S(1)}, u32[]{:S(2)}, u32[]{:S(2)}) collective-permute-start(bf16[2,3,64,128]{3,2,1,0:T(8,128)(2,1)S(1)} %get-tuple-element.64), channel_id=1, source_target_pairs={{0,7},{1,6},{2,5},{3,4},{4,3},{5,2},{6,1},{7,0},{8,15},{9,14},{10,... | collective-permute-start | bytes 294920 | tf_op jit(solution)/shard_map/ppermute | solution.py:266
  81.5 6.6 %collective-permute-done.13.refs_7_.refs_3_ = bf16[2,3,64,128]{3,2,1,0:T(8,128)(2,1)S(1)} collective-permute-done((bf16[2,3,64,128]{3,2,1,0:T(8,128)(2,1)S(1)}, bf16[2,3,64,128]{3,2,1,0:T(8,128)(2,1)S(1)}, u32[]{:S(2)}, u32[]{:S(2)}) %collective-permute-start.13) | collective-permute-done | bytes 98336 | tf_op jit(solution)/shard_map/ppermute | solution.py:266
  88.1 2.6 %collective-permute-done.14.refs_8_.refs_4_ = bf16[2,3,64,128]{3,2,1,0:T(8,128)(2,1)S(1)} collective-permute-done((bf16[2,3,64,128]{3,2,1,0:T(8,128)(2,1)S(1)}, bf16[2,3,64,128]{3,2,1,0:T(8,128)(2,1)S(1)}, u32[]{:S(2)}, u32[]{:S(2)}) %collective-permute-start.14) | collective-permute-done | bytes 98336 | tf_op jit(solution)/shard_map/ppermute | solution.py:266
  90.6 15.8 %attend.3 = (bf16[1024,1024]{1,0:T(8,128)(2,1)}, bf16[1024,1024]{1,0:T(8,128)(2,1)}, f32[2,16,64,128]{3,2,1,0:T(8,128)S(1)}, bf16[2,3,64,128]{3,2,1,0:T(8,128)(2...) custom-call(s32[2]{0:T(128)S(1)} %copy-done.1, ...), custom_call_target="tpu_custom_call", output_to_operand_aliasing={{0}: (16, {}), {1}: (17, {})} | custom-call | flops 3221225472 | bytes 20971520 | tf_op jit(solution)/shard_map/attend/pallas_call | solution.py:238
  106.4 0.9 gather_sum.2
  107.4 1.1 collective-permute-start.20
  108.5 3.6 %collective-permute-start.21 = (bf16[2,3,64,128]{3,2,1,0:T(8,128)(2,1)S(1)}, bf16[2,3,64,128]{3,2,1,0:T(8,128)(2,1)S(1)}, u32[]{:S(2)}, u32[]{:S(2)}) collective-permute-start(bf16[2,3,64,128]{3,2,1,0:T(8,128)(2,1)S(1)} %get-tuple-element.78), channel_id=1, source_target_pairs={{0,2},{1,3},{2,0},{3,1},{4,6},{5,7},{6,4},{7,5},{8,10},{9,11},{10,... | collective-permute-start | bytes 294920 | tf_op jit(solution)/shard_map/ppermute | solution.py:266
  112.1 0.8 collective-permute-start.22
  112.9 2.0 %collective-permute-start.23 = (bf16[2,3,64,128]{3,2,1,0:T(8,128)(2,1)S(1)}, bf16[2,3,64,128]{3,2,1,0:T(8,128)(2,1)S(1)}, u32[]{:S(2)}, u32[]{:S(2)}) collective-permute-start(bf16[2,3,64,128]{3,2,1,0:T(8,128)(2,1)S(1)} %get-tuple-element.80), channel_id=1, source_target_pairs={{0,4},{1,5},{2,6},{3,7},{4,0},{5,1},{6,2},{7,3},{8,12},{9,13},{10,... | collective-permute-start | bytes 294920 | tf_op jit(solution)/shard_map/ppermute | solution.py:266
  115.0 2.4 %collective-permute-start.24 = (bf16[2,3,64,128]{3,2,1,0:T(8,128)(2,1)S(1)}, bf16[2,3,64,128]{3,2,1,0:T(8,128)(2,1)S(1)}, u32[]{:S(2)}, u32[]{:S(2)}) collective-permute-start(bf16[2,3,64,128]{3,2,1,0:T(8,128)(2,1)S(1)} %get-tuple-element.81), channel_id=1, source_target_pairs={{0,5},{1,4},{2,7},{3,6},{4,1},{5,0},{6,3},{7,2},{8,13},{9,12},{10,... | collective-permute-start | bytes 294920 | tf_op jit(solution)/shard_map/ppermute | solution.py:266
  117.4 1.6 %collective-permute-start.25 = (bf16[2,3,64,128]{3,2,1,0:T(8,128)(2,1)S(1)}, bf16[2,3,64,128]{3,2,1,0:T(8,128)(2,1)S(1)}, u32[]{:S(2)}, u32[]{:S(2)}) collective-permute-start(bf16[2,3,64,128]{3,2,1,0:T(8,128)(2,1)S(1)} %get-tuple-element.82), channel_id=1, source_target_pairs={{0,6},{1,7},{2,4},{3,5},{4,2},{5,3},{6,0},{7,1},{8,14},{9,15},{10,... | collective-permute-start | bytes 294920 | tf_op jit(solution)/shard_map/ppermute | solution.py:266
  119.1 2.3 %collective-permute-start.26 = (bf16[2,3,64,128]{3,2,1,0:T(8,128)(2,1)S(1)}, bf16[2,3,64,128]{3,2,1,0:T(8,128)(2,1)S(1)}, u32[]{:S(2)}, u32[]{:S(2)}) collective-permute-start(bf16[2,3,64,128]{3,2,1,0:T(8,128)(2,1)S(1)} %get-tuple-element.83), channel_id=1, source_target_pairs={{0,7},{1,6},{2,5},{3,4},{4,3},{5,2},{6,1},{7,0},{8,15},{9,14},{10,... | collective-permute-start | bytes 294920 | tf_op jit(solution)/shard_map/ppermute | solution.py:266
  121.4 1.7 %collective-permute-start.18 = (bf16[2,256,128]{2,1,0:T(8,128)(2,1)S(1)}, bf16[2,256,128]{2,1,0:T(8,128)(2,1)S(1)}, u32[]{:S(2)}, u32[]{:S(2)}) collective-permute-start(bf16[2,256,128]{2,1,0:T(8,128)(2,1)S(1)} %get-tuple-element.74), channel_id=1, source_target_pairs={{0,16},{8,24},{16,0},{24,8},{1,17},{9,25},{17,1},{25,9},{2,18},{10... | collective-permute-start | bytes 393224 | tf_op jit(solution)/shard_map/ppermute | solution.py:270
  123.1 7.6 %collective-permute-done.24.refs_4_ = bf16[2,3,64,128]{3,2,1,0:T(8,128)(2,1)S(1)} collective-permute-done((bf16[2,3,64,128]{3,2,1,0:T(8,128)(2,1)S(1)}, bf16[2,3,64,128]{3,2,1,0:T(8,128)(2,1)S(1)}, u32[]{:S(2)}, u32[]{:S(2)}) %collective-permute-start.24) | collective-permute-done | bytes 98336 | tf_op jit(solution)/shard_map/ppermute | solution.py:266
  130.6 0.9 gather_sum.3
  131.6 1.1 collective-permute-start.28
  132.7 0.8 collective-permute-start.29
  133.5 4.5 %collective-permute-done.28.refs_6_ = bf16[2,256,128]{2,1,0:T(8,128)(2,1)S(1)} collective-permute-done((bf16[2,256,128]{2,1,0:T(8,128)(2,1)S(1)}, bf16[2,256,128]{2,1,0:T(8,128)(2,1)S(1)}, u32[]{:S(2)}, u32[]{:S(2)}) %collective-permute-start.28) | collective-permute-done | bytes 131104 | tf_op jit(solution)/shard_map/ppermute | solution.py:270
  138.0 1.9 %collective-permute-done.29.refs_7_ = bf16[2,256,128]{2,1,0:T(8,128)(2,1)S(1)} collective-permute-done((bf16[2,256,128]{2,1,0:T(8,128)(2,1)S(1)}, bf16[2,256,128]{2,1,0:T(8,128)(2,1)S(1)}, u32[]{:S(2)}, u32[]{:S(2)}) %collective-permute-start.29) | collective-permute-done | bytes 131104 | tf_op jit(solution)/shard_map/ppermute | solution.py:270
  139.9 1.6 %join.1 = (bf16[256,1024]{1,0:T(8,128)(2,1)}, bf16[256,1024]{1,0:T(8,128)(2,1)}) custom-call(s32[2]{0:T(128)S(1)} %copy-done.1, bf16[2,256,128]{2,1,0:T(8,128)(2,1)S(1)} %get-tuple-element.72.refs_0_, bf16[2,256,128]{2,1,0:T(8,128)(2,1)S(1)} %collective-permute-done.17.refs_1_, bf16[2,256,128]{2,1,0:T(8,128)(2,1)S(1)} %collective-permute-done.18.refs_2_, ...), custom_call_target="tpu_custom_call" | custom-call | tf_op jit(solution)/shard_map/join/pallas_call | solution.py:214
  (39 shorter events, 0.8 us)
Async XLA Ops:
  2.6 13.7 %all-to-all-start = ((s32[8,1,128]{2,1,0:T(1,128)}), s32[8,1,128]{2,1,0:T(1,128)S(1)}, u32[]{:S(2)}, u32[]{:S(2)}) async-start(s32[8,1,128]{2,1,0:T(1,128)} %bitcast.3), calls=%async_computation | async-start | bytes 8192 | tf_op jit(solution)/shard_map/all_to_all | solution.py:315
  13.6 2.8 %collective-permute-start = (bf16[2,2,256,128]{3,2,1,0:T(8,128)(2,1)}, bf16[2,2,256,128]{3,2,1,0:T(8,128)(2,1)S(1)}, u32[]{:S(2)}, u32[]{:S(2)}) collective-permute-start(bf16[2,2,256,128]{3,2,1,0:T(8,128)(2,1)} %get-tuple-element.48), channel_id=1, source_target_pairs={{0,8},{8,0},{16,24},{24,16},{1,9},{9,1},{17,25},{25,17},{2,10},{10... | collective-permute-start | bytes 786440 | tf_op jit(solution)/shard_map/ppermute | solution.py:266
  13.7 9.4 %collective-permute-start.1 = (bf16[2,2,256,128]{3,2,1,0:T(8,128)(2,1)}, bf16[2,2,256,128]{3,2,1,0:T(8,128)(2,1)S(1)}, u32[]{:S(2)}, u32[]{:S(2)}) collective-permute-start(bf16[2,2,256,128]{3,2,1,0:T(8,128)(2,1)} %get-tuple-element.49), channel_id=1, source_target_pairs={{0,16},{8,24},{16,0},{24,8},{1,17},{9,25},{17,1},{25,9},{2,18},{10... | collective-permute-start | bytes 786440 | tf_op jit(solution)/shard_map/ppermute | solution.py:266
  15.2 12.5 %collective-permute-start.2 = (bf16[2,2,256,128]{3,2,1,0:T(8,128)(2,1)}, bf16[2,2,256,128]{3,2,1,0:T(8,128)(2,1)S(1)}, u32[]{:S(2)}, u32[]{:S(2)}) collective-permute-start(bf16[2,2,256,128]{3,2,1,0:T(8,128)(2,1)} %get-tuple-element.50), channel_id=1, source_target_pairs={{0,24},{8,16},{16,8},{24,0},{1,25},{9,17},{17,9},{25,1},{2,26},{10... | collective-permute-start | bytes 786440 | tf_op jit(solution)/shard_map/ppermute | solution.py:266
  27.8 1.0 copy-start
  28.7 0.7 copy-start.1
  30.1 8.2 %collective-permute-start.3 = (bf16[2,3,64,128]{3,2,1,0:T(8,128)(2,1)S(1)}, bf16[2,3,64,128]{3,2,1,0:T(8,128)(2,1)S(1)}, u32[]{:S(2)}, u32[]{:S(2)}) collective-permute-start(bf16[2,3,64,128]{3,2,1,0:T(8,128)(2,1)S(1)} %get-tuple-element.51), channel_id=1, source_target_pairs={{0,1},{1,0},{2,3},{3,2},{4,5},{5,4},{6,7},{7,6},{8,9},{9,8},{10,11... | collective-permute-start | bytes 294920 | tf_op jit(solution)/shard_map/ppermute | solution.py:266
  32.2 9.4 %collective-permute-start.4 = (bf16[2,3,64,128]{3,2,1,0:T(8,128)(2,1)S(1)}, bf16[2,3,64,128]{3,2,1,0:T(8,128)(2,1)S(1)}, u32[]{:S(2)}, u32[]{:S(2)}) collective-permute-start(bf16[2,3,64,128]{3,2,1,0:T(8,128)(2,1)S(1)} %get-tuple-element.52), channel_id=1, source_target_pairs={{0,2},{1,3},{2,0},{3,1},{4,6},{5,7},{6,4},{7,5},{8,10},{9,11},{10,... | collective-permute-start | bytes 294920 | tf_op jit(solution)/shard_map/ppermute | solution.py:266
  33.8 7.8 %collective-permute-start.5 = (bf16[2,3,64,128]{3,2,1,0:T(8,128)(2,1)S(1)}, bf16[2,3,64,128]{3,2,1,0:T(8,128)(2,1)S(1)}, u32[]{:S(2)}, u32[]{:S(2)}) collective-permute-start(bf16[2,3,64,128]{3,2,1,0:T(8,128)(2,1)S(1)} %get-tuple-element.53), channel_id=1, source_target_pairs={{0,3},{1,2},{2,1},{3,0},{4,7},{5,6},{6,5},{7,4},{8,11},{9,10},{10,... | collective-permute-start | bytes 294920 | tf_op jit(solution)/shard_map/ppermute | solution.py:266
  34.0 7.7 %collective-permute-start.6 = (bf16[2,3,64,128]{3,2,1,0:T(8,128)(2,1)S(1)}, bf16[2,3,64,128]{3,2,1,0:T(8,128)(2,1)S(1)}, u32[]{:S(2)}, u32[]{:S(2)}) collective-permute-start(bf16[2,3,64,128]{3,2,1,0:T(8,128)(2,1)S(1)} %get-tuple-element.54), channel_id=1, source_target_pairs={{0,4},{1,5},{2,6},{3,7},{4,0},{5,1},{6,2},{7,3},{8,12},{9,13},{10,... | collective-permute-start | bytes 294920 | tf_op jit(solution)/shard_map/ppermute | solution.py:266
  36.8 15.4 %collective-permute-start.7 = (bf16[2,3,64,128]{3,2,1,0:T(8,128)(2,1)S(1)}, bf16[2,3,64,128]{3,2,1,0:T(8,128)(2,1)S(1)}, u32[]{:S(2)}, u32[]{:S(2)}) collective-permute-start(bf16[2,3,64,128]{3,2,1,0:T(8,128)(2,1)S(1)} %get-tuple-element.55), channel_id=1, source_target_pairs={{0,5},{1,4},{2,7},{3,6},{4,1},{5,0},{6,3},{7,2},{8,13},{9,12},{10,... | collective-permute-start | bytes 294920 | tf_op jit(solution)/shard_map/ppermute | solution.py:266
  38.3 13.9 %collective-permute-start.8 = (bf16[2,3,64,128]{3,2,1,0:T(8,128)(2,1)S(1)}, bf16[2,3,64,128]{3,2,1,0:T(8,128)(2,1)S(1)}, u32[]{:S(2)}, u32[]{:S(2)}) collective-permute-start(bf16[2,3,64,128]{3,2,1,0:T(8,128)(2,1)S(1)} %get-tuple-element.56), channel_id=1, source_target_pairs={{0,6},{1,7},{2,4},{3,5},{4,2},{5,3},{6,0},{7,1},{8,14},{9,15},{10,... | collective-permute-start | bytes 294920 | tf_op jit(solution)/shard_map/ppermute | solution.py:266
  41.5 10.7 %collective-permute-start.9 = (bf16[2,3,64,128]{3,2,1,0:T(8,128)(2,1)S(1)}, bf16[2,3,64,128]{3,2,1,0:T(8,128)(2,1)S(1)}, u32[]{:S(2)}, u32[]{:S(2)}) collective-permute-start(bf16[2,3,64,128]{3,2,1,0:T(8,128)(2,1)S(1)} %get-tuple-element.57), channel_id=1, source_target_pairs={{0,7},{1,6},{2,5},{3,4},{4,3},{5,2},{6,1},{7,0},{8,15},{9,14},{10,... | collective-permute-start | bytes 294920 | tf_op jit(solution)/shard_map/ppermute | solution.py:266
  68.0 8.8 %collective-permute-start.10 = (bf16[2,3,64,128]{3,2,1,0:T(8,128)(2,1)S(1)}, bf16[2,3,64,128]{3,2,1,0:T(8,128)(2,1)S(1)}, u32[]{:S(2)}, u32[]{:S(2)}) collective-permute-start(bf16[2,3,64,128]{3,2,1,0:T(8,128)(2,1)S(1)} %get-tuple-element.58), channel_id=1, source_target_pairs={{0,1},{1,0},{2,3},{3,2},{4,5},{5,4},{6,7},{7,6},{8,9},{9,8},{10,11... | collective-permute-start | bytes 294920 | tf_op jit(solution)/shard_map/ppermute | solution.py:266
  68.7 10.4 %collective-permute-start.11 = (bf16[2,3,64,128]{3,2,1,0:T(8,128)(2,1)S(1)}, bf16[2,3,64,128]{3,2,1,0:T(8,128)(2,1)S(1)}, u32[]{:S(2)}, u32[]{:S(2)}) collective-permute-start(bf16[2,3,64,128]{3,2,1,0:T(8,128)(2,1)S(1)} %get-tuple-element.59), channel_id=1, source_target_pairs={{0,2},{1,3},{2,0},{3,1},{4,6},{5,7},{6,4},{7,5},{8,10},{9,11},{10,... | collective-permute-start | bytes 294920 | tf_op jit(solution)/shard_map/ppermute | solution.py:266
  72.7 8.8 %collective-permute-start.12 = (bf16[2,3,64,128]{3,2,1,0:T(8,128)(2,1)S(1)}, bf16[2,3,64,128]{3,2,1,0:T(8,128)(2,1)S(1)}, u32[]{:S(2)}, u32[]{:S(2)}) collective-permute-start(bf16[2,3,64,128]{3,2,1,0:T(8,128)(2,1)S(1)} %get-tuple-element.60), channel_id=1, source_target_pairs={{0,3},{1,2},{2,1},{3,0},{4,7},{5,6},{6,5},{7,4},{8,11},{9,10},{10,... | collective-permute-start | bytes 294920 | tf_op jit(solution)/shard_map/ppermute | solution.py:266
  73.4 14.7 %collective-permute-start.13 = (bf16[2,3,64,128]{3,2,1,0:T(8,128)(2,1)S(1)}, bf16[2,3,64,128]{3,2,1,0:T(8,128)(2,1)S(1)}, u32[]{:S(2)}, u32[]{:S(2)}) collective-permute-start(bf16[2,3,64,128]{3,2,1,0:T(8,128)(2,1)S(1)} %get-tuple-element.61), channel_id=1, source_target_pairs={{0,4},{1,5},{2,6},{3,7},{4,0},{5,1},{6,2},{7,3},{8,12},{9,13},{10,... | collective-permute-start | bytes 294920 | tf_op jit(solution)/shard_map/ppermute | solution.py:266
  76.8 13.9 %collective-permute-start.14 = (bf16[2,3,64,128]{3,2,1,0:T(8,128)(2,1)S(1)}, bf16[2,3,64,128]{3,2,1,0:T(8,128)(2,1)S(1)}, u32[]{:S(2)}, u32[]{:S(2)}) collective-permute-start(bf16[2,3,64,128]{3,2,1,0:T(8,128)(2,1)S(1)} %get-tuple-element.62), channel_id=1, source_target_pairs={{0,5},{1,4},{2,7},{3,6},{4,1},{5,0},{6,3},{7,2},{8,13},{9,12},{10,... | collective-permute-start | bytes 294920 | tf_op jit(solution)/shard_map/ppermute | solution.py:266
  76.8 13.9 %collective-permute-start.15 = (bf16[2,3,64,128]{3,2,1,0:T(8,128)(2,1)S(1)}, bf16[2,3,64,128]{3,2,1,0:T(8,128)(2,1)S(1)}, u32[]{:S(2)}, u32[]{:S(2)}) collective-permute-start(bf16[2,3,64,128]{3,2,1,0:T(8,128)(2,1)S(1)} %get-tuple-element.63), channel_id=1, source_target_pairs={{0,6},{1,7},{2,4},{3,5},{4,2},{5,3},{6,0},{7,1},{8,14},{9,15},{10,... | collective-permute-start | bytes 294920 | tf_op jit(solution)/shard_map/ppermute | solution.py:266
  79.1 11.5 %collective-permute-start.16 = (bf16[2,3,64,128]{3,2,1,0:T(8,128)(2,1)S(1)}, bf16[2,3,64,128]{3,2,1,0:T(8,128)(2,1)S(1)}, u32[]{:S(2)}, u32[]{:S(2)}) collective-permute-start(bf16[2,3,64,128]{3,2,1,0:T(8,128)(2,1)S(1)} %get-tuple-element.64), channel_id=1, source_target_pairs={{0,7},{1,6},{2,5},{3,4},{4,3},{5,2},{6,1},{7,0},{8,15},{9,14},{10,... | collective-permute-start | bytes 294920 | tf_op jit(solution)/shard_map/ppermute | solution.py:266
  107.3 11.7 %collective-permute-start.19 = (bf16[2,256,128]{2,1,0:T(8,128)(2,1)S(1)}, bf16[2,256,128]{2,1,0:T(8,128)(2,1)S(1)}, u32[]{:S(2)}, u32[]{:S(2)}) collective-permute-start(bf16[2,256,128]{2,1,0:T(8,128)(2,1)S(1)} %get-tuple-element.75), channel_id=1, source_target_pairs={{0,24},{8,16},{16,8},{24,0},{1,25},{9,17},{17,9},{25,1},{2,26},{10... | collective-permute-start | bytes 393224 | tf_op jit(solution)/shard_map/ppermute | solution.py:270
  107.4 7.5 %collective-permute-start.20 = (bf16[2,3,64,128]{3,2,1,0:T(8,128)(2,1)S(1)}, bf16[2,3,64,128]{3,2,1,0:T(8,128)(2,1)S(1)}, u32[]{:S(2)}, u32[]{:S(2)}) collective-permute-start(bf16[2,3,64,128]{3,2,1,0:T(8,128)(2,1)S(1)} %get-tuple-element.77), channel_id=1, source_target_pairs={{0,1},{1,0},{2,3},{3,2},{4,5},{5,4},{6,7},{7,6},{8,9},{9,8},{10,11... | collective-permute-start | bytes 294920 | tf_op jit(solution)/shard_map/ppermute | solution.py:266
  108.5 8.9 %collective-permute-start.21 = (bf16[2,3,64,128]{3,2,1,0:T(8,128)(2,1)S(1)}, bf16[2,3,64,128]{3,2,1,0:T(8,128)(2,1)S(1)}, u32[]{:S(2)}, u32[]{:S(2)}) collective-permute-start(bf16[2,3,64,128]{3,2,1,0:T(8,128)(2,1)S(1)} %get-tuple-element.78), channel_id=1, source_target_pairs={{0,2},{1,3},{2,0},{3,1},{4,6},{5,7},{6,4},{7,5},{8,10},{9,11},{10,... | collective-permute-start | bytes 294920 | tf_op jit(solution)/shard_map/ppermute | solution.py:266
  112.1 9.3 %collective-permute-start.22 = (bf16[2,3,64,128]{3,2,1,0:T(8,128)(2,1)S(1)}, bf16[2,3,64,128]{3,2,1,0:T(8,128)(2,1)S(1)}, u32[]{:S(2)}, u32[]{:S(2)}) collective-permute-start(bf16[2,3,64,128]{3,2,1,0:T(8,128)(2,1)S(1)} %get-tuple-element.79), channel_id=1, source_target_pairs={{0,3},{1,2},{2,1},{3,0},{4,7},{5,6},{6,5},{7,4},{8,11},{9,10},{10,... | collective-permute-start | bytes 294920 | tf_op jit(solution)/shard_map/ppermute | solution.py:266
  112.9 8.5 %collective-permute-start.23 = (bf16[2,3,64,128]{3,2,1,0:T(8,128)(2,1)S(1)}, bf16[2,3,64,128]{3,2,1,0:T(8,128)(2,1)S(1)}, u32[]{:S(2)}, u32[]{:S(2)}) collective-permute-start(bf16[2,3,64,128]{3,2,1,0:T(8,128)(2,1)S(1)} %get-tuple-element.80), channel_id=1, source_target_pairs={{0,4},{1,5},{2,6},{3,7},{4,0},{5,1},{6,2},{7,3},{8,12},{9,13},{10,... | collective-permute-start | bytes 294920 | tf_op jit(solution)/shard_map/ppermute | solution.py:266
  115.0 15.7 %collective-permute-start.24 = (bf16[2,3,64,128]{3,2,1,0:T(8,128)(2,1)S(1)}, bf16[2,3,64,128]{3,2,1,0:T(8,128)(2,1)S(1)}, u32[]{:S(2)}, u32[]{:S(2)}) collective-permute-start(bf16[2,3,64,128]{3,2,1,0:T(8,128)(2,1)S(1)} %get-tuple-element.81), channel_id=1, source_target_pairs={{0,5},{1,4},{2,7},{3,6},{4,1},{5,0},{6,3},{7,2},{8,13},{9,12},{10,... | collective-permute-start | bytes 294920 | tf_op jit(solution)/shard_map/ppermute | solution.py:266
  117.4 13.2 %collective-permute-start.25 = (bf16[2,3,64,128]{3,2,1,0:T(8,128)(2,1)S(1)}, bf16[2,3,64,128]{3,2,1,0:T(8,128)(2,1)S(1)}, u32[]{:S(2)}, u32[]{:S(2)}) collective-permute-start(bf16[2,3,64,128]{3,2,1,0:T(8,128)(2,1)S(1)} %get-tuple-element.82), channel_id=1, source_target_pairs={{0,6},{1,7},{2,4},{3,5},{4,2},{5,3},{6,0},{7,1},{8,14},{9,15},{10,... | collective-permute-start | bytes 294920 | tf_op jit(solution)/shard_map/ppermute | solution.py:266
  119.1 11.6 %collective-permute-start.26 = (bf16[2,3,64,128]{3,2,1,0:T(8,128)(2,1)S(1)}, bf16[2,3,64,128]{3,2,1,0:T(8,128)(2,1)S(1)}, u32[]{:S(2)}, u32[]{:S(2)}) collective-permute-start(bf16[2,3,64,128]{3,2,1,0:T(8,128)(2,1)S(1)} %get-tuple-element.83), channel_id=1, source_target_pairs={{0,7},{1,6},{2,5},{3,4},{4,3},{5,2},{6,1},{7,0},{8,15},{9,14},{10,... | collective-permute-start | bytes 294920 | tf_op jit(solution)/shard_map/ppermute | solution.py:266
  121.4 12.1 %collective-permute-start.17 = (bf16[2,256,128]{2,1,0:T(8,128)(2,1)S(1)}, bf16[2,256,128]{2,1,0:T(8,128)(2,1)S(1)}, u32[]{:S(2)}, u32[]{:S(2)}) collective-permute-start(bf16[2,256,128]{2,1,0:T(8,128)(2,1)S(1)} %get-tuple-element.73), channel_id=1, source_target_pairs={{0,8},{8,0},{16,24},{24,16},{1,9},{9,1},{17,25},{25,17},{2,10},{10... | collective-permute-start | bytes 393224 | tf_op jit(solution)/shard_map/ppermute | solution.py:270
  121.4 12.1 %collective-permute-start.18 = (bf16[2,256,128]{2,1,0:T(8,128)(2,1)S(1)}, bf16[2,256,128]{2,1,0:T(8,128)(2,1)S(1)}, u32[]{:S(2)}, u32[]{:S(2)}) collective-permute-start(bf16[2,256,128]{2,1,0:T(8,128)(2,1)S(1)} %get-tuple-element.74), channel_id=1, source_target_pairs={{0,16},{8,24},{16,0},{24,8},{1,17},{9,25},{17,1},{25,9},{2,18},{10... | collective-permute-start | bytes 393224 | tf_op jit(solution)/shard_map/ppermute | solution.py:270
  131.6 2.0 %collective-permute-start.27 = (bf16[2,256,128]{2,1,0:T(8,128)(2,1)S(1)}, bf16[2,256,128]{2,1,0:T(8,128)(2,1)S(1)}, u32[]{:S(2)}, u32[]{:S(2)}) collective-permute-start(bf16[2,256,128]{2,1,0:T(8,128)(2,1)S(1)} %get-tuple-element.85), channel_id=1, source_target_pairs={{0,8},{8,0},{16,24},{24,16},{1,9},{9,1},{17,25},{25,17},{2,10},{10... | collective-permute-start | bytes 393224 | tf_op jit(solution)/shard_map/ppermute | solution.py:270
  131.6 6.4 %collective-permute-start.28 = (bf16[2,256,128]{2,1,0:T(8,128)(2,1)S(1)}, bf16[2,256,128]{2,1,0:T(8,128)(2,1)S(1)}, u32[]{:S(2)}, u32[]{:S(2)}) collective-permute-start(bf16[2,256,128]{2,1,0:T(8,128)(2,1)S(1)} %get-tuple-element.86), channel_id=1, source_target_pairs={{0,16},{8,24},{16,0},{24,8},{1,17},{9,25},{17,1},{25,9},{2,18},{10... | collective-permute-start | bytes 393224 | tf_op jit(solution)/shard_map/ppermute | solution.py:270
  132.7 7.2 %collective-permute-start.29 = (bf16[2,256,128]{2,1,0:T(8,128)(2,1)S(1)}, bf16[2,256,128]{2,1,0:T(8,128)(2,1)S(1)}, u32[]{:S(2)}, u32[]{:S(2)}) collective-permute-start(bf16[2,256,128]{2,1,0:T(8,128)(2,1)S(1)} %get-tuple-element.87), channel_id=1, source_target_pairs={{0,24},{8,16},{16,8},{24,0},{1,25},{9,17},{17,9},{25,1},{2,26},{10... | collective-permute-start | bytes 393224 | tf_op jit(solution)/shard_map/ppermute | solution.py:270

commit v9 on v8

--- a/solution.py
+++ b/solution.py
@@ -12,7 +12,8 @@
 BLK = 64
 LIST = 8
 CAP = 3
-STEP_BLOCKS = 2
+STEP_BLOCKS = 4
+TOGETHER = 2
 NEG_FILL = -1e30
 SCALE = HEAD_DIM ** (-0.5)
 LOG2E = 1.4426950408889634
@@ -38,6 +39,10 @@
 
 def origin(me, r, count):
     return me ^ r if count & (count - 1) == 0 else (me + count - r) % count
+
+
+def steps_of(count):
+    return [*range(count // 2, count), *range(1, count // 2)] if count > 1 else []
 
 
 def head_columns(place, r, heads, h, head_count):
@@ -95,8 +100,19 @@
 def pick_kernel(place, asked, *refs, heads, shard_count):
     own, outs, table = refs[:heads], refs[heads:-1], refs[-1]
     fill_table(place, own, 0, table)
-    for r, out in enumerate(outs, 1):
+    for r, out in zip(steps_of(shard_count), outs):
         pick(table, asked, partner(place[0], r, shard_count), out)
+
+
+def by_head(ref, b):
+    rows = slice(b * BLK, (b + 1) * BLK)
+    return jnp.concatenate([ref[rows, g * HEAD_DIM : (g + 1) * HEAD_DIM] for g in range(GROUP)], axis=0)
+
+
+def by_row(ref, b, x):
+    rows = slice(b * BLK, (b + 1) * BLK)
+    for g in range(GROUP):
+        ref[rows, g * HEAD_DIM : (g + 1) * HEAD_DIM] = x[g * BLK : (g + 1) * BLK]
 
 
 def attend_kernel(place, source, asked, q_ref, g_ref, *refs, heads, head, last, shard_count):
@@ -111,7 +127,7 @@
     @pl.when(step == 0)
     def _():
         fill_table(place, own, head, table)
-        for r, part in enumerate(far, 1):
+        for r, part in zip(steps_of(shard_count), far):
             first = blocks_here + origin(place[0], r, shard_count) * CAP
             for kv in range(2):
                 for s in range(CAP):
@@ -121,39 +137,41 @@
     key_row = lax.broadcasted_iota(jnp.int32, (BLK, GROUP * BLK), 0)
     query_col = lax.broadcasted_iota(jnp.int32, (BLK, GROUP * BLK), 1) % BLK
     hidden = key_row > query_col
-    for sub in range(STEP_BLOCKS):
-        block = step * STEP_BLOCKS + sub
-        rows = slice(sub * BLK, (sub + 1) * BLK)
-        listed = [source[block * LIST + e] for e in range(LIST)]
-        q = jnp.concatenate([q_ref[rows, g * HEAD_DIM : (g + 1) * HEAD_DIM] for g in range(GROUP)], axis=0)
-        g_out = jnp.concatenate([g_ref[rows, g * HEAD_DIM : (g + 1) * HEAD_DIM] for g in range(GROUP)], axis=0)
-        keys = jnp.concatenate([table[0, at] for at in listed], axis=0)
-        values = jnp.concatenate([table[1, at] for at in listed], axis=0)
-        scores = dot(keys, q, NT)
-        parts = []
-        for e in range(LIST):
-            part = scores[e * BLK : (e + 1) * BLK]
-            mask = hidden if e == 0 else hidden & (listed[e] == block)
-            parts.append(jnp.where(mask, NEG_FILL, part))
-        scores = jnp.concatenate(parts, axis=0)
-        peak = jnp.max(scores, axis=0, keepdims=True)
-        expo = jnp.exp2((scores - peak) * (SCALE * LOG2E))
-        probs = expo * (1.0 / jnp.sum(expo, axis=0, keepdims=True))
-        probs_low = probs.astype(jnp.bfloat16)
-        dprob = dot(values, g_out, NT)
-        delta = jnp.sum(probs * dprob, axis=0, keepdims=True)
-        dscore = (probs * (dprob - delta)).astype(jnp.bfloat16)
-        attended = dot(values, probs_low, TN).T.astype(jnp.bfloat16)
-        dq = (dot(keys, dscore, TN) * SCALE).T.astype(jnp.bfloat16)
-        for g in range(GROUP):
-            cols = slice(g * HEAD_DIM, (g + 1) * HEAD_DIM)
-            o_ref[rows, cols] = attended[g * BLK : (g + 1) * BLK]
-            dq_ref[rows, cols] = dq[g * BLK : (g + 1) * BLK]
-        dk = dot(dscore, q, NN)
-        dv = dot(probs_low, g_out, NN)
-        for e in range(LIST):
-            total[0, listed[e]] += dk[e * BLK : (e + 1) * BLK]
-            total[1, listed[e]] += dv[e * BLK : (e + 1) * BLK]
+    for first in range(0, STEP_BLOCKS, TOGETHER):
+        subs = range(first, first + TOGETHER)
+        listed = {b: [source[(step * STEP_BLOCKS + b) * LIST + e] for e in range(LIST)] for b in subs}
+        q = {b: by_head(q_ref, b) for b in subs}
+        g_out = {b: by_head(g_ref, b) for b in subs}
+        keys = {b: jnp.concatenate([table[0, at] for at in listed[b]], axis=0) for b in subs}
+        values = {b: jnp.concatenate([table[1, at] for at in listed[b]], axis=0) for b in subs}
+        scores = {b: dot(keys[b], q[b], NT) for b in subs}
+        dprob, probs, probs_low, dscore = {}, {}, {}, {}
+        for b in subs:
+            block = step * STEP_BLOCKS + b
+            parts = []
+            for e in range(LIST):
+                mask = hidden if e == 0 else hidden & (listed[b][e] == block)
+                parts.append(jnp.where(mask, NEG_FILL, scores[b][e * BLK : (e + 1) * BLK]))
+            masked = jnp.concatenate(parts, axis=0)
+            dprob[b] = dot(values[b], g_out[b], NT)
+            peak = jnp.max(masked, axis=0, keepdims=True)
+            expo = jnp.exp2((masked - peak) * (SCALE * LOG2E))
+            probs[b] = expo * (1.0 / jnp.sum(expo, axis=0, keepdims=True))
+            probs_low[b] = probs[b].astype(jnp.bfloat16)
+        for b in subs:
+            attended = dot(values[b], probs_low[b], TN).astype(jnp.bfloat16).T
+            by_row(o_ref, b, attended)
+            dv = dot(probs_low[b], g_out[b], NN)
+            delta = jnp.sum(probs[b] * dprob[b], axis=0, keepdims=True)
+            dscore[b] = (probs[b] * (dprob[b] - delta)).astype(jnp.bfloat16)
+            for e in range(LIST):
+                total[1, listed[b][e]] += dv[e * BLK : (e + 1) * BLK]
+        for b in subs:
+            dq = (dot(keys[b], dscore[b], TN) * SCALE).astype(jnp.bfloat16).T
+            by_row(dq_ref, b, dq)
+            dk = dot(dscore[b], q[b], NN)
+            for e in range(LIST):
+                total[0, listed[b][e]] += dk[e * BLK : (e + 1) * BLK]
 
     @pl.when(step == pl.num_programs(0) - 1)
     def _():
@@ -161,7 +179,7 @@
             near_out[kv] = total[kv, :blocks_here] * factor
         if not last:
             fill_table(place, own, head + 1, table)
-        for r, out in enumerate(outs, 1):
+        for r, out in zip(steps_of(shard_count), outs):
             there = partner(place[0], r, shard_count)
 
             @pl.when(there < place[0])
@@ -182,7 +200,7 @@
     back, outs, total = refs[: -heads - 1], refs[-heads - 1 : -1], refs[-1]
     per_quarter = outs[0].shape[1] // BLK
     total[...] = near[...]
-    for r, part in enumerate(back, 1):
+    for r, part in zip(steps_of(shard_count), back):
         there = origin(place[0], r, shard_count)
 
         @pl.when(there > place[0])
@@ -311,11 +329,11 @@
     )
     own = [pieces[0]] + [send(pieces[r], "head", heads, r) for r in range(1, heads)]
 
-    requests, source = requests_of(block_lists.reshape(-1), blocks_here, shard_index, shard_count)
+    requests, source = requests_of(after(block_lists, pieces[0]).reshape(-1), blocks_here, shard_index, shard_count)
     asked = lax.all_to_all(requests, "ctx", split_axis=0, concat_axis=0, tiled=True)
 
     def exchange(arrays):
-        return [send(x, "ctx", shard_count, r) for r, x in enumerate(arrays, 1)]
+        return [send(x, "ctx", shard_count, r) for r, x in zip(steps_of(shard_count), arrays)]
 
     picked = call(
         functools.partial(pick_kernel, heads=heads, shard_count=shard_count),

time: 144 us -> 138 us (0.958); the launches traced: 142 us -> 137 us
  Pallas kernels: 38.7 us -> 32.2 us
  waiting for transfers between devices: 45.9 us -> 50.8 us
  starting transfers between devices: 51.7 us -> 49 us
    pallas_call x2, Pallas kernels: 31.6 us -> 25 us  [attend(): pl.pallas_call(functools.partial(attend_kernel, heads=len(own), head=head...]
    all_to_all x1, waiting for transfers between devices: 0.8 us -> 4.58 us  [per_device(): lax.all_to_all(requests, 'ctx', split_axis=0, concat_axis=0, tiled=True)]
    ppermute x24, starting transfers between devices: 40.7 us -> 37.9 us  [send(): lax.ppermute(x, axis, [(i, partner(i, r, count)) for i in range(count)])]
  transfers between devices with their start and end apart: 31 -> 31, of which waited for: 9 -> 17; matrix products, arithmetic and copies ran while one was open for 1% -> 0% of each run, Pallas kernels for 3% -> 1%
where the time goes in v9:
time: 138 us; the launch traced here: 137 us
  waiting for transfers between devices  50.8 us (37%)
  starting transfers between devices  49 us (36%)
  Pallas kernels  32.2 us (23%)
  local copies, waits for them, and re-layouts  2.57 us (2%)
  other arithmetic  1.88 us (1%)
    ppermute x24, waiting for transfers between devices, send(): lax.ppermute(x, axis, [(i, partner(i, r, count)) for i in range(count)])  39.9 us
    ppermute x24, starting transfers between devices, send(): lax.ppermute(x, axis, [(i, partner(i, r, count)) for i in range(count)])  37.9 us
    pallas_call x2, Pallas kernels, attend(): pl.pallas_call(functools.partial(attend_kernel, heads=len(own), head=head...  25 us
    all_to_all x1, starting transfers between devices, per_device(): lax.all_to_all(requests, 'ctx', split_axis=0, concat_axis=0, tiled=True)  7.28 us
    pallas_call x5, Pallas kernels, call(): pl.pallas_call(kernel, grid_spec=pltpu.PrefetchScalarGridSpec(num_scalar_...  7.16 us
    ppermute x6, waiting for transfers between devices, send_back(): lax.ppermute(x, axis, [(i, origin(i, r, count)) for i in range(count)])  6.4 us
    all_to_all x1, waiting for transfers between devices, per_device(): lax.all_to_all(requests, 'ctx', split_axis=0, concat_axis=0, tiled=True)  4.58 us
    ppermute x6, starting transfers between devices, send_back(): lax.ppermute(x, axis, [(i, origin(i, r, count)) for i in range(count)])  3.78 us
  transfers between devices with their start and end apart: 31, of which 17 were waited for; matrix products, arithmetic and copies ran while one was open for 0% of the time, Pallas kernels for 1%

profile of v9, /device:TPU:0, one launch (start us, length us, event | category | flops | bytes accessed | tf_op | source)
XLA Modules:
  0.0 137.3 jit_solution(10805977084368346363)
XLA Ops:
  0.7 0.7 pad_add_fusion.place
  1.3 3.0 %split.1 = (bf16[2,2,256,128]{3,2,1,0:T(8,128)(2,1)}, bf16[2,2,256,128]{3,2,1,0:T(8,128)(2,1)}, bf16[2,2,256,128]{3,2,1,0:T(8,128)(2,1)}, bf16[2,2,256,128]{3,2,1,0:T(8,128)(2,1)}) custom-call(s32[2]{0:T(128)} %pad_add_fusion.place, bf16[256,1024]{1,0:T(8,128)(2,1)} %k_ref.1, bf16[256,1024]{1,0:T(8,128)(2,1)} %v_ref.1), custom_call_target="tpu_custom_call" | custom-call | tf_op jit(solution)/shard_map/split/pallas_call | solution.py:232
  4.4 0.8 copy.14
  5.6 0.7 select_reduce_fusion
  6.3 7.3 %all-to-all-start = ((s32[8,1,128]{2,1,0:T(1,128)}), s32[8,1,128]{2,1,0:T(1,128)S(1)}, u32[]{:S(2)}, u32[]{:S(2)}) async-start(s32[8,1,128]{2,1,0:T(1,128)} %bitcast.3), calls=%async_computation | async-start | bytes 8192 | tf_op jit(solution)/shard_map/all_to_all | solution.py:333
  13.6 1.6 %collective-permute-start.1 = (bf16[2,2,256,128]{3,2,1,0:T(8,128)(2,1)}, bf16[2,2,256,128]{3,2,1,0:T(8,128)(2,1)S(1)}, u32[]{:S(2)}, u32[]{:S(2)}) collective-permute-start(bf16[2,2,256,128]{3,2,1,0:T(8,128)(2,1)} %get-tuple-element.51), channel_id=1, source_target_pairs={{0,16},{8,24},{16,0},{24,8},{1,17},{9,25},{17,1},{25,9},{2,18},{10... | collective-permute-start | bytes 786440 | tf_op jit(solution)/shard_map/ppermute | solution.py:284
  15.5 4.6 %all-to-all-done = s32[8,1,128]{2,1,0:T(1,128)S(1)} async-done(((s32[8,1,128]{2,1,0:T(1,128)}), s32[8,1,128]{2,1,0:T(1,128)S(1)}, u32[]{:S(2)}, u32[]{:S(2)}) %all-to-all-start) | async-done | bytes 4128 | tf_op jit(solution)/shard_map/all_to_all | solution.py:333
  20.1 2.9 %collective-permute-done.1.refs_2_ = bf16[2,2,256,128]{3,2,1,0:T(8,128)(2,1)S(1)} collective-permute-done((bf16[2,2,256,128]{3,2,1,0:T(8,128)(2,1)}, bf16[2,2,256,128]{3,2,1,0:T(8,128)(2,1)S(1)}, u32[]{:S(2)}, u32[]{:S(2)}) %collective-permute-start.1) | collective-permute-done | bytes 262176 | tf_op jit(solution)/shard_map/ppermute | solution.py:284
  23.0 4.7 %collective-permute-done.2.refs_3_ = bf16[2,2,256,128]{3,2,1,0:T(8,128)(2,1)S(1)} collective-permute-done((bf16[2,2,256,128]{3,2,1,0:T(8,128)(2,1)}, bf16[2,2,256,128]{3,2,1,0:T(8,128)(2,1)S(1)}, u32[]{:S(2)}, u32[]{:S(2)}) %collective-permute-start.2) | collective-permute-done | bytes 262176 | tf_op jit(solution)/shard_map/ppermute | solution.py:284
  27.7 0.9 copy-done
  28.6 0.7 copy-done.1
  29.3 0.7 pick.1
  30.0 3.1 %collective-permute-start.3 = (bf16[2,3,64,128]{3,2,1,0:T(8,128)(2,1)S(1)}, bf16[2,3,64,128]{3,2,1,0:T(8,128)(2,1)S(1)}, u32[]{:S(2)}, u32[]{:S(2)}) collective-permute-start(bf16[2,3,64,128]{3,2,1,0:T(8,128)(2,1)S(1)} %get-tuple-element.53), channel_id=1, source_target_pairs={{0,4},{1,5},{2,6},{3,7},{4,0},{5,1},{6,2},{7,3},{8,12},{9,13},{10,... | collective-permute-start | bytes 294920 | tf_op jit(solution)/shard_map/ppermute | solution.py:284
  33.1 1.5 %collective-permute-start.4 = (bf16[2,3,64,128]{3,2,1,0:T(8,128)(2,1)S(1)}, bf16[2,3,64,128]{3,2,1,0:T(8,128)(2,1)S(1)}, u32[]{:S(2)}, u32[]{:S(2)}) collective-permute-start(bf16[2,3,64,128]{3,2,1,0:T(8,128)(2,1)S(1)} %get-tuple-element.54), channel_id=1, source_target_pairs={{0,5},{1,4},{2,7},{3,6},{4,1},{5,0},{6,3},{7,2},{8,13},{9,12},{10,... | collective-permute-start | bytes 294920 | tf_op jit(solution)/shard_map/ppermute | solution.py:284
  34.7 3.3 %collective-permute-start.5 = (bf16[2,3,64,128]{3,2,1,0:T(8,128)(2,1)S(1)}, bf16[2,3,64,128]{3,2,1,0:T(8,128)(2,1)S(1)}, u32[]{:S(2)}, u32[]{:S(2)}) collective-permute-start(bf16[2,3,64,128]{3,2,1,0:T(8,128)(2,1)S(1)} %get-tuple-element.55), channel_id=1, source_target_pairs={{0,6},{1,7},{2,4},{3,5},{4,2},{5,3},{6,0},{7,1},{8,14},{9,15},{10,... | collective-permute-start | bytes 294920 | tf_op jit(solution)/shard_map/ppermute | solution.py:284
  38.1 1.9 %collective-permute-start.7 = (bf16[2,3,64,128]{3,2,1,0:T(8,128)(2,1)S(1)}, bf16[2,3,64,128]{3,2,1,0:T(8,128)(2,1)S(1)}, u32[]{:S(2)}, u32[]{:S(2)}) collective-permute-start(bf16[2,3,64,128]{3,2,1,0:T(8,128)(2,1)S(1)} %get-tuple-element.57), channel_id=1, source_target_pairs={{0,1},{1,0},{2,3},{3,2},{4,5},{5,4},{6,7},{7,6},{8,9},{9,8},{10,11... | collective-permute-start | bytes 294920 | tf_op jit(solution)/shard_map/ppermute | solution.py:284
  40.1 5.1 %collective-permute-done.3.refs_4_ = bf16[2,3,64,128]{3,2,1,0:T(8,128)(2,1)S(1)} collective-permute-done((bf16[2,3,64,128]{3,2,1,0:T(8,128)(2,1)S(1)}, bf16[2,3,64,128]{3,2,1,0:T(8,128)(2,1)S(1)}, u32[]{:S(2)}, u32[]{:S(2)}) %collective-permute-start.3) | collective-permute-done | bytes 98336 | tf_op jit(solution)/shard_map/ppermute | solution.py:284
  45.1 0.3 collective-permute-start.8
  45.5 3.2 %collective-permute-done.4.refs_5_ = bf16[2,3,64,128]{3,2,1,0:T(8,128)(2,1)S(1)} collective-permute-done((bf16[2,3,64,128]{3,2,1,0:T(8,128)(2,1)S(1)}, bf16[2,3,64,128]{3,2,1,0:T(8,128)(2,1)S(1)}, u32[]{:S(2)}, u32[]{:S(2)}) %collective-permute-start.4) | collective-permute-done | bytes 98336 | tf_op jit(solution)/shard_map/ppermute | solution.py:284
  48.7 1.0 collective-permute-done.8.refs_9_
  49.7 4.5 %collective-permute-done.9.refs_10_ = bf16[2,3,64,128]{3,2,1,0:T(8,128)(2,1)S(1)} collective-permute-done((bf16[2,3,64,128]{3,2,1,0:T(8,128)(2,1)S(1)}, bf16[2,3,64,128]{3,2,1,0:T(8,128)(2,1)S(1)}, u32[]{:S(2)}, u32[]{:S(2)}) %collective-permute-start.9) | collective-permute-done | bytes 98336 | tf_op jit(solution)/shard_map/ppermute | solution.py:284
  54.2 12.5 %attend.2 = (bf16[1024,1024]{1,0:T(8,128)(2,1)}, bf16[1024,1024]{1,0:T(8,128)(2,1)}, f32[2,16,64,128]{3,2,1,0:T(8,128)S(1)}, bf16[2,3,64,128]{3,2,1,0:T(8,128)(2...) custom-call(s32[2]{0:T(128)S(1)} %copy-done.1, ...), custom_call_target="tpu_custom_call" | custom-call | flops 3221225472 | bytes 20971520 | tf_op jit(solution)/shard_map/attend/pallas_call | solution.py:256
  66.7 2.5 %collective-permute-start.10 = (bf16[2,3,64,128]{3,2,1,0:T(8,128)(2,1)S(1)}, bf16[2,3,64,128]{3,2,1,0:T(8,128)(2,1)S(1)}, u32[]{:S(2)}, u32[]{:S(2)}) collective-permute-start(bf16[2,3,64,128]{3,2,1,0:T(8,128)(2,1)S(1)} %get-tuple-element.60), channel_id=1, source_target_pairs={{0,4},{1,5},{2,6},{3,7},{4,0},{5,1},{6,2},{7,3},{8,12},{9,13},{10,... | collective-permute-start | bytes 294920 | tf_op jit(solution)/shard_map/ppermute | solution.py:284
  69.2 3.1 %collective-permute-start.12 = (bf16[2,3,64,128]{3,2,1,0:T(8,128)(2,1)S(1)}, bf16[2,3,64,128]{3,2,1,0:T(8,128)(2,1)S(1)}, u32[]{:S(2)}, u32[]{:S(2)}) collective-permute-start(bf16[2,3,64,128]{3,2,1,0:T(8,128)(2,1)S(1)} %get-tuple-element.62), channel_id=1, source_target_pairs={{0,6},{1,7},{2,4},{3,5},{4,2},{5,3},{6,0},{7,1},{8,14},{9,15},{10,... | collective-permute-start | bytes 294920 | tf_op jit(solution)/shard_map/ppermute | solution.py:284
  72.3 2.0 %collective-permute-start.13 = (bf16[2,3,64,128]{3,2,1,0:T(8,128)(2,1)S(1)}, bf16[2,3,64,128]{3,2,1,0:T(8,128)(2,1)S(1)}, u32[]{:S(2)}, u32[]{:S(2)}) collective-permute-start(bf16[2,3,64,128]{3,2,1,0:T(8,128)(2,1)S(1)} %get-tuple-element.63), channel_id=1, source_target_pairs={{0,7},{1,6},{2,5},{3,4},{4,3},{5,2},{6,1},{7,0},{8,15},{9,14},{10,... | collective-permute-start | bytes 294920 | tf_op jit(solution)/shard_map/ppermute | solution.py:284
  74.5 6.2 %collective-permute-done.10.refs_4_.refs_0_ = bf16[2,3,64,128]{3,2,1,0:T(8,128)(2,1)S(1)} collective-permute-done((bf16[2,3,64,128]{3,2,1,0:T(8,128)(2,1)S(1)}, bf16[2,3,64,128]{3,2,1,0:T(8,128)(2,1)S(1)}, u32[]{:S(2)}, u32[]{:S(2)}) %collective-permute-start.10) | collective-permute-done | bytes 98336 | tf_op jit(solution)/shard_map/ppermute | solution.py:284
  80.9 1.4 %collective-permute-done.11.refs_5_.refs_1_ = bf16[2,3,64,128]{3,2,1,0:T(8,128)(2,1)S(1)} collective-permute-done((bf16[2,3,64,128]{3,2,1,0:T(8,128)(2,1)S(1)}, bf16[2,3,64,128]{3,2,1,0:T(8,128)(2,1)S(1)}, u32[]{:S(2)}, u32[]{:S(2)}) %collective-permute-start.11) | collective-permute-done | bytes 98336 | tf_op jit(solution)/shard_map/ppermute | solution.py:284
  82.7 3.2 %collective-permute-done.15.refs_9_.refs_5_ = bf16[2,3,64,128]{3,2,1,0:T(8,128)(2,1)S(1)} collective-permute-done((bf16[2,3,64,128]{3,2,1,0:T(8,128)(2,1)S(1)}, bf16[2,3,64,128]{3,2,1,0:T(8,128)(2,1)S(1)}, u32[]{:S(2)}, u32[]{:S(2)}) %collective-permute-start.15) | collective-permute-done | bytes 98336 | tf_op jit(solution)/shard_map/ppermute | solution.py:284
  85.9 2.0 %collective-permute-done.16.refs_10_.refs_6_ = bf16[2,3,64,128]{3,2,1,0:T(8,128)(2,1)S(1)} collective-permute-done((bf16[2,3,64,128]{3,2,1,0:T(8,128)(2,1)S(1)}, bf16[2,3,64,128]{3,2,1,0:T(8,128)(2,1)S(1)}, u32[]{:S(2)}, u32[]{:S(2)}) %collective-permute-start.16) | collective-permute-done | bytes 98336 | tf_op jit(solution)/shard_map/ppermute | solution.py:284
  87.9 12.5 %attend.3 = (bf16[1024,1024]{1,0:T(8,128)(2,1)}, bf16[1024,1024]{1,0:T(8,128)(2,1)}, f32[2,16,64,128]{3,2,1,0:T(8,128)S(1)}, bf16[2,3,64,128]{3,2,1,0:T(8,128)(2...) custom-call(s32[2]{0:T(128)S(1)} %copy-done.1, ...), custom_call_target="tpu_custom_call", output_to_operand_aliasing={{0}: (16, {}), {1}: (17, {})} | custom-call | flops 3221225472 | bytes 20971520 | tf_op jit(solution)/shard_map/attend/pallas_call | solution.py:256
  100.4 0.9 gather_sum.2
  101.4 2.0 %collective-permute-start.20 = (bf16[2,3,64,128]{3,2,1,0:T(8,128)(2,1)S(1)}, bf16[2,3,64,128]{3,2,1,0:T(8,128)(2,1)S(1)}, u32[]{:S(2)}, u32[]{:S(2)}) collective-permute-start(bf16[2,3,64,128]{3,2,1,0:T(8,128)(2,1)S(1)} %get-tuple-element.79), channel_id=1, source_target_pairs={{0,4},{1,5},{2,6},{3,7},{4,0},{5,1},{6,2},{7,3},{8,12},{9,13},{10,... | collective-permute-start | bytes 294920 | tf_op jit(solution)/shard_map/ppermute | solution.py:284
  103.4 2.3 %collective-permute-start.21 = (bf16[2,3,64,128]{3,2,1,0:T(8,128)(2,1)S(1)}, bf16[2,3,64,128]{3,2,1,0:T(8,128)(2,1)S(1)}, u32[]{:S(2)}, u32[]{:S(2)}) collective-permute-start(bf16[2,3,64,128]{3,2,1,0:T(8,128)(2,1)S(1)} %get-tuple-element.80), channel_id=1, source_target_pairs={{0,5},{1,4},{2,7},{3,6},{4,1},{5,0},{6,3},{7,2},{8,13},{9,12},{10,... | collective-permute-start | bytes 294920 | tf_op jit(solution)/shard_map/ppermute | solution.py:284
  105.7 2.9 %collective-permute-start.22 = (bf16[2,3,64,128]{3,2,1,0:T(8,128)(2,1)S(1)}, bf16[2,3,64,128]{3,2,1,0:T(8,128)(2,1)S(1)}, u32[]{:S(2)}, u32[]{:S(2)}) collective-permute-start(bf16[2,3,64,128]{3,2,1,0:T(8,128)(2,1)S(1)} %get-tuple-element.81), channel_id=1, source_target_pairs={{0,6},{1,7},{2,4},{3,5},{4,2},{5,3},{6,0},{7,1},{8,14},{9,15},{10,... | collective-permute-start | bytes 294920 | tf_op jit(solution)/shard_map/ppermute | solution.py:284
  108.7 0.4 collective-permute-start.23
  109.1 0.7 collective-permute-done.20.refs_0_
  109.8 8.4 %collective-permute-start.24 = (bf16[2,3,64,128]{3,2,1,0:T(8,128)(2,1)S(1)}, bf16[2,3,64,128]{3,2,1,0:T(8,128)(2,1)S(1)}, u32[]{:S(2)}, u32[]{:S(2)}) collective-permute-start(bf16[2,3,64,128]{3,2,1,0:T(8,128)(2,1)S(1)} %get-tuple-element.83), channel_id=1, source_target_pairs={{0,1},{1,0},{2,3},{3,2},{4,5},{5,4},{6,7},{7,6},{8,9},{9,8},{10,11... | collective-permute-start | bytes 294920 | tf_op jit(solution)/shard_map/ppermute | solution.py:284
  118.2 1.6 %collective-permute-done.21.refs_1_ = bf16[2,3,64,128]{3,2,1,0:T(8,128)(2,1)S(1)} collective-permute-done((bf16[2,3,64,128]{3,2,1,0:T(8,128)(2,1)S(1)}, bf16[2,3,64,128]{3,2,1,0:T(8,128)(2,1)S(1)}, u32[]{:S(2)}, u32[]{:S(2)}) %collective-permute-start.21) | collective-permute-done | bytes 98336 | tf_op jit(solution)/shard_map/ppermute | solution.py:284
  119.8 1.4 collective-permute-start.26
  121.2 1.8 %collective-permute-start.18 = (bf16[2,256,128]{2,1,0:T(8,128)(2,1)S(1)}, bf16[2,256,128]{2,1,0:T(8,128)(2,1)S(1)}, u32[]{:S(2)}, u32[]{:S(2)}) collective-permute-start(bf16[2,256,128]{2,1,0:T(8,128)(2,1)S(1)} %get-tuple-element.76), channel_id=1, source_target_pairs={{0,16},{8,24},{16,0},{24,8},{1,17},{9,25},{17,1},{25,9},{2,18},{10... | collective-permute-start | bytes 393224 | tf_op jit(solution)/shard_map/ppermute | solution.py:288
  123.0 2.5 %collective-permute-done.25.refs_5_ = bf16[2,3,64,128]{3,2,1,0:T(8,128)(2,1)S(1)} collective-permute-done((bf16[2,3,64,128]{3,2,1,0:T(8,128)(2,1)S(1)}, bf16[2,3,64,128]{3,2,1,0:T(8,128)(2,1)S(1)}, u32[]{:S(2)}, u32[]{:S(2)}) %collective-permute-start.25) | collective-permute-done | bytes 98336 | tf_op jit(solution)/shard_map/ppermute | solution.py:284
  125.4 0.9 collective-permute-done.26.refs_6_
  126.4 0.9 gather_sum.3
  127.4 1.1 collective-permute-start.28
  128.5 0.7 collective-permute-start.29
  129.3 4.5 %collective-permute-done.28.refs_6_ = bf16[2,256,128]{2,1,0:T(8,128)(2,1)S(1)} collective-permute-done((bf16[2,256,128]{2,1,0:T(8,128)(2,1)S(1)}, bf16[2,256,128]{2,1,0:T(8,128)(2,1)S(1)}, u32[]{:S(2)}, u32[]{:S(2)}) %collective-permute-start.28) | collective-permute-done | bytes 131104 | tf_op jit(solution)/shard_map/ppermute | solution.py:288
  133.7 1.9 %collective-permute-done.29.refs_7_ = bf16[2,256,128]{2,1,0:T(8,128)(2,1)S(1)} collective-permute-done((bf16[2,256,128]{2,1,0:T(8,128)(2,1)S(1)}, bf16[2,256,128]{2,1,0:T(8,128)(2,1)S(1)}, u32[]{:S(2)}, u32[]{:S(2)}) %collective-permute-start.29) | collective-permute-done | bytes 131104 | tf_op jit(solution)/shard_map/ppermute | solution.py:288
  135.6 1.6 %join.1 = (bf16[256,1024]{1,0:T(8,128)(2,1)}, bf16[256,1024]{1,0:T(8,128)(2,1)}) custom-call(s32[2]{0:T(128)S(1)} %copy-done.1, bf16[2,256,128]{2,1,0:T(8,128)(2,1)S(1)} %get-tuple-element.74.refs_0_, bf16[2,256,128]{2,1,0:T(8,128)(2,1)S(1)} %collective-permute-done.17.refs_1_, bf16[2,256,128]{2,1,0:T(8,128)(2,1)S(1)} %collective-permute-done.18.refs_2_, ...), custom_call_target="tpu_custom_call" | custom-call | tf_op jit(solution)/shard_map/join/pallas_call | solution.py:232
  (39 shorter events, 2.0 us)
Async XLA Ops:
  6.3 13.7 %all-to-all-start = ((s32[8,1,128]{2,1,0:T(1,128)}), s32[8,1,128]{2,1,0:T(1,128)S(1)}, u32[]{:S(2)}, u32[]{:S(2)}) async-start(s32[8,1,128]{2,1,0:T(1,128)} %bitcast.3), calls=%async_computation | async-start | bytes 8192 | tf_op jit(solution)/shard_map/all_to_all | solution.py:333
  13.6 6.5 %collective-permute-start = (bf16[2,2,256,128]{3,2,1,0:T(8,128)(2,1)}, bf16[2,2,256,128]{3,2,1,0:T(8,128)(2,1)S(1)}, u32[]{:S(2)}, u32[]{:S(2)}) collective-permute-start(bf16[2,2,256,128]{3,2,1,0:T(8,128)(2,1)} %get-tuple-element.50), channel_id=1, source_target_pairs={{0,8},{8,0},{16,24},{24,16},{1,9},{9,1},{17,25},{25,17},{2,10},{10... | collective-permute-start | bytes 786440 | tf_op jit(solution)/shard_map/ppermute | solution.py:284
  13.6 9.4 %collective-permute-start.1 = (bf16[2,2,256,128]{3,2,1,0:T(8,128)(2,1)}, bf16[2,2,256,128]{3,2,1,0:T(8,128)(2,1)S(1)}, u32[]{:S(2)}, u32[]{:S(2)}) collective-permute-start(bf16[2,2,256,128]{3,2,1,0:T(8,128)(2,1)} %get-tuple-element.51), channel_id=1, source_target_pairs={{0,16},{8,24},{16,0},{24,8},{1,17},{9,25},{17,1},{25,9},{2,18},{10... | collective-permute-start | bytes 786440 | tf_op jit(solution)/shard_map/ppermute | solution.py:284
  15.2 12.5 %collective-permute-start.2 = (bf16[2,2,256,128]{3,2,1,0:T(8,128)(2,1)}, bf16[2,2,256,128]{3,2,1,0:T(8,128)(2,1)S(1)}, u32[]{:S(2)}, u32[]{:S(2)}) collective-permute-start(bf16[2,2,256,128]{3,2,1,0:T(8,128)(2,1)} %get-tuple-element.52), channel_id=1, source_target_pairs={{0,24},{8,16},{16,8},{24,0},{1,25},{9,17},{17,9},{25,1},{2,26},{10... | collective-permute-start | bytes 786440 | tf_op jit(solution)/shard_map/ppermute | solution.py:284
  27.7 1.0 copy-start
  28.6 0.7 copy-start.1
  30.0 15.1 %collective-permute-start.3 = (bf16[2,3,64,128]{3,2,1,0:T(8,128)(2,1)S(1)}, bf16[2,3,64,128]{3,2,1,0:T(8,128)(2,1)S(1)}, u32[]{:S(2)}, u32[]{:S(2)}) collective-permute-start(bf16[2,3,64,128]{3,2,1,0:T(8,128)(2,1)S(1)} %get-tuple-element.53), channel_id=1, source_target_pairs={{0,4},{1,5},{2,6},{3,7},{4,0},{5,1},{6,2},{7,3},{8,12},{9,13},{10,... | collective-permute-start | bytes 294920 | tf_op jit(solution)/shard_map/ppermute | solution.py:284
  33.1 15.6 %collective-permute-start.4 = (bf16[2,3,64,128]{3,2,1,0:T(8,128)(2,1)S(1)}, bf16[2,3,64,128]{3,2,1,0:T(8,128)(2,1)S(1)}, u32[]{:S(2)}, u32[]{:S(2)}) collective-permute-start(bf16[2,3,64,128]{3,2,1,0:T(8,128)(2,1)S(1)} %get-tuple-element.54), channel_id=1, source_target_pairs={{0,5},{1,4},{2,7},{3,6},{4,1},{5,0},{6,3},{7,2},{8,13},{9,12},{10,... | collective-permute-start | bytes 294920 | tf_op jit(solution)/shard_map/ppermute | solution.py:284
  34.7 14.0 %collective-permute-start.5 = (bf16[2,3,64,128]{3,2,1,0:T(8,128)(2,1)S(1)}, bf16[2,3,64,128]{3,2,1,0:T(8,128)(2,1)S(1)}, u32[]{:S(2)}, u32[]{:S(2)}) collective-permute-start(bf16[2,3,64,128]{3,2,1,0:T(8,128)(2,1)S(1)} %get-tuple-element.55), channel_id=1, source_target_pairs={{0,6},{1,7},{2,4},{3,5},{4,2},{5,3},{6,0},{7,1},{8,14},{9,15},{10,... | collective-permute-start | bytes 294920 | tf_op jit(solution)/shard_map/ppermute | solution.py:284
  38.0 10.7 %collective-permute-start.6 = (bf16[2,3,64,128]{3,2,1,0:T(8,128)(2,1)S(1)}, bf16[2,3,64,128]{3,2,1,0:T(8,128)(2,1)S(1)}, u32[]{:S(2)}, u32[]{:S(2)}) collective-permute-start(bf16[2,3,64,128]{3,2,1,0:T(8,128)(2,1)S(1)} %get-tuple-element.56), channel_id=1, source_target_pairs={{0,7},{1,6},{2,5},{3,4},{4,3},{5,2},{6,1},{7,0},{8,15},{9,14},{10,... | collective-permute-start | bytes 294920 | tf_op jit(solution)/shard_map/ppermute | solution.py:284
  38.1 10.6 %collective-permute-start.7 = (bf16[2,3,64,128]{3,2,1,0:T(8,128)(2,1)S(1)}, bf16[2,3,64,128]{3,2,1,0:T(8,128)(2,1)S(1)}, u32[]{:S(2)}, u32[]{:S(2)}) collective-permute-start(bf16[2,3,64,128]{3,2,1,0:T(8,128)(2,1)S(1)} %get-tuple-element.57), channel_id=1, source_target_pairs={{0,1},{1,0},{2,3},{3,2},{4,5},{5,4},{6,7},{7,6},{8,9},{9,8},{10,11... | collective-permute-start | bytes 294920 | tf_op jit(solution)/shard_map/ppermute | solution.py:284
  45.1 4.6 %collective-permute-start.8 = (bf16[2,3,64,128]{3,2,1,0:T(8,128)(2,1)S(1)}, bf16[2,3,64,128]{3,2,1,0:T(8,128)(2,1)S(1)}, u32[]{:S(2)}, u32[]{:S(2)}) collective-permute-start(bf16[2,3,64,128]{3,2,1,0:T(8,128)(2,1)S(1)} %get-tuple-element.58), channel_id=1, source_target_pairs={{0,2},{1,3},{2,0},{3,1},{4,6},{5,7},{6,4},{7,5},{8,10},{9,11},{10,... | collective-permute-start | bytes 294920 | tf_op jit(solution)/shard_map/ppermute | solution.py:284
  48.7 5.5 %collective-permute-start.9 = (bf16[2,3,64,128]{3,2,1,0:T(8,128)(2,1)S(1)}, bf16[2,3,64,128]{3,2,1,0:T(8,128)(2,1)S(1)}, u32[]{:S(2)}, u32[]{:S(2)}) collective-permute-start(bf16[2,3,64,128]{3,2,1,0:T(8,128)(2,1)S(1)} %get-tuple-element.59), channel_id=1, source_target_pairs={{0,3},{1,2},{2,1},{3,0},{4,7},{5,6},{6,5},{7,4},{8,11},{9,10},{10,... | collective-permute-start | bytes 294920 | tf_op jit(solution)/shard_map/ppermute | solution.py:284
  66.7 14.0 %collective-permute-start.10 = (bf16[2,3,64,128]{3,2,1,0:T(8,128)(2,1)S(1)}, bf16[2,3,64,128]{3,2,1,0:T(8,128)(2,1)S(1)}, u32[]{:S(2)}, u32[]{:S(2)}) collective-permute-start(bf16[2,3,64,128]{3,2,1,0:T(8,128)(2,1)S(1)} %get-tuple-element.60), channel_id=1, source_target_pairs={{0,4},{1,5},{2,6},{3,7},{4,0},{5,1},{6,2},{7,3},{8,12},{9,13},{10,... | collective-permute-start | bytes 294920 | tf_op jit(solution)/shard_map/ppermute | solution.py:284
  69.2 13.2 %collective-permute-start.11 = (bf16[2,3,64,128]{3,2,1,0:T(8,128)(2,1)S(1)}, bf16[2,3,64,128]{3,2,1,0:T(8,128)(2,1)S(1)}, u32[]{:S(2)}, u32[]{:S(2)}) collective-permute-start(bf16[2,3,64,128]{3,2,1,0:T(8,128)(2,1)S(1)} %get-tuple-element.61), channel_id=1, source_target_pairs={{0,5},{1,4},{2,7},{3,6},{4,1},{5,0},{6,3},{7,2},{8,13},{9,12},{10,... | collective-permute-start | bytes 294920 | tf_op jit(solution)/shard_map/ppermute | solution.py:284
  69.2 13.5 %collective-permute-start.12 = (bf16[2,3,64,128]{3,2,1,0:T(8,128)(2,1)S(1)}, bf16[2,3,64,128]{3,2,1,0:T(8,128)(2,1)S(1)}, u32[]{:S(2)}, u32[]{:S(2)}) collective-permute-start(bf16[2,3,64,128]{3,2,1,0:T(8,128)(2,1)S(1)} %get-tuple-element.62), channel_id=1, source_target_pairs={{0,6},{1,7},{2,4},{3,5},{4,2},{5,3},{6,0},{7,1},{8,14},{9,15},{10,... | collective-permute-start | bytes 294920 | tf_op jit(solution)/shard_map/ppermute | solution.py:284
  72.3 10.4 %collective-permute-start.13 = (bf16[2,3,64,128]{3,2,1,0:T(8,128)(2,1)S(1)}, bf16[2,3,64,128]{3,2,1,0:T(8,128)(2,1)S(1)}, u32[]{:S(2)}, u32[]{:S(2)}) collective-permute-start(bf16[2,3,64,128]{3,2,1,0:T(8,128)(2,1)S(1)} %get-tuple-element.63), channel_id=1, source_target_pairs={{0,7},{1,6},{2,5},{3,4},{4,3},{5,2},{6,1},{7,0},{8,15},{9,14},{10,... | collective-permute-start | bytes 294920 | tf_op jit(solution)/shard_map/ppermute | solution.py:284
  74.3 8.4 %collective-permute-start.14 = (bf16[2,3,64,128]{3,2,1,0:T(8,128)(2,1)S(1)}, bf16[2,3,64,128]{3,2,1,0:T(8,128)(2,1)S(1)}, u32[]{:S(2)}, u32[]{:S(2)}) collective-permute-start(bf16[2,3,64,128]{3,2,1,0:T(8,128)(2,1)S(1)} %get-tuple-element.64), channel_id=1, source_target_pairs={{0,1},{1,0},{2,3},{3,2},{4,5},{5,4},{6,7},{7,6},{8,9},{9,8},{10,11... | collective-permute-start | bytes 294920 | tf_op jit(solution)/shard_map/ppermute | solution.py:284
  80.7 5.2 %collective-permute-start.15 = (bf16[2,3,64,128]{3,2,1,0:T(8,128)(2,1)S(1)}, bf16[2,3,64,128]{3,2,1,0:T(8,128)(2,1)S(1)}, u32[]{:S(2)}, u32[]{:S(2)}) collective-permute-start(bf16[2,3,64,128]{3,2,1,0:T(8,128)(2,1)S(1)} %get-tuple-element.65), channel_id=1, source_target_pairs={{0,2},{1,3},{2,0},{3,1},{4,6},{5,7},{6,4},{7,5},{8,10},{9,11},{10,... | collective-permute-start | bytes 294920 | tf_op jit(solution)/shard_map/ppermute | solution.py:284
  82.4 5.5 %collective-permute-start.16 = (bf16[2,3,64,128]{3,2,1,0:T(8,128)(2,1)S(1)}, bf16[2,3,64,128]{3,2,1,0:T(8,128)(2,1)S(1)}, u32[]{:S(2)}, u32[]{:S(2)}) collective-permute-start(bf16[2,3,64,128]{3,2,1,0:T(8,128)(2,1)S(1)} %get-tuple-element.66), channel_id=1, source_target_pairs={{0,3},{1,2},{2,1},{3,0},{4,7},{5,6},{6,5},{7,4},{8,11},{9,10},{10,... | collective-permute-start | bytes 294920 | tf_op jit(solution)/shard_map/ppermute | solution.py:284
  101.3 18.5 %collective-permute-start.19 = (bf16[2,256,128]{2,1,0:T(8,128)(2,1)S(1)}, bf16[2,256,128]{2,1,0:T(8,128)(2,1)S(1)}, u32[]{:S(2)}, u32[]{:S(2)}) collective-permute-start(bf16[2,256,128]{2,1,0:T(8,128)(2,1)S(1)} %get-tuple-element.77), channel_id=1, source_target_pairs={{0,24},{8,16},{16,8},{24,0},{1,25},{9,17},{17,9},{25,1},{2,26},{10... | collective-permute-start | bytes 393224 | tf_op jit(solution)/shard_map/ppermute | solution.py:288
  101.4 8.4 %collective-permute-start.20 = (bf16[2,3,64,128]{3,2,1,0:T(8,128)(2,1)S(1)}, bf16[2,3,64,128]{3,2,1,0:T(8,128)(2,1)S(1)}, u32[]{:S(2)}, u32[]{:S(2)}) collective-permute-start(bf16[2,3,64,128]{3,2,1,0:T(8,128)(2,1)S(1)} %get-tuple-element.79), channel_id=1, source_target_pairs={{0,4},{1,5},{2,6},{3,7},{4,0},{5,1},{6,2},{7,3},{8,12},{9,13},{10,... | collective-permute-start | bytes 294920 | tf_op jit(solution)/shard_map/ppermute | solution.py:284
  103.4 16.4 %collective-permute-start.21 = (bf16[2,3,64,128]{3,2,1,0:T(8,128)(2,1)S(1)}, bf16[2,3,64,128]{3,2,1,0:T(8,128)(2,1)S(1)}, u32[]{:S(2)}, u32[]{:S(2)}) collective-permute-start(bf16[2,3,64,128]{3,2,1,0:T(8,128)(2,1)S(1)} %get-tuple-element.80), channel_id=1, source_target_pairs={{0,5},{1,4},{2,7},{3,6},{4,1},{5,0},{6,3},{7,2},{8,13},{9,12},{10,... | collective-permute-start | bytes 294920 | tf_op jit(solution)/shard_map/ppermute | solution.py:284
  105.7 15.5 %collective-permute-start.22 = (bf16[2,3,64,128]{3,2,1,0:T(8,128)(2,1)S(1)}, bf16[2,3,64,128]{3,2,1,0:T(8,128)(2,1)S(1)}, u32[]{:S(2)}, u32[]{:S(2)}) collective-permute-start(bf16[2,3,64,128]{3,2,1,0:T(8,128)(2,1)S(1)} %get-tuple-element.81), channel_id=1, source_target_pairs={{0,6},{1,7},{2,4},{3,5},{4,2},{5,3},{6,0},{7,1},{8,14},{9,15},{10,... | collective-permute-start | bytes 294920 | tf_op jit(solution)/shard_map/ppermute | solution.py:284
  108.7 12.5 %collective-permute-start.23 = (bf16[2,3,64,128]{3,2,1,0:T(8,128)(2,1)S(1)}, bf16[2,3,64,128]{3,2,1,0:T(8,128)(2,1)S(1)}, u32[]{:S(2)}, u32[]{:S(2)}) collective-permute-start(bf16[2,3,64,128]{3,2,1,0:T(8,128)(2,1)S(1)} %get-tuple-element.82), channel_id=1, source_target_pairs={{0,7},{1,6},{2,5},{3,4},{4,3},{5,2},{6,1},{7,0},{8,15},{9,14},{10,... | collective-permute-start | bytes 294920 | tf_op jit(solution)/shard_map/ppermute | solution.py:284
  109.8 13.1 %collective-permute-start.24 = (bf16[2,3,64,128]{3,2,1,0:T(8,128)(2,1)S(1)}, bf16[2,3,64,128]{3,2,1,0:T(8,128)(2,1)S(1)}, u32[]{:S(2)}, u32[]{:S(2)}) collective-permute-start(bf16[2,3,64,128]{3,2,1,0:T(8,128)(2,1)S(1)} %get-tuple-element.83), channel_id=1, source_target_pairs={{0,1},{1,0},{2,3},{3,2},{4,5},{5,4},{6,7},{7,6},{8,9},{9,8},{10,11... | collective-permute-start | bytes 294920 | tf_op jit(solution)/shard_map/ppermute | solution.py:284
  119.8 5.6 %collective-permute-start.25 = (bf16[2,3,64,128]{3,2,1,0:T(8,128)(2,1)S(1)}, bf16[2,3,64,128]{3,2,1,0:T(8,128)(2,1)S(1)}, u32[]{:S(2)}, u32[]{:S(2)}) collective-permute-start(bf16[2,3,64,128]{3,2,1,0:T(8,128)(2,1)S(1)} %get-tuple-element.84), channel_id=1, source_target_pairs={{0,2},{1,3},{2,0},{3,1},{4,6},{5,7},{6,4},{7,5},{8,10},{9,11},{10,... | collective-permute-start | bytes 294920 | tf_op jit(solution)/shard_map/ppermute | solution.py:284
  119.8 6.6 %collective-permute-start.26 = (bf16[2,3,64,128]{3,2,1,0:T(8,128)(2,1)S(1)}, bf16[2,3,64,128]{3,2,1,0:T(8,128)(2,1)S(1)}, u32[]{:S(2)}, u32[]{:S(2)}) collective-permute-start(bf16[2,3,64,128]{3,2,1,0:T(8,128)(2,1)S(1)} %get-tuple-element.85), channel_id=1, source_target_pairs={{0,3},{1,2},{2,1},{3,0},{4,7},{5,6},{6,5},{7,4},{8,11},{9,10},{10,... | collective-permute-start | bytes 294920 | tf_op jit(solution)/shard_map/ppermute | solution.py:284
  121.2 8.1 %collective-permute-start.17 = (bf16[2,256,128]{2,1,0:T(8,128)(2,1)S(1)}, bf16[2,256,128]{2,1,0:T(8,128)(2,1)S(1)}, u32[]{:S(2)}, u32[]{:S(2)}) collective-permute-start(bf16[2,256,128]{2,1,0:T(8,128)(2,1)S(1)} %get-tuple-element.75), channel_id=1, source_target_pairs={{0,8},{8,0},{16,24},{24,16},{1,9},{9,1},{17,25},{25,17},{2,10},{10... | collective-permute-start | bytes 393224 | tf_op jit(solution)/shard_map/ppermute | solution.py:288
  121.2 8.1 %collective-permute-start.18 = (bf16[2,256,128]{2,1,0:T(8,128)(2,1)S(1)}, bf16[2,256,128]{2,1,0:T(8,128)(2,1)S(1)}, u32[]{:S(2)}, u32[]{:S(2)}) collective-permute-start(bf16[2,256,128]{2,1,0:T(8,128)(2,1)S(1)} %get-tuple-element.76), channel_id=1, source_target_pairs={{0,16},{8,24},{16,0},{24,8},{1,17},{9,25},{17,1},{25,9},{2,18},{10... | collective-permute-start | bytes 393224 | tf_op jit(solution)/shard_map/ppermute | solution.py:288
  127.3 2.0 %collective-permute-start.27 = (bf16[2,256,128]{2,1,0:T(8,128)(2,1)S(1)}, bf16[2,256,128]{2,1,0:T(8,128)(2,1)S(1)}, u32[]{:S(2)}, u32[]{:S(2)}) collective-permute-start(bf16[2,256,128]{2,1,0:T(8,128)(2,1)S(1)} %get-tuple-element.87), channel_id=1, source_target_pairs={{0,8},{8,0},{16,24},{24,16},{1,9},{9,1},{17,25},{25,17},{2,10},{10... | collective-permute-start | bytes 393224 | tf_op jit(solution)/shard_map/ppermute | solution.py:288
  127.4 6.4 %collective-permute-start.28 = (bf16[2,256,128]{2,1,0:T(8,128)(2,1)S(1)}, bf16[2,256,128]{2,1,0:T(8,128)(2,1)S(1)}, u32[]{:S(2)}, u32[]{:S(2)}) collective-permute-start(bf16[2,256,128]{2,1,0:T(8,128)(2,1)S(1)} %get-tuple-element.88), channel_id=1, source_target_pairs={{0,16},{8,24},{16,0},{24,8},{1,17},{9,25},{17,1},{25,9},{2,18},{10... | collective-permute-start | bytes 393224 | tf_op jit(solution)/shard_map/ppermute | solution.py:288
  128.5 7.1 %collective-permute-start.29 = (bf16[2,256,128]{2,1,0:T(8,128)(2,1)S(1)}, bf16[2,256,128]{2,1,0:T(8,128)(2,1)S(1)}, u32[]{:S(2)}, u32[]{:S(2)}) collective-permute-start(bf16[2,256,128]{2,1,0:T(8,128)(2,1)S(1)} %get-tuple-element.89), channel_id=1, source_target_pairs={{0,24},{8,16},{16,8},{24,0},{1,25},{9,17},{17,9},{25,1},{2,26},{10... | collective-permute-start | bytes 393224 | tf_op jit(solution)/shard_map/ppermute | solution.py:288

commit v10 on v9

--- a/solution.py
+++ b/solution.py
@@ -13,7 +13,7 @@
 LIST = 8
 CAP = 3
 STEP_BLOCKS = 4
-TOGETHER = 2
+TOGETHER = 4
 NEG_FILL = -1e30
 SCALE = HEAD_DIM ** (-0.5)
 LOG2E = 1.4426950408889634
@@ -42,7 +42,8 @@
 
 
 def steps_of(count):
-    return [*range(count // 2, count), *range(1, count // 2)] if count > 1 else []
+    short = list(range(1, count // 2))
+    return short[:2] + list(range(max(1, count // 2), count)) + short[2:]
 
 
 def head_columns(place, r, heads, h, head_count):
@@ -126,7 +127,7 @@
 
     @pl.when(step == 0)
     def _():
-        fill_table(place, own, head, table)
+        fill_table(place, own, 0, table)
         for r, part in zip(steps_of(shard_count), far):
             first = blocks_here + origin(place[0], r, shard_count) * CAP
             for kv in range(2):
@@ -178,7 +179,7 @@
         for kv, factor in ((0, SCALE), (1, 1.0)):
             near_out[kv] = total[kv, :blocks_here] * factor
         if not last:
-            fill_table(place, own, head + 1, table)
+            fill_table(place, own, 1, table)
         for r, out in zip(steps_of(shard_count), outs):
             there = partner(place[0], r, shard_count)
 
@@ -219,6 +220,10 @@
 
 def whole(shape):
     return pl.BlockSpec(tuple(shape), lambda *_: (0,) * len(shape))
+
+
+def heads_from(shape, head, count):
+    return pl.BlockSpec((pl.Element(count), *(pl.Element(n) for n in shape[1:])), lambda *_: (head, *(0,) * (len(shape) - 1)))
 
 
 ANYWHERE = pl.BlockSpec(memory_space=pl.ANY)
@@ -260,7 +265,10 @@
         grid_spec=pltpu.PrefetchScalarGridSpec(
             num_scalar_prefetch=3,
             grid=(blocks_here // STEP_BLOCKS,),
-            in_specs=[tile, tile] + [whole(x.shape) for x in arrays] + [ANYWHERE] * len(earlier),
+            in_specs=[tile, tile]
+            + [heads_from(x.shape, head, 1 if last else 2) for x in own]
+            + [whole(x.shape) for x in far]
+            + [ANYWHERE] * len(earlier),
             out_specs=[tile, tile, whole(near_shape)] + [whole(x.shape) for x in out_shapes],
             scratch_shapes=[
                 pltpu.VMEM((2, slots, BLK, HEAD_DIM), jnp.bfloat16),
@@ -329,7 +337,7 @@
     )
     own = [pieces[0]] + [send(pieces[r], "head", heads, r) for r in range(1, heads)]
 
-    requests, source = requests_of(after(block_lists, pieces[0]).reshape(-1), blocks_here, shard_index, shard_count)
+    requests, source = requests_of(after(block_lists, *own[1:2]).reshape(-1), blocks_here, shard_index, shard_count)
     asked = lax.all_to_all(requests, "ctx", split_axis=0, concat_axis=0, tiled=True)
 
     def exchange(arrays):

time: 138 us -> 125 us (0.906)
  waiting for transfers between devices: 50.8 us -> 42.8 us
  starting transfers between devices: 49 us -> 45.6 us
    ppermute x24, waiting for transfers between devices: 39.9 us -> 34.4 us  [send(): lax.ppermute(x, axis, [(i, partner(i, r, count)) for i in range(count)])]
    all_to_all x1, waiting for transfers between devices: 4.58 us -> 2.03 us  [per_device(): lax.all_to_all(requests, 'ctx', split_axis=0, concat_axis=0, tiled=True)]
    ppermute x24, starting transfers between devices: 37.9 us -> 36.2 us  [send(): lax.ppermute(x, axis, [(i, partner(i, r, count)) for i in range(count)])]
  transfers between devices with their start and end apart: 31 -> 31, of which waited for: 17 -> 14; matrix products, arithmetic and copies ran while one was open for 0% -> 2% of each run, Pallas kernels for 1% -> 1%
where the time goes in v10:
time: 125 us
  starting transfers between devices  45.6 us (36%)
  waiting for transfers between devices  42.8 us (34%)
  Pallas kernels  31.4 us (25%)
  local copies, waits for them, and re-layouts  2.52 us (2%)
  other arithmetic  1.83 us (1%)
    ppermute x24, starting transfers between devices, send(): lax.ppermute(x, axis, [(i, partner(i, r, count)) for i in range(count)])  36.2 us
    ppermute x24, waiting for transfers between devices, send(): lax.ppermute(x, axis, [(i, partner(i, r, count)) for i in range(count)])  34.4 us
    pallas_call x2, Pallas kernels, attend(): pl.pallas_call(functools.partial(attend_kernel, heads=len(own), head=head...  24.2 us
    pallas_call x5, Pallas kernels, call(): pl.pallas_call(kernel, grid_spec=pltpu.PrefetchScalarGridSpec(num_scalar_...  7.16 us
    ppermute x6, waiting for transfers between devices, send_back(): lax.ppermute(x, axis, [(i, origin(i, r, count)) for i in range(count)])  6.4 us
    all_to_all x1, starting transfers between devices, per_device(): lax.all_to_all(requests, 'ctx', split_axis=0, concat_axis=0, tiled=True)  6.07 us
    ppermute x6, starting transfers between devices, send_back(): lax.ppermute(x, axis, [(i, origin(i, r, count)) for i in range(count)])  3.39 us
  transfers between devices with their start and end apart: 31, of which 14 were waited for; matrix products, arithmetic and copies ran while one was open for 2% of the time, Pallas kernels for 1%

profile of v10, /device:TPU:0, one launch (start us, length us, event | category | flops | bytes accessed | tf_op | source)
XLA Modules:
  0.0 124.9 jit_solution(5016839246729853667)
XLA Ops:
  0.6 0.6 pad_add_fusion.place
  1.3 3.0 %split.1 = (bf16[2,2,256,128]{3,2,1,0:T(8,128)(2,1)}, bf16[2,2,256,128]{3,2,1,0:T(8,128)(2,1)}, bf16[2,2,256,128]{3,2,1,0:T(8,128)(2,1)}, bf16[2,2,256,128]{3,2,1,0:T(8,128)(2,1)}) custom-call(s32[2]{0:T(128)} %pad_add_fusion.place, bf16[256,1024]{1,0:T(8,128)(2,1)} %k_ref.1, bf16[256,1024]{1,0:T(8,128)(2,1)} %v_ref.1), custom_call_target="tpu_custom_call" | custom-call | tf_op jit(solution)/shard_map/split/pallas_call | solution.py:237
  4.3 0.5 collective-permute-start
  4.8 2.6 %collective-permute-start.1 = (bf16[2,2,256,128]{3,2,1,0:T(8,128)(2,1)}, bf16[2,2,256,128]{3,2,1,0:T(8,128)(2,1)S(1)}, u32[]{:S(2)}, u32[]{:S(2)}) collective-permute-start(bf16[2,2,256,128]{3,2,1,0:T(8,128)(2,1)} %get-tuple-element.51), channel_id=1, source_target_pairs={{0,16},{8,24},{16,0},{24,8},{1,17},{9,25},{17,1},{25,9},{2,18},{10... | collective-permute-start | bytes 786440 | tf_op jit(solution)/shard_map/ppermute | solution.py:292
  7.5 0.8 copy.14
  8.7 0.7 select_reduce_fusion
  9.4 6.1 %all-to-all-start = ((s32[8,1,128]{2,1,0:T(1,128)}), s32[8,1,128]{2,1,0:T(1,128)S(1)}, u32[]{:S(2)}, u32[]{:S(2)}) async-start(s32[8,1,128]{2,1,0:T(1,128)} %bitcast.3), calls=%async_computation | async-start | bytes 8192 | tf_op jit(solution)/shard_map/all_to_all | solution.py:341
  15.5 4.3 %collective-permute-done.2.refs_3_ = bf16[2,2,256,128]{3,2,1,0:T(8,128)(2,1)S(1)} collective-permute-done((bf16[2,2,256,128]{3,2,1,0:T(8,128)(2,1)}, bf16[2,2,256,128]{3,2,1,0:T(8,128)(2,1)S(1)}, u32[]{:S(2)}, u32[]{:S(2)}) %collective-permute-start.2) | collective-permute-done | bytes 262176 | tf_op jit(solution)/shard_map/ppermute | solution.py:292
  19.8 2.0 %all-to-all-done = s32[8,1,128]{2,1,0:T(1,128)S(1)} async-done(((s32[8,1,128]{2,1,0:T(1,128)}), s32[8,1,128]{2,1,0:T(1,128)S(1)}, u32[]{:S(2)}, u32[]{:S(2)}) %all-to-all-start) | async-done | bytes 4128 | tf_op jit(solution)/shard_map/all_to_all | solution.py:341
  21.9 0.9 copy-done
  22.8 0.6 copy-done.1
  23.5 0.7 pick.1
  24.2 0.6 collective-permute-start.3
  24.8 0.6 collective-permute-start.4
  25.5 2.7 %collective-permute-start.5 = (bf16[2,3,64,128]{3,2,1,0:T(8,128)(2,1)S(1)}, bf16[2,3,64,128]{3,2,1,0:T(8,128)(2,1)S(1)}, u32[]{:S(2)}, u32[]{:S(2)}) collective-permute-start(bf16[2,3,64,128]{3,2,1,0:T(8,128)(2,1)S(1)} %get-tuple-element.55), channel_id=1, source_target_pairs={{0,4},{1,5},{2,6},{3,7},{4,0},{5,1},{6,2},{7,3},{8,12},{9,13},{10,... | collective-permute-start | bytes 294920 | tf_op jit(solution)/shard_map/ppermute | solution.py:292
  28.2 1.2 collective-permute-start.6
  29.4 1.6 %collective-permute-start.7 = (bf16[2,3,64,128]{3,2,1,0:T(8,128)(2,1)S(1)}, bf16[2,3,64,128]{3,2,1,0:T(8,128)(2,1)S(1)}, u32[]{:S(2)}, u32[]{:S(2)}) collective-permute-start(bf16[2,3,64,128]{3,2,1,0:T(8,128)(2,1)S(1)} %get-tuple-element.57), channel_id=1, source_target_pairs={{0,6},{1,7},{2,4},{3,5},{4,2},{5,3},{6,0},{7,1},{8,14},{9,15},{10,... | collective-permute-start | bytes 294920 | tf_op jit(solution)/shard_map/ppermute | solution.py:292
  30.9 2.3 %collective-permute-start.8 = (bf16[2,3,64,128]{3,2,1,0:T(8,128)(2,1)S(1)}, bf16[2,3,64,128]{3,2,1,0:T(8,128)(2,1)S(1)}, u32[]{:S(2)}, u32[]{:S(2)}) collective-permute-start(bf16[2,3,64,128]{3,2,1,0:T(8,128)(2,1)S(1)} %get-tuple-element.58), channel_id=1, source_target_pairs={{0,7},{1,6},{2,5},{3,4},{4,3},{5,2},{6,1},{7,0},{8,15},{9,14},{10,... | collective-permute-start | bytes 294920 | tf_op jit(solution)/shard_map/ppermute | solution.py:292
  33.3 0.5 collective-permute-start.9
  33.8 6.2 %collective-permute-done.5.refs_6_ = bf16[2,3,64,128]{3,2,1,0:T(8,128)(2,1)S(1)} collective-permute-done((bf16[2,3,64,128]{3,2,1,0:T(8,128)(2,1)S(1)}, bf16[2,3,64,128]{3,2,1,0:T(8,128)(2,1)S(1)}, u32[]{:S(2)}, u32[]{:S(2)}) %collective-permute-start.5) | collective-permute-done | bytes 98336 | tf_op jit(solution)/shard_map/ppermute | solution.py:292
  40.1 2.2 %collective-permute-done.6.refs_7_ = bf16[2,3,64,128]{3,2,1,0:T(8,128)(2,1)S(1)} collective-permute-done((bf16[2,3,64,128]{3,2,1,0:T(8,128)(2,1)S(1)}, bf16[2,3,64,128]{3,2,1,0:T(8,128)(2,1)S(1)}, u32[]{:S(2)}, u32[]{:S(2)}) %collective-permute-start.6) | collective-permute-done | bytes 98336 | tf_op jit(solution)/shard_map/ppermute | solution.py:292
  42.3 1.3 %collective-permute-done.9.refs_10_ = bf16[2,3,64,128]{3,2,1,0:T(8,128)(2,1)S(1)} collective-permute-done((bf16[2,3,64,128]{3,2,1,0:T(8,128)(2,1)S(1)}, bf16[2,3,64,128]{3,2,1,0:T(8,128)(2,1)S(1)}, u32[]{:S(2)}, u32[]{:S(2)}) %collective-permute-start.9) | collective-permute-done | bytes 98336 | tf_op jit(solution)/shard_map/ppermute | solution.py:292
  43.6 12.1 %attend.2 = (bf16[1024,1024]{1,0:T(8,128)(2,1)}, bf16[1024,1024]{1,0:T(8,128)(2,1)}, f32[2,16,64,128]{3,2,1,0:T(8,128)S(1)}, bf16[2,3,64,128]{3,2,1,0:T(8,128)(2...) custom-call(s32[2]{0:T(128)S(1)} %copy-done.1, ...), custom_call_target="tpu_custom_call" | custom-call | flops 3221225472 | bytes 20971520 | tf_op jit(solution)/shard_map/attend/pallas_call | solution.py:261
  55.7 0.9 collective-permute-start.10
  56.6 3.3 %collective-permute-start.11 = (bf16[2,3,64,128]{3,2,1,0:T(8,128)(2,1)S(1)}, bf16[2,3,64,128]{3,2,1,0:T(8,128)(2,1)S(1)}, u32[]{:S(2)}, u32[]{:S(2)}) collective-permute-start(bf16[2,3,64,128]{3,2,1,0:T(8,128)(2,1)S(1)} %get-tuple-element.61), channel_id=1, source_target_pairs={{0,2},{1,3},{2,0},{3,1},{4,6},{5,7},{6,4},{7,5},{8,10},{9,11},{10,... | collective-permute-start | bytes 294920 | tf_op jit(solution)/shard_map/ppermute | solution.py:292
  59.9 1.1 collective-permute-start.12
  60.9 2.2 %collective-permute-start.13 = (bf16[2,3,64,128]{3,2,1,0:T(8,128)(2,1)S(1)}, bf16[2,3,64,128]{3,2,1,0:T(8,128)(2,1)S(1)}, u32[]{:S(2)}, u32[]{:S(2)}) collective-permute-start(bf16[2,3,64,128]{3,2,1,0:T(8,128)(2,1)S(1)} %get-tuple-element.63), channel_id=1, source_target_pairs={{0,5},{1,4},{2,7},{3,6},{4,1},{5,0},{6,3},{7,2},{8,13},{9,12},{10,... | collective-permute-start | bytes 294920 | tf_op jit(solution)/shard_map/ppermute | solution.py:292
  63.1 2.1 %collective-permute-start.14 = (bf16[2,3,64,128]{3,2,1,0:T(8,128)(2,1)S(1)}, bf16[2,3,64,128]{3,2,1,0:T(8,128)(2,1)S(1)}, u32[]{:S(2)}, u32[]{:S(2)}) collective-permute-start(bf16[2,3,64,128]{3,2,1,0:T(8,128)(2,1)S(1)} %get-tuple-element.64), channel_id=1, source_target_pairs={{0,6},{1,7},{2,4},{3,5},{4,2},{5,3},{6,0},{7,1},{8,14},{9,15},{10,... | collective-permute-start | bytes 294920 | tf_op jit(solution)/shard_map/ppermute | solution.py:292
  65.3 2.3 %collective-permute-start.15 = (bf16[2,3,64,128]{3,2,1,0:T(8,128)(2,1)S(1)}, bf16[2,3,64,128]{3,2,1,0:T(8,128)(2,1)S(1)}, u32[]{:S(2)}, u32[]{:S(2)}) collective-permute-start(bf16[2,3,64,128]{3,2,1,0:T(8,128)(2,1)S(1)} %get-tuple-element.65), channel_id=1, source_target_pairs={{0,7},{1,6},{2,5},{3,4},{4,3},{5,2},{6,1},{7,0},{8,15},{9,14},{10,... | collective-permute-start | bytes 294920 | tf_op jit(solution)/shard_map/ppermute | solution.py:292
  67.5 6.3 %collective-permute-done.12.refs_6_.refs_2_ = bf16[2,3,64,128]{3,2,1,0:T(8,128)(2,1)S(1)} collective-permute-done((bf16[2,3,64,128]{3,2,1,0:T(8,128)(2,1)S(1)}, bf16[2,3,64,128]{3,2,1,0:T(8,128)(2,1)S(1)}, u32[]{:S(2)}, u32[]{:S(2)}) %collective-permute-start.12) | collective-permute-done | bytes 98336 | tf_op jit(solution)/shard_map/ppermute | solution.py:292
  73.9 2.5 %collective-permute-done.13.refs_7_.refs_3_ = bf16[2,3,64,128]{3,2,1,0:T(8,128)(2,1)S(1)} collective-permute-done((bf16[2,3,64,128]{3,2,1,0:T(8,128)(2,1)S(1)}, bf16[2,3,64,128]{3,2,1,0:T(8,128)(2,1)S(1)}, u32[]{:S(2)}, u32[]{:S(2)}) %collective-permute-start.13) | collective-permute-done | bytes 98336 | tf_op jit(solution)/shard_map/ppermute | solution.py:292
  76.4 0.6 collective-permute-done.16.refs_10_.refs_6_
  77.0 12.1 %attend.3 = (bf16[1024,1024]{1,0:T(8,128)(2,1)}, bf16[1024,1024]{1,0:T(8,128)(2,1)}, f32[2,16,64,128]{3,2,1,0:T(8,128)S(1)}, bf16[2,3,64,128]{3,2,1,0:T(8,128)(2...) custom-call(s32[2]{0:T(128)S(1)} %copy-done.1, ...), custom_call_target="tpu_custom_call", output_to_operand_aliasing={{0}: (16, {}), {1}: (17, {})} | custom-call | flops 3221225472 | bytes 20971520 | tf_op jit(solution)/shard_map/attend/pallas_call | solution.py:261
  89.1 0.9 gather_sum.2
  90.8 3.8 %collective-permute-start.21 = (bf16[2,3,64,128]{3,2,1,0:T(8,128)(2,1)S(1)}, bf16[2,3,64,128]{3,2,1,0:T(8,128)(2,1)S(1)}, u32[]{:S(2)}, u32[]{:S(2)}) collective-permute-start(bf16[2,3,64,128]{3,2,1,0:T(8,128)(2,1)S(1)} %get-tuple-element.80), channel_id=1, source_target_pairs={{0,2},{1,3},{2,0},{3,1},{4,6},{5,7},{6,4},{7,5},{8,10},{9,11},{10,... | collective-permute-start | bytes 294920 | tf_op jit(solution)/shard_map/ppermute | solution.py:292
  94.6 3.4 %collective-permute-start.23 = (bf16[2,3,64,128]{3,2,1,0:T(8,128)(2,1)S(1)}, bf16[2,3,64,128]{3,2,1,0:T(8,128)(2,1)S(1)}, u32[]{:S(2)}, u32[]{:S(2)}) collective-permute-start(bf16[2,3,64,128]{3,2,1,0:T(8,128)(2,1)S(1)} %get-tuple-element.82), channel_id=1, source_target_pairs={{0,5},{1,4},{2,7},{3,6},{4,1},{5,0},{6,3},{7,2},{8,13},{9,12},{10,... | collective-permute-start | bytes 294920 | tf_op jit(solution)/shard_map/ppermute | solution.py:292
  98.0 1.3 %collective-permute-start.24 = (bf16[2,3,64,128]{3,2,1,0:T(8,128)(2,1)S(1)}, bf16[2,3,64,128]{3,2,1,0:T(8,128)(2,1)S(1)}, u32[]{:S(2)}, u32[]{:S(2)}) collective-permute-start(bf16[2,3,64,128]{3,2,1,0:T(8,128)(2,1)S(1)} %get-tuple-element.83), channel_id=1, source_target_pairs={{0,6},{1,7},{2,4},{3,5},{4,2},{5,3},{6,0},{7,1},{8,14},{9,15},{10,... | collective-permute-start | bytes 294920 | tf_op jit(solution)/shard_map/ppermute | solution.py:292
  99.3 2.9 %collective-permute-start.25 = (bf16[2,3,64,128]{3,2,1,0:T(8,128)(2,1)S(1)}, bf16[2,3,64,128]{3,2,1,0:T(8,128)(2,1)S(1)}, u32[]{:S(2)}, u32[]{:S(2)}) collective-permute-start(bf16[2,3,64,128]{3,2,1,0:T(8,128)(2,1)S(1)} %get-tuple-element.84), channel_id=1, source_target_pairs={{0,7},{1,6},{2,5},{3,4},{4,3},{5,2},{6,1},{7,0},{8,15},{9,14},{10,... | collective-permute-start | bytes 294920 | tf_op jit(solution)/shard_map/ppermute | solution.py:292
  102.2 7.4 %collective-permute-done.22.refs_2_ = bf16[2,3,64,128]{3,2,1,0:T(8,128)(2,1)S(1)} collective-permute-done((bf16[2,3,64,128]{3,2,1,0:T(8,128)(2,1)S(1)}, bf16[2,3,64,128]{3,2,1,0:T(8,128)(2,1)S(1)}, u32[]{:S(2)}, u32[]{:S(2)}) %collective-permute-start.22) | collective-permute-done | bytes 98336 | tf_op jit(solution)/shard_map/ppermute | solution.py:292
  109.7 2.5 %collective-permute-done.23.refs_3_ = bf16[2,3,64,128]{3,2,1,0:T(8,128)(2,1)S(1)} collective-permute-done((bf16[2,3,64,128]{3,2,1,0:T(8,128)(2,1)S(1)}, bf16[2,3,64,128]{3,2,1,0:T(8,128)(2,1)S(1)}, u32[]{:S(2)}, u32[]{:S(2)}) %collective-permute-start.23) | collective-permute-done | bytes 98336 | tf_op jit(solution)/shard_map/ppermute | solution.py:292
  112.2 1.0 collective-permute-start.18
  113.2 0.9 collective-permute-done.26.refs_6_
  114.0 0.9 gather_sum.3
  115.0 0.6 collective-permute-start.28
  115.6 1.3 %collective-permute-start.29 = (bf16[2,256,128]{2,1,0:T(8,128)(2,1)S(1)}, bf16[2,256,128]{2,1,0:T(8,128)(2,1)S(1)}, u32[]{:S(2)}, u32[]{:S(2)}) collective-permute-start(bf16[2,256,128]{2,1,0:T(8,128)(2,1)S(1)} %get-tuple-element.89), channel_id=1, source_target_pairs={{0,24},{8,16},{16,8},{24,0},{1,25},{9,17},{17,9},{25,1},{2,26},{10... | collective-permute-start | bytes 393224 | tf_op jit(solution)/shard_map/ppermute | solution.py:296
  117.3 4.1 %collective-permute-done.28.refs_6_ = bf16[2,256,128]{2,1,0:T(8,128)(2,1)S(1)} collective-permute-done((bf16[2,256,128]{2,1,0:T(8,128)(2,1)S(1)}, bf16[2,256,128]{2,1,0:T(8,128)(2,1)S(1)}, u32[]{:S(2)}, u32[]{:S(2)}) %collective-permute-start.28) | collective-permute-done | bytes 131104 | tf_op jit(solution)/shard_map/ppermute | solution.py:296
  121.4 1.9 %collective-permute-done.29.refs_7_ = bf16[2,256,128]{2,1,0:T(8,128)(2,1)S(1)} collective-permute-done((bf16[2,256,128]{2,1,0:T(8,128)(2,1)S(1)}, bf16[2,256,128]{2,1,0:T(8,128)(2,1)S(1)}, u32[]{:S(2)}, u32[]{:S(2)}) %collective-permute-start.29) | collective-permute-done | bytes 131104 | tf_op jit(solution)/shard_map/ppermute | solution.py:296
  123.3 1.6 %join.1 = (bf16[256,1024]{1,0:T(8,128)(2,1)}, bf16[256,1024]{1,0:T(8,128)(2,1)}) custom-call(s32[2]{0:T(128)S(1)} %copy-done.1, bf16[2,256,128]{2,1,0:T(8,128)(2,1)S(1)} %get-tuple-element.74.refs_0_, bf16[2,256,128]{2,1,0:T(8,128)(2,1)S(1)} %collective-permute-done.17.refs_1_, bf16[2,256,128]{2,1,0:T(8,128)(2,1)S(1)} %collective-permute-done.18.refs_2_, ...), custom_call_target="tpu_custom_call" | custom-call | tf_op jit(solution)/shard_map/join/pallas_call | solution.py:237
  (39 shorter events, 2.0 us)
Async XLA Ops:
  4.3 3.2 %collective-permute-start = (bf16[2,2,256,128]{3,2,1,0:T(8,128)(2,1)}, bf16[2,2,256,128]{3,2,1,0:T(8,128)(2,1)S(1)}, u32[]{:S(2)}, u32[]{:S(2)}) collective-permute-start(bf16[2,2,256,128]{3,2,1,0:T(8,128)(2,1)} %get-tuple-element.48), channel_id=1, source_target_pairs={{0,8},{8,0},{16,24},{24,16},{1,9},{9,1},{17,25},{25,17},{2,10},{10... | collective-permute-start | bytes 786440 | tf_op jit(solution)/shard_map/ppermute | solution.py:292
  4.8 10.7 %collective-permute-start.1 = (bf16[2,2,256,128]{3,2,1,0:T(8,128)(2,1)}, bf16[2,2,256,128]{3,2,1,0:T(8,128)(2,1)S(1)}, u32[]{:S(2)}, u32[]{:S(2)}) collective-permute-start(bf16[2,2,256,128]{3,2,1,0:T(8,128)(2,1)} %get-tuple-element.51), channel_id=1, source_target_pairs={{0,16},{8,24},{16,0},{24,8},{1,17},{9,25},{17,1},{25,9},{2,18},{10... | collective-permute-start | bytes 786440 | tf_op jit(solution)/shard_map/ppermute | solution.py:292
  7.4 12.5 %collective-permute-start.2 = (bf16[2,2,256,128]{3,2,1,0:T(8,128)(2,1)}, bf16[2,2,256,128]{3,2,1,0:T(8,128)(2,1)S(1)}, u32[]{:S(2)}, u32[]{:S(2)}) collective-permute-start(bf16[2,2,256,128]{3,2,1,0:T(8,128)(2,1)} %get-tuple-element.52), channel_id=1, source_target_pairs={{0,24},{8,16},{16,8},{24,0},{1,25},{9,17},{17,9},{25,1},{2,26},{10... | collective-permute-start | bytes 786440 | tf_op jit(solution)/shard_map/ppermute | solution.py:292
  9.4 12.5 %all-to-all-start = ((s32[8,1,128]{2,1,0:T(1,128)}), s32[8,1,128]{2,1,0:T(1,128)S(1)}, u32[]{:S(2)}, u32[]{:S(2)}) async-start(s32[8,1,128]{2,1,0:T(1,128)} %bitcast.3), calls=%async_computation | async-start | bytes 8192 | tf_op jit(solution)/shard_map/all_to_all | solution.py:341
  21.9 1.0 copy-start
  22.8 0.6 copy-start.1
  24.2 6.8 %collective-permute-start.3 = (bf16[2,3,64,128]{3,2,1,0:T(8,128)(2,1)S(1)}, bf16[2,3,64,128]{3,2,1,0:T(8,128)(2,1)S(1)}, u32[]{:S(2)}, u32[]{:S(2)}) collective-permute-start(bf16[2,3,64,128]{3,2,1,0:T(8,128)(2,1)S(1)} %get-tuple-element.53), channel_id=1, source_target_pairs={{0,1},{1,0},{2,3},{3,2},{4,5},{5,4},{6,7},{7,6},{8,9},{9,8},{10,11... | collective-permute-start | bytes 294920 | tf_op jit(solution)/shard_map/ppermute | solution.py:292
  24.8 8.5 %collective-permute-start.4 = (bf16[2,3,64,128]{3,2,1,0:T(8,128)(2,1)S(1)}, bf16[2,3,64,128]{3,2,1,0:T(8,128)(2,1)S(1)}, u32[]{:S(2)}, u32[]{:S(2)}) collective-permute-start(bf16[2,3,64,128]{3,2,1,0:T(8,128)(2,1)S(1)} %get-tuple-element.54), channel_id=1, source_target_pairs={{0,2},{1,3},{2,0},{3,1},{4,6},{5,7},{6,4},{7,5},{8,10},{9,11},{10,... | collective-permute-start | bytes 294920 | tf_op jit(solution)/shard_map/ppermute | solution.py:292
  25.5 14.5 %collective-permute-start.5 = (bf16[2,3,64,128]{3,2,1,0:T(8,128)(2,1)S(1)}, bf16[2,3,64,128]{3,2,1,0:T(8,128)(2,1)S(1)}, u32[]{:S(2)}, u32[]{:S(2)}) collective-permute-start(bf16[2,3,64,128]{3,2,1,0:T(8,128)(2,1)S(1)} %get-tuple-element.55), channel_id=1, source_target_pairs={{0,4},{1,5},{2,6},{3,7},{4,0},{5,1},{6,2},{7,3},{8,12},{9,13},{10,... | collective-permute-start | bytes 294920 | tf_op jit(solution)/shard_map/ppermute | solution.py:292
  28.2 14.1 %collective-permute-start.6 = (bf16[2,3,64,128]{3,2,1,0:T(8,128)(2,1)S(1)}, bf16[2,3,64,128]{3,2,1,0:T(8,128)(2,1)S(1)}, u32[]{:S(2)}, u32[]{:S(2)}) collective-permute-start(bf16[2,3,64,128]{3,2,1,0:T(8,128)(2,1)S(1)} %get-tuple-element.56), channel_id=1, source_target_pairs={{0,5},{1,4},{2,7},{3,6},{4,1},{5,0},{6,3},{7,2},{8,13},{9,12},{10,... | collective-permute-start | bytes 294920 | tf_op jit(solution)/shard_map/ppermute | solution.py:292
  29.4 12.9 %collective-permute-start.7 = (bf16[2,3,64,128]{3,2,1,0:T(8,128)(2,1)S(1)}, bf16[2,3,64,128]{3,2,1,0:T(8,128)(2,1)S(1)}, u32[]{:S(2)}, u32[]{:S(2)}) collective-permute-start(bf16[2,3,64,128]{3,2,1,0:T(8,128)(2,1)S(1)} %get-tuple-element.57), channel_id=1, source_target_pairs={{0,6},{1,7},{2,4},{3,5},{4,2},{5,3},{6,0},{7,1},{8,14},{9,15},{10,... | collective-permute-start | bytes 294920 | tf_op jit(solution)/shard_map/ppermute | solution.py:292
  30.9 11.3 %collective-permute-start.8 = (bf16[2,3,64,128]{3,2,1,0:T(8,128)(2,1)S(1)}, bf16[2,3,64,128]{3,2,1,0:T(8,128)(2,1)S(1)}, u32[]{:S(2)}, u32[]{:S(2)}) collective-permute-start(bf16[2,3,64,128]{3,2,1,0:T(8,128)(2,1)S(1)} %get-tuple-element.58), channel_id=1, source_target_pairs={{0,7},{1,6},{2,5},{3,4},{4,3},{5,2},{6,1},{7,0},{8,15},{9,14},{10,... | collective-permute-start | bytes 294920 | tf_op jit(solution)/shard_map/ppermute | solution.py:292
  33.3 10.3 %collective-permute-start.9 = (bf16[2,3,64,128]{3,2,1,0:T(8,128)(2,1)S(1)}, bf16[2,3,64,128]{3,2,1,0:T(8,128)(2,1)S(1)}, u32[]{:S(2)}, u32[]{:S(2)}) collective-permute-start(bf16[2,3,64,128]{3,2,1,0:T(8,128)(2,1)S(1)} %get-tuple-element.59), channel_id=1, source_target_pairs={{0,3},{1,2},{2,1},{3,0},{4,7},{5,6},{6,5},{7,4},{8,11},{9,10},{10,... | collective-permute-start | bytes 294920 | tf_op jit(solution)/shard_map/ppermute | solution.py:292
  55.7 9.6 %collective-permute-start.10 = (bf16[2,3,64,128]{3,2,1,0:T(8,128)(2,1)S(1)}, bf16[2,3,64,128]{3,2,1,0:T(8,128)(2,1)S(1)}, u32[]{:S(2)}, u32[]{:S(2)}) collective-permute-start(bf16[2,3,64,128]{3,2,1,0:T(8,128)(2,1)S(1)} %get-tuple-element.60), channel_id=1, source_target_pairs={{0,1},{1,0},{2,3},{3,2},{4,5},{5,4},{6,7},{7,6},{8,9},{9,8},{10,11... | collective-permute-start | bytes 294920 | tf_op jit(solution)/shard_map/ppermute | solution.py:292
  56.6 10.9 %collective-permute-start.11 = (bf16[2,3,64,128]{3,2,1,0:T(8,128)(2,1)S(1)}, bf16[2,3,64,128]{3,2,1,0:T(8,128)(2,1)S(1)}, u32[]{:S(2)}, u32[]{:S(2)}) collective-permute-start(bf16[2,3,64,128]{3,2,1,0:T(8,128)(2,1)S(1)} %get-tuple-element.61), channel_id=1, source_target_pairs={{0,2},{1,3},{2,0},{3,1},{4,6},{5,7},{6,4},{7,5},{8,10},{9,11},{10,... | collective-permute-start | bytes 294920 | tf_op jit(solution)/shard_map/ppermute | solution.py:292
  59.9 14.0 %collective-permute-start.12 = (bf16[2,3,64,128]{3,2,1,0:T(8,128)(2,1)S(1)}, bf16[2,3,64,128]{3,2,1,0:T(8,128)(2,1)S(1)}, u32[]{:S(2)}, u32[]{:S(2)}) collective-permute-start(bf16[2,3,64,128]{3,2,1,0:T(8,128)(2,1)S(1)} %get-tuple-element.62), channel_id=1, source_target_pairs={{0,4},{1,5},{2,6},{3,7},{4,0},{5,1},{6,2},{7,3},{8,12},{9,13},{10,... | collective-permute-start | bytes 294920 | tf_op jit(solution)/shard_map/ppermute | solution.py:292
  60.9 15.4 %collective-permute-start.13 = (bf16[2,3,64,128]{3,2,1,0:T(8,128)(2,1)S(1)}, bf16[2,3,64,128]{3,2,1,0:T(8,128)(2,1)S(1)}, u32[]{:S(2)}, u32[]{:S(2)}) collective-permute-start(bf16[2,3,64,128]{3,2,1,0:T(8,128)(2,1)S(1)} %get-tuple-element.63), channel_id=1, source_target_pairs={{0,5},{1,4},{2,7},{3,6},{4,1},{5,0},{6,3},{7,2},{8,13},{9,12},{10,... | collective-permute-start | bytes 294920 | tf_op jit(solution)/shard_map/ppermute | solution.py:292
  63.1 13.2 %collective-permute-start.14 = (bf16[2,3,64,128]{3,2,1,0:T(8,128)(2,1)S(1)}, bf16[2,3,64,128]{3,2,1,0:T(8,128)(2,1)S(1)}, u32[]{:S(2)}, u32[]{:S(2)}) collective-permute-start(bf16[2,3,64,128]{3,2,1,0:T(8,128)(2,1)S(1)} %get-tuple-element.64), channel_id=1, source_target_pairs={{0,6},{1,7},{2,4},{3,5},{4,2},{5,3},{6,0},{7,1},{8,14},{9,15},{10,... | collective-permute-start | bytes 294920 | tf_op jit(solution)/shard_map/ppermute | solution.py:292
  65.3 11.1 %collective-permute-start.15 = (bf16[2,3,64,128]{3,2,1,0:T(8,128)(2,1)S(1)}, bf16[2,3,64,128]{3,2,1,0:T(8,128)(2,1)S(1)}, u32[]{:S(2)}, u32[]{:S(2)}) collective-permute-start(bf16[2,3,64,128]{3,2,1,0:T(8,128)(2,1)S(1)} %get-tuple-element.65), channel_id=1, source_target_pairs={{0,7},{1,6},{2,5},{3,4},{4,3},{5,2},{6,1},{7,0},{8,15},{9,14},{10,... | collective-permute-start | bytes 294920 | tf_op jit(solution)/shard_map/ppermute | solution.py:292
  67.5 9.4 %collective-permute-start.16 = (bf16[2,3,64,128]{3,2,1,0:T(8,128)(2,1)S(1)}, bf16[2,3,64,128]{3,2,1,0:T(8,128)(2,1)S(1)}, u32[]{:S(2)}, u32[]{:S(2)}) collective-permute-start(bf16[2,3,64,128]{3,2,1,0:T(8,128)(2,1)S(1)} %get-tuple-element.66), channel_id=1, source_target_pairs={{0,3},{1,2},{2,1},{3,0},{4,7},{5,6},{6,5},{7,4},{8,11},{9,10},{10,... | collective-permute-start | bytes 294920 | tf_op jit(solution)/shard_map/ppermute | solution.py:292
  90.0 12.2 %collective-permute-start.19 = (bf16[2,256,128]{2,1,0:T(8,128)(2,1)S(1)}, bf16[2,256,128]{2,1,0:T(8,128)(2,1)S(1)}, u32[]{:S(2)}, u32[]{:S(2)}) collective-permute-start(bf16[2,256,128]{2,1,0:T(8,128)(2,1)S(1)} %get-tuple-element.77), channel_id=1, source_target_pairs={{0,24},{8,16},{16,8},{24,0},{1,25},{9,17},{17,9},{25,1},{2,26},{10... | collective-permute-start | bytes 393224 | tf_op jit(solution)/shard_map/ppermute | solution.py:296
  90.5 7.5 %collective-permute-start.20 = (bf16[2,3,64,128]{3,2,1,0:T(8,128)(2,1)S(1)}, bf16[2,3,64,128]{3,2,1,0:T(8,128)(2,1)S(1)}, u32[]{:S(2)}, u32[]{:S(2)}) collective-permute-start(bf16[2,3,64,128]{3,2,1,0:T(8,128)(2,1)S(1)} %get-tuple-element.79), channel_id=1, source_target_pairs={{0,1},{1,0},{2,3},{3,2},{4,5},{5,4},{6,7},{7,6},{8,9},{9,8},{10,11... | collective-permute-start | bytes 294920 | tf_op jit(solution)/shard_map/ppermute | solution.py:292
  90.8 8.5 %collective-permute-start.21 = (bf16[2,3,64,128]{3,2,1,0:T(8,128)(2,1)S(1)}, bf16[2,3,64,128]{3,2,1,0:T(8,128)(2,1)S(1)}, u32[]{:S(2)}, u32[]{:S(2)}) collective-permute-start(bf16[2,3,64,128]{3,2,1,0:T(8,128)(2,1)S(1)} %get-tuple-element.80), channel_id=1, source_target_pairs={{0,2},{1,3},{2,0},{3,1},{4,6},{5,7},{6,4},{7,5},{8,10},{9,11},{10,... | collective-permute-start | bytes 294920 | tf_op jit(solution)/shard_map/ppermute | solution.py:292
  94.6 15.1 %collective-permute-start.22 = (bf16[2,3,64,128]{3,2,1,0:T(8,128)(2,1)S(1)}, bf16[2,3,64,128]{3,2,1,0:T(8,128)(2,1)S(1)}, u32[]{:S(2)}, u32[]{:S(2)}) collective-permute-start(bf16[2,3,64,128]{3,2,1,0:T(8,128)(2,1)S(1)} %get-tuple-element.81), channel_id=1, source_target_pairs={{0,4},{1,5},{2,6},{3,7},{4,0},{5,1},{6,2},{7,3},{8,12},{9,13},{10,... | collective-permute-start | bytes 294920 | tf_op jit(solution)/shard_map/ppermute | solution.py:292
  94.6 17.6 %collective-permute-start.23 = (bf16[2,3,64,128]{3,2,1,0:T(8,128)(2,1)S(1)}, bf16[2,3,64,128]{3,2,1,0:T(8,128)(2,1)S(1)}, u32[]{:S(2)}, u32[]{:S(2)}) collective-permute-start(bf16[2,3,64,128]{3,2,1,0:T(8,128)(2,1)S(1)} %get-tuple-element.82), channel_id=1, source_target_pairs={{0,5},{1,4},{2,7},{3,6},{4,1},{5,0},{6,3},{7,2},{8,13},{9,12},{10,... | collective-permute-start | bytes 294920 | tf_op jit(solution)/shard_map/ppermute | solution.py:292
  98.0 15.2 %collective-permute-start.24 = (bf16[2,3,64,128]{3,2,1,0:T(8,128)(2,1)S(1)}, bf16[2,3,64,128]{3,2,1,0:T(8,128)(2,1)S(1)}, u32[]{:S(2)}, u32[]{:S(2)}) collective-permute-start(bf16[2,3,64,128]{3,2,1,0:T(8,128)(2,1)S(1)} %get-tuple-element.83), channel_id=1, source_target_pairs={{0,6},{1,7},{2,4},{3,5},{4,2},{5,3},{6,0},{7,1},{8,14},{9,15},{10,... | collective-permute-start | bytes 294920 | tf_op jit(solution)/shard_map/ppermute | solution.py:292
  99.3 13.9 %collective-permute-start.25 = (bf16[2,3,64,128]{3,2,1,0:T(8,128)(2,1)S(1)}, bf16[2,3,64,128]{3,2,1,0:T(8,128)(2,1)S(1)}, u32[]{:S(2)}, u32[]{:S(2)}) collective-permute-start(bf16[2,3,64,128]{3,2,1,0:T(8,128)(2,1)S(1)} %get-tuple-element.84), channel_id=1, source_target_pairs={{0,7},{1,6},{2,5},{3,4},{4,3},{5,2},{6,1},{7,0},{8,15},{9,14},{10,... | collective-permute-start | bytes 294920 | tf_op jit(solution)/shard_map/ppermute | solution.py:292
  102.2 11.8 %collective-permute-start.26 = (bf16[2,3,64,128]{3,2,1,0:T(8,128)(2,1)S(1)}, bf16[2,3,64,128]{3,2,1,0:T(8,128)(2,1)S(1)}, u32[]{:S(2)}, u32[]{:S(2)}) collective-permute-start(bf16[2,3,64,128]{3,2,1,0:T(8,128)(2,1)S(1)} %get-tuple-element.85), channel_id=1, source_target_pairs={{0,3},{1,2},{2,1},{3,0},{4,7},{5,6},{6,5},{7,4},{8,11},{9,10},{10,... | collective-permute-start | bytes 294920 | tf_op jit(solution)/shard_map/ppermute | solution.py:292
  109.7 7.2 %collective-permute-start.17 = (bf16[2,256,128]{2,1,0:T(8,128)(2,1)S(1)}, bf16[2,256,128]{2,1,0:T(8,128)(2,1)S(1)}, u32[]{:S(2)}, u32[]{:S(2)}) collective-permute-start(bf16[2,256,128]{2,1,0:T(8,128)(2,1)S(1)} %get-tuple-element.75), channel_id=1, source_target_pairs={{0,8},{8,0},{16,24},{24,16},{1,9},{9,1},{17,25},{25,17},{2,10},{10... | collective-permute-start | bytes 393224 | tf_op jit(solution)/shard_map/ppermute | solution.py:296
  112.2 5.1 %collective-permute-start.18 = (bf16[2,256,128]{2,1,0:T(8,128)(2,1)S(1)}, bf16[2,256,128]{2,1,0:T(8,128)(2,1)S(1)}, u32[]{:S(2)}, u32[]{:S(2)}) collective-permute-start(bf16[2,256,128]{2,1,0:T(8,128)(2,1)S(1)} %get-tuple-element.76), channel_id=1, source_target_pairs={{0,16},{8,24},{16,0},{24,8},{1,17},{9,25},{17,1},{25,9},{2,18},{10... | collective-permute-start | bytes 393224 | tf_op jit(solution)/shard_map/ppermute | solution.py:296
  115.0 2.3 %collective-permute-start.27 = (bf16[2,256,128]{2,1,0:T(8,128)(2,1)S(1)}, bf16[2,256,128]{2,1,0:T(8,128)(2,1)S(1)}, u32[]{:S(2)}, u32[]{:S(2)}) collective-permute-start(bf16[2,256,128]{2,1,0:T(8,128)(2,1)S(1)} %get-tuple-element.87), channel_id=1, source_target_pairs={{0,8},{8,0},{16,24},{24,16},{1,9},{9,1},{17,25},{25,17},{2,10},{10... | collective-permute-start | bytes 393224 | tf_op jit(solution)/shard_map/ppermute | solution.py:296
  115.0 6.4 %collective-permute-start.28 = (bf16[2,256,128]{2,1,0:T(8,128)(2,1)S(1)}, bf16[2,256,128]{2,1,0:T(8,128)(2,1)S(1)}, u32[]{:S(2)}, u32[]{:S(2)}) collective-permute-start(bf16[2,256,128]{2,1,0:T(8,128)(2,1)S(1)} %get-tuple-element.88), channel_id=1, source_target_pairs={{0,16},{8,24},{16,0},{24,8},{1,17},{9,25},{17,1},{25,9},{2,18},{10... | collective-permute-start | bytes 393224 | tf_op jit(solution)/shard_map/ppermute | solution.py:296
  115.6 7.7 %collective-permute-start.29 = (bf16[2,256,128]{2,1,0:T(8,128)(2,1)S(1)}, bf16[2,256,128]{2,1,0:T(8,128)(2,1)S(1)}, u32[]{:S(2)}, u32[]{:S(2)}) collective-permute-start(bf16[2,256,128]{2,1,0:T(8,128)(2,1)S(1)} %get-tuple-element.89), channel_id=1, source_target_pairs={{0,24},{8,16},{16,8},{24,0},{1,25},{9,17},{17,9},{25,1},{2,26},{10... | collective-permute-start | bytes 393224 | tf_op jit(solution)/shard_map/ppermute | solution.py:296

commit v11 on v10

--- a/solution.py
+++ b/solution.py
@@ -98,10 +98,10 @@
             out[kv, s] = table[kv, block]
 
 
-def pick_kernel(place, asked, *refs, heads, shard_count):
+def pick_kernel(place, asked, *refs, heads, steps, head, shard_count):
     own, outs, table = refs[:heads], refs[heads:-1], refs[-1]
-    fill_table(place, own, 0, table)
-    for r, out in zip(steps_of(shard_count), outs):
+    fill_table(place, own, head, table)
+    for r, out in zip(steps, outs):
         pick(table, asked, partner(place[0], r, shard_count), out)
 
 
@@ -191,7 +191,7 @@
 
             @pl.when(there > place[0])
             def _():
-                if last:
+                if last or r >= shard_count // 2:
                     out[...] = jnp.zeros_like(out)
                 else:
                     pick(table, asked, there, out)
@@ -340,26 +340,37 @@
     requests, source = requests_of(after(block_lists, *own[1:2]).reshape(-1), blocks_here, shard_index, shard_count)
     asked = lax.all_to_all(requests, "ctx", split_axis=0, concat_axis=0, tiled=True)
 
+    steps = steps_of(shard_count)
+    wide = [r for r in steps if r >= shard_count // 2]
+
     def exchange(arrays):
-        return [send(x, "ctx", shard_count, r) for r, x in zip(steps_of(shard_count), arrays)]
-
-    picked = call(
-        functools.partial(pick_kernel, heads=heads, shard_count=shard_count),
-        [place, asked],
-        own,
-        [bf16(2, CAP, BLK, HEAD_DIM)] * (shard_count - 1),
-        [pltpu.VMEM((2, blocks_here, BLK, HEAD_DIM), jnp.bfloat16)],
-        "pick",
-    )
-    come, earlier, nears, backs = exchange(picked), [], [], []
+        return {r: send(x, "ctx", shard_count, r) for r, x in arrays}
+
+    def picked(head, steps):
+        arrays = call(
+            functools.partial(pick_kernel, heads=heads, steps=steps, head=head, shard_count=shard_count),
+            [place, asked],
+            own,
+            [bf16(2, CAP, BLK, HEAD_DIM)] * len(steps),
+            [pltpu.VMEM((2, blocks_here, BLK, HEAD_DIM), jnp.bfloat16)],
+            "pick",
+        )
+        return list(zip(steps, arrays))
+
+    come, earlier, nears, backs = exchange(picked(0, steps)), [], [], []
     for h in range(head_count):
+        last = h == head_count - 1
+        ahead = {}
+        if not last:
+            ahead = exchange([(r, after(x, *come.values())) for r, x in picked(h + 1, wide)])
         attended, query_grad, near, *go = attend(
-            place, source, asked, queries, out_grad, own, come, h, h == head_count - 1, earlier, shard_count
+            place, source, asked, queries, out_grad, own, [come[r] for r in steps], h, last, earlier, shard_count
         )
         earlier = [attended, query_grad]
         nears.append(near)
-        come = exchange(go)
-        backs.append(come)
+        back = exchange(zip(steps, go))
+        backs.append([back[r] for r in steps])
+        come = {**back, **ahead}
     done = []
     for h in range(head_count):
         sums = call(

time: 125 us -> 120 us (0.960)
  waiting for transfers between devices: 42.8 us -> 32.8 us
  starting transfers between devices: 45.6 us -> 50.2 us
    ppermute x24 -> x28, waiting for transfers between devices: 34.4 us -> 24.4 us  [send(): lax.ppermute(x, axis, [(i, partner(i, r, count)) for i in range(count)])]
    ppermute x24 -> x28, starting transfers between devices: 36.2 us -> 39.8 us  [send(): lax.ppermute(x, axis, [(i, partner(i, r, count)) for i in range(count)])]
    pallas_call x5 -> x6, Pallas kernels: 7.16 us -> 7.83 us  [call(): pl.pallas_call(kernel, grid_spec=pltpu.PrefetchScalarGridSpec(num_scalar_...]
  transfers between devices with their start and end apart: 31 -> 35, of which waited for: 14 -> 13; matrix products, arithmetic and copies ran while one was open for 2% -> 2% of each run, Pallas kernels for 1% -> 22%
where the time goes in v11:
time: 120 us
  starting transfers between devices  50.2 us (42%)
  waiting for transfers between devices  32.8 us (27%)
  Pallas kernels  32.1 us (27%)
  local copies, waits for them, and re-layouts  2.48 us (2%)
  other arithmetic  1.79 us (1%)
    ppermute x28, starting transfers between devices, send(): lax.ppermute(x, axis, [(i, partner(i, r, count)) for i in range(count)])  39.8 us
    ppermute x28, waiting for transfers between devices, send(): lax.ppermute(x, axis, [(i, partner(i, r, count)) for i in range(count)])  24.4 us
    pallas_call x2, Pallas kernels, attend(): pl.pallas_call(functools.partial(attend_kernel, heads=len(own), head=head...  24.3 us
    pallas_call x6, Pallas kernels, call(): pl.pallas_call(kernel, grid_spec=pltpu.PrefetchScalarGridSpec(num_scalar_...  7.83 us
    ppermute x6, waiting for transfers between devices, send_back(): lax.ppermute(x, axis, [(i, origin(i, r, count)) for i in range(count)])  6.4 us
    all_to_all x1, starting transfers between devices, per_device(): lax.all_to_all(requests, 'ctx', split_axis=0, concat_axis=0, tiled=True)  6.07 us
    ppermute x6, starting transfers between devices, send_back(): lax.ppermute(x, axis, [(i, origin(i, r, count)) for i in range(count)])  4.3 us
  transfers between devices with their start and end apart: 35, of which 13 were waited for; matrix products, arithmetic and copies ran while one was open for 2% of the time, Pallas kernels for 22%

profile of v11, /device:TPU:0, one launch (start us, length us, event | category | flops | bytes accessed | tf_op | source)
XLA Modules:
  0.0 120.1 jit_solution(12271763391377994193)
XLA Ops:
  1.2 3.0 %split.1 = (bf16[2,2,256,128]{3,2,1,0:T(8,128)(2,1)}, bf16[2,2,256,128]{3,2,1,0:T(8,128)(2,1)}, bf16[2,2,256,128]{3,2,1,0:T(8,128)(2,1)}, bf16[2,2,256,128]{3,2,1,0:T(8,128)(2,1)}) custom-call(s32[2]{0:T(128)} %pad_add_fusion.place, bf16[256,1024]{1,0:T(8,128)(2,1)} %k_ref.1, bf16[256,1024]{1,0:T(8,128)(2,1)} %v_ref.1), custom_call_target="tpu_custom_call" | custom-call | tf_op jit(solution)/shard_map/split/pallas_call | solution.py:237
  4.8 2.6 %collective-permute-start.1 = (bf16[2,2,256,128]{3,2,1,0:T(8,128)(2,1)}, bf16[2,2,256,128]{3,2,1,0:T(8,128)(2,1)S(1)}, u32[]{:S(2)}, u32[]{:S(2)}) collective-permute-start(bf16[2,2,256,128]{3,2,1,0:T(8,128)(2,1)} %get-tuple-element.59), channel_id=1, source_target_pairs={{0,16},{8,24},{16,0},{24,8},{1,17},{9,25},{17,1},{25,9},{2,18},{10... | collective-permute-start | bytes 786440 | tf_op jit(solution)/shard_map/ppermute | solution.py:292
  7.4 0.8 copy.14
  8.7 0.7 select_reduce_fusion
  9.4 6.1 %all-to-all-start = ((s32[8,1,128]{2,1,0:T(1,128)}), s32[8,1,128]{2,1,0:T(1,128)S(1)}, u32[]{:S(2)}, u32[]{:S(2)}) async-start(s32[8,1,128]{2,1,0:T(1,128)} %bitcast.3), calls=%async_computation | async-start | bytes 8192 | tf_op jit(solution)/shard_map/all_to_all | solution.py:341
  15.5 4.3 %collective-permute-done.2.refs_3_ = bf16[2,2,256,128]{3,2,1,0:T(8,128)(2,1)S(1)} collective-permute-done((bf16[2,2,256,128]{3,2,1,0:T(8,128)(2,1)}, bf16[2,2,256,128]{3,2,1,0:T(8,128)(2,1)S(1)}, u32[]{:S(2)}, u32[]{:S(2)}) %collective-permute-start.2) | collective-permute-done | bytes 262176 | tf_op jit(solution)/shard_map/ppermute | solution.py:292
  19.8 2.0 %all-to-all-done = s32[8,1,128]{2,1,0:T(1,128)S(1)} async-done(((s32[8,1,128]{2,1,0:T(1,128)}), s32[8,1,128]{2,1,0:T(1,128)S(1)}, u32[]{:S(2)}, u32[]{:S(2)}) %all-to-all-start) | async-done | bytes 4128 | tf_op jit(solution)/shard_map/all_to_all | solution.py:341
  21.8 0.9 copy-done
  23.4 0.7 pick.2
  24.1 0.6 collective-permute-start.3
  25.5 2.7 %collective-permute-start.5 = (bf16[2,3,64,128]{3,2,1,0:T(8,128)(2,1)S(1)}, bf16[2,3,64,128]{3,2,1,0:T(8,128)(2,1)S(1)}, u32[]{:S(2)}, u32[]{:S(2)}) collective-permute-start(bf16[2,3,64,128]{3,2,1,0:T(8,128)(2,1)S(1)} %get-tuple-element.63), channel_id=1, source_target_pairs={{0,4},{1,5},{2,6},{3,7},{4,0},{5,1},{6,2},{7,3},{8,12},{9,13},{10,... | collective-permute-start | bytes 294920 | tf_op jit(solution)/shard_map/ppermute | solution.py:292
  28.1 1.2 collective-permute-start.6
  29.3 1.6 %collective-permute-start.7 = (bf16[2,3,64,128]{3,2,1,0:T(8,128)(2,1)S(1)}, bf16[2,3,64,128]{3,2,1,0:T(8,128)(2,1)S(1)}, u32[]{:S(2)}, u32[]{:S(2)}) collective-permute-start(bf16[2,3,64,128]{3,2,1,0:T(8,128)(2,1)S(1)} %get-tuple-element.65), channel_id=1, source_target_pairs={{0,6},{1,7},{2,4},{3,5},{4,2},{5,3},{6,0},{7,1},{8,14},{9,15},{10,... | collective-permute-start | bytes 294920 | tf_op jit(solution)/shard_map/ppermute | solution.py:292
  30.9 2.3 %collective-permute-start.8 = (bf16[2,3,64,128]{3,2,1,0:T(8,128)(2,1)S(1)}, bf16[2,3,64,128]{3,2,1,0:T(8,128)(2,1)S(1)}, u32[]{:S(2)}, u32[]{:S(2)}) collective-permute-start(bf16[2,3,64,128]{3,2,1,0:T(8,128)(2,1)S(1)} %get-tuple-element.66), channel_id=1, source_target_pairs={{0,7},{1,6},{2,5},{3,4},{4,3},{5,2},{6,1},{7,0},{8,15},{9,14},{10,... | collective-permute-start | bytes 294920 | tf_op jit(solution)/shard_map/ppermute | solution.py:292
  33.7 0.7 pick.3
  34.4 5.6 %collective-permute-done.5.refs_6_ = bf16[2,3,64,128]{3,2,1,0:T(8,128)(2,1)S(1)} collective-permute-done((bf16[2,3,64,128]{3,2,1,0:T(8,128)(2,1)S(1)}, bf16[2,3,64,128]{3,2,1,0:T(8,128)(2,1)S(1)}, u32[]{:S(2)}, u32[]{:S(2)}) %collective-permute-start.5) | collective-permute-done | bytes 98336 | tf_op jit(solution)/shard_map/ppermute | solution.py:292
  40.0 2.2 %collective-permute-done.6.refs_7_ = bf16[2,3,64,128]{3,2,1,0:T(8,128)(2,1)S(1)} collective-permute-done((bf16[2,3,64,128]{3,2,1,0:T(8,128)(2,1)S(1)}, bf16[2,3,64,128]{3,2,1,0:T(8,128)(2,1)S(1)}, u32[]{:S(2)}, u32[]{:S(2)}) %collective-permute-start.6) | collective-permute-done | bytes 98336 | tf_op jit(solution)/shard_map/ppermute | solution.py:292
  42.2 1.3 %collective-permute-done.9.refs_10_ = bf16[2,3,64,128]{3,2,1,0:T(8,128)(2,1)S(1)} collective-permute-done((bf16[2,3,64,128]{3,2,1,0:T(8,128)(2,1)S(1)}, bf16[2,3,64,128]{3,2,1,0:T(8,128)(2,1)S(1)}, u32[]{:S(2)}, u32[]{:S(2)}) %collective-permute-start.9) | collective-permute-done | bytes 98336 | tf_op jit(solution)/shard_map/ppermute | solution.py:292
  43.5 3.7 %collective-permute-start.12 = (bf16[2,3,64,128]{3,2,1,0:T(8,128)(2,1)S(1)}, bf16[2,3,64,128]{3,2,1,0:T(8,128)(2,1)S(1)}, u32[]{:S(2)}, u32[]{:S(2)}) collective-permute-start(bf16[2,3,64,128]{3,2,1,0:T(8,128)(2,1)S(1)} %get-tuple-element.71), channel_id=1, source_target_pairs={{0,4},{1,5},{2,6},{3,7},{4,0},{5,1},{6,2},{7,3},{8,12},{9,13},{10,... | collective-permute-start | bytes 294920 | tf_op jit(solution)/shard_map/ppermute | solution.py:292
  47.2 0.9 collective-permute-start.13
  48.2 1.3 %collective-permute-start.14 = (bf16[2,3,64,128]{3,2,1,0:T(8,128)(2,1)S(1)}, bf16[2,3,64,128]{3,2,1,0:T(8,128)(2,1)S(1)}, u32[]{:S(2)}, u32[]{:S(2)}) collective-permute-start(bf16[2,3,64,128]{3,2,1,0:T(8,128)(2,1)S(1)} %get-tuple-element.75), channel_id=1, source_target_pairs={{0,6},{1,7},{2,4},{3,5},{4,2},{5,3},{6,0},{7,1},{8,14},{9,15},{10,... | collective-permute-start | bytes 294920 | tf_op jit(solution)/shard_map/ppermute | solution.py:292
  49.5 2.5 %collective-permute-start.15 = (bf16[2,3,64,128]{3,2,1,0:T(8,128)(2,1)S(1)}, bf16[2,3,64,128]{3,2,1,0:T(8,128)(2,1)S(1)}, u32[]{:S(2)}, u32[]{:S(2)}) collective-permute-start(bf16[2,3,64,128]{3,2,1,0:T(8,128)(2,1)S(1)} %get-tuple-element.77), channel_id=1, source_target_pairs={{0,7},{1,6},{2,5},{3,4},{4,3},{5,2},{6,1},{7,0},{8,15},{9,14},{10,... | collective-permute-start | bytes 294920 | tf_op jit(solution)/shard_map/ppermute | solution.py:292
  52.0 12.1 %attend.2 = (bf16[1024,1024]{1,0:T(8,128)(2,1)}, bf16[1024,1024]{1,0:T(8,128)(2,1)}, f32[2,16,64,128]{3,2,1,0:T(8,128)S(1)}, bf16[2,3,64,128]{3,2,1,0:T(8,128)(2...) custom-call(s32[2]{0:T(128)S(1)} %copy-done.1, ...), custom_call_target="tpu_custom_call" | custom-call | flops 3221225472 | bytes 20971520 | tf_op jit(solution)/shard_map/attend/pallas_call | solution.py:261
  64.1 1.5 %collective-permute-start.10 = (bf16[2,3,64,128]{3,2,1,0:T(8,128)(2,1)S(1)}, bf16[2,3,64,128]{3,2,1,0:T(8,128)(2,1)S(1)}, u32[]{:S(2)}, u32[]{:S(2)}) collective-permute-start(bf16[2,3,64,128]{3,2,1,0:T(8,128)(2,1)S(1)} %get-tuple-element.68), channel_id=1, source_target_pairs={{0,1},{1,0},{2,3},{3,2},{4,5},{5,4},{6,7},{7,6},{8,9},{9,8},{10,11... | collective-permute-start | bytes 294920 | tf_op jit(solution)/shard_map/ppermute | solution.py:292
  65.7 1.9 %collective-permute-start.16 = (bf16[2,3,64,128]{3,2,1,0:T(8,128)(2,1)S(1)}, bf16[2,3,64,128]{3,2,1,0:T(8,128)(2,1)S(1)}, u32[]{:S(2)}, u32[]{:S(2)}) collective-permute-start(bf16[2,3,64,128]{3,2,1,0:T(8,128)(2,1)S(1)} %get-tuple-element.78), channel_id=1, source_target_pairs={{0,3},{1,2},{2,1},{3,0},{4,7},{5,6},{6,5},{7,4},{8,11},{9,10},{10,... | collective-permute-start | bytes 294920 | tf_op jit(solution)/shard_map/ppermute | solution.py:292
  67.6 1.1 collective-permute-start.17
  68.7 2.7 %collective-permute-start.18 = (bf16[2,3,64,128]{3,2,1,0:T(8,128)(2,1)S(1)}, bf16[2,3,64,128]{3,2,1,0:T(8,128)(2,1)S(1)}, u32[]{:S(2)}, u32[]{:S(2)}) collective-permute-start(bf16[2,3,64,128]{3,2,1,0:T(8,128)(2,1)S(1)} %get-tuple-element.87), channel_id=1, source_target_pairs={{0,5},{1,4},{2,7},{3,6},{4,1},{5,0},{6,3},{7,2},{8,13},{9,12},{10,... | collective-permute-start | bytes 294920 | tf_op jit(solution)/shard_map/ppermute | solution.py:292
  71.4 1.3 %collective-permute-start.19 = (bf16[2,3,64,128]{3,2,1,0:T(8,128)(2,1)S(1)}, bf16[2,3,64,128]{3,2,1,0:T(8,128)(2,1)S(1)}, u32[]{:S(2)}, u32[]{:S(2)}) collective-permute-start(bf16[2,3,64,128]{3,2,1,0:T(8,128)(2,1)S(1)} %get-tuple-element.88), channel_id=1, source_target_pairs={{0,6},{1,7},{2,4},{3,5},{4,2},{5,3},{6,0},{7,1},{8,14},{9,15},{10,... | collective-permute-start | bytes 294920 | tf_op jit(solution)/shard_map/ppermute | solution.py:292
  72.8 2.5 %collective-permute-start.20 = (bf16[2,3,64,128]{3,2,1,0:T(8,128)(2,1)S(1)}, bf16[2,3,64,128]{3,2,1,0:T(8,128)(2,1)S(1)}, u32[]{:S(2)}, u32[]{:S(2)}) collective-permute-start(bf16[2,3,64,128]{3,2,1,0:T(8,128)(2,1)S(1)} %get-tuple-element.89), channel_id=1, source_target_pairs={{0,7},{1,6},{2,5},{3,4},{4,3},{5,2},{6,1},{7,0},{8,15},{9,14},{10,... | collective-permute-start | bytes 294920 | tf_op jit(solution)/shard_map/ppermute | solution.py:292
  75.3 12.1 %attend.3 = (bf16[1024,1024]{1,0:T(8,128)(2,1)}, bf16[1024,1024]{1,0:T(8,128)(2,1)}, f32[2,16,64,128]{3,2,1,0:T(8,128)S(1)}, bf16[2,3,64,128]{3,2,1,0:T(8,128)(2...) custom-call(s32[2]{0:T(128)S(1)} %copy-done.1, ...), custom_call_target="tpu_custom_call", output_to_operand_aliasing={{0}: (16, {}), {1}: (17, {})} | custom-call | flops 3221225472 | bytes 20971520 | tf_op jit(solution)/shard_map/attend/pallas_call | solution.py:261
  87.4 0.9 gather_sum.2
  88.4 1.5 %collective-permute-start.24 = (bf16[2,3,64,128]{3,2,1,0:T(8,128)(2,1)S(1)}, bf16[2,3,64,128]{3,2,1,0:T(8,128)(2,1)S(1)}, u32[]{:S(2)}, u32[]{:S(2)}) collective-permute-start(bf16[2,3,64,128]{3,2,1,0:T(8,128)(2,1)S(1)} %get-tuple-element.95), channel_id=1, source_target_pairs={{0,1},{1,0},{2,3},{3,2},{4,5},{5,4},{6,7},{7,6},{8,9},{9,8},{10,11... | collective-permute-start | bytes 294920 | tf_op jit(solution)/shard_map/ppermute | solution.py:292
  89.9 1.8 %collective-permute-start.26 = (bf16[2,3,64,128]{3,2,1,0:T(8,128)(2,1)S(1)}, bf16[2,3,64,128]{3,2,1,0:T(8,128)(2,1)S(1)}, u32[]{:S(2)}, u32[]{:S(2)}) collective-permute-start(bf16[2,3,64,128]{3,2,1,0:T(8,128)(2,1)S(1)} %get-tuple-element.97), channel_id=1, source_target_pairs={{0,4},{1,5},{2,6},{3,7},{4,0},{5,1},{6,2},{7,3},{8,12},{9,13},{10,... | collective-permute-start | bytes 294920 | tf_op jit(solution)/shard_map/ppermute | solution.py:292
  91.7 1.2 collective-permute-start.27
  92.9 0.8 collective-permute-done.24.refs_0_
  93.7 1.5 %collective-permute-start.28 = (bf16[2,3,64,128]{3,2,1,0:T(8,128)(2,1)S(1)}, bf16[2,3,64,128]{3,2,1,0:T(8,128)(2,1)S(1)}, u32[]{:S(2)}, u32[]{:S(2)}) collective-permute-start(bf16[2,3,64,128]{3,2,1,0:T(8,128)(2,1)S(1)} %get-tuple-element.99), channel_id=1, source_target_pairs={{0,6},{1,7},{2,4},{3,5},{4,2},{5,3},{6,0},{7,1},{8,14},{9,15},{10,... | collective-permute-start | bytes 294920 | tf_op jit(solution)/shard_map/ppermute | solution.py:292
  95.2 1.6 %collective-permute-done.25.refs_1_ = bf16[2,3,64,128]{3,2,1,0:T(8,128)(2,1)S(1)} collective-permute-done((bf16[2,3,64,128]{3,2,1,0:T(8,128)(2,1)S(1)}, bf16[2,3,64,128]{3,2,1,0:T(8,128)(2,1)S(1)}, u32[]{:S(2)}, u32[]{:S(2)}) %collective-permute-start.25) | collective-permute-done | bytes 98336 | tf_op jit(solution)/shard_map/ppermute | solution.py:292
  96.8 1.6 %collective-permute-start.29 = (bf16[2,3,64,128]{3,2,1,0:T(8,128)(2,1)S(1)}, bf16[2,3,64,128]{3,2,1,0:T(8,128)(2,1)S(1)}, u32[]{:S(2)}, u32[]{:S(2)}) collective-permute-start(bf16[2,3,64,128]{3,2,1,0:T(8,128)(2,1)S(1)} %get-tuple-element.100), channel_id=1, source_target_pairs={{0,7},{1,6},{2,5},{3,4},{4,3},{5,2},{6,1},{7,0},{8,15},{9,14},{10,... | collective-permute-start | bytes 294920 | tf_op jit(solution)/shard_map/ppermute | solution.py:292
  98.4 6.4 %collective-permute-done.26.refs_2_ = bf16[2,3,64,128]{3,2,1,0:T(8,128)(2,1)S(1)} collective-permute-done((bf16[2,3,64,128]{3,2,1,0:T(8,128)(2,1)S(1)}, bf16[2,3,64,128]{3,2,1,0:T(8,128)(2,1)S(1)}, u32[]{:S(2)}, u32[]{:S(2)}) %collective-permute-start.26) | collective-permute-done | bytes 98336 | tf_op jit(solution)/shard_map/ppermute | solution.py:292
  104.8 0.6 collective-permute-start.21
  105.4 1.5 %collective-permute-done.27.refs_3_ = bf16[2,3,64,128]{3,2,1,0:T(8,128)(2,1)S(1)} collective-permute-done((bf16[2,3,64,128]{3,2,1,0:T(8,128)(2,1)S(1)}, bf16[2,3,64,128]{3,2,1,0:T(8,128)(2,1)S(1)}, u32[]{:S(2)}, u32[]{:S(2)}) %collective-permute-start.27) | collective-permute-done | bytes 98336 | tf_op jit(solution)/shard_map/ppermute | solution.py:292
  106.9 1.7 %collective-permute-start.22 = (bf16[2,256,128]{2,1,0:T(8,128)(2,1)S(1)}, bf16[2,256,128]{2,1,0:T(8,128)(2,1)S(1)}, u32[]{:S(2)}, u32[]{:S(2)}) collective-permute-start(bf16[2,256,128]{2,1,0:T(8,128)(2,1)S(1)} %get-tuple-element.92), channel_id=1, source_target_pairs={{0,16},{8,24},{16,0},{24,8},{1,17},{9,25},{17,1},{25,9},{2,18},{10... | collective-permute-start | bytes 393224 | tf_op jit(solution)/shard_map/ppermute | solution.py:296
  109.2 0.9 gather_sum.3
  110.2 0.9 collective-permute-start.32
  111.1 1.0 collective-permute-start.33
  112.7 3.9 %collective-permute-done.32.refs_6_ = bf16[2,256,128]{2,1,0:T(8,128)(2,1)S(1)} collective-permute-done((bf16[2,256,128]{2,1,0:T(8,128)(2,1)S(1)}, bf16[2,256,128]{2,1,0:T(8,128)(2,1)S(1)}, u32[]{:S(2)}, u32[]{:S(2)}) %collective-permute-start.32) | collective-permute-done | bytes 131104 | tf_op jit(solution)/shard_map/ppermute | solution.py:296
  116.6 1.9 %collective-permute-done.33.refs_7_ = bf16[2,256,128]{2,1,0:T(8,128)(2,1)S(1)} collective-permute-done((bf16[2,256,128]{2,1,0:T(8,128)(2,1)S(1)}, bf16[2,256,128]{2,1,0:T(8,128)(2,1)S(1)}, u32[]{:S(2)}, u32[]{:S(2)}) %collective-permute-start.33) | collective-permute-done | bytes 131104 | tf_op jit(solution)/shard_map/ppermute | solution.py:296
  118.5 1.6 %join.1 = (bf16[256,1024]{1,0:T(8,128)(2,1)}, bf16[256,1024]{1,0:T(8,128)(2,1)}) custom-call(s32[2]{0:T(128)S(1)} %copy-done.1, bf16[2,256,128]{2,1,0:T(8,128)(2,1)S(1)} %get-tuple-element.90.refs_0_, bf16[2,256,128]{2,1,0:T(8,128)(2,1)S(1)} %collective-permute-done.21.refs_1_, bf16[2,256,128]{2,1,0:T(8,128)(2,1)S(1)} %collective-permute-done.22.refs_2_, ...), custom_call_target="tpu_custom_call" | custom-call | tf_op jit(solution)/shard_map/join/pallas_call | solution.py:237
  (48 shorter events, 5.1 us)
Async XLA Ops:
  4.3 3.2 %collective-permute-start = (bf16[2,2,256,128]{3,2,1,0:T(8,128)(2,1)}, bf16[2,2,256,128]{3,2,1,0:T(8,128)(2,1)S(1)}, u32[]{:S(2)}, u32[]{:S(2)}) collective-permute-start(bf16[2,2,256,128]{3,2,1,0:T(8,128)(2,1)} %get-tuple-element.56), channel_id=1, source_target_pairs={{0,8},{8,0},{16,24},{24,16},{1,9},{9,1},{17,25},{25,17},{2,10},{10... | collective-permute-start | bytes 786440 | tf_op jit(solution)/shard_map/ppermute | solution.py:292
  4.8 10.7 %collective-permute-start.1 = (bf16[2,2,256,128]{3,2,1,0:T(8,128)(2,1)}, bf16[2,2,256,128]{3,2,1,0:T(8,128)(2,1)S(1)}, u32[]{:S(2)}, u32[]{:S(2)}) collective-permute-start(bf16[2,2,256,128]{3,2,1,0:T(8,128)(2,1)} %get-tuple-element.59), channel_id=1, source_target_pairs={{0,16},{8,24},{16,0},{24,8},{1,17},{9,25},{17,1},{25,9},{2,18},{10... | collective-permute-start | bytes 786440 | tf_op jit(solution)/shard_map/ppermute | solution.py:292
  7.3 12.5 %collective-permute-start.2 = (bf16[2,2,256,128]{3,2,1,0:T(8,128)(2,1)}, bf16[2,2,256,128]{3,2,1,0:T(8,128)(2,1)S(1)}, u32[]{:S(2)}, u32[]{:S(2)}) collective-permute-start(bf16[2,2,256,128]{3,2,1,0:T(8,128)(2,1)} %get-tuple-element.60), channel_id=1, source_target_pairs={{0,24},{8,16},{16,8},{24,0},{1,25},{9,17},{17,9},{25,1},{2,26},{10... | collective-permute-start | bytes 786440 | tf_op jit(solution)/shard_map/ppermute | solution.py:292
  9.4 12.5 %all-to-all-start = ((s32[8,1,128]{2,1,0:T(1,128)}), s32[8,1,128]{2,1,0:T(1,128)S(1)}, u32[]{:S(2)}, u32[]{:S(2)}) async-start(s32[8,1,128]{2,1,0:T(1,128)} %bitcast.3), calls=%async_computation | async-start | bytes 8192 | tf_op jit(solution)/shard_map/all_to_all | solution.py:341
  21.8 1.0 copy-start
  22.8 0.6 copy-start.1
  24.1 6.8 %collective-permute-start.3 = (bf16[2,3,64,128]{3,2,1,0:T(8,128)(2,1)S(1)}, bf16[2,3,64,128]{3,2,1,0:T(8,128)(2,1)S(1)}, u32[]{:S(2)}, u32[]{:S(2)}) collective-permute-start(bf16[2,3,64,128]{3,2,1,0:T(8,128)(2,1)S(1)} %get-tuple-element.61), channel_id=1, source_target_pairs={{0,1},{1,0},{2,3},{3,2},{4,5},{5,4},{6,7},{7,6},{8,9},{9,8},{10,11... | collective-permute-start | bytes 294920 | tf_op jit(solution)/shard_map/ppermute | solution.py:292
  24.7 8.5 %collective-permute-start.4 = (bf16[2,3,64,128]{3,2,1,0:T(8,128)(2,1)S(1)}, bf16[2,3,64,128]{3,2,1,0:T(8,128)(2,1)S(1)}, u32[]{:S(2)}, u32[]{:S(2)}) collective-permute-start(bf16[2,3,64,128]{3,2,1,0:T(8,128)(2,1)S(1)} %get-tuple-element.62), channel_id=1, source_target_pairs={{0,2},{1,3},{2,0},{3,1},{4,6},{5,7},{6,4},{7,5},{8,10},{9,11},{10,... | collective-permute-start | bytes 294920 | tf_op jit(solution)/shard_map/ppermute | solution.py:292
  25.5 14.5 %collective-permute-start.5 = (bf16[2,3,64,128]{3,2,1,0:T(8,128)(2,1)S(1)}, bf16[2,3,64,128]{3,2,1,0:T(8,128)(2,1)S(1)}, u32[]{:S(2)}, u32[]{:S(2)}) collective-permute-start(bf16[2,3,64,128]{3,2,1,0:T(8,128)(2,1)S(1)} %get-tuple-element.63), channel_id=1, source_target_pairs={{0,4},{1,5},{2,6},{3,7},{4,0},{5,1},{6,2},{7,3},{8,12},{9,13},{10,... | collective-permute-start | bytes 294920 | tf_op jit(solution)/shard_map/ppermute | solution.py:292
  28.1 14.1 %collective-permute-start.6 = (bf16[2,3,64,128]{3,2,1,0:T(8,128)(2,1)S(1)}, bf16[2,3,64,128]{3,2,1,0:T(8,128)(2,1)S(1)}, u32[]{:S(2)}, u32[]{:S(2)}) collective-permute-start(bf16[2,3,64,128]{3,2,1,0:T(8,128)(2,1)S(1)} %get-tuple-element.64), channel_id=1, source_target_pairs={{0,5},{1,4},{2,7},{3,6},{4,1},{5,0},{6,3},{7,2},{8,13},{9,12},{10,... | collective-permute-start | bytes 294920 | tf_op jit(solution)/shard_map/ppermute | solution.py:292
  29.3 12.9 %collective-permute-start.7 = (bf16[2,3,64,128]{3,2,1,0:T(8,128)(2,1)S(1)}, bf16[2,3,64,128]{3,2,1,0:T(8,128)(2,1)S(1)}, u32[]{:S(2)}, u32[]{:S(2)}) collective-permute-start(bf16[2,3,64,128]{3,2,1,0:T(8,128)(2,1)S(1)} %get-tuple-element.65), channel_id=1, source_target_pairs={{0,6},{1,7},{2,4},{3,5},{4,2},{5,3},{6,0},{7,1},{8,14},{9,15},{10,... | collective-permute-start | bytes 294920 | tf_op jit(solution)/shard_map/ppermute | solution.py:292
  30.9 11.3 %collective-permute-start.8 = (bf16[2,3,64,128]{3,2,1,0:T(8,128)(2,1)S(1)}, bf16[2,3,64,128]{3,2,1,0:T(8,128)(2,1)S(1)}, u32[]{:S(2)}, u32[]{:S(2)}) collective-permute-start(bf16[2,3,64,128]{3,2,1,0:T(8,128)(2,1)S(1)} %get-tuple-element.66), channel_id=1, source_target_pairs={{0,7},{1,6},{2,5},{3,4},{4,3},{5,2},{6,1},{7,0},{8,15},{9,14},{10,... | collective-permute-start | bytes 294920 | tf_op jit(solution)/shard_map/ppermute | solution.py:292
  33.2 10.3 %collective-permute-start.9 = (bf16[2,3,64,128]{3,2,1,0:T(8,128)(2,1)S(1)}, bf16[2,3,64,128]{3,2,1,0:T(8,128)(2,1)S(1)}, u32[]{:S(2)}, u32[]{:S(2)}) collective-permute-start(bf16[2,3,64,128]{3,2,1,0:T(8,128)(2,1)S(1)} %get-tuple-element.67), channel_id=1, source_target_pairs={{0,3},{1,2},{2,1},{3,0},{4,7},{5,6},{6,5},{7,4},{8,11},{9,10},{10,... | collective-permute-start | bytes 294920 | tf_op jit(solution)/shard_map/ppermute | solution.py:292
  43.5 22.1 %collective-permute-start.12 = (bf16[2,3,64,128]{3,2,1,0:T(8,128)(2,1)S(1)}, bf16[2,3,64,128]{3,2,1,0:T(8,128)(2,1)S(1)}, u32[]{:S(2)}, u32[]{:S(2)}) collective-permute-start(bf16[2,3,64,128]{3,2,1,0:T(8,128)(2,1)S(1)} %get-tuple-element.71), channel_id=1, source_target_pairs={{0,4},{1,5},{2,6},{3,7},{4,0},{5,1},{6,2},{7,3},{8,12},{9,13},{10,... | collective-permute-start | bytes 294920 | tf_op jit(solution)/shard_map/ppermute | solution.py:292
  47.2 18.5 %collective-permute-start.13 = (bf16[2,3,64,128]{3,2,1,0:T(8,128)(2,1)S(1)}, bf16[2,3,64,128]{3,2,1,0:T(8,128)(2,1)S(1)}, u32[]{:S(2)}, u32[]{:S(2)}) collective-permute-start(bf16[2,3,64,128]{3,2,1,0:T(8,128)(2,1)S(1)} %get-tuple-element.73), channel_id=1, source_target_pairs={{0,5},{1,4},{2,7},{3,6},{4,1},{5,0},{6,3},{7,2},{8,13},{9,12},{10,... | collective-permute-start | bytes 294920 | tf_op jit(solution)/shard_map/ppermute | solution.py:292
  48.2 19.5 %collective-permute-start.14 = (bf16[2,3,64,128]{3,2,1,0:T(8,128)(2,1)S(1)}, bf16[2,3,64,128]{3,2,1,0:T(8,128)(2,1)S(1)}, u32[]{:S(2)}, u32[]{:S(2)}) collective-permute-start(bf16[2,3,64,128]{3,2,1,0:T(8,128)(2,1)S(1)} %get-tuple-element.75), channel_id=1, source_target_pairs={{0,6},{1,7},{2,4},{3,5},{4,2},{5,3},{6,0},{7,1},{8,14},{9,15},{10,... | collective-permute-start | bytes 294920 | tf_op jit(solution)/shard_map/ppermute | solution.py:292
  49.5 19.2 %collective-permute-start.15 = (bf16[2,3,64,128]{3,2,1,0:T(8,128)(2,1)S(1)}, bf16[2,3,64,128]{3,2,1,0:T(8,128)(2,1)S(1)}, u32[]{:S(2)}, u32[]{:S(2)}) collective-permute-start(bf16[2,3,64,128]{3,2,1,0:T(8,128)(2,1)S(1)} %get-tuple-element.77), channel_id=1, source_target_pairs={{0,7},{1,6},{2,5},{3,4},{4,3},{5,2},{6,1},{7,0},{8,15},{9,14},{10,... | collective-permute-start | bytes 294920 | tf_op jit(solution)/shard_map/ppermute | solution.py:292
  64.1 7.3 %collective-permute-start.10 = (bf16[2,3,64,128]{3,2,1,0:T(8,128)(2,1)S(1)}, bf16[2,3,64,128]{3,2,1,0:T(8,128)(2,1)S(1)}, u32[]{:S(2)}, u32[]{:S(2)}) collective-permute-start(bf16[2,3,64,128]{3,2,1,0:T(8,128)(2,1)S(1)} %get-tuple-element.68), channel_id=1, source_target_pairs={{0,1},{1,0},{2,3},{3,2},{4,5},{5,4},{6,7},{7,6},{8,9},{9,8},{10,11... | collective-permute-start | bytes 294920 | tf_op jit(solution)/shard_map/ppermute | solution.py:292
  65.6 7.2 %collective-permute-start.11 = (bf16[2,3,64,128]{3,2,1,0:T(8,128)(2,1)S(1)}, bf16[2,3,64,128]{3,2,1,0:T(8,128)(2,1)S(1)}, u32[]{:S(2)}, u32[]{:S(2)}) collective-permute-start(bf16[2,3,64,128]{3,2,1,0:T(8,128)(2,1)S(1)} %get-tuple-element.69), channel_id=1, source_target_pairs={{0,2},{1,3},{2,0},{3,1},{4,6},{5,7},{6,4},{7,5},{8,10},{9,11},{10,... | collective-permute-start | bytes 294920 | tf_op jit(solution)/shard_map/ppermute | solution.py:292
  65.7 9.6 %collective-permute-start.16 = (bf16[2,3,64,128]{3,2,1,0:T(8,128)(2,1)S(1)}, bf16[2,3,64,128]{3,2,1,0:T(8,128)(2,1)S(1)}, u32[]{:S(2)}, u32[]{:S(2)}) collective-permute-start(bf16[2,3,64,128]{3,2,1,0:T(8,128)(2,1)S(1)} %get-tuple-element.78), channel_id=1, source_target_pairs={{0,3},{1,2},{2,1},{3,0},{4,7},{5,6},{6,5},{7,4},{8,11},{9,10},{10,... | collective-permute-start | bytes 294920 | tf_op jit(solution)/shard_map/ppermute | solution.py:292
  67.6 19.8 %collective-permute-start.17 = (bf16[2,3,64,128]{3,2,1,0:T(8,128)(2,1)S(1)}, bf16[2,3,64,128]{3,2,1,0:T(8,128)(2,1)S(1)}, u32[]{:S(2)}, u32[]{:S(2)}) collective-permute-start(bf16[2,3,64,128]{3,2,1,0:T(8,128)(2,1)S(1)} %get-tuple-element.86), channel_id=1, source_target_pairs={{0,4},{1,5},{2,6},{3,7},{4,0},{5,1},{6,2},{7,3},{8,12},{9,13},{10,... | collective-permute-start | bytes 294920 | tf_op jit(solution)/shard_map/ppermute | solution.py:292
  68.7 18.7 %collective-permute-start.18 = (bf16[2,3,64,128]{3,2,1,0:T(8,128)(2,1)S(1)}, bf16[2,3,64,128]{3,2,1,0:T(8,128)(2,1)S(1)}, u32[]{:S(2)}, u32[]{:S(2)}) collective-permute-start(bf16[2,3,64,128]{3,2,1,0:T(8,128)(2,1)S(1)} %get-tuple-element.87), channel_id=1, source_target_pairs={{0,5},{1,4},{2,7},{3,6},{4,1},{5,0},{6,3},{7,2},{8,13},{9,12},{10,... | collective-permute-start | bytes 294920 | tf_op jit(solution)/shard_map/ppermute | solution.py:292
  71.4 16.0 %collective-permute-start.19 = (bf16[2,3,64,128]{3,2,1,0:T(8,128)(2,1)S(1)}, bf16[2,3,64,128]{3,2,1,0:T(8,128)(2,1)S(1)}, u32[]{:S(2)}, u32[]{:S(2)}) collective-permute-start(bf16[2,3,64,128]{3,2,1,0:T(8,128)(2,1)S(1)} %get-tuple-element.88), channel_id=1, source_target_pairs={{0,6},{1,7},{2,4},{3,5},{4,2},{5,3},{6,0},{7,1},{8,14},{9,15},{10,... | collective-permute-start | bytes 294920 | tf_op jit(solution)/shard_map/ppermute | solution.py:292
  72.8 14.7 %collective-permute-start.20 = (bf16[2,3,64,128]{3,2,1,0:T(8,128)(2,1)S(1)}, bf16[2,3,64,128]{3,2,1,0:T(8,128)(2,1)S(1)}, u32[]{:S(2)}, u32[]{:S(2)}) collective-permute-start(bf16[2,3,64,128]{3,2,1,0:T(8,128)(2,1)S(1)} %get-tuple-element.89), channel_id=1, source_target_pairs={{0,7},{1,6},{2,5},{3,4},{4,3},{5,2},{6,1},{7,0},{8,15},{9,14},{10,... | collective-permute-start | bytes 294920 | tf_op jit(solution)/shard_map/ppermute | solution.py:292
  88.4 10.1 %collective-permute-start.23 = (bf16[2,256,128]{2,1,0:T(8,128)(2,1)S(1)}, bf16[2,256,128]{2,1,0:T(8,128)(2,1)S(1)}, u32[]{:S(2)}, u32[]{:S(2)}) collective-permute-start(bf16[2,256,128]{2,1,0:T(8,128)(2,1)S(1)} %get-tuple-element.93), channel_id=1, source_target_pairs={{0,24},{8,16},{16,8},{24,0},{1,25},{9,17},{17,9},{25,1},{2,26},{10... | collective-permute-start | bytes 393224 | tf_op jit(solution)/shard_map/ppermute | solution.py:296
  88.4 5.2 %collective-permute-start.24 = (bf16[2,3,64,128]{3,2,1,0:T(8,128)(2,1)S(1)}, bf16[2,3,64,128]{3,2,1,0:T(8,128)(2,1)S(1)}, u32[]{:S(2)}, u32[]{:S(2)}) collective-permute-start(bf16[2,3,64,128]{3,2,1,0:T(8,128)(2,1)S(1)} %get-tuple-element.95), channel_id=1, source_target_pairs={{0,1},{1,0},{2,3},{3,2},{4,5},{5,4},{6,7},{7,6},{8,9},{9,8},{10,11... | collective-permute-start | bytes 294920 | tf_op jit(solution)/shard_map/ppermute | solution.py:292
  89.9 6.9 %collective-permute-start.25 = (bf16[2,3,64,128]{3,2,1,0:T(8,128)(2,1)S(1)}, bf16[2,3,64,128]{3,2,1,0:T(8,128)(2,1)S(1)}, u32[]{:S(2)}, u32[]{:S(2)}) collective-permute-start(bf16[2,3,64,128]{3,2,1,0:T(8,128)(2,1)S(1)} %get-tuple-element.96), channel_id=1, source_target_pairs={{0,2},{1,3},{2,0},{3,1},{4,6},{5,7},{6,4},{7,5},{8,10},{9,11},{10,... | collective-permute-start | bytes 294920 | tf_op jit(solution)/shard_map/ppermute | solution.py:292
  89.9 14.9 %collective-permute-start.26 = (bf16[2,3,64,128]{3,2,1,0:T(8,128)(2,1)S(1)}, bf16[2,3,64,128]{3,2,1,0:T(8,128)(2,1)S(1)}, u32[]{:S(2)}, u32[]{:S(2)}) collective-permute-start(bf16[2,3,64,128]{3,2,1,0:T(8,128)(2,1)S(1)} %get-tuple-element.97), channel_id=1, source_target_pairs={{0,4},{1,5},{2,6},{3,7},{4,0},{5,1},{6,2},{7,3},{8,12},{9,13},{10,... | collective-permute-start | bytes 294920 | tf_op jit(solution)/shard_map/ppermute | solution.py:292
  91.7 15.2 %collective-permute-start.27 = (bf16[2,3,64,128]{3,2,1,0:T(8,128)(2,1)S(1)}, bf16[2,3,64,128]{3,2,1,0:T(8,128)(2,1)S(1)}, u32[]{:S(2)}, u32[]{:S(2)}) collective-permute-start(bf16[2,3,64,128]{3,2,1,0:T(8,128)(2,1)S(1)} %get-tuple-element.98), channel_id=1, source_target_pairs={{0,5},{1,4},{2,7},{3,6},{4,1},{5,0},{6,3},{7,2},{8,13},{9,12},{10,... | collective-permute-start | bytes 294920 | tf_op jit(solution)/shard_map/ppermute | solution.py:292
  93.7 14.9 %collective-permute-start.28 = (bf16[2,3,64,128]{3,2,1,0:T(8,128)(2,1)S(1)}, bf16[2,3,64,128]{3,2,1,0:T(8,128)(2,1)S(1)}, u32[]{:S(2)}, u32[]{:S(2)}) collective-permute-start(bf16[2,3,64,128]{3,2,1,0:T(8,128)(2,1)S(1)} %get-tuple-element.99), channel_id=1, source_target_pairs={{0,6},{1,7},{2,4},{3,5},{4,2},{5,3},{6,0},{7,1},{8,14},{9,15},{10,... | collective-permute-start | bytes 294920 | tf_op jit(solution)/shard_map/ppermute | solution.py:292
  96.8 11.8 %collective-permute-start.29 = (bf16[2,3,64,128]{3,2,1,0:T(8,128)(2,1)S(1)}, bf16[2,3,64,128]{3,2,1,0:T(8,128)(2,1)S(1)}, u32[]{:S(2)}, u32[]{:S(2)}) collective-permute-start(bf16[2,3,64,128]{3,2,1,0:T(8,128)(2,1)S(1)} %get-tuple-element.100), channel_id=1, source_target_pairs={{0,7},{1,6},{2,5},{3,4},{4,3},{5,2},{6,1},{7,0},{8,15},{9,14},{10,... | collective-permute-start | bytes 294920 | tf_op jit(solution)/shard_map/ppermute | solution.py:292
  98.4 10.8 %collective-permute-start.30 = (bf16[2,3,64,128]{3,2,1,0:T(8,128)(2,1)S(1)}, bf16[2,3,64,128]{3,2,1,0:T(8,128)(2,1)S(1)}, u32[]{:S(2)}, u32[]{:S(2)}) collective-permute-start(bf16[2,3,64,128]{3,2,1,0:T(8,128)(2,1)S(1)} %get-tuple-element.101), channel_id=1, source_target_pairs={{0,3},{1,2},{2,1},{3,0},{4,7},{5,6},{6,5},{7,4},{8,11},{9,10},{10,... | collective-permute-start | bytes 294920 | tf_op jit(solution)/shard_map/ppermute | solution.py:292
  104.8 7.3 %collective-permute-start.21 = (bf16[2,256,128]{2,1,0:T(8,128)(2,1)S(1)}, bf16[2,256,128]{2,1,0:T(8,128)(2,1)S(1)}, u32[]{:S(2)}, u32[]{:S(2)}) collective-permute-start(bf16[2,256,128]{2,1,0:T(8,128)(2,1)S(1)} %get-tuple-element.91), channel_id=1, source_target_pairs={{0,8},{8,0},{16,24},{24,16},{1,9},{9,1},{17,25},{25,17},{2,10},{10... | collective-permute-start | bytes 393224 | tf_op jit(solution)/shard_map/ppermute | solution.py:296
  106.9 5.7 %collective-permute-start.22 = (bf16[2,256,128]{2,1,0:T(8,128)(2,1)S(1)}, bf16[2,256,128]{2,1,0:T(8,128)(2,1)S(1)}, u32[]{:S(2)}, u32[]{:S(2)}) collective-permute-start(bf16[2,256,128]{2,1,0:T(8,128)(2,1)S(1)} %get-tuple-element.92), channel_id=1, source_target_pairs={{0,16},{8,24},{16,0},{24,8},{1,17},{9,25},{17,1},{25,9},{2,18},{10... | collective-permute-start | bytes 393224 | tf_op jit(solution)/shard_map/ppermute | solution.py:296
  110.1 2.5 %collective-permute-start.31 = (bf16[2,256,128]{2,1,0:T(8,128)(2,1)S(1)}, bf16[2,256,128]{2,1,0:T(8,128)(2,1)S(1)}, u32[]{:S(2)}, u32[]{:S(2)}) collective-permute-start(bf16[2,256,128]{2,1,0:T(8,128)(2,1)S(1)} %get-tuple-element.103), channel_id=1, source_target_pairs={{0,8},{8,0},{16,24},{24,16},{1,9},{9,1},{17,25},{25,17},{2,10},{10... | collective-permute-start | bytes 393224 | tf_op jit(solution)/shard_map/ppermute | solution.py:296
  110.2 6.3 %collective-permute-start.32 = (bf16[2,256,128]{2,1,0:T(8,128)(2,1)S(1)}, bf16[2,256,128]{2,1,0:T(8,128)(2,1)S(1)}, u32[]{:S(2)}, u32[]{:S(2)}) collective-permute-start(bf16[2,256,128]{2,1,0:T(8,128)(2,1)S(1)} %get-tuple-element.104), channel_id=1, source_target_pairs={{0,16},{8,24},{16,0},{24,8},{1,17},{9,25},{17,1},{25,9},{2,18},{10... | collective-permute-start | bytes 393224 | tf_op jit(solution)/shard_map/ppermute | solution.py:296
  111.1 7.4 %collective-permute-start.33 = (bf16[2,256,128]{2,1,0:T(8,128)(2,1)S(1)}, bf16[2,256,128]{2,1,0:T(8,128)(2,1)S(1)}, u32[]{:S(2)}, u32[]{:S(2)}) collective-permute-start(bf16[2,256,128]{2,1,0:T(8,128)(2,1)S(1)} %get-tuple-element.105), channel_id=1, source_target_pairs={{0,24},{8,16},{16,8},{24,0},{1,25},{9,17},{17,9},{25,1},{2,26},{10... | collective-permute-start | bytes 393224 | tf_op jit(solution)/shard_map/ppermute | solution.py:296

commit v12 on v11

--- a/solution.py
+++ b/solution.py
@@ -44,6 +44,10 @@
 def steps_of(count):
     short = list(range(1, count // 2))
     return short[:2] + list(range(max(1, count // 2), count)) + short[2:]
+
+
+def near_steps(count):
+    return range(1, count // 2)
 
 
 def head_columns(place, r, heads, h, head_count):
@@ -100,9 +104,13 @@
 
 def pick_kernel(place, asked, *refs, heads, steps, head, shard_count):
     own, outs, table = refs[:heads], refs[heads:-1], refs[-1]
-    fill_table(place, own, head, table)
-    for r, out in zip(steps, outs):
-        pick(table, asked, partner(place[0], r, shard_count), out)
+    for h in range(own[0].shape[0]):
+        mine = [(r, out if len(out.shape) == 4 else out.at[h]) for r, out in zip(steps, outs)
+                if h == head or len(out.shape) == 5]
+        if mine:
+            fill_table(place, own, h, table)
+        for r, out in mine:
+            pick(table, asked, partner(place[0], r, shard_count), out)
 
 
 def by_head(ref, b):
@@ -116,9 +124,10 @@
         ref[rows, g * HEAD_DIM : (g + 1) * HEAD_DIM] = x[g * BLK : (g + 1) * BLK]
 
 
-def attend_kernel(place, source, asked, q_ref, g_ref, *refs, heads, head, last, shard_count):
+def attend_kernel(place, source, q_ref, g_ref, *refs, heads, head, kept, shard_count):
     steps = shard_count - 1
     own, far = refs[:heads], refs[heads : heads + steps]
+    near_grads = refs[heads + steps : heads + steps + kept]
     table, total = refs[-2:]
     outs = refs[-2 - steps : -2]
     o_ref, dq_ref, near_out = refs[-5 - steps : -2 - steps]
@@ -130,6 +139,7 @@
         fill_table(place, own, 0, table)
         for r, part in zip(steps_of(shard_count), far):
             first = blocks_here + origin(place[0], r, shard_count) * CAP
+            part = part.at[head] if len(part.shape) == 5 else part
             for kv in range(2):
                 for s in range(CAP):
                     table[kv, first + s] = part[kv, s]
@@ -178,10 +188,13 @@
     def _():
         for kv, factor in ((0, SCALE), (1, 1.0)):
             near_out[kv] = total[kv, :blocks_here] * factor
-        if not last:
-            fill_table(place, own, 1, table)
+        kept_refs = list(near_grads)
         for r, out in zip(steps_of(shard_count), outs):
             there = partner(place[0], r, shard_count)
+            if len(out.shape) == 5:
+                if head:
+                    out[:head] = kept_refs.pop(0)[...]
+                out = out.at[head]
 
             @pl.when(there < place[0])
             def _():
@@ -191,18 +204,16 @@
 
             @pl.when(there > place[0])
             def _():
-                if last or r >= shard_count // 2:
-                    out[...] = jnp.zeros_like(out)
-                else:
-                    pick(table, asked, there, out)
-
-
-def gather_sum_kernel(place, asked, near, *refs, heads, shard_count):
+                out[...] = jnp.zeros_like(out)
+
+
+def gather_sum_kernel(place, asked, near, *refs, heads, head, shard_count):
     back, outs, total = refs[: -heads - 1], refs[-heads - 1 : -1], refs[-1]
     per_quarter = outs[0].shape[1] // BLK
     total[...] = near[...]
     for r, part in zip(steps_of(shard_count), back):
         there = origin(place[0], r, shard_count)
+        part = part.at[head] if len(part.shape) == 5 else part
 
         @pl.when(there > place[0])
         def _():
@@ -249,25 +260,26 @@
     )(*scalars, *arrays)
 
 
-def attend(place, source, asked, queries, out_grad, own, far, head, last, earlier, shard_count):
+def attend(place, source, queries, out_grad, own, far, near_grads, head, earlier, shard_count):
     tokens_here, width = queries.shape
     blocks_here = tokens_here // BLK
     slots = blocks_here + shard_count * CAP
     tile = pl.BlockSpec((STEP_BLOCKS * BLK, GROUP * HEAD_DIM), lambda i, *_: (i, head))
     near_shape = (2, blocks_here, BLK, HEAD_DIM)
-    arrays = [*own, *far]
-    first = 5 + len(arrays)
-    out_shapes = [bf16(2, CAP, BLK, HEAD_DIM)] * (shard_count - 1)
+    arrays = [*own, *far, *near_grads]
+    first = 4 + len(arrays)
+    one = (2, CAP, BLK, HEAD_DIM)
+    out_shapes = [bf16(head + 1, *one) if r in near_steps(shard_count) else bf16(*one) for r in steps_of(shard_count)]
     return pl.pallas_call(
         functools.partial(
-            attend_kernel, heads=len(own), head=head, last=last, shard_count=shard_count
+            attend_kernel, heads=len(own), head=head, kept=len(near_grads), shard_count=shard_count
         ),
         grid_spec=pltpu.PrefetchScalarGridSpec(
-            num_scalar_prefetch=3,
+            num_scalar_prefetch=2,
             grid=(blocks_here // STEP_BLOCKS,),
             in_specs=[tile, tile]
-            + [heads_from(x.shape, head, 1 if last else 2) for x in own]
-            + [whole(x.shape) for x in far]
+            + [heads_from(x.shape, head, 1) for x in own]
+            + [whole(x.shape) for x in [*far, *near_grads]]
             + [ANYWHERE] * len(earlier),
             out_specs=[tile, tile, whole(near_shape)] + [whole(x.shape) for x in out_shapes],
             scratch_shapes=[
@@ -285,7 +297,7 @@
             transcendentals=blocks_here * LIST * BLK * GROUP * BLK,
         ),
         name="attend",
-    )(place, source, asked, queries, out_grad, *arrays, *earlier)
+    )(place, source, queries, out_grad, *arrays, *earlier)
 
 
 def send(x, axis, count, r):
@@ -341,7 +353,9 @@
     asked = lax.all_to_all(requests, "ctx", split_axis=0, concat_axis=0, tiled=True)
 
     steps = steps_of(shard_count)
-    wide = [r for r in steps if r >= shard_count // 2]
+    near = [r for r in steps if r in near_steps(shard_count)]
+    wide = [r for r in steps if r not in near]
+    one = (2, CAP, BLK, HEAD_DIM)
 
     def exchange(arrays):
         return {r: send(x, "ctx", shard_count, r) for r, x in arrays}
@@ -351,32 +365,35 @@
             functools.partial(pick_kernel, heads=heads, steps=steps, head=head, shard_count=shard_count),
             [place, asked],
             own,
-            [bf16(2, CAP, BLK, HEAD_DIM)] * len(steps),
+            [bf16(head_count, *one) if r in near else bf16(*one) for r in steps],
             [pltpu.VMEM((2, blocks_here, BLK, HEAD_DIM), jnp.bfloat16)],
             "pick",
         )
         return list(zip(steps, arrays))
 
-    come, earlier, nears, backs = exchange(picked(0, steps)), [], [], []
+    come, near_grads, earlier, nears, backs = exchange(picked(0, steps)), [], [], [], []
     for h in range(head_count):
-        last = h == head_count - 1
         ahead = {}
-        if not last:
-            ahead = exchange([(r, after(x, *come.values())) for r, x in picked(h + 1, wide)])
-        attended, query_grad, near, *go = attend(
-            place, source, asked, queries, out_grad, own, [come[r] for r in steps], h, last, earlier, shard_count
+        if h + 1 < head_count:
+            ahead = exchange([(r, after(x, *[come[n] for n in near[:2]])) for r, x in picked(h + 1, wide)])
+        attended, query_grad, local, *go = attend(
+            place, source, queries, out_grad, own, [come[r] for r in steps], near_grads, h, earlier, shard_count
         )
-        earlier = [attended, query_grad]
-        nears.append(near)
-        back = exchange(zip(steps, go))
-        backs.append([back[r] for r in steps])
-        come = {**back, **ahead}
+        go = dict(zip(steps, go))
+        earlier, near_grads = [attended, query_grad], [go[r] for r in near]
+        nears.append(local)
+        if h + 1 == head_count:
+            sent = [x for back in backs for x in back.values()]
+            near_back = exchange([(r, after(go[r], *sent)) for r in near])
+        backs.append(exchange([(r, go[r]) for r in wide]))
+        come = {**come, **ahead}
+    backs = [[{**near_back, **back}[r] for r in steps] for back in backs]
     done = []
     for h in range(head_count):
         sums = call(
-            functools.partial(gather_sum_kernel, heads=heads, shard_count=shard_count),
+            functools.partial(gather_sum_kernel, heads=heads, head=h, shard_count=shard_count),
             [place, asked],
-            [after(nears[h], nears[-1], *done[-1:]), *backs[h]],
+            [after(nears[h], *[backs[-1][steps.index(r)] for r in wide[: len(wide) // 2]], *done[-1:]), *backs[h]],
             [bf16(2, quarter, HEAD_DIM)] * heads,
             [pltpu.VMEM((2, blocks_here, BLK, HEAD_DIM), jnp.float32)],
             "gather_sum",

time: 120 us -> 125 us (1.042)
  starting transfers between devices: 50.2 us -> 57.7 us
  waiting for transfers between devices: 32.8 us -> 28.5 us
    ppermute x28 -> x25, starting transfers between devices: 39.8 us -> 48.1 us  [send(): lax.ppermute(x, axis, [(i, partner(i, r, count)) for i in range(count)])]
    ppermute x28 -> x25, waiting for transfers between devices: 24.4 us -> 20.1 us  [send(): lax.ppermute(x, axis, [(i, partner(i, r, count)) for i in range(count)])]
  transfers between devices with their start and end apart: 35 -> 32, of which waited for: 13 -> 10; matrix products, arithmetic and copies ran while one was open for 2% -> 2% of each run, Pallas kernels for 22% -> 21%
where the time goes in v12:
time: 125 us; the launch traced here: 124 us
  starting transfers between devices  57.7 us (46%)
  Pallas kernels  32.6 us (26%)
  waiting for transfers between devices  28.5 us (23%)
  local copies, waits for them, and re-layouts  2.56 us (2%)
  other arithmetic  1.87 us (1%)
    ppermute x25, starting transfers between devices, send(): lax.ppermute(x, axis, [(i, partner(i, r, count)) for i in range(count)])  48.1 us
    pallas_call x2, Pallas kernels, attend(): pl.pallas_call(functools.partial(attend_kernel, heads=len(own), head=head...  24.6 us
    ppermute x25, waiting for transfers between devices, send(): lax.ppermute(x, axis, [(i, partner(i, r, count)) for i in range(count)])  20.1 us
    pallas_call x6, Pallas kernels, call(): pl.pallas_call(kernel, grid_spec=pltpu.PrefetchScalarGridSpec(num_scalar_...  7.97 us
    ppermute x6, waiting for transfers between devices, send_back(): lax.ppermute(x, axis, [(i, origin(i, r, count)) for i in range(count)])  6.4 us
    all_to_all x1, starting transfers between devices, per_device(): lax.all_to_all(requests, 'ctx', split_axis=0, concat_axis=0, tiled=True)  6.07 us
    ppermute x6, starting transfers between devices, send_back(): lax.ppermute(x, axis, [(i, origin(i, r, count)) for i in range(count)])  3.51 us
  transfers between devices with their start and end apart: 32, of which 10 were waited for; matrix products, arithmetic and copies ran while one was open for 2% of the time, Pallas kernels for 21%

profile of v12, /device:TPU:0, one launch (start us, length us, event | category | flops | bytes accessed | tf_op | source)
XLA Modules:
  0.0 124.1 jit_solution(12324974259346782792)
XLA Ops:
  0.6 0.7 pad_add_fusion.place
  1.3 3.0 %split.1 = (bf16[2,2,256,128]{3,2,1,0:T(8,128)(2,1)}, bf16[2,2,256,128]{3,2,1,0:T(8,128)(2,1)}, bf16[2,2,256,128]{3,2,1,0:T(8,128)(2,1)}, bf16[2,2,256,128]{3,2,1,0:T(8,128)(2,1)}) custom-call(s32[2]{0:T(128)} %pad_add_fusion.place, bf16[256,1024]{1,0:T(8,128)(2,1)} %k_ref.1, bf16[256,1024]{1,0:T(8,128)(2,1)} %v_ref.1), custom_call_target="tpu_custom_call" | custom-call | tf_op jit(solution)/shard_map/split/pallas_call | solution.py:248
  4.8 2.6 %collective-permute-start.1 = (bf16[2,2,256,128]{3,2,1,0:T(8,128)(2,1)}, bf16[2,2,256,128]{3,2,1,0:T(8,128)(2,1)S(1)}, u32[]{:S(2)}, u32[]{:S(2)}) collective-permute-start(bf16[2,2,256,128]{3,2,1,0:T(8,128)(2,1)} %get-tuple-element.62), channel_id=1, source_target_pairs={{0,16},{8,24},{16,0},{24,8},{1,17},{9,25},{17,1},{25,9},{2,18},{10... | collective-permute-start | bytes 786440 | tf_op jit(solution)/shard_map/ppermute | solution.py:304
  7.5 0.8 copy.14
  8.7 0.7 select_reduce_fusion
  9.4 6.1 %all-to-all-start = ((s32[8,1,128]{2,1,0:T(1,128)}), s32[8,1,128]{2,1,0:T(1,128)S(1)}, u32[]{:S(2)}, u32[]{:S(2)}) async-start(s32[8,1,128]{2,1,0:T(1,128)} %bitcast.3), calls=%async_computation | async-start | bytes 8192 | tf_op jit(solution)/shard_map/all_to_all | solution.py:353
  15.5 4.3 %collective-permute-done.2.refs_3_ = bf16[2,2,256,128]{3,2,1,0:T(8,128)(2,1)S(1)} collective-permute-done((bf16[2,2,256,128]{3,2,1,0:T(8,128)(2,1)}, bf16[2,2,256,128]{3,2,1,0:T(8,128)(2,1)S(1)}, u32[]{:S(2)}, u32[]{:S(2)}) %collective-permute-start.2) | collective-permute-done | bytes 262176 | tf_op jit(solution)/shard_map/ppermute | solution.py:304
  19.9 2.0 %all-to-all-done = s32[8,1,128]{2,1,0:T(1,128)S(1)} async-done(((s32[8,1,128]{2,1,0:T(1,128)}), s32[8,1,128]{2,1,0:T(1,128)S(1)}, u32[]{:S(2)}, u32[]{:S(2)}) %all-to-all-start) | async-done | bytes 4128 | tf_op jit(solution)/shard_map/all_to_all | solution.py:353
  21.9 0.9 copy-done.1
  22.9 0.7 copy-done.2
  23.5 0.8 pick.2
  24.4 0.6 collective-permute-start.3
  25.0 0.6 collective-permute-start.4
  25.8 2.7 %collective-permute-start.10 = (bf16[2,3,64,128]{3,2,1,0:T(8,128)(2,1)S(1)}, bf16[2,3,64,128]{3,2,1,0:T(8,128)(2,1)S(1)}, u32[]{:S(2)}, u32[]{:S(2)}) collective-permute-start(bf16[2,3,64,128]{3,2,1,0:T(8,128)(2,1)S(1)} %get-tuple-element.75), channel_id=1, source_target_pairs={{0,4},{1,5},{2,6},{3,7},{4,0},{5,1},{6,2},{7,3},{8,12},{9,13},{10,... | collective-permute-start | bytes 294920 | tf_op jit(solution)/shard_map/ppermute | solution.py:304
  28.4 1.2 collective-permute-start.11
  29.6 1.6 %collective-permute-start.12 = (bf16[2,3,64,128]{3,2,1,0:T(8,128)(2,1)S(1)}, bf16[2,3,64,128]{3,2,1,0:T(8,128)(2,1)S(1)}, u32[]{:S(2)}, u32[]{:S(2)}) collective-permute-start(bf16[2,3,64,128]{3,2,1,0:T(8,128)(2,1)S(1)} %get-tuple-element.77), channel_id=1, source_target_pairs={{0,6},{1,7},{2,4},{3,5},{4,2},{5,3},{6,0},{7,1},{8,14},{9,15},{10,... | collective-permute-start | bytes 294920 | tf_op jit(solution)/shard_map/ppermute | solution.py:304
  31.2 3.5 %collective-permute-start.13 = (bf16[2,3,64,128]{3,2,1,0:T(8,128)(2,1)S(1)}, bf16[2,3,64,128]{3,2,1,0:T(8,128)(2,1)S(1)}, u32[]{:S(2)}, u32[]{:S(2)}) collective-permute-start(bf16[2,3,64,128]{3,2,1,0:T(8,128)(2,1)S(1)} %get-tuple-element.78), channel_id=1, source_target_pairs={{0,7},{1,6},{2,5},{3,4},{4,3},{5,2},{6,1},{7,0},{8,15},{9,14},{10,... | collective-permute-start | bytes 294920 | tf_op jit(solution)/shard_map/ppermute | solution.py:304
  34.7 0.7 pick.3
  35.3 3.3 %collective-permute-start.5 = (bf16[2,3,64,128]{3,2,1,0:T(8,128)(2,1)S(1)}, bf16[2,3,64,128]{3,2,1,0:T(8,128)(2,1)S(1)}, u32[]{:S(2)}, u32[]{:S(2)}) collective-permute-start(bf16[2,3,64,128]{3,2,1,0:T(8,128)(2,1)S(1)} %get-tuple-element.67), channel_id=1, source_target_pairs={{0,4},{1,5},{2,6},{3,7},{4,0},{5,1},{6,2},{7,3},{8,12},{9,13},{10,... | collective-permute-start | bytes 294920 | tf_op jit(solution)/shard_map/ppermute | solution.py:304
  38.7 4.8 %collective-permute-done.11.refs_7_ = bf16[2,3,64,128]{3,2,1,0:T(8,128)(2,1)S(1)} collective-permute-done((bf16[2,3,64,128]{3,2,1,0:T(8,128)(2,1)S(1)}, bf16[2,3,64,128]{3,2,1,0:T(8,128)(2,1)S(1)}, u32[]{:S(2)}, u32[]{:S(2)}) %collective-permute-start.11) | collective-permute-done | bytes 98336 | tf_op jit(solution)/shard_map/ppermute | solution.py:304
  43.4 1.9 %collective-permute-start.7 = (bf16[2,3,64,128]{3,2,1,0:T(8,128)(2,1)S(1)}, bf16[2,3,64,128]{3,2,1,0:T(8,128)(2,1)S(1)}, u32[]{:S(2)}, u32[]{:S(2)}) collective-permute-start(bf16[2,3,64,128]{3,2,1,0:T(8,128)(2,1)S(1)} %get-tuple-element.71), channel_id=1, source_target_pairs={{0,6},{1,7},{2,4},{3,5},{4,2},{5,3},{6,0},{7,1},{8,14},{9,15},{10,... | collective-permute-start | bytes 294920 | tf_op jit(solution)/shard_map/ppermute | solution.py:304
  45.3 2.4 %collective-permute-start.8 = (bf16[2,3,64,128]{3,2,1,0:T(8,128)(2,1)S(1)}, bf16[2,3,64,128]{3,2,1,0:T(8,128)(2,1)S(1)}, u32[]{:S(2)}, u32[]{:S(2)}) collective-permute-start(bf16[2,3,64,128]{3,2,1,0:T(8,128)(2,1)S(1)} %get-tuple-element.73), channel_id=1, source_target_pairs={{0,7},{1,6},{2,5},{3,4},{4,3},{5,2},{6,1},{7,0},{8,15},{9,14},{10,... | collective-permute-start | bytes 294920 | tf_op jit(solution)/shard_map/ppermute | solution.py:304
  47.7 12.0 %attend.2 = (bf16[1024,1024]{1,0:T(8,128)(2,1)}, bf16[1024,1024]{1,0:T(8,128)(2,1)}, f32[2,16,64,128]{3,2,1,0:T(8,128)S(1)}, bf16[1,2,3,64,128]{4,3,2,1,0:T(8,12...) custom-call(s32[2]{0:T(128)S(1)} %copy-done.2, ...), custom_call_target="tpu_custom_call" | custom-call | flops 3221225472 | bytes 20971520 | tf_op jit(solution)/shard_map/attend/pallas_call | solution.py:273
  59.8 10.8 %collective-permute-start.16 = (bf16[2,3,64,128]{3,2,1,0:T(8,128)(2,1)S(1)}, bf16[2,3,64,128]{3,2,1,0:T(8,128)(2,1)S(1)}, u32[]{:S(2)}, u32[]{:S(2)}) collective-permute-start(bf16[2,3,64,128]{3,2,1,0:T(8,128)(2,1)S(1)} %get-tuple-element.91), channel_id=1, source_target_pairs={{0,4},{1,5},{2,6},{3,7},{4,0},{5,1},{6,2},{7,3},{8,12},{9,13},{10,... | collective-permute-start | bytes 294920 | tf_op jit(solution)/shard_map/ppermute | solution.py:304
  70.6 0.5 collective-permute-start.17
  71.1 2.0 %collective-permute-start.18 = (bf16[2,3,64,128]{3,2,1,0:T(8,128)(2,1)S(1)}, bf16[2,3,64,128]{3,2,1,0:T(8,128)(2,1)S(1)}, u32[]{:S(2)}, u32[]{:S(2)}) collective-permute-start(bf16[2,3,64,128]{3,2,1,0:T(8,128)(2,1)S(1)} %get-tuple-element.93), channel_id=1, source_target_pairs={{0,6},{1,7},{2,4},{3,5},{4,2},{5,3},{6,0},{7,1},{8,14},{9,15},{10,... | collective-permute-start | bytes 294920 | tf_op jit(solution)/shard_map/ppermute | solution.py:304
  73.2 2.2 %collective-permute-start.19 = (bf16[2,3,64,128]{3,2,1,0:T(8,128)(2,1)S(1)}, bf16[2,3,64,128]{3,2,1,0:T(8,128)(2,1)S(1)}, u32[]{:S(2)}, u32[]{:S(2)}) collective-permute-start(bf16[2,3,64,128]{3,2,1,0:T(8,128)(2,1)S(1)} %get-tuple-element.94), channel_id=1, source_target_pairs={{0,7},{1,6},{2,5},{3,4},{4,3},{5,2},{6,1},{7,0},{8,15},{9,14},{10,... | collective-permute-start | bytes 294920 | tf_op jit(solution)/shard_map/ppermute | solution.py:304
  75.4 12.6 %attend.3 = (bf16[1024,1024]{1,0:T(8,128)(2,1)}, bf16[1024,1024]{1,0:T(8,128)(2,1)}, f32[2,16,64,128]{3,2,1,0:T(8,128)}, bf16[2,2,3,64,128]{4,3,2,1,0:T(8,128)(2...) custom-call(s32[2]{0:T(128)S(1)} %copy-done.2, ...), custom_call_target="tpu_custom_call", output_to_operand_aliasing={{0}: (18, {}), {1}: (19, {})} | custom-call | flops 3221225472 | bytes 20971520 | tf_op jit(solution)/shard_map/attend/pallas_call | solution.py:273
  88.0 1.1 collective-permute-start.20
  89.1 0.6 collective-permute-start.21
  89.7 1.8 %collective-permute-start.22 = (bf16[2,2,3,64,128]{4,3,2,1,0:T(8,128)(2,1)S(1)}, bf16[2,2,3,64,128]{4,3,2,1,0:T(8,128)(2,1)S(1)}, u32[]{:S(2)}, u32[]{:S(2)}) collective-permute-start(bf16[2,2,3,64,128]{4,3,2,1,0:T(8,128)(2,1)S(1)} %get-tuple-element.99), channel_id=1, source_target_pairs={{0,3},{1,2},{2,1},{3,0},{4,7},{5,6},{6,5},{7,4},{8,11},{9,10},{10,... | collective-permute-start | bytes 589832 | tf_op jit(solution)/shard_map/ppermute | solution.py:304
  91.6 1.0 collective-permute-start.14
  92.6 2.4 %collective-permute-start.15 = (bf16[2,3,64,128]{3,2,1,0:T(8,128)(2,1)S(1)}, bf16[2,3,64,128]{3,2,1,0:T(8,128)(2,1)S(1)}, u32[]{:S(2)}, u32[]{:S(2)}) collective-permute-start(bf16[2,3,64,128]{3,2,1,0:T(8,128)(2,1)S(1)} %get-tuple-element.88), channel_id=1, source_target_pairs={{0,5},{1,4},{2,7},{3,6},{4,1},{5,0},{6,3},{7,2},{8,13},{9,12},{10,... | collective-permute-start | bytes 294920 | tf_op jit(solution)/shard_map/ppermute | solution.py:304
  95.0 4.1 %collective-permute-done.14.refs_2_ = bf16[2,3,64,128]{3,2,1,0:T(8,128)(2,1)S(1)} collective-permute-done((bf16[2,3,64,128]{3,2,1,0:T(8,128)(2,1)S(1)}, bf16[2,3,64,128]{3,2,1,0:T(8,128)(2,1)S(1)}, u32[]{:S(2)}, u32[]{:S(2)}) %collective-permute-start.14) | collective-permute-done | bytes 98336 | tf_op jit(solution)/shard_map/ppermute | solution.py:304
  99.1 1.6 %collective-permute-done.15.refs_3_ = bf16[2,3,64,128]{3,2,1,0:T(8,128)(2,1)S(1)} collective-permute-done((bf16[2,3,64,128]{3,2,1,0:T(8,128)(2,1)S(1)}, bf16[2,3,64,128]{3,2,1,0:T(8,128)(2,1)S(1)}, u32[]{:S(2)}, u32[]{:S(2)}) %collective-permute-start.15) | collective-permute-done | bytes 98336 | tf_op jit(solution)/shard_map/ppermute | solution.py:304
  100.8 1.0 collective-permute-done.22.refs_6_
  101.8 0.9 gather_sum.2
  102.7 2.0 %collective-permute-start.26 = (bf16[2,3,64,128]{3,2,1,0:T(8,128)(2,1)S(1)}, bf16[2,3,64,128]{3,2,1,0:T(8,128)(2,1)S(1)}, u32[]{:S(2)}, u32[]{:S(2)}) collective-permute-start(bf16[2,3,64,128]{3,2,1,0:T(8,128)(2,1)S(1)} %get-tuple-element.106), channel_id=1, source_target_pairs={{0,6},{1,7},{2,4},{3,5},{4,2},{5,3},{6,0},{7,1},{8,14},{9,15},{10,... | collective-permute-start | bytes 294920 | tf_op jit(solution)/shard_map/ppermute | solution.py:304
  104.7 2.8 %collective-permute-start.27 = (bf16[2,3,64,128]{3,2,1,0:T(8,128)(2,1)S(1)}, bf16[2,3,64,128]{3,2,1,0:T(8,128)(2,1)S(1)}, u32[]{:S(2)}, u32[]{:S(2)}) collective-permute-start(bf16[2,3,64,128]{3,2,1,0:T(8,128)(2,1)S(1)} %get-tuple-element.107), channel_id=1, source_target_pairs={{0,7},{1,6},{2,5},{3,4},{4,3},{5,2},{6,1},{7,0},{8,15},{9,14},{10,... | collective-permute-start | bytes 294920 | tf_op jit(solution)/shard_map/ppermute | solution.py:304
  107.5 1.0 collective-permute-start.23
  108.5 0.5 collective-permute-start.24
  109.0 0.9 collective-permute-done.26.refs_4_
  109.9 3.3 %collective-permute-done.27.refs_5_ = bf16[2,3,64,128]{3,2,1,0:T(8,128)(2,1)S(1)} collective-permute-done((bf16[2,3,64,128]{3,2,1,0:T(8,128)(2,1)S(1)}, bf16[2,3,64,128]{3,2,1,0:T(8,128)(2,1)S(1)}, u32[]{:S(2)}, u32[]{:S(2)}) %collective-permute-start.27) | collective-permute-done | bytes 98336 | tf_op jit(solution)/shard_map/ppermute | solution.py:304
  113.2 0.9 gather_sum.3
  114.2 1.3 %collective-permute-start.29 = (bf16[2,256,128]{2,1,0:T(8,128)(2,1)S(1)}, bf16[2,256,128]{2,1,0:T(8,128)(2,1)S(1)}, u32[]{:S(2)}, u32[]{:S(2)}) collective-permute-start(bf16[2,256,128]{2,1,0:T(8,128)(2,1)S(1)} %get-tuple-element.110), channel_id=1, source_target_pairs={{0,16},{8,24},{16,0},{24,8},{1,17},{9,25},{17,1},{25,9},{2,18},{10... | collective-permute-start | bytes 393224 | tf_op jit(solution)/shard_map/ppermute | solution.py:308
  116.1 4.5 %collective-permute-done.29.refs_6_ = bf16[2,256,128]{2,1,0:T(8,128)(2,1)S(1)} collective-permute-done((bf16[2,256,128]{2,1,0:T(8,128)(2,1)S(1)}, bf16[2,256,128]{2,1,0:T(8,128)(2,1)S(1)}, u32[]{:S(2)}, u32[]{:S(2)}) %collective-permute-start.29) | collective-permute-done | bytes 131104 | tf_op jit(solution)/shard_map/ppermute | solution.py:308
  120.5 1.9 %collective-permute-done.30.refs_7_ = bf16[2,256,128]{2,1,0:T(8,128)(2,1)S(1)} collective-permute-done((bf16[2,256,128]{2,1,0:T(8,128)(2,1)S(1)}, bf16[2,256,128]{2,1,0:T(8,128)(2,1)S(1)}, u32[]{:S(2)}, u32[]{:S(2)}) %collective-permute-start.30) | collective-permute-done | bytes 131104 | tf_op jit(solution)/shard_map/ppermute | solution.py:308
  122.4 1.6 %join.1 = (bf16[256,1024]{1,0:T(8,128)(2,1)}, bf16[256,1024]{1,0:T(8,128)(2,1)}) custom-call(s32[2]{0:T(128)S(1)} %copy-done.2, bf16[2,256,128]{2,1,0:T(8,128)(2,1)S(1)} %get-tuple-element.100.refs_0_, bf16[2,256,128]{2,1,0:T(8,128)(2,1)S(1)} %collective-permute-done.23.refs_1_, bf16[2,256,128]{2,1,0:T(8,128)(2,1)S(1)} %collective-permute-done.24.refs_2_, ...), custom_call_target="tpu_custom_call" | custom-call | tf_op jit(solution)/shard_map/join/pallas_call | solution.py:248
  (44 shorter events, 2.0 us)
Async XLA Ops:
  4.3 3.2 %collective-permute-start = (bf16[2,2,256,128]{3,2,1,0:T(8,128)(2,1)}, bf16[2,2,256,128]{3,2,1,0:T(8,128)(2,1)S(1)}, u32[]{:S(2)}, u32[]{:S(2)}) collective-permute-start(bf16[2,2,256,128]{3,2,1,0:T(8,128)(2,1)} %get-tuple-element.59), channel_id=1, source_target_pairs={{0,8},{8,0},{16,24},{24,16},{1,9},{9,1},{17,25},{25,17},{2,10},{10... | collective-permute-start | bytes 786440 | tf_op jit(solution)/shard_map/ppermute | solution.py:304
  4.8 10.7 %collective-permute-start.1 = (bf16[2,2,256,128]{3,2,1,0:T(8,128)(2,1)}, bf16[2,2,256,128]{3,2,1,0:T(8,128)(2,1)S(1)}, u32[]{:S(2)}, u32[]{:S(2)}) collective-permute-start(bf16[2,2,256,128]{3,2,1,0:T(8,128)(2,1)} %get-tuple-element.62), channel_id=1, source_target_pairs={{0,16},{8,24},{16,0},{24,8},{1,17},{9,25},{17,1},{25,9},{2,18},{10... | collective-permute-start | bytes 786440 | tf_op jit(solution)/shard_map/ppermute | solution.py:304
  7.4 12.5 %collective-permute-start.2 = (bf16[2,2,256,128]{3,2,1,0:T(8,128)(2,1)}, bf16[2,2,256,128]{3,2,1,0:T(8,128)(2,1)S(1)}, u32[]{:S(2)}, u32[]{:S(2)}) collective-permute-start(bf16[2,2,256,128]{3,2,1,0:T(8,128)(2,1)} %get-tuple-element.63), channel_id=1, source_target_pairs={{0,24},{8,16},{16,8},{24,0},{1,25},{9,17},{17,9},{25,1},{2,26},{10... | collective-permute-start | bytes 786440 | tf_op jit(solution)/shard_map/ppermute | solution.py:304
  9.4 12.5 %all-to-all-start = ((s32[8,1,128]{2,1,0:T(1,128)}), s32[8,1,128]{2,1,0:T(1,128)S(1)}, u32[]{:S(2)}, u32[]{:S(2)}) async-start(s32[8,1,128]{2,1,0:T(1,128)} %bitcast.3), calls=%async_computation | async-start | bytes 8192 | tf_op jit(solution)/shard_map/all_to_all | solution.py:353
  21.9 1.0 copy-start.1
  22.9 0.7 copy-start.2
  24.4 6.8 %collective-permute-start.3 = (bf16[2,2,3,64,128]{4,3,2,1,0:T(8,128)(2,1)S(1)}, bf16[2,2,3,64,128]{4,3,2,1,0:T(8,128)(2,1)S(1)}, u32[]{:S(2)}, u32[]{:S(2)}) collective-permute-start(bf16[2,2,3,64,128]{4,3,2,1,0:T(8,128)(2,1)S(1)} %get-tuple-element.64), channel_id=1, source_target_pairs={{0,1},{1,0},{2,3},{3,2},{4,5},{5,4},{6,7},{7,6},{8,9},{9,8},{10,11... | collective-permute-start | bytes 589832 | tf_op jit(solution)/shard_map/ppermute | solution.py:304
  25.0 9.7 %collective-permute-start.4 = (bf16[2,2,3,64,128]{4,3,2,1,0:T(8,128)(2,1)S(1)}, bf16[2,2,3,64,128]{4,3,2,1,0:T(8,128)(2,1)S(1)}, u32[]{:S(2)}, u32[]{:S(2)}) collective-permute-start(bf16[2,2,3,64,128]{4,3,2,1,0:T(8,128)(2,1)S(1)} %get-tuple-element.65), channel_id=1, source_target_pairs={{0,2},{1,3},{2,0},{3,1},{4,6},{5,7},{6,4},{7,5},{8,10},{9,11},{10,... | collective-permute-start | bytes 589832 | tf_op jit(solution)/shard_map/ppermute | solution.py:304
  25.8 9.6 %collective-permute-start.10 = (bf16[2,3,64,128]{3,2,1,0:T(8,128)(2,1)S(1)}, bf16[2,3,64,128]{3,2,1,0:T(8,128)(2,1)S(1)}, u32[]{:S(2)}, u32[]{:S(2)}) collective-permute-start(bf16[2,3,64,128]{3,2,1,0:T(8,128)(2,1)S(1)} %get-tuple-element.75), channel_id=1, source_target_pairs={{0,4},{1,5},{2,6},{3,7},{4,0},{5,1},{6,2},{7,3},{8,12},{9,13},{10,... | collective-permute-start | bytes 294920 | tf_op jit(solution)/shard_map/ppermute | solution.py:304
  28.4 15.0 %collective-permute-start.11 = (bf16[2,3,64,128]{3,2,1,0:T(8,128)(2,1)S(1)}, bf16[2,3,64,128]{3,2,1,0:T(8,128)(2,1)S(1)}, u32[]{:S(2)}, u32[]{:S(2)}) collective-permute-start(bf16[2,3,64,128]{3,2,1,0:T(8,128)(2,1)S(1)} %get-tuple-element.76), channel_id=1, source_target_pairs={{0,5},{1,4},{2,7},{3,6},{4,1},{5,0},{6,3},{7,2},{8,13},{9,12},{10,... | collective-permute-start | bytes 294920 | tf_op jit(solution)/shard_map/ppermute | solution.py:304
  29.6 13.8 %collective-permute-start.12 = (bf16[2,3,64,128]{3,2,1,0:T(8,128)(2,1)S(1)}, bf16[2,3,64,128]{3,2,1,0:T(8,128)(2,1)S(1)}, u32[]{:S(2)}, u32[]{:S(2)}) collective-permute-start(bf16[2,3,64,128]{3,2,1,0:T(8,128)(2,1)S(1)} %get-tuple-element.77), channel_id=1, source_target_pairs={{0,6},{1,7},{2,4},{3,5},{4,2},{5,3},{6,0},{7,1},{8,14},{9,15},{10,... | collective-permute-start | bytes 294920 | tf_op jit(solution)/shard_map/ppermute | solution.py:304
  31.2 14.2 %collective-permute-start.13 = (bf16[2,3,64,128]{3,2,1,0:T(8,128)(2,1)S(1)}, bf16[2,3,64,128]{3,2,1,0:T(8,128)(2,1)S(1)}, u32[]{:S(2)}, u32[]{:S(2)}) collective-permute-start(bf16[2,3,64,128]{3,2,1,0:T(8,128)(2,1)S(1)} %get-tuple-element.78), channel_id=1, source_target_pairs={{0,7},{1,6},{2,5},{3,4},{4,3},{5,2},{6,1},{7,0},{8,15},{9,14},{10,... | collective-permute-start | bytes 294920 | tf_op jit(solution)/shard_map/ppermute | solution.py:304
  34.6 13.1 %collective-permute-start.9 = (bf16[2,2,3,64,128]{4,3,2,1,0:T(8,128)(2,1)S(1)}, bf16[2,2,3,64,128]{4,3,2,1,0:T(8,128)(2,1)S(1)}, u32[]{:S(2)}, u32[]{:S(2)}) collective-permute-start(bf16[2,2,3,64,128]{4,3,2,1,0:T(8,128)(2,1)S(1)} %get-tuple-element.74), channel_id=1, source_target_pairs={{0,3},{1,2},{2,1},{3,0},{4,7},{5,6},{6,5},{7,4},{8,11},{9,10},{10,... | collective-permute-start | bytes 589832 | tf_op jit(solution)/shard_map/ppermute | solution.py:304
  35.3 35.2 %collective-permute-start.5 = (bf16[2,3,64,128]{3,2,1,0:T(8,128)(2,1)S(1)}, bf16[2,3,64,128]{3,2,1,0:T(8,128)(2,1)S(1)}, u32[]{:S(2)}, u32[]{:S(2)}) collective-permute-start(bf16[2,3,64,128]{3,2,1,0:T(8,128)(2,1)S(1)} %get-tuple-element.67), channel_id=1, source_target_pairs={{0,4},{1,5},{2,6},{3,7},{4,0},{5,1},{6,2},{7,3},{8,12},{9,13},{10,... | collective-permute-start | bytes 294920 | tf_op jit(solution)/shard_map/ppermute | solution.py:304
  43.4 27.7 %collective-permute-start.6 = (bf16[2,3,64,128]{3,2,1,0:T(8,128)(2,1)S(1)}, bf16[2,3,64,128]{3,2,1,0:T(8,128)(2,1)S(1)}, u32[]{:S(2)}, u32[]{:S(2)}) collective-permute-start(bf16[2,3,64,128]{3,2,1,0:T(8,128)(2,1)S(1)} %get-tuple-element.69), channel_id=1, source_target_pairs={{0,5},{1,4},{2,7},{3,6},{4,1},{5,0},{6,3},{7,2},{8,13},{9,12},{10,... | collective-permute-start | bytes 294920 | tf_op jit(solution)/shard_map/ppermute | solution.py:304
  43.4 29.7 %collective-permute-start.7 = (bf16[2,3,64,128]{3,2,1,0:T(8,128)(2,1)S(1)}, bf16[2,3,64,128]{3,2,1,0:T(8,128)(2,1)S(1)}, u32[]{:S(2)}, u32[]{:S(2)}) collective-permute-start(bf16[2,3,64,128]{3,2,1,0:T(8,128)(2,1)S(1)} %get-tuple-element.71), channel_id=1, source_target_pairs={{0,6},{1,7},{2,4},{3,5},{4,2},{5,3},{6,0},{7,1},{8,14},{9,15},{10,... | collective-permute-start | bytes 294920 | tf_op jit(solution)/shard_map/ppermute | solution.py:304
  45.3 30.0 %collective-permute-start.8 = (bf16[2,3,64,128]{3,2,1,0:T(8,128)(2,1)S(1)}, bf16[2,3,64,128]{3,2,1,0:T(8,128)(2,1)S(1)}, u32[]{:S(2)}, u32[]{:S(2)}) collective-permute-start(bf16[2,3,64,128]{3,2,1,0:T(8,128)(2,1)S(1)} %get-tuple-element.73), channel_id=1, source_target_pairs={{0,7},{1,6},{2,5},{3,4},{4,3},{5,2},{6,1},{7,0},{8,15},{9,14},{10,... | collective-permute-start | bytes 294920 | tf_op jit(solution)/shard_map/ppermute | solution.py:304
  59.8 28.2 %collective-permute-start.16 = (bf16[2,3,64,128]{3,2,1,0:T(8,128)(2,1)S(1)}, bf16[2,3,64,128]{3,2,1,0:T(8,128)(2,1)S(1)}, u32[]{:S(2)}, u32[]{:S(2)}) collective-permute-start(bf16[2,3,64,128]{3,2,1,0:T(8,128)(2,1)S(1)} %get-tuple-element.91), channel_id=1, source_target_pairs={{0,4},{1,5},{2,6},{3,7},{4,0},{5,1},{6,2},{7,3},{8,12},{9,13},{10,... | collective-permute-start | bytes 294920 | tf_op jit(solution)/shard_map/ppermute | solution.py:304
  70.6 17.4 %collective-permute-start.17 = (bf16[2,3,64,128]{3,2,1,0:T(8,128)(2,1)S(1)}, bf16[2,3,64,128]{3,2,1,0:T(8,128)(2,1)S(1)}, u32[]{:S(2)}, u32[]{:S(2)}) collective-permute-start(bf16[2,3,64,128]{3,2,1,0:T(8,128)(2,1)S(1)} %get-tuple-element.92), channel_id=1, source_target_pairs={{0,5},{1,4},{2,7},{3,6},{4,1},{5,0},{6,3},{7,2},{8,13},{9,12},{10,... | collective-permute-start | bytes 294920 | tf_op jit(solution)/shard_map/ppermute | solution.py:304
  71.1 16.9 %collective-permute-start.18 = (bf16[2,3,64,128]{3,2,1,0:T(8,128)(2,1)S(1)}, bf16[2,3,64,128]{3,2,1,0:T(8,128)(2,1)S(1)}, u32[]{:S(2)}, u32[]{:S(2)}) collective-permute-start(bf16[2,3,64,128]{3,2,1,0:T(8,128)(2,1)S(1)} %get-tuple-element.93), channel_id=1, source_target_pairs={{0,6},{1,7},{2,4},{3,5},{4,2},{5,3},{6,0},{7,1},{8,14},{9,15},{10,... | collective-permute-start | bytes 294920 | tf_op jit(solution)/shard_map/ppermute | solution.py:304
  73.2 14.9 %collective-permute-start.19 = (bf16[2,3,64,128]{3,2,1,0:T(8,128)(2,1)S(1)}, bf16[2,3,64,128]{3,2,1,0:T(8,128)(2,1)S(1)}, u32[]{:S(2)}, u32[]{:S(2)}) collective-permute-start(bf16[2,3,64,128]{3,2,1,0:T(8,128)(2,1)S(1)} %get-tuple-element.94), channel_id=1, source_target_pairs={{0,7},{1,6},{2,5},{3,4},{4,3},{5,2},{6,1},{7,0},{8,15},{9,14},{10,... | collective-permute-start | bytes 294920 | tf_op jit(solution)/shard_map/ppermute | solution.py:304
  88.0 25.2 %copy-start = (f32[2,16,64,128]{3,2,1,0:T(8,128)S(1)}, f32[2,16,64,128]{3,2,1,0:T(8,128)}, u32[]{:S(2)}) copy-start(f32[2,16,64,128]{3,2,1,0:T(8,128)} %get-tuple-element.105.near) | copy-start | bytes 3145732
  88.0 12.7 %collective-permute-start.20 = (bf16[2,2,3,64,128]{4,3,2,1,0:T(8,128)(2,1)S(1)}, bf16[2,2,3,64,128]{4,3,2,1,0:T(8,128)(2,1)S(1)}, u32[]{:S(2)}, u32[]{:S(2)}) collective-permute-start(bf16[2,2,3,64,128]{4,3,2,1,0:T(8,128)(2,1)S(1)} %get-tuple-element.95), channel_id=1, source_target_pairs={{0,1},{1,0},{2,3},{3,2},{4,5},{5,4},{6,7},{7,6},{8,9},{9,8},{10,11... | collective-permute-start | bytes 589832 | tf_op jit(solution)/shard_map/ppermute | solution.py:304
  89.1 11.6 %collective-permute-start.21 = (bf16[2,2,3,64,128]{4,3,2,1,0:T(8,128)(2,1)S(1)}, bf16[2,2,3,64,128]{4,3,2,1,0:T(8,128)(2,1)S(1)}, u32[]{:S(2)}, u32[]{:S(2)}) collective-permute-start(bf16[2,2,3,64,128]{4,3,2,1,0:T(8,128)(2,1)S(1)} %get-tuple-element.97), channel_id=1, source_target_pairs={{0,2},{1,3},{2,0},{3,1},{4,6},{5,7},{6,4},{7,5},{8,10},{9,11},{10,... | collective-permute-start | bytes 589832 | tf_op jit(solution)/shard_map/ppermute | solution.py:304
  89.7 12.0 %collective-permute-start.22 = (bf16[2,2,3,64,128]{4,3,2,1,0:T(8,128)(2,1)S(1)}, bf16[2,2,3,64,128]{4,3,2,1,0:T(8,128)(2,1)S(1)}, u32[]{:S(2)}, u32[]{:S(2)}) collective-permute-start(bf16[2,2,3,64,128]{4,3,2,1,0:T(8,128)(2,1)S(1)} %get-tuple-element.99), channel_id=1, source_target_pairs={{0,3},{1,2},{2,1},{3,0},{4,7},{5,6},{6,5},{7,4},{8,11},{9,10},{10,... | collective-permute-start | bytes 589832 | tf_op jit(solution)/shard_map/ppermute | solution.py:304
  91.6 7.5 %collective-permute-start.14 = (bf16[2,3,64,128]{3,2,1,0:T(8,128)(2,1)S(1)}, bf16[2,3,64,128]{3,2,1,0:T(8,128)(2,1)S(1)}, u32[]{:S(2)}, u32[]{:S(2)}) collective-permute-start(bf16[2,3,64,128]{3,2,1,0:T(8,128)(2,1)S(1)} %get-tuple-element.87), channel_id=1, source_target_pairs={{0,4},{1,5},{2,6},{3,7},{4,0},{5,1},{6,2},{7,3},{8,12},{9,13},{10,... | collective-permute-start | bytes 294920 | tf_op jit(solution)/shard_map/ppermute | solution.py:304
  92.6 8.1 %collective-permute-start.15 = (bf16[2,3,64,128]{3,2,1,0:T(8,128)(2,1)S(1)}, bf16[2,3,64,128]{3,2,1,0:T(8,128)(2,1)S(1)}, u32[]{:S(2)}, u32[]{:S(2)}) collective-permute-start(bf16[2,3,64,128]{3,2,1,0:T(8,128)(2,1)S(1)} %get-tuple-element.88), channel_id=1, source_target_pairs={{0,5},{1,4},{2,7},{3,6},{4,1},{5,0},{6,3},{7,2},{8,13},{9,12},{10,... | collective-permute-start | bytes 294920 | tf_op jit(solution)/shard_map/ppermute | solution.py:304
  102.7 6.4 %collective-permute-start.25 = (bf16[2,256,128]{2,1,0:T(8,128)(2,1)S(1)}, bf16[2,256,128]{2,1,0:T(8,128)(2,1)S(1)}, u32[]{:S(2)}, u32[]{:S(2)}) collective-permute-start(bf16[2,256,128]{2,1,0:T(8,128)(2,1)S(1)} %get-tuple-element.103), channel_id=1, source_target_pairs={{0,24},{8,16},{16,8},{24,0},{1,25},{9,17},{17,9},{25,1},{2,26},{10... | collective-permute-start | bytes 393224 | tf_op jit(solution)/shard_map/ppermute | solution.py:308
  102.7 7.1 %collective-permute-start.26 = (bf16[2,3,64,128]{3,2,1,0:T(8,128)(2,1)S(1)}, bf16[2,3,64,128]{3,2,1,0:T(8,128)(2,1)S(1)}, u32[]{:S(2)}, u32[]{:S(2)}) collective-permute-start(bf16[2,3,64,128]{3,2,1,0:T(8,128)(2,1)S(1)} %get-tuple-element.106), channel_id=1, source_target_pairs={{0,6},{1,7},{2,4},{3,5},{4,2},{5,3},{6,0},{7,1},{8,14},{9,15},{10,... | collective-permute-start | bytes 294920 | tf_op jit(solution)/shard_map/ppermute | solution.py:304
  104.7 8.5 %collective-permute-start.27 = (bf16[2,3,64,128]{3,2,1,0:T(8,128)(2,1)S(1)}, bf16[2,3,64,128]{3,2,1,0:T(8,128)(2,1)S(1)}, u32[]{:S(2)}, u32[]{:S(2)}) collective-permute-start(bf16[2,3,64,128]{3,2,1,0:T(8,128)(2,1)S(1)} %get-tuple-element.107), channel_id=1, source_target_pairs={{0,7},{1,6},{2,5},{3,4},{4,3},{5,2},{6,1},{7,0},{8,15},{9,14},{10,... | collective-permute-start | bytes 294920 | tf_op jit(solution)/shard_map/ppermute | solution.py:304
  107.5 8.5 %collective-permute-start.23 = (bf16[2,256,128]{2,1,0:T(8,128)(2,1)S(1)}, bf16[2,256,128]{2,1,0:T(8,128)(2,1)S(1)}, u32[]{:S(2)}, u32[]{:S(2)}) collective-permute-start(bf16[2,256,128]{2,1,0:T(8,128)(2,1)S(1)} %get-tuple-element.101), channel_id=1, source_target_pairs={{0,8},{8,0},{16,24},{24,16},{1,9},{9,1},{17,25},{25,17},{2,10},{10... | collective-permute-start | bytes 393224 | tf_op jit(solution)/shard_map/ppermute | solution.py:308
  108.5 7.6 %collective-permute-start.24 = (bf16[2,256,128]{2,1,0:T(8,128)(2,1)S(1)}, bf16[2,256,128]{2,1,0:T(8,128)(2,1)S(1)}, u32[]{:S(2)}, u32[]{:S(2)}) collective-permute-start(bf16[2,256,128]{2,1,0:T(8,128)(2,1)S(1)} %get-tuple-element.102), channel_id=1, source_target_pairs={{0,16},{8,24},{16,0},{24,8},{1,17},{9,25},{17,1},{25,9},{2,18},{10... | collective-permute-start | bytes 393224 | tf_op jit(solution)/shard_map/ppermute | solution.py:308
  114.1 2.0 %collective-permute-start.28 = (bf16[2,256,128]{2,1,0:T(8,128)(2,1)S(1)}, bf16[2,256,128]{2,1,0:T(8,128)(2,1)S(1)}, u32[]{:S(2)}, u32[]{:S(2)}) collective-permute-start(bf16[2,256,128]{2,1,0:T(8,128)(2,1)S(1)} %get-tuple-element.109), channel_id=1, source_target_pairs={{0,8},{8,0},{16,24},{24,16},{1,9},{9,1},{17,25},{25,17},{2,10},{10... | collective-permute-start | bytes 393224 | tf_op jit(solution)/shard_map/ppermute | solution.py:308
  114.2 6.3 %collective-permute-start.29 = (bf16[2,256,128]{2,1,0:T(8,128)(2,1)S(1)}, bf16[2,256,128]{2,1,0:T(8,128)(2,1)S(1)}, u32[]{:S(2)}, u32[]{:S(2)}) collective-permute-start(bf16[2,256,128]{2,1,0:T(8,128)(2,1)S(1)} %get-tuple-element.110), channel_id=1, source_target_pairs={{0,16},{8,24},{16,0},{24,8},{1,17},{9,25},{17,1},{25,9},{2,18},{10... | collective-permute-start | bytes 393224 | tf_op jit(solution)/shard_map/ppermute | solution.py:308
  115.5 6.9 %collective-permute-start.30 = (bf16[2,256,128]{2,1,0:T(8,128)(2,1)S(1)}, bf16[2,256,128]{2,1,0:T(8,128)(2,1)S(1)}, u32[]{:S(2)}, u32[]{:S(2)}) collective-permute-start(bf16[2,256,128]{2,1,0:T(8,128)(2,1)S(1)} %get-tuple-element.111), channel_id=1, source_target_pairs={{0,24},{8,16},{16,8},{24,0},{1,25},{9,17},{17,9},{25,1},{2,26},{10... | collective-permute-start | bytes 393224 | tf_op jit(solution)/shard_map/ppermute | solution.py:308

commit v13 on v11

--- a/solution.py
+++ b/solution.py
@@ -13,6 +13,7 @@
 LIST = 8
 CAP = 3
 STEP_BLOCKS = 4
+SPLIT_STEPS = 4
 TOGETHER = 4
 NEG_FILL = -1e30
 SCALE = HEAD_DIM ** (-0.5)
@@ -51,20 +52,13 @@
     return pl.ds(pl.multiple_of(col, HEAD_DIM), HEAD_DIM)
 
 
-def split_kernel(place, k_ref, v_ref, *refs):
-    *outs, sem = refs
+def split_kernel(place, k_ref, v_ref, *outs):
     heads, head_count = len(outs), outs[0].shape[0]
-    copies = []
     for r, out in enumerate(outs):
         for h in range(head_count):
             cols = head_columns(place, r, heads, h, head_count)
-            for kv, ref in enumerate((k_ref, v_ref)):
-                at = (r * head_count + h) * 2 + kv
-                copies.append(pltpu.make_async_copy(ref.at[:, cols], out.at[h, kv], sem.at[at]))
-    for copy in copies:
-        copy.start()
-    for copy in copies:
-        copy.wait()
+            out[h, 0] = k_ref[:, cols]
+            out[h, 1] = v_ref[:, cols]
 
 
 def join_kernel(place, *refs, heads):
@@ -249,6 +243,23 @@
     )(*scalars, *arrays)
 
 
+def split(place, key_states, value_states, heads, head_count):
+    quarter, width = key_states.shape
+    rows = quarter // SPLIT_STEPS
+    return pl.pallas_call(
+        split_kernel,
+        grid_spec=pltpu.PrefetchScalarGridSpec(
+            num_scalar_prefetch=1,
+            grid=(SPLIT_STEPS,),
+            in_specs=[pl.BlockSpec((rows, width), lambda i, *_: (i, 0))] * 2,
+            out_specs=[pl.BlockSpec((head_count, 2, rows, HEAD_DIM), lambda i, *_: (0, 0, i, 0))] * heads,
+        ),
+        out_shape=[bf16(head_count, 2, quarter, HEAD_DIM)] * heads,
+        compiler_params=params(VMEM_MOST),
+        name="split",
+    )(place, key_states, value_states)
+
+
 def attend(place, source, asked, queries, out_grad, own, far, head, last, earlier, shard_count):
     tokens_here, width = queries.shape
     blocks_here = tokens_here // BLK
@@ -325,16 +336,7 @@
     head_count = key_states.shape[1] // heads // HEAD_DIM
     place = jnp.stack([shard_index, lax.axis_index("head")]).astype(jnp.int32)
 
-    pieces = call(
-        split_kernel,
-        [place],
-        [key_states, value_states],
-        [bf16(head_count, 2, quarter, HEAD_DIM)] * heads,
-        [pltpu.SemaphoreType.DMA((2 * heads * head_count,))],
-        "split",
-        any_in=True,
-        limit=VMEM_MOST,
-    )
+    pieces = split(place, key_states, value_states, heads, head_count)
     own = [pieces[0]] + [send(pieces[r], "head", heads, r) for r in range(1, heads)]
 
     requests, source = requests_of(after(block_lists, *own[1:2]).reshape(-1), blocks_here, shard_index, shard_count)
@@ -362,7 +364,7 @@
         last = h == head_count - 1
         ahead = {}
         if not last:
-            ahead = exchange([(r, after(x, *come.values())) for r, x in picked(h + 1, wide)])
+            ahead = exchange([(r, after(x, *[come[n] for n in steps[:3]])) for r, x in picked(h + 1, wide)])
         attended, query_grad, near, *go = attend(
             place, source, asked, queries, out_grad, own, [come[r] for r in steps], h, last, earlier, shard_count
         )

time: 120 us -> 126 us (1.050)
  starting transfers between devices: 50.2 us -> 55.7 us
    ppermute x28, starting transfers between devices: 39.8 us -> 45.2 us  [send(): lax.ppermute(x, axis, [(i, partner(i, r, count)) for i in range(count)])]
    pallas_call x0 -> x1, Pallas kernels: none -> 4.16 us  [split(): pl.pallas_call(split_kernel, grid_spec=pltpu.PrefetchScalarGridSpec(num_s...]
    pallas_call x6 -> x5, Pallas kernels: 7.83 us -> 4.8 us  [call(): pl.pallas_call(kernel, grid_spec=pltpu.PrefetchScalarGridSpec(num_scalar_...]
  transfers between devices with their start and end apart: 35 -> 35, of which waited for: 13 -> 12; matrix products, arithmetic and copies ran while one was open for 2% -> 2% of each run, Pallas kernels for 22% -> 21%
where the time goes in v13:
time: 126 us
  starting transfers between devices  55.7 us (44%)
  Pallas kernels  33.2 us (26%)
  waiting for transfers between devices  31.7 us (25%)
  local copies, waits for them, and re-layouts  2.48 us (2%)
  other arithmetic  1.79 us (1%)
    ppermute x28, starting transfers between devices, send(): lax.ppermute(x, axis, [(i, partner(i, r, count)) for i in range(count)])  45.2 us
    pallas_call x2, Pallas kernels, attend(): pl.pallas_call(functools.partial(attend_kernel, heads=len(own), head=head...  24.3 us
    ppermute x28, waiting for transfers between devices, send(): lax.ppermute(x, axis, [(i, partner(i, r, count)) for i in range(count)])  23.3 us
    ppermute x6, waiting for transfers between devices, send_back(): lax.ppermute(x, axis, [(i, origin(i, r, count)) for i in range(count)])  6.4 us
    all_to_all x1, starting transfers between devices, per_device(): lax.all_to_all(requests, 'ctx', split_axis=0, concat_axis=0, tiled=True)  6.07 us
    pallas_call x5, Pallas kernels, call(): pl.pallas_call(kernel, grid_spec=pltpu.PrefetchScalarGridSpec(num_scalar_...  4.8 us
    ppermute x6, starting transfers between devices, send_back(): lax.ppermute(x, axis, [(i, origin(i, r, count)) for i in range(count)])  4.45 us
    pallas_call x1, Pallas kernels, split(): pl.pallas_call(split_kernel, grid_spec=pltpu.PrefetchScalarGridSpec(num_s...  4.16 us
  transfers between devices with their start and end apart: 35, of which 12 were waited for; matrix products, arithmetic and copies ran while one was open for 2% of the time, Pallas kernels for 21%

profile of v13, /device:TPU:0, one launch (start us, length us, event | category | flops | bytes accessed | tf_op | source)
XLA Modules:
  0.0 125.6 jit_solution(3599178074276006147)
XLA Ops:
  1.2 4.2 %split.1 = (bf16[2,2,256,128]{3,2,1,0:T(8,128)(2,1)}, bf16[2,2,256,128]{3,2,1,0:T(8,128)(2,1)}, bf16[2,2,256,128]{3,2,1,0:T(8,128)(2,1)}, bf16[2,2,256,128]{3,2,1,0:T(8,128)(2,1)}) custom-call(s32[2]{0:T(128)} %pad_add_fusion.place, bf16[256,1024]{1,0:T(8,128)(2,1)} %k_ref.1, bf16[256,1024]{1,0:T(8,128)(2,1)} %v_ref.1), custom_call_target="tpu_custom_call" | custom-call | tf_op jit(solution)/shard_map/split/pallas_call | solution.py:249
  5.8 2.6 %collective-permute-start.1 = (bf16[2,2,256,128]{3,2,1,0:T(8,128)(2,1)}, bf16[2,2,256,128]{3,2,1,0:T(8,128)(2,1)S(1)}, u32[]{:S(2)}, u32[]{:S(2)}) collective-permute-start(bf16[2,2,256,128]{3,2,1,0:T(8,128)(2,1)} %get-tuple-element.59), channel_id=1, source_target_pairs={{0,16},{8,24},{16,0},{24,8},{1,17},{9,25},{17,1},{25,9},{2,18},{10... | collective-permute-start | bytes 786440 | tf_op jit(solution)/shard_map/ppermute | solution.py:303
  8.5 0.8 copy.14
  9.7 0.7 select_reduce_fusion
  10.4 6.1 %all-to-all-start = ((s32[8,1,128]{2,1,0:T(1,128)}), s32[8,1,128]{2,1,0:T(1,128)S(1)}, u32[]{:S(2)}, u32[]{:S(2)}) async-start(s32[8,1,128]{2,1,0:T(1,128)} %bitcast.3), calls=%async_computation | async-start | bytes 8192 | tf_op jit(solution)/shard_map/all_to_all | solution.py:343
  16.5 4.3 %collective-permute-done.2.refs_3_ = bf16[2,2,256,128]{3,2,1,0:T(8,128)(2,1)S(1)} collective-permute-done((bf16[2,2,256,128]{3,2,1,0:T(8,128)(2,1)}, bf16[2,2,256,128]{3,2,1,0:T(8,128)(2,1)S(1)}, u32[]{:S(2)}, u32[]{:S(2)}) %collective-permute-start.2) | collective-permute-done | bytes 262176 | tf_op jit(solution)/shard_map/ppermute | solution.py:303
  20.9 2.0 %all-to-all-done = s32[8,1,128]{2,1,0:T(1,128)S(1)} async-done(((s32[8,1,128]{2,1,0:T(1,128)}), s32[8,1,128]{2,1,0:T(1,128)S(1)}, u32[]{:S(2)}, u32[]{:S(2)}) %all-to-all-start) | async-done | bytes 4128 | tf_op jit(solution)/shard_map/all_to_all | solution.py:343
  22.9 0.9 copy-done
  23.8 0.6 copy-done.1
  24.4 0.7 pick.2
  25.1 0.6 collective-permute-start.3
  25.8 0.6 collective-permute-start.4
  26.5 2.7 %collective-permute-start.5 = (bf16[2,3,64,128]{3,2,1,0:T(8,128)(2,1)S(1)}, bf16[2,3,64,128]{3,2,1,0:T(8,128)(2,1)S(1)}, u32[]{:S(2)}, u32[]{:S(2)}) collective-permute-start(bf16[2,3,64,128]{3,2,1,0:T(8,128)(2,1)S(1)} %get-tuple-element.63), channel_id=1, source_target_pairs={{0,4},{1,5},{2,6},{3,7},{4,0},{5,1},{6,2},{7,3},{8,12},{9,13},{10,... | collective-permute-start | bytes 294920 | tf_op jit(solution)/shard_map/ppermute | solution.py:303
  29.2 1.2 collective-permute-start.6
  30.4 1.6 %collective-permute-start.7 = (bf16[2,3,64,128]{3,2,1,0:T(8,128)(2,1)S(1)}, bf16[2,3,64,128]{3,2,1,0:T(8,128)(2,1)S(1)}, u32[]{:S(2)}, u32[]{:S(2)}) collective-permute-start(bf16[2,3,64,128]{3,2,1,0:T(8,128)(2,1)S(1)} %get-tuple-element.65), channel_id=1, source_target_pairs={{0,6},{1,7},{2,4},{3,5},{4,2},{5,3},{6,0},{7,1},{8,14},{9,15},{10,... | collective-permute-start | bytes 294920 | tf_op jit(solution)/shard_map/ppermute | solution.py:303
  31.9 2.3 %collective-permute-start.8 = (bf16[2,3,64,128]{3,2,1,0:T(8,128)(2,1)S(1)}, bf16[2,3,64,128]{3,2,1,0:T(8,128)(2,1)S(1)}, u32[]{:S(2)}, u32[]{:S(2)}) collective-permute-start(bf16[2,3,64,128]{3,2,1,0:T(8,128)(2,1)S(1)} %get-tuple-element.66), channel_id=1, source_target_pairs={{0,7},{1,6},{2,5},{3,4},{4,3},{5,2},{6,1},{7,0},{8,15},{9,14},{10,... | collective-permute-start | bytes 294920 | tf_op jit(solution)/shard_map/ppermute | solution.py:303
  34.8 0.7 pick.3
  35.5 5.6 %collective-permute-done.5.refs_6_ = bf16[2,3,64,128]{3,2,1,0:T(8,128)(2,1)S(1)} collective-permute-done((bf16[2,3,64,128]{3,2,1,0:T(8,128)(2,1)S(1)}, bf16[2,3,64,128]{3,2,1,0:T(8,128)(2,1)S(1)}, u32[]{:S(2)}, u32[]{:S(2)}) %collective-permute-start.5) | collective-permute-done | bytes 98336 | tf_op jit(solution)/shard_map/ppermute | solution.py:303
  41.0 3.3 %collective-permute-done.6.refs_7_ = bf16[2,3,64,128]{3,2,1,0:T(8,128)(2,1)S(1)} collective-permute-done((bf16[2,3,64,128]{3,2,1,0:T(8,128)(2,1)S(1)}, bf16[2,3,64,128]{3,2,1,0:T(8,128)(2,1)S(1)}, u32[]{:S(2)}, u32[]{:S(2)}) %collective-permute-start.6) | collective-permute-done | bytes 98336 | tf_op jit(solution)/shard_map/ppermute | solution.py:303
  44.3 3.8 %collective-permute-start.14 = (bf16[2,3,64,128]{3,2,1,0:T(8,128)(2,1)S(1)}, bf16[2,3,64,128]{3,2,1,0:T(8,128)(2,1)S(1)}, u32[]{:S(2)}, u32[]{:S(2)}) collective-permute-start(bf16[2,3,64,128]{3,2,1,0:T(8,128)(2,1)S(1)} %get-tuple-element.75), channel_id=1, source_target_pairs={{0,6},{1,7},{2,4},{3,5},{4,2},{5,3},{6,0},{7,1},{8,14},{9,15},{10,... | collective-permute-start | bytes 294920 | tf_op jit(solution)/shard_map/ppermute | solution.py:303
  48.1 1.1 collective-permute-start.15
  49.2 12.1 %attend.2 = (bf16[1024,1024]{1,0:T(8,128)(2,1)}, bf16[1024,1024]{1,0:T(8,128)(2,1)}, f32[2,16,64,128]{3,2,1,0:T(8,128)S(1)}, bf16[2,3,64,128]{3,2,1,0:T(8,128)(2...) custom-call(s32[2]{0:T(128)S(1)} %copy-done.1, ...), custom_call_target="tpu_custom_call" | custom-call | flops 3221225472 | bytes 20971520 | tf_op jit(solution)/shard_map/attend/pallas_call | solution.py:272
  61.8 10.1 %collective-permute-start.11 = (bf16[2,3,64,128]{3,2,1,0:T(8,128)(2,1)S(1)}, bf16[2,3,64,128]{3,2,1,0:T(8,128)(2,1)S(1)}, u32[]{:S(2)}, u32[]{:S(2)}) collective-permute-start(bf16[2,3,64,128]{3,2,1,0:T(8,128)(2,1)S(1)} %get-tuple-element.69), channel_id=1, source_target_pairs={{0,2},{1,3},{2,0},{3,1},{4,6},{5,7},{6,4},{7,5},{8,10},{9,11},{10,... | collective-permute-start | bytes 294920 | tf_op jit(solution)/shard_map/ppermute | solution.py:303
  71.9 1.1 collective-permute-start.16
  73.0 1.3 %collective-permute-start.17 = (bf16[2,3,64,128]{3,2,1,0:T(8,128)(2,1)S(1)}, bf16[2,3,64,128]{3,2,1,0:T(8,128)(2,1)S(1)}, u32[]{:S(2)}, u32[]{:S(2)}) collective-permute-start(bf16[2,3,64,128]{3,2,1,0:T(8,128)(2,1)S(1)} %get-tuple-element.86), channel_id=1, source_target_pairs={{0,4},{1,5},{2,6},{3,7},{4,0},{5,1},{6,2},{7,3},{8,12},{9,13},{10,... | collective-permute-start | bytes 294920 | tf_op jit(solution)/shard_map/ppermute | solution.py:303
  74.3 1.6 %collective-permute-start.18 = (bf16[2,3,64,128]{3,2,1,0:T(8,128)(2,1)S(1)}, bf16[2,3,64,128]{3,2,1,0:T(8,128)(2,1)S(1)}, u32[]{:S(2)}, u32[]{:S(2)}) collective-permute-start(bf16[2,3,64,128]{3,2,1,0:T(8,128)(2,1)S(1)} %get-tuple-element.87), channel_id=1, source_target_pairs={{0,5},{1,4},{2,7},{3,6},{4,1},{5,0},{6,3},{7,2},{8,13},{9,12},{10,... | collective-permute-start | bytes 294920 | tf_op jit(solution)/shard_map/ppermute | solution.py:303
  75.9 1.5 %collective-permute-start.19 = (bf16[2,3,64,128]{3,2,1,0:T(8,128)(2,1)S(1)}, bf16[2,3,64,128]{3,2,1,0:T(8,128)(2,1)S(1)}, u32[]{:S(2)}, u32[]{:S(2)}) collective-permute-start(bf16[2,3,64,128]{3,2,1,0:T(8,128)(2,1)S(1)} %get-tuple-element.88), channel_id=1, source_target_pairs={{0,6},{1,7},{2,4},{3,5},{4,2},{5,3},{6,0},{7,1},{8,14},{9,15},{10,... | collective-permute-start | bytes 294920 | tf_op jit(solution)/shard_map/ppermute | solution.py:303
  77.4 3.3 %collective-permute-start.20 = (bf16[2,3,64,128]{3,2,1,0:T(8,128)(2,1)S(1)}, bf16[2,3,64,128]{3,2,1,0:T(8,128)(2,1)S(1)}, u32[]{:S(2)}, u32[]{:S(2)}) collective-permute-start(bf16[2,3,64,128]{3,2,1,0:T(8,128)(2,1)S(1)} %get-tuple-element.89), channel_id=1, source_target_pairs={{0,7},{1,6},{2,5},{3,4},{4,3},{5,2},{6,1},{7,0},{8,15},{9,14},{10,... | collective-permute-start | bytes 294920 | tf_op jit(solution)/shard_map/ppermute | solution.py:303
  80.7 12.1 %attend.3 = (bf16[1024,1024]{1,0:T(8,128)(2,1)}, bf16[1024,1024]{1,0:T(8,128)(2,1)}, f32[2,16,64,128]{3,2,1,0:T(8,128)S(1)}, bf16[2,3,64,128]{3,2,1,0:T(8,128)(2...) custom-call(s32[2]{0:T(128)S(1)} %copy-done.1, ...), custom_call_target="tpu_custom_call", output_to_operand_aliasing={{0}: (16, {}), {1}: (17, {})} | custom-call | flops 3221225472 | bytes 20971520 | tf_op jit(solution)/shard_map/attend/pallas_call | solution.py:272
  92.8 0.9 gather_sum.2
  93.8 0.6 collective-permute-start.24
  94.4 1.9 %collective-permute-start.26 = (bf16[2,3,64,128]{3,2,1,0:T(8,128)(2,1)S(1)}, bf16[2,3,64,128]{3,2,1,0:T(8,128)(2,1)S(1)}, u32[]{:S(2)}, u32[]{:S(2)}) collective-permute-start(bf16[2,3,64,128]{3,2,1,0:T(8,128)(2,1)S(1)} %get-tuple-element.97), channel_id=1, source_target_pairs={{0,4},{1,5},{2,6},{3,7},{4,0},{5,1},{6,2},{7,3},{8,12},{9,13},{10,... | collective-permute-start | bytes 294920 | tf_op jit(solution)/shard_map/ppermute | solution.py:303
  96.3 2.1 %collective-permute-start.27 = (bf16[2,3,64,128]{3,2,1,0:T(8,128)(2,1)S(1)}, bf16[2,3,64,128]{3,2,1,0:T(8,128)(2,1)S(1)}, u32[]{:S(2)}, u32[]{:S(2)}) collective-permute-start(bf16[2,3,64,128]{3,2,1,0:T(8,128)(2,1)S(1)} %get-tuple-element.98), channel_id=1, source_target_pairs={{0,5},{1,4},{2,7},{3,6},{4,1},{5,0},{6,3},{7,2},{8,13},{9,12},{10,... | collective-permute-start | bytes 294920 | tf_op jit(solution)/shard_map/ppermute | solution.py:303
  98.4 0.7 collective-permute-done.24.refs_0_
  99.1 1.3 %collective-permute-start.28 = (bf16[2,3,64,128]{3,2,1,0:T(8,128)(2,1)S(1)}, bf16[2,3,64,128]{3,2,1,0:T(8,128)(2,1)S(1)}, u32[]{:S(2)}, u32[]{:S(2)}) collective-permute-start(bf16[2,3,64,128]{3,2,1,0:T(8,128)(2,1)S(1)} %get-tuple-element.99), channel_id=1, source_target_pairs={{0,6},{1,7},{2,4},{3,5},{4,2},{5,3},{6,0},{7,1},{8,14},{9,15},{10,... | collective-permute-start | bytes 294920 | tf_op jit(solution)/shard_map/ppermute | solution.py:303
  100.4 0.9 collective-permute-done.25.refs_1_
  101.3 2.5 %collective-permute-start.29 = (bf16[2,3,64,128]{3,2,1,0:T(8,128)(2,1)S(1)}, bf16[2,3,64,128]{3,2,1,0:T(8,128)(2,1)S(1)}, u32[]{:S(2)}, u32[]{:S(2)}) collective-permute-start(bf16[2,3,64,128]{3,2,1,0:T(8,128)(2,1)S(1)} %get-tuple-element.100), channel_id=1, source_target_pairs={{0,7},{1,6},{2,5},{3,4},{4,3},{5,2},{6,1},{7,0},{8,15},{9,14},{10,... | collective-permute-start | bytes 294920 | tf_op jit(solution)/shard_map/ppermute | solution.py:303
  103.8 5.2 %collective-permute-done.26.refs_2_ = bf16[2,3,64,128]{3,2,1,0:T(8,128)(2,1)S(1)} collective-permute-done((bf16[2,3,64,128]{3,2,1,0:T(8,128)(2,1)S(1)}, bf16[2,3,64,128]{3,2,1,0:T(8,128)(2,1)S(1)}, u32[]{:S(2)}, u32[]{:S(2)}) %collective-permute-start.26) | collective-permute-done | bytes 98336 | tf_op jit(solution)/shard_map/ppermute | solution.py:303
  109.0 0.9 collective-permute-start.21
  109.9 2.7 %collective-permute-done.27.refs_3_ = bf16[2,3,64,128]{3,2,1,0:T(8,128)(2,1)S(1)} collective-permute-done((bf16[2,3,64,128]{3,2,1,0:T(8,128)(2,1)S(1)}, bf16[2,3,64,128]{3,2,1,0:T(8,128)(2,1)S(1)}, u32[]{:S(2)}, u32[]{:S(2)}) %collective-permute-start.27) | collective-permute-done | bytes 98336 | tf_op jit(solution)/shard_map/ppermute | solution.py:303
  112.6 1.5 %collective-permute-start.22 = (bf16[2,256,128]{2,1,0:T(8,128)(2,1)S(1)}, bf16[2,256,128]{2,1,0:T(8,128)(2,1)S(1)}, u32[]{:S(2)}, u32[]{:S(2)}) collective-permute-start(bf16[2,256,128]{2,1,0:T(8,128)(2,1)S(1)} %get-tuple-element.92), channel_id=1, source_target_pairs={{0,16},{8,24},{16,0},{24,8},{1,17},{9,25},{17,1},{25,9},{2,18},{10... | collective-permute-start | bytes 393224 | tf_op jit(solution)/shard_map/ppermute | solution.py:307
  114.1 0.6 collective-permute-done.30.refs_6_
  114.7 0.9 gather_sum.3
  115.7 0.7 collective-permute-start.32
  116.5 1.1 collective-permute-start.33
  118.0 4.0 %collective-permute-done.32.refs_6_ = bf16[2,256,128]{2,1,0:T(8,128)(2,1)S(1)} collective-permute-done((bf16[2,256,128]{2,1,0:T(8,128)(2,1)S(1)}, bf16[2,256,128]{2,1,0:T(8,128)(2,1)S(1)}, u32[]{:S(2)}, u32[]{:S(2)}) %collective-permute-start.32) | collective-permute-done | bytes 131104 | tf_op jit(solution)/shard_map/ppermute | solution.py:307
  122.1 1.9 %collective-permute-done.33.refs_7_ = bf16[2,256,128]{2,1,0:T(8,128)(2,1)S(1)} collective-permute-done((bf16[2,256,128]{2,1,0:T(8,128)(2,1)S(1)}, bf16[2,256,128]{2,1,0:T(8,128)(2,1)S(1)}, u32[]{:S(2)}, u32[]{:S(2)}) %collective-permute-start.33) | collective-permute-done | bytes 131104 | tf_op jit(solution)/shard_map/ppermute | solution.py:307
  124.0 1.6 %join.1 = (bf16[256,1024]{1,0:T(8,128)(2,1)}, bf16[256,1024]{1,0:T(8,128)(2,1)}) custom-call(s32[2]{0:T(128)S(1)} %copy-done.1, bf16[2,256,128]{2,1,0:T(8,128)(2,1)S(1)} %get-tuple-element.90.refs_0_, bf16[2,256,128]{2,1,0:T(8,128)(2,1)S(1)} %collective-permute-done.21.refs_1_, bf16[2,256,128]{2,1,0:T(8,128)(2,1)S(1)} %collective-permute-done.22.refs_2_, ...), custom_call_target="tpu_custom_call" | custom-call | tf_op jit(solution)/shard_map/join/pallas_call | solution.py:231
  (48 shorter events, 3.5 us)
Async XLA Ops:
  5.4 3.1 %collective-permute-start = (bf16[2,2,256,128]{3,2,1,0:T(8,128)(2,1)}, bf16[2,2,256,128]{3,2,1,0:T(8,128)(2,1)S(1)}, u32[]{:S(2)}, u32[]{:S(2)}) collective-permute-start(bf16[2,2,256,128]{3,2,1,0:T(8,128)(2,1)} %get-tuple-element.56), channel_id=1, source_target_pairs={{0,8},{8,0},{16,24},{24,16},{1,9},{9,1},{17,25},{25,17},{2,10},{10... | collective-permute-start | bytes 786440 | tf_op jit(solution)/shard_map/ppermute | solution.py:303
  5.8 10.7 %collective-permute-start.1 = (bf16[2,2,256,128]{3,2,1,0:T(8,128)(2,1)}, bf16[2,2,256,128]{3,2,1,0:T(8,128)(2,1)S(1)}, u32[]{:S(2)}, u32[]{:S(2)}) collective-permute-start(bf16[2,2,256,128]{3,2,1,0:T(8,128)(2,1)} %get-tuple-element.59), channel_id=1, source_target_pairs={{0,16},{8,24},{16,0},{24,8},{1,17},{9,25},{17,1},{25,9},{2,18},{10... | collective-permute-start | bytes 786440 | tf_op jit(solution)/shard_map/ppermute | solution.py:303
  8.4 12.5 %collective-permute-start.2 = (bf16[2,2,256,128]{3,2,1,0:T(8,128)(2,1)}, bf16[2,2,256,128]{3,2,1,0:T(8,128)(2,1)S(1)}, u32[]{:S(2)}, u32[]{:S(2)}) collective-permute-start(bf16[2,2,256,128]{3,2,1,0:T(8,128)(2,1)} %get-tuple-element.60), channel_id=1, source_target_pairs={{0,24},{8,16},{16,8},{24,0},{1,25},{9,17},{17,9},{25,1},{2,26},{10... | collective-permute-start | bytes 786440 | tf_op jit(solution)/shard_map/ppermute | solution.py:303
  10.4 12.5 %all-to-all-start = ((s32[8,1,128]{2,1,0:T(1,128)}), s32[8,1,128]{2,1,0:T(1,128)S(1)}, u32[]{:S(2)}, u32[]{:S(2)}) async-start(s32[8,1,128]{2,1,0:T(1,128)} %bitcast.3), calls=%async_computation | async-start | bytes 8192 | tf_op jit(solution)/shard_map/all_to_all | solution.py:343
  22.9 1.0 copy-start
  23.8 0.6 copy-start.1
  25.1 6.8 %collective-permute-start.3 = (bf16[2,3,64,128]{3,2,1,0:T(8,128)(2,1)S(1)}, bf16[2,3,64,128]{3,2,1,0:T(8,128)(2,1)S(1)}, u32[]{:S(2)}, u32[]{:S(2)}) collective-permute-start(bf16[2,3,64,128]{3,2,1,0:T(8,128)(2,1)S(1)} %get-tuple-element.61), channel_id=1, source_target_pairs={{0,1},{1,0},{2,3},{3,2},{4,5},{5,4},{6,7},{7,6},{8,9},{9,8},{10,11... | collective-permute-start | bytes 294920 | tf_op jit(solution)/shard_map/ppermute | solution.py:303
  25.8 8.5 %collective-permute-start.4 = (bf16[2,3,64,128]{3,2,1,0:T(8,128)(2,1)S(1)}, bf16[2,3,64,128]{3,2,1,0:T(8,128)(2,1)S(1)}, u32[]{:S(2)}, u32[]{:S(2)}) collective-permute-start(bf16[2,3,64,128]{3,2,1,0:T(8,128)(2,1)S(1)} %get-tuple-element.62), channel_id=1, source_target_pairs={{0,2},{1,3},{2,0},{3,1},{4,6},{5,7},{6,4},{7,5},{8,10},{9,11},{10,... | collective-permute-start | bytes 294920 | tf_op jit(solution)/shard_map/ppermute | solution.py:303
  26.5 14.5 %collective-permute-start.5 = (bf16[2,3,64,128]{3,2,1,0:T(8,128)(2,1)S(1)}, bf16[2,3,64,128]{3,2,1,0:T(8,128)(2,1)S(1)}, u32[]{:S(2)}, u32[]{:S(2)}) collective-permute-start(bf16[2,3,64,128]{3,2,1,0:T(8,128)(2,1)S(1)} %get-tuple-element.63), channel_id=1, source_target_pairs={{0,4},{1,5},{2,6},{3,7},{4,0},{5,1},{6,2},{7,3},{8,12},{9,13},{10,... | collective-permute-start | bytes 294920 | tf_op jit(solution)/shard_map/ppermute | solution.py:303
  29.2 15.1 %collective-permute-start.6 = (bf16[2,3,64,128]{3,2,1,0:T(8,128)(2,1)S(1)}, bf16[2,3,64,128]{3,2,1,0:T(8,128)(2,1)S(1)}, u32[]{:S(2)}, u32[]{:S(2)}) collective-permute-start(bf16[2,3,64,128]{3,2,1,0:T(8,128)(2,1)S(1)} %get-tuple-element.64), channel_id=1, source_target_pairs={{0,5},{1,4},{2,7},{3,6},{4,1},{5,0},{6,3},{7,2},{8,13},{9,12},{10,... | collective-permute-start | bytes 294920 | tf_op jit(solution)/shard_map/ppermute | solution.py:303
  30.4 14.0 %collective-permute-start.7 = (bf16[2,3,64,128]{3,2,1,0:T(8,128)(2,1)S(1)}, bf16[2,3,64,128]{3,2,1,0:T(8,128)(2,1)S(1)}, u32[]{:S(2)}, u32[]{:S(2)}) collective-permute-start(bf16[2,3,64,128]{3,2,1,0:T(8,128)(2,1)S(1)} %get-tuple-element.65), channel_id=1, source_target_pairs={{0,6},{1,7},{2,4},{3,5},{4,2},{5,3},{6,0},{7,1},{8,14},{9,15},{10,... | collective-permute-start | bytes 294920 | tf_op jit(solution)/shard_map/ppermute | solution.py:303
  31.9 16.2 %collective-permute-start.8 = (bf16[2,3,64,128]{3,2,1,0:T(8,128)(2,1)S(1)}, bf16[2,3,64,128]{3,2,1,0:T(8,128)(2,1)S(1)}, u32[]{:S(2)}, u32[]{:S(2)}) collective-permute-start(bf16[2,3,64,128]{3,2,1,0:T(8,128)(2,1)S(1)} %get-tuple-element.66), channel_id=1, source_target_pairs={{0,7},{1,6},{2,5},{3,4},{4,3},{5,2},{6,1},{7,0},{8,15},{9,14},{10,... | collective-permute-start | bytes 294920 | tf_op jit(solution)/shard_map/ppermute | solution.py:303
  34.2 15.0 %collective-permute-start.9 = (bf16[2,3,64,128]{3,2,1,0:T(8,128)(2,1)S(1)}, bf16[2,3,64,128]{3,2,1,0:T(8,128)(2,1)S(1)}, u32[]{:S(2)}, u32[]{:S(2)}) collective-permute-start(bf16[2,3,64,128]{3,2,1,0:T(8,128)(2,1)S(1)} %get-tuple-element.67), channel_id=1, source_target_pairs={{0,3},{1,2},{2,1},{3,0},{4,7},{5,6},{6,5},{7,4},{8,11},{9,10},{10,... | collective-permute-start | bytes 294920 | tf_op jit(solution)/shard_map/ppermute | solution.py:303
  41.0 20.8 %collective-permute-start.12 = (bf16[2,3,64,128]{3,2,1,0:T(8,128)(2,1)S(1)}, bf16[2,3,64,128]{3,2,1,0:T(8,128)(2,1)S(1)}, u32[]{:S(2)}, u32[]{:S(2)}) collective-permute-start(bf16[2,3,64,128]{3,2,1,0:T(8,128)(2,1)S(1)} %get-tuple-element.71), channel_id=1, source_target_pairs={{0,4},{1,5},{2,6},{3,7},{4,0},{5,1},{6,2},{7,3},{8,12},{9,13},{10,... | collective-permute-start | bytes 294920 | tf_op jit(solution)/shard_map/ppermute | solution.py:303
  44.3 27.6 %collective-permute-start.13 = (bf16[2,3,64,128]{3,2,1,0:T(8,128)(2,1)S(1)}, bf16[2,3,64,128]{3,2,1,0:T(8,128)(2,1)S(1)}, u32[]{:S(2)}, u32[]{:S(2)}) collective-permute-start(bf16[2,3,64,128]{3,2,1,0:T(8,128)(2,1)S(1)} %get-tuple-element.73), channel_id=1, source_target_pairs={{0,5},{1,4},{2,7},{3,6},{4,1},{5,0},{6,3},{7,2},{8,13},{9,12},{10,... | collective-permute-start | bytes 294920 | tf_op jit(solution)/shard_map/ppermute | solution.py:303
  44.3 28.7 %collective-permute-start.14 = (bf16[2,3,64,128]{3,2,1,0:T(8,128)(2,1)S(1)}, bf16[2,3,64,128]{3,2,1,0:T(8,128)(2,1)S(1)}, u32[]{:S(2)}, u32[]{:S(2)}) collective-permute-start(bf16[2,3,64,128]{3,2,1,0:T(8,128)(2,1)S(1)} %get-tuple-element.75), channel_id=1, source_target_pairs={{0,6},{1,7},{2,4},{3,5},{4,2},{5,3},{6,0},{7,1},{8,14},{9,15},{10,... | collective-permute-start | bytes 294920 | tf_op jit(solution)/shard_map/ppermute | solution.py:303
  48.1 26.2 %collective-permute-start.15 = (bf16[2,3,64,128]{3,2,1,0:T(8,128)(2,1)S(1)}, bf16[2,3,64,128]{3,2,1,0:T(8,128)(2,1)S(1)}, u32[]{:S(2)}, u32[]{:S(2)}) collective-permute-start(bf16[2,3,64,128]{3,2,1,0:T(8,128)(2,1)S(1)} %get-tuple-element.77), channel_id=1, source_target_pairs={{0,7},{1,6},{2,5},{3,4},{4,3},{5,2},{6,1},{7,0},{8,15},{9,14},{10,... | collective-permute-start | bytes 294920 | tf_op jit(solution)/shard_map/ppermute | solution.py:303
  61.3 14.6 %collective-permute-start.10 = (bf16[2,3,64,128]{3,2,1,0:T(8,128)(2,1)S(1)}, bf16[2,3,64,128]{3,2,1,0:T(8,128)(2,1)S(1)}, u32[]{:S(2)}, u32[]{:S(2)}) collective-permute-start(bf16[2,3,64,128]{3,2,1,0:T(8,128)(2,1)S(1)} %get-tuple-element.68), channel_id=1, source_target_pairs={{0,1},{1,0},{2,3},{3,2},{4,5},{5,4},{6,7},{7,6},{8,9},{9,8},{10,11... | collective-permute-start | bytes 294920 | tf_op jit(solution)/shard_map/ppermute | solution.py:303
  61.8 15.6 %collective-permute-start.11 = (bf16[2,3,64,128]{3,2,1,0:T(8,128)(2,1)S(1)}, bf16[2,3,64,128]{3,2,1,0:T(8,128)(2,1)S(1)}, u32[]{:S(2)}, u32[]{:S(2)}) collective-permute-start(bf16[2,3,64,128]{3,2,1,0:T(8,128)(2,1)S(1)} %get-tuple-element.69), channel_id=1, source_target_pairs={{0,2},{1,3},{2,0},{3,1},{4,6},{5,7},{6,4},{7,5},{8,10},{9,11},{10,... | collective-permute-start | bytes 294920 | tf_op jit(solution)/shard_map/ppermute | solution.py:303
  71.9 8.8 %collective-permute-start.16 = (bf16[2,3,64,128]{3,2,1,0:T(8,128)(2,1)S(1)}, bf16[2,3,64,128]{3,2,1,0:T(8,128)(2,1)S(1)}, u32[]{:S(2)}, u32[]{:S(2)}) collective-permute-start(bf16[2,3,64,128]{3,2,1,0:T(8,128)(2,1)S(1)} %get-tuple-element.78), channel_id=1, source_target_pairs={{0,3},{1,2},{2,1},{3,0},{4,7},{5,6},{6,5},{7,4},{8,11},{9,10},{10,... | collective-permute-start | bytes 294920 | tf_op jit(solution)/shard_map/ppermute | solution.py:303
  73.0 19.8 %collective-permute-start.17 = (bf16[2,3,64,128]{3,2,1,0:T(8,128)(2,1)S(1)}, bf16[2,3,64,128]{3,2,1,0:T(8,128)(2,1)S(1)}, u32[]{:S(2)}, u32[]{:S(2)}) collective-permute-start(bf16[2,3,64,128]{3,2,1,0:T(8,128)(2,1)S(1)} %get-tuple-element.86), channel_id=1, source_target_pairs={{0,4},{1,5},{2,6},{3,7},{4,0},{5,1},{6,2},{7,3},{8,12},{9,13},{10,... | collective-permute-start | bytes 294920 | tf_op jit(solution)/shard_map/ppermute | solution.py:303
  74.3 18.5 %collective-permute-start.18 = (bf16[2,3,64,128]{3,2,1,0:T(8,128)(2,1)S(1)}, bf16[2,3,64,128]{3,2,1,0:T(8,128)(2,1)S(1)}, u32[]{:S(2)}, u32[]{:S(2)}) collective-permute-start(bf16[2,3,64,128]{3,2,1,0:T(8,128)(2,1)S(1)} %get-tuple-element.87), channel_id=1, source_target_pairs={{0,5},{1,4},{2,7},{3,6},{4,1},{5,0},{6,3},{7,2},{8,13},{9,12},{10,... | collective-permute-start | bytes 294920 | tf_op jit(solution)/shard_map/ppermute | solution.py:303
  75.9 16.9 %collective-permute-start.19 = (bf16[2,3,64,128]{3,2,1,0:T(8,128)(2,1)S(1)}, bf16[2,3,64,128]{3,2,1,0:T(8,128)(2,1)S(1)}, u32[]{:S(2)}, u32[]{:S(2)}) collective-permute-start(bf16[2,3,64,128]{3,2,1,0:T(8,128)(2,1)S(1)} %get-tuple-element.88), channel_id=1, source_target_pairs={{0,6},{1,7},{2,4},{3,5},{4,2},{5,3},{6,0},{7,1},{8,14},{9,15},{10,... | collective-permute-start | bytes 294920 | tf_op jit(solution)/shard_map/ppermute | solution.py:303
  77.4 15.4 %collective-permute-start.20 = (bf16[2,3,64,128]{3,2,1,0:T(8,128)(2,1)S(1)}, bf16[2,3,64,128]{3,2,1,0:T(8,128)(2,1)S(1)}, u32[]{:S(2)}, u32[]{:S(2)}) collective-permute-start(bf16[2,3,64,128]{3,2,1,0:T(8,128)(2,1)S(1)} %get-tuple-element.89), channel_id=1, source_target_pairs={{0,7},{1,6},{2,5},{3,4},{4,3},{5,2},{6,1},{7,0},{8,15},{9,14},{10,... | collective-permute-start | bytes 294920 | tf_op jit(solution)/shard_map/ppermute | solution.py:303
  93.7 10.1 %collective-permute-start.23 = (bf16[2,256,128]{2,1,0:T(8,128)(2,1)S(1)}, bf16[2,256,128]{2,1,0:T(8,128)(2,1)S(1)}, u32[]{:S(2)}, u32[]{:S(2)}) collective-permute-start(bf16[2,256,128]{2,1,0:T(8,128)(2,1)S(1)} %get-tuple-element.93), channel_id=1, source_target_pairs={{0,24},{8,16},{16,8},{24,0},{1,25},{9,17},{17,9},{25,1},{2,26},{10... | collective-permute-start | bytes 393224 | tf_op jit(solution)/shard_map/ppermute | solution.py:307
  93.8 5.2 %collective-permute-start.24 = (bf16[2,3,64,128]{3,2,1,0:T(8,128)(2,1)S(1)}, bf16[2,3,64,128]{3,2,1,0:T(8,128)(2,1)S(1)}, u32[]{:S(2)}, u32[]{:S(2)}) collective-permute-start(bf16[2,3,64,128]{3,2,1,0:T(8,128)(2,1)S(1)} %get-tuple-element.95), channel_id=1, source_target_pairs={{0,1},{1,0},{2,3},{3,2},{4,5},{5,4},{6,7},{7,6},{8,9},{9,8},{10,11... | collective-permute-start | bytes 294920 | tf_op jit(solution)/shard_map/ppermute | solution.py:303
  94.4 6.9 %collective-permute-start.25 = (bf16[2,3,64,128]{3,2,1,0:T(8,128)(2,1)S(1)}, bf16[2,3,64,128]{3,2,1,0:T(8,128)(2,1)S(1)}, u32[]{:S(2)}, u32[]{:S(2)}) collective-permute-start(bf16[2,3,64,128]{3,2,1,0:T(8,128)(2,1)S(1)} %get-tuple-element.96), channel_id=1, source_target_pairs={{0,2},{1,3},{2,0},{3,1},{4,6},{5,7},{6,4},{7,5},{8,10},{9,11},{10,... | collective-permute-start | bytes 294920 | tf_op jit(solution)/shard_map/ppermute | solution.py:303
  94.4 14.6 %collective-permute-start.26 = (bf16[2,3,64,128]{3,2,1,0:T(8,128)(2,1)S(1)}, bf16[2,3,64,128]{3,2,1,0:T(8,128)(2,1)S(1)}, u32[]{:S(2)}, u32[]{:S(2)}) collective-permute-start(bf16[2,3,64,128]{3,2,1,0:T(8,128)(2,1)S(1)} %get-tuple-element.97), channel_id=1, source_target_pairs={{0,4},{1,5},{2,6},{3,7},{4,0},{5,1},{6,2},{7,3},{8,12},{9,13},{10,... | collective-permute-start | bytes 294920 | tf_op jit(solution)/shard_map/ppermute | solution.py:303
  96.3 16.2 %collective-permute-start.27 = (bf16[2,3,64,128]{3,2,1,0:T(8,128)(2,1)S(1)}, bf16[2,3,64,128]{3,2,1,0:T(8,128)(2,1)S(1)}, u32[]{:S(2)}, u32[]{:S(2)}) collective-permute-start(bf16[2,3,64,128]{3,2,1,0:T(8,128)(2,1)S(1)} %get-tuple-element.98), channel_id=1, source_target_pairs={{0,5},{1,4},{2,7},{3,6},{4,1},{5,0},{6,3},{7,2},{8,13},{9,12},{10,... | collective-permute-start | bytes 294920 | tf_op jit(solution)/shard_map/ppermute | solution.py:303
  99.1 15.1 %collective-permute-start.28 = (bf16[2,3,64,128]{3,2,1,0:T(8,128)(2,1)S(1)}, bf16[2,3,64,128]{3,2,1,0:T(8,128)(2,1)S(1)}, u32[]{:S(2)}, u32[]{:S(2)}) collective-permute-start(bf16[2,3,64,128]{3,2,1,0:T(8,128)(2,1)S(1)} %get-tuple-element.99), channel_id=1, source_target_pairs={{0,6},{1,7},{2,4},{3,5},{4,2},{5,3},{6,0},{7,1},{8,14},{9,15},{10,... | collective-permute-start | bytes 294920 | tf_op jit(solution)/shard_map/ppermute | solution.py:303
  101.3 12.8 %collective-permute-start.29 = (bf16[2,3,64,128]{3,2,1,0:T(8,128)(2,1)S(1)}, bf16[2,3,64,128]{3,2,1,0:T(8,128)(2,1)S(1)}, u32[]{:S(2)}, u32[]{:S(2)}) collective-permute-start(bf16[2,3,64,128]{3,2,1,0:T(8,128)(2,1)S(1)} %get-tuple-element.100), channel_id=1, source_target_pairs={{0,7},{1,6},{2,5},{3,4},{4,3},{5,2},{6,1},{7,0},{8,15},{9,14},{10,... | collective-permute-start | bytes 294920 | tf_op jit(solution)/shard_map/ppermute | solution.py:303
  103.8 10.9 %collective-permute-start.30 = (bf16[2,3,64,128]{3,2,1,0:T(8,128)(2,1)S(1)}, bf16[2,3,64,128]{3,2,1,0:T(8,128)(2,1)S(1)}, u32[]{:S(2)}, u32[]{:S(2)}) collective-permute-start(bf16[2,3,64,128]{3,2,1,0:T(8,128)(2,1)S(1)} %get-tuple-element.101), channel_id=1, source_target_pairs={{0,3},{1,2},{2,1},{3,0},{4,7},{5,6},{6,5},{7,4},{8,11},{9,10},{10,... | collective-permute-start | bytes 294920 | tf_op jit(solution)/shard_map/ppermute | solution.py:303
  109.0 8.6 %collective-permute-start.21 = (bf16[2,256,128]{2,1,0:T(8,128)(2,1)S(1)}, bf16[2,256,128]{2,1,0:T(8,128)(2,1)S(1)}, u32[]{:S(2)}, u32[]{:S(2)}) collective-permute-start(bf16[2,256,128]{2,1,0:T(8,128)(2,1)S(1)} %get-tuple-element.91), channel_id=1, source_target_pairs={{0,8},{8,0},{16,24},{24,16},{1,9},{9,1},{17,25},{25,17},{2,10},{10... | collective-permute-start | bytes 393224 | tf_op jit(solution)/shard_map/ppermute | solution.py:307
  112.6 5.5 %collective-permute-start.22 = (bf16[2,256,128]{2,1,0:T(8,128)(2,1)S(1)}, bf16[2,256,128]{2,1,0:T(8,128)(2,1)S(1)}, u32[]{:S(2)}, u32[]{:S(2)}) collective-permute-start(bf16[2,256,128]{2,1,0:T(8,128)(2,1)S(1)} %get-tuple-element.92), channel_id=1, source_target_pairs={{0,16},{8,24},{16,0},{24,8},{1,17},{9,25},{17,1},{25,9},{2,18},{10... | collective-permute-start | bytes 393224 | tf_op jit(solution)/shard_map/ppermute | solution.py:307
  115.6 2.4 %collective-permute-start.31 = (bf16[2,256,128]{2,1,0:T(8,128)(2,1)S(1)}, bf16[2,256,128]{2,1,0:T(8,128)(2,1)S(1)}, u32[]{:S(2)}, u32[]{:S(2)}) collective-permute-start(bf16[2,256,128]{2,1,0:T(8,128)(2,1)S(1)} %get-tuple-element.103), channel_id=1, source_target_pairs={{0,8},{8,0},{16,24},{24,16},{1,9},{9,1},{17,25},{25,17},{2,10},{10... | collective-permute-start | bytes 393224 | tf_op jit(solution)/shard_map/ppermute | solution.py:307
  115.7 6.3 %collective-permute-start.32 = (bf16[2,256,128]{2,1,0:T(8,128)(2,1)S(1)}, bf16[2,256,128]{2,1,0:T(8,128)(2,1)S(1)}, u32[]{:S(2)}, u32[]{:S(2)}) collective-permute-start(bf16[2,256,128]{2,1,0:T(8,128)(2,1)S(1)} %get-tuple-element.104), channel_id=1, source_target_pairs={{0,16},{8,24},{16,0},{24,8},{1,17},{9,25},{17,1},{25,9},{2,18},{10... | collective-permute-start | bytes 393224 | tf_op jit(solution)/shard_map/ppermute | solution.py:307
  116.5 7.5 %collective-permute-start.33 = (bf16[2,256,128]{2,1,0:T(8,128)(2,1)S(1)}, bf16[2,256,128]{2,1,0:T(8,128)(2,1)S(1)}, u32[]{:S(2)}, u32[]{:S(2)}) collective-permute-start(bf16[2,256,128]{2,1,0:T(8,128)(2,1)S(1)} %get-tuple-element.105), channel_id=1, source_target_pairs={{0,24},{8,16},{16,8},{24,0},{1,25},{9,17},{17,9},{25,1},{2,26},{10... | collective-permute-start | bytes 393224 | tf_op jit(solution)/shard_map/ppermute | solution.py:307

commit v14 on v11

--- a/solution.py
+++ b/solution.py
@@ -177,7 +177,7 @@
     @pl.when(step == pl.num_programs(0) - 1)
     def _():
         for kv, factor in ((0, SCALE), (1, 1.0)):
-            near_out[kv] = total[kv, :blocks_here] * factor
+            near_out[kv] = (total[kv, :blocks_here] * factor).astype(jnp.bfloat16)
         if not last:
             fill_table(place, own, 1, table)
         for r, out in zip(steps_of(shard_count), outs):
@@ -200,7 +200,7 @@
 def gather_sum_kernel(place, asked, near, *refs, heads, shard_count):
     back, outs, total = refs[: -heads - 1], refs[-heads - 1 : -1], refs[-1]
     per_quarter = outs[0].shape[1] // BLK
-    total[...] = near[...]
+    total[...] = near[...].astype(jnp.float32)
     for r, part in zip(steps_of(shard_count), back):
         there = origin(place[0], r, shard_count)
 
@@ -275,7 +275,7 @@
                 pltpu.VMEM((2, slots, BLK, HEAD_DIM), jnp.float32),
             ],
         ),
-        out_shape=[bf16(tokens_here, width), bf16(tokens_here, width), jax.ShapeDtypeStruct(near_shape, jnp.float32)]
+        out_shape=[bf16(tokens_here, width), bf16(tokens_here, width), bf16(*near_shape)]
         + out_shapes,
         input_output_aliases={first: 0, first + 1: 1} if earlier else {},
         compiler_params=params(),

time: 120 us -> 120 us (level)
  transfers between devices with their start and end apart: 35 -> 35, of which waited for: 13 -> 13; matrix products, arithmetic and copies ran while one was open for 2% -> 2% of each run, Pallas kernels for 22% -> 21%
where the time goes in v14:
time: 120 us
  starting transfers between devices  50.1 us (42%)
  waiting for transfers between devices  32.9 us (27%)
  Pallas kernels  32.1 us (27%)
  local copies, waits for them, and re-layouts  2.48 us (2%)
  other arithmetic  1.79 us (1%)
    ppermute x28, starting transfers between devices, send(): lax.ppermute(x, axis, [(i, partner(i, r, count)) for i in range(count)])  39.8 us
    ppermute x28, waiting for transfers between devices, send(): lax.ppermute(x, axis, [(i, partner(i, r, count)) for i in range(count)])  24.5 us
    pallas_call x2, Pallas kernels, attend(): pl.pallas_call(functools.partial(attend_kernel, heads=len(own), head=head...  24.2 us
    pallas_call x6, Pallas kernels, call(): pl.pallas_call(kernel, grid_spec=pltpu.PrefetchScalarGridSpec(num_scalar_...  7.83 us
    ppermute x6, waiting for transfers between devices, send_back(): lax.ppermute(x, axis, [(i, origin(i, r, count)) for i in range(count)])  6.4 us
    all_to_all x1, starting transfers between devices, per_device(): lax.all_to_all(requests, 'ctx', split_axis=0, concat_axis=0, tiled=True)  6.07 us
    ppermute x6, starting transfers between devices, send_back(): lax.ppermute(x, axis, [(i, origin(i, r, count)) for i in range(count)])  4.25 us
  transfers between devices with their start and end apart: 35, of which 13 were waited for; matrix products, arithmetic and copies ran while one was open for 2% of the time, Pallas kernels for 21%

profile of v14, /device:TPU:0, one launch (start us, length us, event | category | flops | bytes accessed | tf_op | source)
XLA Modules:
  0.0 120.1 jit_solution(9592527972797806706)
XLA Ops:
  1.2 3.0 %split.1 = (bf16[2,2,256,128]{3,2,1,0:T(8,128)(2,1)}, bf16[2,2,256,128]{3,2,1,0:T(8,128)(2,1)}, bf16[2,2,256,128]{3,2,1,0:T(8,128)(2,1)}, bf16[2,2,256,128]{3,2,1,0:T(8,128)(2,1)}) custom-call(s32[2]{0:T(128)} %pad_add_fusion.place, bf16[256,1024]{1,0:T(8,128)(2,1)} %k_ref.1, bf16[256,1024]{1,0:T(8,128)(2,1)} %v_ref.1), custom_call_target="tpu_custom_call" | custom-call | tf_op jit(solution)/shard_map/split/pallas_call | solution.py:237
  4.8 2.6 %collective-permute-start.1 = (bf16[2,2,256,128]{3,2,1,0:T(8,128)(2,1)}, bf16[2,2,256,128]{3,2,1,0:T(8,128)(2,1)S(1)}, u32[]{:S(2)}, u32[]{:S(2)}) collective-permute-start(bf16[2,2,256,128]{3,2,1,0:T(8,128)(2,1)} %get-tuple-element.59), channel_id=1, source_target_pairs={{0,16},{8,24},{16,0},{24,8},{1,17},{9,25},{17,1},{25,9},{2,18},{10... | collective-permute-start | bytes 786440 | tf_op jit(solution)/shard_map/ppermute | solution.py:292
  7.4 0.8 copy.14
  8.7 0.7 select_reduce_fusion
  9.4 6.1 %all-to-all-start = ((s32[8,1,128]{2,1,0:T(1,128)}), s32[8,1,128]{2,1,0:T(1,128)S(1)}, u32[]{:S(2)}, u32[]{:S(2)}) async-start(s32[8,1,128]{2,1,0:T(1,128)} %bitcast.3), calls=%async_computation | async-start | bytes 8192 | tf_op jit(solution)/shard_map/all_to_all | solution.py:341
  15.5 4.3 %collective-permute-done.2.refs_3_ = bf16[2,2,256,128]{3,2,1,0:T(8,128)(2,1)S(1)} collective-permute-done((bf16[2,2,256,128]{3,2,1,0:T(8,128)(2,1)}, bf16[2,2,256,128]{3,2,1,0:T(8,128)(2,1)S(1)}, u32[]{:S(2)}, u32[]{:S(2)}) %collective-permute-start.2) | collective-permute-done | bytes 262176 | tf_op jit(solution)/shard_map/ppermute | solution.py:292
  19.8 2.0 %all-to-all-done = s32[8,1,128]{2,1,0:T(1,128)S(1)} async-done(((s32[8,1,128]{2,1,0:T(1,128)}), s32[8,1,128]{2,1,0:T(1,128)S(1)}, u32[]{:S(2)}, u32[]{:S(2)}) %all-to-all-start) | async-done | bytes 4128 | tf_op jit(solution)/shard_map/all_to_all | solution.py:341
  21.8 0.9 copy-done
  23.4 0.7 pick.2
  24.1 0.6 collective-permute-start.3
  25.5 2.7 %collective-permute-start.5 = (bf16[2,3,64,128]{3,2,1,0:T(8,128)(2,1)S(1)}, bf16[2,3,64,128]{3,2,1,0:T(8,128)(2,1)S(1)}, u32[]{:S(2)}, u32[]{:S(2)}) collective-permute-start(bf16[2,3,64,128]{3,2,1,0:T(8,128)(2,1)S(1)} %get-tuple-element.63), channel_id=1, source_target_pairs={{0,4},{1,5},{2,6},{3,7},{4,0},{5,1},{6,2},{7,3},{8,12},{9,13},{10,... | collective-permute-start | bytes 294920 | tf_op jit(solution)/shard_map/ppermute | solution.py:292
  28.1 1.2 collective-permute-start.6
  29.3 1.6 %collective-permute-start.7 = (bf16[2,3,64,128]{3,2,1,0:T(8,128)(2,1)S(1)}, bf16[2,3,64,128]{3,2,1,0:T(8,128)(2,1)S(1)}, u32[]{:S(2)}, u32[]{:S(2)}) collective-permute-start(bf16[2,3,64,128]{3,2,1,0:T(8,128)(2,1)S(1)} %get-tuple-element.65), channel_id=1, source_target_pairs={{0,6},{1,7},{2,4},{3,5},{4,2},{5,3},{6,0},{7,1},{8,14},{9,15},{10,... | collective-permute-start | bytes 294920 | tf_op jit(solution)/shard_map/ppermute | solution.py:292
  30.9 2.3 %collective-permute-start.8 = (bf16[2,3,64,128]{3,2,1,0:T(8,128)(2,1)S(1)}, bf16[2,3,64,128]{3,2,1,0:T(8,128)(2,1)S(1)}, u32[]{:S(2)}, u32[]{:S(2)}) collective-permute-start(bf16[2,3,64,128]{3,2,1,0:T(8,128)(2,1)S(1)} %get-tuple-element.66), channel_id=1, source_target_pairs={{0,7},{1,6},{2,5},{3,4},{4,3},{5,2},{6,1},{7,0},{8,15},{9,14},{10,... | collective-permute-start | bytes 294920 | tf_op jit(solution)/shard_map/ppermute | solution.py:292
  33.7 0.7 pick.3
  34.4 5.6 %collective-permute-done.5.refs_6_ = bf16[2,3,64,128]{3,2,1,0:T(8,128)(2,1)S(1)} collective-permute-done((bf16[2,3,64,128]{3,2,1,0:T(8,128)(2,1)S(1)}, bf16[2,3,64,128]{3,2,1,0:T(8,128)(2,1)S(1)}, u32[]{:S(2)}, u32[]{:S(2)}) %collective-permute-start.5) | collective-permute-done | bytes 98336 | tf_op jit(solution)/shard_map/ppermute | solution.py:292
  40.0 2.2 %collective-permute-done.6.refs_7_ = bf16[2,3,64,128]{3,2,1,0:T(8,128)(2,1)S(1)} collective-permute-done((bf16[2,3,64,128]{3,2,1,0:T(8,128)(2,1)S(1)}, bf16[2,3,64,128]{3,2,1,0:T(8,128)(2,1)S(1)}, u32[]{:S(2)}, u32[]{:S(2)}) %collective-permute-start.6) | collective-permute-done | bytes 98336 | tf_op jit(solution)/shard_map/ppermute | solution.py:292
  42.2 1.3 %collective-permute-done.9.refs_10_ = bf16[2,3,64,128]{3,2,1,0:T(8,128)(2,1)S(1)} collective-permute-done((bf16[2,3,64,128]{3,2,1,0:T(8,128)(2,1)S(1)}, bf16[2,3,64,128]{3,2,1,0:T(8,128)(2,1)S(1)}, u32[]{:S(2)}, u32[]{:S(2)}) %collective-permute-start.9) | collective-permute-done | bytes 98336 | tf_op jit(solution)/shard_map/ppermute | solution.py:292
  43.5 3.7 %collective-permute-start.12 = (bf16[2,3,64,128]{3,2,1,0:T(8,128)(2,1)S(1)}, bf16[2,3,64,128]{3,2,1,0:T(8,128)(2,1)S(1)}, u32[]{:S(2)}, u32[]{:S(2)}) collective-permute-start(bf16[2,3,64,128]{3,2,1,0:T(8,128)(2,1)S(1)} %get-tuple-element.71), channel_id=1, source_target_pairs={{0,4},{1,5},{2,6},{3,7},{4,0},{5,1},{6,2},{7,3},{8,12},{9,13},{10,... | collective-permute-start | bytes 294920 | tf_op jit(solution)/shard_map/ppermute | solution.py:292
  47.2 0.9 collective-permute-start.13
  48.2 1.3 %collective-permute-start.14 = (bf16[2,3,64,128]{3,2,1,0:T(8,128)(2,1)S(1)}, bf16[2,3,64,128]{3,2,1,0:T(8,128)(2,1)S(1)}, u32[]{:S(2)}, u32[]{:S(2)}) collective-permute-start(bf16[2,3,64,128]{3,2,1,0:T(8,128)(2,1)S(1)} %get-tuple-element.75), channel_id=1, source_target_pairs={{0,6},{1,7},{2,4},{3,5},{4,2},{5,3},{6,0},{7,1},{8,14},{9,15},{10,... | collective-permute-start | bytes 294920 | tf_op jit(solution)/shard_map/ppermute | solution.py:292
  49.5 2.5 %collective-permute-start.15 = (bf16[2,3,64,128]{3,2,1,0:T(8,128)(2,1)S(1)}, bf16[2,3,64,128]{3,2,1,0:T(8,128)(2,1)S(1)}, u32[]{:S(2)}, u32[]{:S(2)}) collective-permute-start(bf16[2,3,64,128]{3,2,1,0:T(8,128)(2,1)S(1)} %get-tuple-element.77), channel_id=1, source_target_pairs={{0,7},{1,6},{2,5},{3,4},{4,3},{5,2},{6,1},{7,0},{8,15},{9,14},{10,... | collective-permute-start | bytes 294920 | tf_op jit(solution)/shard_map/ppermute | solution.py:292
  52.0 12.1 %attend.2 = (bf16[1024,1024]{1,0:T(8,128)(2,1)}, bf16[1024,1024]{1,0:T(8,128)(2,1)}, bf16[2,16,64,128]{3,2,1,0:T(8,128)(2,1)S(1)}, bf16[2,3,64,128]{3,2,1,0:T(8,...) custom-call(s32[2]{0:T(128)S(1)} %copy-done.1, ...), custom_call_target="tpu_custom_call" | custom-call | flops 3221225472 | bytes 20971520 | tf_op jit(solution)/shard_map/attend/pallas_call | solution.py:261
  64.1 1.5 %collective-permute-start.10 = (bf16[2,3,64,128]{3,2,1,0:T(8,128)(2,1)S(1)}, bf16[2,3,64,128]{3,2,1,0:T(8,128)(2,1)S(1)}, u32[]{:S(2)}, u32[]{:S(2)}) collective-permute-start(bf16[2,3,64,128]{3,2,1,0:T(8,128)(2,1)S(1)} %get-tuple-element.68), channel_id=1, source_target_pairs={{0,1},{1,0},{2,3},{3,2},{4,5},{5,4},{6,7},{7,6},{8,9},{9,8},{10,11... | collective-permute-start | bytes 294920 | tf_op jit(solution)/shard_map/ppermute | solution.py:292
  65.7 1.9 %collective-permute-start.16 = (bf16[2,3,64,128]{3,2,1,0:T(8,128)(2,1)S(1)}, bf16[2,3,64,128]{3,2,1,0:T(8,128)(2,1)S(1)}, u32[]{:S(2)}, u32[]{:S(2)}) collective-permute-start(bf16[2,3,64,128]{3,2,1,0:T(8,128)(2,1)S(1)} %get-tuple-element.78), channel_id=1, source_target_pairs={{0,3},{1,2},{2,1},{3,0},{4,7},{5,6},{6,5},{7,4},{8,11},{9,10},{10,... | collective-permute-start | bytes 294920 | tf_op jit(solution)/shard_map/ppermute | solution.py:292
  67.6 1.1 collective-permute-start.17
  68.7 2.8 %collective-permute-start.18 = (bf16[2,3,64,128]{3,2,1,0:T(8,128)(2,1)S(1)}, bf16[2,3,64,128]{3,2,1,0:T(8,128)(2,1)S(1)}, u32[]{:S(2)}, u32[]{:S(2)}) collective-permute-start(bf16[2,3,64,128]{3,2,1,0:T(8,128)(2,1)S(1)} %get-tuple-element.87), channel_id=1, source_target_pairs={{0,5},{1,4},{2,7},{3,6},{4,1},{5,0},{6,3},{7,2},{8,13},{9,12},{10,... | collective-permute-start | bytes 294920 | tf_op jit(solution)/shard_map/ppermute | solution.py:292
  71.4 1.3 %collective-permute-start.19 = (bf16[2,3,64,128]{3,2,1,0:T(8,128)(2,1)S(1)}, bf16[2,3,64,128]{3,2,1,0:T(8,128)(2,1)S(1)}, u32[]{:S(2)}, u32[]{:S(2)}) collective-permute-start(bf16[2,3,64,128]{3,2,1,0:T(8,128)(2,1)S(1)} %get-tuple-element.88), channel_id=1, source_target_pairs={{0,6},{1,7},{2,4},{3,5},{4,2},{5,3},{6,0},{7,1},{8,14},{9,15},{10,... | collective-permute-start | bytes 294920 | tf_op jit(solution)/shard_map/ppermute | solution.py:292
  72.8 2.5 %collective-permute-start.20 = (bf16[2,3,64,128]{3,2,1,0:T(8,128)(2,1)S(1)}, bf16[2,3,64,128]{3,2,1,0:T(8,128)(2,1)S(1)}, u32[]{:S(2)}, u32[]{:S(2)}) collective-permute-start(bf16[2,3,64,128]{3,2,1,0:T(8,128)(2,1)S(1)} %get-tuple-element.89), channel_id=1, source_target_pairs={{0,7},{1,6},{2,5},{3,4},{4,3},{5,2},{6,1},{7,0},{8,15},{9,14},{10,... | collective-permute-start | bytes 294920 | tf_op jit(solution)/shard_map/ppermute | solution.py:292
  75.3 12.1 %attend.3 = (bf16[1024,1024]{1,0:T(8,128)(2,1)}, bf16[1024,1024]{1,0:T(8,128)(2,1)}, bf16[2,16,64,128]{3,2,1,0:T(8,128)(2,1)S(1)}, bf16[2,3,64,128]{3,2,1,0:T(8,...) custom-call(s32[2]{0:T(128)S(1)} %copy-done.1, ...), custom_call_target="tpu_custom_call", output_to_operand_aliasing={{0}: (16, {}), {1}: (17, {})} | custom-call | flops 3221225472 | bytes 20971520 | tf_op jit(solution)/shard_map/attend/pallas_call | solution.py:261
  87.4 0.9 gather_sum.2
  88.4 1.5 %collective-permute-start.24 = (bf16[2,3,64,128]{3,2,1,0:T(8,128)(2,1)S(1)}, bf16[2,3,64,128]{3,2,1,0:T(8,128)(2,1)S(1)}, u32[]{:S(2)}, u32[]{:S(2)}) collective-permute-start(bf16[2,3,64,128]{3,2,1,0:T(8,128)(2,1)S(1)} %get-tuple-element.95), channel_id=1, source_target_pairs={{0,1},{1,0},{2,3},{3,2},{4,5},{5,4},{6,7},{7,6},{8,9},{9,8},{10,11... | collective-permute-start | bytes 294920 | tf_op jit(solution)/shard_map/ppermute | solution.py:292
  89.9 1.8 %collective-permute-start.26 = (bf16[2,3,64,128]{3,2,1,0:T(8,128)(2,1)S(1)}, bf16[2,3,64,128]{3,2,1,0:T(8,128)(2,1)S(1)}, u32[]{:S(2)}, u32[]{:S(2)}) collective-permute-start(bf16[2,3,64,128]{3,2,1,0:T(8,128)(2,1)S(1)} %get-tuple-element.97), channel_id=1, source_target_pairs={{0,4},{1,5},{2,6},{3,7},{4,0},{5,1},{6,2},{7,3},{8,12},{9,13},{10,... | collective-permute-start | bytes 294920 | tf_op jit(solution)/shard_map/ppermute | solution.py:292
  91.7 1.2 collective-permute-start.27
  92.9 0.8 collective-permute-done.24.refs_0_
  93.7 1.5 %collective-permute-start.28 = (bf16[2,3,64,128]{3,2,1,0:T(8,128)(2,1)S(1)}, bf16[2,3,64,128]{3,2,1,0:T(8,128)(2,1)S(1)}, u32[]{:S(2)}, u32[]{:S(2)}) collective-permute-start(bf16[2,3,64,128]{3,2,1,0:T(8,128)(2,1)S(1)} %get-tuple-element.99), channel_id=1, source_target_pairs={{0,6},{1,7},{2,4},{3,5},{4,2},{5,3},{6,0},{7,1},{8,14},{9,15},{10,... | collective-permute-start | bytes 294920 | tf_op jit(solution)/shard_map/ppermute | solution.py:292
  95.2 1.6 %collective-permute-done.25.refs_1_ = bf16[2,3,64,128]{3,2,1,0:T(8,128)(2,1)S(1)} collective-permute-done((bf16[2,3,64,128]{3,2,1,0:T(8,128)(2,1)S(1)}, bf16[2,3,64,128]{3,2,1,0:T(8,128)(2,1)S(1)}, u32[]{:S(2)}, u32[]{:S(2)}) %collective-permute-start.25) | collective-permute-done | bytes 98336 | tf_op jit(solution)/shard_map/ppermute | solution.py:292
  96.8 1.6 %collective-permute-start.29 = (bf16[2,3,64,128]{3,2,1,0:T(8,128)(2,1)S(1)}, bf16[2,3,64,128]{3,2,1,0:T(8,128)(2,1)S(1)}, u32[]{:S(2)}, u32[]{:S(2)}) collective-permute-start(bf16[2,3,64,128]{3,2,1,0:T(8,128)(2,1)S(1)} %get-tuple-element.100), channel_id=1, source_target_pairs={{0,7},{1,6},{2,5},{3,4},{4,3},{5,2},{6,1},{7,0},{8,15},{9,14},{10,... | collective-permute-start | bytes 294920 | tf_op jit(solution)/shard_map/ppermute | solution.py:292
  98.4 6.4 %collective-permute-done.26.refs_2_ = bf16[2,3,64,128]{3,2,1,0:T(8,128)(2,1)S(1)} collective-permute-done((bf16[2,3,64,128]{3,2,1,0:T(8,128)(2,1)S(1)}, bf16[2,3,64,128]{3,2,1,0:T(8,128)(2,1)S(1)}, u32[]{:S(2)}, u32[]{:S(2)}) %collective-permute-start.26) | collective-permute-done | bytes 98336 | tf_op jit(solution)/shard_map/ppermute | solution.py:292
  105.4 1.5 %collective-permute-done.27.refs_3_ = bf16[2,3,64,128]{3,2,1,0:T(8,128)(2,1)S(1)} collective-permute-done((bf16[2,3,64,128]{3,2,1,0:T(8,128)(2,1)S(1)}, bf16[2,3,64,128]{3,2,1,0:T(8,128)(2,1)S(1)}, u32[]{:S(2)}, u32[]{:S(2)}) %collective-permute-start.27) | collective-permute-done | bytes 98336 | tf_op jit(solution)/shard_map/ppermute | solution.py:292
  106.9 1.6 %collective-permute-start.22 = (bf16[2,256,128]{2,1,0:T(8,128)(2,1)S(1)}, bf16[2,256,128]{2,1,0:T(8,128)(2,1)S(1)}, u32[]{:S(2)}, u32[]{:S(2)}) collective-permute-start(bf16[2,256,128]{2,1,0:T(8,128)(2,1)S(1)} %get-tuple-element.92), channel_id=1, source_target_pairs={{0,16},{8,24},{16,0},{24,8},{1,17},{9,25},{17,1},{25,9},{2,18},{10... | collective-permute-start | bytes 393224 | tf_op jit(solution)/shard_map/ppermute | solution.py:296
  108.6 0.6 collective-permute-done.30.refs_6_
  109.2 0.9 gather_sum.3
  110.2 0.9 collective-permute-start.32
  111.1 1.0 collective-permute-start.33
  112.6 3.9 %collective-permute-done.32.refs_6_ = bf16[2,256,128]{2,1,0:T(8,128)(2,1)S(1)} collective-permute-done((bf16[2,256,128]{2,1,0:T(8,128)(2,1)S(1)}, bf16[2,256,128]{2,1,0:T(8,128)(2,1)S(1)}, u32[]{:S(2)}, u32[]{:S(2)}) %collective-permute-start.32) | collective-permute-done | bytes 131104 | tf_op jit(solution)/shard_map/ppermute | solution.py:296
  116.5 1.9 %collective-permute-done.33.refs_7_ = bf16[2,256,128]{2,1,0:T(8,128)(2,1)S(1)} collective-permute-done((bf16[2,256,128]{2,1,0:T(8,128)(2,1)S(1)}, bf16[2,256,128]{2,1,0:T(8,128)(2,1)S(1)}, u32[]{:S(2)}, u32[]{:S(2)}) %collective-permute-start.33) | collective-permute-done | bytes 131104 | tf_op jit(solution)/shard_map/ppermute | solution.py:296
  118.4 1.6 %join.1 = (bf16[256,1024]{1,0:T(8,128)(2,1)}, bf16[256,1024]{1,0:T(8,128)(2,1)}) custom-call(s32[2]{0:T(128)S(1)} %copy-done.1, bf16[2,256,128]{2,1,0:T(8,128)(2,1)S(1)} %get-tuple-element.90.refs_0_, bf16[2,256,128]{2,1,0:T(8,128)(2,1)S(1)} %collective-permute-done.21.refs_1_, bf16[2,256,128]{2,1,0:T(8,128)(2,1)S(1)} %collective-permute-done.22.refs_2_, ...), custom_call_target="tpu_custom_call" | custom-call | tf_op jit(solution)/shard_map/join/pallas_call | solution.py:237
  (48 shorter events, 5.1 us)
Async XLA Ops:
  4.3 3.2 %collective-permute-start = (bf16[2,2,256,128]{3,2,1,0:T(8,128)(2,1)}, bf16[2,2,256,128]{3,2,1,0:T(8,128)(2,1)S(1)}, u32[]{:S(2)}, u32[]{:S(2)}) collective-permute-start(bf16[2,2,256,128]{3,2,1,0:T(8,128)(2,1)} %get-tuple-element.56), channel_id=1, source_target_pairs={{0,8},{8,0},{16,24},{24,16},{1,9},{9,1},{17,25},{25,17},{2,10},{10... | collective-permute-start | bytes 786440 | tf_op jit(solution)/shard_map/ppermute | solution.py:292
  4.8 10.7 %collective-permute-start.1 = (bf16[2,2,256,128]{3,2,1,0:T(8,128)(2,1)}, bf16[2,2,256,128]{3,2,1,0:T(8,128)(2,1)S(1)}, u32[]{:S(2)}, u32[]{:S(2)}) collective-permute-start(bf16[2,2,256,128]{3,2,1,0:T(8,128)(2,1)} %get-tuple-element.59), channel_id=1, source_target_pairs={{0,16},{8,24},{16,0},{24,8},{1,17},{9,25},{17,1},{25,9},{2,18},{10... | collective-permute-start | bytes 786440 | tf_op jit(solution)/shard_map/ppermute | solution.py:292
  7.3 12.5 %collective-permute-start.2 = (bf16[2,2,256,128]{3,2,1,0:T(8,128)(2,1)}, bf16[2,2,256,128]{3,2,1,0:T(8,128)(2,1)S(1)}, u32[]{:S(2)}, u32[]{:S(2)}) collective-permute-start(bf16[2,2,256,128]{3,2,1,0:T(8,128)(2,1)} %get-tuple-element.60), channel_id=1, source_target_pairs={{0,24},{8,16},{16,8},{24,0},{1,25},{9,17},{17,9},{25,1},{2,26},{10... | collective-permute-start | bytes 786440 | tf_op jit(solution)/shard_map/ppermute | solution.py:292
  9.4 12.5 %all-to-all-start = ((s32[8,1,128]{2,1,0:T(1,128)}), s32[8,1,128]{2,1,0:T(1,128)S(1)}, u32[]{:S(2)}, u32[]{:S(2)}) async-start(s32[8,1,128]{2,1,0:T(1,128)} %bitcast.3), calls=%async_computation | async-start | bytes 8192 | tf_op jit(solution)/shard_map/all_to_all | solution.py:341
  21.8 1.0 copy-start
  22.8 0.6 copy-start.1
  24.1 6.8 %collective-permute-start.3 = (bf16[2,3,64,128]{3,2,1,0:T(8,128)(2,1)S(1)}, bf16[2,3,64,128]{3,2,1,0:T(8,128)(2,1)S(1)}, u32[]{:S(2)}, u32[]{:S(2)}) collective-permute-start(bf16[2,3,64,128]{3,2,1,0:T(8,128)(2,1)S(1)} %get-tuple-element.61), channel_id=1, source_target_pairs={{0,1},{1,0},{2,3},{3,2},{4,5},{5,4},{6,7},{7,6},{8,9},{9,8},{10,11... | collective-permute-start | bytes 294920 | tf_op jit(solution)/shard_map/ppermute | solution.py:292
  24.7 8.5 %collective-permute-start.4 = (bf16[2,3,64,128]{3,2,1,0:T(8,128)(2,1)S(1)}, bf16[2,3,64,128]{3,2,1,0:T(8,128)(2,1)S(1)}, u32[]{:S(2)}, u32[]{:S(2)}) collective-permute-start(bf16[2,3,64,128]{3,2,1,0:T(8,128)(2,1)S(1)} %get-tuple-element.62), channel_id=1, source_target_pairs={{0,2},{1,3},{2,0},{3,1},{4,6},{5,7},{6,4},{7,5},{8,10},{9,11},{10,... | collective-permute-start | bytes 294920 | tf_op jit(solution)/shard_map/ppermute | solution.py:292
  25.5 14.5 %collective-permute-start.5 = (bf16[2,3,64,128]{3,2,1,0:T(8,128)(2,1)S(1)}, bf16[2,3,64,128]{3,2,1,0:T(8,128)(2,1)S(1)}, u32[]{:S(2)}, u32[]{:S(2)}) collective-permute-start(bf16[2,3,64,128]{3,2,1,0:T(8,128)(2,1)S(1)} %get-tuple-element.63), channel_id=1, source_target_pairs={{0,4},{1,5},{2,6},{3,7},{4,0},{5,1},{6,2},{7,3},{8,12},{9,13},{10,... | collective-permute-start | bytes 294920 | tf_op jit(solution)/shard_map/ppermute | solution.py:292
  28.1 14.1 %collective-permute-start.6 = (bf16[2,3,64,128]{3,2,1,0:T(8,128)(2,1)S(1)}, bf16[2,3,64,128]{3,2,1,0:T(8,128)(2,1)S(1)}, u32[]{:S(2)}, u32[]{:S(2)}) collective-permute-start(bf16[2,3,64,128]{3,2,1,0:T(8,128)(2,1)S(1)} %get-tuple-element.64), channel_id=1, source_target_pairs={{0,5},{1,4},{2,7},{3,6},{4,1},{5,0},{6,3},{7,2},{8,13},{9,12},{10,... | collective-permute-start | bytes 294920 | tf_op jit(solution)/shard_map/ppermute | solution.py:292
  29.3 12.9 %collective-permute-start.7 = (bf16[2,3,64,128]{3,2,1,0:T(8,128)(2,1)S(1)}, bf16[2,3,64,128]{3,2,1,0:T(8,128)(2,1)S(1)}, u32[]{:S(2)}, u32[]{:S(2)}) collective-permute-start(bf16[2,3,64,128]{3,2,1,0:T(8,128)(2,1)S(1)} %get-tuple-element.65), channel_id=1, source_target_pairs={{0,6},{1,7},{2,4},{3,5},{4,2},{5,3},{6,0},{7,1},{8,14},{9,15},{10,... | collective-permute-start | bytes 294920 | tf_op jit(solution)/shard_map/ppermute | solution.py:292
  30.9 11.3 %collective-permute-start.8 = (bf16[2,3,64,128]{3,2,1,0:T(8,128)(2,1)S(1)}, bf16[2,3,64,128]{3,2,1,0:T(8,128)(2,1)S(1)}, u32[]{:S(2)}, u32[]{:S(2)}) collective-permute-start(bf16[2,3,64,128]{3,2,1,0:T(8,128)(2,1)S(1)} %get-tuple-element.66), channel_id=1, source_target_pairs={{0,7},{1,6},{2,5},{3,4},{4,3},{5,2},{6,1},{7,0},{8,15},{9,14},{10,... | collective-permute-start | bytes 294920 | tf_op jit(solution)/shard_map/ppermute | solution.py:292
  33.2 10.3 %collective-permute-start.9 = (bf16[2,3,64,128]{3,2,1,0:T(8,128)(2,1)S(1)}, bf16[2,3,64,128]{3,2,1,0:T(8,128)(2,1)S(1)}, u32[]{:S(2)}, u32[]{:S(2)}) collective-permute-start(bf16[2,3,64,128]{3,2,1,0:T(8,128)(2,1)S(1)} %get-tuple-element.67), channel_id=1, source_target_pairs={{0,3},{1,2},{2,1},{3,0},{4,7},{5,6},{6,5},{7,4},{8,11},{9,10},{10,... | collective-permute-start | bytes 294920 | tf_op jit(solution)/shard_map/ppermute | solution.py:292
  43.5 22.1 %collective-permute-start.12 = (bf16[2,3,64,128]{3,2,1,0:T(8,128)(2,1)S(1)}, bf16[2,3,64,128]{3,2,1,0:T(8,128)(2,1)S(1)}, u32[]{:S(2)}, u32[]{:S(2)}) collective-permute-start(bf16[2,3,64,128]{3,2,1,0:T(8,128)(2,1)S(1)} %get-tuple-element.71), channel_id=1, source_target_pairs={{0,4},{1,5},{2,6},{3,7},{4,0},{5,1},{6,2},{7,3},{8,12},{9,13},{10,... | collective-permute-start | bytes 294920 | tf_op jit(solution)/shard_map/ppermute | solution.py:292
  47.2 18.4 %collective-permute-start.13 = (bf16[2,3,64,128]{3,2,1,0:T(8,128)(2,1)S(1)}, bf16[2,3,64,128]{3,2,1,0:T(8,128)(2,1)S(1)}, u32[]{:S(2)}, u32[]{:S(2)}) collective-permute-start(bf16[2,3,64,128]{3,2,1,0:T(8,128)(2,1)S(1)} %get-tuple-element.73), channel_id=1, source_target_pairs={{0,5},{1,4},{2,7},{3,6},{4,1},{5,0},{6,3},{7,2},{8,13},{9,12},{10,... | collective-permute-start | bytes 294920 | tf_op jit(solution)/shard_map/ppermute | solution.py:292
  48.2 19.5 %collective-permute-start.14 = (bf16[2,3,64,128]{3,2,1,0:T(8,128)(2,1)S(1)}, bf16[2,3,64,128]{3,2,1,0:T(8,128)(2,1)S(1)}, u32[]{:S(2)}, u32[]{:S(2)}) collective-permute-start(bf16[2,3,64,128]{3,2,1,0:T(8,128)(2,1)S(1)} %get-tuple-element.75), channel_id=1, source_target_pairs={{0,6},{1,7},{2,4},{3,5},{4,2},{5,3},{6,0},{7,1},{8,14},{9,15},{10,... | collective-permute-start | bytes 294920 | tf_op jit(solution)/shard_map/ppermute | solution.py:292
  49.5 19.2 %collective-permute-start.15 = (bf16[2,3,64,128]{3,2,1,0:T(8,128)(2,1)S(1)}, bf16[2,3,64,128]{3,2,1,0:T(8,128)(2,1)S(1)}, u32[]{:S(2)}, u32[]{:S(2)}) collective-permute-start(bf16[2,3,64,128]{3,2,1,0:T(8,128)(2,1)S(1)} %get-tuple-element.77), channel_id=1, source_target_pairs={{0,7},{1,6},{2,5},{3,4},{4,3},{5,2},{6,1},{7,0},{8,15},{9,14},{10,... | collective-permute-start | bytes 294920 | tf_op jit(solution)/shard_map/ppermute | solution.py:292
  64.1 7.3 %collective-permute-start.10 = (bf16[2,3,64,128]{3,2,1,0:T(8,128)(2,1)S(1)}, bf16[2,3,64,128]{3,2,1,0:T(8,128)(2,1)S(1)}, u32[]{:S(2)}, u32[]{:S(2)}) collective-permute-start(bf16[2,3,64,128]{3,2,1,0:T(8,128)(2,1)S(1)} %get-tuple-element.68), channel_id=1, source_target_pairs={{0,1},{1,0},{2,3},{3,2},{4,5},{5,4},{6,7},{7,6},{8,9},{9,8},{10,11... | collective-permute-start | bytes 294920 | tf_op jit(solution)/shard_map/ppermute | solution.py:292
  65.6 7.2 %collective-permute-start.11 = (bf16[2,3,64,128]{3,2,1,0:T(8,128)(2,1)S(1)}, bf16[2,3,64,128]{3,2,1,0:T(8,128)(2,1)S(1)}, u32[]{:S(2)}, u32[]{:S(2)}) collective-permute-start(bf16[2,3,64,128]{3,2,1,0:T(8,128)(2,1)S(1)} %get-tuple-element.69), channel_id=1, source_target_pairs={{0,2},{1,3},{2,0},{3,1},{4,6},{5,7},{6,4},{7,5},{8,10},{9,11},{10,... | collective-permute-start | bytes 294920 | tf_op jit(solution)/shard_map/ppermute | solution.py:292
  65.7 9.6 %collective-permute-start.16 = (bf16[2,3,64,128]{3,2,1,0:T(8,128)(2,1)S(1)}, bf16[2,3,64,128]{3,2,1,0:T(8,128)(2,1)S(1)}, u32[]{:S(2)}, u32[]{:S(2)}) collective-permute-start(bf16[2,3,64,128]{3,2,1,0:T(8,128)(2,1)S(1)} %get-tuple-element.78), channel_id=1, source_target_pairs={{0,3},{1,2},{2,1},{3,0},{4,7},{5,6},{6,5},{7,4},{8,11},{9,10},{10,... | collective-permute-start | bytes 294920 | tf_op jit(solution)/shard_map/ppermute | solution.py:292
  67.6 19.8 %collective-permute-start.17 = (bf16[2,3,64,128]{3,2,1,0:T(8,128)(2,1)S(1)}, bf16[2,3,64,128]{3,2,1,0:T(8,128)(2,1)S(1)}, u32[]{:S(2)}, u32[]{:S(2)}) collective-permute-start(bf16[2,3,64,128]{3,2,1,0:T(8,128)(2,1)S(1)} %get-tuple-element.86), channel_id=1, source_target_pairs={{0,4},{1,5},{2,6},{3,7},{4,0},{5,1},{6,2},{7,3},{8,12},{9,13},{10,... | collective-permute-start | bytes 294920 | tf_op jit(solution)/shard_map/ppermute | solution.py:292
  68.7 18.7 %collective-permute-start.18 = (bf16[2,3,64,128]{3,2,1,0:T(8,128)(2,1)S(1)}, bf16[2,3,64,128]{3,2,1,0:T(8,128)(2,1)S(1)}, u32[]{:S(2)}, u32[]{:S(2)}) collective-permute-start(bf16[2,3,64,128]{3,2,1,0:T(8,128)(2,1)S(1)} %get-tuple-element.87), channel_id=1, source_target_pairs={{0,5},{1,4},{2,7},{3,6},{4,1},{5,0},{6,3},{7,2},{8,13},{9,12},{10,... | collective-permute-start | bytes 294920 | tf_op jit(solution)/shard_map/ppermute | solution.py:292
  71.4 15.9 %collective-permute-start.19 = (bf16[2,3,64,128]{3,2,1,0:T(8,128)(2,1)S(1)}, bf16[2,3,64,128]{3,2,1,0:T(8,128)(2,1)S(1)}, u32[]{:S(2)}, u32[]{:S(2)}) collective-permute-start(bf16[2,3,64,128]{3,2,1,0:T(8,128)(2,1)S(1)} %get-tuple-element.88), channel_id=1, source_target_pairs={{0,6},{1,7},{2,4},{3,5},{4,2},{5,3},{6,0},{7,1},{8,14},{9,15},{10,... | collective-permute-start | bytes 294920 | tf_op jit(solution)/shard_map/ppermute | solution.py:292
  72.8 14.6 %collective-permute-start.20 = (bf16[2,3,64,128]{3,2,1,0:T(8,128)(2,1)S(1)}, bf16[2,3,64,128]{3,2,1,0:T(8,128)(2,1)S(1)}, u32[]{:S(2)}, u32[]{:S(2)}) collective-permute-start(bf16[2,3,64,128]{3,2,1,0:T(8,128)(2,1)S(1)} %get-tuple-element.89), channel_id=1, source_target_pairs={{0,7},{1,6},{2,5},{3,4},{4,3},{5,2},{6,1},{7,0},{8,15},{9,14},{10,... | collective-permute-start | bytes 294920 | tf_op jit(solution)/shard_map/ppermute | solution.py:292
  88.3 10.1 %collective-permute-start.23 = (bf16[2,256,128]{2,1,0:T(8,128)(2,1)S(1)}, bf16[2,256,128]{2,1,0:T(8,128)(2,1)S(1)}, u32[]{:S(2)}, u32[]{:S(2)}) collective-permute-start(bf16[2,256,128]{2,1,0:T(8,128)(2,1)S(1)} %get-tuple-element.93), channel_id=1, source_target_pairs={{0,24},{8,16},{16,8},{24,0},{1,25},{9,17},{17,9},{25,1},{2,26},{10... | collective-permute-start | bytes 393224 | tf_op jit(solution)/shard_map/ppermute | solution.py:296
  88.4 5.3 %collective-permute-start.24 = (bf16[2,3,64,128]{3,2,1,0:T(8,128)(2,1)S(1)}, bf16[2,3,64,128]{3,2,1,0:T(8,128)(2,1)S(1)}, u32[]{:S(2)}, u32[]{:S(2)}) collective-permute-start(bf16[2,3,64,128]{3,2,1,0:T(8,128)(2,1)S(1)} %get-tuple-element.95), channel_id=1, source_target_pairs={{0,1},{1,0},{2,3},{3,2},{4,5},{5,4},{6,7},{7,6},{8,9},{9,8},{10,11... | collective-permute-start | bytes 294920 | tf_op jit(solution)/shard_map/ppermute | solution.py:292
  89.9 6.9 %collective-permute-start.25 = (bf16[2,3,64,128]{3,2,1,0:T(8,128)(2,1)S(1)}, bf16[2,3,64,128]{3,2,1,0:T(8,128)(2,1)S(1)}, u32[]{:S(2)}, u32[]{:S(2)}) collective-permute-start(bf16[2,3,64,128]{3,2,1,0:T(8,128)(2,1)S(1)} %get-tuple-element.96), channel_id=1, source_target_pairs={{0,2},{1,3},{2,0},{3,1},{4,6},{5,7},{6,4},{7,5},{8,10},{9,11},{10,... | collective-permute-start | bytes 294920 | tf_op jit(solution)/shard_map/ppermute | solution.py:292
  89.9 14.9 %collective-permute-start.26 = (bf16[2,3,64,128]{3,2,1,0:T(8,128)(2,1)S(1)}, bf16[2,3,64,128]{3,2,1,0:T(8,128)(2,1)S(1)}, u32[]{:S(2)}, u32[]{:S(2)}) collective-permute-start(bf16[2,3,64,128]{3,2,1,0:T(8,128)(2,1)S(1)} %get-tuple-element.97), channel_id=1, source_target_pairs={{0,4},{1,5},{2,6},{3,7},{4,0},{5,1},{6,2},{7,3},{8,12},{9,13},{10,... | collective-permute-start | bytes 294920 | tf_op jit(solution)/shard_map/ppermute | solution.py:292
  91.7 15.2 %collective-permute-start.27 = (bf16[2,3,64,128]{3,2,1,0:T(8,128)(2,1)S(1)}, bf16[2,3,64,128]{3,2,1,0:T(8,128)(2,1)S(1)}, u32[]{:S(2)}, u32[]{:S(2)}) collective-permute-start(bf16[2,3,64,128]{3,2,1,0:T(8,128)(2,1)S(1)} %get-tuple-element.98), channel_id=1, source_target_pairs={{0,5},{1,4},{2,7},{3,6},{4,1},{5,0},{6,3},{7,2},{8,13},{9,12},{10,... | collective-permute-start | bytes 294920 | tf_op jit(solution)/shard_map/ppermute | solution.py:292
  93.7 14.9 %collective-permute-start.28 = (bf16[2,3,64,128]{3,2,1,0:T(8,128)(2,1)S(1)}, bf16[2,3,64,128]{3,2,1,0:T(8,128)(2,1)S(1)}, u32[]{:S(2)}, u32[]{:S(2)}) collective-permute-start(bf16[2,3,64,128]{3,2,1,0:T(8,128)(2,1)S(1)} %get-tuple-element.99), channel_id=1, source_target_pairs={{0,6},{1,7},{2,4},{3,5},{4,2},{5,3},{6,0},{7,1},{8,14},{9,15},{10,... | collective-permute-start | bytes 294920 | tf_op jit(solution)/shard_map/ppermute | solution.py:292
  96.8 11.7 %collective-permute-start.29 = (bf16[2,3,64,128]{3,2,1,0:T(8,128)(2,1)S(1)}, bf16[2,3,64,128]{3,2,1,0:T(8,128)(2,1)S(1)}, u32[]{:S(2)}, u32[]{:S(2)}) collective-permute-start(bf16[2,3,64,128]{3,2,1,0:T(8,128)(2,1)S(1)} %get-tuple-element.100), channel_id=1, source_target_pairs={{0,7},{1,6},{2,5},{3,4},{4,3},{5,2},{6,1},{7,0},{8,15},{9,14},{10,... | collective-permute-start | bytes 294920 | tf_op jit(solution)/shard_map/ppermute | solution.py:292
  98.4 10.8 %collective-permute-start.30 = (bf16[2,3,64,128]{3,2,1,0:T(8,128)(2,1)S(1)}, bf16[2,3,64,128]{3,2,1,0:T(8,128)(2,1)S(1)}, u32[]{:S(2)}, u32[]{:S(2)}) collective-permute-start(bf16[2,3,64,128]{3,2,1,0:T(8,128)(2,1)S(1)} %get-tuple-element.101), channel_id=1, source_target_pairs={{0,3},{1,2},{2,1},{3,0},{4,7},{5,6},{6,5},{7,4},{8,11},{9,10},{10,... | collective-permute-start | bytes 294920 | tf_op jit(solution)/shard_map/ppermute | solution.py:292
  104.8 7.3 %collective-permute-start.21 = (bf16[2,256,128]{2,1,0:T(8,128)(2,1)S(1)}, bf16[2,256,128]{2,1,0:T(8,128)(2,1)S(1)}, u32[]{:S(2)}, u32[]{:S(2)}) collective-permute-start(bf16[2,256,128]{2,1,0:T(8,128)(2,1)S(1)} %get-tuple-element.91), channel_id=1, source_target_pairs={{0,8},{8,0},{16,24},{24,16},{1,9},{9,1},{17,25},{25,17},{2,10},{10... | collective-permute-start | bytes 393224 | tf_op jit(solution)/shard_map/ppermute | solution.py:296
  106.9 5.7 %collective-permute-start.22 = (bf16[2,256,128]{2,1,0:T(8,128)(2,1)S(1)}, bf16[2,256,128]{2,1,0:T(8,128)(2,1)S(1)}, u32[]{:S(2)}, u32[]{:S(2)}) collective-permute-start(bf16[2,256,128]{2,1,0:T(8,128)(2,1)S(1)} %get-tuple-element.92), channel_id=1, source_target_pairs={{0,16},{8,24},{16,0},{24,8},{1,17},{9,25},{17,1},{25,9},{2,18},{10... | collective-permute-start | bytes 393224 | tf_op jit(solution)/shard_map/ppermute | solution.py:296
  110.1 2.5 %collective-permute-start.31 = (bf16[2,256,128]{2,1,0:T(8,128)(2,1)S(1)}, bf16[2,256,128]{2,1,0:T(8,128)(2,1)S(1)}, u32[]{:S(2)}, u32[]{:S(2)}) collective-permute-start(bf16[2,256,128]{2,1,0:T(8,128)(2,1)S(1)} %get-tuple-element.103), channel_id=1, source_target_pairs={{0,8},{8,0},{16,24},{24,16},{1,9},{9,1},{17,25},{25,17},{2,10},{10... | collective-permute-start | bytes 393224 | tf_op jit(solution)/shard_map/ppermute | solution.py:296
  110.2 6.3 %collective-permute-start.32 = (bf16[2,256,128]{2,1,0:T(8,128)(2,1)S(1)}, bf16[2,256,128]{2,1,0:T(8,128)(2,1)S(1)}, u32[]{:S(2)}, u32[]{:S(2)}) collective-permute-start(bf16[2,256,128]{2,1,0:T(8,128)(2,1)S(1)} %get-tuple-element.104), channel_id=1, source_target_pairs={{0,16},{8,24},{16,0},{24,8},{1,17},{9,25},{17,1},{25,9},{2,18},{10... | collective-permute-start | bytes 393224 | tf_op jit(solution)/shard_map/ppermute | solution.py:296
  111.1 7.4 %collective-permute-start.33 = (bf16[2,256,128]{2,1,0:T(8,128)(2,1)S(1)}, bf16[2,256,128]{2,1,0:T(8,128)(2,1)S(1)}, u32[]{:S(2)}, u32[]{:S(2)}) collective-permute-start(bf16[2,256,128]{2,1,0:T(8,128)(2,1)S(1)} %get-tuple-element.105), channel_id=1, source_target_pairs={{0,24},{8,16},{16,8},{24,0},{1,25},{9,17},{17,9},{25,1},{2,26},{10... | collective-permute-start | bytes 393224 | tf_op jit(solution)/shard_map/ppermute | solution.py:296

commit v15 on v14

--- a/solution.py
+++ b/solution.py
@@ -160,7 +160,7 @@
             probs[b] = expo * (1.0 / jnp.sum(expo, axis=0, keepdims=True))
             probs_low[b] = probs[b].astype(jnp.bfloat16)
         for b in subs:
-            attended = dot(values[b], probs_low[b], TN).astype(jnp.bfloat16).T
+            attended = dot(probs_low[b], values[b], TN).astype(jnp.bfloat16)
             by_row(o_ref, b, attended)
             dv = dot(probs_low[b], g_out[b], NN)
             delta = jnp.sum(probs[b] * dprob[b], axis=0, keepdims=True)
@@ -168,7 +168,7 @@
             for e in range(LIST):
                 total[1, listed[b][e]] += dv[e * BLK : (e + 1) * BLK]
         for b in subs:
-            dq = (dot(keys[b], dscore[b], TN) * SCALE).astype(jnp.bfloat16).T
+            dq = (dot(dscore[b], keys[b], TN) * SCALE).astype(jnp.bfloat16)
             by_row(dq_ref, b, dq)
             dk = dot(dscore[b], q[b], NN)
             for e in range(LIST):

time: 120 us -> 122 us (1.017)
  Pallas kernels: 32.1 us -> 34 us
    pallas_call x2, Pallas kernels: 24.2 us -> 26.2 us  [attend(): pl.pallas_call(functools.partial(attend_kernel, heads=len(own), head=head...]
  transfers between devices with their start and end apart: 35 -> 35, of which waited for: 13 -> 13; matrix products, arithmetic and copies ran while one was open for 2% -> 2% of each run, Pallas kernels for 21% -> 23%
where the time goes in v15:
time: 122 us
  starting transfers between devices  50.1 us (41%)
  Pallas kernels  34 us (28%)
  waiting for transfers between devices  32.9 us (27%)
  local copies, waits for them, and re-layouts  2.48 us (2%)
  other arithmetic  1.79 us (1%)
    ppermute x28, starting transfers between devices, send(): lax.ppermute(x, axis, [(i, partner(i, r, count)) for i in range(count)])  39.8 us
    pallas_call x2, Pallas kernels, attend(): pl.pallas_call(functools.partial(attend_kernel, heads=len(own), head=head...  26.2 us
    ppermute x28, waiting for transfers between devices, send(): lax.ppermute(x, axis, [(i, partner(i, r, count)) for i in range(count)])  24.4 us
    pallas_call x6, Pallas kernels, call(): pl.pallas_call(kernel, grid_spec=pltpu.PrefetchScalarGridSpec(num_scalar_...  7.83 us
    ppermute x6, waiting for transfers between devices, send_back(): lax.ppermute(x, axis, [(i, origin(i, r, count)) for i in range(count)])  6.4 us
    all_to_all x1, starting transfers between devices, per_device(): lax.all_to_all(requests, 'ctx', split_axis=0, concat_axis=0, tiled=True)  6.07 us
    ppermute x6, starting transfers between devices, send_back(): lax.ppermute(x, axis, [(i, origin(i, r, count)) for i in range(count)])  4.29 us
  transfers between devices with their start and end apart: 35, of which 13 were waited for; matrix products, arithmetic and copies ran while one was open for 2% of the time, Pallas kernels for 23%

profile of v15, /device:TPU:0, one launch (start us, length us, event | category | flops | bytes accessed | tf_op | source)
XLA Modules:
  0.0 122.0 jit_solution(2447854853842464547)
XLA Ops:
  1.2 3.0 %split.1 = (bf16[2,2,256,128]{3,2,1,0:T(8,128)(2,1)}, bf16[2,2,256,128]{3,2,1,0:T(8,128)(2,1)}, bf16[2,2,256,128]{3,2,1,0:T(8,128)(2,1)}, bf16[2,2,256,128]{3,2,1,0:T(8,128)(2,1)}) custom-call(s32[2]{0:T(128)} %pad_add_fusion.place, bf16[256,1024]{1,0:T(8,128)(2,1)} %k_ref.1, bf16[256,1024]{1,0:T(8,128)(2,1)} %v_ref.1), custom_call_target="tpu_custom_call" | custom-call | tf_op jit(solution)/shard_map/split/pallas_call | solution.py:237
  4.8 2.6 %collective-permute-start.1 = (bf16[2,2,256,128]{3,2,1,0:T(8,128)(2,1)}, bf16[2,2,256,128]{3,2,1,0:T(8,128)(2,1)S(1)}, u32[]{:S(2)}, u32[]{:S(2)}) collective-permute-start(bf16[2,2,256,128]{3,2,1,0:T(8,128)(2,1)} %get-tuple-element.59), channel_id=1, source_target_pairs={{0,16},{8,24},{16,0},{24,8},{1,17},{9,25},{17,1},{25,9},{2,18},{10... | collective-permute-start | bytes 786440 | tf_op jit(solution)/shard_map/ppermute | solution.py:292
  7.4 0.8 copy.14
  8.7 0.7 select_reduce_fusion
  9.4 6.1 %all-to-all-start = ((s32[8,1,128]{2,1,0:T(1,128)}), s32[8,1,128]{2,1,0:T(1,128)S(1)}, u32[]{:S(2)}, u32[]{:S(2)}) async-start(s32[8,1,128]{2,1,0:T(1,128)} %bitcast.3), calls=%async_computation | async-start | bytes 8192 | tf_op jit(solution)/shard_map/all_to_all | solution.py:341
  15.5 4.3 %collective-permute-done.2.refs_3_ = bf16[2,2,256,128]{3,2,1,0:T(8,128)(2,1)S(1)} collective-permute-done((bf16[2,2,256,128]{3,2,1,0:T(8,128)(2,1)}, bf16[2,2,256,128]{3,2,1,0:T(8,128)(2,1)S(1)}, u32[]{:S(2)}, u32[]{:S(2)}) %collective-permute-start.2) | collective-permute-done | bytes 262176 | tf_op jit(solution)/shard_map/ppermute | solution.py:292
  19.8 2.0 %all-to-all-done = s32[8,1,128]{2,1,0:T(1,128)S(1)} async-done(((s32[8,1,128]{2,1,0:T(1,128)}), s32[8,1,128]{2,1,0:T(1,128)S(1)}, u32[]{:S(2)}, u32[]{:S(2)}) %all-to-all-start) | async-done | bytes 4128 | tf_op jit(solution)/shard_map/all_to_all | solution.py:341
  21.8 0.9 copy-done
  23.4 0.7 pick.2
  24.1 0.6 collective-permute-start.3
  25.5 2.7 %collective-permute-start.5 = (bf16[2,3,64,128]{3,2,1,0:T(8,128)(2,1)S(1)}, bf16[2,3,64,128]{3,2,1,0:T(8,128)(2,1)S(1)}, u32[]{:S(2)}, u32[]{:S(2)}) collective-permute-start(bf16[2,3,64,128]{3,2,1,0:T(8,128)(2,1)S(1)} %get-tuple-element.63), channel_id=1, source_target_pairs={{0,4},{1,5},{2,6},{3,7},{4,0},{5,1},{6,2},{7,3},{8,12},{9,13},{10,... | collective-permute-start | bytes 294920 | tf_op jit(solution)/shard_map/ppermute | solution.py:292
  28.1 1.2 collective-permute-start.6
  29.3 1.6 %collective-permute-start.7 = (bf16[2,3,64,128]{3,2,1,0:T(8,128)(2,1)S(1)}, bf16[2,3,64,128]{3,2,1,0:T(8,128)(2,1)S(1)}, u32[]{:S(2)}, u32[]{:S(2)}) collective-permute-start(bf16[2,3,64,128]{3,2,1,0:T(8,128)(2,1)S(1)} %get-tuple-element.65), channel_id=1, source_target_pairs={{0,6},{1,7},{2,4},{3,5},{4,2},{5,3},{6,0},{7,1},{8,14},{9,15},{10,... | collective-permute-start | bytes 294920 | tf_op jit(solution)/shard_map/ppermute | solution.py:292
  30.9 2.3 %collective-permute-start.8 = (bf16[2,3,64,128]{3,2,1,0:T(8,128)(2,1)S(1)}, bf16[2,3,64,128]{3,2,1,0:T(8,128)(2,1)S(1)}, u32[]{:S(2)}, u32[]{:S(2)}) collective-permute-start(bf16[2,3,64,128]{3,2,1,0:T(8,128)(2,1)S(1)} %get-tuple-element.66), channel_id=1, source_target_pairs={{0,7},{1,6},{2,5},{3,4},{4,3},{5,2},{6,1},{7,0},{8,15},{9,14},{10,... | collective-permute-start | bytes 294920 | tf_op jit(solution)/shard_map/ppermute | solution.py:292
  33.7 0.7 pick.3
  34.4 5.6 %collective-permute-done.5.refs_6_ = bf16[2,3,64,128]{3,2,1,0:T(8,128)(2,1)S(1)} collective-permute-done((bf16[2,3,64,128]{3,2,1,0:T(8,128)(2,1)S(1)}, bf16[2,3,64,128]{3,2,1,0:T(8,128)(2,1)S(1)}, u32[]{:S(2)}, u32[]{:S(2)}) %collective-permute-start.5) | collective-permute-done | bytes 98336 | tf_op jit(solution)/shard_map/ppermute | solution.py:292
  40.0 2.2 %collective-permute-done.6.refs_7_ = bf16[2,3,64,128]{3,2,1,0:T(8,128)(2,1)S(1)} collective-permute-done((bf16[2,3,64,128]{3,2,1,0:T(8,128)(2,1)S(1)}, bf16[2,3,64,128]{3,2,1,0:T(8,128)(2,1)S(1)}, u32[]{:S(2)}, u32[]{:S(2)}) %collective-permute-start.6) | collective-permute-done | bytes 98336 | tf_op jit(solution)/shard_map/ppermute | solution.py:292
  42.2 1.3 %collective-permute-done.9.refs_10_ = bf16[2,3,64,128]{3,2,1,0:T(8,128)(2,1)S(1)} collective-permute-done((bf16[2,3,64,128]{3,2,1,0:T(8,128)(2,1)S(1)}, bf16[2,3,64,128]{3,2,1,0:T(8,128)(2,1)S(1)}, u32[]{:S(2)}, u32[]{:S(2)}) %collective-permute-start.9) | collective-permute-done | bytes 98336 | tf_op jit(solution)/shard_map/ppermute | solution.py:292
  43.5 3.7 %collective-permute-start.12 = (bf16[2,3,64,128]{3,2,1,0:T(8,128)(2,1)S(1)}, bf16[2,3,64,128]{3,2,1,0:T(8,128)(2,1)S(1)}, u32[]{:S(2)}, u32[]{:S(2)}) collective-permute-start(bf16[2,3,64,128]{3,2,1,0:T(8,128)(2,1)S(1)} %get-tuple-element.71), channel_id=1, source_target_pairs={{0,4},{1,5},{2,6},{3,7},{4,0},{5,1},{6,2},{7,3},{8,12},{9,13},{10,... | collective-permute-start | bytes 294920 | tf_op jit(solution)/shard_map/ppermute | solution.py:292
  47.2 0.9 collective-permute-start.13
  48.2 1.3 %collective-permute-start.14 = (bf16[2,3,64,128]{3,2,1,0:T(8,128)(2,1)S(1)}, bf16[2,3,64,128]{3,2,1,0:T(8,128)(2,1)S(1)}, u32[]{:S(2)}, u32[]{:S(2)}) collective-permute-start(bf16[2,3,64,128]{3,2,1,0:T(8,128)(2,1)S(1)} %get-tuple-element.75), channel_id=1, source_target_pairs={{0,6},{1,7},{2,4},{3,5},{4,2},{5,3},{6,0},{7,1},{8,14},{9,15},{10,... | collective-permute-start | bytes 294920 | tf_op jit(solution)/shard_map/ppermute | solution.py:292
  49.5 2.5 %collective-permute-start.15 = (bf16[2,3,64,128]{3,2,1,0:T(8,128)(2,1)S(1)}, bf16[2,3,64,128]{3,2,1,0:T(8,128)(2,1)S(1)}, u32[]{:S(2)}, u32[]{:S(2)}) collective-permute-start(bf16[2,3,64,128]{3,2,1,0:T(8,128)(2,1)S(1)} %get-tuple-element.77), channel_id=1, source_target_pairs={{0,7},{1,6},{2,5},{3,4},{4,3},{5,2},{6,1},{7,0},{8,15},{9,14},{10,... | collective-permute-start | bytes 294920 | tf_op jit(solution)/shard_map/ppermute | solution.py:292
  52.0 13.1 %attend.2 = (bf16[1024,1024]{1,0:T(8,128)(2,1)}, bf16[1024,1024]{1,0:T(8,128)(2,1)}, bf16[2,16,64,128]{3,2,1,0:T(8,128)(2,1)S(1)}, bf16[2,3,64,128]{3,2,1,0:T(8,...) custom-call(s32[2]{0:T(128)S(1)} %copy-done.1, ...), custom_call_target="tpu_custom_call" | custom-call | flops 3221225472 | bytes 20971520 | tf_op jit(solution)/shard_map/attend/pallas_call | solution.py:261
  65.1 1.5 %collective-permute-start.10 = (bf16[2,3,64,128]{3,2,1,0:T(8,128)(2,1)S(1)}, bf16[2,3,64,128]{3,2,1,0:T(8,128)(2,1)S(1)}, u32[]{:S(2)}, u32[]{:S(2)}) collective-permute-start(bf16[2,3,64,128]{3,2,1,0:T(8,128)(2,1)S(1)} %get-tuple-element.68), channel_id=1, source_target_pairs={{0,1},{1,0},{2,3},{3,2},{4,5},{5,4},{6,7},{7,6},{8,9},{9,8},{10,11... | collective-permute-start | bytes 294920 | tf_op jit(solution)/shard_map/ppermute | solution.py:292
  66.6 1.9 %collective-permute-start.16 = (bf16[2,3,64,128]{3,2,1,0:T(8,128)(2,1)S(1)}, bf16[2,3,64,128]{3,2,1,0:T(8,128)(2,1)S(1)}, u32[]{:S(2)}, u32[]{:S(2)}) collective-permute-start(bf16[2,3,64,128]{3,2,1,0:T(8,128)(2,1)S(1)} %get-tuple-element.78), channel_id=1, source_target_pairs={{0,3},{1,2},{2,1},{3,0},{4,7},{5,6},{6,5},{7,4},{8,11},{9,10},{10,... | collective-permute-start | bytes 294920 | tf_op jit(solution)/shard_map/ppermute | solution.py:292
  68.6 1.1 collective-permute-start.17
  69.7 2.7 %collective-permute-start.18 = (bf16[2,3,64,128]{3,2,1,0:T(8,128)(2,1)S(1)}, bf16[2,3,64,128]{3,2,1,0:T(8,128)(2,1)S(1)}, u32[]{:S(2)}, u32[]{:S(2)}) collective-permute-start(bf16[2,3,64,128]{3,2,1,0:T(8,128)(2,1)S(1)} %get-tuple-element.87), channel_id=1, source_target_pairs={{0,5},{1,4},{2,7},{3,6},{4,1},{5,0},{6,3},{7,2},{8,13},{9,12},{10,... | collective-permute-start | bytes 294920 | tf_op jit(solution)/shard_map/ppermute | solution.py:292
  72.4 1.3 %collective-permute-start.19 = (bf16[2,3,64,128]{3,2,1,0:T(8,128)(2,1)S(1)}, bf16[2,3,64,128]{3,2,1,0:T(8,128)(2,1)S(1)}, u32[]{:S(2)}, u32[]{:S(2)}) collective-permute-start(bf16[2,3,64,128]{3,2,1,0:T(8,128)(2,1)S(1)} %get-tuple-element.88), channel_id=1, source_target_pairs={{0,6},{1,7},{2,4},{3,5},{4,2},{5,3},{6,0},{7,1},{8,14},{9,15},{10,... | collective-permute-start | bytes 294920 | tf_op jit(solution)/shard_map/ppermute | solution.py:292
  73.7 2.5 %collective-permute-start.20 = (bf16[2,3,64,128]{3,2,1,0:T(8,128)(2,1)S(1)}, bf16[2,3,64,128]{3,2,1,0:T(8,128)(2,1)S(1)}, u32[]{:S(2)}, u32[]{:S(2)}) collective-permute-start(bf16[2,3,64,128]{3,2,1,0:T(8,128)(2,1)S(1)} %get-tuple-element.89), channel_id=1, source_target_pairs={{0,7},{1,6},{2,5},{3,4},{4,3},{5,2},{6,1},{7,0},{8,15},{9,14},{10,... | collective-permute-start | bytes 294920 | tf_op jit(solution)/shard_map/ppermute | solution.py:292
  76.2 13.1 %attend.3 = (bf16[1024,1024]{1,0:T(8,128)(2,1)}, bf16[1024,1024]{1,0:T(8,128)(2,1)}, bf16[2,16,64,128]{3,2,1,0:T(8,128)(2,1)S(1)}, bf16[2,3,64,128]{3,2,1,0:T(8,...) custom-call(s32[2]{0:T(128)S(1)} %copy-done.1, ...), custom_call_target="tpu_custom_call", output_to_operand_aliasing={{0}: (16, {}), {1}: (17, {})} | custom-call | flops 3221225472 | bytes 20971520 | tf_op jit(solution)/shard_map/attend/pallas_call | solution.py:261
  89.4 0.9 gather_sum.2
  90.4 1.5 %collective-permute-start.24 = (bf16[2,3,64,128]{3,2,1,0:T(8,128)(2,1)S(1)}, bf16[2,3,64,128]{3,2,1,0:T(8,128)(2,1)S(1)}, u32[]{:S(2)}, u32[]{:S(2)}) collective-permute-start(bf16[2,3,64,128]{3,2,1,0:T(8,128)(2,1)S(1)} %get-tuple-element.95), channel_id=1, source_target_pairs={{0,1},{1,0},{2,3},{3,2},{4,5},{5,4},{6,7},{7,6},{8,9},{9,8},{10,11... | collective-permute-start | bytes 294920 | tf_op jit(solution)/shard_map/ppermute | solution.py:292
  91.9 1.8 %collective-permute-start.26 = (bf16[2,3,64,128]{3,2,1,0:T(8,128)(2,1)S(1)}, bf16[2,3,64,128]{3,2,1,0:T(8,128)(2,1)S(1)}, u32[]{:S(2)}, u32[]{:S(2)}) collective-permute-start(bf16[2,3,64,128]{3,2,1,0:T(8,128)(2,1)S(1)} %get-tuple-element.97), channel_id=1, source_target_pairs={{0,4},{1,5},{2,6},{3,7},{4,0},{5,1},{6,2},{7,3},{8,12},{9,13},{10,... | collective-permute-start | bytes 294920 | tf_op jit(solution)/shard_map/ppermute | solution.py:292
  93.6 1.2 collective-permute-start.27
  94.8 0.8 collective-permute-done.24.refs_0_
  95.6 1.5 %collective-permute-start.28 = (bf16[2,3,64,128]{3,2,1,0:T(8,128)(2,1)S(1)}, bf16[2,3,64,128]{3,2,1,0:T(8,128)(2,1)S(1)}, u32[]{:S(2)}, u32[]{:S(2)}) collective-permute-start(bf16[2,3,64,128]{3,2,1,0:T(8,128)(2,1)S(1)} %get-tuple-element.99), channel_id=1, source_target_pairs={{0,6},{1,7},{2,4},{3,5},{4,2},{5,3},{6,0},{7,1},{8,14},{9,15},{10,... | collective-permute-start | bytes 294920 | tf_op jit(solution)/shard_map/ppermute | solution.py:292
  97.1 1.7 %collective-permute-done.25.refs_1_ = bf16[2,3,64,128]{3,2,1,0:T(8,128)(2,1)S(1)} collective-permute-done((bf16[2,3,64,128]{3,2,1,0:T(8,128)(2,1)S(1)}, bf16[2,3,64,128]{3,2,1,0:T(8,128)(2,1)S(1)}, u32[]{:S(2)}, u32[]{:S(2)}) %collective-permute-start.25) | collective-permute-done | bytes 98336 | tf_op jit(solution)/shard_map/ppermute | solution.py:292
  98.8 1.5 %collective-permute-start.29 = (bf16[2,3,64,128]{3,2,1,0:T(8,128)(2,1)S(1)}, bf16[2,3,64,128]{3,2,1,0:T(8,128)(2,1)S(1)}, u32[]{:S(2)}, u32[]{:S(2)}) collective-permute-start(bf16[2,3,64,128]{3,2,1,0:T(8,128)(2,1)S(1)} %get-tuple-element.100), channel_id=1, source_target_pairs={{0,7},{1,6},{2,5},{3,4},{4,3},{5,2},{6,1},{7,0},{8,15},{9,14},{10,... | collective-permute-start | bytes 294920 | tf_op jit(solution)/shard_map/ppermute | solution.py:292
  100.3 6.4 %collective-permute-done.26.refs_2_ = bf16[2,3,64,128]{3,2,1,0:T(8,128)(2,1)S(1)} collective-permute-done((bf16[2,3,64,128]{3,2,1,0:T(8,128)(2,1)S(1)}, bf16[2,3,64,128]{3,2,1,0:T(8,128)(2,1)S(1)}, u32[]{:S(2)}, u32[]{:S(2)}) %collective-permute-start.26) | collective-permute-done | bytes 98336 | tf_op jit(solution)/shard_map/ppermute | solution.py:292
  107.4 1.5 %collective-permute-done.27.refs_3_ = bf16[2,3,64,128]{3,2,1,0:T(8,128)(2,1)S(1)} collective-permute-done((bf16[2,3,64,128]{3,2,1,0:T(8,128)(2,1)S(1)}, bf16[2,3,64,128]{3,2,1,0:T(8,128)(2,1)S(1)}, u32[]{:S(2)}, u32[]{:S(2)}) %collective-permute-start.27) | collective-permute-done | bytes 98336 | tf_op jit(solution)/shard_map/ppermute | solution.py:292
  108.9 1.7 %collective-permute-start.22 = (bf16[2,256,128]{2,1,0:T(8,128)(2,1)S(1)}, bf16[2,256,128]{2,1,0:T(8,128)(2,1)S(1)}, u32[]{:S(2)}, u32[]{:S(2)}) collective-permute-start(bf16[2,256,128]{2,1,0:T(8,128)(2,1)S(1)} %get-tuple-element.92), channel_id=1, source_target_pairs={{0,16},{8,24},{16,0},{24,8},{1,17},{9,25},{17,1},{25,9},{2,18},{10... | collective-permute-start | bytes 393224 | tf_op jit(solution)/shard_map/ppermute | solution.py:296
  110.5 0.6 collective-permute-done.30.refs_6_
  111.1 0.9 gather_sum.3
  112.2 0.9 collective-permute-start.32
  113.0 1.0 collective-permute-start.33
  114.6 3.9 %collective-permute-done.32.refs_6_ = bf16[2,256,128]{2,1,0:T(8,128)(2,1)S(1)} collective-permute-done((bf16[2,256,128]{2,1,0:T(8,128)(2,1)S(1)}, bf16[2,256,128]{2,1,0:T(8,128)(2,1)S(1)}, u32[]{:S(2)}, u32[]{:S(2)}) %collective-permute-start.32) | collective-permute-done | bytes 131104 | tf_op jit(solution)/shard_map/ppermute | solution.py:296
  118.5 1.9 %collective-permute-done.33.refs_7_ = bf16[2,256,128]{2,1,0:T(8,128)(2,1)S(1)} collective-permute-done((bf16[2,256,128]{2,1,0:T(8,128)(2,1)S(1)}, bf16[2,256,128]{2,1,0:T(8,128)(2,1)S(1)}, u32[]{:S(2)}, u32[]{:S(2)}) %collective-permute-start.33) | collective-permute-done | bytes 131104 | tf_op jit(solution)/shard_map/ppermute | solution.py:296
  120.4 1.6 %join.1 = (bf16[256,1024]{1,0:T(8,128)(2,1)}, bf16[256,1024]{1,0:T(8,128)(2,1)}) custom-call(s32[2]{0:T(128)S(1)} %copy-done.1, bf16[2,256,128]{2,1,0:T(8,128)(2,1)S(1)} %get-tuple-element.90.refs_0_, bf16[2,256,128]{2,1,0:T(8,128)(2,1)S(1)} %collective-permute-done.21.refs_1_, bf16[2,256,128]{2,1,0:T(8,128)(2,1)S(1)} %collective-permute-done.22.refs_2_, ...), custom_call_target="tpu_custom_call" | custom-call | tf_op jit(solution)/shard_map/join/pallas_call | solution.py:237
  (48 shorter events, 5.1 us)
Async XLA Ops:
  4.3 3.2 %collective-permute-start = (bf16[2,2,256,128]{3,2,1,0:T(8,128)(2,1)}, bf16[2,2,256,128]{3,2,1,0:T(8,128)(2,1)S(1)}, u32[]{:S(2)}, u32[]{:S(2)}) collective-permute-start(bf16[2,2,256,128]{3,2,1,0:T(8,128)(2,1)} %get-tuple-element.56), channel_id=1, source_target_pairs={{0,8},{8,0},{16,24},{24,16},{1,9},{9,1},{17,25},{25,17},{2,10},{10... | collective-permute-start | bytes 786440 | tf_op jit(solution)/shard_map/ppermute | solution.py:292
  4.8 10.7 %collective-permute-start.1 = (bf16[2,2,256,128]{3,2,1,0:T(8,128)(2,1)}, bf16[2,2,256,128]{3,2,1,0:T(8,128)(2,1)S(1)}, u32[]{:S(2)}, u32[]{:S(2)}) collective-permute-start(bf16[2,2,256,128]{3,2,1,0:T(8,128)(2,1)} %get-tuple-element.59), channel_id=1, source_target_pairs={{0,16},{8,24},{16,0},{24,8},{1,17},{9,25},{17,1},{25,9},{2,18},{10... | collective-permute-start | bytes 786440 | tf_op jit(solution)/shard_map/ppermute | solution.py:292
  7.3 12.5 %collective-permute-start.2 = (bf16[2,2,256,128]{3,2,1,0:T(8,128)(2,1)}, bf16[2,2,256,128]{3,2,1,0:T(8,128)(2,1)S(1)}, u32[]{:S(2)}, u32[]{:S(2)}) collective-permute-start(bf16[2,2,256,128]{3,2,1,0:T(8,128)(2,1)} %get-tuple-element.60), channel_id=1, source_target_pairs={{0,24},{8,16},{16,8},{24,0},{1,25},{9,17},{17,9},{25,1},{2,26},{10... | collective-permute-start | bytes 786440 | tf_op jit(solution)/shard_map/ppermute | solution.py:292
  9.4 12.5 %all-to-all-start = ((s32[8,1,128]{2,1,0:T(1,128)}), s32[8,1,128]{2,1,0:T(1,128)S(1)}, u32[]{:S(2)}, u32[]{:S(2)}) async-start(s32[8,1,128]{2,1,0:T(1,128)} %bitcast.3), calls=%async_computation | async-start | bytes 8192 | tf_op jit(solution)/shard_map/all_to_all | solution.py:341
  21.8 1.0 copy-start
  22.8 0.6 copy-start.1
  24.1 6.8 %collective-permute-start.3 = (bf16[2,3,64,128]{3,2,1,0:T(8,128)(2,1)S(1)}, bf16[2,3,64,128]{3,2,1,0:T(8,128)(2,1)S(1)}, u32[]{:S(2)}, u32[]{:S(2)}) collective-permute-start(bf16[2,3,64,128]{3,2,1,0:T(8,128)(2,1)S(1)} %get-tuple-element.61), channel_id=1, source_target_pairs={{0,1},{1,0},{2,3},{3,2},{4,5},{5,4},{6,7},{7,6},{8,9},{9,8},{10,11... | collective-permute-start | bytes 294920 | tf_op jit(solution)/shard_map/ppermute | solution.py:292
  24.7 8.5 %collective-permute-start.4 = (bf16[2,3,64,128]{3,2,1,0:T(8,128)(2,1)S(1)}, bf16[2,3,64,128]{3,2,1,0:T(8,128)(2,1)S(1)}, u32[]{:S(2)}, u32[]{:S(2)}) collective-permute-start(bf16[2,3,64,128]{3,2,1,0:T(8,128)(2,1)S(1)} %get-tuple-element.62), channel_id=1, source_target_pairs={{0,2},{1,3},{2,0},{3,1},{4,6},{5,7},{6,4},{7,5},{8,10},{9,11},{10,... | collective-permute-start | bytes 294920 | tf_op jit(solution)/shard_map/ppermute | solution.py:292
  25.5 14.5 %collective-permute-start.5 = (bf16[2,3,64,128]{3,2,1,0:T(8,128)(2,1)S(1)}, bf16[2,3,64,128]{3,2,1,0:T(8,128)(2,1)S(1)}, u32[]{:S(2)}, u32[]{:S(2)}) collective-permute-start(bf16[2,3,64,128]{3,2,1,0:T(8,128)(2,1)S(1)} %get-tuple-element.63), channel_id=1, source_target_pairs={{0,4},{1,5},{2,6},{3,7},{4,0},{5,1},{6,2},{7,3},{8,12},{9,13},{10,... | collective-permute-start | bytes 294920 | tf_op jit(solution)/shard_map/ppermute | solution.py:292
  28.1 14.1 %collective-permute-start.6 = (bf16[2,3,64,128]{3,2,1,0:T(8,128)(2,1)S(1)}, bf16[2,3,64,128]{3,2,1,0:T(8,128)(2,1)S(1)}, u32[]{:S(2)}, u32[]{:S(2)}) collective-permute-start(bf16[2,3,64,128]{3,2,1,0:T(8,128)(2,1)S(1)} %get-tuple-element.64), channel_id=1, source_target_pairs={{0,5},{1,4},{2,7},{3,6},{4,1},{5,0},{6,3},{7,2},{8,13},{9,12},{10,... | collective-permute-start | bytes 294920 | tf_op jit(solution)/shard_map/ppermute | solution.py:292
  29.3 12.9 %collective-permute-start.7 = (bf16[2,3,64,128]{3,2,1,0:T(8,128)(2,1)S(1)}, bf16[2,3,64,128]{3,2,1,0:T(8,128)(2,1)S(1)}, u32[]{:S(2)}, u32[]{:S(2)}) collective-permute-start(bf16[2,3,64,128]{3,2,1,0:T(8,128)(2,1)S(1)} %get-tuple-element.65), channel_id=1, source_target_pairs={{0,6},{1,7},{2,4},{3,5},{4,2},{5,3},{6,0},{7,1},{8,14},{9,15},{10,... | collective-permute-start | bytes 294920 | tf_op jit(solution)/shard_map/ppermute | solution.py:292
  30.9 11.3 %collective-permute-start.8 = (bf16[2,3,64,128]{3,2,1,0:T(8,128)(2,1)S(1)}, bf16[2,3,64,128]{3,2,1,0:T(8,128)(2,1)S(1)}, u32[]{:S(2)}, u32[]{:S(2)}) collective-permute-start(bf16[2,3,64,128]{3,2,1,0:T(8,128)(2,1)S(1)} %get-tuple-element.66), channel_id=1, source_target_pairs={{0,7},{1,6},{2,5},{3,4},{4,3},{5,2},{6,1},{7,0},{8,15},{9,14},{10,... | collective-permute-start | bytes 294920 | tf_op jit(solution)/shard_map/ppermute | solution.py:292
  33.2 10.3 %collective-permute-start.9 = (bf16[2,3,64,128]{3,2,1,0:T(8,128)(2,1)S(1)}, bf16[2,3,64,128]{3,2,1,0:T(8,128)(2,1)S(1)}, u32[]{:S(2)}, u32[]{:S(2)}) collective-permute-start(bf16[2,3,64,128]{3,2,1,0:T(8,128)(2,1)S(1)} %get-tuple-element.67), channel_id=1, source_target_pairs={{0,3},{1,2},{2,1},{3,0},{4,7},{5,6},{6,5},{7,4},{8,11},{9,10},{10,... | collective-permute-start | bytes 294920 | tf_op jit(solution)/shard_map/ppermute | solution.py:292
  43.5 23.0 %collective-permute-start.12 = (bf16[2,3,64,128]{3,2,1,0:T(8,128)(2,1)S(1)}, bf16[2,3,64,128]{3,2,1,0:T(8,128)(2,1)S(1)}, u32[]{:S(2)}, u32[]{:S(2)}) collective-permute-start(bf16[2,3,64,128]{3,2,1,0:T(8,128)(2,1)S(1)} %get-tuple-element.71), channel_id=1, source_target_pairs={{0,4},{1,5},{2,6},{3,7},{4,0},{5,1},{6,2},{7,3},{8,12},{9,13},{10,... | collective-permute-start | bytes 294920 | tf_op jit(solution)/shard_map/ppermute | solution.py:292
  47.2 19.4 %collective-permute-start.13 = (bf16[2,3,64,128]{3,2,1,0:T(8,128)(2,1)S(1)}, bf16[2,3,64,128]{3,2,1,0:T(8,128)(2,1)S(1)}, u32[]{:S(2)}, u32[]{:S(2)}) collective-permute-start(bf16[2,3,64,128]{3,2,1,0:T(8,128)(2,1)S(1)} %get-tuple-element.73), channel_id=1, source_target_pairs={{0,5},{1,4},{2,7},{3,6},{4,1},{5,0},{6,3},{7,2},{8,13},{9,12},{10,... | collective-permute-start | bytes 294920 | tf_op jit(solution)/shard_map/ppermute | solution.py:292
  48.2 20.4 %collective-permute-start.14 = (bf16[2,3,64,128]{3,2,1,0:T(8,128)(2,1)S(1)}, bf16[2,3,64,128]{3,2,1,0:T(8,128)(2,1)S(1)}, u32[]{:S(2)}, u32[]{:S(2)}) collective-permute-start(bf16[2,3,64,128]{3,2,1,0:T(8,128)(2,1)S(1)} %get-tuple-element.75), channel_id=1, source_target_pairs={{0,6},{1,7},{2,4},{3,5},{4,2},{5,3},{6,0},{7,1},{8,14},{9,15},{10,... | collective-permute-start | bytes 294920 | tf_op jit(solution)/shard_map/ppermute | solution.py:292
  49.5 20.2 %collective-permute-start.15 = (bf16[2,3,64,128]{3,2,1,0:T(8,128)(2,1)S(1)}, bf16[2,3,64,128]{3,2,1,0:T(8,128)(2,1)S(1)}, u32[]{:S(2)}, u32[]{:S(2)}) collective-permute-start(bf16[2,3,64,128]{3,2,1,0:T(8,128)(2,1)S(1)} %get-tuple-element.77), channel_id=1, source_target_pairs={{0,7},{1,6},{2,5},{3,4},{4,3},{5,2},{6,1},{7,0},{8,15},{9,14},{10,... | collective-permute-start | bytes 294920 | tf_op jit(solution)/shard_map/ppermute | solution.py:292
  65.1 7.3 %collective-permute-start.10 = (bf16[2,3,64,128]{3,2,1,0:T(8,128)(2,1)S(1)}, bf16[2,3,64,128]{3,2,1,0:T(8,128)(2,1)S(1)}, u32[]{:S(2)}, u32[]{:S(2)}) collective-permute-start(bf16[2,3,64,128]{3,2,1,0:T(8,128)(2,1)S(1)} %get-tuple-element.68), channel_id=1, source_target_pairs={{0,1},{1,0},{2,3},{3,2},{4,5},{5,4},{6,7},{7,6},{8,9},{9,8},{10,11... | collective-permute-start | bytes 294920 | tf_op jit(solution)/shard_map/ppermute | solution.py:292
  66.5 7.2 %collective-permute-start.11 = (bf16[2,3,64,128]{3,2,1,0:T(8,128)(2,1)S(1)}, bf16[2,3,64,128]{3,2,1,0:T(8,128)(2,1)S(1)}, u32[]{:S(2)}, u32[]{:S(2)}) collective-permute-start(bf16[2,3,64,128]{3,2,1,0:T(8,128)(2,1)S(1)} %get-tuple-element.69), channel_id=1, source_target_pairs={{0,2},{1,3},{2,0},{3,1},{4,6},{5,7},{6,4},{7,5},{8,10},{9,11},{10,... | collective-permute-start | bytes 294920 | tf_op jit(solution)/shard_map/ppermute | solution.py:292
  66.6 9.6 %collective-permute-start.16 = (bf16[2,3,64,128]{3,2,1,0:T(8,128)(2,1)S(1)}, bf16[2,3,64,128]{3,2,1,0:T(8,128)(2,1)S(1)}, u32[]{:S(2)}, u32[]{:S(2)}) collective-permute-start(bf16[2,3,64,128]{3,2,1,0:T(8,128)(2,1)S(1)} %get-tuple-element.78), channel_id=1, source_target_pairs={{0,3},{1,2},{2,1},{3,0},{4,7},{5,6},{6,5},{7,4},{8,11},{9,10},{10,... | collective-permute-start | bytes 294920 | tf_op jit(solution)/shard_map/ppermute | solution.py:292
  68.6 20.8 %collective-permute-start.17 = (bf16[2,3,64,128]{3,2,1,0:T(8,128)(2,1)S(1)}, bf16[2,3,64,128]{3,2,1,0:T(8,128)(2,1)S(1)}, u32[]{:S(2)}, u32[]{:S(2)}) collective-permute-start(bf16[2,3,64,128]{3,2,1,0:T(8,128)(2,1)S(1)} %get-tuple-element.86), channel_id=1, source_target_pairs={{0,4},{1,5},{2,6},{3,7},{4,0},{5,1},{6,2},{7,3},{8,12},{9,13},{10,... | collective-permute-start | bytes 294920 | tf_op jit(solution)/shard_map/ppermute | solution.py:292
  69.7 19.7 %collective-permute-start.18 = (bf16[2,3,64,128]{3,2,1,0:T(8,128)(2,1)S(1)}, bf16[2,3,64,128]{3,2,1,0:T(8,128)(2,1)S(1)}, u32[]{:S(2)}, u32[]{:S(2)}) collective-permute-start(bf16[2,3,64,128]{3,2,1,0:T(8,128)(2,1)S(1)} %get-tuple-element.87), channel_id=1, source_target_pairs={{0,5},{1,4},{2,7},{3,6},{4,1},{5,0},{6,3},{7,2},{8,13},{9,12},{10,... | collective-permute-start | bytes 294920 | tf_op jit(solution)/shard_map/ppermute | solution.py:292
  72.4 16.9 %collective-permute-start.19 = (bf16[2,3,64,128]{3,2,1,0:T(8,128)(2,1)S(1)}, bf16[2,3,64,128]{3,2,1,0:T(8,128)(2,1)S(1)}, u32[]{:S(2)}, u32[]{:S(2)}) collective-permute-start(bf16[2,3,64,128]{3,2,1,0:T(8,128)(2,1)S(1)} %get-tuple-element.88), channel_id=1, source_target_pairs={{0,6},{1,7},{2,4},{3,5},{4,2},{5,3},{6,0},{7,1},{8,14},{9,15},{10,... | collective-permute-start | bytes 294920 | tf_op jit(solution)/shard_map/ppermute | solution.py:292
  73.7 15.6 %collective-permute-start.20 = (bf16[2,3,64,128]{3,2,1,0:T(8,128)(2,1)S(1)}, bf16[2,3,64,128]{3,2,1,0:T(8,128)(2,1)S(1)}, u32[]{:S(2)}, u32[]{:S(2)}) collective-permute-start(bf16[2,3,64,128]{3,2,1,0:T(8,128)(2,1)S(1)} %get-tuple-element.89), channel_id=1, source_target_pairs={{0,7},{1,6},{2,5},{3,4},{4,3},{5,2},{6,1},{7,0},{8,15},{9,14},{10,... | collective-permute-start | bytes 294920 | tf_op jit(solution)/shard_map/ppermute | solution.py:292
  90.3 10.1 %collective-permute-start.23 = (bf16[2,256,128]{2,1,0:T(8,128)(2,1)S(1)}, bf16[2,256,128]{2,1,0:T(8,128)(2,1)S(1)}, u32[]{:S(2)}, u32[]{:S(2)}) collective-permute-start(bf16[2,256,128]{2,1,0:T(8,128)(2,1)S(1)} %get-tuple-element.93), channel_id=1, source_target_pairs={{0,24},{8,16},{16,8},{24,0},{1,25},{9,17},{17,9},{25,1},{2,26},{10... | collective-permute-start | bytes 393224 | tf_op jit(solution)/shard_map/ppermute | solution.py:296
  90.4 5.2 %collective-permute-start.24 = (bf16[2,3,64,128]{3,2,1,0:T(8,128)(2,1)S(1)}, bf16[2,3,64,128]{3,2,1,0:T(8,128)(2,1)S(1)}, u32[]{:S(2)}, u32[]{:S(2)}) collective-permute-start(bf16[2,3,64,128]{3,2,1,0:T(8,128)(2,1)S(1)} %get-tuple-element.95), channel_id=1, source_target_pairs={{0,1},{1,0},{2,3},{3,2},{4,5},{5,4},{6,7},{7,6},{8,9},{9,8},{10,11... | collective-permute-start | bytes 294920 | tf_op jit(solution)/shard_map/ppermute | solution.py:292
  91.9 6.9 %collective-permute-start.25 = (bf16[2,3,64,128]{3,2,1,0:T(8,128)(2,1)S(1)}, bf16[2,3,64,128]{3,2,1,0:T(8,128)(2,1)S(1)}, u32[]{:S(2)}, u32[]{:S(2)}) collective-permute-start(bf16[2,3,64,128]{3,2,1,0:T(8,128)(2,1)S(1)} %get-tuple-element.96), channel_id=1, source_target_pairs={{0,2},{1,3},{2,0},{3,1},{4,6},{5,7},{6,4},{7,5},{8,10},{9,11},{10,... | collective-permute-start | bytes 294920 | tf_op jit(solution)/shard_map/ppermute | solution.py:292
  91.9 14.9 %collective-permute-start.26 = (bf16[2,3,64,128]{3,2,1,0:T(8,128)(2,1)S(1)}, bf16[2,3,64,128]{3,2,1,0:T(8,128)(2,1)S(1)}, u32[]{:S(2)}, u32[]{:S(2)}) collective-permute-start(bf16[2,3,64,128]{3,2,1,0:T(8,128)(2,1)S(1)} %get-tuple-element.97), channel_id=1, source_target_pairs={{0,4},{1,5},{2,6},{3,7},{4,0},{5,1},{6,2},{7,3},{8,12},{9,13},{10,... | collective-permute-start | bytes 294920 | tf_op jit(solution)/shard_map/ppermute | solution.py:292
  93.6 15.2 %collective-permute-start.27 = (bf16[2,3,64,128]{3,2,1,0:T(8,128)(2,1)S(1)}, bf16[2,3,64,128]{3,2,1,0:T(8,128)(2,1)S(1)}, u32[]{:S(2)}, u32[]{:S(2)}) collective-permute-start(bf16[2,3,64,128]{3,2,1,0:T(8,128)(2,1)S(1)} %get-tuple-element.98), channel_id=1, source_target_pairs={{0,5},{1,4},{2,7},{3,6},{4,1},{5,0},{6,3},{7,2},{8,13},{9,12},{10,... | collective-permute-start | bytes 294920 | tf_op jit(solution)/shard_map/ppermute | solution.py:292
  95.6 14.9 %collective-permute-start.28 = (bf16[2,3,64,128]{3,2,1,0:T(8,128)(2,1)S(1)}, bf16[2,3,64,128]{3,2,1,0:T(8,128)(2,1)S(1)}, u32[]{:S(2)}, u32[]{:S(2)}) collective-permute-start(bf16[2,3,64,128]{3,2,1,0:T(8,128)(2,1)S(1)} %get-tuple-element.99), channel_id=1, source_target_pairs={{0,6},{1,7},{2,4},{3,5},{4,2},{5,3},{6,0},{7,1},{8,14},{9,15},{10,... | collective-permute-start | bytes 294920 | tf_op jit(solution)/shard_map/ppermute | solution.py:292
  98.8 11.7 %collective-permute-start.29 = (bf16[2,3,64,128]{3,2,1,0:T(8,128)(2,1)S(1)}, bf16[2,3,64,128]{3,2,1,0:T(8,128)(2,1)S(1)}, u32[]{:S(2)}, u32[]{:S(2)}) collective-permute-start(bf16[2,3,64,128]{3,2,1,0:T(8,128)(2,1)S(1)} %get-tuple-element.100), channel_id=1, source_target_pairs={{0,7},{1,6},{2,5},{3,4},{4,3},{5,2},{6,1},{7,0},{8,15},{9,14},{10,... | collective-permute-start | bytes 294920 | tf_op jit(solution)/shard_map/ppermute | solution.py:292
  100.3 10.8 %collective-permute-start.30 = (bf16[2,3,64,128]{3,2,1,0:T(8,128)(2,1)S(1)}, bf16[2,3,64,128]{3,2,1,0:T(8,128)(2,1)S(1)}, u32[]{:S(2)}, u32[]{:S(2)}) collective-permute-start(bf16[2,3,64,128]{3,2,1,0:T(8,128)(2,1)S(1)} %get-tuple-element.101), channel_id=1, source_target_pairs={{0,3},{1,2},{2,1},{3,0},{4,7},{5,6},{6,5},{7,4},{8,11},{9,10},{10,... | collective-permute-start | bytes 294920 | tf_op jit(solution)/shard_map/ppermute | solution.py:292
  106.7 7.3 %collective-permute-start.21 = (bf16[2,256,128]{2,1,0:T(8,128)(2,1)S(1)}, bf16[2,256,128]{2,1,0:T(8,128)(2,1)S(1)}, u32[]{:S(2)}, u32[]{:S(2)}) collective-permute-start(bf16[2,256,128]{2,1,0:T(8,128)(2,1)S(1)} %get-tuple-element.91), channel_id=1, source_target_pairs={{0,8},{8,0},{16,24},{24,16},{1,9},{9,1},{17,25},{25,17},{2,10},{10... | collective-permute-start | bytes 393224 | tf_op jit(solution)/shard_map/ppermute | solution.py:296
  108.9 5.7 %collective-permute-start.22 = (bf16[2,256,128]{2,1,0:T(8,128)(2,1)S(1)}, bf16[2,256,128]{2,1,0:T(8,128)(2,1)S(1)}, u32[]{:S(2)}, u32[]{:S(2)}) collective-permute-start(bf16[2,256,128]{2,1,0:T(8,128)(2,1)S(1)} %get-tuple-element.92), channel_id=1, source_target_pairs={{0,16},{8,24},{16,0},{24,8},{1,17},{9,25},{17,1},{25,9},{2,18},{10... | collective-permute-start | bytes 393224 | tf_op jit(solution)/shard_map/ppermute | solution.py:296
  112.1 2.5 %collective-permute-start.31 = (bf16[2,256,128]{2,1,0:T(8,128)(2,1)S(1)}, bf16[2,256,128]{2,1,0:T(8,128)(2,1)S(1)}, u32[]{:S(2)}, u32[]{:S(2)}) collective-permute-start(bf16[2,256,128]{2,1,0:T(8,128)(2,1)S(1)} %get-tuple-element.103), channel_id=1, source_target_pairs={{0,8},{8,0},{16,24},{24,16},{1,9},{9,1},{17,25},{25,17},{2,10},{10... | collective-permute-start | bytes 393224 | tf_op jit(solution)/shard_map/ppermute | solution.py:296
  112.2 6.3 %collective-permute-start.32 = (bf16[2,256,128]{2,1,0:T(8,128)(2,1)S(1)}, bf16[2,256,128]{2,1,0:T(8,128)(2,1)S(1)}, u32[]{:S(2)}, u32[]{:S(2)}) collective-permute-start(bf16[2,256,128]{2,1,0:T(8,128)(2,1)S(1)} %get-tuple-element.104), channel_id=1, source_target_pairs={{0,16},{8,24},{16,0},{24,8},{1,17},{9,25},{17,1},{25,9},{2,18},{10... | collective-permute-start | bytes 393224 | tf_op jit(solution)/shard_map/ppermute | solution.py:296
  113.0 7.4 %collective-permute-start.33 = (bf16[2,256,128]{2,1,0:T(8,128)(2,1)S(1)}, bf16[2,256,128]{2,1,0:T(8,128)(2,1)S(1)}, u32[]{:S(2)}, u32[]{:S(2)}) collective-permute-start(bf16[2,256,128]{2,1,0:T(8,128)(2,1)S(1)} %get-tuple-element.105), channel_id=1, source_target_pairs={{0,24},{8,16},{16,8},{24,0},{1,25},{9,17},{17,9},{25,1},{2,26},{10... | collective-permute-start | bytes 393224 | tf_op jit(solution)/shard_map/ppermute | solution.py:296

commit v16 on v15

--- a/solution.py
+++ b/solution.py
@@ -110,6 +110,12 @@
     return jnp.concatenate([ref[rows, g * HEAD_DIM : (g + 1) * HEAD_DIM] for g in range(GROUP)], axis=0)
 
 
+def beside(turned, kv, listed):
+    left = lax.broadcasted_iota(jnp.int32, (HEAD_DIM, 2 * BLK), 1) < BLK
+    pairs = zip(listed[::2], listed[1::2])
+    return jnp.concatenate([jnp.where(left, turned[kv, a], turned[kv, b]) for a, b in pairs], axis=1)
+
+
 def by_row(ref, b, x):
     rows = slice(b * BLK, (b + 1) * BLK)
     for g in range(GROUP):
@@ -119,9 +125,9 @@
 def attend_kernel(place, source, asked, q_ref, g_ref, *refs, heads, head, last, shard_count):
     steps = shard_count - 1
     own, far = refs[:heads], refs[heads : heads + steps]
-    table, total = refs[-2:]
-    outs = refs[-2 - steps : -2]
-    o_ref, dq_ref, near_out = refs[-5 - steps : -2 - steps]
+    table, turned, total = refs[-3:]
+    outs = refs[-3 - steps : -3]
+    o_ref, dq_ref, near_out = refs[-6 - steps : -3 - steps]
     step = pl.program_id(0)
     blocks_here = near_out.shape[1]
 
@@ -133,6 +139,10 @@
             for kv in range(2):
                 for s in range(CAP):
                     table[kv, first + s] = part[kv, s]
+        for kv in range(2):
+            for slot in range(table.shape[1]):
+                block = table[kv, slot].T
+                turned[kv, slot] = jnp.concatenate([block, block], axis=1)
         total[...] = jnp.zeros_like(total)
 
     key_row = lax.broadcasted_iota(jnp.int32, (BLK, GROUP * BLK), 0)
@@ -160,7 +170,7 @@
             probs[b] = expo * (1.0 / jnp.sum(expo, axis=0, keepdims=True))
             probs_low[b] = probs[b].astype(jnp.bfloat16)
         for b in subs:
-            attended = dot(probs_low[b], values[b], TN).astype(jnp.bfloat16)
+            attended = dot(beside(turned, 1, listed[b]), probs_low[b], NN).astype(jnp.bfloat16).T
             by_row(o_ref, b, attended)
             dv = dot(probs_low[b], g_out[b], NN)
             delta = jnp.sum(probs[b] * dprob[b], axis=0, keepdims=True)
@@ -168,7 +178,7 @@
             for e in range(LIST):
                 total[1, listed[b][e]] += dv[e * BLK : (e + 1) * BLK]
         for b in subs:
-            dq = (dot(dscore[b], keys[b], TN) * SCALE).astype(jnp.bfloat16)
+            dq = (dot(beside(turned, 0, listed[b]), dscore[b], NN) * SCALE).astype(jnp.bfloat16).T
             by_row(dq_ref, b, dq)
             dk = dot(dscore[b], q[b], NN)
             for e in range(LIST):
@@ -272,6 +282,7 @@
             out_specs=[tile, tile, whole(near_shape)] + [whole(x.shape) for x in out_shapes],
             scratch_shapes=[
                 pltpu.VMEM((2, slots, BLK, HEAD_DIM), jnp.bfloat16),
+                pltpu.VMEM((2, slots, HEAD_DIM, 2 * BLK), jnp.bfloat16),
                 pltpu.VMEM((2, slots, BLK, HEAD_DIM), jnp.float32),
             ],
         ),

time: 122 us -> 124 us (1.016)
  transfers between devices with their start and end apart: 35 -> 35, of which waited for: 13 -> 13; matrix products, arithmetic and copies ran while one was open for 2% -> 2% of each run, Pallas kernels for 23% -> 24%
where the time goes in v16:
time: 124 us; the launch traced here: 123 us
  starting transfers between devices  50.2 us (40%)
  Pallas kernels  35.2 us (28%)
  waiting for transfers between devices  32.8 us (26%)
  local copies, waits for them, and re-layouts  2.48 us (2%)
  other arithmetic  1.79 us (1%)
    ppermute x28, starting transfers between devices, send(): lax.ppermute(x, axis, [(i, partner(i, r, count)) for i in range(count)])  39.9 us
    pallas_call x2, Pallas kernels, attend(): pl.pallas_call(functools.partial(attend_kernel, heads=len(own), head=head...  27.4 us
    ppermute x28, waiting for transfers between devices, send(): lax.ppermute(x, axis, [(i, partner(i, r, count)) for i in range(count)])  24.3 us
    pallas_call x6, Pallas kernels, call(): pl.pallas_call(kernel, grid_spec=pltpu.PrefetchScalarGridSpec(num_scalar_...  7.83 us
    ppermute x6, waiting for transfers between devices, send_back(): lax.ppermute(x, axis, [(i, origin(i, r, count)) for i in range(count)])  6.4 us
    all_to_all x1, starting transfers between devices, per_device(): lax.all_to_all(requests, 'ctx', split_axis=0, concat_axis=0, tiled=True)  6.07 us
    ppermute x6, starting transfers between devices, send_back(): lax.ppermute(x, axis, [(i, origin(i, r, count)) for i in range(count)])  4.29 us
  transfers between devices with their start and end apart: 35, of which 13 were waited for; matrix products, arithmetic and copies ran while one was open for 2% of the time, Pallas kernels for 24%

profile of v16, /device:TPU:0, one launch (start us, length us, event | category | flops | bytes accessed | tf_op | source)
XLA Modules:
  0.0 123.3 jit_solution(7914019607310516619)
XLA Ops:
  1.2 3.0 %split.1 = (bf16[2,2,256,128]{3,2,1,0:T(8,128)(2,1)}, bf16[2,2,256,128]{3,2,1,0:T(8,128)(2,1)}, bf16[2,2,256,128]{3,2,1,0:T(8,128)(2,1)}, bf16[2,2,256,128]{3,2,1,0:T(8,128)(2,1)}) custom-call(s32[2]{0:T(128)} %pad_add_fusion.place, bf16[256,1024]{1,0:T(8,128)(2,1)} %k_ref.1, bf16[256,1024]{1,0:T(8,128)(2,1)} %v_ref.1), custom_call_target="tpu_custom_call" | custom-call | tf_op jit(solution)/shard_map/split/pallas_call | solution.py:247
  4.8 2.6 %collective-permute-start.1 = (bf16[2,2,256,128]{3,2,1,0:T(8,128)(2,1)}, bf16[2,2,256,128]{3,2,1,0:T(8,128)(2,1)S(1)}, u32[]{:S(2)}, u32[]{:S(2)}) collective-permute-start(bf16[2,2,256,128]{3,2,1,0:T(8,128)(2,1)} %get-tuple-element.59), channel_id=1, source_target_pairs={{0,16},{8,24},{16,0},{24,8},{1,17},{9,25},{17,1},{25,9},{2,18},{10... | collective-permute-start | bytes 786440 | tf_op jit(solution)/shard_map/ppermute | solution.py:303
  7.4 0.8 copy.14
  8.7 0.7 select_reduce_fusion
  9.4 6.1 %all-to-all-start = ((s32[8,1,128]{2,1,0:T(1,128)}), s32[8,1,128]{2,1,0:T(1,128)S(1)}, u32[]{:S(2)}, u32[]{:S(2)}) async-start(s32[8,1,128]{2,1,0:T(1,128)} %bitcast.3), calls=%async_computation | async-start | bytes 8192 | tf_op jit(solution)/shard_map/all_to_all | solution.py:352
  15.5 4.3 %collective-permute-done.2.refs_3_ = bf16[2,2,256,128]{3,2,1,0:T(8,128)(2,1)S(1)} collective-permute-done((bf16[2,2,256,128]{3,2,1,0:T(8,128)(2,1)}, bf16[2,2,256,128]{3,2,1,0:T(8,128)(2,1)S(1)}, u32[]{:S(2)}, u32[]{:S(2)}) %collective-permute-start.2) | collective-permute-done | bytes 262176 | tf_op jit(solution)/shard_map/ppermute | solution.py:303
  19.8 2.0 %all-to-all-done = s32[8,1,128]{2,1,0:T(1,128)S(1)} async-done(((s32[8,1,128]{2,1,0:T(1,128)}), s32[8,1,128]{2,1,0:T(1,128)S(1)}, u32[]{:S(2)}, u32[]{:S(2)}) %all-to-all-start) | async-done | bytes 4128 | tf_op jit(solution)/shard_map/all_to_all | solution.py:352
  21.8 0.9 copy-done
  23.4 0.7 pick.2
  24.1 0.6 collective-permute-start.3
  25.5 2.7 %collective-permute-start.5 = (bf16[2,3,64,128]{3,2,1,0:T(8,128)(2,1)S(1)}, bf16[2,3,64,128]{3,2,1,0:T(8,128)(2,1)S(1)}, u32[]{:S(2)}, u32[]{:S(2)}) collective-permute-start(bf16[2,3,64,128]{3,2,1,0:T(8,128)(2,1)S(1)} %get-tuple-element.63), channel_id=1, source_target_pairs={{0,4},{1,5},{2,6},{3,7},{4,0},{5,1},{6,2},{7,3},{8,12},{9,13},{10,... | collective-permute-start | bytes 294920 | tf_op jit(solution)/shard_map/ppermute | solution.py:303
  28.1 1.2 collective-permute-start.6
  29.3 1.6 %collective-permute-start.7 = (bf16[2,3,64,128]{3,2,1,0:T(8,128)(2,1)S(1)}, bf16[2,3,64,128]{3,2,1,0:T(8,128)(2,1)S(1)}, u32[]{:S(2)}, u32[]{:S(2)}) collective-permute-start(bf16[2,3,64,128]{3,2,1,0:T(8,128)(2,1)S(1)} %get-tuple-element.65), channel_id=1, source_target_pairs={{0,6},{1,7},{2,4},{3,5},{4,2},{5,3},{6,0},{7,1},{8,14},{9,15},{10,... | collective-permute-start | bytes 294920 | tf_op jit(solution)/shard_map/ppermute | solution.py:303
  30.9 2.3 %collective-permute-start.8 = (bf16[2,3,64,128]{3,2,1,0:T(8,128)(2,1)S(1)}, bf16[2,3,64,128]{3,2,1,0:T(8,128)(2,1)S(1)}, u32[]{:S(2)}, u32[]{:S(2)}) collective-permute-start(bf16[2,3,64,128]{3,2,1,0:T(8,128)(2,1)S(1)} %get-tuple-element.66), channel_id=1, source_target_pairs={{0,7},{1,6},{2,5},{3,4},{4,3},{5,2},{6,1},{7,0},{8,15},{9,14},{10,... | collective-permute-start | bytes 294920 | tf_op jit(solution)/shard_map/ppermute | solution.py:303
  33.7 0.7 pick.3
  34.4 5.6 %collective-permute-done.5.refs_6_ = bf16[2,3,64,128]{3,2,1,0:T(8,128)(2,1)S(1)} collective-permute-done((bf16[2,3,64,128]{3,2,1,0:T(8,128)(2,1)S(1)}, bf16[2,3,64,128]{3,2,1,0:T(8,128)(2,1)S(1)}, u32[]{:S(2)}, u32[]{:S(2)}) %collective-permute-start.5) | collective-permute-done | bytes 98336 | tf_op jit(solution)/shard_map/ppermute | solution.py:303
  40.0 2.2 %collective-permute-done.6.refs_7_ = bf16[2,3,64,128]{3,2,1,0:T(8,128)(2,1)S(1)} collective-permute-done((bf16[2,3,64,128]{3,2,1,0:T(8,128)(2,1)S(1)}, bf16[2,3,64,128]{3,2,1,0:T(8,128)(2,1)S(1)}, u32[]{:S(2)}, u32[]{:S(2)}) %collective-permute-start.6) | collective-permute-done | bytes 98336 | tf_op jit(solution)/shard_map/ppermute | solution.py:303
  42.2 1.3 %collective-permute-done.9.refs_10_ = bf16[2,3,64,128]{3,2,1,0:T(8,128)(2,1)S(1)} collective-permute-done((bf16[2,3,64,128]{3,2,1,0:T(8,128)(2,1)S(1)}, bf16[2,3,64,128]{3,2,1,0:T(8,128)(2,1)S(1)}, u32[]{:S(2)}, u32[]{:S(2)}) %collective-permute-start.9) | collective-permute-done | bytes 98336 | tf_op jit(solution)/shard_map/ppermute | solution.py:303
  43.5 3.7 %collective-permute-start.12 = (bf16[2,3,64,128]{3,2,1,0:T(8,128)(2,1)S(1)}, bf16[2,3,64,128]{3,2,1,0:T(8,128)(2,1)S(1)}, u32[]{:S(2)}, u32[]{:S(2)}) collective-permute-start(bf16[2,3,64,128]{3,2,1,0:T(8,128)(2,1)S(1)} %get-tuple-element.71), channel_id=1, source_target_pairs={{0,4},{1,5},{2,6},{3,7},{4,0},{5,1},{6,2},{7,3},{8,12},{9,13},{10,... | collective-permute-start | bytes 294920 | tf_op jit(solution)/shard_map/ppermute | solution.py:303
  47.2 0.9 collective-permute-start.13
  48.2 1.3 %collective-permute-start.14 = (bf16[2,3,64,128]{3,2,1,0:T(8,128)(2,1)S(1)}, bf16[2,3,64,128]{3,2,1,0:T(8,128)(2,1)S(1)}, u32[]{:S(2)}, u32[]{:S(2)}) collective-permute-start(bf16[2,3,64,128]{3,2,1,0:T(8,128)(2,1)S(1)} %get-tuple-element.75), channel_id=1, source_target_pairs={{0,6},{1,7},{2,4},{3,5},{4,2},{5,3},{6,0},{7,1},{8,14},{9,15},{10,... | collective-permute-start | bytes 294920 | tf_op jit(solution)/shard_map/ppermute | solution.py:303
  49.5 2.5 %collective-permute-start.15 = (bf16[2,3,64,128]{3,2,1,0:T(8,128)(2,1)S(1)}, bf16[2,3,64,128]{3,2,1,0:T(8,128)(2,1)S(1)}, u32[]{:S(2)}, u32[]{:S(2)}) collective-permute-start(bf16[2,3,64,128]{3,2,1,0:T(8,128)(2,1)S(1)} %get-tuple-element.77), channel_id=1, source_target_pairs={{0,7},{1,6},{2,5},{3,4},{4,3},{5,2},{6,1},{7,0},{8,15},{9,14},{10,... | collective-permute-start | bytes 294920 | tf_op jit(solution)/shard_map/ppermute | solution.py:303
  52.0 13.7 %attend.2 = (bf16[1024,1024]{1,0:T(8,128)(2,1)}, bf16[1024,1024]{1,0:T(8,128)(2,1)}, bf16[2,16,64,128]{3,2,1,0:T(8,128)(2,1)S(1)}, bf16[2,3,64,128]{3,2,1,0:T(8,...) custom-call(s32[2]{0:T(128)S(1)} %copy-done.1, ...), custom_call_target="tpu_custom_call" | custom-call | flops 3221225472 | bytes 20971520 | tf_op jit(solution)/shard_map/attend/pallas_call | solution.py:271
  65.7 1.4 %collective-permute-start.10 = (bf16[2,3,64,128]{3,2,1,0:T(8,128)(2,1)S(1)}, bf16[2,3,64,128]{3,2,1,0:T(8,128)(2,1)S(1)}, u32[]{:S(2)}, u32[]{:S(2)}) collective-permute-start(bf16[2,3,64,128]{3,2,1,0:T(8,128)(2,1)S(1)} %get-tuple-element.68), channel_id=1, source_target_pairs={{0,1},{1,0},{2,3},{3,2},{4,5},{5,4},{6,7},{7,6},{8,9},{9,8},{10,11... | collective-permute-start | bytes 294920 | tf_op jit(solution)/shard_map/ppermute | solution.py:303
  67.2 2.0 %collective-permute-start.16 = (bf16[2,3,64,128]{3,2,1,0:T(8,128)(2,1)S(1)}, bf16[2,3,64,128]{3,2,1,0:T(8,128)(2,1)S(1)}, u32[]{:S(2)}, u32[]{:S(2)}) collective-permute-start(bf16[2,3,64,128]{3,2,1,0:T(8,128)(2,1)S(1)} %get-tuple-element.78), channel_id=1, source_target_pairs={{0,3},{1,2},{2,1},{3,0},{4,7},{5,6},{6,5},{7,4},{8,11},{9,10},{10,... | collective-permute-start | bytes 294920 | tf_op jit(solution)/shard_map/ppermute | solution.py:303
  69.2 1.1 collective-permute-start.17
  70.3 2.7 %collective-permute-start.18 = (bf16[2,3,64,128]{3,2,1,0:T(8,128)(2,1)S(1)}, bf16[2,3,64,128]{3,2,1,0:T(8,128)(2,1)S(1)}, u32[]{:S(2)}, u32[]{:S(2)}) collective-permute-start(bf16[2,3,64,128]{3,2,1,0:T(8,128)(2,1)S(1)} %get-tuple-element.87), channel_id=1, source_target_pairs={{0,5},{1,4},{2,7},{3,6},{4,1},{5,0},{6,3},{7,2},{8,13},{9,12},{10,... | collective-permute-start | bytes 294920 | tf_op jit(solution)/shard_map/ppermute | solution.py:303
  73.0 1.3 %collective-permute-start.19 = (bf16[2,3,64,128]{3,2,1,0:T(8,128)(2,1)S(1)}, bf16[2,3,64,128]{3,2,1,0:T(8,128)(2,1)S(1)}, u32[]{:S(2)}, u32[]{:S(2)}) collective-permute-start(bf16[2,3,64,128]{3,2,1,0:T(8,128)(2,1)S(1)} %get-tuple-element.88), channel_id=1, source_target_pairs={{0,6},{1,7},{2,4},{3,5},{4,2},{5,3},{6,0},{7,1},{8,14},{9,15},{10,... | collective-permute-start | bytes 294920 | tf_op jit(solution)/shard_map/ppermute | solution.py:303
  74.3 2.5 %collective-permute-start.20 = (bf16[2,3,64,128]{3,2,1,0:T(8,128)(2,1)S(1)}, bf16[2,3,64,128]{3,2,1,0:T(8,128)(2,1)S(1)}, u32[]{:S(2)}, u32[]{:S(2)}) collective-permute-start(bf16[2,3,64,128]{3,2,1,0:T(8,128)(2,1)S(1)} %get-tuple-element.89), channel_id=1, source_target_pairs={{0,7},{1,6},{2,5},{3,4},{4,3},{5,2},{6,1},{7,0},{8,15},{9,14},{10,... | collective-permute-start | bytes 294920 | tf_op jit(solution)/shard_map/ppermute | solution.py:303
  76.9 13.7 %attend.3 = (bf16[1024,1024]{1,0:T(8,128)(2,1)}, bf16[1024,1024]{1,0:T(8,128)(2,1)}, bf16[2,16,64,128]{3,2,1,0:T(8,128)(2,1)S(1)}, bf16[2,3,64,128]{3,2,1,0:T(8,...) custom-call(s32[2]{0:T(128)S(1)} %copy-done.1, ...), custom_call_target="tpu_custom_call", output_to_operand_aliasing={{0}: (16, {}), {1}: (17, {})} | custom-call | flops 3221225472 | bytes 20971520 | tf_op jit(solution)/shard_map/attend/pallas_call | solution.py:271
  90.6 0.9 gather_sum.2
  91.6 1.5 %collective-permute-start.24 = (bf16[2,3,64,128]{3,2,1,0:T(8,128)(2,1)S(1)}, bf16[2,3,64,128]{3,2,1,0:T(8,128)(2,1)S(1)}, u32[]{:S(2)}, u32[]{:S(2)}) collective-permute-start(bf16[2,3,64,128]{3,2,1,0:T(8,128)(2,1)S(1)} %get-tuple-element.95), channel_id=1, source_target_pairs={{0,1},{1,0},{2,3},{3,2},{4,5},{5,4},{6,7},{7,6},{8,9},{9,8},{10,11... | collective-permute-start | bytes 294920 | tf_op jit(solution)/shard_map/ppermute | solution.py:303
  93.1 1.7 %collective-permute-start.26 = (bf16[2,3,64,128]{3,2,1,0:T(8,128)(2,1)S(1)}, bf16[2,3,64,128]{3,2,1,0:T(8,128)(2,1)S(1)}, u32[]{:S(2)}, u32[]{:S(2)}) collective-permute-start(bf16[2,3,64,128]{3,2,1,0:T(8,128)(2,1)S(1)} %get-tuple-element.97), channel_id=1, source_target_pairs={{0,4},{1,5},{2,6},{3,7},{4,0},{5,1},{6,2},{7,3},{8,12},{9,13},{10,... | collective-permute-start | bytes 294920 | tf_op jit(solution)/shard_map/ppermute | solution.py:303
  94.8 1.2 collective-permute-start.27
  96.0 0.8 collective-permute-done.24.refs_0_
  96.8 1.6 %collective-permute-start.28 = (bf16[2,3,64,128]{3,2,1,0:T(8,128)(2,1)S(1)}, bf16[2,3,64,128]{3,2,1,0:T(8,128)(2,1)S(1)}, u32[]{:S(2)}, u32[]{:S(2)}) collective-permute-start(bf16[2,3,64,128]{3,2,1,0:T(8,128)(2,1)S(1)} %get-tuple-element.99), channel_id=1, source_target_pairs={{0,6},{1,7},{2,4},{3,5},{4,2},{5,3},{6,0},{7,1},{8,14},{9,15},{10,... | collective-permute-start | bytes 294920 | tf_op jit(solution)/shard_map/ppermute | solution.py:303
  98.4 1.6 %collective-permute-done.25.refs_1_ = bf16[2,3,64,128]{3,2,1,0:T(8,128)(2,1)S(1)} collective-permute-done((bf16[2,3,64,128]{3,2,1,0:T(8,128)(2,1)S(1)}, bf16[2,3,64,128]{3,2,1,0:T(8,128)(2,1)S(1)}, u32[]{:S(2)}, u32[]{:S(2)}) %collective-permute-start.25) | collective-permute-done | bytes 98336 | tf_op jit(solution)/shard_map/ppermute | solution.py:303
  100.0 1.6 %collective-permute-start.29 = (bf16[2,3,64,128]{3,2,1,0:T(8,128)(2,1)S(1)}, bf16[2,3,64,128]{3,2,1,0:T(8,128)(2,1)S(1)}, u32[]{:S(2)}, u32[]{:S(2)}) collective-permute-start(bf16[2,3,64,128]{3,2,1,0:T(8,128)(2,1)S(1)} %get-tuple-element.100), channel_id=1, source_target_pairs={{0,7},{1,6},{2,5},{3,4},{4,3},{5,2},{6,1},{7,0},{8,15},{9,14},{10,... | collective-permute-start | bytes 294920 | tf_op jit(solution)/shard_map/ppermute | solution.py:303
  101.6 6.3 %collective-permute-done.26.refs_2_ = bf16[2,3,64,128]{3,2,1,0:T(8,128)(2,1)S(1)} collective-permute-done((bf16[2,3,64,128]{3,2,1,0:T(8,128)(2,1)S(1)}, bf16[2,3,64,128]{3,2,1,0:T(8,128)(2,1)S(1)}, u32[]{:S(2)}, u32[]{:S(2)}) %collective-permute-start.26) | collective-permute-done | bytes 98336 | tf_op jit(solution)/shard_map/ppermute | solution.py:303
  108.5 1.5 %collective-permute-done.27.refs_3_ = bf16[2,3,64,128]{3,2,1,0:T(8,128)(2,1)S(1)} collective-permute-done((bf16[2,3,64,128]{3,2,1,0:T(8,128)(2,1)S(1)}, bf16[2,3,64,128]{3,2,1,0:T(8,128)(2,1)S(1)}, u32[]{:S(2)}, u32[]{:S(2)}) %collective-permute-start.27) | collective-permute-done | bytes 98336 | tf_op jit(solution)/shard_map/ppermute | solution.py:303
  110.1 1.7 %collective-permute-start.22 = (bf16[2,256,128]{2,1,0:T(8,128)(2,1)S(1)}, bf16[2,256,128]{2,1,0:T(8,128)(2,1)S(1)}, u32[]{:S(2)}, u32[]{:S(2)}) collective-permute-start(bf16[2,256,128]{2,1,0:T(8,128)(2,1)S(1)} %get-tuple-element.92), channel_id=1, source_target_pairs={{0,16},{8,24},{16,0},{24,8},{1,17},{9,25},{17,1},{25,9},{2,18},{10... | collective-permute-start | bytes 393224 | tf_op jit(solution)/shard_map/ppermute | solution.py:307
  111.7 0.6 collective-permute-done.30.refs_6_
  112.4 0.9 gather_sum.3
  113.4 0.9 collective-permute-start.32
  114.2 1.0 collective-permute-start.33
  115.8 3.9 %collective-permute-done.32.refs_6_ = bf16[2,256,128]{2,1,0:T(8,128)(2,1)S(1)} collective-permute-done((bf16[2,256,128]{2,1,0:T(8,128)(2,1)S(1)}, bf16[2,256,128]{2,1,0:T(8,128)(2,1)S(1)}, u32[]{:S(2)}, u32[]{:S(2)}) %collective-permute-start.32) | collective-permute-done | bytes 131104 | tf_op jit(solution)/shard_map/ppermute | solution.py:307
  119.7 1.9 %collective-permute-done.33.refs_7_ = bf16[2,256,128]{2,1,0:T(8,128)(2,1)S(1)} collective-permute-done((bf16[2,256,128]{2,1,0:T(8,128)(2,1)S(1)}, bf16[2,256,128]{2,1,0:T(8,128)(2,1)S(1)}, u32[]{:S(2)}, u32[]{:S(2)}) %collective-permute-start.33) | collective-permute-done | bytes 131104 | tf_op jit(solution)/shard_map/ppermute | solution.py:307
  121.6 1.6 %join.1 = (bf16[256,1024]{1,0:T(8,128)(2,1)}, bf16[256,1024]{1,0:T(8,128)(2,1)}) custom-call(s32[2]{0:T(128)S(1)} %copy-done.1, bf16[2,256,128]{2,1,0:T(8,128)(2,1)S(1)} %get-tuple-element.90.refs_0_, bf16[2,256,128]{2,1,0:T(8,128)(2,1)S(1)} %collective-permute-done.21.refs_1_, bf16[2,256,128]{2,1,0:T(8,128)(2,1)S(1)} %collective-permute-done.22.refs_2_, ...), custom_call_target="tpu_custom_call" | custom-call | tf_op jit(solution)/shard_map/join/pallas_call | solution.py:247
  (48 shorter events, 5.1 us)
Async XLA Ops:
  4.3 3.2 %collective-permute-start = (bf16[2,2,256,128]{3,2,1,0:T(8,128)(2,1)}, bf16[2,2,256,128]{3,2,1,0:T(8,128)(2,1)S(1)}, u32[]{:S(2)}, u32[]{:S(2)}) collective-permute-start(bf16[2,2,256,128]{3,2,1,0:T(8,128)(2,1)} %get-tuple-element.56), channel_id=1, source_target_pairs={{0,8},{8,0},{16,24},{24,16},{1,9},{9,1},{17,25},{25,17},{2,10},{10... | collective-permute-start | bytes 786440 | tf_op jit(solution)/shard_map/ppermute | solution.py:303
  4.8 10.7 %collective-permute-start.1 = (bf16[2,2,256,128]{3,2,1,0:T(8,128)(2,1)}, bf16[2,2,256,128]{3,2,1,0:T(8,128)(2,1)S(1)}, u32[]{:S(2)}, u32[]{:S(2)}) collective-permute-start(bf16[2,2,256,128]{3,2,1,0:T(8,128)(2,1)} %get-tuple-element.59), channel_id=1, source_target_pairs={{0,16},{8,24},{16,0},{24,8},{1,17},{9,25},{17,1},{25,9},{2,18},{10... | collective-permute-start | bytes 786440 | tf_op jit(solution)/shard_map/ppermute | solution.py:303
  7.3 12.5 %collective-permute-start.2 = (bf16[2,2,256,128]{3,2,1,0:T(8,128)(2,1)}, bf16[2,2,256,128]{3,2,1,0:T(8,128)(2,1)S(1)}, u32[]{:S(2)}, u32[]{:S(2)}) collective-permute-start(bf16[2,2,256,128]{3,2,1,0:T(8,128)(2,1)} %get-tuple-element.60), channel_id=1, source_target_pairs={{0,24},{8,16},{16,8},{24,0},{1,25},{9,17},{17,9},{25,1},{2,26},{10... | collective-permute-start | bytes 786440 | tf_op jit(solution)/shard_map/ppermute | solution.py:303
  9.4 12.5 %all-to-all-start = ((s32[8,1,128]{2,1,0:T(1,128)}), s32[8,1,128]{2,1,0:T(1,128)S(1)}, u32[]{:S(2)}, u32[]{:S(2)}) async-start(s32[8,1,128]{2,1,0:T(1,128)} %bitcast.3), calls=%async_computation | async-start | bytes 8192 | tf_op jit(solution)/shard_map/all_to_all | solution.py:352
  21.8 1.0 copy-start
  22.8 0.6 copy-start.1
  24.1 6.8 %collective-permute-start.3 = (bf16[2,3,64,128]{3,2,1,0:T(8,128)(2,1)S(1)}, bf16[2,3,64,128]{3,2,1,0:T(8,128)(2,1)S(1)}, u32[]{:S(2)}, u32[]{:S(2)}) collective-permute-start(bf16[2,3,64,128]{3,2,1,0:T(8,128)(2,1)S(1)} %get-tuple-element.61), channel_id=1, source_target_pairs={{0,1},{1,0},{2,3},{3,2},{4,5},{5,4},{6,7},{7,6},{8,9},{9,8},{10,11... | collective-permute-start | bytes 294920 | tf_op jit(solution)/shard_map/ppermute | solution.py:303
  24.7 8.5 %collective-permute-start.4 = (bf16[2,3,64,128]{3,2,1,0:T(8,128)(2,1)S(1)}, bf16[2,3,64,128]{3,2,1,0:T(8,128)(2,1)S(1)}, u32[]{:S(2)}, u32[]{:S(2)}) collective-permute-start(bf16[2,3,64,128]{3,2,1,0:T(8,128)(2,1)S(1)} %get-tuple-element.62), channel_id=1, source_target_pairs={{0,2},{1,3},{2,0},{3,1},{4,6},{5,7},{6,4},{7,5},{8,10},{9,11},{10,... | collective-permute-start | bytes 294920 | tf_op jit(solution)/shard_map/ppermute | solution.py:303
  25.5 14.5 %collective-permute-start.5 = (bf16[2,3,64,128]{3,2,1,0:T(8,128)(2,1)S(1)}, bf16[2,3,64,128]{3,2,1,0:T(8,128)(2,1)S(1)}, u32[]{:S(2)}, u32[]{:S(2)}) collective-permute-start(bf16[2,3,64,128]{3,2,1,0:T(8,128)(2,1)S(1)} %get-tuple-element.63), channel_id=1, source_target_pairs={{0,4},{1,5},{2,6},{3,7},{4,0},{5,1},{6,2},{7,3},{8,12},{9,13},{10,... | collective-permute-start | bytes 294920 | tf_op jit(solution)/shard_map/ppermute | solution.py:303
  28.1 14.1 %collective-permute-start.6 = (bf16[2,3,64,128]{3,2,1,0:T(8,128)(2,1)S(1)}, bf16[2,3,64,128]{3,2,1,0:T(8,128)(2,1)S(1)}, u32[]{:S(2)}, u32[]{:S(2)}) collective-permute-start(bf16[2,3,64,128]{3,2,1,0:T(8,128)(2,1)S(1)} %get-tuple-element.64), channel_id=1, source_target_pairs={{0,5},{1,4},{2,7},{3,6},{4,1},{5,0},{6,3},{7,2},{8,13},{9,12},{10,... | collective-permute-start | bytes 294920 | tf_op jit(solution)/shard_map/ppermute | solution.py:303
  29.3 12.9 %collective-permute-start.7 = (bf16[2,3,64,128]{3,2,1,0:T(8,128)(2,1)S(1)}, bf16[2,3,64,128]{3,2,1,0:T(8,128)(2,1)S(1)}, u32[]{:S(2)}, u32[]{:S(2)}) collective-permute-start(bf16[2,3,64,128]{3,2,1,0:T(8,128)(2,1)S(1)} %get-tuple-element.65), channel_id=1, source_target_pairs={{0,6},{1,7},{2,4},{3,5},{4,2},{5,3},{6,0},{7,1},{8,14},{9,15},{10,... | collective-permute-start | bytes 294920 | tf_op jit(solution)/shard_map/ppermute | solution.py:303
  30.9 11.3 %collective-permute-start.8 = (bf16[2,3,64,128]{3,2,1,0:T(8,128)(2,1)S(1)}, bf16[2,3,64,128]{3,2,1,0:T(8,128)(2,1)S(1)}, u32[]{:S(2)}, u32[]{:S(2)}) collective-permute-start(bf16[2,3,64,128]{3,2,1,0:T(8,128)(2,1)S(1)} %get-tuple-element.66), channel_id=1, source_target_pairs={{0,7},{1,6},{2,5},{3,4},{4,3},{5,2},{6,1},{7,0},{8,15},{9,14},{10,... | collective-permute-start | bytes 294920 | tf_op jit(solution)/shard_map/ppermute | solution.py:303
  33.2 10.3 %collective-permute-start.9 = (bf16[2,3,64,128]{3,2,1,0:T(8,128)(2,1)S(1)}, bf16[2,3,64,128]{3,2,1,0:T(8,128)(2,1)S(1)}, u32[]{:S(2)}, u32[]{:S(2)}) collective-permute-start(bf16[2,3,64,128]{3,2,1,0:T(8,128)(2,1)S(1)} %get-tuple-element.67), channel_id=1, source_target_pairs={{0,3},{1,2},{2,1},{3,0},{4,7},{5,6},{6,5},{7,4},{8,11},{9,10},{10,... | collective-permute-start | bytes 294920 | tf_op jit(solution)/shard_map/ppermute | solution.py:303
  43.5 23.7 %collective-permute-start.12 = (bf16[2,3,64,128]{3,2,1,0:T(8,128)(2,1)S(1)}, bf16[2,3,64,128]{3,2,1,0:T(8,128)(2,1)S(1)}, u32[]{:S(2)}, u32[]{:S(2)}) collective-permute-start(bf16[2,3,64,128]{3,2,1,0:T(8,128)(2,1)S(1)} %get-tuple-element.71), channel_id=1, source_target_pairs={{0,4},{1,5},{2,6},{3,7},{4,0},{5,1},{6,2},{7,3},{8,12},{9,13},{10,... | collective-permute-start | bytes 294920 | tf_op jit(solution)/shard_map/ppermute | solution.py:303
  47.2 20.0 %collective-permute-start.13 = (bf16[2,3,64,128]{3,2,1,0:T(8,128)(2,1)S(1)}, bf16[2,3,64,128]{3,2,1,0:T(8,128)(2,1)S(1)}, u32[]{:S(2)}, u32[]{:S(2)}) collective-permute-start(bf16[2,3,64,128]{3,2,1,0:T(8,128)(2,1)S(1)} %get-tuple-element.73), channel_id=1, source_target_pairs={{0,5},{1,4},{2,7},{3,6},{4,1},{5,0},{6,3},{7,2},{8,13},{9,12},{10,... | collective-permute-start | bytes 294920 | tf_op jit(solution)/shard_map/ppermute | solution.py:303
  48.2 21.0 %collective-permute-start.14 = (bf16[2,3,64,128]{3,2,1,0:T(8,128)(2,1)S(1)}, bf16[2,3,64,128]{3,2,1,0:T(8,128)(2,1)S(1)}, u32[]{:S(2)}, u32[]{:S(2)}) collective-permute-start(bf16[2,3,64,128]{3,2,1,0:T(8,128)(2,1)S(1)} %get-tuple-element.75), channel_id=1, source_target_pairs={{0,6},{1,7},{2,4},{3,5},{4,2},{5,3},{6,0},{7,1},{8,14},{9,15},{10,... | collective-permute-start | bytes 294920 | tf_op jit(solution)/shard_map/ppermute | solution.py:303
  49.5 20.8 %collective-permute-start.15 = (bf16[2,3,64,128]{3,2,1,0:T(8,128)(2,1)S(1)}, bf16[2,3,64,128]{3,2,1,0:T(8,128)(2,1)S(1)}, u32[]{:S(2)}, u32[]{:S(2)}) collective-permute-start(bf16[2,3,64,128]{3,2,1,0:T(8,128)(2,1)S(1)} %get-tuple-element.77), channel_id=1, source_target_pairs={{0,7},{1,6},{2,5},{3,4},{4,3},{5,2},{6,1},{7,0},{8,15},{9,14},{10,... | collective-permute-start | bytes 294920 | tf_op jit(solution)/shard_map/ppermute | solution.py:303
  65.7 7.3 %collective-permute-start.10 = (bf16[2,3,64,128]{3,2,1,0:T(8,128)(2,1)S(1)}, bf16[2,3,64,128]{3,2,1,0:T(8,128)(2,1)S(1)}, u32[]{:S(2)}, u32[]{:S(2)}) collective-permute-start(bf16[2,3,64,128]{3,2,1,0:T(8,128)(2,1)S(1)} %get-tuple-element.68), channel_id=1, source_target_pairs={{0,1},{1,0},{2,3},{3,2},{4,5},{5,4},{6,7},{7,6},{8,9},{9,8},{10,11... | collective-permute-start | bytes 294920 | tf_op jit(solution)/shard_map/ppermute | solution.py:303
  67.1 7.2 %collective-permute-start.11 = (bf16[2,3,64,128]{3,2,1,0:T(8,128)(2,1)S(1)}, bf16[2,3,64,128]{3,2,1,0:T(8,128)(2,1)S(1)}, u32[]{:S(2)}, u32[]{:S(2)}) collective-permute-start(bf16[2,3,64,128]{3,2,1,0:T(8,128)(2,1)S(1)} %get-tuple-element.69), channel_id=1, source_target_pairs={{0,2},{1,3},{2,0},{3,1},{4,6},{5,7},{6,4},{7,5},{8,10},{9,11},{10,... | collective-permute-start | bytes 294920 | tf_op jit(solution)/shard_map/ppermute | solution.py:303
  67.2 9.6 %collective-permute-start.16 = (bf16[2,3,64,128]{3,2,1,0:T(8,128)(2,1)S(1)}, bf16[2,3,64,128]{3,2,1,0:T(8,128)(2,1)S(1)}, u32[]{:S(2)}, u32[]{:S(2)}) collective-permute-start(bf16[2,3,64,128]{3,2,1,0:T(8,128)(2,1)S(1)} %get-tuple-element.78), channel_id=1, source_target_pairs={{0,3},{1,2},{2,1},{3,0},{4,7},{5,6},{6,5},{7,4},{8,11},{9,10},{10,... | collective-permute-start | bytes 294920 | tf_op jit(solution)/shard_map/ppermute | solution.py:303
  69.2 21.4 %collective-permute-start.17 = (bf16[2,3,64,128]{3,2,1,0:T(8,128)(2,1)S(1)}, bf16[2,3,64,128]{3,2,1,0:T(8,128)(2,1)S(1)}, u32[]{:S(2)}, u32[]{:S(2)}) collective-permute-start(bf16[2,3,64,128]{3,2,1,0:T(8,128)(2,1)S(1)} %get-tuple-element.86), channel_id=1, source_target_pairs={{0,4},{1,5},{2,6},{3,7},{4,0},{5,1},{6,2},{7,3},{8,12},{9,13},{10,... | collective-permute-start | bytes 294920 | tf_op jit(solution)/shard_map/ppermute | solution.py:303
  70.3 20.3 %collective-permute-start.18 = (bf16[2,3,64,128]{3,2,1,0:T(8,128)(2,1)S(1)}, bf16[2,3,64,128]{3,2,1,0:T(8,128)(2,1)S(1)}, u32[]{:S(2)}, u32[]{:S(2)}) collective-permute-start(bf16[2,3,64,128]{3,2,1,0:T(8,128)(2,1)S(1)} %get-tuple-element.87), channel_id=1, source_target_pairs={{0,5},{1,4},{2,7},{3,6},{4,1},{5,0},{6,3},{7,2},{8,13},{9,12},{10,... | collective-permute-start | bytes 294920 | tf_op jit(solution)/shard_map/ppermute | solution.py:303
  73.0 17.5 %collective-permute-start.19 = (bf16[2,3,64,128]{3,2,1,0:T(8,128)(2,1)S(1)}, bf16[2,3,64,128]{3,2,1,0:T(8,128)(2,1)S(1)}, u32[]{:S(2)}, u32[]{:S(2)}) collective-permute-start(bf16[2,3,64,128]{3,2,1,0:T(8,128)(2,1)S(1)} %get-tuple-element.88), channel_id=1, source_target_pairs={{0,6},{1,7},{2,4},{3,5},{4,2},{5,3},{6,0},{7,1},{8,14},{9,15},{10,... | collective-permute-start | bytes 294920 | tf_op jit(solution)/shard_map/ppermute | solution.py:303
  74.3 16.2 %collective-permute-start.20 = (bf16[2,3,64,128]{3,2,1,0:T(8,128)(2,1)S(1)}, bf16[2,3,64,128]{3,2,1,0:T(8,128)(2,1)S(1)}, u32[]{:S(2)}, u32[]{:S(2)}) collective-permute-start(bf16[2,3,64,128]{3,2,1,0:T(8,128)(2,1)S(1)} %get-tuple-element.89), channel_id=1, source_target_pairs={{0,7},{1,6},{2,5},{3,4},{4,3},{5,2},{6,1},{7,0},{8,15},{9,14},{10,... | collective-permute-start | bytes 294920 | tf_op jit(solution)/shard_map/ppermute | solution.py:303
  91.5 10.1 %collective-permute-start.23 = (bf16[2,256,128]{2,1,0:T(8,128)(2,1)S(1)}, bf16[2,256,128]{2,1,0:T(8,128)(2,1)S(1)}, u32[]{:S(2)}, u32[]{:S(2)}) collective-permute-start(bf16[2,256,128]{2,1,0:T(8,128)(2,1)S(1)} %get-tuple-element.93), channel_id=1, source_target_pairs={{0,24},{8,16},{16,8},{24,0},{1,25},{9,17},{17,9},{25,1},{2,26},{10... | collective-permute-start | bytes 393224 | tf_op jit(solution)/shard_map/ppermute | solution.py:307
  91.6 5.2 %collective-permute-start.24 = (bf16[2,3,64,128]{3,2,1,0:T(8,128)(2,1)S(1)}, bf16[2,3,64,128]{3,2,1,0:T(8,128)(2,1)S(1)}, u32[]{:S(2)}, u32[]{:S(2)}) collective-permute-start(bf16[2,3,64,128]{3,2,1,0:T(8,128)(2,1)S(1)} %get-tuple-element.95), channel_id=1, source_target_pairs={{0,1},{1,0},{2,3},{3,2},{4,5},{5,4},{6,7},{7,6},{8,9},{9,8},{10,11... | collective-permute-start | bytes 294920 | tf_op jit(solution)/shard_map/ppermute | solution.py:303
  93.1 6.9 %collective-permute-start.25 = (bf16[2,3,64,128]{3,2,1,0:T(8,128)(2,1)S(1)}, bf16[2,3,64,128]{3,2,1,0:T(8,128)(2,1)S(1)}, u32[]{:S(2)}, u32[]{:S(2)}) collective-permute-start(bf16[2,3,64,128]{3,2,1,0:T(8,128)(2,1)S(1)} %get-tuple-element.96), channel_id=1, source_target_pairs={{0,2},{1,3},{2,0},{3,1},{4,6},{5,7},{6,4},{7,5},{8,10},{9,11},{10,... | collective-permute-start | bytes 294920 | tf_op jit(solution)/shard_map/ppermute | solution.py:303
  93.1 14.9 %collective-permute-start.26 = (bf16[2,3,64,128]{3,2,1,0:T(8,128)(2,1)S(1)}, bf16[2,3,64,128]{3,2,1,0:T(8,128)(2,1)S(1)}, u32[]{:S(2)}, u32[]{:S(2)}) collective-permute-start(bf16[2,3,64,128]{3,2,1,0:T(8,128)(2,1)S(1)} %get-tuple-element.97), channel_id=1, source_target_pairs={{0,4},{1,5},{2,6},{3,7},{4,0},{5,1},{6,2},{7,3},{8,12},{9,13},{10,... | collective-permute-start | bytes 294920 | tf_op jit(solution)/shard_map/ppermute | solution.py:303
  94.8 15.3 %collective-permute-start.27 = (bf16[2,3,64,128]{3,2,1,0:T(8,128)(2,1)S(1)}, bf16[2,3,64,128]{3,2,1,0:T(8,128)(2,1)S(1)}, u32[]{:S(2)}, u32[]{:S(2)}) collective-permute-start(bf16[2,3,64,128]{3,2,1,0:T(8,128)(2,1)S(1)} %get-tuple-element.98), channel_id=1, source_target_pairs={{0,5},{1,4},{2,7},{3,6},{4,1},{5,0},{6,3},{7,2},{8,13},{9,12},{10,... | collective-permute-start | bytes 294920 | tf_op jit(solution)/shard_map/ppermute | solution.py:303
  96.8 14.9 %collective-permute-start.28 = (bf16[2,3,64,128]{3,2,1,0:T(8,128)(2,1)S(1)}, bf16[2,3,64,128]{3,2,1,0:T(8,128)(2,1)S(1)}, u32[]{:S(2)}, u32[]{:S(2)}) collective-permute-start(bf16[2,3,64,128]{3,2,1,0:T(8,128)(2,1)S(1)} %get-tuple-element.99), channel_id=1, source_target_pairs={{0,6},{1,7},{2,4},{3,5},{4,2},{5,3},{6,0},{7,1},{8,14},{9,15},{10,... | collective-permute-start | bytes 294920 | tf_op jit(solution)/shard_map/ppermute | solution.py:303
  100.0 11.8 %collective-permute-start.29 = (bf16[2,3,64,128]{3,2,1,0:T(8,128)(2,1)S(1)}, bf16[2,3,64,128]{3,2,1,0:T(8,128)(2,1)S(1)}, u32[]{:S(2)}, u32[]{:S(2)}) collective-permute-start(bf16[2,3,64,128]{3,2,1,0:T(8,128)(2,1)S(1)} %get-tuple-element.100), channel_id=1, source_target_pairs={{0,7},{1,6},{2,5},{3,4},{4,3},{5,2},{6,1},{7,0},{8,15},{9,14},{10,... | collective-permute-start | bytes 294920 | tf_op jit(solution)/shard_map/ppermute | solution.py:303
  101.6 10.8 %collective-permute-start.30 = (bf16[2,3,64,128]{3,2,1,0:T(8,128)(2,1)S(1)}, bf16[2,3,64,128]{3,2,1,0:T(8,128)(2,1)S(1)}, u32[]{:S(2)}, u32[]{:S(2)}) collective-permute-start(bf16[2,3,64,128]{3,2,1,0:T(8,128)(2,1)S(1)} %get-tuple-element.101), channel_id=1, source_target_pairs={{0,3},{1,2},{2,1},{3,0},{4,7},{5,6},{6,5},{7,4},{8,11},{9,10},{10,... | collective-permute-start | bytes 294920 | tf_op jit(solution)/shard_map/ppermute | solution.py:303
  107.9 7.3 %collective-permute-start.21 = (bf16[2,256,128]{2,1,0:T(8,128)(2,1)S(1)}, bf16[2,256,128]{2,1,0:T(8,128)(2,1)S(1)}, u32[]{:S(2)}, u32[]{:S(2)}) collective-permute-start(bf16[2,256,128]{2,1,0:T(8,128)(2,1)S(1)} %get-tuple-element.91), channel_id=1, source_target_pairs={{0,8},{8,0},{16,24},{24,16},{1,9},{9,1},{17,25},{25,17},{2,10},{10... | collective-permute-start | bytes 393224 | tf_op jit(solution)/shard_map/ppermute | solution.py:307
  110.1 5.7 %collective-permute-start.22 = (bf16[2,256,128]{2,1,0:T(8,128)(2,1)S(1)}, bf16[2,256,128]{2,1,0:T(8,128)(2,1)S(1)}, u32[]{:S(2)}, u32[]{:S(2)}) collective-permute-start(bf16[2,256,128]{2,1,0:T(8,128)(2,1)S(1)} %get-tuple-element.92), channel_id=1, source_target_pairs={{0,16},{8,24},{16,0},{24,8},{1,17},{9,25},{17,1},{25,9},{2,18},{10... | collective-permute-start | bytes 393224 | tf_op jit(solution)/shard_map/ppermute | solution.py:307
  113.3 2.5 %collective-permute-start.31 = (bf16[2,256,128]{2,1,0:T(8,128)(2,1)S(1)}, bf16[2,256,128]{2,1,0:T(8,128)(2,1)S(1)}, u32[]{:S(2)}, u32[]{:S(2)}) collective-permute-start(bf16[2,256,128]{2,1,0:T(8,128)(2,1)S(1)} %get-tuple-element.103), channel_id=1, source_target_pairs={{0,8},{8,0},{16,24},{24,16},{1,9},{9,1},{17,25},{25,17},{2,10},{10... | collective-permute-start | bytes 393224 | tf_op jit(solution)/shard_map/ppermute | solution.py:307
  113.4 6.3 %collective-permute-start.32 = (bf16[2,256,128]{2,1,0:T(8,128)(2,1)S(1)}, bf16[2,256,128]{2,1,0:T(8,128)(2,1)S(1)}, u32[]{:S(2)}, u32[]{:S(2)}) collective-permute-start(bf16[2,256,128]{2,1,0:T(8,128)(2,1)S(1)} %get-tuple-element.104), channel_id=1, source_target_pairs={{0,16},{8,24},{16,0},{24,8},{1,17},{9,25},{17,1},{25,9},{2,18},{10... | collective-permute-start | bytes 393224 | tf_op jit(solution)/shard_map/ppermute | solution.py:307
  114.2 7.4 %collective-permute-start.33 = (bf16[2,256,128]{2,1,0:T(8,128)(2,1)S(1)}, bf16[2,256,128]{2,1,0:T(8,128)(2,1)S(1)}, u32[]{:S(2)}, u32[]{:S(2)}) collective-permute-start(bf16[2,256,128]{2,1,0:T(8,128)(2,1)S(1)} %get-tuple-element.105), channel_id=1, source_target_pairs={{0,24},{8,16},{16,8},{24,0},{1,25},{9,17},{17,9},{25,1},{2,26},{10... | collective-permute-start | bytes 393224 | tf_op jit(solution)/shard_map/ppermute | solution.py:307
